TPU v7x, 32 devices: a whole 2x2x4 slice. The times are simulated.
32 devices in a mesh: seq: 8 (over z, x), head: 4 (over y, core).
Axes of the slice: x: 2, y: 2, z: 4, core: 2. Of those that a mesh axis runs over, the one named last changes fastest.
Arguments:
- tokens: bfloat16 [2048, 3072], P('seq', 'head'), may hold values from -6 to 6
- norm_gain: float32 [3072], replicated, may hold values from 0.1 to 1.9
- w_query: bfloat16 [3072, 3072], P(None, 'head'), may hold values from -0.109375 to 0.109375
- w_key: bfloat16 [3072, 1024], P(None, 'head'), may hold values from -0.3125 to 0.3125
- w_value: bfloat16 [3072, 1024], P(None, 'head'), may hold values from -0.109375 to 0.109375
- w_out: bfloat16 [3072, 3072], P('head'), may hold values from -0.109375 to 0.109375
- keys_cache: bfloat16 [16384, 1024], P('seq', 'head'), may hold values from -120 to 120
- values_cache: bfloat16 [16384, 1024], P('seq', 'head'), may hold values from -6 to 6
- cached_lengths: int32 [4], replicated, may hold values from 0 to 3584, as said below
- rope_offsets: int32 [4], replicated, may hold values from 0 to 8191
Outputs:
- attn_proj: bfloat16 [2048, 3072], P('seq', 'head')
- keys_updated: bfloat16 [16384, 1024], P('seq', 'head')
- values_updated: bfloat16 [16384, 1024], P('seq', 'head')
Inputs may be any that keep to these rules, and one draw needn't show every extreme that they name: `cached_lengths`: in every draw one request has exactly 3584 cached tokens.
All inputs are finite; a program needn't handle non-finite values.
Results may differ from a plain program's by a relative error of at most 0.02.
Values may be sent and summed in bfloat16 or wider, within the bound.
No kernel may reach another device: no remote copies, remote signals or barrier semaphores. Data moves between devices by JAX's collectives and lax.ppermute only.
A program may use at most 128 MiB of HBM per device.

v0:
```python
import math

import jax
import jax.numpy as jnp
from jax import lax
from jax.sharding import PartitionSpec as P

HD = 128


rope_base = 500000.0
neg_large = -1e30


def shifted(shard, axis, by):
    devices = lax.axis_size(axis)
    return lax.ppermute(shard, axis, [(i, (i + by) % devices) for i in range(devices)])


def rotate(vectors, positions):
    half_width = vectors.shape[-1] // 2
    frequency = rope_base ** (-jnp.arange(half_width, dtype=jnp.float32) * 2.0 / vectors.shape[-1])
    angles = positions.astype(jnp.float32)[:, None] * frequency[None, :]
    cosine = jnp.cos(angles)[:, None, :]
    sine_part = jnp.sin(angles)[:, None, :]
    first_half = vectors[..., :half_width]
    second_half = vectors[..., half_width:]
    return jnp.concatenate(
        [
            first_half * cosine - second_half * sine_part,
            second_half * cosine + first_half * sine_part,
        ],
        -1,
    )


def shards(
    tokens,
    norm_gain,
    w_query,
    w_key,
    w_value,
    w_out,
    keys_cache,
    values_cache,
    cached_lengths,
    rope_offsets,
):
    gathered = lax.all_gather(tokens, "head", axis=1, tiled=True)
    row_count = gathered.shape[0]
    requests = cached_lengths.shape[0]
    groups = lax.axis_size("seq") // requests
    member = lax.axis_index("seq")
    request = member % requests
    position_in = member // requests
    length = lax.dynamic_index_in_dim(cached_lengths, request, 0, False)
    offset = lax.dynamic_index_in_dim(rope_offsets, request, 0, False)
    widened = gathered.astype(jnp.float32)
    normed = (
        widened * lax.rsqrt(jnp.mean(widened * widened, -1, keepdims=True) + 1e-05) * norm_gain
    ).astype(jnp.bfloat16)
    index_new = position_in * row_count + jnp.arange(row_count, dtype=jnp.int32)
    positions = offset + length + index_new
    kv_heads = w_key.shape[1] // HD
    q_heads = w_query.shape[1] // HD
    repeat = q_heads // kv_heads
    queries = rotate(
        jnp.dot(normed, w_query, preferred_element_type=jnp.float32).reshape(
            row_count, q_heads, HD
        ),
        positions,
    ).astype(jnp.bfloat16)
    new_keys = (
        rotate(
            jnp.dot(normed, w_key, preferred_element_type=jnp.float32).reshape(
                row_count, kv_heads, HD
            ),
            positions,
        )
        .astype(jnp.bfloat16)
        .reshape(row_count, kv_heads * HD)
    )
    new_values = jnp.dot(normed, w_value, preferred_element_type=jnp.float32).astype(jnp.bfloat16)
    grouped = (
        queries.reshape(row_count, kv_heads, repeat, HD)
        .transpose(1, 2, 0, 3)
        .reshape(kv_heads, repeat * row_count, HD)
    )
    slab_rows = keys_cache.shape[0]
    score_scale = 1.0 / math.sqrt(HD)

    def attend(softmax_state, query_group, key_block, value_block, visible):
        running_max, denominator, accumulated = softmax_state
        scores = (
            jnp.einsum(
                "gqd,kgd->gqk",
                query_group,
                key_block.reshape(-1, kv_heads, HD),
                preferred_element_type=jnp.float32,
            )
            * score_scale
        )
        masked = jnp.where(visible, scores, neg_large)
        new_max = jnp.maximum(running_max, jnp.max(masked, -1))
        weights = jnp.where(visible, jnp.exp(masked - new_max[..., None]), 0.0)
        factor = jnp.exp(running_max - new_max)
        denominator = denominator * factor + jnp.sum(weights, -1)
        accumulated = accumulated * factor[..., None] + jnp.einsum(
            "gqk,kgd->gqd",
            weights.astype(jnp.bfloat16),
            value_block.reshape(-1, kv_heads, HD),
            preferred_element_type=jnp.float32,
        )
        return (new_max, denominator, accumulated)

    def attend_pair(
        softmax_state,
        query_anchor,
        query_group,
        slab_keys,
        slab_values,
        slab_source,
        fresh_keys,
        fresh_values,
        fresh_source,
    ):
        query_index = jnp.tile(
            query_anchor * row_count + jnp.arange(row_count, dtype=jnp.int32), repeat
        )
        slots = slab_source * slab_rows + jnp.arange(slab_rows, dtype=jnp.int32)
        old_visible = (slots < length)[None, None, :]
        fresh_index = fresh_source * row_count + jnp.arange(row_count, dtype=jnp.int32)
        fresh_visible = (fresh_index[None, :] <= query_index[:, None])[None]
        softmax_state = attend(softmax_state, query_group, slab_keys, slab_values, old_visible)
        softmax_state = attend(softmax_state, query_group, fresh_keys, fresh_values, fresh_visible)
        return softmax_state

    def write_fresh(out_keys, out_values, fresh_keys, fresh_values, fresh_source):
        fresh_index = fresh_source * row_count + jnp.arange(row_count, dtype=jnp.int32)
        local_slot = length + fresh_index - position_in * slab_rows
        target = jnp.where((local_slot >= 0) & (local_slot < slab_rows), local_slot, slab_rows)
        out_keys = out_keys.at[target].set(fresh_keys, mode="drop")
        out_values = out_values.at[target].set(fresh_values, mode="drop")
        return (out_keys, out_values)

    def absorb(loop_carry, incoming, source):
        softmax_state, out_keys, out_values = loop_carry
        fresh_keys = incoming[0, slab_rows:]
        fresh_values = incoming[1, slab_rows:]
        softmax_state = attend_pair(
            softmax_state,
            position_in,
            grouped,
            incoming[0, :slab_rows],
            incoming[1, :slab_rows],
            source,
            fresh_keys,
            fresh_values,
            source,
        )
        out_keys, out_values = write_fresh(out_keys, out_values, fresh_keys, fresh_values, source)
        return (softmax_state, out_keys, out_values)

    start_state = (
        jnp.full((kv_heads, repeat * row_count), neg_large, jnp.float32),
        jnp.zeros((kv_heads, repeat * row_count), jnp.float32),
        jnp.zeros((kv_heads, repeat * row_count, HD), jnp.float32),
    )
    outgoing = jnp.stack(
        [
            jnp.concatenate([keys_cache, new_keys], 0),
            jnp.concatenate([values_cache, new_values], 0),
        ],
        0,
    )
    loop_carry = absorb((start_state, keys_cache, values_cache), outgoing, position_in)

    def cycle_step(cycle_turn, cycle_carry):
        held_blocks, inner_carry = cycle_carry
        held_blocks = shifted(held_blocks, "seq", requests)
        source = (position_in - cycle_turn) % groups
        return (held_blocks, absorb(inner_carry, held_blocks, source))

    unused, loop_carry = lax.fori_loop(1, groups, cycle_step, (outgoing, loop_carry))
    final_state, keys_updated, values_updated = loop_carry
    running_max, denominator, accumulated = final_state
    attended = (
        (accumulated / denominator[..., None])
        .reshape(kv_heads, repeat, row_count, HD)
        .transpose(2, 0, 1, 3)
        .reshape(row_count, q_heads * HD)
        .astype(jnp.bfloat16)
    )
    partial_value = jnp.dot(attended, w_out, preferred_element_type=jnp.float32)
    summed = lax.psum(partial_value.astype(jnp.bfloat16), "head").astype(jnp.float32)
    share_width = partial_value.shape[1] // lax.axis_size("head")
    projected = lax.dynamic_slice_in_dim(
        summed, lax.axis_index("head") * share_width, share_width, 1
    )
    return (projected.astype(jnp.bfloat16), keys_updated, values_updated)


def solution(mesh):
    return jax.shard_map(
        shards,
        mesh=mesh,
        in_specs=(
            P("seq", "head"),
            P(),
            P(None, "head"),
            P(None, "head"),
            P(None, "head"),
            P("head", None),
            P("seq", "head"),
            P("seq", "head"),
            P(),
            P(),
        ),
        out_specs=(P("seq", "head"), P("seq", "head"), P("seq", "head")),
        check_vma=False,
    )
```

profile of v0, /device:TPU:0, one launch (start us, length us, event | category | flops | bytes accessed | tf_op | source)
XLA Modules:
  0.0 225.4 jit_solution(11791692788970292337)
XLA Ops:
  7.2 1.3 copy.58
  8.6 2.3 %copy.59 = bf16[2048,256]{1,0:T(8,128)(2,1)} copy(bf16[2048,256]{1,0:T(8,128)(2,1)} %param.17) | data formatting | bytes 2097152
  11.0 0.6 dynamic_slice.11
  11.6 0.6 dynamic_slice.10
  13.6 2.3 %copy.24 = bf16[2048,256]{0,1:T(8,128)(2,1)} copy(bf16[2048,256]{1,0:T(8,128)(2,1)} %copy.59) | data formatting | bytes 2097152 | tf_op args[7]
  15.8 1.4 copy.22
  17.3 0.3 multiply_cosine_fusion
  17.6 15.8 %all-gather.2.cloned.1.call-done = bf16[256,3072]{1,0:T(8,128)(2,1)} async-done(((bf16[256,768]{1,0:T(8,128)(2,1)}), bf16[256,3072]{1,0:T(8,128)(2,1)}) %all-gather.2.cloned.1.call-update) | async-done | bytes 1572880 | tf_op jit(solution)/shard_map/all_gather | solution.py:49
  33.4 1.8 fusion.12
  35.2 2.0 convolution_convert_fusion.1
  37.3 0.1 copy.25
  37.4 2.9 %fusion.60 = f32[256,256]{0,1:T(8,128)S(1)} fusion(bf16[3072,256]{1,0:T(8,128)(2,1)} %param.13, bf16[256,3072]{1,0:T(8,128)(2,1)} %all-gather.2.cloned.1.call-done, f32[3072]{0:T(1024)S(1)} %copy-done.11, f32[256]{0:T(256)S(1)} %add_rsqrt_fusion), kind=kOutput, calls=%fused_computation.93 | convolution fusion | flops 405798912 | bytes 3421184 | tf_op jit(solution)/shard_map/dot_general | solution.py:75
  40.5 1.7 pad_maximum_fusion
  42.3 2.4 %collective-permute-start = (bf16[2,2304,256]{1,2,0:T(8,128)(2,1)}, bf16[2,2304,256]{1,2,0:T(8,128)(2,1)}, u32[]{:S(2)}, u32[]{:S(2)}) collective-permute-start(bf16[2,2304,256]{1,2,0:T(8,128)(2,1)} %pad_maximum_fusion), channel_id=1, source_target_pairs={{0,16},{4,20},{8,24},{12,28},{16,0},{20,4},{24,8},{28,12},{1,17},{... | collective-permute-start | bytes 7077896 | tf_op jit(solution)/shard_map/while/body/eval_jaxpr/ppermute | solution.py:17
  44.7 0.3 broadcast_compare_fusion.1
  45.0 0.8 add_compare_fusion
  45.8 1.1 slice.56
  46.9 4.4 %fusion.62 = f32[256,768]{0,1:T(8,128)S(1)} fusion(bf16[3072,768]{1,0:T(8,128)(2,1)} %param.12, bf16[256,3072]{1,0:T(8,128)(2,1)S(1)} %copy-done.7, f32[3072]{0:T(1024)S(1)} %copy-done.11, f32[256]{0:T(256)S(1)} %add_rsqrt_fusion), kind=kOutput, calls=%fused_computation.94 | convolution fusion | flops 1211105280 | bytes 7091200 | tf_op jit(solution)/shard_map/dot_general | solution.py:68
  51.3 0.1 subtract_convert_fusion
  51.5 0.2 copy.21
  51.7 1.0 slice_bitcast_fusion.2
  52.8 0.7 slice_bitcast_fusion.3
  53.4 0.5 fusion.68
  53.9 2.2 fusion
  56.1 91.3 %collective-permute-done = bf16[2,2304,256]{1,2,0:T(8,128)(2,1)} collective-permute-done((bf16[2,2304,256]{1,2,0:T(8,128)(2,1)}, bf16[2,2304,256]{1,2,0:T(8,128)(2,1)}, u32[]{:S(2)}, u32[]{:S(2)}) %collective-permute-start) | collective-permute-done | bytes 2359328 | tf_op jit(solution)/shard_map/while/body/eval_jaxpr/ppermute | solution.py:17
  147.4 1.7 slice_bitcast_fusion
  149.1 0.5 fusion.67
  149.6 1.7 fusion.66
  151.4 2.1 fusion.1
  153.6 0.3 fusion.18
  153.9 0.6 fusion.41
  154.5 3.5 %fusion.2 = f32[2,768]{1,0:T(2,128)S(1)} fusion(f32[2,768,2048]{2,1,0:T(8,128)S(1)} %get-tuple-element.70, f32[2,768]{1,0:T(2,128)S(1)} %get-tuple-element.58, pred[2048]{0:T(1024)(128)(4,1)S(1)} %get-tuple-element.72), kind=kLoop, calls=%fused_computation.10 | loop fusion | flops 15727104 | bytes 12597248 | tf_op jit(solution)/shard_map/reduce_sum | solution.py:107
  158.0 3.3 %fusion.4 = f32[2,768]{1,0:T(2,128)S(1)} fusion(f32[2,768,2048]{2,1,0:T(8,128)S(1)} %get-tuple-element.66, f32[2,768]{1,0:T(2,128)S(1)} %get-tuple-element.30, pred[2048]{0:T(1024)(128)(4,1)S(1)} %get-tuple-element.71), kind=kLoop, calls=%fused_computation.12 | loop fusion | flops 15727104 | bytes 12597248 | tf_op jit(solution)/shard_map/while/body/eval_jaxpr/reduce_sum | solution.py:107
  161.2 0.3 fusion.16
  161.6 2.9 %fusion.32 = f32[2,768,128]{2,1,0:T(8,128)S(1)} fusion(bf16[2048,2,128]{0,2,1:T(8,128)(2,1)S(1)} %bitcast.57, f32[2,768,2048]{2,1,0:T(8,128)S(1)} %get-tuple-element.70, f32[2,768]{1,0:T(2,128)S(1)} %get-tuple-element.58, pred[2048]{0:T(1024)(128)(4,1)S(1)} %get-tuple-element.72, f32[2,768]{1,0:T(2,128)S(1)} %get-tuple-element.28, ...), kind=kOutput, calls=%fused_computation.39 | convolution fusion | flops 821428224 | bytes 14438400 | tf_op jit(solution)/shard_map/gqk,kgd->gqd/dot_general | solution.py:108
  164.5 0.8 fusion.15
  165.4 3.2 %fusion.38 = bf16[2,768,128]{2,1,0:T(8,128)(2,1)S(1)} fusion(f32[2,768,128]{2,1,0:T(8,128)S(1)} %fusion.41, f32[2,768,128]{2,1,0:T(8,128)S(1)} %fusion.15, bf16[2048,2,128]{0,2,1:T(8,128)(2,1)S(1)} %bitcast.65, f32[2,768,2048]{2,1,0:T(8,128)S(1)} %get-tuple-element.66, f32[2,768]{1,0:T(2,128)S(1)} %get-tuple-element.30, ...), kind=kOutput, calls=%fused_computation.44 | convolution fusion | flops 822018048 | bytes 15618048 | tf_op jit(solution)/shard_map/while/body/eval_jaxpr/gqk,kgd->gqd/dot_general | solution.py:108
  168.6 0.2 copy.35
  168.8 4.9 %convolution_convert_fusion = bf16[256,3072]{1,0:T(8,128)(2,1)} fusion(bf16[256,768]{0,1:T(8,128)(2,1)S(1)} %bitcast.64, bf16[768,3072]{1,0:T(8,128)(2,1)} %param.15), kind=kOutput, calls=%fused_computation.20 | convolution fusion | flops 1208745984 | bytes 6684672 | tf_op jit(solution)/shard_map/dot_general | solution.py:194
  173.8 0.7 compare_select_fusion.1
  174.5 0.7 compare_select_fusion
  175.2 0.1 copy.38
  175.4 3.8 %scatter_fusion.2 = bf16[2048,256]{1,0:T(8,128)(2,1)} fusion(bf16[2048,256]{1,0:T(8,128)(2,1)} %copy.59, s32[256]{0:T(256)S(1)} %bitcast.78, bf16[256,256]{1,0:T(8,128)(2,1)S(1)} %copy.38), kind=kCustom, calls=%fused_computation.2 | custom fusion | bytes 394240 | tf_op jit(solution)/shard_map/scatter | solution.py:143
  179.3 2.3 %scatter_fusion = bf16[2048,256]{1,0:T(8,128)(2,1)S(1)} fusion(bf16[2048,256]{1,0:T(8,128)(2,1)S(1)} %copy.58, s32[256]{0:T(256)S(1)} %bitcast.79, bf16[256,256]{1,0:T(8,128)(2,1)S(1)} %copy.36), kind=kCustom, calls=%fused_computation | custom fusion | bytes 394240 | tf_op jit(solution)/shard_map/scatter | solution.py:142
  181.8 3.8 %scatter_fusion.3 = bf16[2048,256]{1,0:T(8,128)(2,1)} fusion(bf16[2048,256]{1,0:T(8,128)(2,1)} %scatter_fusion.2, s32[256]{0:T(256)S(1)} %bitcast.76, bf16[256,256]{1,0:T(8,128)(2,1)S(1)} %copy.39), kind=kCustom, calls=%fused_computation.3 | custom fusion | bytes 394240 | tf_op jit(solution)/shard_map/while/body/eval_jaxpr/scatter | solution.py:143
  185.6 2.1 scatter_fusion.1
  187.7 29.1 %all-reduce.2.cloned.1.call-done = bf16[256,3072]{1,0:T(8,128)(2,1)} async-done(((bf16[256,3072]{1,0:T(8,128)(2,1)}), bf16[256,3072]{1,0:T(8,128)(2,1)}) %all-reduce.2.cloned.1.call-update) | async-done | bytes 1572880 | tf_op jit(solution)/shard_map/psum | solution.py:195
  216.8 1.8 convert_convert_fusion
  (50 shorter events, 0.8 us)
Async XLA Ops:
  7.2 28.0 %copy-start = (bf16[3072,256]{1,0:T(8,128)(2,1)S(1)}, bf16[3072,256]{1,0:T(8,128)(2,1)}, u32[]{:S(2)}) copy-start(bf16[3072,256]{1,0:T(8,128)(2,1)} %param.14) | copy-start | bytes 4718596
  7.2 4.4 %copy-start.13 = (s32[4]{0:T(128)S(1)}, s32[4]{0:T(128)}, u32[]{:S(2)}) copy-start(s32[4]{0:T(128)} %param.18) | copy-start | bytes 52
  7.2 3.8 %copy-start.12 = (s32[4]{0:T(128)S(1)}, s32[4]{0:T(128)}, u32[]{:S(2)}) copy-start(s32[4]{0:T(128)} %param.19) | copy-start | bytes 52
  7.2 26.2 %all-gather.2.cloned.1.call-start = ((), (), s32[]{:S(2)}) async-start(), calls=%async_computation | async-start | bytes 1966080 | tf_op jit(solution)/shard_map/all_gather | solution.py:49
  10.8 24.4 %copy-start.11 = (f32[3072]{0:T(1024)S(1)}, f32[3072]{0:T(1024)}, u32[]{:S(2)}) copy-start(f32[3072]{0:T(1024)} %param.11) | copy-start | bytes 36868
  10.9 205.9 %all-reduce.2.cloned.1.call-start = ((), (), s32[]{:S(2)}) async-start(), calls=%async_computation.1 | async-start | bytes 3145728 | tf_op jit(solution)/shard_map/psum | solution.py:195
  37.2 3.1 %copy-start.5 = (bf16[2048,256]{0,1:T(8,128)(2,1)S(1)}, bf16[2048,256]{0,1:T(8,128)(2,1)}, u32[]{:S(2)}) copy-start(bf16[2048,256]{0,1:T(8,128)(2,1)} %copy.24) | copy-start | bytes 3145732
  37.4 3.1 %copy-start.4 = (bf16[2048,256]{0,1:T(8,128)(2,1)S(1)}, bf16[2048,256]{0,1:T(8,128)(2,1)}, u32[]{:S(2)}) copy-start(bf16[2048,256]{0,1:T(8,128)(2,1)} %copy.22) | copy-start | bytes 3145732
  40.4 1.8 copy-start.3
  42.3 105.2 %collective-permute-start = (bf16[2,2304,256]{1,2,0:T(8,128)(2,1)}, bf16[2,2304,256]{1,2,0:T(8,128)(2,1)}, u32[]{:S(2)}, u32[]{:S(2)}) collective-permute-start(bf16[2,2304,256]{1,2,0:T(8,128)(2,1)} %pad_maximum_fusion), channel_id=1, source_target_pairs={{0,16},{4,20},{8,24},{12,28},{16,0},{20,4},{24,8},{28,12},{1,17},{... | collective-permute-start | bytes 7077896 | tf_op jit(solution)/shard_map/while/body/eval_jaxpr/ppermute | solution.py:17
  45.0 1.9 copy-start.7
  51.7 2.2 copy-start.6
  157.9 3.7 %slice-start = ((bf16[1,2304,256]{1,2,0:T(8,128)(2,1)}), bf16[1,2048,256]{1,2,0:T(8,128)(2,1)S(1)}, s32[]{:S(2)}) async-start(bf16[1,2304,256]{1,2,0:T(8,128)(2,1)} %copy-done.3), calls=%async_computation.2 | async-start | bytes 2097152 | tf_op jit(solution)/shard_map/slice | solution.py:155
  168.8 6.5 %copy-start.8 = (bf16[256,256]{0,1:T(8,128)(2,1)S(1)}, bf16[256,256]{0,1:T(8,128)(2,1)}, u32[]{:S(2)}) copy-start(bf16[256,256]{0,1:T(8,128)(2,1)} %get-tuple-element.51) | copy-start | bytes 393220
  173.7 7.8 %copy-start.10 = (bf16[256,256]{0,1:T(8,128)(2,1)S(1)}, bf16[256,256]{0,1:T(8,128)(2,1)}, u32[]{:S(2)}) copy-start(bf16[256,256]{0,1:T(8,128)(2,1)} %get-tuple-element.32) | copy-start | bytes 393220
  173.8 7.9 %copy-start.9 = (bf16[256,256]{0,1:T(8,128)(2,1)S(1)}, bf16[256,256]{0,1:T(8,128)(2,1)}, u32[]{:S(2)}) copy-start(bf16[256,256]{0,1:T(8,128)(2,1)} %get-tuple-element.44) | copy-start | bytes 393220
  179.3 39.3 %copy-start.1 = (bf16[3072,256]{1,0:T(8,128)(2,1)S(1)}, bf16[3072,256]{1,0:T(8,128)(2,1)}, u32[]{:S(2)}) copy-start(bf16[3072,256]{1,0:T(8,128)(2,1)} %param.14) | copy-start | bytes 4718596
  187.7 30.8 %copy-start.2 = (bf16[2048,256]{1,0:T(8,128)(2,1)}, bf16[2048,256]{1,0:T(8,128)(2,1)S(1)}, u32[]{:S(2)}) copy-start(bf16[2048,256]{1,0:T(8,128)(2,1)S(1)} %scatter_fusion.1) | copy-start | bytes 3145732
Sparse Core Ops, SparseCore 0:
  11.0 22.3 all-gather.1
  173.9 42.8 all-reduce.1
where the time goes:
time: 226 us; the launch traced here: 225 us
  waiting for transfers between devices  136 us (60%)
  local copies, waits for them, and re-layouts  27.7 us (12%)
  matrix products  27.2 us (12%)
  other arithmetic  16 us (7%)
  between operations  15.8 us (7%)
  starting transfers between devices  2.49 us (1%)
    ppermute x1, waiting for transfers between devices, shifted(): lax.ppermute(shard, axis, [(i, (i + by) % devices) for i in range(devices)])  91.3 us
    psum x1, waiting for transfers between devices, shards(): lax.psum(partial_value.astype(jnp.bfloat16), 'head').astype(jnp.float32)  29.1 us
    all_gather x1, waiting for transfers between devices, shards(): gathered = lax.all_gather(tokens, 'head', axis=1, tiled=True)  15.8 us
    scatter x2, local copies, waits for them, and re-layouts, write_fresh(): out_values = out_values.at[target].set(fresh_values, mode='drop')  7.64 us
    dot_general x4, matrix products, attend(): jnp.einsum('gqk,kgd->gqd', weights.astype(jnp.bfloat16), value_block.resh...  7.56 us
    reduce_sum x4, other arithmetic, attend(): denominator = denominator * factor + jnp.sum(weights, -1)  7.42 us
    unnamed x32, local copies, waits for them, and re-layouts  7.34 us
    dot_general x4, matrix products, attend(): jnp.einsum('gqd,kgd->gqk', query_group, key_block.reshape(-1, kv_heads, H...  5.32 us
  transfers between devices with their start and end apart: 3, of which 3 were waited for; matrix products, arithmetic and copies ran while one was open for 13% of the time, Pallas kernels for 0%

commit v1 on v0

v1 whole, which is shorter than its diff:
```python
import functools
import math

import jax
import jax.numpy as jnp
from jax import lax
from jax.experimental import pallas as pl
from jax.experimental.pallas import tpu as pltpu
from jax.sharding import PartitionSpec as P

HD = 128
LANES = 128
STAT_ROWS = 8
ROW_TILE = 16
CORES = 2
MIB = 1 << 20

rope_base = 500000.0
neg_large = -1e30
log2_scale = math.log2(math.e) / math.sqrt(HD)

VMEM = pl.BlockSpec(memory_space=pltpu.VMEM)
SMEM = pl.BlockSpec(memory_space=pltpu.SMEM)


def shifted(shard, axis, by):
    devices = lax.axis_size(axis)
    return lax.ppermute(shard, axis, [(i, (i + by) % devices) for i in range(devices)])


def other_core(shard):
    devices = lax.axis_size("head")
    return lax.ppermute(shard, "head", [(i, i ^ 1) for i in range(devices)])


def rope_tables(positions):
    half_width = HD // 2
    frequency = rope_base ** (-jnp.arange(half_width, dtype=jnp.float32) * 2.0 / HD)
    angles = positions.astype(jnp.float32)[:, None] * frequency[None, :]
    cosine = jnp.cos(angles)
    sine = jnp.sin(angles)
    return jnp.concatenate([cosine, cosine], -1), jnp.concatenate([-sine, sine], -1)


def rotate(vectors, cosine, sine):
    return vectors * cosine + pltpu.roll(vectors, HD // 2, 1) * sine


def normed_slices(owner, x_refs, gain):
    rows, width = x_refs[0].shape
    total = jnp.zeros((rows, 1), jnp.float32)
    for x_ref in x_refs:
        wide = x_ref[...].astype(jnp.float32)
        total = total + jnp.sum(wide * wide, -1, keepdims=True)
    factor = lax.rsqrt(total / (width * len(x_refs)) + 1e-05)
    for index, x_ref in enumerate(x_refs):
        wide = x_ref[...].astype(jnp.float32)
        yield (wide * factor * gain[owner[index]]).astype(jnp.bfloat16)


def weight_rows(owner, index, width):
    return pl.ds(pl.multiple_of(owner[index] * width, LANES), width)


def dot(left, right):
    return jnp.dot(left, right, preferred_element_type=jnp.float32)


def dot_transposed(left, right):
    return lax.dot_general(
        left, right, (((1,), (1,)), ((), ())), preferred_element_type=jnp.float32
    )


def stat_rows(columns, rows):
    lane = lax.broadcasted_iota(jnp.int32, (rows, LANES), 1)
    table = jnp.zeros((rows, LANES), jnp.float32)
    for index, column in enumerate(columns):
        table = jnp.where(lane == index, column, table)
    return table.T[:STAT_ROWS]


def attend_kernel(slices, kv_heads, keep_queries, owner, visible_slots, *refs):
    x_refs = refs[:slices]
    gain, w_query, cosine, sine, keys, values = refs[slices : slices + 6]
    partial, stats = refs[slices + 6 : slices + 8]
    rows, width = x_refs[0].shape
    q_heads = w_query.shape[1] // HD
    repeat = q_heads // kv_heads
    product = jnp.zeros((rows, q_heads * HD), jnp.float32)
    for index, normed in enumerate(normed_slices(owner, x_refs, gain)):
        product = product + dot(normed, w_query[weight_rows(owner, index, width), :])
    slot = lax.broadcasted_iota(jnp.int32, (1, keys.shape[0]), 1)
    visible = slot < visible_slots[0]
    columns = []
    for head in range(q_heads):
        own = slice(head * HD, (head + 1) * HD)
        shared = slice(head // repeat * HD, (head // repeat + 1) * HD)
        query = rotate(product[:, own], cosine[...], sine[...]).astype(jnp.bfloat16)
        if keep_queries:
            refs[slices + 8][:, own] = query
        scores = jnp.where(visible, dot_transposed(query, keys[:, shared]), neg_large)
        largest = jnp.max(scores, -1, keepdims=True)
        weights = jnp.exp2((scores - largest) * log2_scale)
        denominator = jnp.sum(weights, -1, keepdims=True)
        summed = dot(weights.astype(jnp.bfloat16), values[:, shared])
        partial[:, own] = (summed / denominator).astype(partial.dtype)
        columns.append(largest * log2_scale + jnp.log2(denominator))
    stats[...] = stat_rows(columns, rows)


def attend(owner, visible_slots, pieces, gain, w_query, tables, keys, values, kv_heads, own):
    rows, width = pieces[0].shape
    out_width = w_query.shape[1]
    out_shape = [
        jax.ShapeDtypeStruct((rows, out_width), jnp.float32 if own else jnp.bfloat16),
        jax.ShapeDtypeStruct((STAT_ROWS, rows), jnp.float32),
    ]
    if own:
        out_shape.append(jax.ShapeDtypeStruct((rows, out_width), jnp.bfloat16))
    slots = keys.shape[0]
    flops = 2 * rows * out_width * (w_query.shape[0] + 2 * slots)
    return pl.pallas_call(
        functools.partial(attend_kernel, len(pieces), kv_heads, own),
        out_shape=out_shape,
        in_specs=[SMEM, SMEM] + [VMEM] * (len(pieces) + 6),
        out_specs=[VMEM] * len(out_shape),
        compiler_params=pltpu.CompilerParams(vmem_limit_bytes=48 * MIB),
        cost_estimate=pl.CostEstimate(
            flops=flops,
            bytes_accessed=2 * (w_query.size + 2 * keys.size + 2 * rows * out_width),
            transcendentals=rows * out_width // HD * slots,
        ),
        name="attend_own" if own else "attend_partner",
    )(owner, visible_slots, *pieces, gain, w_query, *tables, keys, values)


def fresh_kernel(slices, kv_heads, owner, *refs):
    x_refs = refs[:slices]
    gain, w_key, w_value, cosine, sine, new_keys, new_values = refs[slices:]
    rows, width = x_refs[0].shape
    key_sum = jnp.zeros(new_keys.shape, jnp.float32)
    value_sum = jnp.zeros(new_values.shape, jnp.float32)
    for index, normed in enumerate(normed_slices(owner, x_refs, gain)):
        along = weight_rows(owner, index, width)
        key_sum = key_sum + dot(normed, w_key[along, :])
        value_sum = value_sum + dot(normed, w_value[along, :])
    for head in range(kv_heads):
        own = slice(head * HD, (head + 1) * HD)
        new_keys[:, own] = rotate(key_sum[:, own], cosine[...], sine[...]).astype(jnp.bfloat16)
    new_values[...] = value_sum.astype(jnp.bfloat16)


def fresh(owner, pieces, gain, w_key, w_value, tables, kv_heads):
    rows = pieces[0].shape[0]
    shape = jax.ShapeDtypeStruct((rows, w_key.shape[1]), jnp.bfloat16)
    return pl.pallas_call(
        functools.partial(fresh_kernel, len(pieces), kv_heads),
        out_shape=[shape, shape],
        in_specs=[SMEM] + [VMEM] * (len(pieces) + 5),
        out_specs=[VMEM, VMEM],
        compiler_params=pltpu.CompilerParams(vmem_limit_bytes=32 * MIB),
        cost_estimate=pl.CostEstimate(
            flops=4 * rows * w_key.size, bytes_accessed=4 * w_key.size, transcendentals=0
        ),
        name="fresh_kv",
    )(owner, *pieces, gain, w_key, w_value, *tables)


def write_rows(target, fresh_rows, first):
    rows = fresh_rows.shape[0]
    slab_rows = target.shape[0]
    span = rows + ROW_TILE
    start = jnp.clip(first // ROW_TILE * ROW_TILE, 0, slab_rows - span)
    window = pl.ds(pl.multiple_of(start, ROW_TILE), span)
    shift = start - first
    place = lax.broadcasted_iota(jnp.int32, (span, rows), 0) + shift
    chosen = place == lax.broadcasted_iota(jnp.int32, (span, rows), 1)
    moved = dot(chosen.astype(jnp.bfloat16), fresh_rows)
    row = lax.broadcasted_iota(jnp.int32, (span, target.shape[1]), 0) + shift
    inside = (row >= 0) & (row < rows)
    old = target[window, :].astype(jnp.float32)
    target[window, :] = jnp.where(inside, moved, old).astype(jnp.bfloat16)


def update_kernel(sources, kv_heads, first_token, first_slot, queries, *refs):
    key_refs = refs[:sources]
    value_refs = refs[sources : 2 * sources]
    keys, values, partial, stats, keys_updated, values_updated = refs[2 * sources :]
    rows = queries.shape[0]
    q_heads = queries.shape[1] // HD
    repeat = q_heads // kv_heads
    fresh_keys = jnp.concatenate([ref[...] for ref in key_refs], 0)
    fresh_values = jnp.concatenate([ref[...] for ref in value_refs], 0)
    token = lax.broadcasted_iota(jnp.int32, (rows, rows), 0)
    within = lax.broadcasted_iota(jnp.int32, (rows, rows), 1)
    visible = jnp.concatenate(
        [
            within + first_token[source] <= token + first_token[0]
            for source in range(sources)
        ],
        1,
    )
    columns = []
    for head in range(q_heads):
        own = slice(head * HD, (head + 1) * HD)
        shared = slice(head // repeat * HD, (head // repeat + 1) * HD)
        scores = jnp.where(
            visible, dot_transposed(queries[:, own], fresh_keys[:, shared]), neg_large
        )
        largest = jnp.max(scores, -1, keepdims=True)
        weights = jnp.exp2((scores - largest) * log2_scale)
        denominator = jnp.sum(weights, -1, keepdims=True)
        summed = dot(weights.astype(jnp.bfloat16), fresh_values[:, shared])
        partial[:, own] = summed / denominator
        columns.append(largest * log2_scale + jnp.log2(denominator))
    stats[...] = stat_rows(columns, rows)
    keys_updated[...] = keys[...]
    values_updated[...] = values[...]
    for source in range(sources):
        write_rows(keys_updated, key_refs[source][...], first_slot[source])
        write_rows(values_updated, value_refs[source][...], first_slot[source])


def update(first_token, first_slot, queries, new_keys, new_values, keys, values, kv_heads):
    rows, width = queries.shape
    sources = len(new_keys)
    slab = jax.ShapeDtypeStruct(keys.shape, keys.dtype)
    return pl.pallas_call(
        functools.partial(update_kernel, sources, kv_heads),
        out_shape=[
            jax.ShapeDtypeStruct((rows, width), jnp.float32),
            jax.ShapeDtypeStruct((STAT_ROWS, rows), jnp.float32),
            slab,
            slab,
        ],
        in_specs=[SMEM, SMEM] + [VMEM] * (2 * sources + 3),
        out_specs=[VMEM] * 4,
        compiler_params=pltpu.CompilerParams(vmem_limit_bytes=48 * MIB),
        cost_estimate=pl.CostEstimate(
            flops=4 * rows * width * rows * sources,
            bytes_accessed=8 * keys.size,
            transcendentals=rows * width // HD * rows * sources,
        ),
        name="fresh_attend_update",
    )(first_token, first_slot, queries, *new_keys, *new_values, keys, values)


def project_kernel(count, block_of, *refs):
    partials = refs[:count]
    stats = refs[count : 2 * count]
    w_out, projected = refs[2 * count :]
    rows = partials[0].shape[0]
    blocks, _, width = projected.shape
    padding = jnp.zeros((LANES - STAT_ROWS, rows), jnp.float32)
    logs = [jnp.concatenate([stat[...], padding], 0).T for stat in stats]
    largest = functools.reduce(jnp.maximum, logs)
    shares = [jnp.exp2(log - largest) for log in logs]
    total = functools.reduce(jnp.add, shares)
    heads = []
    for head in range(partials[0].shape[1] // HD):
        own = slice(head * HD, (head + 1) * HD)
        column = slice(head, head + 1)
        merged = functools.reduce(
            jnp.add,
            [
                part[:, own].astype(jnp.float32) * share[:, column]
                for part, share in zip(partials, shares)
            ],
        )
        heads.append((merged / total[:, column]).astype(jnp.bfloat16))
    attended = jnp.concatenate(heads, 1)
    for block in range(blocks):
        along = pl.ds(pl.multiple_of(block_of[block] * width, LANES), width)
        projected[block] = dot(attended, w_out[:, along]).astype(projected.dtype)


def project(block_of, partials, stats, w_out):
    rows, width = partials[0].shape
    blocks = block_of.shape[0]
    return pl.pallas_call(
        functools.partial(project_kernel, len(partials)),
        out_shape=jax.ShapeDtypeStruct((blocks, rows, w_out.shape[1] // blocks), jnp.bfloat16),
        in_specs=[SMEM] + [VMEM] * (2 * len(partials) + 1),
        out_specs=VMEM,
        compiler_params=pltpu.CompilerParams(vmem_limit_bytes=40 * MIB),
        cost_estimate=pl.CostEstimate(
            flops=2 * rows * w_out.size, bytes_accessed=2 * w_out.size, transcendentals=0
        ),
        name="combine_project",
    )(block_of, *partials, *stats, w_out)


def shards(
    tokens,
    norm_gain,
    w_query,
    w_key,
    w_value,
    w_out,
    keys_cache,
    values_cache,
    cached_lengths,
    rope_offsets,
):
    rows, width = tokens.shape
    slab_rows = keys_cache.shape[0]
    requests = cached_lengths.shape[0]
    groups = lax.axis_size("seq") // requests
    heads = lax.axis_size("head")
    chips = heads // CORES
    kv_heads = w_key.shape[1] // HD
    member = lax.axis_index("seq")
    head_member = lax.axis_index("head")
    request = member % requests
    position_in = member // requests
    length = lax.dynamic_index_in_dim(cached_lengths, request, 0, False)
    offset = lax.dynamic_index_in_dim(rope_offsets, request, 0, False)
    gain = norm_gain.reshape(heads, 1, width)

    chip_shifts = [(head_member - CORES * k) % heads for k in range(chips)]
    owner = jnp.stack(chip_shifts + [one ^ 1 for one in chip_shifts]).astype(jnp.int32)

    def all_features(own):
        along = [own] + [shifted(own, "head", CORES * k) for k in range(1, chips)]
        return along + [other_core(piece) for piece in along]

    arrived = [tokens] + [shifted(tokens, "seq", k * requests) for k in range(1, groups)]
    sources = [(position_in - k) % groups for k in range(groups)]
    index_new = jnp.arange(rows, dtype=jnp.int32)
    tables = [rope_tables(offset + length + s * rows + index_new) for s in sources]
    visible_slots = jnp.clip(length - position_in * slab_rows, 0, slab_rows).reshape(1)

    pieces = [all_features(piece) for piece in arrived]
    partials = []
    stats = []
    for k in range(1, groups):
        partial, stat = attend(
            owner, visible_slots, pieces[k], gain, w_query, tables[k], keys_cache, values_cache,
            kv_heads, False,
        )
        partials.append(shifted(partial, "seq", -k * requests))
        stats.append(shifted(stat, "seq", -k * requests))
    partial, stat, queries = attend(
        owner, visible_slots, pieces[0], gain, w_query, tables[0], keys_cache, values_cache,
        kv_heads, True,
    )
    partials.append(partial)
    stats.append(stat)
    new_rows = [
        fresh(owner, pieces[k], gain, w_key, w_value, tables[k], kv_heads) for k in range(groups)
    ]
    first_token = jnp.stack([s * rows for s in sources]).astype(jnp.int32)
    first_slot = length - position_in * slab_rows + first_token
    partial, stat, keys_updated, values_updated = update(
        first_token, first_slot, queries, [k for k, _ in new_rows], [v for _, v in new_rows],
        keys_cache, values_cache, kv_heads,
    )
    partials.append(partial)
    stats.append(stat)

    ahead = [(head_member + CORES * k) % heads for k in range(chips)]
    block_of = jnp.stack(ahead + [one ^ 1 for one in ahead]).astype(jnp.int32)
    projected = project(block_of, partials, stats, w_out)
    received = other_core(projected[chips:])
    summed = projected[:chips].astype(jnp.float32) + received.astype(jnp.float32)
    total = summed[0]
    for k in range(1, chips):
        arrived_sum = shifted(summed[k].astype(jnp.bfloat16), "head", CORES * k)
        total = total + arrived_sum.astype(jnp.float32)
    return (total.astype(jnp.bfloat16), keys_updated, values_updated)


def solution(mesh):
    return jax.shard_map(
        shards,
        mesh=mesh,
        in_specs=(
            P("seq", "head"),
            P(),
            P(None, "head"),
            P(None, "head"),
            P(None, "head"),
            P("head", None),
            P("seq", "head"),
            P("seq", "head"),
            P(),
            P(),
        ),
        out_specs=(P("seq", "head"), P("seq", "head"), P("seq", "head")),
        check_vma=False,
    )
```

time: 226 us -> 88.8 us (0.39)
  waiting for transfers between devices: 136 us -> 30.1 us
  Pallas kernels: 0 us -> 33.8 us
  matrix products: 27.2 us -> 0 us
  local copies, waits for them, and re-layouts: 27.7 us -> 2.71 us
  between operations: 15.8 us -> 2.99 us
  starting transfers between devices: 2.49 us -> 12.2 us
  other arithmetic: 16 us -> 6.67 us
    ppermute x1 -> x6, waiting for transfers between devices: 91.3 us -> 27.8 us  [shifted(): lax.ppermute(shard, axis, [(i, (i + by) % devices) for i in range(devices)])]
    pallas_call x0 -> x6, Pallas kernels: none -> 33.8 us  [the longest x2 21.2 us: attend(): pl.pallas_call(functools.partial(attend_kernel, len(pieces), kv_heads, ow...]
    psum x1 -> x0, waiting for transfers between devices: 29.1 us -> none  [shards(): lax.psum(partial_value.astype(jnp.bfloat16), 'head').astype(jnp.float32)]
    dot_general x12 -> x0, matrix products: 27.2 us -> none  [the longest x4 7.56 us: attend(): jnp.einsum('gqk,kgd->gqd', weights.astype(jnp.bfloat16), value_block.resh...]
    all_gather x1 -> x0, waiting for transfers between devices: 15.8 us -> none  [shards(): gathered = lax.all_gather(tokens, 'head', axis=1, tiled=True)]
    scatter x4 -> x0, local copies, waits for them, and re-layouts: 12 us -> none  [the longest x2 7.64 us: write_fresh(): out_values = out_values.at[target].set(fresh_values, mode='drop')]
    reduce_sum x5 -> x0, other arithmetic: 9.21 us -> none  [the longest x4 7.42 us: attend(): denominator = denominator * factor + jnp.sum(weights, -1)]
    ppermute x1 -> x6, starting transfers between devices: 2.41 us -> 11.5 us  [shifted(): lax.ppermute(shard, axis, [(i, (i + by) % devices) for i in range(devices)])]
  transfers between devices with their start and end apart: 3 -> 11, of which waited for: 3 -> 4; matrix products, arithmetic and copies ran while one was open for 13% -> 9% of each run, Pallas kernels for 0% -> 35%
where the time goes in v1:
time: 88.8 us; the launch traced here: 88.5 us
  Pallas kernels  33.8 us (38%)
  waiting for transfers between devices  30.1 us (34%)
  starting transfers between devices  12.2 us (14%)
  other arithmetic  6.67 us (8%)
  between operations  2.99 us (3%)
  local copies, waits for them, and re-layouts  2.71 us (3%)
    ppermute x6, waiting for transfers between devices, shifted(): lax.ppermute(shard, axis, [(i, (i + by) % devices) for i in range(devices)])  27.8 us
    pallas_call x2, Pallas kernels, attend(): pl.pallas_call(functools.partial(attend_kernel, len(pieces), kv_heads, ow...  21.2 us
    ppermute x6, starting transfers between devices, shifted(): lax.ppermute(shard, axis, [(i, (i + by) % devices) for i in range(devices)])  11.5 us
    pallas_call x2, Pallas kernels, fresh(): pl.pallas_call(functools.partial(fresh_kernel, len(pieces), kv_heads), ou...  5.18 us
    pallas_call x1, Pallas kernels, update(): pl.pallas_call(functools.partial(update_kernel, sources, kv_heads), out_s...  4.29 us
    pallas_call x1, Pallas kernels, project(): pl.pallas_call(functools.partial(project_kernel, len(partials)), out_shap...  3.12 us
    concatenate x2, other arithmetic, rope_tables(): jnp.concatenate([cosine, cosine], -1)  2.46 us
    ppermute x5, waiting for transfers between devices, other_core(): return lax.ppermute(shard, 'head', [(i, i ^ 1) for i in range(devices)])  2.28 us
  transfers between devices with their start and end apart: 11, of which 4 were waited for; matrix products, arithmetic and copies ran while one was open for 9% of the time, Pallas kernels for 35%

profile of v1, /device:TPU:0, one launch (start us, length us, event | category | flops | bytes accessed | tf_op | source)
XLA Modules:
  0.0 88.5 jit_solution(14539084475429523436)
XLA Ops:
  0.7 4.1 %collective-permute-start = (bf16[256,768]{1,0:T(8,128)(2,1)}, bf16[256,768]{1,0:T(8,128)(2,1)S(1)}, u32[]{:S(2)}, u32[]{:S(2)}) collective-permute-start(bf16[256,768]{1,0:T(8,128)(2,1)} %refs_0_.3), channel_id=1, source_target_pairs={{0,16},{4,20},{8,24},{12,28},{16,0},{20,4},{24,8},{28,12},{1,17},{... | collective-permute-start | bytes 1179656 | tf_op jit(solution)/shard_map/ppermute | solution.py:28
  4.8 0.0 collective-permute-start.6
  4.8 1.5 %collective-permute-start.5 = (bf16[256,768]{1,0:T(8,128)(2,1)}, bf16[256,768]{1,0:T(8,128)(2,1)S(1)}, u32[]{:S(2)}, u32[]{:S(2)}) collective-permute-start(bf16[256,768]{1,0:T(8,128)(2,1)} %refs_0_.3), channel_id=1, source_target_pairs={{0,2},{1,3},{2,0},{3,1},{4,6},{5,7},{6,4},{7,5},{8,10},{9,11},{10,... | collective-permute-start | bytes 1179656 | tf_op jit(solution)/shard_map/ppermute | solution.py:28
  6.3 1.2 %dynamic_slice.8 = s32[1]{0:T(128)} dynamic-slice(s32[4]{0:T(128)} %param.19, s32[]{:T(128)S(6)} %select_n.42), dynamic_slice_sizes={1} | dynamic-slice | bytes 12 | tf_op jit(solution)/shard_map/jit(dynamic_index_in_dim)/dynamic_slice | solution.py:318
  7.5 1.3 %dynamic_slice.7 = s32[1]{0:T(128)} dynamic-slice(s32[4]{0:T(128)} %param.18, s32[]{:T(128)S(6)} %select_n.42), dynamic_slice_sizes={1} | dynamic-slice | bytes 12 | tf_op jit(solution)/shard_map/jit(dynamic_index_in_dim)/dynamic_slice | solution.py:317
  10.2 12.3 %collective-permute-done.refs_0_ = bf16[256,768]{1,0:T(8,128)(2,1)S(1)} collective-permute-done((bf16[256,768]{1,0:T(8,128)(2,1)}, bf16[256,768]{1,0:T(8,128)(2,1)S(1)}, u32[]{:S(2)}, u32[]{:S(2)}) %collective-permute-start) | collective-permute-done | bytes 393248 | tf_op jit(solution)/shard_map/ppermute | solution.py:28
  22.5 1.6 %collective-permute-start.1 = (bf16[256,768]{1,0:T(8,128)(2,1)S(1)}, bf16[256,768]{1,0:T(8,128)(2,1)}, u32[]{:S(2)}, u32[]{:S(2)}) collective-permute-start(bf16[256,768]{1,0:T(8,128)(2,1)S(1)} %collective-permute-done.refs_0_), channel_id=1, source_target_pairs={{0,2},{1,3},{2,0},{3,1},{4,6},{5,7},{6,4},{7,5},{8,10},{9,11},{10,... | collective-permute-start | bytes 1179656 | tf_op jit(solution)/shard_map/ppermute | solution.py:28
  24.1 1.8 %fusion.4 = (f32[256,64]{1,0:T(8,128)}, f32[256,64]{1,0:T(8,128)}, f32[256,64]{1,0:T(8,128)}, f32[256,64]{1,0:T(8,128)}, f32[256,64]{1,0:T(8,128)}, /*index=5*/f32[256,64]{1,0:T(8,128)}) fusion(f32[64]{0:T(128)S(1)} %multiply_power_fusion, f32[256]{0:T(256)S(1)} %add_convert_fusion, f32[256]{0:T(256)S(1)} %add_convert_fusion.1), kind=kLoop, calls=%fused_computation.15 | loop fusion | flops 65536 | bytes 395520 | tf_op jit(solution)/shard_map/neg | solution.py:42
  26.6 0.7 broadcast_add_fusion
  27.3 0.0 collective-permute-start.2
  27.3 5.6 %collective-permute-done.1.refs_1_ = bf16[256,768]{1,0:T(8,128)(2,1)} collective-permute-done((bf16[256,768]{1,0:T(8,128)(2,1)S(1)}, bf16[256,768]{1,0:T(8,128)(2,1)}, u32[]{:S(2)}, u32[]{:S(2)}) %collective-permute-start.1) | collective-permute-done | bytes 393248 | tf_op jit(solution)/shard_map/ppermute | solution.py:28
  32.9 0.0 collective-permute-start.3
  32.9 0.1 pad_add_fusion.1.owner
  33.0 1.2 %pad_maximum_fusion.2 = (f32[256,128]{1,0:T(8,128)S(1)}, f32[256,128]{1,0:T(8,128)S(1)}) fusion(f32[256,64]{1,0:T(8,128)} %get-tuple-element.32, f32[256,64]{1,0:T(8,128)} %get-tuple-element.33, f32[256,64]{1,0:T(8,128)} %get-tuple-element.31), kind=kLoop, calls=%fused_computation.12 | loop fusion | flops 65536 | bytes 458752 | tf_op jit(solution)/shard_map/concatenate | solution.py:42
  34.2 0.0 collective-permute-done.5.refs_1_
  34.3 0.6 collective-permute-start.7
  34.8 0.6 pad_add_fusion.block_of
  35.4 1.2 %pad_maximum_fusion = (f32[256,128]{1,0:T(8,128)S(1)}, f32[256,128]{1,0:T(8,128)S(1)}) fusion(f32[256,64]{1,0:T(8,128)} %get-tuple-element.37, f32[256,64]{1,0:T(8,128)} %get-tuple-element.38, f32[256,64]{1,0:T(8,128)} %get-tuple-element.39), kind=kLoop, calls=%fused_computation.10 | loop fusion | flops 65536 | bytes 458752 | tf_op jit(solution)/shard_map/concatenate | solution.py:42
  36.6 0.0 collective-permute-done.2.refs_2_
  36.7 0.0 collective-permute-done.3.refs_3_
  36.7 0.0 copy-start
  36.7 0.0 copy-start.1
  36.7 0.0 copy-start.4
  36.7 10.7 %attend_partner.1 = (bf16[256,768]{1,0:T(8,128)(2,1)S(1)}, f32[8,256]{1,0:T(8,128)S(1)}) custom-call(s32[4]{0:T(128)S(1)} %pad_add_fusion.1.owner, s32[1]{0:T(128)} %bitcast.7.visible_slots, bf16[256,768]{1,0:T(8,128)(2,1)S(1)} %collective-permute-done.refs_0_, bf16[256,768]{1,0:T(8,128)(2,1)} %collective-permute-done.1.refs_1_, ...), custom_call_target="tpu_custom_call" | custom-call | flops 2818572288 | bytes 7602176 | tf_op jit(solution)/shard_map/attend_partner/pallas_call | solution.py:123
  47.4 0.1 collective-permute-start.4
  47.5 0.0 collective-permute-done.6.refs_2_
  47.5 0.0 collective-permute-done.7.refs_3_
  47.5 0.0 copy-done
  47.6 0.0 copy-done.1
  47.6 0.0 copy-done.4
  47.6 0.0 slice-start
  47.6 2.6 %fresh_kv.2 = (bf16[256,256]{1,0:T(8,128)(2,1)S(1)}, bf16[256,256]{1,0:T(8,128)(2,1)S(1)}) custom-call(s32[4]{0:T(128)S(1)} %pad_add_fusion.1.owner, bf16[256,768]{1,0:T(8,128)(2,1)S(1)} %copy-done.4, bf16[256,768]{1,0:T(8,128)(2,1)S(1)} %collective-permute-done.5.refs_1_, bf16[256,768]{1,0:T(8,128)(2,1)S(1)} %collective-permute-done.6.refs_2_, ...), custom_call_target="tpu_custom_call" | custom-call | flops 805306368 | bytes 3145728 | tf_op jit(solution)/shard_map/fresh_kv/pallas_call | solution.py:157
  50.1 0.0 slice-start.1
  50.2 10.5 %attend_own.1 = (f32[256,768]{1,0:T(8,128)S(1)}, f32[8,256]{1,0:T(8,128)S(1)}, bf16[256,768]{1,0:T(8,128)(2,1)S(1)}) custom-call(s32[4]{0:T(128)S(1)} %pad_add_fusion.1.owner, s32[1]{0:T(128)} %bitcast.7.visible_slots, bf16[256,768]{1,0:T(8,128)(2,1)S(1)} %copy-done.4, bf16[256,768]{1,0:T(8,128)(2,1)S(1)} %collective-permute-done.5.refs_1_, ...), custom_call_target="tpu_custom_call" | custom-call | flops 2818572288 | bytes 7602176 | tf_op jit(solution)/shard_map/attend_own/pallas_call | solution.py:123
  60.7 3.0 %collective-permute-start.8 = (f32[8,256]{1,0:T(8,128)S(1)}, f32[8,256]{1,0:T(8,128)S(1)}, u32[]{:S(2)}, u32[]{:S(2)}) collective-permute-start(f32[8,256]{1,0:T(8,128)S(1)} %get-tuple-element.24), channel_id=1, source_target_pairs={{0,16},{4,20},{8,24},{12,28},{16,0},{20,4},{24,8},{28,12},{1,17},{... | collective-permute-start | bytes 24584 | tf_op jit(solution)/shard_map/ppermute | solution.py:28
  63.7 2.6 %fresh_kv.3 = (bf16[256,256]{1,0:T(8,128)(2,1)S(1)}, bf16[256,256]{1,0:T(8,128)(2,1)S(1)}) custom-call(s32[4]{0:T(128)S(1)} %pad_add_fusion.1.owner, bf16[256,768]{1,0:T(8,128)(2,1)S(1)} %collective-permute-done.refs_0_, bf16[256,768]{1,0:T(8,128)(2,1)} %collective-permute-done.1.refs_1_, bf16[256,768]{1,0:T(8,128)(2,1)} %collective-permute-done.2.refs_2_, ...), custom_call_target="tpu_custom_call" | custom-call | flops 805306368 | bytes 3145728 | tf_op jit(solution)/shard_map/fresh_kv/pallas_call | solution.py:157
  66.3 0.0 copy-start.6
  66.4 4.3 %fresh_attend_update.1 = (f32[256,768]{1,0:T(8,128)S(1)}, f32[8,256]{1,0:T(8,128)S(1)}, bf16[2048,256]{1,0:T(8,128)(2,1)}, bf16[2048,256]{1,0:T(8,128)(2,1)}) custom-call(s32[2]{0:T(128)S(1)} %copy-done.8, s32[2]{0:T(128)S(1)} %copy-done.7, bf16[256,768]{1,0:T(8,128)(2,1)S(1)} %get-tuple-element.18.queries, bf16[256,256]{1,0:T(8,128)(2,1)S(1)} %get-tuple-element.19.refs_0_, ...), custom_call_target="tpu_custom_call" | custom-call | flops 402653184 | bytes 4194304 | tf_op jit(solution)/shard_map/fresh_attend_update/pallas_call | solution.py:229
  70.7 0.0 collective-permute-done.8.refs_3_
  70.7 0.0 collective-permute-done.4.refs_0_
  70.7 3.1 %combine_project.1 = bf16[4,256,768]{2,1,0:T(8,128)(2,1)S(1)} custom-call(s32[4]{0:T(128)S(1)} %copy-done.6, bf16[256,768]{1,0:T(8,128)(2,1)S(1)} %collective-permute-done.4.refs_0_, f32[256,768]{1,0:T(8,128)S(1)} %get-tuple-element.17.refs_1_, f32[256,768]{1,0:T(8,128)S(1)} %get-tuple-element.23.refs_2_, f32[8,256]{1,0:T(8,128)S(1)} %collective-permute-done.8.refs_3_, ...), custom_call_target="tpu_custom_call" | custom-call | flops 1207959552 | bytes 4718592 | tf_op jit(solution)/shard_map/combine_project/pallas_call | solution.py:281
  73.8 0.1 slice.18
  73.9 0.1 collective-permute-start.9
  74.0 2.3 %collective-permute-done.9 = bf16[2,256,768]{2,1,0:T(8,128)(2,1)S(1)} collective-permute-done((bf16[2,256,768]{2,1,0:T(8,128)(2,1)S(1)}, bf16[2,256,768]{2,1,0:T(8,128)(2,1)S(1)}, u32[]{:S(2)}, u32[]{:S(2)}) %collective-permute-start.9) | collective-permute-done | bytes 786464 | tf_op jit(solution)/shard_map/ppermute | solution.py:33
  76.2 0.2 convert_add_fusion
  76.5 1.3 %collective-permute-start.10 = (bf16[256,768]{1,0:T(8,128)(2,1)S(1)}, bf16[256,768]{1,0:T(8,128)(2,1)S(1)}, u32[]{:S(2)}, u32[]{:S(2)}) collective-permute-start(bf16[256,768]{1,0:T(8,128)(2,1)S(1)} %fusion.2), channel_id=1, source_target_pairs={{0,2},{1,3},{2,0},{3,1},{4,6},{5,7},{6,4},{7,5},{8,10},{9,11},{10,... | collective-permute-start | bytes 1179656 | tf_op jit(solution)/shard_map/ppermute | solution.py:28
  77.8 9.9 %collective-permute-done.10 = bf16[256,768]{1,0:T(8,128)(2,1)S(1)} collective-permute-done((bf16[256,768]{1,0:T(8,128)(2,1)S(1)}, bf16[256,768]{1,0:T(8,128)(2,1)S(1)}, u32[]{:S(2)}, u32[]{:S(2)}) %collective-permute-start.10) | collective-permute-done | bytes 393248 | tf_op jit(solution)/shard_map/ppermute | solution.py:28
  87.7 0.8 fusion.1
  (18 shorter events, 0.1 us)
Async XLA Ops:
  0.6 36.0 %copy-start.3 = (bf16[2048,256]{1,0:T(8,128)(2,1)S(1)}, bf16[2048,256]{1,0:T(8,128)(2,1)}, u32[]{:S(2)}) copy-start(bf16[2048,256]{1,0:T(8,128)(2,1)} %refs_5_.9) | copy-start | bytes 3145732
  0.6 36.0 %copy-start.2 = (bf16[2048,256]{1,0:T(8,128)(2,1)S(1)}, bf16[2048,256]{1,0:T(8,128)(2,1)}, u32[]{:S(2)}) copy-start(bf16[2048,256]{1,0:T(8,128)(2,1)} %refs_4_.1) | copy-start | bytes 3145732
  0.7 36.0 %copy-start.5 = (f32[3072]{0:T(1024)S(1)}, f32[3072]{0:T(1024)}, u32[]{:S(2)}) copy-start(f32[3072]{0:T(1024)} %param.11) | copy-start | bytes 36868
  0.7 21.9 %collective-permute-start = (bf16[256,768]{1,0:T(8,128)(2,1)}, bf16[256,768]{1,0:T(8,128)(2,1)S(1)}, u32[]{:S(2)}, u32[]{:S(2)}) collective-permute-start(bf16[256,768]{1,0:T(8,128)(2,1)} %refs_0_.3), channel_id=1, source_target_pairs={{0,16},{4,20},{8,24},{12,28},{16,0},{20,4},{24,8},{28,12},{1,17},{... | collective-permute-start | bytes 1179656 | tf_op jit(solution)/shard_map/ppermute | solution.py:28
  4.8 42.8 %collective-permute-start.6 = (bf16[256,768]{1,0:T(8,128)(2,1)}, bf16[256,768]{1,0:T(8,128)(2,1)S(1)}, u32[]{:S(2)}, u32[]{:S(2)}) collective-permute-start(bf16[256,768]{1,0:T(8,128)(2,1)} %refs_0_.3), channel_id=1, source_target_pairs={{0,1},{1,0},{2,3},{3,2},{4,5},{5,4},{6,7},{7,6},{8,9},{9,8},{10,11... | collective-permute-start | bytes 1179656 | tf_op jit(solution)/shard_map/ppermute | solution.py:33
  4.8 29.5 %collective-permute-start.5 = (bf16[256,768]{1,0:T(8,128)(2,1)}, bf16[256,768]{1,0:T(8,128)(2,1)S(1)}, u32[]{:S(2)}, u32[]{:S(2)}) collective-permute-start(bf16[256,768]{1,0:T(8,128)(2,1)} %refs_0_.3), channel_id=1, source_target_pairs={{0,2},{1,3},{2,0},{3,1},{4,6},{5,7},{6,4},{7,5},{8,10},{9,11},{10,... | collective-permute-start | bytes 1179656 | tf_op jit(solution)/shard_map/ppermute | solution.py:28
  22.5 10.4 %collective-permute-start.1 = (bf16[256,768]{1,0:T(8,128)(2,1)S(1)}, bf16[256,768]{1,0:T(8,128)(2,1)}, u32[]{:S(2)}, u32[]{:S(2)}) collective-permute-start(bf16[256,768]{1,0:T(8,128)(2,1)S(1)} %collective-permute-done.refs_0_), channel_id=1, source_target_pairs={{0,2},{1,3},{2,0},{3,1},{4,6},{5,7},{6,4},{7,5},{8,10},{9,11},{10,... | collective-permute-start | bytes 1179656 | tf_op jit(solution)/shard_map/ppermute | solution.py:28
  27.3 9.3 %collective-permute-start.2 = (bf16[256,768]{1,0:T(8,128)(2,1)S(1)}, bf16[256,768]{1,0:T(8,128)(2,1)}, u32[]{:S(2)}, u32[]{:S(2)}) collective-permute-start(bf16[256,768]{1,0:T(8,128)(2,1)S(1)} %collective-permute-done.refs_0_), channel_id=1, source_target_pairs={{0,1},{1,0},{2,3},{3,2},{4,5},{5,4},{6,7},{7,6},{8,9},{9,8},{10,11... | collective-permute-start | bytes 1179656 | tf_op jit(solution)/shard_map/ppermute | solution.py:33
  32.9 3.7 %collective-permute-start.3 = (bf16[256,768]{1,0:T(8,128)(2,1)}, bf16[256,768]{1,0:T(8,128)(2,1)}, u32[]{:S(2)}, u32[]{:S(2)}) collective-permute-start(bf16[256,768]{1,0:T(8,128)(2,1)} %collective-permute-done.1.refs_1_), channel_id=1, source_target_pairs={{0,1},{1,0},{2,3},{3,2},{4,5},{5,4},{6,7},{7,6},{8,9},{9,8},{10,11... | collective-permute-start | bytes 1179656 | tf_op jit(solution)/shard_map/ppermute | solution.py:33
  34.3 13.3 %collective-permute-start.7 = (bf16[256,768]{1,0:T(8,128)(2,1)S(1)}, bf16[256,768]{1,0:T(8,128)(2,1)}, u32[]{:S(2)}, u32[]{:S(2)}) collective-permute-start(bf16[256,768]{1,0:T(8,128)(2,1)S(1)} %collective-permute-done.5.refs_1_), channel_id=1, source_target_pairs={{0,1},{1,0},{2,3},{3,2},{4,5},{5,4},{6,7},{7,6},{8,9},{9,8},{10,11... | collective-permute-start | bytes 1179656 | tf_op jit(solution)/shard_map/ppermute | solution.py:33
  36.7 10.9 %copy-start = (bf16[3072,256]{1,0:T(8,128)(2,1)S(1)}, bf16[3072,256]{1,0:T(8,128)(2,1)}, u32[]{:S(2)}) copy-start(bf16[3072,256]{1,0:T(8,128)(2,1)} %refs_5_.8) | copy-start | bytes 4718596
  36.7 10.8 %copy-start.1 = (bf16[3072,256]{1,0:T(8,128)(2,1)S(1)}, bf16[3072,256]{1,0:T(8,128)(2,1)}, u32[]{:S(2)}) copy-start(bf16[3072,256]{1,0:T(8,128)(2,1)} %refs_6_.4) | copy-start | bytes 4718596
  36.7 10.8 %copy-start.4 = (bf16[256,768]{1,0:T(8,128)(2,1)S(1)}, bf16[256,768]{1,0:T(8,128)(2,1)}, u32[]{:S(2)}) copy-start(bf16[256,768]{1,0:T(8,128)(2,1)} %refs_0_.3) | copy-start | bytes 1179652
  47.4 23.2 %collective-permute-start.4 = (bf16[256,768]{1,0:T(8,128)(2,1)S(1)}, bf16[256,768]{1,0:T(8,128)(2,1)S(1)}, u32[]{:S(2)}, u32[]{:S(2)}) collective-permute-start(bf16[256,768]{1,0:T(8,128)(2,1)S(1)} %get-tuple-element.16), channel_id=1, source_target_pairs={{0,16},{4,20},{8,24},{12,28},{16,0},{20,4},{24,8},{28,12},{1,17},{... | collective-permute-start | bytes 1179656 | tf_op jit(solution)/shard_map/ppermute | solution.py:28
  47.6 23.1 %slice-start = ((s8[4718592]{0:T(1024)(128)(4,1)}), s8[4194304]{0:T(1024)(128)(4,1)S(1)}, s32[]{:S(2)}) async-start(s8[4718592]{0:T(1024)(128)(4,1)} %bitcast.20), calls=%async_computation | async-start | bytes 8388608
  50.1 20.5 %slice-start.1 = ((s8[4718592]{0:T(1024)(128)(4,1)}), s8[524288]{0:T(1024)(128)(4,1)S(1)}, s32[]{:S(2)}) async-start(s8[4718592]{0:T(1024)(128)(4,1)} %bitcast.20), calls=%async_computation.1 | async-start | bytes 1048576
  60.7 5.6 %copy-start.7 = (s32[2]{0:T(128)S(1)}, s32[2]{0:T(128)}, u32[]{:S(2)}) copy-start(s32[2]{0:T(128)} %get-tuple-element.29.first_slot) | copy-start | bytes 28
  60.7 5.6 %copy-start.8 = (s32[2]{0:T(128)S(1)}, s32[2]{0:T(128)}, u32[]{:S(2)}) copy-start(s32[2]{0:T(128)} %get-tuple-element.30.first_token) | copy-start | bytes 28
  60.7 9.9 %collective-permute-start.8 = (f32[8,256]{1,0:T(8,128)S(1)}, f32[8,256]{1,0:T(8,128)S(1)}, u32[]{:S(2)}, u32[]{:S(2)}) collective-permute-start(f32[8,256]{1,0:T(8,128)S(1)} %get-tuple-element.24), channel_id=1, source_target_pairs={{0,16},{4,20},{8,24},{12,28},{16,0},{20,4},{24,8},{28,12},{1,17},{... | collective-permute-start | bytes 24584 | tf_op jit(solution)/shard_map/ppermute | solution.py:28
  66.3 4.3 %copy-start.6 = (s32[4]{0:T(128)S(1)}, s32[4]{0:T(128)}, u32[]{:S(2)}) copy-start(s32[4]{0:T(128)} %pad_add_fusion.block_of) | copy-start | bytes 52
  73.9 2.4 %collective-permute-start.9 = (bf16[2,256,768]{2,1,0:T(8,128)(2,1)S(1)}, bf16[2,256,768]{2,1,0:T(8,128)(2,1)S(1)}, u32[]{:S(2)}, u32[]{:S(2)}) collective-permute-start(bf16[2,256,768]{2,1,0:T(8,128)(2,1)S(1)} %slice.18), channel_id=1, source_target_pairs={{0,1},{1,0},{2,3},{3,2},{4,5},{5,4},{6,7},{7,6},{8,9},{9,8},{10,11... | collective-permute-start | bytes 2359304 | tf_op jit(solution)/shard_map/ppermute | solution.py:33
  76.5 11.2 %collective-permute-start.10 = (bf16[256,768]{1,0:T(8,128)(2,1)S(1)}, bf16[256,768]{1,0:T(8,128)(2,1)S(1)}, u32[]{:S(2)}, u32[]{:S(2)}) collective-permute-start(bf16[256,768]{1,0:T(8,128)(2,1)S(1)} %fusion.2), channel_id=1, source_target_pairs={{0,2},{1,3},{2,0},{3,1},{4,6},{5,7},{6,4},{7,5},{8,10},{9,11},{10,... | collective-permute-start | bytes 1179656 | tf_op jit(solution)/shard_map/ppermute | solution.py:28

commit v2 on v1

v2 whole, which is shorter than its diff:
```python
import functools
import math

import jax
import jax.numpy as jnp
from jax import lax
from jax.experimental import pallas as pl
from jax.experimental.pallas import tpu as pltpu
from jax.sharding import PartitionSpec as P

HD = 128
LANES = 128
STAT_ROWS = 8
ROW_TILE = 16
CORES = 2
CHUNKS = 2
MIB = 1 << 20

rope_base = 500000.0
neg_large = -1e30
log2_scale = math.log2(math.e) / math.sqrt(HD)

VMEM = pl.BlockSpec(memory_space=pltpu.VMEM)
SMEM = pl.BlockSpec(memory_space=pltpu.SMEM)


def shifted(shard, axis, by):
    devices = lax.axis_size(axis)
    return lax.ppermute(shard, axis, [(i, (i + by) % devices) for i in range(devices)])


def other_core(shard):
    devices = lax.axis_size("head")
    return lax.ppermute(shard, "head", [(i, i ^ 1) for i in range(devices)])


def all_features(own):
    chips = lax.axis_size("head") // CORES
    along = [own] + [shifted(own, "head", CORES * k) for k in range(1, chips)]
    return along + [other_core(piece) for piece in along]


def place_of(requests):
    member = lax.axis_index("seq")
    return lax.rem(member, requests), lax.div(member, requests)


def source_of(position_in, turn, groups):
    return lax.rem(position_in + (groups - turn), groups)


def dot(left, right):
    return jnp.dot(left, right, preferred_element_type=jnp.float32)


def dot_transposed(left, right):
    return lax.dot_general(
        left, right, (((1,), (1,)), ((), ())), preferred_element_type=jnp.float32
    )


def call(kernel, out_shape, scalars, arrays, limit, flops, transcendentals, name):
    moved = sum(a.size * a.dtype.itemsize for a in arrays)
    moved += sum(math.prod(s.shape) * s.dtype.itemsize for s in out_shape)
    return pl.pallas_call(
        kernel,
        out_shape=out_shape,
        in_specs=[SMEM] * len(scalars) + [VMEM] * len(arrays),
        out_specs=[VMEM] * len(out_shape),
        compiler_params=pltpu.CompilerParams(vmem_limit_bytes=limit * MIB),
        cost_estimate=pl.CostEstimate(
            flops=flops, bytes_accessed=moved, transcendentals=transcendentals
        ),
        name=name,
    )(*scalars, *arrays)


def prepare_kernel(groups, rows, lengths, offsets, keys, values, cosine, sine, wide_keys, wide_values):
    request, position_in = place_of(lengths.shape[0])
    length = lengths[request]
    slots = keys.shape[0]
    lane = lax.broadcasted_iota(jnp.int32, (rows, LANES), 1)
    row = lax.broadcasted_iota(jnp.int32, (rows, LANES), 0)
    half = lax.rem(lane, HD // 2).astype(jnp.float32)
    frequency = jnp.exp2(half * (-2.0 / HD * math.log2(rope_base)))
    sign = jnp.where(lane < HD // 2, -1.0, 1.0)
    for turn in range(groups):
        first = offsets[request] + length + source_of(position_in, turn, groups) * rows
        angles = (row + first).astype(jnp.float32) * frequency
        part = slice(turn * rows, (turn + 1) * rows)
        cosine[part] = jnp.cos(angles)
        sine[part] = jnp.sin(angles) * sign
    slot = lax.broadcasted_iota(jnp.int32, (slots, LANES), 0) + position_in * slots
    lane = lax.broadcasted_iota(jnp.int32, (slots, LANES), 1)
    bias = jnp.where((lane == 0) & (slot >= length), neg_large, 0.0).astype(jnp.bfloat16)
    ones = jnp.where(lane == 0, 1.0, 0.0).astype(jnp.bfloat16)
    for head in range(keys.shape[1] // HD):
        own = slice(head * HD, (head + 1) * HD)
        wide_keys[head, :, :HD] = keys[:, own]
        wide_keys[head, :, HD:] = bias
        wide_values[head, :, :HD] = values[:, own]
        wide_values[head, :, HD:] = ones


def prepare(lengths, offsets, keys, values, groups, rows):
    table = jax.ShapeDtypeStruct((groups * rows, LANES), jnp.float32)
    slots, width = keys.shape
    wide = jax.ShapeDtypeStruct((width // HD, slots, HD + LANES), jnp.bfloat16)
    return call(
        functools.partial(prepare_kernel, groups, rows),
        [table, table, wide, wide],
        [lengths, offsets],
        [keys, values],
        24,
        40 * groups * rows * LANES,
        0,
        "rope_tables_wide_caches",
    )


def rotate(vectors, cosine, sine):
    return vectors * cosine + pltpu.roll(vectors, HD // 2, 1) * sine


def project_normed(pieces, gain, weights):
    heads = gain.shape[0]
    width = gain.shape[2]
    me = lax.axis_index("head")
    squares = 0.0
    sums = [0.0] * len(weights)
    for index, piece in enumerate(pieces):
        owner = lax.rem(me + (heads - CORES * (index % (heads // CORES))), heads)
        if index >= heads // CORES:
            owner = owner ^ 1
        wide = piece.astype(jnp.float32)
        scaled = (wide * gain[owner]).astype(jnp.bfloat16)
        along = pl.ds(pl.multiple_of(owner * width, LANES), width)
        for place, weight in enumerate(weights):
            sums[place] = sums[place] + dot(scaled, weight[along, :])
        squares = squares + jnp.sum(wide * wide, -1, keepdims=True)
    factor = lax.rsqrt(squares / (heads * width) + 1e-05)
    return [total * factor for total in sums]


def stat_rows(columns, rows):
    lane = lax.broadcasted_iota(jnp.int32, (rows, LANES), 1)
    table = jnp.zeros((rows, LANES), jnp.float32)
    for index, column in enumerate(columns):
        table = jnp.where(lane == index, column, table)
    return table.T[:STAT_ROWS]


def attend_kernel(count, own, row_at, table_at, *refs):
    x_refs = refs[:count]
    gain, w_query, cosine, sine, wide_keys, wide_values = refs[count : count + 6]
    outputs = refs[count + 6 :]
    rows = outputs[0].shape[0] - (0 if own else ROW_TILE)
    pieces = [ref[row_at : row_at + rows] for ref in x_refs]
    (product,) = project_normed(pieces, gain, [w_query])
    cosine = cosine[table_at : table_at + rows]
    sine = sine[table_at : table_at + rows]
    kv_heads = wide_keys.shape[0]
    repeat = product.shape[1] // HD // kv_heads
    lane = lax.broadcasted_iota(jnp.int32, (repeat * rows, LANES), 1)
    mark = jnp.where(lane == 0, 1.0, 0.0).astype(jnp.bfloat16)
    queries = [
        (rotate(product[:, head * HD : (head + 1) * HD], cosine, sine) * log2_scale).astype(
            jnp.bfloat16
        )
        for head in range(kv_heads * repeat)
    ]
    scores = []
    for head in range(kv_heads):
        stacked = jnp.concatenate(queries[head * repeat : (head + 1) * repeat], 0)
        scores.append(dot_transposed(jnp.concatenate([stacked, mark], 1), wide_keys[head]))
    columns = []
    for head in range(kv_heads):
        largest = jnp.max(scores[head], -1, keepdims=True)
        weights = jnp.exp2(scores[head] - largest).astype(jnp.bfloat16)
        summed = dot(weights, wide_values[head])
        denominator = summed[:, HD : HD + 1]
        result = summed[:, :HD] / denominator
        logs = largest + jnp.log2(denominator)
        for turn in range(repeat):
            part = slice(turn * rows, (turn + 1) * rows)
            at = (head * repeat + turn) * HD
            outputs[0][:rows, at : at + HD] = result[part].astype(outputs[0].dtype)
            columns.append(logs[part])
    stats = stat_rows(columns, rows)
    if own:
        outputs[1][...] = stats
        outputs[2][...] = jnp.concatenate(queries, 1)
        return
    tail = jnp.zeros((ROW_TILE, outputs[0].shape[1]), jnp.bfloat16)
    outputs[0][rows:] = tail
    rest = jnp.concatenate([stats, jnp.zeros((ROW_TILE - STAT_ROWS, rows), jnp.float32)], 0)
    for part in range(3):
        rounded = rest.astype(jnp.bfloat16)
        outputs[0][rows:, part * rows : (part + 1) * rows] = rounded
        rest = rest - rounded.astype(jnp.float32)


def attend(pieces, gain, w_query, tables, wide_keys, wide_values, own, rows, row_at, table_at):
    out_width = w_query.shape[1]
    slots = wide_keys.shape[1]
    if own:
        out_shape = [
            jax.ShapeDtypeStruct((rows, out_width), jnp.float32),
            jax.ShapeDtypeStruct((STAT_ROWS, rows), jnp.float32),
            jax.ShapeDtypeStruct((rows, out_width), jnp.bfloat16),
        ]
    else:
        out_shape = [jax.ShapeDtypeStruct((rows + ROW_TILE, out_width), jnp.bfloat16)]
    return call(
        functools.partial(attend_kernel, len(pieces), own, row_at, table_at),
        out_shape,
        [],
        [*pieces, gain, w_query, *tables, wide_keys, wide_values],
        28,
        2 * rows * out_width * (w_query.shape[0] + 4 * slots),
        rows * out_width // HD * slots,
        "attend_own" if own else "attend_partner",
    )


def fresh_kernel(chunks, table_at, *refs):
    x_refs = refs[:-7]
    gain, w_key, w_value, cosine, sine, new_keys, new_values = refs[-7:]
    count = len(x_refs) // chunks
    rows = new_keys.shape[0]
    pieces = [
        jnp.concatenate([x_refs[chunk * count + index][...] for chunk in range(chunks)], 0)
        for index in range(count)
    ]
    keys, values = project_normed(pieces, gain, [w_key, w_value])
    cosine = cosine[table_at : table_at + rows]
    sine = sine[table_at : table_at + rows]
    for head in range(keys.shape[1] // HD):
        own = slice(head * HD, (head + 1) * HD)
        new_keys[:, own] = rotate(keys[:, own], cosine, sine).astype(jnp.bfloat16)
    new_values[...] = values.astype(jnp.bfloat16)


def fresh(chunks, gain, w_key, w_value, tables, table_at):
    rows = sum(pieces[0].shape[0] for pieces in chunks)
    shape = jax.ShapeDtypeStruct((rows, w_key.shape[1]), jnp.bfloat16)
    return call(
        functools.partial(fresh_kernel, len(chunks), table_at),
        [shape, shape],
        [],
        [*(piece for pieces in chunks for piece in pieces), gain, w_key, w_value, *tables],
        20,
        4 * rows * w_key.size,
        0,
        "fresh_kv",
    )


def write_rows(target, fresh_rows, first):
    rows = fresh_rows.shape[0]
    slab_rows = target.shape[0]
    span = rows + ROW_TILE
    start = jnp.clip(first, 0, slab_rows - span)
    start = start - lax.rem(start, ROW_TILE)
    window = pl.ds(pl.multiple_of(start, ROW_TILE), span)
    shift = start - first
    place = lax.broadcasted_iota(jnp.int32, (span, rows), 0) + shift
    chosen = place == lax.broadcasted_iota(jnp.int32, (span, rows), 1)
    moved = dot(chosen.astype(jnp.bfloat16), fresh_rows)
    row = lax.broadcasted_iota(jnp.int32, (span, target.shape[1]), 0) + shift
    inside = (row >= 0) & (row < rows)
    old = target[window, :].astype(jnp.float32)
    target[window, :] = jnp.where(inside, moved, old).astype(jnp.bfloat16)


def update_kernel(groups, chunks, kv_heads, lengths, *refs):
    query_refs = refs[:chunks]
    key_refs = refs[chunks : chunks + groups]
    value_refs = refs[chunks + groups : chunks + 2 * groups]
    keys, values, partial, stats, keys_updated, values_updated = refs[chunks + 2 * groups :]
    request, position_in = place_of(lengths.shape[0])
    sources = [source_of(position_in, turn, groups) for turn in range(groups)]
    rows, width = partial.shape
    repeat = width // HD // kv_heads
    queries = jnp.concatenate([ref[...] for ref in query_refs], 0)
    fresh_keys = jnp.concatenate([ref[...] for ref in key_refs], 0)
    fresh_values = jnp.concatenate([ref[...] for ref in value_refs], 0)
    token = lax.broadcasted_iota(jnp.int32, (rows, rows), 0)
    within = lax.broadcasted_iota(jnp.int32, (rows, rows), 1)
    visible = jnp.concatenate(
        [within + source * rows <= token + position_in * rows for source in sources], 1
    )
    columns = []
    for head in range(kv_heads * repeat):
        own = slice(head * HD, (head + 1) * HD)
        shared = slice(head // repeat * HD, (head // repeat + 1) * HD)
        scores = jnp.where(
            visible, dot_transposed(queries[:, own], fresh_keys[:, shared]), neg_large
        )
        largest = jnp.max(scores, -1, keepdims=True)
        weights = jnp.exp2(scores - largest)
        denominator = jnp.sum(weights, -1, keepdims=True)
        summed = dot(weights.astype(jnp.bfloat16), fresh_values[:, shared])
        partial[:, own] = summed / denominator
        columns.append(largest + jnp.log2(denominator))
    stats[...] = stat_rows(columns, rows)
    keys_updated[...] = keys[...]
    values_updated[...] = values[...]
    for turn in range(groups):
        first = lengths[request] + sources[turn] * rows - position_in * keys.shape[0]
        write_rows(keys_updated, key_refs[turn][...], first)
        write_rows(values_updated, value_refs[turn][...], first)


def update(lengths, queries, new_keys, new_values, keys, values):
    rows = sum(query.shape[0] for query in queries)
    width = queries[0].shape[1]
    groups = len(new_keys)
    slab = jax.ShapeDtypeStruct(keys.shape, keys.dtype)
    return call(
        functools.partial(update_kernel, groups, len(queries), keys.shape[1] // HD),
        [
            jax.ShapeDtypeStruct((rows, width), jnp.float32),
            jax.ShapeDtypeStruct((STAT_ROWS, rows), jnp.float32),
            slab,
            slab,
        ],
        [lengths],
        [*queries, *new_keys, *new_values, keys, values],
        28,
        4 * rows * width * rows * groups,
        rows * width // HD * rows * groups,
        "fresh_attend_update",
    )


def project_kernel(row_at, own_partial, own_stats, fresh_partial, fresh_stats, *refs):
    received = refs[:-3]
    w_out, near, far = refs[-3:]
    rows, width = own_partial.shape
    chips, _, block_width = near.shape
    heads = 2 * chips
    part = slice(row_at, row_at + rows)
    padding = jnp.zeros((LANES - STAT_ROWS, rows), jnp.float32)
    stats = [own_stats[...], fresh_stats[:, part]]
    for ref in received:
        stats.append(
            sum(
                ref[rows:, turn * rows : (turn + 1) * rows].astype(jnp.float32)
                for turn in range(3)
            )[:STAT_ROWS]
        )
    logs = [jnp.concatenate([stat, padding], 0).T for stat in stats]
    largest = functools.reduce(jnp.maximum, logs)
    shares = [jnp.exp2(log - largest) for log in logs]
    total = functools.reduce(jnp.add, shares)
    shares = [share / total for share in shares]
    attended = []
    for head in range(width // HD):
        own = slice(head * HD, (head + 1) * HD)
        column = slice(head, head + 1)
        merged = own_partial[:, own] * shares[0][:, column]
        merged = merged + fresh_partial[part, own] * shares[1][:, column]
        for ref, share in zip(received, shares[2:]):
            merged = merged + ref[:rows, own].astype(jnp.float32) * share[:, column]
        attended.append(merged.astype(jnp.bfloat16))
    attended = jnp.concatenate(attended, 1)
    me = lax.axis_index("head")
    for target, flip in ((far, 1), (near, 0)):
        for ahead in range(chips):
            block = lax.rem(me + CORES * ahead, heads) ^ flip
            along = pl.ds(pl.multiple_of(block * block_width, LANES), block_width)
            target[ahead] = dot(attended, w_out[:, along]).astype(target.dtype)


def project(row_at, own, fresh_part, received, w_out, chips):
    rows = own[0].shape[0]
    shape = jax.ShapeDtypeStruct((chips, rows, w_out.shape[1] // (2 * chips)), jnp.bfloat16)
    return call(
        functools.partial(project_kernel, row_at),
        [shape, shape],
        [],
        [*own, *fresh_part, *received, w_out],
        20,
        2 * rows * w_out.size,
        0,
        "combine_project",
    )


def shards(
    tokens,
    norm_gain,
    w_query,
    w_key,
    w_value,
    w_out,
    keys_cache,
    values_cache,
    cached_lengths,
    rope_offsets,
):
    rows, width = tokens.shape
    requests = cached_lengths.shape[0]
    groups = lax.axis_size("seq") // requests
    heads = lax.axis_size("head")
    chips = heads // CORES
    chunk_rows = rows // CHUNKS
    gain = norm_gain.reshape(heads, 1, width)

    arrived = [
        [
            shifted(tokens[at : at + chunk_rows], "seq", turn * requests)
            for at in range(0, rows, chunk_rows)
        ]
        for turn in range(1, groups)
    ]
    *tables, wide_keys, wide_values = prepare(
        cached_lengths, rope_offsets, keys_cache, values_cache, groups, rows
    )

    def attend_chunk(pieces, own, chunk, turn):
        return attend(
            pieces, gain, w_query, tables, wide_keys, wide_values, own, chunk_rows,
            chunk * chunk_rows if own else 0, turn * rows + chunk * chunk_rows,
        )

    own_pieces = all_features(tokens)
    own_parts = [attend_chunk(own_pieces, True, chunk, 0) for chunk in range(CHUNKS)]
    new_rows = [fresh([own_pieces], gain, w_key, w_value, tables, 0)]
    received = [[] for _ in range(CHUNKS)]
    for turn in range(1, groups):
        chunks = [all_features(piece) for piece in arrived[turn - 1]]
        for chunk in range(CHUNKS):
            (packed,) = attend_chunk(chunks[chunk], False, chunk, turn)
            received[chunk].append(shifted(packed, "seq", -turn * requests))
        new_rows.append(fresh(chunks, gain, w_key, w_value, tables, turn * rows))
    *fresh_part, keys_updated, values_updated = update(
        cached_lengths, [part[2] for part in own_parts], [k for k, _ in new_rows],
        [v for _, v in new_rows], keys_cache, values_cache,
    )
    outputs = []
    for chunk in range(CHUNKS):
        near, far = project(
            chunk * chunk_rows, own_parts[chunk][:2], fresh_part, received[chunk], w_out, chips
        )
        summed = near.astype(jnp.float32) + other_core(far).astype(jnp.float32)
        total = summed[0]
        for ahead in range(1, chips):
            piece = shifted(summed[ahead].astype(jnp.bfloat16), "head", CORES * ahead)
            total = total + piece.astype(jnp.float32)
        outputs.append(total.astype(jnp.bfloat16))
    return (jnp.concatenate(outputs, 0), keys_updated, values_updated)


def solution(mesh):
    return jax.shard_map(
        shards,
        mesh=mesh,
        in_specs=(
            P("seq", "head"),
            P(),
            P(None, "head"),
            P(None, "head"),
            P(None, "head"),
            P("head", None),
            P("seq", "head"),
            P("seq", "head"),
            P(),
            P(),
        ),
        out_specs=(P("seq", "head"), P("seq", "head"), P("seq", "head")),
        check_vma=False,
    )
```

time: 88.8 us -> 85.9 us (0.967)
  Pallas kernels: 33.8 us -> 24.9 us
  starting transfers between devices: 12.2 us -> 18 us
  other arithmetic: 6.67 us -> 1.01 us
  local copies, waits for them, and re-layouts: 2.71 us -> 7.24 us
  waiting for transfers between devices: 30.1 us -> 33.7 us
  between operations: 2.99 us -> 0.87 us
    pallas_call x6 -> x10, Pallas kernels: 33.8 us -> 24.9 us  [call(): pl.pallas_call(kernel, out_shape=out_shape, in_specs=[SMEM] * len(scalars...]
    unnamed x22 -> x32, local copies, waits for them, and re-layouts: 0.06 us -> 6.14 us
    ppermute x6 -> x9, waiting for transfers between devices: 27.8 us -> 33.6 us  [shifted(): lax.ppermute(shard, axis, [(i, (i + by) % devices) for i in range(devices)])]
    ppermute x6 -> x9, starting transfers between devices: 11.5 us -> 16.3 us  [shifted(): lax.ppermute(shard, axis, [(i, (i + by) % devices) for i in range(devices)])]
    dynamic_slice x2 -> x0, local copies, waits for them, and re-layouts: 2.56 us -> none  [the longest x1 1.32 us: shards(): length = lax.dynamic_index_in_dim(cached_lengths, request, 0, False)]
    ppermute x5 -> x8, waiting for transfers between devices: 2.28 us -> 0.02 us  [other_core(): return lax.ppermute(shard, 'head', [(i, i ^ 1) for i in range(devices)])]
    neg x1 -> x0, other arithmetic: 1.84 us -> none  [rope_tables(): -sine]
    concatenate x2 -> x1, other arithmetic: 2.46 us -> 0.77 us  [shards(): return (jnp.concatenate(outputs, 0), keys_updated, values_updated)]
  transfers between devices with their start and end apart: 11 -> 17, of which waited for: 4 -> 6; matrix products, arithmetic and copies ran while one was open for 9% -> 0% of each run, Pallas kernels for 35% -> 27%
where the time goes in v2:
time: 85.9 us; the launch traced here: 85.6 us
  waiting for transfers between devices  33.7 us (39%)
  Pallas kernels  24.9 us (29%)
  starting transfers between devices  18 us (21%)
  local copies, waits for them, and re-layouts  7.24 us (8%)
  other arithmetic  1.01 us (1%)
  between operations  0.87 us (1%)
    ppermute x9, waiting for transfers between devices, shifted(): lax.ppermute(shard, axis, [(i, (i + by) % devices) for i in range(devices)])  33.6 us
    pallas_call x10, Pallas kernels, call(): pl.pallas_call(kernel, out_shape=out_shape, in_specs=[SMEM] * len(scalars...  24.9 us
    ppermute x9, starting transfers between devices, shifted(): lax.ppermute(shard, axis, [(i, (i + by) % devices) for i in range(devices)])  16.3 us
    unnamed x32, local copies, waits for them, and re-layouts  6.14 us
    ppermute x8, starting transfers between devices, other_core(): return lax.ppermute(shard, 'head', [(i, i ^ 1) for i in range(devices)])  1.72 us
  transfers between devices with their start and end apart: 17, of which 6 were waited for; matrix products, arithmetic and copies ran while one was open for 0% of the time, Pallas kernels for 27%

profile of v2, /device:TPU:0, one launch (start us, length us, event | category | flops | bytes accessed | tf_op | source)
XLA Modules:
  0.0 85.6 jit_solution(6439766630861435701)
XLA Ops:
  0.6 1.1 %fusion.6 = (bf16[128,768]{1,0:T(8,128)(2,1)S(1)}, bf16[128,768]{1,0:T(8,128)(2,1)S(1)}) fusion(bf16[256,768]{1,0:T(8,128)(2,1)} %refs_0_.5), kind=kLoop, calls=%fused_computation.13 | loop fusion | bytes 786432 | tf_op jit(solution)/shard_map/slice | solution.py:413
  1.7 4.1 %collective-permute-start.7 = (bf16[128,768]{1,0:T(8,128)(2,1)S(1)}, bf16[128,768]{1,0:T(8,128)(2,1)S(1)}, u32[]{:S(2)}, u32[]{:S(2)}) collective-permute-start(bf16[128,768]{1,0:T(8,128)(2,1)S(1)} %get-tuple-element.47), channel_id=1, source_target_pairs={{0,16},{4,20},{8,24},{12,28},{16,0},{20,4},{24,8},{28,12},{1,17},{... | collective-permute-start | bytes 589832 | tf_op jit(solution)/shard_map/ppermute | solution.py:29
  5.8 1.5 %collective-permute-start = (bf16[256,768]{1,0:T(8,128)(2,1)}, bf16[256,768]{1,0:T(8,128)(2,1)S(1)}, u32[]{:S(2)}, u32[]{:S(2)}) collective-permute-start(bf16[256,768]{1,0:T(8,128)(2,1)} %refs_0_.5), channel_id=1, source_target_pairs={{0,2},{1,3},{2,0},{3,1},{4,6},{5,7},{6,4},{7,5},{8,10},{9,11},{10,... | collective-permute-start | bytes 1179656 | tf_op jit(solution)/shard_map/ppermute | solution.py:29
  7.3 0.3 collective-permute-start.3
  7.7 12.3 %collective-permute-done.7.refs_4_.refs_0_ = bf16[128,768]{1,0:T(8,128)(2,1)S(1)} collective-permute-done((bf16[128,768]{1,0:T(8,128)(2,1)S(1)}, bf16[128,768]{1,0:T(8,128)(2,1)S(1)}, u32[]{:S(2)}, u32[]{:S(2)}) %collective-permute-start.7) | collective-permute-done | bytes 196640 | tf_op jit(solution)/shard_map/ppermute | solution.py:29
  20.0 1.9 %collective-permute-start.8 = (bf16[128,768]{1,0:T(8,128)(2,1)S(1)}, bf16[128,768]{1,0:T(8,128)(2,1)S(1)}, u32[]{:S(2)}, u32[]{:S(2)}) collective-permute-start(bf16[128,768]{1,0:T(8,128)(2,1)S(1)} %collective-permute-done.7.refs_4_.refs_0_), channel_id=1, source_target_pairs={{0,2},{1,3},{2,0},{3,1},{4,6},{5,7},{6,4},{7,5},{8,10},{9,11},{10,... | collective-permute-start | bytes 589832 | tf_op jit(solution)/shard_map/ppermute | solution.py:29
  21.8 0.0 collective-permute-start.9
  21.8 1.5 %collective-permute-done.3.refs_0_ = bf16[128,768]{1,0:T(8,128)(2,1)S(1)} collective-permute-done((bf16[128,768]{1,0:T(8,128)(2,1)S(1)}, bf16[128,768]{1,0:T(8,128)(2,1)S(1)}, u32[]{:S(2)}, u32[]{:S(2)}) %collective-permute-start.3) | collective-permute-done | bytes 196640 | tf_op jit(solution)/shard_map/ppermute | solution.py:29
  23.3 1.6 %collective-permute-start.4 = (bf16[128,768]{1,0:T(8,128)(2,1)S(1)}, bf16[128,768]{1,0:T(8,128)(2,1)S(1)}, u32[]{:S(2)}, u32[]{:S(2)}) collective-permute-start(bf16[128,768]{1,0:T(8,128)(2,1)S(1)} %collective-permute-done.3.refs_0_), channel_id=1, source_target_pairs={{0,2},{1,3},{2,0},{3,1},{4,6},{5,7},{6,4},{7,5},{8,10},{9,11},{10,... | collective-permute-start | bytes 589832 | tf_op jit(solution)/shard_map/ppermute | solution.py:29
  24.9 1.1 %collective-permute-done.8.refs_5_.refs_1_ = bf16[128,768]{1,0:T(8,128)(2,1)S(1)} collective-permute-done((bf16[128,768]{1,0:T(8,128)(2,1)S(1)}, bf16[128,768]{1,0:T(8,128)(2,1)S(1)}, u32[]{:S(2)}, u32[]{:S(2)}) %collective-permute-start.8) | collective-permute-done | bytes 196640 | tf_op jit(solution)/shard_map/ppermute | solution.py:29
  26.0 0.5 collective-permute-start.1
  26.5 0.0 collective-permute-done.refs_1_
  26.5 0.0 collective-permute-start.2
  26.5 1.2 %copy-done.4 = bf16[2048,256]{1,0:T(8,128)(2,1)S(1)} copy-done((bf16[2048,256]{1,0:T(8,128)(2,1)S(1)}, bf16[2048,256]{1,0:T(8,128)(2,1)}, u32[]{:S(2)}) %copy-start.4) | copy-done | bytes 1048600
  27.7 1.2 %copy-done.6 = bf16[2048,256]{1,0:T(8,128)(2,1)S(1)} copy-done((bf16[2048,256]{1,0:T(8,128)(2,1)S(1)}, bf16[2048,256]{1,0:T(8,128)(2,1)}, u32[]{:S(2)}) %copy-start.6) | copy-done | bytes 1048600
  29.0 0.7 copy-done.9
  29.6 0.7 copy-done.11
  30.3 2.2 %rope_tables_wide_caches.1 = (f32[512,128]{1,0:T(8,128)S(1)}, f32[512,128]{1,0:T(8,128)S(1)}, bf16[2,2048,256]{2,1,0:T(8,128)(2,1)S(1)}, bf16[2,2048,256]{2,1,0:T(8,128)(2,1)S(1)}) custom-call(s32[4]{0:T(128)S(1)} %copy-done.9, s32[4]{0:T(128)S(1)} %copy-done.11, bf16[2048,256]{1,0:T(8,128)(2,1)S(1)} %copy-done.4, bf16[2048,256]{1,0:T(8,128)(2,1)S(1)} %copy-done.6), custom_call_target="tpu_custom_call" | custom-call | flops 2621440 | bytes 6815744 | tf_op jit(solution)/shard_map/rope_tables_wide_caches/pallas_call | solution.py:65
  32.5 0.0 collective-permute-done.9.refs_6_.refs_2_
  32.5 0.6 collective-permute-start.5
  33.1 0.1 collective-permute-start.6
  33.1 0.0 collective-permute-done.10.refs_7_.refs_3_
  33.2 2.3 %copy-done = bf16[3072,768]{1,0:T(8,128)(2,1)S(1)} copy-done((bf16[3072,768]{1,0:T(8,128)(2,1)S(1)}, bf16[3072,768]{1,0:T(8,128)(2,1)}, u32[]{:S(2)}) %copy-start) | copy-done | bytes 4718616
  35.5 3.4 %attend_partner.3 = bf16[144,768]{1,0:T(8,128)(2,1)S(1)} custom-call(bf16[128,768]{1,0:T(8,128)(2,1)S(1)} %collective-permute-done.7.refs_4_.refs_0_, bf16[128,768]{1,0:T(8,128)(2,1)S(1)} %collective-permute-done.8.refs_5_.refs_1_, bf16[128,768]{1,0:T(8,128)(2,1)S(1)} %collective-permute-done.9.refs_6_.refs_2_, ...), custom_call_target="tpu_custom_call" | custom-call | flops 2214592512 | bytes 10457088 | tf_op jit(solution)/shard_map/attend_partner/pallas_call | solution.py:65
  38.9 0.1 collective-permute-start.14
  38.9 0.0 collective-permute-done.5.refs_2_
  39.0 1.1 %fresh_kv.3 = (bf16[256,256]{1,0:T(8,128)(2,1)S(1)}, bf16[256,256]{1,0:T(8,128)(2,1)S(1)}) custom-call(bf16[128,768]{1,0:T(8,128)(2,1)S(1)} %collective-permute-done.3.refs_0_, bf16[128,768]{1,0:T(8,128)(2,1)S(1)} %collective-permute-done.4.refs_1_, bf16[128,768]{1,0:T(8,128)(2,1)S(1)} %collective-permute-done.5.refs_2_, ...), custom_call_target="tpu_custom_call" | custom-call | flops 805306368 | bytes 5517312 | tf_op jit(solution)/shard_map/fresh_kv/pallas_call | solution.py:65
  40.1 1.1 %fresh_kv.2 = (bf16[256,256]{1,0:T(8,128)(2,1)S(1)}, bf16[256,256]{1,0:T(8,128)(2,1)S(1)}) custom-call(bf16[256,768]{1,0:T(8,128)(2,1)S(1)} %copy-done.1, bf16[256,768]{1,0:T(8,128)(2,1)S(1)} %collective-permute-done.refs_1_, bf16[256,768]{1,0:T(8,128)(2,1)S(1)} %collective-permute-done.1.refs_2_, bf16[256,768]{1,0:T(8,128)(2,1)S(1)} %collective-permute-done.2.refs_3_, ...), custom_call_target="tpu_custom_call" | custom-call | flops 805306368 | bytes 5517312 | tf_op jit(solution)/shard_map/fresh_kv/pallas_call | solution.py:65
  41.2 0.0 slice-start.2
  41.3 3.3 %attend_own.3 = (f32[128,768]{1,0:T(8,128)S(1)}, f32[8,128]{1,0:T(8,128)S(1)}, bf16[128,768]{1,0:T(8,128)(2,1)S(1)}) custom-call(bf16[256,768]{1,0:T(8,128)(2,1)S(1)} %copy-done.1, bf16[256,768]{1,0:T(8,128)(2,1)S(1)} %collective-permute-done.refs_1_, bf16[256,768]{1,0:T(8,128)(2,1)S(1)} %collective-permute-done.1.refs_2_, ...), custom_call_target="tpu_custom_call" | custom-call | flops 2214592512 | bytes 11616256 | tf_op jit(solution)/shard_map/attend_own/pallas_call | solution.py:65
  44.6 0.0 slice-start.3
  44.6 3.5 %attend_own.2 = (f32[128,768]{1,0:T(8,128)S(1)}, f32[8,128]{1,0:T(8,128)S(1)}, bf16[128,768]{1,0:T(8,128)(2,1)S(1)}) custom-call(bf16[256,768]{1,0:T(8,128)(2,1)S(1)} %copy-done.1, bf16[256,768]{1,0:T(8,128)(2,1)S(1)} %collective-permute-done.refs_1_, bf16[256,768]{1,0:T(8,128)(2,1)S(1)} %collective-permute-done.1.refs_2_, ...), custom_call_target="tpu_custom_call" | custom-call | flops 2214592512 | bytes 11616256 | tf_op jit(solution)/shard_map/attend_own/pallas_call | solution.py:65
  48.1 4.2 %fresh_attend_update.1 = (f32[256,768]{1,0:T(8,128)S(1)}, f32[8,256]{1,0:T(8,128)S(1)}, bf16[2048,256]{1,0:T(8,128)(2,1)}, bf16[2048,256]{1,0:T(8,128)(2,1)}) custom-call(s32[4]{0:T(128)S(1)} %copy-done.10, bf16[128,768]{1,0:T(8,128)(2,1)S(1)} %get-tuple-element.31.refs_0_, bf16[128,768]{1,0:T(8,128)(2,1)S(1)} %get-tuple-element.32.refs_1_, ...), custom_call_target="tpu_custom_call" | custom-call | flops 402653184 | bytes 5906432 | tf_op jit(solution)/shard_map/fresh_attend_update/pallas_call | solution.py:65
  52.3 0.0 collective-permute-done.14.refs_0_
  52.3 1.4 %combine_project.3 = (bf16[2,128,768]{2,1,0:T(8,128)(2,1)S(1)}, bf16[2,128,768]{2,1,0:T(8,128)(2,1)S(1)}) custom-call(f32[128,768]{1,0:T(8,128)S(1)} %get-tuple-element.41.own_partial, f32[8,128]{1,0:T(8,128)S(1)} %get-tuple-element.42.own_stats, f32[256,768]{1,0:T(8,128)S(1)} %get-tuple-element.37.fresh_partial, ...), custom_call_target="tpu_custom_call" | custom-call | flops 603979776 | bytes 6918144 | tf_op jit(solution)/shard_map/combine_project/pallas_call | solution.py:65
  53.8 0.5 collective-permute-start.15
  54.2 3.3 %attend_partner.2 = bf16[144,768]{1,0:T(8,128)(2,1)S(1)} custom-call(bf16[128,768]{1,0:T(8,128)(2,1)S(1)} %collective-permute-done.3.refs_0_, bf16[128,768]{1,0:T(8,128)(2,1)S(1)} %collective-permute-done.4.refs_1_, bf16[128,768]{1,0:T(8,128)(2,1)S(1)} %collective-permute-done.5.refs_2_, bf16[128,768]{1,0:T(8,128)(2,1)S(1)} %collective-permute-done.6.refs_3_, ...), custom_call_target="tpu_custom_call" | custom-call | flops 2214592512 | bytes 10457088 | tf_op jit(solution)/shard_map/attend_partner/pallas_call | solution.py:65
  57.5 2.7 %collective-permute-start.11 = (bf16[144,768]{1,0:T(8,128)(2,1)S(1)}, bf16[144,768]{1,0:T(8,128)(2,1)S(1)}, u32[]{:S(2)}, u32[]{:S(2)}) collective-permute-start(bf16[144,768]{1,0:T(8,128)(2,1)S(1)} %attend_partner.2), channel_id=1, source_target_pairs={{0,16},{4,20},{8,24},{12,28},{16,0},{20,4},{24,8},{28,12},{1,17},{... | collective-permute-start | bytes 663560 | tf_op jit(solution)/shard_map/ppermute | solution.py:29
  60.2 10.7 %collective-permute-done.11.refs_0_ = bf16[144,768]{1,0:T(8,128)(2,1)S(1)} collective-permute-done((bf16[144,768]{1,0:T(8,128)(2,1)S(1)}, bf16[144,768]{1,0:T(8,128)(2,1)S(1)}, u32[]{:S(2)}, u32[]{:S(2)}) %collective-permute-start.11) | collective-permute-done | bytes 221216 | tf_op jit(solution)/shard_map/ppermute | solution.py:29
  70.9 1.4 %combine_project.2 = (bf16[2,128,768]{2,1,0:T(8,128)(2,1)S(1)}, bf16[2,128,768]{2,1,0:T(8,128)(2,1)S(1)}) custom-call(f32[128,768]{1,0:T(8,128)S(1)} %get-tuple-element.29.own_partial, f32[8,128]{1,0:T(8,128)S(1)} %get-tuple-element.30.own_stats, f32[256,768]{1,0:T(8,128)S(1)} %get-tuple-element.37.fresh_partial, ...), custom_call_target="tpu_custom_call" | custom-call | flops 603979776 | bytes 6918144 | tf_op jit(solution)/shard_map/combine_project/pallas_call | solution.py:65
  72.3 0.1 collective-permute-start.12
  72.4 0.1 convert_add_fusion
  72.5 2.5 %collective-permute-start.16 = (bf16[128,768]{1,0:T(8,128)(2,1)S(1)}, bf16[128,768]{1,0:T(8,128)(2,1)S(1)}, u32[]{:S(2)}, u32[]{:S(2)}) collective-permute-start(bf16[128,768]{1,0:T(8,128)(2,1)S(1)} %fusion.5), channel_id=1, source_target_pairs={{0,2},{1,3},{2,0},{3,1},{4,6},{5,7},{6,4},{7,5},{8,10},{9,11},{10,... | collective-permute-start | bytes 589832 | tf_op jit(solution)/shard_map/ppermute | solution.py:29
  75.1 0.1 convert_add_fusion.1
  75.2 1.6 %collective-permute-start.13 = (bf16[128,768]{1,0:T(8,128)(2,1)S(1)}, bf16[128,768]{1,0:T(8,128)(2,1)S(1)}, u32[]{:S(2)}, u32[]{:S(2)}) collective-permute-start(bf16[128,768]{1,0:T(8,128)(2,1)S(1)} %fusion.4), channel_id=1, source_target_pairs={{0,2},{1,3},{2,0},{3,1},{4,6},{5,7},{6,4},{7,5},{8,10},{9,11},{10,... | collective-permute-start | bytes 589832 | tf_op jit(solution)/shard_map/ppermute | solution.py:29
  76.8 4.1 %collective-permute-done.16 = bf16[128,768]{1,0:T(8,128)(2,1)S(1)} collective-permute-done((bf16[128,768]{1,0:T(8,128)(2,1)S(1)}, bf16[128,768]{1,0:T(8,128)(2,1)S(1)}, u32[]{:S(2)}, u32[]{:S(2)}) %collective-permute-start.16) | collective-permute-done | bytes 196640 | tf_op jit(solution)/shard_map/ppermute | solution.py:29
  80.8 4.0 %collective-permute-done.13 = bf16[128,768]{1,0:T(8,128)(2,1)S(1)} collective-permute-done((bf16[128,768]{1,0:T(8,128)(2,1)S(1)}, bf16[128,768]{1,0:T(8,128)(2,1)S(1)}, u32[]{:S(2)}, u32[]{:S(2)}) %collective-permute-start.13) | collective-permute-done | bytes 196640 | tf_op jit(solution)/shard_map/ppermute | solution.py:29
  84.9 0.8 pad_maximum_fusion
  (38 shorter events, 0.2 us)
Async XLA Ops:
  0.6 32.5 %copy-start.8 = (f32[3072]{0:T(1024)S(1)}, f32[3072]{0:T(1024)}, u32[]{:S(2)}) copy-start(f32[3072]{0:T(1024)} %param.11) | copy-start | bytes 36868
  1.7 18.3 %collective-permute-start.7 = (bf16[128,768]{1,0:T(8,128)(2,1)S(1)}, bf16[128,768]{1,0:T(8,128)(2,1)S(1)}, u32[]{:S(2)}, u32[]{:S(2)}) collective-permute-start(bf16[128,768]{1,0:T(8,128)(2,1)S(1)} %get-tuple-element.47), channel_id=1, source_target_pairs={{0,16},{4,20},{8,24},{12,28},{16,0},{20,4},{24,8},{28,12},{1,17},{... | collective-permute-start | bytes 589832 | tf_op jit(solution)/shard_map/ppermute | solution.py:29
  5.8 20.7 %collective-permute-start = (bf16[256,768]{1,0:T(8,128)(2,1)}, bf16[256,768]{1,0:T(8,128)(2,1)S(1)}, u32[]{:S(2)}, u32[]{:S(2)}) collective-permute-start(bf16[256,768]{1,0:T(8,128)(2,1)} %refs_0_.5), channel_id=1, source_target_pairs={{0,2},{1,3},{2,0},{3,1},{4,6},{5,7},{6,4},{7,5},{8,10},{9,11},{10,... | collective-permute-start | bytes 1179656 | tf_op jit(solution)/shard_map/ppermute | solution.py:29
  7.3 16.0 %collective-permute-start.3 = (bf16[128,768]{1,0:T(8,128)(2,1)S(1)}, bf16[128,768]{1,0:T(8,128)(2,1)S(1)}, u32[]{:S(2)}, u32[]{:S(2)}) collective-permute-start(bf16[128,768]{1,0:T(8,128)(2,1)S(1)} %get-tuple-element.48), channel_id=1, source_target_pairs={{0,16},{4,20},{8,24},{12,28},{16,0},{20,4},{24,8},{28,12},{1,17},{... | collective-permute-start | bytes 589832 | tf_op jit(solution)/shard_map/ppermute | solution.py:29
  20.0 6.0 %collective-permute-start.8 = (bf16[128,768]{1,0:T(8,128)(2,1)S(1)}, bf16[128,768]{1,0:T(8,128)(2,1)S(1)}, u32[]{:S(2)}, u32[]{:S(2)}) collective-permute-start(bf16[128,768]{1,0:T(8,128)(2,1)S(1)} %collective-permute-done.7.refs_4_.refs_0_), channel_id=1, source_target_pairs={{0,2},{1,3},{2,0},{3,1},{4,6},{5,7},{6,4},{7,5},{8,10},{9,11},{10,... | collective-permute-start | bytes 589832 | tf_op jit(solution)/shard_map/ppermute | solution.py:29
  21.8 10.7 %collective-permute-start.9 = (bf16[128,768]{1,0:T(8,128)(2,1)S(1)}, bf16[128,768]{1,0:T(8,128)(2,1)S(1)}, u32[]{:S(2)}, u32[]{:S(2)}) collective-permute-start(bf16[128,768]{1,0:T(8,128)(2,1)S(1)} %collective-permute-done.7.refs_4_.refs_0_), channel_id=1, source_target_pairs={{0,1},{1,0},{2,3},{3,2},{4,5},{5,4},{6,7},{7,6},{8,9},{9,8},{10,11... | collective-permute-start | bytes 589832 | tf_op jit(solution)/shard_map/ppermute | solution.py:34
  23.3 9.7 %collective-permute-start.4 = (bf16[128,768]{1,0:T(8,128)(2,1)S(1)}, bf16[128,768]{1,0:T(8,128)(2,1)S(1)}, u32[]{:S(2)}, u32[]{:S(2)}) collective-permute-start(bf16[128,768]{1,0:T(8,128)(2,1)S(1)} %collective-permute-done.3.refs_0_), channel_id=1, source_target_pairs={{0,2},{1,3},{2,0},{3,1},{4,6},{5,7},{6,4},{7,5},{8,10},{9,11},{10,... | collective-permute-start | bytes 589832 | tf_op jit(solution)/shard_map/ppermute | solution.py:29
  26.0 7.2 %collective-permute-start.10 = (bf16[128,768]{1,0:T(8,128)(2,1)S(1)}, bf16[128,768]{1,0:T(8,128)(2,1)S(1)}, u32[]{:S(2)}, u32[]{:S(2)}) collective-permute-start(bf16[128,768]{1,0:T(8,128)(2,1)S(1)} %collective-permute-done.8.refs_5_.refs_1_), channel_id=1, source_target_pairs={{0,1},{1,0},{2,3},{3,2},{4,5},{5,4},{6,7},{7,6},{8,9},{9,8},{10,11... | collective-permute-start | bytes 589832 | tf_op jit(solution)/shard_map/ppermute | solution.py:34
  26.0 14.1 %collective-permute-start.1 = (bf16[256,768]{1,0:T(8,128)(2,1)}, bf16[256,768]{1,0:T(8,128)(2,1)S(1)}, u32[]{:S(2)}, u32[]{:S(2)}) collective-permute-start(bf16[256,768]{1,0:T(8,128)(2,1)} %refs_0_.5), channel_id=1, source_target_pairs={{0,1},{1,0},{2,3},{3,2},{4,5},{5,4},{6,7},{7,6},{8,9},{9,8},{10,11... | collective-permute-start | bytes 1179656 | tf_op jit(solution)/shard_map/ppermute | solution.py:34
  26.5 13.6 %collective-permute-start.2 = (bf16[256,768]{1,0:T(8,128)(2,1)S(1)}, bf16[256,768]{1,0:T(8,128)(2,1)S(1)}, u32[]{:S(2)}, u32[]{:S(2)}) collective-permute-start(bf16[256,768]{1,0:T(8,128)(2,1)S(1)} %collective-permute-done.refs_1_), channel_id=1, source_target_pairs={{0,1},{1,0},{2,3},{3,2},{4,5},{5,4},{6,7},{7,6},{8,9},{9,8},{10,11... | collective-permute-start | bytes 1179656 | tf_op jit(solution)/shard_map/ppermute | solution.py:34
  26.5 1.2 %copy-start.4 = (bf16[2048,256]{1,0:T(8,128)(2,1)S(1)}, bf16[2048,256]{1,0:T(8,128)(2,1)}, u32[]{:S(2)}) copy-start(bf16[2048,256]{1,0:T(8,128)(2,1)} %refs_6_.3) | copy-start | bytes 3145732
  27.7 1.2 %copy-start.6 = (bf16[2048,256]{1,0:T(8,128)(2,1)S(1)}, bf16[2048,256]{1,0:T(8,128)(2,1)}, u32[]{:S(2)}) copy-start(bf16[2048,256]{1,0:T(8,128)(2,1)} %refs_7_.1) | copy-start | bytes 3145732
  29.0 0.7 copy-start.9
  29.6 0.7 copy-start.11
  32.5 6.4 %collective-permute-start.5 = (bf16[128,768]{1,0:T(8,128)(2,1)S(1)}, bf16[128,768]{1,0:T(8,128)(2,1)S(1)}, u32[]{:S(2)}, u32[]{:S(2)}) collective-permute-start(bf16[128,768]{1,0:T(8,128)(2,1)S(1)} %collective-permute-done.3.refs_0_), channel_id=1, source_target_pairs={{0,1},{1,0},{2,3},{3,2},{4,5},{5,4},{6,7},{7,6},{8,9},{9,8},{10,11... | collective-permute-start | bytes 589832 | tf_op jit(solution)/shard_map/ppermute | solution.py:34
  33.1 5.9 %collective-permute-start.6 = (bf16[128,768]{1,0:T(8,128)(2,1)S(1)}, bf16[128,768]{1,0:T(8,128)(2,1)S(1)}, u32[]{:S(2)}, u32[]{:S(2)}) collective-permute-start(bf16[128,768]{1,0:T(8,128)(2,1)S(1)} %collective-permute-done.4.refs_1_), channel_id=1, source_target_pairs={{0,1},{1,0},{2,3},{3,2},{4,5},{5,4},{6,7},{7,6},{8,9},{9,8},{10,11... | collective-permute-start | bytes 589832 | tf_op jit(solution)/shard_map/ppermute | solution.py:34
  33.2 2.3 %copy-start = (bf16[3072,768]{1,0:T(8,128)(2,1)S(1)}, bf16[3072,768]{1,0:T(8,128)(2,1)}, u32[]{:S(2)}) copy-start(bf16[3072,768]{1,0:T(8,128)(2,1)} %refs_5_.9) | copy-start | bytes 14155780
  35.5 3.5 %copy-start.2 = (bf16[3072,256]{1,0:T(8,128)(2,1)S(1)}, bf16[3072,256]{1,0:T(8,128)(2,1)}, u32[]{:S(2)}) copy-start(bf16[3072,256]{1,0:T(8,128)(2,1)} %refs_9_.1) | copy-start | bytes 4718596
  35.5 3.5 %copy-start.3 = (bf16[3072,256]{1,0:T(8,128)(2,1)S(1)}, bf16[3072,256]{1,0:T(8,128)(2,1)}, u32[]{:S(2)}) copy-start(bf16[3072,256]{1,0:T(8,128)(2,1)} %refs_10_.1) | copy-start | bytes 4718596
  35.5 5.7 %slice-start = ((s8[4718592]{0:T(1024)(128)(4,1)}), s8[4194304]{0:T(1024)(128)(4,1)S(1)}, s32[]{:S(2)}) async-start(s8[4718592]{0:T(1024)(128)(4,1)} %bitcast.17), calls=%async_computation | async-start | bytes 8388608
  38.9 1.2 %copy-start.1 = (bf16[256,768]{1,0:T(8,128)(2,1)S(1)}, bf16[256,768]{1,0:T(8,128)(2,1)}, u32[]{:S(2)}) copy-start(bf16[256,768]{1,0:T(8,128)(2,1)} %refs_0_.5) | copy-start | bytes 1179652
  38.9 2.4 %slice-start.1 = ((s8[4718592]{0:T(1024)(128)(4,1)}), s8[524288]{0:T(1024)(128)(4,1)S(1)}, s32[]{:S(2)}) async-start(s8[4718592]{0:T(1024)(128)(4,1)} %bitcast.17), calls=%async_computation.1 | async-start | bytes 1048576
  38.9 13.5 %collective-permute-start.14 = (bf16[144,768]{1,0:T(8,128)(2,1)S(1)}, bf16[144,768]{1,0:T(8,128)(2,1)S(1)}, u32[]{:S(2)}, u32[]{:S(2)}) collective-permute-start(bf16[144,768]{1,0:T(8,128)(2,1)S(1)} %attend_partner.3), channel_id=1, source_target_pairs={{0,16},{4,20},{8,24},{12,28},{16,0},{20,4},{24,8},{28,12},{1,17},{... | collective-permute-start | bytes 663560 | tf_op jit(solution)/shard_map/ppermute | solution.py:29
  41.2 11.1 %slice-start.2 = ((s8[4718592]{0:T(1024)(128)(4,1)}), s8[4194304]{0:T(1024)(128)(4,1)S(1)}, s32[]{:S(2)}) async-start(s8[4718592]{0:T(1024)(128)(4,1)} %bitcast.19), calls=%async_computation.2 | async-start | bytes 8388608
  44.6 3.5 %copy-start.5 = (bf16[2048,256]{1,0:T(8,128)(2,1)S(1)}, bf16[2048,256]{1,0:T(8,128)(2,1)}, u32[]{:S(2)}) copy-start(bf16[2048,256]{1,0:T(8,128)(2,1)} %refs_6_.3) | copy-start | bytes 3145732
  44.6 3.5 %copy-start.7 = (bf16[2048,256]{1,0:T(8,128)(2,1)S(1)}, bf16[2048,256]{1,0:T(8,128)(2,1)}, u32[]{:S(2)}) copy-start(bf16[2048,256]{1,0:T(8,128)(2,1)} %refs_7_.1) | copy-start | bytes 3145732
  44.6 3.5 %copy-start.10 = (s32[4]{0:T(128)S(1)}, s32[4]{0:T(128)}, u32[]{:S(2)}) copy-start(s32[4]{0:T(128)} %lengths.3) | copy-start | bytes 52
  44.6 7.8 %slice-start.3 = ((s8[4718592]{0:T(1024)(128)(4,1)}), s8[524288]{0:T(1024)(128)(4,1)S(1)}, s32[]{:S(2)}) async-start(s8[4718592]{0:T(1024)(128)(4,1)} %bitcast.19), calls=%async_computation.3 | async-start | bytes 1048576
  53.8 18.6 %collective-permute-start.15 = (bf16[2,128,768]{2,1,0:T(8,128)(2,1)S(1)}, bf16[2,128,768]{2,1,0:T(8,128)(2,1)S(1)}, u32[]{:S(2)}, u32[]{:S(2)}) collective-permute-start(bf16[2,128,768]{2,1,0:T(8,128)(2,1)S(1)} %get-tuple-element.44), channel_id=1, source_target_pairs={{0,1},{1,0},{2,3},{3,2},{4,5},{5,4},{6,7},{7,6},{8,9},{9,8},{10,11... | collective-permute-start | bytes 1179656 | tf_op jit(solution)/shard_map/ppermute | solution.py:34
  57.5 13.4 %collective-permute-start.11 = (bf16[144,768]{1,0:T(8,128)(2,1)S(1)}, bf16[144,768]{1,0:T(8,128)(2,1)S(1)}, u32[]{:S(2)}, u32[]{:S(2)}) collective-permute-start(bf16[144,768]{1,0:T(8,128)(2,1)S(1)} %attend_partner.2), channel_id=1, source_target_pairs={{0,16},{4,20},{8,24},{12,28},{16,0},{20,4},{24,8},{28,12},{1,17},{... | collective-permute-start | bytes 663560 | tf_op jit(solution)/shard_map/ppermute | solution.py:29
  72.3 2.8 %collective-permute-start.12 = (bf16[2,128,768]{2,1,0:T(8,128)(2,1)S(1)}, bf16[2,128,768]{2,1,0:T(8,128)(2,1)S(1)}, u32[]{:S(2)}, u32[]{:S(2)}) collective-permute-start(bf16[2,128,768]{2,1,0:T(8,128)(2,1)S(1)} %get-tuple-element.40), channel_id=1, source_target_pairs={{0,1},{1,0},{2,3},{3,2},{4,5},{5,4},{6,7},{7,6},{8,9},{9,8},{10,11... | collective-permute-start | bytes 1179656 | tf_op jit(solution)/shard_map/ppermute | solution.py:34
  72.5 8.3 %collective-permute-start.16 = (bf16[128,768]{1,0:T(8,128)(2,1)S(1)}, bf16[128,768]{1,0:T(8,128)(2,1)S(1)}, u32[]{:S(2)}, u32[]{:S(2)}) collective-permute-start(bf16[128,768]{1,0:T(8,128)(2,1)S(1)} %fusion.5), channel_id=1, source_target_pairs={{0,2},{1,3},{2,0},{3,1},{4,6},{5,7},{6,4},{7,5},{8,10},{9,11},{10,... | collective-permute-start | bytes 589832 | tf_op jit(solution)/shard_map/ppermute | solution.py:29
  75.2 9.7 %collective-permute-start.13 = (bf16[128,768]{1,0:T(8,128)(2,1)S(1)}, bf16[128,768]{1,0:T(8,128)(2,1)S(1)}, u32[]{:S(2)}, u32[]{:S(2)}) collective-permute-start(bf16[128,768]{1,0:T(8,128)(2,1)S(1)} %fusion.4), channel_id=1, source_target_pairs={{0,2},{1,3},{2,0},{3,1},{4,6},{5,7},{6,4},{7,5},{8,10},{9,11},{10,... | collective-permute-start | bytes 589832 | tf_op jit(solution)/shard_map/ppermute | solution.py:29

commit v3 on v2

v3 whole, which is shorter than its diff:
```python
import functools
import math

import jax
import jax.numpy as jnp
from jax import lax
from jax.experimental import pallas as pl
from jax.experimental.pallas import tpu as pltpu
from jax.sharding import PartitionSpec as P

HD = 128
LANES = 128
STAT_ROWS = 8
ROW_TILE = 16
CORES = 2
CHUNKS = 2
COST_WEIGHT = 0.02
MIB = 1 << 20

rope_base = 500000.0
neg_large = -1e30
log2_scale = math.log2(math.e) / math.sqrt(HD)

VMEM = pl.BlockSpec(memory_space=pltpu.VMEM)
SMEM = pl.BlockSpec(memory_space=pltpu.SMEM)
ANY = pl.BlockSpec(memory_space=pl.ANY)


def shifted(shard, axis, by):
    devices = lax.axis_size(axis)
    return lax.ppermute(shard, axis, [(i, (i + by) % devices) for i in range(devices)])


def other_core(shard):
    devices = lax.axis_size("head")
    return lax.ppermute(shard, "head", [(i, i ^ 1) for i in range(devices)])


def other_chips(own):
    chips = lax.axis_size("head") // CORES
    return [shifted(own, "head", CORES * k) for k in range(1, chips)]


def place_of(requests):
    member = lax.axis_index("seq")
    return lax.rem(member, requests), lax.div(member, requests)


def source_of(position_in, turn, groups):
    return lax.rem(position_in + (groups - turn), groups)


def dot(left, right):
    return jnp.dot(left, right, preferred_element_type=jnp.float32)


def dot_transposed(left, right):
    return lax.dot_general(
        left, right, (((1,), (1,)), ((), ())), preferred_element_type=jnp.float32
    )


def call(kernel, out_shape, scalars, arrays, limit, flops, transcendentals, name, earlier=()):
    moved = sum(a.size * a.dtype.itemsize for a in arrays)
    moved += sum(math.prod(s.shape) * s.dtype.itemsize for s in out_shape)
    read = len(scalars) + len(arrays)
    skipped = len(earlier)

    def body(*refs):
        kernel(*refs[:read], *refs[read + skipped :])

    return pl.pallas_call(
        body,
        out_shape=out_shape,
        in_specs=[SMEM] * len(scalars) + [VMEM] * len(arrays) + [ANY] * skipped,
        out_specs=[VMEM] * len(out_shape),
        compiler_params=pltpu.CompilerParams(vmem_limit_bytes=limit * MIB),
        cost_estimate=pl.CostEstimate(
            flops=int(COST_WEIGHT * flops),
            bytes_accessed=int(COST_WEIGHT * moved),
            transcendentals=int(COST_WEIGHT * transcendentals),
        ),
        name=name,
    )(*scalars, *arrays, *earlier)


def whole_of(blocks):
    parts = [block[...] for block in blocks]
    return jnp.concatenate(parts, 0) if len(parts) > 1 else parts[0]


def relay_kernel(count, *refs):
    whole = whole_of(refs[:count])
    at = 0
    for ref in refs[count:]:
        ref[...] = whole[at : at + ref.shape[0]]
        at = (at + ref.shape[0]) % whole.shape[0]


def relay(blocks, sizes, earlier):
    shapes = [jax.ShapeDtypeStruct((size, *blocks[0].shape[1:]), blocks[0].dtype) for size in sizes]
    kernel = functools.partial(relay_kernel, len(blocks))
    return call(kernel, shapes, [], [*blocks], 4, 0, 0, "relay", earlier)


def prepare_kernel(groups, lengths, offsets, tokens, keys, values, *outputs):
    late, cosine, sine, wide_keys, wide_values = outputs
    rows = tokens.shape[0]
    late[...] = tokens[rows - late.shape[0] :]
    request, position_in = place_of(lengths.shape[0])
    length = lengths[request]
    slots = keys.shape[0]
    lane = lax.broadcasted_iota(jnp.int32, (rows, LANES), 1)
    row = lax.broadcasted_iota(jnp.int32, (rows, LANES), 0)
    half = lax.rem(lane, HD // 2).astype(jnp.float32)
    frequency = jnp.exp2(half * (-2.0 / HD * math.log2(rope_base)))
    sign = jnp.where(lane < HD // 2, -1.0, 1.0)
    for turn in range(groups):
        first = offsets[request] + length + source_of(position_in, turn, groups) * rows
        angles = (row + first).astype(jnp.float32) * frequency
        part = slice(turn * rows, (turn + 1) * rows)
        cosine[part] = jnp.cos(angles)
        sine[part] = jnp.sin(angles) * sign
    slot = lax.broadcasted_iota(jnp.int32, (slots, LANES), 0) + position_in * slots
    lane = lax.broadcasted_iota(jnp.int32, (slots, LANES), 1)
    bias = jnp.where((lane == 0) & (slot >= length), neg_large, 0.0).astype(jnp.bfloat16)
    ones = jnp.where(lane == 0, 1.0, 0.0).astype(jnp.bfloat16)
    for head in range(keys.shape[1] // HD):
        own = slice(head * HD, (head + 1) * HD)
        wide_keys[head, :, :HD] = keys[:, own]
        wide_keys[head, :, HD:] = bias
        wide_values[head, :, :HD] = values[:, own]
        wide_values[head, :, HD:] = ones


def prepare(lengths, offsets, tokens, keys, values, groups, late_rows):
    rows, token_width = tokens.shape
    late = jax.ShapeDtypeStruct((late_rows, token_width), tokens.dtype)
    table = jax.ShapeDtypeStruct((groups * rows, LANES), jnp.float32)
    slots, width = keys.shape
    wide = jax.ShapeDtypeStruct((width // HD, slots, HD + LANES), jnp.bfloat16)
    return call(
        functools.partial(prepare_kernel, groups),
        [late, table, table, wide, wide],
        [lengths, offsets],
        [tokens, keys, values],
        24,
        40 * groups * rows * LANES,
        0,
        "rope_tables_wide_caches",
    )


def rotate(vectors, cosine, sine):
    return vectors * cosine + pltpu.roll(vectors, HD // 2, 1) * sine


def project_normed(pieces, gain, weights):
    heads = gain.shape[0]
    width = gain.shape[2]
    me = lax.axis_index("head")
    squares = 0.0
    sums = [0.0] * len(weights)
    for index, piece in enumerate(pieces):
        owner = lax.rem(me + (heads - CORES * (index % (heads // CORES))), heads)
        if index >= heads // CORES:
            owner = owner ^ 1
        wide = piece.astype(jnp.float32)
        scaled = (wide * gain[owner]).astype(jnp.bfloat16)
        along = pl.ds(pl.multiple_of(owner * width, LANES), width)
        for place, weight in enumerate(weights):
            sums[place] = sums[place] + dot(scaled, weight[along, :])
        squares = squares + jnp.sum(wide * wide, -1, keepdims=True)
    factor = lax.rsqrt(squares / (heads * width) + 1e-05)
    return [total * factor for total in sums]


def stat_rows(columns, rows):
    lane = lax.broadcasted_iota(jnp.int32, (rows, LANES), 1)
    table = jnp.zeros((rows, LANES), jnp.float32)
    for index, column in enumerate(columns):
        table = jnp.where(lane == index, column, table)
    return table.T[:STAT_ROWS]


def split_refs(counts, refs):
    parts = []
    for count in counts:
        parts.append(refs[:count])
        refs = refs[count:]
    return parts, refs


def rows_of(blocks, row_at, rows):
    parts = []
    at = 0
    for block in blocks:
        size = block.shape[0]
        low, high = max(row_at - at, 0), min(row_at + rows - at, size)
        if low < high:
            parts.append(block[low:high])
        at += size
    return jnp.concatenate(parts, 0) if len(parts) > 1 else parts[0]


def attend_kernel(counts, own, row_at, rows, table_at, *refs):
    blocks, refs = split_refs(counts, refs)
    gain, w_query, cosine, sine, wide_keys, wide_values, *outputs = refs
    pieces = [rows_of(one, row_at, rows) for one in blocks]
    (product,) = project_normed(pieces, gain, [w_query])
    cosine = cosine[table_at : table_at + rows]
    sine = sine[table_at : table_at + rows]
    kv_heads = wide_keys.shape[0]
    repeat = product.shape[1] // HD // kv_heads
    queries = [
        (rotate(product[:, head * HD : (head + 1) * HD], cosine, sine) * log2_scale).astype(
            jnp.bfloat16
        )
        for head in range(kv_heads * repeat)
    ]
    step = min(rows, LANES)
    lane = lax.broadcasted_iota(jnp.int32, (repeat * step, LANES), 1)
    mark = jnp.where(lane == 0, 1.0, 0.0).astype(jnp.bfloat16)
    tiles = [(head, at) for head in range(kv_heads) for at in range(0, rows, step)]

    def scores_of(head, at):
        stacked = jnp.concatenate(
            [query[at : at + step] for query in queries[head * repeat : (head + 1) * repeat]], 0
        )
        return dot_transposed(jnp.concatenate([stacked, mark], 1), wide_keys[head])

    columns = {}
    following = scores_of(*tiles[0])
    for index, (head, at) in enumerate(tiles):
        scores = following
        if index + 1 < len(tiles):
            following = scores_of(*tiles[index + 1])
        largest = jnp.max(scores, -1, keepdims=True)
        weights = jnp.exp2(scores - largest).astype(jnp.bfloat16)
        summed = dot(weights, wide_values[head])
        denominator = summed[:, HD : HD + 1]
        result = summed[:, :HD] / denominator
        logs = largest + jnp.log2(denominator)
        for turn in range(repeat):
            part = slice(turn * step, (turn + 1) * step)
            to = slice((head * repeat + turn) * HD, (head * repeat + turn + 1) * HD)
            outputs[0][at : at + step, to] = result[part].astype(outputs[0].dtype)
            columns.setdefault(head * repeat + turn, []).append(logs[part])
    stats = stat_rows([jnp.concatenate(parts, 0) for parts in columns.values()], rows)
    if own:
        outputs[1][...] = stats
        outputs[2][...] = jnp.concatenate(queries, 1)
        return
    outputs[0][rows:] = jnp.zeros((ROW_TILE, outputs[0].shape[1]), jnp.bfloat16)
    rest = jnp.concatenate([stats, jnp.zeros((ROW_TILE - STAT_ROWS, rows), jnp.float32)], 0)
    for part in range(3):
        rounded = rest.astype(jnp.bfloat16)
        outputs[0][rows:, part * rows : (part + 1) * rows] = rounded
        rest = rest - rounded.astype(jnp.float32)


def attend(
    pieces, gain, w_query, tables, wide_keys, wide_values, own, row_at, rows, table_at, earlier
):
    counts = [len(blocks) for blocks in pieces]
    flat = [block for blocks in pieces for block in blocks]
    out_width = w_query.shape[1]
    slots = wide_keys.shape[1]
    if own:
        out_shape = [
            jax.ShapeDtypeStruct((rows, out_width), jnp.float32),
            jax.ShapeDtypeStruct((STAT_ROWS, rows), jnp.float32),
            jax.ShapeDtypeStruct((rows, out_width), jnp.bfloat16),
        ]
    else:
        out_shape = [jax.ShapeDtypeStruct((rows + ROW_TILE, out_width), jnp.bfloat16)]
    return call(
        functools.partial(attend_kernel, counts, own, row_at, rows, table_at),
        out_shape,
        [],
        [*flat, gain, w_query, *tables, wide_keys, wide_values],
        28,
        2 * rows * out_width * (w_query.shape[0] + 4 * slots),
        rows * out_width // HD * slots,
        "attend_own" if own else "attend_partner",
        earlier,
    )


def fresh_kernel(counts, table_at, *refs):
    blocks, refs = split_refs(counts, refs)
    gain, w_key, w_value, cosine, sine, new_keys, new_values = refs
    rows = new_keys.shape[0]
    pieces = [whole_of(one) for one in blocks]
    keys, values = project_normed(pieces, gain, [w_key, w_value])
    cosine = cosine[table_at : table_at + rows]
    sine = sine[table_at : table_at + rows]
    for head in range(keys.shape[1] // HD):
        own = slice(head * HD, (head + 1) * HD)
        new_keys[:, own] = rotate(keys[:, own], cosine, sine).astype(jnp.bfloat16)
    new_values[...] = values.astype(jnp.bfloat16)


def fresh(pieces, gain, w_key, w_value, tables, table_at, earlier):
    flat = [block for blocks in pieces for block in blocks]
    rows = sum(block.shape[0] for block in pieces[0])
    shape = jax.ShapeDtypeStruct((rows, w_key.shape[1]), jnp.bfloat16)
    return call(
        functools.partial(fresh_kernel, [len(blocks) for blocks in pieces], table_at),
        [shape, shape],
        [],
        [*flat, gain, w_key, w_value, *tables],
        20,
        4 * rows * w_key.size,
        0,
        "fresh_kv",
        earlier,
    )


def write_rows(target, fresh_rows, first):
    rows = fresh_rows.shape[0]
    slab_rows = target.shape[0]
    span = rows + ROW_TILE
    start = jnp.clip(first, 0, slab_rows - span)
    start = start - lax.rem(start, ROW_TILE)
    window = pl.ds(pl.multiple_of(start, ROW_TILE), span)
    shift = start - first
    place = lax.broadcasted_iota(jnp.int32, (span, rows), 0) + shift
    chosen = place == lax.broadcasted_iota(jnp.int32, (span, rows), 1)
    moved = dot(chosen.astype(jnp.bfloat16), fresh_rows)
    row = lax.broadcasted_iota(jnp.int32, (span, target.shape[1]), 0) + shift
    inside = (row >= 0) & (row < rows)
    old = target[window, :].astype(jnp.float32)
    target[window, :] = jnp.where(inside, moved, old).astype(jnp.bfloat16)


def attend_fresh_kernel(groups, requests, *refs):
    query_refs, refs = refs[:CHUNKS], refs[CHUNKS:]
    old_refs, refs = refs[: 2 * CHUNKS], refs[2 * CHUNKS :]
    key_refs, value_refs, refs = refs[:groups], refs[groups : 2 * groups], refs[2 * groups :]
    partial, stats = refs
    position_in = place_of(requests)[1]
    sources = [source_of(position_in, turn, groups) for turn in range(groups)]
    rows, width = partial.shape
    kv_heads = key_refs[0].shape[1] // HD
    repeat = width // HD // kv_heads
    queries = whole_of(query_refs)
    old_partial = whole_of(old_refs[0::2])
    old_stats = jnp.concatenate([ref[...] for ref in old_refs[1::2]], 1)
    fresh_keys = whole_of(key_refs)
    fresh_values = whole_of(value_refs)
    token = lax.rem(lax.broadcasted_iota(jnp.int32, (repeat * rows, rows), 0), rows)
    within = lax.broadcasted_iota(jnp.int32, (repeat * rows, rows), 1)
    visible = jnp.concatenate(
        [within + source * rows <= token + position_in * rows for source in sources], 1
    )
    padding = jnp.zeros((LANES - STAT_ROWS, rows), jnp.float32)
    old_logs = jnp.concatenate([old_stats, padding], 0).T
    columns = []
    for head in range(kv_heads):
        own = [
            slice((head * repeat + turn) * HD, (head * repeat + turn + 1) * HD)
            for turn in range(repeat)
        ]
        shared = slice(head * HD, (head + 1) * HD)
        stacked = jnp.concatenate([queries[:, one] for one in own], 0)
        scores = jnp.where(visible, dot_transposed(stacked, fresh_keys[:, shared]), neg_large)
        largest = jnp.max(scores, -1, keepdims=True)
        weights = jnp.exp2(scores - largest)
        denominator = jnp.sum(weights, -1, keepdims=True)
        summed = dot(weights.astype(jnp.bfloat16), fresh_values[:, shared])
        for turn, one in enumerate(own):
            part = slice(turn * rows, (turn + 1) * rows)
            old_log = old_logs[:, head * repeat + turn : head * repeat + turn + 1]
            top = jnp.maximum(old_log, largest[part])
            old_share = jnp.exp2(old_log - top)
            share = jnp.exp2(largest[part] - top)
            total = old_share + share * denominator[part]
            partial[:, one] = (old_partial[:, one] * old_share + summed[part] * share) / total
            columns.append(top + jnp.log2(total))
    stats[...] = stat_rows(columns, rows)


def attend_fresh(requests, queries, old, new_keys, new_values):
    groups = len(new_keys)
    rows = new_keys[0].shape[0]
    width = queries[0].shape[1]
    return call(
        functools.partial(attend_fresh_kernel, groups, requests),
        [
            jax.ShapeDtypeStruct((rows, width), jnp.float32),
            jax.ShapeDtypeStruct((STAT_ROWS, rows), jnp.float32),
        ],
        [],
        [*queries, *old, *new_keys, *new_values],
        24,
        4 * rows * width * rows * groups,
        rows * width // HD * rows * groups,
        "attend_fresh",
    )


def update_kernel(groups, lengths, *refs):
    key_refs, value_refs, refs = refs[:groups], refs[groups : 2 * groups], refs[2 * groups :]
    keys, values, keys_updated, values_updated = refs
    request, position_in = place_of(lengths.shape[0])
    rows = key_refs[0].shape[0]
    keys_updated[...] = keys[...]
    values_updated[...] = values[...]
    for turn in range(groups):
        source = source_of(position_in, turn, groups)
        first = lengths[request] + source * rows - position_in * keys.shape[0]
        write_rows(keys_updated, key_refs[turn][...], first)
        write_rows(values_updated, value_refs[turn][...], first)


def update(lengths, new_keys, new_values, keys, values, earlier):
    groups = len(new_keys)
    slab = jax.ShapeDtypeStruct(keys.shape, keys.dtype)
    return call(
        functools.partial(update_kernel, groups),
        [slab, slab],
        [lengths],
        [*new_keys, *new_values, keys, values],
        20,
        4 * new_keys[0].size * new_keys[0].shape[0] * groups,
        0,
        "update_caches",
        earlier,
    )


def project_kernel(row_at, own_partial, own_stats, *refs):
    heads = lax.axis_size("head")
    chips = heads // CORES
    outputs = 3 * chips - 1
    received = refs[: -1 - outputs]
    w_out = refs[-1 - outputs]
    near, far = refs[-outputs:][:chips], refs[-outputs:][chips:]
    width = own_partial.shape[1]
    rows, block_width = near[0].shape
    part = slice(row_at, row_at + rows)
    padding = jnp.zeros((LANES - STAT_ROWS, rows), jnp.float32)
    stats = [own_stats[:, part]]
    for ref in received:
        stats.append(
            sum(
                ref[rows:, turn * rows : (turn + 1) * rows].astype(jnp.float32)
                for turn in range(3)
            )[:STAT_ROWS]
        )
    logs = [jnp.concatenate([stat, padding], 0).T for stat in stats]
    largest = functools.reduce(jnp.maximum, logs)
    shares = [jnp.exp2(log - largest) for log in logs]
    total = functools.reduce(jnp.add, shares)
    shares = [share / total for share in shares]
    attended = []
    for head in range(width // HD):
        own = slice(head * HD, (head + 1) * HD)
        column = slice(head, head + 1)
        merged = own_partial[part, own] * shares[0][:, column]
        for ref, share in zip(received, shares[1:]):
            merged = merged + ref[:rows, own].astype(jnp.float32) * share[:, column]
        attended.append(merged.astype(jnp.bfloat16))
    attended = jnp.concatenate(attended, 1)
    me = lax.axis_index("head")
    def product(ahead, flip):
        block = lax.rem(me + CORES * ahead, heads) ^ flip
        along = pl.ds(pl.multiple_of(block * block_width, LANES), block_width)
        return dot(attended, w_out[:, along]).astype(jnp.bfloat16)

    middle = block_width // 2
    for ahead in range(1, chips):
        result = product(ahead, 1)
        far[2 * ahead - 1][...] = result[:, :middle]
        far[2 * ahead][...] = result[:, middle:]
    far[0][...] = product(0, 1)
    for ahead in range(chips):
        near[ahead][...] = product(ahead, 0)


def project(row_at, rows, own, received, w_out, heads, earlier):
    chips = heads // CORES
    width = w_out.shape[1] // heads
    shape = jax.ShapeDtypeStruct((rows, width), jnp.bfloat16)
    half = jax.ShapeDtypeStruct((rows, width // 2), jnp.bfloat16)
    blocks = call(
        functools.partial(project_kernel, row_at),
        [shape] * chips + [shape] + [half] * (2 * chips - 2),
        [],
        [*own, *received, w_out],
        20,
        2 * rows * w_out.size,
        0,
        "combine_project",
        earlier,
    )
    near, far = blocks[:chips], blocks[chips:]
    return near, [far[:1]] + [far[2 * k - 1 : 2 * k + 1] for k in range(1, chips)]


def sum_kernel(count, *refs):
    total = refs[0][...].astype(jnp.float32)
    total = total + jnp.concatenate([ref[...] for ref in refs[1:count]], 1).astype(jnp.float32)
    refs[count][...] = total.astype(jnp.bfloat16)


def sum_cores(near, far, earlier):
    return call(
        functools.partial(sum_kernel, 1 + len(far)),
        [jax.ShapeDtypeStruct(near.shape, near.dtype)],
        [],
        [near, *far],
        8,
        near.size,
        0,
        "sum_cores",
        earlier,
    )[0]


def finish_kernel(*refs):
    *parts, result = refs
    count = len(parts) // CHUNKS
    rows = parts[0].shape[0]
    for chunk in range(CHUNKS):
        total = 0.0
        for ref in parts[chunk * count : (chunk + 1) * count]:
            total = total + ref[...].astype(jnp.float32)
        result[chunk * rows : (chunk + 1) * rows] = total.astype(jnp.bfloat16)


def finish(parts):
    rows, width = parts[0].shape
    shape = jax.ShapeDtypeStruct((CHUNKS * rows, width), jnp.bfloat16)
    return call(finish_kernel, [shape], [], parts, 8, CHUNKS * rows * width, 0, "finish")[0]


def shards(
    tokens,
    norm_gain,
    w_query,
    w_key,
    w_value,
    w_out,
    keys_cache,
    values_cache,
    cached_lengths,
    rope_offsets,
):
    rows, width = tokens.shape
    requests = cached_lengths.shape[0]
    groups = lax.axis_size("seq") // requests
    heads = lax.axis_size("head")
    chips = heads // CORES
    chunk_rows = rows // CHUNKS
    gain = norm_gain.reshape(heads, 1, width)

    early = tokens[:chunk_rows]
    late, *tables, wide_keys, wide_values = prepare(
        cached_lengths, rope_offsets, tokens, keys_cache, values_cache, groups, rows - chunk_rows
    )
    sent = [early, late]
    arrived = [
        [shifted(piece, "seq", turn * requests) for piece in sent] for turn in range(1, groups)
    ]

    def attend_rows(pieces, own, chunk, turn, earlier):
        at = chunk * chunk_rows
        return attend(
            pieces, gain, w_query, tables, wide_keys, wide_values, own, at if own else 0,
            chunk_rows, turn * rows + at, earlier,
        )

    half = chunk_rows // 2
    first = [relay([pieces[0]], [chunk_rows, half, half], [late]) for pieces in arrived]
    earlier = [cut[0] for cut in first]
    own_cuts = [
        relay([piece], [rows, half, half, rows - chunk_rows], earlier)
        for piece in other_chips(tokens)
    ]
    own_pieces = [[tokens]] + [[cut[0]] for cut in own_cuts] + [[other_core(tokens)]]
    own_pieces += [[other_core(block) for block in cut[1:]] for cut in own_cuts]
    own_early = [
        blocks if len(blocks) == 1 else blocks[: len(blocks) - 1] for blocks in own_pieces
    ]
    *own_part, queries = attend_rows(own_early, True, 0, 0, earlier)
    own_queries = [queries]
    earlier = [queries]
    gathered = []
    for cut in first:
        blocks = zip(*[other_chips(piece) for piece in cut[1:]])
        from_chips = [relay(one, [chunk_rows], earlier)[0] for one in blocks]
        along = [cut[0]] + from_chips
        gathered.append([along + [other_core(one) for one in along]])
        earlier = earlier + from_chips
    second = [relay([pieces[1]], [rows - chunk_rows], earlier)[0] for pieces in arrived]
    new_rows = [fresh(own_pieces, gain, w_key, w_value, tables, 0, second)]
    earlier = [new_rows[0][0]]
    received = [[] for _ in range(CHUNKS)]
    for turn in range(1, groups):
        pieces = [[block] for block in gathered[turn - 1][0]]
        (packed,) = attend_rows(pieces, False, 0, turn, earlier)
        received[0].append(shifted(packed, "seq", -turn * requests))
        earlier = [packed]
    for pieces, piece in zip(gathered, second):
        from_chips = [
            relay([one], [rows - chunk_rows], earlier)[0] for one in other_chips(piece)
        ]
        along = [piece] + from_chips
        pieces.append(along + [other_core(one) for one in along])
        earlier = earlier + from_chips
    *late_part, queries = attend_rows(own_pieces, True, 1, 0, earlier)
    own_part += late_part
    own_queries.append(queries)
    earlier = [queries]
    for turn in range(1, groups):
        pieces = [[block] for block in gathered[turn - 1][1]]
        (packed,) = attend_rows(pieces, False, 1, turn, earlier)
        received[1].append(shifted(packed, "seq", -turn * requests))
        earlier = [packed]
    for turn in range(1, groups):
        pieces = [list(blocks) for blocks in zip(*gathered[turn - 1])]
        new_rows.append(fresh(pieces, gain, w_key, w_value, tables, turn * rows, earlier))
    new_keys, new_values = zip(*new_rows)
    own_part = attend_fresh(requests, own_queries, own_part, new_keys, new_values)

    parts = []
    earlier = before_sums = []
    for chunk in range(CHUNKS):
        nears, fars = project(
            chunk * chunk_rows, chunk_rows, own_part, received[chunk], w_out, heads, earlier
        )
        fars = [[other_core(part) for part in far] for far in fars]
        earlier = [nears[0]] + before_sums
        if chunk == 0:
            keys_updated, values_updated = update(
                cached_lengths, new_keys, new_values, keys_cache, values_cache, earlier
            )
            earlier = [keys_updated]
        sums = [sum_cores(near, far, earlier) for near, far in zip(nears[1:], fars[1:])]
        from_chips = [shifted(one, "head", CORES * k) for k, one in enumerate(sums, 1)]
        parts += [nears[0], *fars[0], *from_chips]
        earlier, before_sums = sums, from_chips
    return (finish(parts), keys_updated, values_updated)


def solution(mesh):
    return jax.shard_map(
        shards,
        mesh=mesh,
        in_specs=(
            P("seq", "head"),
            P(),
            P(None, "head"),
            P(None, "head"),
            P(None, "head"),
            P("head", None),
            P("seq", "head"),
            P("seq", "head"),
            P(),
            P(),
        ),
        out_specs=(P("seq", "head"), P("seq", "head"), P("seq", "head")),
        check_vma=False,
    )
```

time: 85.9 us -> 72 us (0.84)
  the two profiles are of different devices: /device:TPU:0 before, /device:TPU:26 now
where the time goes in v3:
time: 72 us; the launch traced here: 71.6 us
  Pallas kernels  28.8 us (40%)
  waiting for transfers between devices  17.7 us (25%)
  starting transfers between devices  14.5 us (20%)
  local copies, waits for them, and re-layouts  9.79 us (14%)
  between operations  0.87 us (1%)
    pallas_call x19, Pallas kernels, call(): pl.pallas_call(body, out_shape=out_shape, in_specs=[SMEM] * len(scalars)...  28.8 us
    ppermute x10, waiting for transfers between devices, shifted(): lax.ppermute(shard, axis, [(i, (i + by) % devices) for i in range(devices)])  17.2 us
    ppermute x10, starting transfers between devices, shifted(): lax.ppermute(shard, axis, [(i, (i + by) % devices) for i in range(devices)])  11.3 us
    unnamed x34, local copies, waits for them, and re-layouts  8.82 us
    ppermute x14, starting transfers between devices, other_core(): return lax.ppermute(shard, 'head', [(i, i ^ 1) for i in range(devices)])  3.11 us
  transfers between devices with their start and end apart: 24, of which 6 were waited for; matrix products, arithmetic and copies ran while one was open for 1% of the time, Pallas kernels for 39%

profile of v3, /device:TPU:26, one launch (start us, length us, event | category | flops | bytes accessed | tf_op | source)
XLA Modules:
  0.0 71.6 jit_solution(2442265305899985445)
XLA Ops:
  0.6 1.6 %collective-permute-start = (bf16[256,768]{1,0:T(8,128)(2,1)}, bf16[256,768]{1,0:T(8,128)(2,1)S(1)}, u32[]{:S(2)}, u32[]{:S(2)}) collective-permute-start(bf16[256,768]{1,0:T(8,128)(2,1)} %refs_0_.8), channel_id=1, source_target_pairs={{0,2},{1,3},{2,0},{3,1},{4,6},{5,7},{6,4},{7,5},{8,10},{9,11},{10,... | collective-permute-start | bytes 1179656 | tf_op jit(solution)/shard_map/ppermute | solution.py:31
  2.2 1.0 %slice.3 = bf16[128,768]{1,0:T(8,128)(2,1)S(1)} slice(bf16[256,768]{1,0:T(8,128)(2,1)} %refs_0_.8), slice={[0:128], [0:768]} | slice | bytes 393216 | tf_op jit(solution)/shard_map/slice | solution.py:560
  3.2 0.4 collective-permute-start.1
  3.6 1.0 %copy-done.2 = bf16[256,768]{1,0:T(8,128)(2,1)S(1)} copy-done((bf16[256,768]{1,0:T(8,128)(2,1)S(1)}, bf16[256,768]{1,0:T(8,128)(2,1)}, u32[]{:S(2)}) %copy-start.2) | copy-done | bytes 393240
  4.6 1.2 %copy-done.6 = bf16[2048,256]{1,0:T(8,128)(2,1)S(1)} copy-done((bf16[2048,256]{1,0:T(8,128)(2,1)S(1)}, bf16[2048,256]{1,0:T(8,128)(2,1)}, u32[]{:S(2)}) %copy-start.6) | copy-done | bytes 1048600
  5.8 1.2 %copy-done.8 = bf16[2048,256]{1,0:T(8,128)(2,1)S(1)} copy-done((bf16[2048,256]{1,0:T(8,128)(2,1)S(1)}, bf16[2048,256]{1,0:T(8,128)(2,1)}, u32[]{:S(2)}) %copy-start.8) | copy-done | bytes 1048600
  7.1 0.7 copy-done.12
  7.7 0.7 copy-done.14
  8.4 2.2 %rope_tables_wide_caches.1 = (bf16[128,768]{1,0:T(8,128)(2,1)S(1)}, f32[512,128]{1,0:T(8,128)S(1)}, f32[512,128]{1,0:T(8,128)S(1)}, bf16[2,2048,256]{2,1,0:T(8,128)(2,1)S(1)}, bf16[2,2048,256]{2,1,0:T(8,128)(2,1)S(1)}) custom-call(s32[4]{0:T(128)S(1)} %copy-done.12, s32[4]{0:T(128)S(1)} %copy-done.14, bf16[256,768]{1,0:T(8,128)(2,1)S(1)} %copy-done.2, ...), custom_call_target="tpu_custom_call" | custom-call | flops 52428 | bytes 148111 | tf_op jit(solution)/shard_map/rope_tables_wide_caches/pallas_call | solution.py:72
  10.6 2.7 %collective-permute-start.10 = (bf16[128,768]{1,0:T(8,128)(2,1)S(1)}, bf16[128,768]{1,0:T(8,128)(2,1)S(1)}, u32[]{:S(2)}, u32[]{:S(2)}) collective-permute-start(bf16[128,768]{1,0:T(8,128)(2,1)S(1)} %get-tuple-element.39.refs_1_), channel_id=1, source_target_pairs={{0,16},{4,20},{8,24},{12,28},{16,0},{20,4},{24,8},{28,12},{1,17},{... | collective-permute-start | bytes 589832 | tf_op jit(solution)/shard_map/ppermute | solution.py:31
  13.2 6.6 %collective-permute-done.1.refs_0_ = bf16[128,768]{1,0:T(8,128)(2,1)S(1)} collective-permute-done((bf16[128,768]{1,0:T(8,128)(2,1)S(1)}, bf16[128,768]{1,0:T(8,128)(2,1)S(1)}, u32[]{:S(2)}, u32[]{:S(2)}) %collective-permute-start.1) | collective-permute-done | bytes 196640 | tf_op jit(solution)/shard_map/ppermute | solution.py:31
  19.9 0.1 collective-permute-start.3
  20.0 0.5 collective-permute-start.4
  20.5 0.5 collective-permute-start.6
  21.0 1.5 %collective-permute-start.7 = (bf16[64,768]{1,0:T(8,128)(2,1)S(1)}, bf16[64,768]{1,0:T(8,128)(2,1)S(1)}, u32[]{:S(2)}, u32[]{:S(2)}) collective-permute-start(bf16[64,768]{1,0:T(8,128)(2,1)S(1)} %get-tuple-element.51), channel_id=1, source_target_pairs={{0,2},{1,3},{2,0},{3,1},{4,6},{5,7},{6,4},{7,5},{8,10},{9,11},{10,... | collective-permute-start | bytes 294920 | tf_op jit(solution)/shard_map/ppermute | solution.py:31
  22.5 0.5 collective-permute-start.5
  23.0 2.3 %copy-done = bf16[3072,768]{1,0:T(8,128)(2,1)S(1)} copy-done((bf16[3072,768]{1,0:T(8,128)(2,1)S(1)}, bf16[3072,768]{1,0:T(8,128)(2,1)}, u32[]{:S(2)}) %copy-start) | copy-done | bytes 4718616
  25.4 3.5 %attend_own.2 = (f32[128,768]{1,0:T(8,128)S(1)}, f32[8,128]{1,0:T(8,128)S(1)}, bf16[128,768]{1,0:T(8,128)(2,1)S(1)}) custom-call(bf16[256,768]{1,0:T(8,128)(2,1)S(1)} %copy-done.3, bf16[256,768]{1,0:T(8,128)(2,1)S(1)} %get-tuple-element.41.refs_1_, bf16[256,768]{1,0:T(8,128)(2,1)S(1)} %collective-permute-done.2.refs_2_, ...), custom_call_target="tpu_custom_call" | custom-call | flops 44291848 | bytes 228392 | tf_op jit(solution)/shard_map/attend_own/pallas_call | solution.py:72
  28.9 0.1 collective-permute-start.9
  29.1 0.6 collective-permute-start.11
  29.6 0.2 collective-permute-start.12
  29.8 1.1 %fresh_kv.2 = (bf16[256,256]{1,0:T(8,128)(2,1)S(1)}, bf16[256,256]{1,0:T(8,128)(2,1)S(1)}) custom-call(bf16[256,768]{1,0:T(8,128)(2,1)S(1)} %copy-done.3, bf16[256,768]{1,0:T(8,128)(2,1)S(1)} %get-tuple-element.41.refs_1_, bf16[256,768]{1,0:T(8,128)(2,1)S(1)} %collective-permute-done.2.refs_2_, bf16[64,768]{1,0:T(8,128)(2,1)S(1)} %collective-permute-done.3.refs_3_, ...), custom_call_target="tpu_custom_call" | custom-call | flops 16106127 | bytes 110346 | tf_op jit(solution)/shard_map/fresh_kv/pallas_call | solution.py:72
  30.9 0.5 copy-done.1
  31.4 3.5 %attend_partner.2.refs_1_.refs_12_ = bf16[144,768]{1,0:T(8,128)(2,1)S(1)} custom-call(bf16[128,768]{1,0:T(8,128)(2,1)S(1)} %get-tuple-element.40.refs_1_.refs_11_.refs_0_, bf16[128,768]{1,0:T(8,128)(2,1)S(1)} %relay.7.refs_2_.refs_1_, bf16[128,768]{1,0:T(8,128)(2,1)S(1)} %collective-permute-done.8.refs_2_.refs_4_, ...), custom_call_target="tpu_custom_call" | custom-call | flops 44291848 | bytes 209141 | tf_op jit(solution)/shard_map/attend_partner/pallas_call | solution.py:72
  34.9 1.4 %collective-permute-done.11.refs_0_ = bf16[128,768]{1,0:T(8,128)(2,1)S(1)} collective-permute-done((bf16[128,768]{1,0:T(8,128)(2,1)S(1)}, bf16[128,768]{1,0:T(8,128)(2,1)S(1)}, u32[]{:S(2)}, u32[]{:S(2)}) %collective-permute-start.11) | collective-permute-done | bytes 196640 | tf_op jit(solution)/shard_map/ppermute | solution.py:31
  36.5 0.1 collective-permute-start.14
  36.5 3.8 %attend_own.3 = (f32[128,768]{1,0:T(8,128)S(1)}, f32[8,128]{1,0:T(8,128)S(1)}, bf16[128,768]{1,0:T(8,128)(2,1)S(1)}) custom-call(bf16[256,768]{1,0:T(8,128)(2,1)S(1)} %copy-done.3, bf16[256,768]{1,0:T(8,128)(2,1)S(1)} %get-tuple-element.41.refs_1_, bf16[256,768]{1,0:T(8,128)(2,1)S(1)} %collective-permute-done.2.refs_2_, ...), custom_call_target="tpu_custom_call" | custom-call | flops 44291848 | bytes 232325 | tf_op jit(solution)/shard_map/attend_own/pallas_call | solution.py:72
  40.3 3.5 %attend_partner.3.refs_13_ = bf16[144,768]{1,0:T(8,128)(2,1)S(1)} custom-call(bf16[128,768]{1,0:T(8,128)(2,1)S(1)} %relay.8.refs_11_.refs_0_.refs_1_, bf16[128,768]{1,0:T(8,128)(2,1)S(1)} %relay.9.refs_13_.refs_1_.refs_3_, bf16[128,768]{1,0:T(8,128)(2,1)S(1)} %collective-permute-done.12.refs_2_.refs_5_, ...), custom_call_target="tpu_custom_call" | custom-call | flops 44291848 | bytes 209141 | tf_op jit(solution)/shard_map/attend_partner/pallas_call | solution.py:72
  43.8 2.9 %collective-permute-start.19 = (bf16[144,768]{1,0:T(8,128)(2,1)S(1)}, bf16[144,768]{1,0:T(8,128)(2,1)S(1)}, u32[]{:S(2)}, u32[]{:S(2)}) collective-permute-start(bf16[144,768]{1,0:T(8,128)(2,1)S(1)} %attend_partner.3.refs_13_), channel_id=1, source_target_pairs={{0,16},{4,20},{8,24},{12,28},{16,0},{20,4},{24,8},{28,12},{1,17},{... | collective-permute-start | bytes 663560 | tf_op jit(solution)/shard_map/ppermute | solution.py:31
  46.8 1.1 %fresh_kv.3 = (bf16[256,256]{1,0:T(8,128)(2,1)S(1)}, bf16[256,256]{1,0:T(8,128)(2,1)S(1)}) custom-call(bf16[128,768]{1,0:T(8,128)(2,1)S(1)} %get-tuple-element.40.refs_1_.refs_11_.refs_0_, bf16[128,768]{1,0:T(8,128)(2,1)S(1)} %relay.8.refs_11_.refs_0_.refs_1_, bf16[128,768]{1,0:T(8,128)(2,1)S(1)} %relay.7.refs_2_.refs_1_, ...), custom_call_target="tpu_custom_call" | custom-call | flops 16106127 | bytes 110346 | tf_op jit(solution)/shard_map/fresh_kv/pallas_call | solution.py:72
  47.9 4.3 %attend_fresh.1 = (f32[256,768]{1,0:T(8,128)S(1)}, f32[8,256]{1,0:T(8,128)S(1)}) custom-call(bf16[128,768]{1,0:T(8,128)(2,1)S(1)} %get-tuple-element.48.refs_2_.refs_1_.refs_0_, bf16[128,768]{1,0:T(8,128)(2,1)S(1)} %get-tuple-element.53.refs_10_.refs_1_, f32[128,768]{1,0:T(8,128)S(1)} %get-tuple-element.54.refs_2_, f32[8,128]{1,0:T(8,128)S(1)} %get-tuple-element.55.refs_3_, ...), custom_call_target="tpu_custom_call" | custom-call | flops 8053063 | bytes 50135 | tf_op jit(solution)/shard_map/attend_fresh/pallas_call | solution.py:72
  52.3 1.2 %combine_project.2 = (bf16[128,768]{1,0:T(8,128)(2,1)S(1)}, bf16[128,768]{1,0:T(8,128)(2,1)S(1)}, bf16[128,768]{1,0:T(8,128)(2,1)S(1)}, bf16[128,384]{1,0:T(8,128)(2,1)S(1)}, bf16[128,384]{1,0:T(8,128)(2,1)S(1)}) custom-call(f32[256,768]{1,0:T(8,128)S(1)} %get-tuple-element.61.refs_0_, f32[8,256]{1,0:T(8,128)S(1)} %get-tuple-element.62.refs_1_, ...), custom_call_target="tpu_custom_call" | custom-call | flops 12079595 | bytes 130416 | tf_op jit(solution)/shard_map/combine_project/pallas_call | solution.py:72
  53.5 0.1 collective-permute-start.16
  53.6 0.5 collective-permute-start.17
  54.1 2.3 %update_caches.1 = (bf16[2048,256]{1,0:T(8,128)(2,1)}, bf16[2048,256]{1,0:T(8,128)(2,1)}) custom-call(s32[4]{0:T(128)S(1)} %copy-done.13, bf16[256,256]{1,0:T(8,128)(2,1)S(1)} %get-tuple-element.52.refs_10_.refs_6_.refs_1_, bf16[256,256]{1,0:T(8,128)(2,1)S(1)} %get-tuple-element.58.refs_7_.refs_2_, bf16[256,256]{1,0:T(8,128)(2,1)S(1)} %get-tuple-element.59.refs_8_.refs_3_, ...), custom_call_target="tpu_custom_call" | custom-call | flops 2684354 | bytes 94371 | tf_op jit(solution)/shard_map/update_caches/pallas_call | solution.py:72
  56.3 1.2 %copy-done.10 = bf16[2048,256]{1,0:T(8,128)(2,1)S(1)} copy-done((bf16[2048,256]{1,0:T(8,128)(2,1)S(1)}, bf16[2048,256]{1,0:T(8,128)(2,1)}, u32[]{:S(2)}) %copy-start.10) | copy-done | bytes 1048600
  57.6 0.6 collective-permute-start.18
  58.2 1.2 %combine_project.3 = (bf16[128,768]{1,0:T(8,128)(2,1)S(1)}, bf16[128,768]{1,0:T(8,128)(2,1)S(1)}, bf16[128,768]{1,0:T(8,128)(2,1)S(1)}, bf16[128,384]{1,0:T(8,128)(2,1)S(1)}, bf16[128,384]{1,0:T(8,128)(2,1)S(1)}) custom-call(f32[256,768]{1,0:T(8,128)S(1)} %get-tuple-element.61.refs_0_, f32[8,256]{1,0:T(8,128)S(1)} %get-tuple-element.62.refs_1_, ...), custom_call_target="tpu_custom_call" | custom-call | flops 12079595 | bytes 130416 | tf_op jit(solution)/shard_map/combine_project/pallas_call | solution.py:72
  59.4 0.1 collective-permute-start.21
  59.5 0.5 collective-permute-start.22
  60.0 0.1 collective-permute-start.15
  60.1 0.4 collective-permute-start.20
  60.5 0.3 collective-permute-done.21.refs_1_
  60.8 0.2 collective-permute-done.22.refs_2_
  60.9 3.7 %collective-permute-done.18.refs_4_.refs_2_ = bf16[128,768]{1,0:T(8,128)(2,1)S(1)} collective-permute-done((bf16[128,768]{1,0:T(8,128)(2,1)S(1)}, bf16[128,768]{1,0:T(8,128)(2,1)S(1)}, u32[]{:S(2)}, u32[]{:S(2)}) %collective-permute-start.18) | collective-permute-done | bytes 196640 | tf_op jit(solution)/shard_map/ppermute | solution.py:31
  64.6 0.6 collective-permute-start.23
  65.2 5.6 %collective-permute-done.23.refs_5_ = bf16[128,768]{1,0:T(8,128)(2,1)S(1)} collective-permute-done((bf16[128,768]{1,0:T(8,128)(2,1)S(1)}, bf16[128,768]{1,0:T(8,128)(2,1)S(1)}, u32[]{:S(2)}, u32[]{:S(2)}) %collective-permute-start.23) | collective-permute-done | bytes 196640 | tf_op jit(solution)/shard_map/ppermute | solution.py:31
  70.7 0.9 %finish.1 = bf16[256,768]{1,0:T(8,128)(2,1)} custom-call(bf16[128,768]{1,0:T(8,128)(2,1)S(1)} %get-tuple-element.63.refs_7_.refs_0_, bf16[128,768]{1,0:T(8,128)(2,1)S(1)} %collective-permute-done.15.refs_1_, bf16[128,768]{1,0:T(8,128)(2,1)S(1)} %collective-permute-done.18.refs_4_.refs_2_, bf16[128,768]{1,0:T(8,128)(2,1)S(1)} %get-tuple-element.69.refs_3_, ...), custom_call_target="tpu_custom_call" | custom-call | flops 3932 | bytes 31457 | tf_op jit(solution)/shard_map/finish/pallas_call | solution.py:72
  (55 shorter events, 0.4 us)
Async XLA Ops:
  0.6 22.4 %copy-start.3 = (bf16[256,768]{1,0:T(8,128)(2,1)S(1)}, bf16[256,768]{1,0:T(8,128)(2,1)}, u32[]{:S(2)}) copy-start(bf16[256,768]{1,0:T(8,128)(2,1)} %refs_0_.8) | copy-start | bytes 1179652
  0.6 19.2 %collective-permute-start = (bf16[256,768]{1,0:T(8,128)(2,1)}, bf16[256,768]{1,0:T(8,128)(2,1)S(1)}, u32[]{:S(2)}, u32[]{:S(2)}) collective-permute-start(bf16[256,768]{1,0:T(8,128)(2,1)} %refs_0_.8), channel_id=1, source_target_pairs={{0,2},{1,3},{2,0},{3,1},{4,6},{5,7},{6,4},{7,5},{8,10},{9,11},{10,... | collective-permute-start | bytes 1179656 | tf_op jit(solution)/shard_map/ppermute | solution.py:31
  2.2 18.8 %collective-permute-start.2 = (bf16[256,768]{1,0:T(8,128)(2,1)}, bf16[256,768]{1,0:T(8,128)(2,1)S(1)}, u32[]{:S(2)}, u32[]{:S(2)}) collective-permute-start(bf16[256,768]{1,0:T(8,128)(2,1)} %refs_0_.8), channel_id=1, source_target_pairs={{0,1},{1,0},{2,3},{3,2},{4,5},{5,4},{6,7},{7,6},{8,9},{9,8},{10,11... | collective-permute-start | bytes 1179656 | tf_op jit(solution)/shard_map/ppermute | solution.py:36
  3.2 16.6 %collective-permute-start.1 = (bf16[128,768]{1,0:T(8,128)(2,1)S(1)}, bf16[128,768]{1,0:T(8,128)(2,1)S(1)}, u32[]{:S(2)}, u32[]{:S(2)}) collective-permute-start(bf16[128,768]{1,0:T(8,128)(2,1)S(1)} %slice.3), channel_id=1, source_target_pairs={{0,16},{4,20},{8,24},{12,28},{16,0},{20,4},{24,8},{28,12},{1,17},{... | collective-permute-start | bytes 589832 | tf_op jit(solution)/shard_map/ppermute | solution.py:31
  3.6 1.0 %copy-start.2 = (bf16[256,768]{1,0:T(8,128)(2,1)S(1)}, bf16[256,768]{1,0:T(8,128)(2,1)}, u32[]{:S(2)}) copy-start(bf16[256,768]{1,0:T(8,128)(2,1)} %refs_0_.8) | copy-start | bytes 1179652
  4.6 1.2 %copy-start.6 = (bf16[2048,256]{1,0:T(8,128)(2,1)S(1)}, bf16[2048,256]{1,0:T(8,128)(2,1)}, u32[]{:S(2)}) copy-start(bf16[2048,256]{1,0:T(8,128)(2,1)} %refs_5_.5) | copy-start | bytes 3145732
  5.8 1.2 %copy-start.8 = (bf16[2048,256]{1,0:T(8,128)(2,1)S(1)}, bf16[2048,256]{1,0:T(8,128)(2,1)}, u32[]{:S(2)}) copy-start(bf16[2048,256]{1,0:T(8,128)(2,1)} %refs_6_.3) | copy-start | bytes 3145732
  7.1 0.7 copy-start.12
  7.7 0.7 copy-start.14
  8.4 14.7 %copy-start.11 = (f32[3072]{0:T(1024)S(1)}, f32[3072]{0:T(1024)}, u32[]{:S(2)}) copy-start(f32[3072]{0:T(1024)} %param.11) | copy-start | bytes 36868
  10.6 18.5 %collective-permute-start.10 = (bf16[128,768]{1,0:T(8,128)(2,1)S(1)}, bf16[128,768]{1,0:T(8,128)(2,1)S(1)}, u32[]{:S(2)}, u32[]{:S(2)}) collective-permute-start(bf16[128,768]{1,0:T(8,128)(2,1)S(1)} %get-tuple-element.39.refs_1_), channel_id=1, source_target_pairs={{0,16},{4,20},{8,24},{12,28},{16,0},{20,4},{24,8},{28,12},{1,17},{... | collective-permute-start | bytes 589832 | tf_op jit(solution)/shard_map/ppermute | solution.py:31
  19.9 2.6 %collective-permute-start.3 = (bf16[64,768]{1,0:T(8,128)(2,1)S(1)}, bf16[64,768]{1,0:T(8,128)(2,1)S(1)}, u32[]{:S(2)}, u32[]{:S(2)}) collective-permute-start(bf16[64,768]{1,0:T(8,128)(2,1)S(1)} %get-tuple-element.42), channel_id=1, source_target_pairs={{0,1},{1,0},{2,3},{3,2},{4,5},{5,4},{6,7},{7,6},{8,9},{9,8},{10,11... | collective-permute-start | bytes 294920 | tf_op jit(solution)/shard_map/ppermute | solution.py:36
  20.0 2.5 %collective-permute-start.4 = (bf16[64,768]{1,0:T(8,128)(2,1)S(1)}, bf16[64,768]{1,0:T(8,128)(2,1)S(1)}, u32[]{:S(2)}, u32[]{:S(2)}) collective-permute-start(bf16[64,768]{1,0:T(8,128)(2,1)S(1)} %get-tuple-element.43), channel_id=1, source_target_pairs={{0,1},{1,0},{2,3},{3,2},{4,5},{5,4},{6,7},{7,6},{8,9},{9,8},{10,11... | collective-permute-start | bytes 294920 | tf_op jit(solution)/shard_map/ppermute | solution.py:36
  20.5 8.4 %collective-permute-start.6 = (bf16[64,768]{1,0:T(8,128)(2,1)S(1)}, bf16[64,768]{1,0:T(8,128)(2,1)S(1)}, u32[]{:S(2)}, u32[]{:S(2)}) collective-permute-start(bf16[64,768]{1,0:T(8,128)(2,1)S(1)} %get-tuple-element.50), channel_id=1, source_target_pairs={{0,2},{1,3},{2,0},{3,1},{4,6},{5,7},{6,4},{7,5},{8,10},{9,11},{10,... | collective-permute-start | bytes 294920 | tf_op jit(solution)/shard_map/ppermute | solution.py:31
  21.0 7.9 %collective-permute-start.7 = (bf16[64,768]{1,0:T(8,128)(2,1)S(1)}, bf16[64,768]{1,0:T(8,128)(2,1)S(1)}, u32[]{:S(2)}, u32[]{:S(2)}) collective-permute-start(bf16[64,768]{1,0:T(8,128)(2,1)S(1)} %get-tuple-element.51), channel_id=1, source_target_pairs={{0,2},{1,3},{2,0},{3,1},{4,6},{5,7},{6,4},{7,5},{8,10},{9,11},{10,... | collective-permute-start | bytes 294920 | tf_op jit(solution)/shard_map/ppermute | solution.py:31
  22.5 8.4 %collective-permute-start.8 = (bf16[128,768]{1,0:T(8,128)(2,1)S(1)}, bf16[128,768]{1,0:T(8,128)(2,1)S(1)}, u32[]{:S(2)}, u32[]{:S(2)}) collective-permute-start(bf16[128,768]{1,0:T(8,128)(2,1)S(1)} %get-tuple-element.40.refs_1_.refs_11_.refs_0_), channel_id=1, source_target_pairs={{0,1},{1,0},{2,3},{3,2},{4,5},{5,4},{6,7},{7,6},{8,9},{9,8},{10,11... | collective-permute-start | bytes 589832 | tf_op jit(solution)/shard_map/ppermute | solution.py:36
  22.5 7.3 %collective-permute-start.5 = (bf16[128,768]{1,0:T(8,128)(2,1)S(1)}, bf16[128,768]{1,0:T(8,128)(2,1)S(1)}, u32[]{:S(2)}, u32[]{:S(2)}) collective-permute-start(bf16[128,768]{1,0:T(8,128)(2,1)S(1)} %get-tuple-element.49), channel_id=1, source_target_pairs={{0,1},{1,0},{2,3},{3,2},{4,5},{5,4},{6,7},{7,6},{8,9},{9,8},{10,11... | collective-permute-start | bytes 589832 | tf_op jit(solution)/shard_map/ppermute | solution.py:36
  23.0 2.3 %copy-start = (bf16[3072,768]{1,0:T(8,128)(2,1)S(1)}, bf16[3072,768]{1,0:T(8,128)(2,1)}, u32[]{:S(2)}) copy-start(bf16[3072,768]{1,0:T(8,128)(2,1)} %refs_5_.4) | copy-start | bytes 14155780
  25.4 4.4 %copy-start.4 = (bf16[3072,256]{1,0:T(8,128)(2,1)S(1)}, bf16[3072,256]{1,0:T(8,128)(2,1)}, u32[]{:S(2)}) copy-start(bf16[3072,256]{1,0:T(8,128)(2,1)} %refs_9_.1) | copy-start | bytes 4718596
  25.4 4.4 %copy-start.5 = (bf16[3072,256]{1,0:T(8,128)(2,1)S(1)}, bf16[3072,256]{1,0:T(8,128)(2,1)}, u32[]{:S(2)}) copy-start(bf16[3072,256]{1,0:T(8,128)(2,1)} %refs_10_.1) | copy-start | bytes 4718596
  28.9 2.0 %collective-permute-start.9 = (bf16[128,768]{1,0:T(8,128)(2,1)S(1)}, bf16[128,768]{1,0:T(8,128)(2,1)S(1)}, u32[]{:S(2)}, u32[]{:S(2)}) collective-permute-start(bf16[128,768]{1,0:T(8,128)(2,1)S(1)} %relay.7.refs_2_.refs_1_), channel_id=1, source_target_pairs={{0,1},{1,0},{2,3},{3,2},{4,5},{5,4},{6,7},{7,6},{8,9},{9,8},{10,11... | collective-permute-start | bytes 589832 | tf_op jit(solution)/shard_map/ppermute | solution.py:36
  29.0 2.3 %copy-start.1 = (bf16[3072,768]{1,0:T(8,128)(2,1)S(1)}, bf16[3072,768]{1,0:T(8,128)(2,1)}, u32[]{:S(2)}) copy-start(bf16[3072,768]{1,0:T(8,128)(2,1)} %refs_5_.4) | copy-start | bytes 14155780
  29.1 7.3 %collective-permute-start.11 = (bf16[128,768]{1,0:T(8,128)(2,1)S(1)}, bf16[128,768]{1,0:T(8,128)(2,1)S(1)}, u32[]{:S(2)}, u32[]{:S(2)}) collective-permute-start(bf16[128,768]{1,0:T(8,128)(2,1)S(1)} %relay.8.refs_11_.refs_0_.refs_1_), channel_id=1, source_target_pairs={{0,2},{1,3},{2,0},{3,1},{4,6},{5,7},{6,4},{7,5},{8,10},{9,11},{10,... | collective-permute-start | bytes 589832 | tf_op jit(solution)/shard_map/ppermute | solution.py:31
  29.6 10.7 %collective-permute-start.12 = (bf16[128,768]{1,0:T(8,128)(2,1)S(1)}, bf16[128,768]{1,0:T(8,128)(2,1)S(1)}, u32[]{:S(2)}, u32[]{:S(2)}) collective-permute-start(bf16[128,768]{1,0:T(8,128)(2,1)S(1)} %relay.8.refs_11_.refs_0_.refs_1_), channel_id=1, source_target_pairs={{0,1},{1,0},{2,3},{3,2},{4,5},{5,4},{6,7},{7,6},{8,9},{9,8},{10,11... | collective-permute-start | bytes 589832 | tf_op jit(solution)/shard_map/ppermute | solution.py:36
  36.4 3.9 %collective-permute-start.13 = (bf16[128,768]{1,0:T(8,128)(2,1)S(1)}, bf16[128,768]{1,0:T(8,128)(2,1)S(1)}, u32[]{:S(2)}, u32[]{:S(2)}) collective-permute-start(bf16[128,768]{1,0:T(8,128)(2,1)S(1)} %relay.9.refs_13_.refs_1_.refs_3_), channel_id=1, source_target_pairs={{0,1},{1,0},{2,3},{3,2},{4,5},{5,4},{6,7},{7,6},{8,9},{9,8},{10,11... | collective-permute-start | bytes 589832 | tf_op jit(solution)/shard_map/ppermute | solution.py:36
  36.5 15.7 %collective-permute-start.14 = (bf16[144,768]{1,0:T(8,128)(2,1)S(1)}, bf16[144,768]{1,0:T(8,128)(2,1)S(1)}, u32[]{:S(2)}, u32[]{:S(2)}) collective-permute-start(bf16[144,768]{1,0:T(8,128)(2,1)S(1)} %attend_partner.2.refs_1_.refs_12_), channel_id=1, source_target_pairs={{0,16},{4,20},{8,24},{12,28},{16,0},{20,4},{24,8},{28,12},{1,17},{... | collective-permute-start | bytes 663560 | tf_op jit(solution)/shard_map/ppermute | solution.py:31
  40.3 11.9 %slice-start = ((s8[4718592]{0:T(1024)(128)(4,1)}), s8[4194304]{0:T(1024)(128)(4,1)S(1)}, s32[]{:S(2)}) async-start(s8[4718592]{0:T(1024)(128)(4,1)} %bitcast.1), calls=%async_computation | async-start | bytes 8388608
  40.3 11.9 %slice-start.1 = ((s8[4718592]{0:T(1024)(128)(4,1)}), s8[524288]{0:T(1024)(128)(4,1)S(1)}, s32[]{:S(2)}) async-start(s8[4718592]{0:T(1024)(128)(4,1)} %bitcast.1), calls=%async_computation.1 | async-start | bytes 1048576
  43.8 14.3 %collective-permute-start.19 = (bf16[144,768]{1,0:T(8,128)(2,1)S(1)}, bf16[144,768]{1,0:T(8,128)(2,1)S(1)}, u32[]{:S(2)}, u32[]{:S(2)}) collective-permute-start(bf16[144,768]{1,0:T(8,128)(2,1)S(1)} %attend_partner.3.refs_13_), channel_id=1, source_target_pairs={{0,16},{4,20},{8,24},{12,28},{16,0},{20,4},{24,8},{28,12},{1,17},{... | collective-permute-start | bytes 663560 | tf_op jit(solution)/shard_map/ppermute | solution.py:31
  52.2 1.8 %copy-start.7 = (bf16[2048,256]{1,0:T(8,128)(2,1)S(1)}, bf16[2048,256]{1,0:T(8,128)(2,1)}, u32[]{:S(2)}) copy-start(bf16[2048,256]{1,0:T(8,128)(2,1)} %refs_5_.5) | copy-start | bytes 3145732
  52.2 1.8 %copy-start.9 = (bf16[2048,256]{1,0:T(8,128)(2,1)S(1)}, bf16[2048,256]{1,0:T(8,128)(2,1)}, u32[]{:S(2)}) copy-start(bf16[2048,256]{1,0:T(8,128)(2,1)} %refs_6_.3) | copy-start | bytes 3145732
  52.2 1.8 %copy-start.13 = (s32[4]{0:T(128)S(1)}, s32[4]{0:T(128)}, u32[]{:S(2)}) copy-start(s32[4]{0:T(128)} %refs_0_.9) | copy-start | bytes 52
  53.5 2.8 %collective-permute-start.16 = (bf16[128,384]{1,0:T(8,128)(2,1)S(1)}, bf16[128,384]{1,0:T(8,128)(2,1)S(1)}, u32[]{:S(2)}, u32[]{:S(2)}) collective-permute-start(bf16[128,384]{1,0:T(8,128)(2,1)S(1)} %get-tuple-element.66), channel_id=1, source_target_pairs={{0,1},{1,0},{2,3},{3,2},{4,5},{5,4},{6,7},{7,6},{8,9},{9,8},{10,11... | collective-permute-start | bytes 294920 | tf_op jit(solution)/shard_map/ppermute | solution.py:36
  53.6 2.8 %collective-permute-start.17 = (bf16[128,384]{1,0:T(8,128)(2,1)S(1)}, bf16[128,384]{1,0:T(8,128)(2,1)S(1)}, u32[]{:S(2)}, u32[]{:S(2)}) collective-permute-start(bf16[128,384]{1,0:T(8,128)(2,1)S(1)} %get-tuple-element.67), channel_id=1, source_target_pairs={{0,1},{1,0},{2,3},{3,2},{4,5},{5,4},{6,7},{7,6},{8,9},{9,8},{10,11... | collective-permute-start | bytes 294920 | tf_op jit(solution)/shard_map/ppermute | solution.py:36
  56.3 1.2 %copy-start.10 = (bf16[2048,256]{1,0:T(8,128)(2,1)S(1)}, bf16[2048,256]{1,0:T(8,128)(2,1)}, u32[]{:S(2)}) copy-start(bf16[2048,256]{1,0:T(8,128)(2,1)} %get-tuple-element.37.refs_3_) | copy-start | bytes 3145732
  57.6 7.0 %collective-permute-start.18 = (bf16[128,768]{1,0:T(8,128)(2,1)S(1)}, bf16[128,768]{1,0:T(8,128)(2,1)S(1)}, u32[]{:S(2)}, u32[]{:S(2)}) collective-permute-start(bf16[128,768]{1,0:T(8,128)(2,1)S(1)} %sum_cores.2.refs_4_), channel_id=1, source_target_pairs={{0,2},{1,3},{2,0},{3,1},{4,6},{5,7},{6,4},{7,5},{8,10},{9,11},{10,... | collective-permute-start | bytes 589832 | tf_op jit(solution)/shard_map/ppermute | solution.py:31
  59.4 1.4 %collective-permute-start.21 = (bf16[128,384]{1,0:T(8,128)(2,1)S(1)}, bf16[128,384]{1,0:T(8,128)(2,1)S(1)}, u32[]{:S(2)}, u32[]{:S(2)}) collective-permute-start(bf16[128,384]{1,0:T(8,128)(2,1)S(1)} %get-tuple-element.72), channel_id=1, source_target_pairs={{0,1},{1,0},{2,3},{3,2},{4,5},{5,4},{6,7},{7,6},{8,9},{9,8},{10,11... | collective-permute-start | bytes 294920 | tf_op jit(solution)/shard_map/ppermute | solution.py:36
  59.5 1.4 %collective-permute-start.22 = (bf16[128,384]{1,0:T(8,128)(2,1)S(1)}, bf16[128,384]{1,0:T(8,128)(2,1)S(1)}, u32[]{:S(2)}, u32[]{:S(2)}) collective-permute-start(bf16[128,384]{1,0:T(8,128)(2,1)S(1)} %get-tuple-element.73), channel_id=1, source_target_pairs={{0,1},{1,0},{2,3},{3,2},{4,5},{5,4},{6,7},{7,6},{8,9},{9,8},{10,11... | collective-permute-start | bytes 294920 | tf_op jit(solution)/shard_map/ppermute | solution.py:36
  60.0 5.2 %collective-permute-start.15 = (bf16[128,768]{1,0:T(8,128)(2,1)S(1)}, bf16[128,768]{1,0:T(8,128)(2,1)S(1)}, u32[]{:S(2)}, u32[]{:S(2)}) collective-permute-start(bf16[128,768]{1,0:T(8,128)(2,1)S(1)} %get-tuple-element.64), channel_id=1, source_target_pairs={{0,1},{1,0},{2,3},{3,2},{4,5},{5,4},{6,7},{7,6},{8,9},{9,8},{10,11... | collective-permute-start | bytes 589832 | tf_op jit(solution)/shard_map/ppermute | solution.py:36
  60.1 5.1 %collective-permute-start.20 = (bf16[128,768]{1,0:T(8,128)(2,1)S(1)}, bf16[128,768]{1,0:T(8,128)(2,1)S(1)}, u32[]{:S(2)}, u32[]{:S(2)}) collective-permute-start(bf16[128,768]{1,0:T(8,128)(2,1)S(1)} %get-tuple-element.70), channel_id=1, source_target_pairs={{0,1},{1,0},{2,3},{3,2},{4,5},{5,4},{6,7},{7,6},{8,9},{9,8},{10,11... | collective-permute-start | bytes 589832 | tf_op jit(solution)/shard_map/ppermute | solution.py:36
  64.6 6.1 %collective-permute-start.23 = (bf16[128,768]{1,0:T(8,128)(2,1)S(1)}, bf16[128,768]{1,0:T(8,128)(2,1)S(1)}, u32[]{:S(2)}, u32[]{:S(2)}) collective-permute-start(bf16[128,768]{1,0:T(8,128)(2,1)S(1)} %sum_cores.3), channel_id=1, source_target_pairs={{0,2},{1,3},{2,0},{3,1},{4,6},{5,7},{6,4},{7,5},{8,10},{9,11},{10,... | collective-permute-start | bytes 589832 | tf_op jit(solution)/shard_map/ppermute | solution.py:31

commit v4 on v3

--- a/solution.py
+++ b/solution.py
@@ -15,6 +15,8 @@
 CORES = 2
 CHUNKS = 2
 COST_WEIGHT = 0.02
+FIRST_MICROS = 1
+FLOPS_PER_MICRO = 1_000_000_000
 MIB = 1 << 20
 
 rope_base = 500000.0
@@ -22,7 +24,6 @@
 log2_scale = math.log2(math.e) / math.sqrt(HD)
 
 VMEM = pl.BlockSpec(memory_space=pltpu.VMEM)
-SMEM = pl.BlockSpec(memory_space=pltpu.SMEM)
 ANY = pl.BlockSpec(memory_space=pl.ANY)
 
 
@@ -60,10 +61,13 @@
     )
 
 
-def call(kernel, out_shape, scalars, arrays, limit, flops, transcendentals, name, earlier=()):
+def call(
+    kernel, out_shape, arrays, limit, flops, transcendentals, name, earlier=(),
+    scratch=(), micros=0,
+):
     moved = sum(a.size * a.dtype.itemsize for a in arrays)
     moved += sum(math.prod(s.shape) * s.dtype.itemsize for s in out_shape)
-    read = len(scalars) + len(arrays)
+    read = len(arrays)
     skipped = len(earlier)
 
     def body(*refs):
@@ -72,16 +76,17 @@
     return pl.pallas_call(
         body,
         out_shape=out_shape,
-        in_specs=[SMEM] * len(scalars) + [VMEM] * len(arrays) + [ANY] * skipped,
+        in_specs=[VMEM] * len(arrays) + [ANY] * skipped,
         out_specs=[VMEM] * len(out_shape),
+        scratch_shapes=scratch,
         compiler_params=pltpu.CompilerParams(vmem_limit_bytes=limit * MIB),
         cost_estimate=pl.CostEstimate(
-            flops=int(COST_WEIGHT * flops),
+            flops=max(int(COST_WEIGHT * flops), micros * FLOPS_PER_MICRO),
             bytes_accessed=int(COST_WEIGHT * moved),
             transcendentals=int(COST_WEIGHT * transcendentals),
         ),
         name=name,
-    )(*scalars, *arrays, *earlier)
+    )(*arrays, *earlier)
 
 
 def whole_of(blocks):
@@ -100,54 +105,101 @@
 def relay(blocks, sizes, earlier):
     shapes = [jax.ShapeDtypeStruct((size, *blocks[0].shape[1:]), blocks[0].dtype) for size in sizes]
     kernel = functools.partial(relay_kernel, len(blocks))
-    return call(kernel, shapes, [], [*blocks], 4, 0, 0, "relay", earlier)
-
-
-def prepare_kernel(groups, lengths, offsets, tokens, keys, values, *outputs):
-    late, cosine, sine, wide_keys, wide_values = outputs
+    return call(kernel, shapes, [*blocks], 4, 0, 0, "relay", earlier)
+
+
+def mark_kernel(mark):
+    lane = lax.broadcasted_iota(jnp.int32, mark.shape, 1)
+    mark[...] = jnp.where(lane == 0, 1.0, 0.0).astype(mark.dtype)
+
+
+def marks(rows):
+    shape = jax.ShapeDtypeStruct((rows, LANES), jnp.bfloat16)
+    return call(mark_kernel, [shape], [], 4, 0, 0, "marks", micros=FIRST_MICROS)[0]
+
+
+def tables_kernel(groups, tokens, lengths_in, offsets_in, late, cosine, sine, *scratch):
+    lengths, offsets, semaphores = scratch
+    numbers = [
+        pltpu.make_async_copy(lengths_in, lengths, semaphores.at[0]),
+        pltpu.make_async_copy(offsets_in, offsets, semaphores.at[1]),
+    ]
+    for copy in numbers:
+        copy.start()
     rows = tokens.shape[0]
     late[...] = tokens[rows - late.shape[0] :]
+    for copy in numbers:
+        copy.wait()
     request, position_in = place_of(lengths.shape[0])
-    length = lengths[request]
-    slots = keys.shape[0]
     lane = lax.broadcasted_iota(jnp.int32, (rows, LANES), 1)
     row = lax.broadcasted_iota(jnp.int32, (rows, LANES), 0)
     half = lax.rem(lane, HD // 2).astype(jnp.float32)
     frequency = jnp.exp2(half * (-2.0 / HD * math.log2(rope_base)))
     sign = jnp.where(lane < HD // 2, -1.0, 1.0)
     for turn in range(groups):
-        first = offsets[request] + length + source_of(position_in, turn, groups) * rows
+        first = source_of(position_in, turn, groups) * rows
+        first = first + offsets[request] + lengths[request]
         angles = (row + first).astype(jnp.float32) * frequency
         part = slice(turn * rows, (turn + 1) * rows)
         cosine[part] = jnp.cos(angles)
         sine[part] = jnp.sin(angles) * sign
-    slot = lax.broadcasted_iota(jnp.int32, (slots, LANES), 0) + position_in * slots
-    lane = lax.broadcasted_iota(jnp.int32, (slots, LANES), 1)
-    bias = jnp.where((lane == 0) & (slot >= length), neg_large, 0.0).astype(jnp.bfloat16)
-    ones = jnp.where(lane == 0, 1.0, 0.0).astype(jnp.bfloat16)
-    for head in range(keys.shape[1] // HD):
-        own = slice(head * HD, (head + 1) * HD)
-        wide_keys[head, :, :HD] = keys[:, own]
-        wide_keys[head, :, HD:] = bias
-        wide_values[head, :, :HD] = values[:, own]
-        wide_values[head, :, HD:] = ones
-
-
-def prepare(lengths, offsets, tokens, keys, values, groups, late_rows):
+
+
+def rope_tables(tokens, lengths, offsets, groups, late_rows, earlier):
     rows, token_width = tokens.shape
     late = jax.ShapeDtypeStruct((late_rows, token_width), tokens.dtype)
     table = jax.ShapeDtypeStruct((groups * rows, LANES), jnp.float32)
+    return call(
+        functools.partial(tables_kernel, groups),
+        [late, table, table],
+        [tokens, lengths, offsets],
+        12,
+        0,
+        0,
+        "rope_tables",
+        earlier,
+        [
+            pltpu.SMEM(lengths.shape, lengths.dtype),
+            pltpu.SMEM(offsets.shape, offsets.dtype),
+            pltpu.SemaphoreType.DMA((2,)),
+        ],
+        FIRST_MICROS,
+    )
+
+
+def widen_kernel(keys, values, mark, lengths_in, wide_keys, wide_values, lengths, semaphore):
+    number = pltpu.make_async_copy(lengths_in, lengths, semaphore)
+    number.start()
+    slots = keys.shape[0]
+    heads = keys.shape[1] // HD
+    for head in range(heads):
+        own = slice(head * HD, (head + 1) * HD)
+        wide_keys[head, :, :HD] = keys[:, own]
+        wide_values[head, :, :HD] = values[:, own]
+        wide_values[head, :, HD:] = mark[:slots]
+    number.wait()
+    request, position_in = place_of(lengths.shape[0])
+    slot = lax.broadcasted_iota(jnp.int32, (slots, LANES), 0) + position_in * slots
+    lane = lax.broadcasted_iota(jnp.int32, (slots, LANES), 1)
+    bias = jnp.where((lane == 0) & (slot >= lengths[request]), neg_large, 0.0).astype(jnp.bfloat16)
+    for head in range(heads):
+        wide_keys[head, :, HD:] = bias
+
+
+def widen(keys, values, mark, lengths, earlier):
     slots, width = keys.shape
     wide = jax.ShapeDtypeStruct((width // HD, slots, HD + LANES), jnp.bfloat16)
     return call(
-        functools.partial(prepare_kernel, groups),
-        [late, table, table, wide, wide],
-        [lengths, offsets],
-        [tokens, keys, values],
-        24,
-        40 * groups * rows * LANES,
+        widen_kernel,
+        [wide, wide],
+        [keys, values, mark, lengths],
+        12,
         0,
-        "rope_tables_wide_caches",
+        0,
+        "widen_caches",
+        earlier,
+        [pltpu.SMEM(lengths.shape, lengths.dtype), pltpu.SemaphoreType.DMA],
+        FIRST_MICROS,
     )
 
 
@@ -205,7 +257,7 @@
 
 def attend_kernel(counts, own, row_at, rows, table_at, *refs):
     blocks, refs = split_refs(counts, refs)
-    gain, w_query, cosine, sine, wide_keys, wide_values, *outputs = refs
+    gain, w_query, cosine, sine, wide_keys, wide_values, mark, *outputs = refs
     pieces = [rows_of(one, row_at, rows) for one in blocks]
     (product,) = project_normed(pieces, gain, [w_query])
     cosine = cosine[table_at : table_at + rows]
@@ -219,8 +271,7 @@
         for head in range(kv_heads * repeat)
     ]
     step = min(rows, LANES)
-    lane = lax.broadcasted_iota(jnp.int32, (repeat * step, LANES), 1)
-    mark = jnp.where(lane == 0, 1.0, 0.0).astype(jnp.bfloat16)
+    mark = mark[: repeat * step]
     tiles = [(head, at) for head in range(kv_heads) for at in range(0, rows, step)]
 
     def scores_of(head, at):
@@ -260,7 +311,8 @@
 
 
 def attend(
-    pieces, gain, w_query, tables, wide_keys, wide_values, own, row_at, rows, table_at, earlier
+    pieces, gain, w_query, tables, wide_keys, wide_values, mark, own, row_at, rows, table_at,
+    earlier,
 ):
     counts = [len(blocks) for blocks in pieces]
     flat = [block for blocks in pieces for block in blocks]
@@ -277,8 +329,7 @@
     return call(
         functools.partial(attend_kernel, counts, own, row_at, rows, table_at),
         out_shape,
-        [],
-        [*flat, gain, w_query, *tables, wide_keys, wide_values],
+        [*flat, gain, w_query, *tables, wide_keys, wide_values, mark],
         28,
         2 * rows * out_width * (w_query.shape[0] + 4 * slots),
         rows * out_width // HD * slots,
@@ -308,7 +359,6 @@
     return call(
         functools.partial(fresh_kernel, [len(blocks) for blocks in pieces], table_at),
         [shape, shape],
-        [],
         [*flat, gain, w_key, w_value, *tables],
         20,
         4 * rows * w_key.size,
@@ -337,26 +387,23 @@
 
 def attend_fresh_kernel(groups, requests, *refs):
     query_refs, refs = refs[:CHUNKS], refs[CHUNKS:]
-    old_refs, refs = refs[: 2 * CHUNKS], refs[2 * CHUNKS :]
     key_refs, value_refs, refs = refs[:groups], refs[groups : 2 * groups], refs[2 * groups :]
     partial, stats = refs
     position_in = place_of(requests)[1]
-    sources = [source_of(position_in, turn, groups) for turn in range(groups)]
     rows, width = partial.shape
     kv_heads = key_refs[0].shape[1] // HD
     repeat = width // HD // kv_heads
     queries = whole_of(query_refs)
-    old_partial = whole_of(old_refs[0::2])
-    old_stats = jnp.concatenate([ref[...] for ref in old_refs[1::2]], 1)
-    fresh_keys = whole_of(key_refs)
-    fresh_values = whole_of(value_refs)
-    token = lax.rem(lax.broadcasted_iota(jnp.int32, (repeat * rows, rows), 0), rows)
-    within = lax.broadcasted_iota(jnp.int32, (repeat * rows, rows), 1)
-    visible = jnp.concatenate(
-        [within + source * rows <= token + position_in * rows for source in sources], 1
-    )
-    padding = jnp.zeros((LANES - STAT_ROWS, rows), jnp.float32)
-    old_logs = jnp.concatenate([old_stats, padding], 0).T
+    token = lax.broadcasted_iota(jnp.int32, (rows, rows), 0)
+    within = lax.broadcasted_iota(jnp.int32, (rows, rows), 1)
+    causal = jnp.where(within <= token, 0.0, neg_large)
+    causal = jnp.concatenate([causal] * repeat, 0)
+    lane = lax.broadcasted_iota(jnp.int32, (rows, LANES), 1)
+    ones = jnp.where(lane == 0, 1.0, 0.0).astype(jnp.bfloat16)
+    hidden = [jnp.zeros((rows, LANES), jnp.bfloat16)]
+    for turn in range(1, groups):
+        later = source_of(position_in, turn, groups) > position_in
+        hidden.append(jnp.where((lane == 0) & later, neg_large, 0.0).astype(jnp.bfloat16))
     columns = []
     for head in range(kv_heads):
         own = [
@@ -365,24 +412,27 @@
         ]
         shared = slice(head * HD, (head + 1) * HD)
         stacked = jnp.concatenate([queries[:, one] for one in own], 0)
-        scores = jnp.where(visible, dot_transposed(stacked, fresh_keys[:, shared]), neg_large)
+        stacked = jnp.concatenate([stacked, jnp.concatenate([ones] * repeat, 0)], 1)
+        scores = [
+            dot_transposed(stacked, jnp.concatenate([ref[:, shared], bias], 1))
+            for ref, bias in zip(key_refs, hidden)
+        ]
+        scores = jnp.concatenate([scores[0] + causal] + scores[1:], 1)
         largest = jnp.max(scores, -1, keepdims=True)
-        weights = jnp.exp2(scores - largest)
-        denominator = jnp.sum(weights, -1, keepdims=True)
-        summed = dot(weights.astype(jnp.bfloat16), fresh_values[:, shared])
+        weights = jnp.exp2(scores - largest).astype(jnp.bfloat16)
+        wide_values = [jnp.concatenate([ref[:, shared], ones], 1) for ref in value_refs]
+        summed = dot(weights, jnp.concatenate(wide_values, 0))
+        denominator = summed[:, HD : HD + 1]
+        result = summed[:, :HD] / denominator
+        logs = largest + jnp.log2(denominator)
         for turn, one in enumerate(own):
             part = slice(turn * rows, (turn + 1) * rows)
-            old_log = old_logs[:, head * repeat + turn : head * repeat + turn + 1]
-            top = jnp.maximum(old_log, largest[part])
-            old_share = jnp.exp2(old_log - top)
-            share = jnp.exp2(largest[part] - top)
-            total = old_share + share * denominator[part]
-            partial[:, one] = (old_partial[:, one] * old_share + summed[part] * share) / total
-            columns.append(top + jnp.log2(total))
+            partial[:, one] = result[part]
+            columns.append(logs[part])
     stats[...] = stat_rows(columns, rows)
 
 
-def attend_fresh(requests, queries, old, new_keys, new_values):
+def attend_fresh(requests, queries, new_keys, new_values):
     groups = len(new_keys)
     rows = new_keys[0].shape[0]
     width = queries[0].shape[1]
@@ -392,8 +442,7 @@
             jax.ShapeDtypeStruct((rows, width), jnp.float32),
             jax.ShapeDtypeStruct((STAT_ROWS, rows), jnp.float32),
         ],
-        [],
-        [*queries, *old, *new_keys, *new_values],
+        [*queries, *new_keys, *new_values],
         24,
         4 * rows * width * rows * groups,
         rows * width // HD * rows * groups,
@@ -401,13 +450,17 @@
     )
 
 
-def update_kernel(groups, lengths, *refs):
+def update_kernel(groups, *refs):
     key_refs, value_refs, refs = refs[:groups], refs[groups : 2 * groups], refs[2 * groups :]
-    keys, values, keys_updated, values_updated = refs
+    keys, values, lengths_in, keys_updated, values_updated, done, lengths, semaphore = refs
+    number = pltpu.make_async_copy(lengths_in, lengths, semaphore)
+    number.start()
+    keys_updated[...] = keys[...]
+    values_updated[...] = values[...]
+    done[...] = jnp.zeros(done.shape, done.dtype)
+    number.wait()
     request, position_in = place_of(lengths.shape[0])
     rows = key_refs[0].shape[0]
-    keys_updated[...] = keys[...]
-    values_updated[...] = values[...]
     for turn in range(groups):
         source = source_of(position_in, turn, groups)
         first = lengths[request] + source * rows - position_in * keys.shape[0]
@@ -420,18 +473,18 @@
     slab = jax.ShapeDtypeStruct(keys.shape, keys.dtype)
     return call(
         functools.partial(update_kernel, groups),
-        [slab, slab],
-        [lengths],
-        [*new_keys, *new_values, keys, values],
+        [slab, slab, jax.ShapeDtypeStruct((STAT_ROWS, LANES), jnp.float32)],
+        [*new_keys, *new_values, keys, values, lengths],
         20,
         4 * new_keys[0].size * new_keys[0].shape[0] * groups,
         0,
         "update_caches",
         earlier,
-    )
-
-
-def project_kernel(row_at, own_partial, own_stats, *refs):
+        [pltpu.SMEM(lengths.shape, lengths.dtype), pltpu.SemaphoreType.DMA],
+    )
+
+
+def project_kernel(row_at, own_partial, own_stats, fresh_partial, fresh_stats, *refs):
     heads = lax.axis_size("head")
     chips = heads // CORES
     outputs = 3 * chips - 1
@@ -442,7 +495,7 @@
     rows, block_width = near[0].shape
     part = slice(row_at, row_at + rows)
     padding = jnp.zeros((LANES - STAT_ROWS, rows), jnp.float32)
-    stats = [own_stats[:, part]]
+    stats = [own_stats[...], fresh_stats[:, part]]
     for ref in received:
         stats.append(
             sum(
@@ -459,8 +512,9 @@
     for head in range(width // HD):
         own = slice(head * HD, (head + 1) * HD)
         column = slice(head, head + 1)
-        merged = own_partial[part, own] * shares[0][:, column]
-        for ref, share in zip(received, shares[1:]):
+        merged = own_partial[:, own] * shares[0][:, column]
+        merged = merged + fresh_partial[part, own] * shares[1][:, column]
+        for ref, share in zip(received, shares[2:]):
             merged = merged + ref[:rows, own].astype(jnp.float32) * share[:, column]
         attended.append(merged.astype(jnp.bfloat16))
     attended = jnp.concatenate(attended, 1)
@@ -480,7 +534,7 @@
         near[ahead][...] = product(ahead, 0)
 
 
-def project(row_at, rows, own, received, w_out, heads, earlier):
+def project(row_at, rows, own, fresh_part, received, w_out, heads, earlier):
     chips = heads // CORES
     width = w_out.shape[1] // heads
     shape = jax.ShapeDtypeStruct((rows, width), jnp.bfloat16)
@@ -488,8 +542,7 @@
     blocks = call(
         functools.partial(project_kernel, row_at),
         [shape] * chips + [shape] + [half] * (2 * chips - 2),
-        [],
-        [*own, *received, w_out],
+        [*own, *fresh_part, *received, w_out],
         20,
         2 * rows * w_out.size,
         0,
@@ -510,7 +563,6 @@
     return call(
         functools.partial(sum_kernel, 1 + len(far)),
         [jax.ShapeDtypeStruct(near.shape, near.dtype)],
-        [],
         [near, *far],
         8,
         near.size,
@@ -531,10 +583,11 @@
         result[chunk * rows : (chunk + 1) * rows] = total.astype(jnp.bfloat16)
 
 
-def finish(parts):
+def finish(parts, earlier):
     rows, width = parts[0].shape
     shape = jax.ShapeDtypeStruct((CHUNKS * rows, width), jnp.bfloat16)
-    return call(finish_kernel, [shape], [], parts, 8, CHUNKS * rows * width, 0, "finish")[0]
+    flops = CHUNKS * rows * width
+    return call(finish_kernel, [shape], parts, 8, flops, 0, "finish", earlier)[0]
 
 
 def shards(
@@ -558,9 +611,11 @@
     gain = norm_gain.reshape(heads, 1, width)
 
     early = tokens[:chunk_rows]
-    late, *tables, wide_keys, wide_values = prepare(
-        cached_lengths, rope_offsets, tokens, keys_cache, values_cache, groups, rows - chunk_rows
-    )
+    mark = marks(keys_cache.shape[0])
+    late, *tables = rope_tables(
+        tokens, cached_lengths, rope_offsets, groups, rows - chunk_rows, [mark]
+    )
+    wide_keys, wide_values = widen(keys_cache, values_cache, mark, cached_lengths, [late])
     sent = [early, late]
     arrived = [
         [shifted(piece, "seq", turn * requests) for piece in sent] for turn in range(1, groups)
@@ -569,12 +624,12 @@
     def attend_rows(pieces, own, chunk, turn, earlier):
         at = chunk * chunk_rows
         return attend(
-            pieces, gain, w_query, tables, wide_keys, wide_values, own, at if own else 0,
+            pieces, gain, w_query, tables, wide_keys, wide_values, mark, own, at if own else 0,
             chunk_rows, turn * rows + at, earlier,
         )
 
     half = chunk_rows // 2
-    first = [relay([pieces[0]], [chunk_rows, half, half], [late]) for pieces in arrived]
+    first = [relay([pieces[0]], [chunk_rows, half, half], [wide_keys]) for pieces in arrived]
     earlier = [cut[0] for cut in first]
     own_cuts = [
         relay([piece], [rows, half, half, rows - chunk_rows], earlier)
@@ -624,26 +679,25 @@
         pieces = [list(blocks) for blocks in zip(*gathered[turn - 1])]
         new_rows.append(fresh(pieces, gain, w_key, w_value, tables, turn * rows, earlier))
     new_keys, new_values = zip(*new_rows)
-    own_part = attend_fresh(requests, own_queries, own_part, new_keys, new_values)
+    fresh_part = attend_fresh(requests, own_queries, new_keys, new_values)
 
     parts = []
     earlier = before_sums = []
     for chunk in range(CHUNKS):
         nears, fars = project(
-            chunk * chunk_rows, chunk_rows, own_part, received[chunk], w_out, heads, earlier
+            chunk * chunk_rows, chunk_rows, own_part[2 * chunk : 2 * chunk + 2], fresh_part,
+            received[chunk], w_out, heads, earlier,
         )
         fars = [[other_core(part) for part in far] for far in fars]
         earlier = [nears[0]] + before_sums
-        if chunk == 0:
-            keys_updated, values_updated = update(
-                cached_lengths, new_keys, new_values, keys_cache, values_cache, earlier
-            )
-            earlier = [keys_updated]
         sums = [sum_cores(near, far, earlier) for near, far in zip(nears[1:], fars[1:])]
         from_chips = [shifted(one, "head", CORES * k) for k, one in enumerate(sums, 1)]
         parts += [nears[0], *fars[0], *from_chips]
         earlier, before_sums = sums, from_chips
-    return (finish(parts), keys_updated, values_updated)
+    keys_updated, values_updated, done = update(
+        cached_lengths, new_keys, new_values, keys_cache, values_cache, earlier
+    )
+    return (finish(parts, [done]), keys_updated, values_updated)
 
 
 def solution(mesh):

time: 72 us -> 71.1 us (0.987)
  the two profiles are of different devices: /device:TPU:26 before, /device:TPU:0 now
where the time goes in v4:
time: 71.1 us; the launch traced here: 71 us
  Pallas kernels  27.3 us (38%)
  waiting for transfers between devices  26.3 us (37%)
  starting transfers between devices  15.4 us (22%)
  local copies, waits for them, and re-layouts  1.03 us (1%)
  between operations  0.95 us (1%)
    pallas_call x21, Pallas kernels, call(): pl.pallas_call(body, out_shape=out_shape, in_specs=[VMEM] * len(arrays) +...  27.3 us
    ppermute x10, waiting for transfers between devices, shifted(): lax.ppermute(shard, axis, [(i, (i + by) % devices) for i in range(devices)])  24.9 us
    ppermute x10, starting transfers between devices, shifted(): lax.ppermute(shard, axis, [(i, (i + by) % devices) for i in range(devices)])  12.2 us
    ppermute x14, starting transfers between devices, other_core(): return lax.ppermute(shard, 'head', [(i, i ^ 1) for i in range(devices)])  3.15 us
  transfers between devices with their start and end apart: 24, of which 10 were waited for; matrix products, arithmetic and copies ran while one was open for 1% of the time, Pallas kernels for 37%

profile of v4, /device:TPU:0, one launch (start us, length us, event | category | flops | bytes accessed | tf_op | source)
XLA Modules:
  0.0 71.0 jit_solution(11725585088980651774)
XLA Ops:
  0.7 3.0 %collective-permute-start = (bf16[256,768]{1,0:T(8,128)(2,1)}, bf16[256,768]{1,0:T(8,128)(2,1)S(1)}, u32[]{:S(2)}, u32[]{:S(2)}) collective-permute-start(bf16[256,768]{1,0:T(8,128)(2,1)} %refs_0_.9), channel_id=1, source_target_pairs={{0,2},{1,3},{2,0},{3,1},{4,6},{5,7},{6,4},{7,5},{8,10},{9,11},{10,... | collective-permute-start | bytes 1179656 | tf_op jit(solution)/shard_map/ppermute | solution.py:32
  3.7 1.0 %slice.3 = bf16[128,768]{1,0:T(8,128)(2,1)S(1)} slice(bf16[256,768]{1,0:T(8,128)(2,1)} %refs_0_.9), slice={[0:128], [0:768]} | slice | bytes 393216 | tf_op jit(solution)/shard_map/slice | solution.py:613
  4.7 2.7 %collective-permute-start.1 = (bf16[128,768]{1,0:T(8,128)(2,1)S(1)}, bf16[128,768]{1,0:T(8,128)(2,1)S(1)}, u32[]{:S(2)}, u32[]{:S(2)}) collective-permute-start(bf16[128,768]{1,0:T(8,128)(2,1)S(1)} %slice.3), channel_id=1, source_target_pairs={{0,16},{4,20},{8,24},{12,28},{16,0},{20,4},{24,8},{28,12},{1,17},{... | collective-permute-start | bytes 589832 | tf_op jit(solution)/shard_map/ppermute | solution.py:32
  7.4 1.6 %rope_tables.1 = (bf16[128,768]{1,0:T(8,128)(2,1)S(1)}, f32[512,128]{1,0:T(8,128)S(1)}, f32[512,128]{1,0:T(8,128)S(1)}) custom-call(bf16[256,768]{1,0:T(8,128)(2,1)S(1)} %copy-done.2, s32[4]{0:T(128)S(1)} %copy-done.6, s32[4]{0:T(128)S(1)} %copy-done.7, bf16[2048,128]{1,0:T(8,128)(2,1)S(1)} %marks.1.refs_3_.refs_2_.refs_11_.refs_10_.refs_12_), custom_call_target="tpu_custom_call" | custom-call | flops 1000000000 | bytes 22282 | tf_op jit(solution)/shard_map/rope_tables/pallas_call | solution.py:76
  9.0 0.4 collective-permute-start.10
  9.4 0.8 %widen_caches.1 = (bf16[2,2048,256]{2,1,0:T(8,128)(2,1)S(1)}, bf16[2,2048,256]{2,1,0:T(8,128)(2,1)S(1)}) custom-call(bf16[2048,256]{1,0:T(8,128)(2,1)S(1)} %copy-done.3, bf16[2048,256]{1,0:T(8,128)(2,1)S(1)} %copy-done.4, bf16[2048,128]{1,0:T(8,128)(2,1)S(1)} %marks.1.refs_3_.refs_2_.refs_11_.refs_10_.refs_12_, s32[4]{0:T(128)S(1)} %copy-done.6, ...), custom_call_target="tpu_custom_call" | custom-call | flops 1000000000 | bytes 136315 | tf_op jit(solution)/shard_map/widen_caches/pallas_call | solution.py:76
  10.2 11.5 %collective-permute-done.1.refs_0_ = bf16[128,768]{1,0:T(8,128)(2,1)S(1)} collective-permute-done((bf16[128,768]{1,0:T(8,128)(2,1)S(1)}, bf16[128,768]{1,0:T(8,128)(2,1)S(1)}, u32[]{:S(2)}, u32[]{:S(2)}) %collective-permute-start.1) | collective-permute-done | bytes 196640 | tf_op jit(solution)/shard_map/ppermute | solution.py:32
  21.8 0.1 relay.6
  21.9 0.1 collective-permute-start.3
  21.9 0.5 collective-permute-start.4
  22.4 0.2 collective-permute-start.6
  22.7 1.8 %collective-permute-start.7 = (bf16[64,768]{1,0:T(8,128)(2,1)S(1)}, bf16[64,768]{1,0:T(8,128)(2,1)S(1)}, u32[]{:S(2)}, u32[]{:S(2)}) collective-permute-start(bf16[64,768]{1,0:T(8,128)(2,1)S(1)} %get-tuple-element.54), channel_id=1, source_target_pairs={{0,2},{1,3},{2,0},{3,1},{4,6},{5,7},{6,4},{7,5},{8,10},{9,11},{10,... | collective-permute-start | bytes 294920 | tf_op jit(solution)/shard_map/ppermute | solution.py:32
  24.5 0.5 collective-permute-start.5
  25.0 3.5 %attend_own.2 = (f32[128,768]{1,0:T(8,128)S(1)}, f32[8,128]{1,0:T(8,128)S(1)}, bf16[128,768]{1,0:T(8,128)(2,1)S(1)}) custom-call(bf16[256,768]{1,0:T(8,128)(2,1)S(1)} %copy-done.2, bf16[256,768]{1,0:T(8,128)(2,1)S(1)} %get-tuple-element.43.refs_1_, bf16[256,768]{1,0:T(8,128)(2,1)S(1)} %collective-permute-done.2.refs_2_, ...), custom_call_target="tpu_custom_call" | custom-call | flops 44291848 | bytes 238878 | tf_op jit(solution)/shard_map/attend_own/pallas_call | solution.py:76
  28.6 0.8 %collective-permute-done.7.refs_1_ = bf16[64,768]{1,0:T(8,128)(2,1)S(1)} collective-permute-done((bf16[64,768]{1,0:T(8,128)(2,1)S(1)}, bf16[64,768]{1,0:T(8,128)(2,1)S(1)}, u32[]{:S(2)}, u32[]{:S(2)}) %collective-permute-start.7) | collective-permute-done | bytes 98336 | tf_op jit(solution)/shard_map/ppermute | solution.py:32
  29.3 0.1 collective-permute-start.9
  29.5 0.3 collective-permute-start.11
  29.8 0.3 collective-permute-start.12
  30.1 1.1 %fresh_kv.2 = (bf16[256,256]{1,0:T(8,128)(2,1)S(1)}, bf16[256,256]{1,0:T(8,128)(2,1)S(1)}) custom-call(bf16[256,768]{1,0:T(8,128)(2,1)S(1)} %copy-done.2, bf16[256,768]{1,0:T(8,128)(2,1)S(1)} %get-tuple-element.43.refs_1_, bf16[256,768]{1,0:T(8,128)(2,1)S(1)} %collective-permute-done.2.refs_2_, bf16[64,768]{1,0:T(8,128)(2,1)S(1)} %collective-permute-done.3.refs_3_, ...), custom_call_target="tpu_custom_call" | custom-call | flops 16106127 | bytes 110346 | tf_op jit(solution)/shard_map/fresh_kv/pallas_call | solution.py:76
  31.2 3.5 %attend_partner.2.refs_1_.refs_13_ = bf16[144,768]{1,0:T(8,128)(2,1)S(1)} custom-call(bf16[128,768]{1,0:T(8,128)(2,1)S(1)} %get-tuple-element.42.refs_1_.refs_12_.refs_0_, bf16[128,768]{1,0:T(8,128)(2,1)S(1)} %relay.7.refs_2_.refs_1_, bf16[128,768]{1,0:T(8,128)(2,1)S(1)} %collective-permute-done.8.refs_2_.refs_4_, ...), custom_call_target="tpu_custom_call" | custom-call | flops 44291848 | bytes 219627 | tf_op jit(solution)/shard_map/attend_partner/pallas_call | solution.py:76
  34.8 2.1 %collective-permute-done.11.refs_0_ = bf16[128,768]{1,0:T(8,128)(2,1)S(1)} collective-permute-done((bf16[128,768]{1,0:T(8,128)(2,1)S(1)}, bf16[128,768]{1,0:T(8,128)(2,1)S(1)}, u32[]{:S(2)}, u32[]{:S(2)}) %collective-permute-start.11) | collective-permute-done | bytes 196640 | tf_op jit(solution)/shard_map/ppermute | solution.py:32
  36.8 0.1 collective-permute-start.13
  36.9 0.1 collective-permute-start.14
  37.0 3.7 %attend_own.3 = (f32[128,768]{1,0:T(8,128)S(1)}, f32[8,128]{1,0:T(8,128)S(1)}, bf16[128,768]{1,0:T(8,128)(2,1)S(1)}) custom-call(bf16[256,768]{1,0:T(8,128)(2,1)S(1)} %copy-done.2, bf16[256,768]{1,0:T(8,128)(2,1)S(1)} %get-tuple-element.43.refs_1_, bf16[256,768]{1,0:T(8,128)(2,1)S(1)} %collective-permute-done.2.refs_2_, ...), custom_call_target="tpu_custom_call" | custom-call | flops 44291848 | bytes 242810 | tf_op jit(solution)/shard_map/attend_own/pallas_call | solution.py:76
  40.7 3.5 %attend_partner.3.refs_13_ = bf16[144,768]{1,0:T(8,128)(2,1)S(1)} custom-call(bf16[128,768]{1,0:T(8,128)(2,1)S(1)} %relay.8.refs_11_.refs_0_.refs_1_, bf16[128,768]{1,0:T(8,128)(2,1)S(1)} %relay.9.refs_14_.refs_1_.refs_3_, bf16[128,768]{1,0:T(8,128)(2,1)S(1)} %collective-permute-done.12.refs_2_.refs_5_, ...), custom_call_target="tpu_custom_call" | custom-call | flops 44291848 | bytes 219627 | tf_op jit(solution)/shard_map/attend_partner/pallas_call | solution.py:76
  44.3 2.9 %collective-permute-start.19 = (bf16[144,768]{1,0:T(8,128)(2,1)S(1)}, bf16[144,768]{1,0:T(8,128)(2,1)S(1)}, u32[]{:S(2)}, u32[]{:S(2)}) collective-permute-start(bf16[144,768]{1,0:T(8,128)(2,1)S(1)} %attend_partner.3.refs_13_), channel_id=1, source_target_pairs={{0,16},{4,20},{8,24},{12,28},{16,0},{20,4},{24,8},{28,12},{1,17},{... | collective-permute-start | bytes 663560 | tf_op jit(solution)/shard_map/ppermute | solution.py:32
  47.2 1.1 %fresh_kv.3 = (bf16[256,256]{1,0:T(8,128)(2,1)S(1)}, bf16[256,256]{1,0:T(8,128)(2,1)S(1)}) custom-call(bf16[128,768]{1,0:T(8,128)(2,1)S(1)} %get-tuple-element.42.refs_1_.refs_12_.refs_0_, bf16[128,768]{1,0:T(8,128)(2,1)S(1)} %relay.8.refs_11_.refs_0_.refs_1_, bf16[128,768]{1,0:T(8,128)(2,1)S(1)} %relay.7.refs_2_.refs_1_, ...), custom_call_target="tpu_custom_call" | custom-call | flops 16106127 | bytes 110346 | tf_op jit(solution)/shard_map/fresh_kv/pallas_call | solution.py:76
  48.3 2.3 %attend_fresh.1 = (f32[256,768]{1,0:T(8,128)S(1)}, f32[8,256]{1,0:T(8,128)S(1)}) custom-call(bf16[128,768]{1,0:T(8,128)(2,1)S(1)} %get-tuple-element.51.refs_2_.refs_1_.refs_0_, bf16[128,768]{1,0:T(8,128)(2,1)S(1)} %get-tuple-element.56.refs_11_.refs_1_, bf16[256,256]{1,0:T(8,128)(2,1)S(1)} %get-tuple-element.55.refs_11_.refs_2_.refs_0_, ...), custom_call_target="tpu_custom_call" | custom-call | flops 8053063 | bytes 34242 | tf_op jit(solution)/shard_map/attend_fresh/pallas_call | solution.py:76
  50.6 0.2 collective-permute-done.14.refs_4_
  50.8 1.4 %combine_project.2 = (bf16[128,768]{1,0:T(8,128)(2,1)S(1)}, bf16[128,768]{1,0:T(8,128)(2,1)S(1)}, bf16[128,768]{1,0:T(8,128)(2,1)S(1)}, bf16[128,384]{1,0:T(8,128)(2,1)S(1)}, bf16[128,384]{1,0:T(8,128)(2,1)S(1)}) custom-call(f32[128,768]{1,0:T(8,128)S(1)} %get-tuple-element.49.refs_0_, f32[8,128]{1,0:T(8,128)S(1)} %get-tuple-element.50.refs_1_, ...), custom_call_target="tpu_custom_call" | custom-call | flops 12079595 | bytes 138362 | tf_op jit(solution)/shard_map/combine_project/pallas_call | solution.py:76
  52.3 0.1 collective-permute-start.16
  52.3 0.5 collective-permute-start.17
  52.8 0.8 %collective-permute-done.16.refs_1_ = bf16[128,384]{1,0:T(8,128)(2,1)S(1)} collective-permute-done((bf16[128,384]{1,0:T(8,128)(2,1)S(1)}, bf16[128,384]{1,0:T(8,128)(2,1)S(1)}, u32[]{:S(2)}, u32[]{:S(2)}) %collective-permute-start.16) | collective-permute-done | bytes 98336 | tf_op jit(solution)/shard_map/ppermute | solution.py:37
  53.6 0.2 collective-permute-done.17.refs_2_
  53.8 0.1 sum_cores.2.refs_6_
  53.8 0.4 collective-permute-start.18
  54.2 5.7 %collective-permute-done.19.refs_4_ = bf16[144,768]{1,0:T(8,128)(2,1)S(1)} collective-permute-done((bf16[144,768]{1,0:T(8,128)(2,1)S(1)}, bf16[144,768]{1,0:T(8,128)(2,1)S(1)}, u32[]{:S(2)}, u32[]{:S(2)}) %collective-permute-start.19) | collective-permute-done | bytes 221216 | tf_op jit(solution)/shard_map/ppermute | solution.py:32
  59.9 1.4 %combine_project.3 = (bf16[128,768]{1,0:T(8,128)(2,1)S(1)}, bf16[128,768]{1,0:T(8,128)(2,1)S(1)}, bf16[128,768]{1,0:T(8,128)(2,1)S(1)}, bf16[128,384]{1,0:T(8,128)(2,1)S(1)}, bf16[128,384]{1,0:T(8,128)(2,1)S(1)}) custom-call(f32[128,768]{1,0:T(8,128)S(1)} %get-tuple-element.67.refs_0_, f32[8,128]{1,0:T(8,128)S(1)} %get-tuple-element.68.refs_1_, ...), custom_call_target="tpu_custom_call" | custom-call | flops 12079595 | bytes 138362 | tf_op jit(solution)/shard_map/combine_project/pallas_call | solution.py:76
  61.3 0.1 collective-permute-start.21
  61.4 0.5 collective-permute-start.22
  61.9 0.1 collective-permute-start.15
  61.9 0.4 collective-permute-start.20
  62.4 0.3 collective-permute-done.21.refs_1_
  62.7 0.2 collective-permute-done.22.refs_2_
  62.9 0.4 collective-permute-start.23
  63.2 2.2 %update_caches.1 = (bf16[2048,256]{1,0:T(8,128)(2,1)}, bf16[2048,256]{1,0:T(8,128)(2,1)}, f32[8,128]{1,0:T(8,128)S(1)}) custom-call(bf16[256,256]{1,0:T(8,128)(2,1)S(1)} %get-tuple-element.55.refs_11_.refs_2_.refs_0_, bf16[256,256]{1,0:T(8,128)(2,1)S(1)} %get-tuple-element.57.refs_3_.refs_1_, bf16[256,256]{1,0:T(8,128)(2,1)S(1)} %get-tuple-element.58.refs_4_.refs_2_, ...), custom_call_target="tpu_custom_call" | custom-call | flops 2684354 | bytes 94454 | tf_op jit(solution)/shard_map/update_caches/pallas_call | solution.py:76
  65.4 4.7 %collective-permute-done.23.refs_5_ = bf16[128,768]{1,0:T(8,128)(2,1)S(1)} collective-permute-done((bf16[128,768]{1,0:T(8,128)(2,1)S(1)}, bf16[128,768]{1,0:T(8,128)(2,1)S(1)}, u32[]{:S(2)}, u32[]{:S(2)}) %collective-permute-start.23) | collective-permute-done | bytes 196640 | tf_op jit(solution)/shard_map/ppermute | solution.py:32
  70.1 0.9 %finish.1 = bf16[256,768]{1,0:T(8,128)(2,1)} custom-call(bf16[128,768]{1,0:T(8,128)(2,1)S(1)} %get-tuple-element.62.refs_3_.refs_0_, bf16[128,768]{1,0:T(8,128)(2,1)S(1)} %collective-permute-done.15.refs_1_, bf16[128,768]{1,0:T(8,128)(2,1)S(1)} %collective-permute-done.18.refs_4_.refs_2_, bf16[128,768]{1,0:T(8,128)(2,1)S(1)} %get-tuple-element.69.refs_3_, ...), custom_call_target="tpu_custom_call" | custom-call | flops 3932 | bytes 31457 | tf_op jit(solution)/shard_map/finish/pallas_call | solution.py:76
  (48 shorter events, 0.3 us)
Async XLA Ops:
  0.6 6.7 %copy-start.2 = (bf16[256,768]{1,0:T(8,128)(2,1)S(1)}, bf16[256,768]{1,0:T(8,128)(2,1)}, u32[]{:S(2)}) copy-start(bf16[256,768]{1,0:T(8,128)(2,1)} %refs_0_.9) | copy-start | bytes 1179652
  0.6 6.7 %copy-start.6 = (s32[4]{0:T(128)S(1)}, s32[4]{0:T(128)}, u32[]{:S(2)}) copy-start(s32[4]{0:T(128)} %refs_6_.3) | copy-start | bytes 52
  0.7 6.7 %copy-start.7 = (s32[4]{0:T(128)S(1)}, s32[4]{0:T(128)}, u32[]{:S(2)}) copy-start(s32[4]{0:T(128)} %refs_2_.1) | copy-start | bytes 52
  0.7 21.1 %collective-permute-start = (bf16[256,768]{1,0:T(8,128)(2,1)}, bf16[256,768]{1,0:T(8,128)(2,1)S(1)}, u32[]{:S(2)}, u32[]{:S(2)}) collective-permute-start(bf16[256,768]{1,0:T(8,128)(2,1)} %refs_0_.9), channel_id=1, source_target_pairs={{0,2},{1,3},{2,0},{3,1},{4,6},{5,7},{6,4},{7,5},{8,10},{9,11},{10,... | collective-permute-start | bytes 1179656 | tf_op jit(solution)/shard_map/ppermute | solution.py:32
  3.7 19.0 %collective-permute-start.2 = (bf16[256,768]{1,0:T(8,128)(2,1)}, bf16[256,768]{1,0:T(8,128)(2,1)S(1)}, u32[]{:S(2)}, u32[]{:S(2)}) collective-permute-start(bf16[256,768]{1,0:T(8,128)(2,1)} %refs_0_.9), channel_id=1, source_target_pairs={{0,1},{1,0},{2,3},{3,2},{4,5},{5,4},{6,7},{7,6},{8,9},{9,8},{10,11... | collective-permute-start | bytes 1179656 | tf_op jit(solution)/shard_map/ppermute | solution.py:37
  4.7 17.1 %collective-permute-start.1 = (bf16[128,768]{1,0:T(8,128)(2,1)S(1)}, bf16[128,768]{1,0:T(8,128)(2,1)S(1)}, u32[]{:S(2)}, u32[]{:S(2)}) collective-permute-start(bf16[128,768]{1,0:T(8,128)(2,1)S(1)} %slice.3), channel_id=1, source_target_pairs={{0,16},{4,20},{8,24},{12,28},{16,0},{20,4},{24,8},{28,12},{1,17},{... | collective-permute-start | bytes 589832 | tf_op jit(solution)/shard_map/ppermute | solution.py:32
  7.3 17.7 %slice-start = ((s8[4718592]{0:T(1024)(128)(4,1)}), s8[4194304]{0:T(1024)(128)(4,1)S(1)}, s32[]{:S(2)}) async-start(s8[4718592]{0:T(1024)(128)(4,1)} %bitcast.1), calls=%async_computation | async-start | bytes 8388608
  7.4 2.0 %copy-start.3 = (bf16[2048,256]{1,0:T(8,128)(2,1)S(1)}, bf16[2048,256]{1,0:T(8,128)(2,1)}, u32[]{:S(2)}) copy-start(bf16[2048,256]{1,0:T(8,128)(2,1)} %refs_4_.1) | copy-start | bytes 3145732
  7.4 2.0 %copy-start.4 = (bf16[2048,256]{1,0:T(8,128)(2,1)S(1)}, bf16[2048,256]{1,0:T(8,128)(2,1)}, u32[]{:S(2)}) copy-start(bf16[2048,256]{1,0:T(8,128)(2,1)} %refs_5_.9) | copy-start | bytes 3145732
  7.4 17.6 %slice-start.1 = ((s8[4718592]{0:T(1024)(128)(4,1)}), s8[524288]{0:T(1024)(128)(4,1)S(1)}, s32[]{:S(2)}) async-start(s8[4718592]{0:T(1024)(128)(4,1)} %bitcast.1), calls=%async_computation.1 | async-start | bytes 1048576
  9.0 20.4 %collective-permute-start.10 = (bf16[128,768]{1,0:T(8,128)(2,1)S(1)}, bf16[128,768]{1,0:T(8,128)(2,1)S(1)}, u32[]{:S(2)}, u32[]{:S(2)}) collective-permute-start(bf16[128,768]{1,0:T(8,128)(2,1)S(1)} %get-tuple-element.40.refs_4_), channel_id=1, source_target_pairs={{0,16},{4,20},{8,24},{12,28},{16,0},{20,4},{24,8},{28,12},{1,17},{... | collective-permute-start | bytes 589832 | tf_op jit(solution)/shard_map/ppermute | solution.py:32
  10.2 14.8 %copy-start.5 = (f32[3072]{0:T(1024)S(1)}, f32[3072]{0:T(1024)}, u32[]{:S(2)}) copy-start(f32[3072]{0:T(1024)} %param.11) | copy-start | bytes 36868
  21.9 2.6 %collective-permute-start.3 = (bf16[64,768]{1,0:T(8,128)(2,1)S(1)}, bf16[64,768]{1,0:T(8,128)(2,1)S(1)}, u32[]{:S(2)}, u32[]{:S(2)}) collective-permute-start(bf16[64,768]{1,0:T(8,128)(2,1)S(1)} %get-tuple-element.44), channel_id=1, source_target_pairs={{0,1},{1,0},{2,3},{3,2},{4,5},{5,4},{6,7},{7,6},{8,9},{9,8},{10,11... | collective-permute-start | bytes 294920 | tf_op jit(solution)/shard_map/ppermute | solution.py:37
  21.9 2.5 %collective-permute-start.4 = (bf16[64,768]{1,0:T(8,128)(2,1)S(1)}, bf16[64,768]{1,0:T(8,128)(2,1)S(1)}, u32[]{:S(2)}, u32[]{:S(2)}) collective-permute-start(bf16[64,768]{1,0:T(8,128)(2,1)S(1)} %get-tuple-element.45), channel_id=1, source_target_pairs={{0,1},{1,0},{2,3},{3,2},{4,5},{5,4},{6,7},{7,6},{8,9},{9,8},{10,11... | collective-permute-start | bytes 294920 | tf_op jit(solution)/shard_map/ppermute | solution.py:37
  22.4 6.1 %collective-permute-start.6 = (bf16[64,768]{1,0:T(8,128)(2,1)S(1)}, bf16[64,768]{1,0:T(8,128)(2,1)S(1)}, u32[]{:S(2)}, u32[]{:S(2)}) collective-permute-start(bf16[64,768]{1,0:T(8,128)(2,1)S(1)} %get-tuple-element.53), channel_id=1, source_target_pairs={{0,2},{1,3},{2,0},{3,1},{4,6},{5,7},{6,4},{7,5},{8,10},{9,11},{10,... | collective-permute-start | bytes 294920 | tf_op jit(solution)/shard_map/ppermute | solution.py:32
  22.7 6.6 %collective-permute-start.7 = (bf16[64,768]{1,0:T(8,128)(2,1)S(1)}, bf16[64,768]{1,0:T(8,128)(2,1)S(1)}, u32[]{:S(2)}, u32[]{:S(2)}) collective-permute-start(bf16[64,768]{1,0:T(8,128)(2,1)S(1)} %get-tuple-element.54), channel_id=1, source_target_pairs={{0,2},{1,3},{2,0},{3,1},{4,6},{5,7},{6,4},{7,5},{8,10},{9,11},{10,... | collective-permute-start | bytes 294920 | tf_op jit(solution)/shard_map/ppermute | solution.py:32
  24.5 6.7 %collective-permute-start.8 = (bf16[128,768]{1,0:T(8,128)(2,1)S(1)}, bf16[128,768]{1,0:T(8,128)(2,1)S(1)}, u32[]{:S(2)}, u32[]{:S(2)}) collective-permute-start(bf16[128,768]{1,0:T(8,128)(2,1)S(1)} %get-tuple-element.42.refs_1_.refs_12_.refs_0_), channel_id=1, source_target_pairs={{0,1},{1,0},{2,3},{3,2},{4,5},{5,4},{6,7},{7,6},{8,9},{9,8},{10,11... | collective-permute-start | bytes 589832 | tf_op jit(solution)/shard_map/ppermute | solution.py:37
  24.5 5.6 %collective-permute-start.5 = (bf16[128,768]{1,0:T(8,128)(2,1)S(1)}, bf16[128,768]{1,0:T(8,128)(2,1)S(1)}, u32[]{:S(2)}, u32[]{:S(2)}) collective-permute-start(bf16[128,768]{1,0:T(8,128)(2,1)S(1)} %get-tuple-element.52), channel_id=1, source_target_pairs={{0,1},{1,0},{2,3},{3,2},{4,5},{5,4},{6,7},{7,6},{8,9},{9,8},{10,11... | collective-permute-start | bytes 589832 | tf_op jit(solution)/shard_map/ppermute | solution.py:37
  25.0 5.1 %copy-start = (bf16[3072,256]{1,0:T(8,128)(2,1)S(1)}, bf16[3072,256]{1,0:T(8,128)(2,1)}, u32[]{:S(2)}) copy-start(bf16[3072,256]{1,0:T(8,128)(2,1)} %refs_9_.1) | copy-start | bytes 4718596
  25.0 5.1 %copy-start.1 = (bf16[3072,256]{1,0:T(8,128)(2,1)S(1)}, bf16[3072,256]{1,0:T(8,128)(2,1)}, u32[]{:S(2)}) copy-start(bf16[3072,256]{1,0:T(8,128)(2,1)} %refs_10_.1) | copy-start | bytes 4718596
  29.3 1.9 %collective-permute-start.9 = (bf16[128,768]{1,0:T(8,128)(2,1)S(1)}, bf16[128,768]{1,0:T(8,128)(2,1)S(1)}, u32[]{:S(2)}, u32[]{:S(2)}) collective-permute-start(bf16[128,768]{1,0:T(8,128)(2,1)S(1)} %relay.7.refs_2_.refs_1_), channel_id=1, source_target_pairs={{0,1},{1,0},{2,3},{3,2},{4,5},{5,4},{6,7},{7,6},{8,9},{9,8},{10,11... | collective-permute-start | bytes 589832 | tf_op jit(solution)/shard_map/ppermute | solution.py:37
  29.5 7.4 %collective-permute-start.11 = (bf16[128,768]{1,0:T(8,128)(2,1)S(1)}, bf16[128,768]{1,0:T(8,128)(2,1)S(1)}, u32[]{:S(2)}, u32[]{:S(2)}) collective-permute-start(bf16[128,768]{1,0:T(8,128)(2,1)S(1)} %relay.8.refs_11_.refs_0_.refs_1_), channel_id=1, source_target_pairs={{0,2},{1,3},{2,0},{3,1},{4,6},{5,7},{6,4},{7,5},{8,10},{9,11},{10,... | collective-permute-start | bytes 589832 | tf_op jit(solution)/shard_map/ppermute | solution.py:32
  29.8 10.9 %collective-permute-start.12 = (bf16[128,768]{1,0:T(8,128)(2,1)S(1)}, bf16[128,768]{1,0:T(8,128)(2,1)S(1)}, u32[]{:S(2)}, u32[]{:S(2)}) collective-permute-start(bf16[128,768]{1,0:T(8,128)(2,1)S(1)} %relay.8.refs_11_.refs_0_.refs_1_), channel_id=1, source_target_pairs={{0,1},{1,0},{2,3},{3,2},{4,5},{5,4},{6,7},{7,6},{8,9},{9,8},{10,11... | collective-permute-start | bytes 589832 | tf_op jit(solution)/shard_map/ppermute | solution.py:37
  36.8 3.9 %collective-permute-start.13 = (bf16[128,768]{1,0:T(8,128)(2,1)S(1)}, bf16[128,768]{1,0:T(8,128)(2,1)S(1)}, u32[]{:S(2)}, u32[]{:S(2)}) collective-permute-start(bf16[128,768]{1,0:T(8,128)(2,1)S(1)} %relay.9.refs_14_.refs_1_.refs_3_), channel_id=1, source_target_pairs={{0,1},{1,0},{2,3},{3,2},{4,5},{5,4},{6,7},{7,6},{8,9},{9,8},{10,11... | collective-permute-start | bytes 589832 | tf_op jit(solution)/shard_map/ppermute | solution.py:37
  36.9 13.9 %collective-permute-start.14 = (bf16[144,768]{1,0:T(8,128)(2,1)S(1)}, bf16[144,768]{1,0:T(8,128)(2,1)S(1)}, u32[]{:S(2)}, u32[]{:S(2)}) collective-permute-start(bf16[144,768]{1,0:T(8,128)(2,1)S(1)} %attend_partner.2.refs_1_.refs_13_), channel_id=1, source_target_pairs={{0,16},{4,20},{8,24},{12,28},{16,0},{20,4},{24,8},{28,12},{1,17},{... | collective-permute-start | bytes 663560 | tf_op jit(solution)/shard_map/ppermute | solution.py:32
  40.7 10.1 %slice-start.2 = ((s8[4718592]{0:T(1024)(128)(4,1)}), s8[4194304]{0:T(1024)(128)(4,1)S(1)}, s32[]{:S(2)}) async-start(s8[4718592]{0:T(1024)(128)(4,1)} %bitcast.3), calls=%async_computation.2 | async-start | bytes 8388608
  40.7 10.1 %slice-start.3 = ((s8[4718592]{0:T(1024)(128)(4,1)}), s8[524288]{0:T(1024)(128)(4,1)S(1)}, s32[]{:S(2)}) async-start(s8[4718592]{0:T(1024)(128)(4,1)} %bitcast.3), calls=%async_computation.3 | async-start | bytes 1048576
  44.3 15.6 %collective-permute-start.19 = (bf16[144,768]{1,0:T(8,128)(2,1)S(1)}, bf16[144,768]{1,0:T(8,128)(2,1)S(1)}, u32[]{:S(2)}, u32[]{:S(2)}) collective-permute-start(bf16[144,768]{1,0:T(8,128)(2,1)S(1)} %attend_partner.3.refs_13_), channel_id=1, source_target_pairs={{0,16},{4,20},{8,24},{12,28},{16,0},{20,4},{24,8},{28,12},{1,17},{... | collective-permute-start | bytes 663560 | tf_op jit(solution)/shard_map/ppermute | solution.py:32
  52.3 1.4 %collective-permute-start.16 = (bf16[128,384]{1,0:T(8,128)(2,1)S(1)}, bf16[128,384]{1,0:T(8,128)(2,1)S(1)}, u32[]{:S(2)}, u32[]{:S(2)}) collective-permute-start(bf16[128,384]{1,0:T(8,128)(2,1)S(1)} %get-tuple-element.65), channel_id=1, source_target_pairs={{0,1},{1,0},{2,3},{3,2},{4,5},{5,4},{6,7},{7,6},{8,9},{9,8},{10,11... | collective-permute-start | bytes 294920 | tf_op jit(solution)/shard_map/ppermute | solution.py:37
  52.3 1.4 %collective-permute-start.17 = (bf16[128,384]{1,0:T(8,128)(2,1)S(1)}, bf16[128,384]{1,0:T(8,128)(2,1)S(1)}, u32[]{:S(2)}, u32[]{:S(2)}) collective-permute-start(bf16[128,384]{1,0:T(8,128)(2,1)S(1)} %get-tuple-element.66), channel_id=1, source_target_pairs={{0,1},{1,0},{2,3},{3,2},{4,5},{5,4},{6,7},{7,6},{8,9},{9,8},{10,11... | collective-permute-start | bytes 294920 | tf_op jit(solution)/shard_map/ppermute | solution.py:37
  53.8 8.5 %collective-permute-start.18 = (bf16[128,768]{1,0:T(8,128)(2,1)S(1)}, bf16[128,768]{1,0:T(8,128)(2,1)S(1)}, u32[]{:S(2)}, u32[]{:S(2)}) collective-permute-start(bf16[128,768]{1,0:T(8,128)(2,1)S(1)} %sum_cores.2.refs_6_), channel_id=1, source_target_pairs={{0,2},{1,3},{2,0},{3,1},{4,6},{5,7},{6,4},{7,5},{8,10},{9,11},{10,... | collective-permute-start | bytes 589832 | tf_op jit(solution)/shard_map/ppermute | solution.py:32
  61.3 1.4 %collective-permute-start.21 = (bf16[128,384]{1,0:T(8,128)(2,1)S(1)}, bf16[128,384]{1,0:T(8,128)(2,1)S(1)}, u32[]{:S(2)}, u32[]{:S(2)}) collective-permute-start(bf16[128,384]{1,0:T(8,128)(2,1)S(1)} %get-tuple-element.72), channel_id=1, source_target_pairs={{0,1},{1,0},{2,3},{3,2},{4,5},{5,4},{6,7},{7,6},{8,9},{9,8},{10,11... | collective-permute-start | bytes 294920 | tf_op jit(solution)/shard_map/ppermute | solution.py:37
  61.4 1.4 %collective-permute-start.22 = (bf16[128,384]{1,0:T(8,128)(2,1)S(1)}, bf16[128,384]{1,0:T(8,128)(2,1)S(1)}, u32[]{:S(2)}, u32[]{:S(2)}) collective-permute-start(bf16[128,384]{1,0:T(8,128)(2,1)S(1)} %get-tuple-element.73), channel_id=1, source_target_pairs={{0,1},{1,0},{2,3},{3,2},{4,5},{5,4},{6,7},{7,6},{8,9},{9,8},{10,11... | collective-permute-start | bytes 294920 | tf_op jit(solution)/shard_map/ppermute | solution.py:37
  61.9 3.5 %collective-permute-start.15 = (bf16[128,768]{1,0:T(8,128)(2,1)S(1)}, bf16[128,768]{1,0:T(8,128)(2,1)S(1)}, u32[]{:S(2)}, u32[]{:S(2)}) collective-permute-start(bf16[128,768]{1,0:T(8,128)(2,1)S(1)} %get-tuple-element.63), channel_id=1, source_target_pairs={{0,1},{1,0},{2,3},{3,2},{4,5},{5,4},{6,7},{7,6},{8,9},{9,8},{10,11... | collective-permute-start | bytes 589832 | tf_op jit(solution)/shard_map/ppermute | solution.py:37
  61.9 3.5 %collective-permute-start.20 = (bf16[128,768]{1,0:T(8,128)(2,1)S(1)}, bf16[128,768]{1,0:T(8,128)(2,1)S(1)}, u32[]{:S(2)}, u32[]{:S(2)}) collective-permute-start(bf16[128,768]{1,0:T(8,128)(2,1)S(1)} %get-tuple-element.70), channel_id=1, source_target_pairs={{0,1},{1,0},{2,3},{3,2},{4,5},{5,4},{6,7},{7,6},{8,9},{9,8},{10,11... | collective-permute-start | bytes 589832 | tf_op jit(solution)/shard_map/ppermute | solution.py:37
  62.9 7.2 %collective-permute-start.23 = (bf16[128,768]{1,0:T(8,128)(2,1)S(1)}, bf16[128,768]{1,0:T(8,128)(2,1)S(1)}, u32[]{:S(2)}, u32[]{:S(2)}) collective-permute-start(bf16[128,768]{1,0:T(8,128)(2,1)S(1)} %sum_cores.3.refs_7_), channel_id=1, source_target_pairs={{0,2},{1,3},{2,0},{3,1},{4,6},{5,7},{6,4},{7,5},{8,10},{9,11},{10,... | collective-permute-start | bytes 589832 | tf_op jit(solution)/shard_map/ppermute | solution.py:32

commit v5 on v4

--- a/solution.py
+++ b/solution.py
@@ -14,7 +14,7 @@
 ROW_TILE = 16
 CORES = 2
 CHUNKS = 2
-COST_WEIGHT = 0.02
+COST_WEIGHT = 0.0005
 FIRST_MICROS = 1
 FLOPS_PER_MICRO = 1_000_000_000
 MIB = 1 << 20
@@ -118,7 +118,7 @@
     return call(mark_kernel, [shape], [], 4, 0, 0, "marks", micros=FIRST_MICROS)[0]
 
 
-def tables_kernel(groups, tokens, lengths_in, offsets_in, late, cosine, sine, *scratch):
+def tables_kernel(groups, lengths_in, offsets_in, cosine, sine, *scratch):
     lengths, offsets, semaphores = scratch
     numbers = [
         pltpu.make_async_copy(lengths_in, lengths, semaphores.at[0]),
@@ -126,8 +126,7 @@
     ]
     for copy in numbers:
         copy.start()
-    rows = tokens.shape[0]
-    late[...] = tokens[rows - late.shape[0] :]
+    rows = cosine.shape[0] // groups
     for copy in numbers:
         copy.wait()
     request, position_in = place_of(lengths.shape[0])
@@ -145,14 +144,12 @@
         sine[part] = jnp.sin(angles) * sign
 
 
-def rope_tables(tokens, lengths, offsets, groups, late_rows, earlier):
-    rows, token_width = tokens.shape
-    late = jax.ShapeDtypeStruct((late_rows, token_width), tokens.dtype)
+def rope_tables(lengths, offsets, groups, rows, earlier):
     table = jax.ShapeDtypeStruct((groups * rows, LANES), jnp.float32)
     return call(
         functools.partial(tables_kernel, groups),
-        [late, table, table],
-        [tokens, lengths, offsets],
+        [table, table],
+        [lengths, offsets],
         12,
         0,
         0,
@@ -612,14 +609,8 @@
 
     early = tokens[:chunk_rows]
     mark = marks(keys_cache.shape[0])
-    late, *tables = rope_tables(
-        tokens, cached_lengths, rope_offsets, groups, rows - chunk_rows, [mark]
-    )
-    wide_keys, wide_values = widen(keys_cache, values_cache, mark, cached_lengths, [late])
-    sent = [early, late]
-    arrived = [
-        [shifted(piece, "seq", turn * requests) for piece in sent] for turn in range(1, groups)
-    ]
+    tables = rope_tables(cached_lengths, rope_offsets, groups, rows, [mark])
+    wide_keys, wide_values = widen(keys_cache, values_cache, mark, cached_lengths, tables[:1])
 
     def attend_rows(pieces, own, chunk, turn, earlier):
         at = chunk * chunk_rows
@@ -629,12 +620,14 @@
         )
 
     half = chunk_rows // 2
-    first = [relay([pieces[0]], [chunk_rows, half, half], [wide_keys]) for pieces in arrived]
+    first = [shifted(early, "seq", turn * requests) for turn in range(1, groups)]
+    from_chips = other_chips(tokens)
+    (late,) = relay([tokens[chunk_rows:]], [rows - chunk_rows], from_chips + [wide_keys])
+    second = [shifted(late, "seq", turn * requests) for turn in range(1, groups)]
+    own_cuts = [relay([piece], [rows, half, half, rows - chunk_rows], [late]) for piece in from_chips]
+    earlier = [cut[0] for cut in own_cuts]
+    first = [relay([piece], [chunk_rows, half, half], earlier) for piece in first]
     earlier = [cut[0] for cut in first]
-    own_cuts = [
-        relay([piece], [rows, half, half, rows - chunk_rows], earlier)
-        for piece in other_chips(tokens)
-    ]
     own_pieces = [[tokens]] + [[cut[0]] for cut in own_cuts] + [[other_core(tokens)]]
     own_pieces += [[other_core(block) for block in cut[1:]] for cut in own_cuts]
     own_early = [
@@ -650,7 +643,7 @@
         along = [cut[0]] + from_chips
         gathered.append([along + [other_core(one) for one in along]])
         earlier = earlier + from_chips
-    second = [relay([pieces[1]], [rows - chunk_rows], earlier)[0] for pieces in arrived]
+    second = [relay([piece], [rows - chunk_rows], earlier)[0] for piece in second]
     new_rows = [fresh(own_pieces, gain, w_key, w_value, tables, 0, second)]
     earlier = [new_rows[0][0]]
     received = [[] for _ in range(CHUNKS)]

time: 71.1 us -> 67.4 us (0.948)
  waiting for transfers between devices: 26.3 us -> 19.2 us
  starting transfers between devices: 15.4 us -> 19 us
    ppermute x10, waiting for transfers between devices: 24.9 us -> 17.8 us  [shifted(): lax.ppermute(shard, axis, [(i, (i + by) % devices) for i in range(devices)])]
    ppermute x10, starting transfers between devices: 12.2 us -> 15.7 us  [shifted(): lax.ppermute(shard, axis, [(i, (i + by) % devices) for i in range(devices)])]
    pallas_call x21 -> x22, Pallas kernels: 27.3 us -> 27 us  [call(): pl.pallas_call(body, out_shape=out_shape, in_specs=[VMEM] * len(arrays) +...]
  transfers between devices with their start and end apart: 24 -> 24, of which waited for: 10 -> 9; matrix products, arithmetic and copies ran while one was open for 1% -> 2% of each run, Pallas kernels for 37% -> 39%
where the time goes in v5:
time: 67.4 us; the launch traced here: 67.2 us
  Pallas kernels  27 us (40%)
  waiting for transfers between devices  19.2 us (28%)
  starting transfers between devices  19 us (28%)
  local copies, waits for them, and re-layouts  1.11 us (2%)
  between operations  0.96 us (1%)
    pallas_call x22, Pallas kernels, call(): pl.pallas_call(body, out_shape=out_shape, in_specs=[VMEM] * len(arrays) +...  27 us
    ppermute x10, waiting for transfers between devices, shifted(): lax.ppermute(shard, axis, [(i, (i + by) % devices) for i in range(devices)])  17.8 us
    ppermute x10, starting transfers between devices, shifted(): lax.ppermute(shard, axis, [(i, (i + by) % devices) for i in range(devices)])  15.7 us
    ppermute x14, starting transfers between devices, other_core(): return lax.ppermute(shard, 'head', [(i, i ^ 1) for i in range(devices)])  3.23 us
    ppermute x14, waiting for transfers between devices, other_core(): return lax.ppermute(shard, 'head', [(i, i ^ 1) for i in range(devices)])  1.4 us
  transfers between devices with their start and end apart: 24, of which 9 were waited for; matrix products, arithmetic and copies ran while one was open for 2% of the time, Pallas kernels for 39%

profile of v5, /device:TPU:0, one launch (start us, length us, event | category | flops | bytes accessed | tf_op | source)
XLA Modules:
  0.0 67.2 jit_solution(4760233372749404064)
XLA Ops:
  0.7 3.0 %collective-permute-start = (bf16[256,768]{1,0:T(8,128)(2,1)}, bf16[256,768]{1,0:T(8,128)(2,1)S(1)}, u32[]{:S(2)}, u32[]{:S(2)}) collective-permute-start(bf16[256,768]{1,0:T(8,128)(2,1)} %refs_0_.9), channel_id=1, source_target_pairs={{0,2},{1,3},{2,0},{3,1},{4,6},{5,7},{6,4},{7,5},{8,10},{9,11},{10,... | collective-permute-start | bytes 1179656 | tf_op jit(solution)/shard_map/ppermute | solution.py:32
  3.7 1.0 %fusion = (bf16[128,768]{1,0:T(8,128)(2,1)S(1)}, bf16[128,768]{1,0:T(8,128)(2,1)S(1)}) fusion(bf16[256,768]{1,0:T(8,128)(2,1)} %refs_0_.9), kind=kLoop, calls=%fused_computation | loop fusion | bytes 786432 | tf_op jit(solution)/shard_map/slice | solution.py:610
  4.7 2.7 %collective-permute-start.4 = (bf16[128,768]{1,0:T(8,128)(2,1)S(1)}, bf16[128,768]{1,0:T(8,128)(2,1)S(1)}, u32[]{:S(2)}, u32[]{:S(2)}) collective-permute-start(bf16[128,768]{1,0:T(8,128)(2,1)S(1)} %get-tuple-element.75), channel_id=1, source_target_pairs={{0,16},{4,20},{8,24},{12,28},{16,0},{20,4},{24,8},{28,12},{1,17},{... | collective-permute-start | bytes 589832 | tf_op jit(solution)/shard_map/ppermute | solution.py:32
  7.5 1.6 %rope_tables.1 = (f32[512,128]{1,0:T(8,128)S(1)}, f32[512,128]{1,0:T(8,128)S(1)}) custom-call(s32[4]{0:T(128)S(1)} %copy-done.6, s32[4]{0:T(128)S(1)} %copy-done.7, bf16[2048,128]{1,0:T(8,128)(2,1)S(1)} %marks.1.refs_2_.refs_11_.refs_10_.refs_12_), custom_call_target="tpu_custom_call" | custom-call | flops 1000000000 | bytes 262 | tf_op jit(solution)/shard_map/rope_tables/pallas_call | solution.py:76
  9.1 0.8 %widen_caches.1 = (bf16[2,2048,256]{2,1,0:T(8,128)(2,1)S(1)}, bf16[2,2048,256]{2,1,0:T(8,128)(2,1)S(1)}) custom-call(bf16[2048,256]{1,0:T(8,128)(2,1)S(1)} %copy-done.3, bf16[2048,256]{1,0:T(8,128)(2,1)S(1)} %copy-done.4, bf16[2048,128]{1,0:T(8,128)(2,1)S(1)} %marks.1.refs_2_.refs_11_.refs_10_.refs_12_, s32[4]{0:T(128)S(1)} %copy-done.6, ...), custom_call_target="tpu_custom_call" | custom-call | flops 1000000000 | bytes 3407 | tf_op jit(solution)/shard_map/widen_caches/pallas_call | solution.py:76
  9.9 3.1 %collective-permute-done.refs_1_.refs_0_ = bf16[256,768]{1,0:T(8,128)(2,1)S(1)} collective-permute-done((bf16[256,768]{1,0:T(8,128)(2,1)}, bf16[256,768]{1,0:T(8,128)(2,1)S(1)}, u32[]{:S(2)}, u32[]{:S(2)}) %collective-permute-start) | collective-permute-done | bytes 393248 | tf_op jit(solution)/shard_map/ppermute | solution.py:32
  13.0 2.9 %collective-permute-start.10 = (bf16[128,768]{1,0:T(8,128)(2,1)S(1)}, bf16[128,768]{1,0:T(8,128)(2,1)S(1)}, u32[]{:S(2)}, u32[]{:S(2)}) collective-permute-start(bf16[128,768]{1,0:T(8,128)(2,1)S(1)} %relay.6.refs_1_), channel_id=1, source_target_pairs={{0,16},{4,20},{8,24},{12,28},{16,0},{20,4},{24,8},{28,12},{1,17},{... | collective-permute-start | bytes 589832 | tf_op jit(solution)/shard_map/ppermute | solution.py:32
  15.9 0.1 relay.7
  16.0 0.1 collective-permute-start.2
  16.0 0.5 collective-permute-start.3
  16.5 5.3 %collective-permute-done.4.refs_0_ = bf16[128,768]{1,0:T(8,128)(2,1)S(1)} collective-permute-done((bf16[128,768]{1,0:T(8,128)(2,1)S(1)}, bf16[128,768]{1,0:T(8,128)(2,1)S(1)}, u32[]{:S(2)}, u32[]{:S(2)}) %collective-permute-start.4) | collective-permute-done | bytes 196640 | tf_op jit(solution)/shard_map/ppermute | solution.py:32
  21.9 0.1 collective-permute-start.6
  21.9 2.0 %collective-permute-start.7 = (bf16[64,768]{1,0:T(8,128)(2,1)S(1)}, bf16[64,768]{1,0:T(8,128)(2,1)S(1)}, u32[]{:S(2)}, u32[]{:S(2)}) collective-permute-start(bf16[64,768]{1,0:T(8,128)(2,1)S(1)} %get-tuple-element.52), channel_id=1, source_target_pairs={{0,2},{1,3},{2,0},{3,1},{4,6},{5,7},{6,4},{7,5},{8,10},{9,11},{10,... | collective-permute-start | bytes 294920 | tf_op jit(solution)/shard_map/ppermute | solution.py:32
  24.0 0.5 collective-permute-start.8
  24.5 3.4 %attend_own.2 = (f32[128,768]{1,0:T(8,128)S(1)}, f32[8,128]{1,0:T(8,128)S(1)}, bf16[128,768]{1,0:T(8,128)(2,1)S(1)}) custom-call(bf16[256,768]{1,0:T(8,128)(2,1)S(1)} %copy-done, bf16[256,768]{1,0:T(8,128)(2,1)S(1)} %get-tuple-element.41.refs_1_, bf16[256,768]{1,0:T(8,128)(2,1)S(1)} %collective-permute-done.1.refs_2_, ...), custom_call_target="tpu_custom_call" | custom-call | flops 1107296 | bytes 5971 | tf_op jit(solution)/shard_map/attend_own/pallas_call | solution.py:76
  28.0 0.1 collective-permute-start.9
  28.1 0.6 collective-permute-start.11
  28.8 1.1 %fresh_kv.2 = (bf16[256,256]{1,0:T(8,128)(2,1)S(1)}, bf16[256,256]{1,0:T(8,128)(2,1)S(1)}) custom-call(bf16[256,768]{1,0:T(8,128)(2,1)S(1)} %copy-done, bf16[256,768]{1,0:T(8,128)(2,1)S(1)} %get-tuple-element.41.refs_1_, bf16[256,768]{1,0:T(8,128)(2,1)S(1)} %collective-permute-done.1.refs_2_, bf16[64,768]{1,0:T(8,128)(2,1)S(1)} %collective-permute-done.2.refs_3_, ...), custom_call_target="tpu_custom_call" | custom-call | flops 402653 | bytes 2758 | tf_op jit(solution)/shard_map/fresh_kv/pallas_call | solution.py:76
  29.9 3.4 %attend_partner.2.refs_1_.refs_13_ = bf16[144,768]{1,0:T(8,128)(2,1)S(1)} custom-call(bf16[128,768]{1,0:T(8,128)(2,1)S(1)} %get-tuple-element.46.refs_12_.refs_0_, bf16[128,768]{1,0:T(8,128)(2,1)S(1)} %relay.9.refs_2_.refs_1_, bf16[128,768]{1,0:T(8,128)(2,1)S(1)} %collective-permute-done.8.refs_2_.refs_4_, ...), custom_call_target="tpu_custom_call" | custom-call | flops 1107296 | bytes 5490 | tf_op jit(solution)/shard_map/attend_partner/pallas_call | solution.py:76
  33.4 0.0 collective-permute-start.14
  33.4 0.3 collective-permute-start.12
  33.7 1.7 %collective-permute-done.11.refs_0_ = bf16[128,768]{1,0:T(8,128)(2,1)S(1)} collective-permute-done((bf16[128,768]{1,0:T(8,128)(2,1)S(1)}, bf16[128,768]{1,0:T(8,128)(2,1)S(1)}, u32[]{:S(2)}, u32[]{:S(2)}) %collective-permute-start.11) | collective-permute-done | bytes 196640 | tf_op jit(solution)/shard_map/ppermute | solution.py:32
  35.5 0.1 collective-permute-start.13
  35.5 3.6 %attend_own.3 = (f32[128,768]{1,0:T(8,128)S(1)}, f32[8,128]{1,0:T(8,128)S(1)}, bf16[128,768]{1,0:T(8,128)(2,1)S(1)}) custom-call(bf16[256,768]{1,0:T(8,128)(2,1)S(1)} %copy-done, bf16[256,768]{1,0:T(8,128)(2,1)S(1)} %get-tuple-element.41.refs_1_, bf16[256,768]{1,0:T(8,128)(2,1)S(1)} %collective-permute-done.1.refs_2_, ...), custom_call_target="tpu_custom_call" | custom-call | flops 1107296 | bytes 6070 | tf_op jit(solution)/shard_map/attend_own/pallas_call | solution.py:76
  39.2 3.4 %attend_partner.3.refs_13_ = bf16[144,768]{1,0:T(8,128)(2,1)S(1)} custom-call(bf16[128,768]{1,0:T(8,128)(2,1)S(1)} %relay.10.refs_11_.refs_0_.refs_1_, bf16[128,768]{1,0:T(8,128)(2,1)S(1)} %relay.11.refs_14_.refs_1_.refs_3_, bf16[128,768]{1,0:T(8,128)(2,1)S(1)} %collective-permute-done.12.refs_2_.refs_5_, ...), custom_call_target="tpu_custom_call" | custom-call | flops 1107296 | bytes 5490 | tf_op jit(solution)/shard_map/attend_partner/pallas_call | solution.py:76
  42.6 1.4 %collective-permute-start.19 = (bf16[144,768]{1,0:T(8,128)(2,1)S(1)}, bf16[144,768]{1,0:T(8,128)(2,1)S(1)}, u32[]{:S(2)}, u32[]{:S(2)}) collective-permute-start(bf16[144,768]{1,0:T(8,128)(2,1)S(1)} %attend_partner.3.refs_13_), channel_id=1, source_target_pairs={{0,16},{4,20},{8,24},{12,28},{16,0},{20,4},{24,8},{28,12},{1,17},{... | collective-permute-start | bytes 663560 | tf_op jit(solution)/shard_map/ppermute | solution.py:32
  44.1 1.1 %fresh_kv.3 = (bf16[256,256]{1,0:T(8,128)(2,1)S(1)}, bf16[256,256]{1,0:T(8,128)(2,1)S(1)}) custom-call(bf16[128,768]{1,0:T(8,128)(2,1)S(1)} %get-tuple-element.46.refs_12_.refs_0_, bf16[128,768]{1,0:T(8,128)(2,1)S(1)} %relay.10.refs_11_.refs_0_.refs_1_, bf16[128,768]{1,0:T(8,128)(2,1)S(1)} %relay.9.refs_2_.refs_1_, ...), custom_call_target="tpu_custom_call" | custom-call | flops 402653 | bytes 2758 | tf_op jit(solution)/shard_map/fresh_kv/pallas_call | solution.py:76
  45.2 2.3 %attend_fresh.1 = (f32[256,768]{1,0:T(8,128)S(1)}, f32[8,256]{1,0:T(8,128)S(1)}) custom-call(bf16[128,768]{1,0:T(8,128)(2,1)S(1)} %get-tuple-element.49.refs_2_.refs_1_.refs_0_, bf16[128,768]{1,0:T(8,128)(2,1)S(1)} %get-tuple-element.54.refs_11_.refs_1_, bf16[256,256]{1,0:T(8,128)(2,1)S(1)} %get-tuple-element.53.refs_11_.refs_2_.refs_0_, ...), custom_call_target="tpu_custom_call" | custom-call | flops 201326 | bytes 856 | tf_op jit(solution)/shard_map/attend_fresh/pallas_call | solution.py:76
  47.5 1.4 %combine_project.2 = (bf16[128,768]{1,0:T(8,128)(2,1)S(1)}, bf16[128,768]{1,0:T(8,128)(2,1)S(1)}, bf16[128,768]{1,0:T(8,128)(2,1)S(1)}, bf16[128,384]{1,0:T(8,128)(2,1)S(1)}, bf16[128,384]{1,0:T(8,128)(2,1)S(1)}) custom-call(f32[128,768]{1,0:T(8,128)S(1)} %get-tuple-element.47.refs_0_, f32[8,128]{1,0:T(8,128)S(1)} %get-tuple-element.48.refs_1_, ...), custom_call_target="tpu_custom_call" | custom-call | flops 301989 | bytes 3459 | tf_op jit(solution)/shard_map/combine_project/pallas_call | solution.py:76
  48.9 0.1 collective-permute-start.16
  49.0 0.5 collective-permute-start.17
  49.5 0.8 %collective-permute-done.16.refs_1_ = bf16[128,384]{1,0:T(8,128)(2,1)S(1)} collective-permute-done((bf16[128,384]{1,0:T(8,128)(2,1)S(1)}, bf16[128,384]{1,0:T(8,128)(2,1)S(1)}, u32[]{:S(2)}, u32[]{:S(2)}) %collective-permute-start.16) | collective-permute-done | bytes 98336 | tf_op jit(solution)/shard_map/ppermute | solution.py:37
  50.3 0.2 collective-permute-done.17.refs_2_
  50.4 0.1 sum_cores.2.refs_6_
  50.5 1.5 %collective-permute-start.18 = (bf16[128,768]{1,0:T(8,128)(2,1)S(1)}, bf16[128,768]{1,0:T(8,128)(2,1)S(1)}, u32[]{:S(2)}, u32[]{:S(2)}) collective-permute-start(bf16[128,768]{1,0:T(8,128)(2,1)S(1)} %sum_cores.2.refs_6_), channel_id=1, source_target_pairs={{0,2},{1,3},{2,0},{3,1},{4,6},{5,7},{6,4},{7,5},{8,10},{9,11},{10,... | collective-permute-start | bytes 589832 | tf_op jit(solution)/shard_map/ppermute | solution.py:32
  52.0 4.1 %collective-permute-done.19.refs_4_ = bf16[144,768]{1,0:T(8,128)(2,1)S(1)} collective-permute-done((bf16[144,768]{1,0:T(8,128)(2,1)S(1)}, bf16[144,768]{1,0:T(8,128)(2,1)S(1)}, u32[]{:S(2)}, u32[]{:S(2)}) %collective-permute-start.19) | collective-permute-done | bytes 221216 | tf_op jit(solution)/shard_map/ppermute | solution.py:32
  56.1 1.4 %combine_project.3 = (bf16[128,768]{1,0:T(8,128)(2,1)S(1)}, bf16[128,768]{1,0:T(8,128)(2,1)S(1)}, bf16[128,768]{1,0:T(8,128)(2,1)S(1)}, bf16[128,384]{1,0:T(8,128)(2,1)S(1)}, bf16[128,384]{1,0:T(8,128)(2,1)S(1)}) custom-call(f32[128,768]{1,0:T(8,128)S(1)} %get-tuple-element.65.refs_0_, f32[8,128]{1,0:T(8,128)S(1)} %get-tuple-element.66.refs_1_, ...), custom_call_target="tpu_custom_call" | custom-call | flops 301989 | bytes 3459 | tf_op jit(solution)/shard_map/combine_project/pallas_call | solution.py:76
  57.5 0.1 collective-permute-start.21
  57.6 0.5 collective-permute-start.22
  58.1 0.1 collective-permute-start.15
  58.2 0.4 collective-permute-start.20
  58.6 0.3 collective-permute-done.21.refs_1_
  58.9 0.2 collective-permute-done.22.refs_2_
  59.0 0.1 sum_cores.3.refs_7_
  59.1 1.5 %collective-permute-start.23 = (bf16[128,768]{1,0:T(8,128)(2,1)S(1)}, bf16[128,768]{1,0:T(8,128)(2,1)S(1)}, u32[]{:S(2)}, u32[]{:S(2)}) collective-permute-start(bf16[128,768]{1,0:T(8,128)(2,1)S(1)} %sum_cores.3.refs_7_), channel_id=1, source_target_pairs={{0,2},{1,3},{2,0},{3,1},{4,6},{5,7},{6,4},{7,5},{8,10},{9,11},{10,... | collective-permute-start | bytes 589832 | tf_op jit(solution)/shard_map/ppermute | solution.py:32
  60.6 2.2 %update_caches.1 = (bf16[2048,256]{1,0:T(8,128)(2,1)}, bf16[2048,256]{1,0:T(8,128)(2,1)}, f32[8,128]{1,0:T(8,128)S(1)}) custom-call(bf16[256,256]{1,0:T(8,128)(2,1)S(1)} %get-tuple-element.53.refs_11_.refs_2_.refs_0_, bf16[256,256]{1,0:T(8,128)(2,1)S(1)} %get-tuple-element.55.refs_3_.refs_1_, bf16[256,256]{1,0:T(8,128)(2,1)S(1)} %get-tuple-element.56.refs_4_.refs_2_, ...), custom_call_target="tpu_custom_call" | custom-call | flops 67108 | bytes 2361 | tf_op jit(solution)/shard_map/update_caches/pallas_call | solution.py:76
  62.8 3.6 %collective-permute-done.23.refs_5_ = bf16[128,768]{1,0:T(8,128)(2,1)S(1)} collective-permute-done((bf16[128,768]{1,0:T(8,128)(2,1)S(1)}, bf16[128,768]{1,0:T(8,128)(2,1)S(1)}, u32[]{:S(2)}, u32[]{:S(2)}) %collective-permute-start.23) | collective-permute-done | bytes 196640 | tf_op jit(solution)/shard_map/ppermute | solution.py:32
  66.3 0.9 %finish.1 = bf16[256,768]{1,0:T(8,128)(2,1)} custom-call(bf16[128,768]{1,0:T(8,128)(2,1)S(1)} %get-tuple-element.60.refs_3_.refs_0_, bf16[128,768]{1,0:T(8,128)(2,1)S(1)} %collective-permute-done.15.refs_1_, bf16[128,768]{1,0:T(8,128)(2,1)S(1)} %collective-permute-done.18.refs_4_.refs_2_, bf16[128,768]{1,0:T(8,128)(2,1)S(1)} %get-tuple-element.67.refs_3_, ...), custom_call_target="tpu_custom_call" | custom-call | flops 98 | bytes 786 | tf_op jit(solution)/shard_map/finish/pallas_call | solution.py:76
  (49 shorter events, 0.2 us)
Async XLA Ops:
  0.6 6.8 %copy-start.6 = (s32[4]{0:T(128)S(1)}, s32[4]{0:T(128)}, u32[]{:S(2)}) copy-start(s32[4]{0:T(128)} %refs_6_.3) | copy-start | bytes 52
  0.6 6.8 %copy-start.7 = (s32[4]{0:T(128)S(1)}, s32[4]{0:T(128)}, u32[]{:S(2)}) copy-start(s32[4]{0:T(128)} %refs_1_.2) | copy-start | bytes 52
  0.7 12.4 %collective-permute-start = (bf16[256,768]{1,0:T(8,128)(2,1)}, bf16[256,768]{1,0:T(8,128)(2,1)S(1)}, u32[]{:S(2)}, u32[]{:S(2)}) collective-permute-start(bf16[256,768]{1,0:T(8,128)(2,1)} %refs_0_.9), channel_id=1, source_target_pairs={{0,2},{1,3},{2,0},{3,1},{4,6},{5,7},{6,4},{7,5},{8,10},{9,11},{10,... | collective-permute-start | bytes 1179656 | tf_op jit(solution)/shard_map/ppermute | solution.py:32
  3.7 18.3 %collective-permute-start.1 = (bf16[256,768]{1,0:T(8,128)(2,1)}, bf16[256,768]{1,0:T(8,128)(2,1)S(1)}, u32[]{:S(2)}, u32[]{:S(2)}) collective-permute-start(bf16[256,768]{1,0:T(8,128)(2,1)} %refs_0_.9), channel_id=1, source_target_pairs={{0,1},{1,0},{2,3},{3,2},{4,5},{5,4},{6,7},{7,6},{8,9},{9,8},{10,11... | collective-permute-start | bytes 1179656 | tf_op jit(solution)/shard_map/ppermute | solution.py:37
  4.7 17.1 %collective-permute-start.4 = (bf16[128,768]{1,0:T(8,128)(2,1)S(1)}, bf16[128,768]{1,0:T(8,128)(2,1)S(1)}, u32[]{:S(2)}, u32[]{:S(2)}) collective-permute-start(bf16[128,768]{1,0:T(8,128)(2,1)S(1)} %get-tuple-element.75), channel_id=1, source_target_pairs={{0,16},{4,20},{8,24},{12,28},{16,0},{20,4},{24,8},{28,12},{1,17},{... | collective-permute-start | bytes 589832 | tf_op jit(solution)/shard_map/ppermute | solution.py:32
  7.4 1.6 %copy-start.3 = (bf16[2048,256]{1,0:T(8,128)(2,1)S(1)}, bf16[2048,256]{1,0:T(8,128)(2,1)}, u32[]{:S(2)}) copy-start(bf16[2048,256]{1,0:T(8,128)(2,1)} %refs_4_.1) | copy-start | bytes 3145732
  7.4 1.7 %copy-start.4 = (bf16[2048,256]{1,0:T(8,128)(2,1)S(1)}, bf16[2048,256]{1,0:T(8,128)(2,1)}, u32[]{:S(2)}) copy-start(bf16[2048,256]{1,0:T(8,128)(2,1)} %refs_5_.9) | copy-start | bytes 3145732
  7.5 17.0 %slice-start = ((s8[4718592]{0:T(1024)(128)(4,1)}), s8[4194304]{0:T(1024)(128)(4,1)S(1)}, s32[]{:S(2)}) async-start(s8[4718592]{0:T(1024)(128)(4,1)} %bitcast.1), calls=%async_computation | async-start | bytes 8388608
  9.1 15.4 %slice-start.1 = ((s8[4718592]{0:T(1024)(128)(4,1)}), s8[524288]{0:T(1024)(128)(4,1)S(1)}, s32[]{:S(2)}) async-start(s8[4718592]{0:T(1024)(128)(4,1)} %bitcast.1), calls=%async_computation.1 | async-start | bytes 1048576
  9.9 14.6 %copy-start = (bf16[256,768]{1,0:T(8,128)(2,1)S(1)}, bf16[256,768]{1,0:T(8,128)(2,1)}, u32[]{:S(2)}) copy-start(bf16[256,768]{1,0:T(8,128)(2,1)} %refs_0_.9) | copy-start | bytes 1179652
  9.9 14.6 %copy-start.5 = (f32[3072]{0:T(1024)S(1)}, f32[3072]{0:T(1024)}, u32[]{:S(2)}) copy-start(f32[3072]{0:T(1024)} %param.11) | copy-start | bytes 36868
  13.0 15.1 %collective-permute-start.10 = (bf16[128,768]{1,0:T(8,128)(2,1)S(1)}, bf16[128,768]{1,0:T(8,128)(2,1)S(1)}, u32[]{:S(2)}, u32[]{:S(2)}) collective-permute-start(bf16[128,768]{1,0:T(8,128)(2,1)S(1)} %relay.6.refs_1_), channel_id=1, source_target_pairs={{0,16},{4,20},{8,24},{12,28},{16,0},{20,4},{24,8},{28,12},{1,17},{... | collective-permute-start | bytes 589832 | tf_op jit(solution)/shard_map/ppermute | solution.py:32
  16.0 8.0 %collective-permute-start.2 = (bf16[64,768]{1,0:T(8,128)(2,1)S(1)}, bf16[64,768]{1,0:T(8,128)(2,1)S(1)}, u32[]{:S(2)}, u32[]{:S(2)}) collective-permute-start(bf16[64,768]{1,0:T(8,128)(2,1)S(1)} %get-tuple-element.42), channel_id=1, source_target_pairs={{0,1},{1,0},{2,3},{3,2},{4,5},{5,4},{6,7},{7,6},{8,9},{9,8},{10,11... | collective-permute-start | bytes 294920 | tf_op jit(solution)/shard_map/ppermute | solution.py:37
  16.0 7.9 %collective-permute-start.3 = (bf16[64,768]{1,0:T(8,128)(2,1)S(1)}, bf16[64,768]{1,0:T(8,128)(2,1)S(1)}, u32[]{:S(2)}, u32[]{:S(2)}) collective-permute-start(bf16[64,768]{1,0:T(8,128)(2,1)S(1)} %get-tuple-element.43), channel_id=1, source_target_pairs={{0,1},{1,0},{2,3},{3,2},{4,5},{5,4},{6,7},{7,6},{8,9},{9,8},{10,11... | collective-permute-start | bytes 294920 | tf_op jit(solution)/shard_map/ppermute | solution.py:37
  21.9 6.1 %collective-permute-start.6 = (bf16[64,768]{1,0:T(8,128)(2,1)S(1)}, bf16[64,768]{1,0:T(8,128)(2,1)S(1)}, u32[]{:S(2)}, u32[]{:S(2)}) collective-permute-start(bf16[64,768]{1,0:T(8,128)(2,1)S(1)} %get-tuple-element.51), channel_id=1, source_target_pairs={{0,2},{1,3},{2,0},{3,1},{4,6},{5,7},{6,4},{7,5},{8,10},{9,11},{10,... | collective-permute-start | bytes 294920 | tf_op jit(solution)/shard_map/ppermute | solution.py:32
  21.9 6.0 %collective-permute-start.7 = (bf16[64,768]{1,0:T(8,128)(2,1)S(1)}, bf16[64,768]{1,0:T(8,128)(2,1)S(1)}, u32[]{:S(2)}, u32[]{:S(2)}) collective-permute-start(bf16[64,768]{1,0:T(8,128)(2,1)S(1)} %get-tuple-element.52), channel_id=1, source_target_pairs={{0,2},{1,3},{2,0},{3,1},{4,6},{5,7},{6,4},{7,5},{8,10},{9,11},{10,... | collective-permute-start | bytes 294920 | tf_op jit(solution)/shard_map/ppermute | solution.py:32
  24.0 4.8 %collective-permute-start.5 = (bf16[128,768]{1,0:T(8,128)(2,1)S(1)}, bf16[128,768]{1,0:T(8,128)(2,1)S(1)}, u32[]{:S(2)}, u32[]{:S(2)}) collective-permute-start(bf16[128,768]{1,0:T(8,128)(2,1)S(1)} %get-tuple-element.50), channel_id=1, source_target_pairs={{0,1},{1,0},{2,3},{3,2},{4,5},{5,4},{6,7},{7,6},{8,9},{9,8},{10,11... | collective-permute-start | bytes 589832 | tf_op jit(solution)/shard_map/ppermute | solution.py:37
  24.0 6.0 %collective-permute-start.8 = (bf16[128,768]{1,0:T(8,128)(2,1)S(1)}, bf16[128,768]{1,0:T(8,128)(2,1)S(1)}, u32[]{:S(2)}, u32[]{:S(2)}) collective-permute-start(bf16[128,768]{1,0:T(8,128)(2,1)S(1)} %get-tuple-element.46.refs_12_.refs_0_), channel_id=1, source_target_pairs={{0,1},{1,0},{2,3},{3,2},{4,5},{5,4},{6,7},{7,6},{8,9},{9,8},{10,11... | collective-permute-start | bytes 589832 | tf_op jit(solution)/shard_map/ppermute | solution.py:37
  24.5 4.3 %copy-start.1 = (bf16[3072,256]{1,0:T(8,128)(2,1)S(1)}, bf16[3072,256]{1,0:T(8,128)(2,1)}, u32[]{:S(2)}) copy-start(bf16[3072,256]{1,0:T(8,128)(2,1)} %refs_9_.1) | copy-start | bytes 4718596
  24.5 4.3 %copy-start.2 = (bf16[3072,256]{1,0:T(8,128)(2,1)S(1)}, bf16[3072,256]{1,0:T(8,128)(2,1)}, u32[]{:S(2)}) copy-start(bf16[3072,256]{1,0:T(8,128)(2,1)} %refs_10_.1) | copy-start | bytes 4718596
  28.0 2.0 %collective-permute-start.9 = (bf16[128,768]{1,0:T(8,128)(2,1)S(1)}, bf16[128,768]{1,0:T(8,128)(2,1)S(1)}, u32[]{:S(2)}, u32[]{:S(2)}) collective-permute-start(bf16[128,768]{1,0:T(8,128)(2,1)S(1)} %relay.9.refs_2_.refs_1_), channel_id=1, source_target_pairs={{0,1},{1,0},{2,3},{3,2},{4,5},{5,4},{6,7},{7,6},{8,9},{9,8},{10,11... | collective-permute-start | bytes 589832 | tf_op jit(solution)/shard_map/ppermute | solution.py:37
  28.1 7.3 %collective-permute-start.11 = (bf16[128,768]{1,0:T(8,128)(2,1)S(1)}, bf16[128,768]{1,0:T(8,128)(2,1)S(1)}, u32[]{:S(2)}, u32[]{:S(2)}) collective-permute-start(bf16[128,768]{1,0:T(8,128)(2,1)S(1)} %relay.10.refs_11_.refs_0_.refs_1_), channel_id=1, source_target_pairs={{0,2},{1,3},{2,0},{3,1},{4,6},{5,7},{6,4},{7,5},{8,10},{9,11},{10,... | collective-permute-start | bytes 589832 | tf_op jit(solution)/shard_map/ppermute | solution.py:32
  33.4 14.1 %collective-permute-start.14 = (bf16[144,768]{1,0:T(8,128)(2,1)S(1)}, bf16[144,768]{1,0:T(8,128)(2,1)S(1)}, u32[]{:S(2)}, u32[]{:S(2)}) collective-permute-start(bf16[144,768]{1,0:T(8,128)(2,1)S(1)} %attend_partner.2.refs_1_.refs_13_), channel_id=1, source_target_pairs={{0,16},{4,20},{8,24},{12,28},{16,0},{20,4},{24,8},{28,12},{1,17},{... | collective-permute-start | bytes 663560 | tf_op jit(solution)/shard_map/ppermute | solution.py:32
  33.4 5.7 %collective-permute-start.12 = (bf16[128,768]{1,0:T(8,128)(2,1)S(1)}, bf16[128,768]{1,0:T(8,128)(2,1)S(1)}, u32[]{:S(2)}, u32[]{:S(2)}) collective-permute-start(bf16[128,768]{1,0:T(8,128)(2,1)S(1)} %relay.10.refs_11_.refs_0_.refs_1_), channel_id=1, source_target_pairs={{0,1},{1,0},{2,3},{3,2},{4,5},{5,4},{6,7},{7,6},{8,9},{9,8},{10,11... | collective-permute-start | bytes 589832 | tf_op jit(solution)/shard_map/ppermute | solution.py:37
  35.5 3.7 %collective-permute-start.13 = (bf16[128,768]{1,0:T(8,128)(2,1)S(1)}, bf16[128,768]{1,0:T(8,128)(2,1)S(1)}, u32[]{:S(2)}, u32[]{:S(2)}) collective-permute-start(bf16[128,768]{1,0:T(8,128)(2,1)S(1)} %relay.11.refs_14_.refs_1_.refs_3_), channel_id=1, source_target_pairs={{0,1},{1,0},{2,3},{3,2},{4,5},{5,4},{6,7},{7,6},{8,9},{9,8},{10,11... | collective-permute-start | bytes 589832 | tf_op jit(solution)/shard_map/ppermute | solution.py:37
  39.2 8.3 %slice-start.2 = ((s8[4718592]{0:T(1024)(128)(4,1)}), s8[4194304]{0:T(1024)(128)(4,1)S(1)}, s32[]{:S(2)}) async-start(s8[4718592]{0:T(1024)(128)(4,1)} %bitcast.3), calls=%async_computation.2 | async-start | bytes 8388608
  39.2 8.3 %slice-start.3 = ((s8[4718592]{0:T(1024)(128)(4,1)}), s8[524288]{0:T(1024)(128)(4,1)S(1)}, s32[]{:S(2)}) async-start(s8[4718592]{0:T(1024)(128)(4,1)} %bitcast.3), calls=%async_computation.3 | async-start | bytes 1048576
  42.6 13.5 %collective-permute-start.19 = (bf16[144,768]{1,0:T(8,128)(2,1)S(1)}, bf16[144,768]{1,0:T(8,128)(2,1)S(1)}, u32[]{:S(2)}, u32[]{:S(2)}) collective-permute-start(bf16[144,768]{1,0:T(8,128)(2,1)S(1)} %attend_partner.3.refs_13_), channel_id=1, source_target_pairs={{0,16},{4,20},{8,24},{12,28},{16,0},{20,4},{24,8},{28,12},{1,17},{... | collective-permute-start | bytes 663560 | tf_op jit(solution)/shard_map/ppermute | solution.py:32
  48.9 1.4 %collective-permute-start.16 = (bf16[128,384]{1,0:T(8,128)(2,1)S(1)}, bf16[128,384]{1,0:T(8,128)(2,1)S(1)}, u32[]{:S(2)}, u32[]{:S(2)}) collective-permute-start(bf16[128,384]{1,0:T(8,128)(2,1)S(1)} %get-tuple-element.63), channel_id=1, source_target_pairs={{0,1},{1,0},{2,3},{3,2},{4,5},{5,4},{6,7},{7,6},{8,9},{9,8},{10,11... | collective-permute-start | bytes 294920 | tf_op jit(solution)/shard_map/ppermute | solution.py:37
  49.0 1.4 %collective-permute-start.17 = (bf16[128,384]{1,0:T(8,128)(2,1)S(1)}, bf16[128,384]{1,0:T(8,128)(2,1)S(1)}, u32[]{:S(2)}, u32[]{:S(2)}) collective-permute-start(bf16[128,384]{1,0:T(8,128)(2,1)S(1)} %get-tuple-element.64), channel_id=1, source_target_pairs={{0,1},{1,0},{2,3},{3,2},{4,5},{5,4},{6,7},{7,6},{8,9},{9,8},{10,11... | collective-permute-start | bytes 294920 | tf_op jit(solution)/shard_map/ppermute | solution.py:37
  50.5 8.2 %collective-permute-start.18 = (bf16[128,768]{1,0:T(8,128)(2,1)S(1)}, bf16[128,768]{1,0:T(8,128)(2,1)S(1)}, u32[]{:S(2)}, u32[]{:S(2)}) collective-permute-start(bf16[128,768]{1,0:T(8,128)(2,1)S(1)} %sum_cores.2.refs_6_), channel_id=1, source_target_pairs={{0,2},{1,3},{2,0},{3,1},{4,6},{5,7},{6,4},{7,5},{8,10},{9,11},{10,... | collective-permute-start | bytes 589832 | tf_op jit(solution)/shard_map/ppermute | solution.py:32
  57.5 1.4 %collective-permute-start.21 = (bf16[128,384]{1,0:T(8,128)(2,1)S(1)}, bf16[128,384]{1,0:T(8,128)(2,1)S(1)}, u32[]{:S(2)}, u32[]{:S(2)}) collective-permute-start(bf16[128,384]{1,0:T(8,128)(2,1)S(1)} %get-tuple-element.70), channel_id=1, source_target_pairs={{0,1},{1,0},{2,3},{3,2},{4,5},{5,4},{6,7},{7,6},{8,9},{9,8},{10,11... | collective-permute-start | bytes 294920 | tf_op jit(solution)/shard_map/ppermute | solution.py:37
  57.6 1.4 %collective-permute-start.22 = (bf16[128,384]{1,0:T(8,128)(2,1)S(1)}, bf16[128,384]{1,0:T(8,128)(2,1)S(1)}, u32[]{:S(2)}, u32[]{:S(2)}) collective-permute-start(bf16[128,384]{1,0:T(8,128)(2,1)S(1)} %get-tuple-element.71), channel_id=1, source_target_pairs={{0,1},{1,0},{2,3},{3,2},{4,5},{5,4},{6,7},{7,6},{8,9},{9,8},{10,11... | collective-permute-start | bytes 294920 | tf_op jit(solution)/shard_map/ppermute | solution.py:37
  58.1 4.6 %collective-permute-start.15 = (bf16[128,768]{1,0:T(8,128)(2,1)S(1)}, bf16[128,768]{1,0:T(8,128)(2,1)S(1)}, u32[]{:S(2)}, u32[]{:S(2)}) collective-permute-start(bf16[128,768]{1,0:T(8,128)(2,1)S(1)} %get-tuple-element.61), channel_id=1, source_target_pairs={{0,1},{1,0},{2,3},{3,2},{4,5},{5,4},{6,7},{7,6},{8,9},{9,8},{10,11... | collective-permute-start | bytes 589832 | tf_op jit(solution)/shard_map/ppermute | solution.py:37
  58.2 4.6 %collective-permute-start.20 = (bf16[128,768]{1,0:T(8,128)(2,1)S(1)}, bf16[128,768]{1,0:T(8,128)(2,1)S(1)}, u32[]{:S(2)}, u32[]{:S(2)}) collective-permute-start(bf16[128,768]{1,0:T(8,128)(2,1)S(1)} %get-tuple-element.68), channel_id=1, source_target_pairs={{0,1},{1,0},{2,3},{3,2},{4,5},{5,4},{6,7},{7,6},{8,9},{9,8},{10,11... | collective-permute-start | bytes 589832 | tf_op jit(solution)/shard_map/ppermute | solution.py:37
  59.1 7.2 %collective-permute-start.23 = (bf16[128,768]{1,0:T(8,128)(2,1)S(1)}, bf16[128,768]{1,0:T(8,128)(2,1)S(1)}, u32[]{:S(2)}, u32[]{:S(2)}) collective-permute-start(bf16[128,768]{1,0:T(8,128)(2,1)S(1)} %sum_cores.3.refs_7_), channel_id=1, source_target_pairs={{0,2},{1,3},{2,0},{3,1},{4,6},{5,7},{6,4},{7,5},{8,10},{9,11},{10,... | collective-permute-start | bytes 589832 | tf_op jit(solution)/shard_map/ppermute | solution.py:32

commit v6 on v5

--- a/solution.py
+++ b/solution.py
@@ -481,15 +481,15 @@
     )
 
 
-def project_kernel(row_at, own_partial, own_stats, fresh_partial, fresh_stats, *refs):
+def combine_kernel(row_at, own_partial, own_stats, fresh_partial, fresh_stats, *refs):
     heads = lax.axis_size("head")
     chips = heads // CORES
-    outputs = 3 * chips - 1
+    outputs = 2 * chips - 1
     received = refs[: -1 - outputs]
-    w_out = refs[-1 - outputs]
-    near, far = refs[-outputs:][:chips], refs[-outputs:][chips:]
+    w_out, merged_rows = refs[-1 - outputs], refs[-outputs]
+    far = refs[1 - outputs :]
     width = own_partial.shape[1]
-    rows, block_width = near[0].shape
+    rows = merged_rows.shape[0]
     part = slice(row_at, row_at + rows)
     padding = jnp.zeros((LANES - STAT_ROWS, rows), jnp.float32)
     stats = [own_stats[...], fresh_stats[:, part]]
@@ -515,39 +515,59 @@
             merged = merged + ref[:rows, own].astype(jnp.float32) * share[:, column]
         attended.append(merged.astype(jnp.bfloat16))
     attended = jnp.concatenate(attended, 1)
-    me = lax.axis_index("head")
-    def product(ahead, flip):
-        block = lax.rem(me + CORES * ahead, heads) ^ flip
-        along = pl.ds(pl.multiple_of(block * block_width, LANES), block_width)
-        return dot(attended, w_out[:, along]).astype(jnp.bfloat16)
-
-    middle = block_width // 2
+    merged_rows[...] = attended
     for ahead in range(1, chips):
-        result = product(ahead, 1)
-        far[2 * ahead - 1][...] = result[:, :middle]
-        far[2 * ahead][...] = result[:, middle:]
-    far[0][...] = product(0, 1)
-    for ahead in range(chips):
-        near[ahead][...] = product(ahead, 0)
-
-
-def project(row_at, rows, own, fresh_part, received, w_out, heads, earlier):
+        result = block_product(attended, w_out, ahead, 1)
+        middle = result.shape[1] // 2
+        far[2 * ahead - 2][...] = result[:, :middle]
+        far[2 * ahead - 1][...] = result[:, middle:]
+
+
+def block_product(attended, w_out, ahead, flip):
+    heads = lax.axis_size("head")
+    block_width = w_out.shape[1] // heads
+    block = lax.rem(lax.axis_index("head") + CORES * ahead, heads) ^ flip
+    along = pl.ds(pl.multiple_of(block * block_width, LANES), block_width)
+    return dot(attended, w_out[:, along]).astype(jnp.bfloat16)
+
+
+def project_kernel(merged_rows, w_out, far, *near):
+    attended = merged_rows[...]
+    far[...] = block_product(attended, w_out, 0, 1)
+    for ahead, target in enumerate(near):
+        target[...] = block_product(attended, w_out, ahead, 0)
+
+
+def combine(row_at, rows, own, fresh_part, received, w_out, heads, earlier):
     chips = heads // CORES
     width = w_out.shape[1] // heads
-    shape = jax.ShapeDtypeStruct((rows, width), jnp.bfloat16)
+    merged = jax.ShapeDtypeStruct((rows, own[0].shape[1]), jnp.bfloat16)
     half = jax.ShapeDtypeStruct((rows, width // 2), jnp.bfloat16)
-    blocks = call(
-        functools.partial(project_kernel, row_at),
-        [shape] * chips + [shape] + [half] * (2 * chips - 2),
+    merged, *far = call(
+        functools.partial(combine_kernel, row_at),
+        [merged] + [half] * (2 * chips - 2),
         [*own, *fresh_part, *received, w_out],
         20,
-        2 * rows * w_out.size,
-        0,
-        "combine_project",
+        rows * w_out.size,
+        0,
+        "combine",
         earlier,
     )
-    near, far = blocks[:chips], blocks[chips:]
-    return near, [far[:1]] + [far[2 * k - 1 : 2 * k + 1] for k in range(1, chips)]
+    return merged, [far[2 * k : 2 * k + 2] for k in range(chips - 1)]
+
+
+def project(merged, w_out, heads):
+    block = jax.ShapeDtypeStruct((merged.shape[0], w_out.shape[1] // heads), jnp.bfloat16)
+    far, *near = call(
+        project_kernel,
+        [block] * (1 + heads // CORES),
+        [merged, w_out],
+        20,
+        2 * merged.shape[0] * w_out.size,
+        0,
+        "project",
+    )
+    return far, near
 
 
 def sum_kernel(count, *refs):
@@ -625,26 +645,36 @@
     (late,) = relay([tokens[chunk_rows:]], [rows - chunk_rows], from_chips + [wide_keys])
     second = [shifted(late, "seq", turn * requests) for turn in range(1, groups)]
     own_cuts = [relay([piece], [rows, half, half, rows - chunk_rows], [late]) for piece in from_chips]
-    earlier = [cut[0] for cut in own_cuts]
-    first = [relay([piece], [chunk_rows, half, half], earlier) for piece in first]
-    earlier = [cut[0] for cut in first]
     own_pieces = [[tokens]] + [[cut[0]] for cut in own_cuts] + [[other_core(tokens)]]
     own_pieces += [[other_core(block) for block in cut[1:]] for cut in own_cuts]
     own_early = [
         blocks if len(blocks) == 1 else blocks[: len(blocks) - 1] for blocks in own_pieces
     ]
-    *own_part, queries = attend_rows(own_early, True, 0, 0, earlier)
+    *own_part, queries = attend_rows(own_early, True, 0, 0, [cut[0] for cut in own_cuts])
     own_queries = [queries]
+
     earlier = [queries]
+    first = [relay([piece], [chunk_rows], earlier)[0] for piece in first]
+    first_from_chips = [other_chips(piece) for piece in first]
+    *late_part, queries = attend_rows(own_pieces, True, 1, 0, first)
+    own_part += late_part
+    own_queries.append(queries)
+    earlier = [queries]
+    second = [relay([piece], [rows - chunk_rows], earlier)[0] for piece in second]
+    second_from_chips = [other_chips(piece) for piece in second]
+    earlier = second
+
+    def gather_cores(piece, from_chips, earlier):
+        passed = [relay([one], [one.shape[0]], earlier)[0] for one in from_chips]
+        along = [piece] + passed
+        return along + [other_core(one) for one in along], passed
+
     gathered = []
-    for cut in first:
-        blocks = zip(*[other_chips(piece) for piece in cut[1:]])
-        from_chips = [relay(one, [chunk_rows], earlier)[0] for one in blocks]
-        along = [cut[0]] + from_chips
-        gathered.append([along + [other_core(one) for one in along]])
-        earlier = earlier + from_chips
-    second = [relay([piece], [rows - chunk_rows], earlier)[0] for piece in second]
-    new_rows = [fresh(own_pieces, gain, w_key, w_value, tables, 0, second)]
+    for piece, from_chips in zip(first, first_from_chips):
+        along, passed = gather_cores(piece, from_chips, earlier)
+        gathered.append([along])
+        earlier = earlier + passed
+    new_rows = [fresh(own_pieces, gain, w_key, w_value, tables, 0, earlier)]
     earlier = [new_rows[0][0]]
     received = [[] for _ in range(CHUNKS)]
     for turn in range(1, groups):
@@ -652,17 +682,10 @@
         (packed,) = attend_rows(pieces, False, 0, turn, earlier)
         received[0].append(shifted(packed, "seq", -turn * requests))
         earlier = [packed]
-    for pieces, piece in zip(gathered, second):
-        from_chips = [
-            relay([one], [rows - chunk_rows], earlier)[0] for one in other_chips(piece)
-        ]
-        along = [piece] + from_chips
-        pieces.append(along + [other_core(one) for one in along])
-        earlier = earlier + from_chips
-    *late_part, queries = attend_rows(own_pieces, True, 1, 0, earlier)
-    own_part += late_part
-    own_queries.append(queries)
-    earlier = [queries]
+    for blocks, piece, from_chips in zip(gathered, second, second_from_chips):
+        along, passed = gather_cores(piece, from_chips, earlier)
+        blocks.append(along)
+        earlier = earlier + passed
     for turn in range(1, groups):
         pieces = [[block] for block in gathered[turn - 1][1]]
         (packed,) = attend_rows(pieces, False, 1, turn, earlier)
@@ -677,15 +700,16 @@
     parts = []
     earlier = before_sums = []
     for chunk in range(CHUNKS):
-        nears, fars = project(
+        merged, fars = combine(
             chunk * chunk_rows, chunk_rows, own_part[2 * chunk : 2 * chunk + 2], fresh_part,
             received[chunk], w_out, heads, earlier,
         )
         fars = [[other_core(part) for part in far] for far in fars]
-        earlier = [nears[0]] + before_sums
-        sums = [sum_cores(near, far, earlier) for near, far in zip(nears[1:], fars[1:])]
+        far, near = project(merged, w_out, heads)
+        earlier = [far] + before_sums
+        sums = [sum_cores(one, parts_far, earlier) for one, parts_far in zip(near[1:], fars)]
         from_chips = [shifted(one, "head", CORES * k) for k, one in enumerate(sums, 1)]
-        parts += [nears[0], *fars[0], *from_chips]
+        parts += [near[0], other_core(far), *from_chips]
         earlier, before_sums = sums, from_chips
     keys_updated, values_updated, done = update(
         cached_lengths, new_keys, new_values, keys_cache, values_cache, earlier

time: 67.4 us -> 70.2 us (1.042)
  waiting for transfers between devices: 19.2 us -> 22.7 us
    ppermute x10 -> x9, waiting for transfers between devices: 17.8 us -> 21 us  [shifted(): lax.ppermute(shard, axis, [(i, (i + by) % devices) for i in range(devices)])]
    ppermute x10 -> x9, starting transfers between devices: 15.7 us -> 15.3 us  [shifted(): lax.ppermute(shard, axis, [(i, (i + by) % devices) for i in range(devices)])]
    pallas_call x22 -> x24, Pallas kernels: 27 us -> 26.6 us  [call(): pl.pallas_call(body, out_shape=out_shape, in_specs=[VMEM] * len(arrays) +...]
  transfers between devices with their start and end apart: 24 -> 23, of which waited for: 9 -> 11; matrix products, arithmetic and copies ran while one was open for 2% -> 1% of each run, Pallas kernels for 39% -> 37%
where the time goes in v6:
time: 70.2 us; the launch traced here: 70 us
  Pallas kernels  26.6 us (38%)
  waiting for transfers between devices  22.7 us (32%)
  starting transfers between devices  18.6 us (26%)
  local copies, waits for them, and re-layouts  1.19 us (2%)
  between operations  0.98 us (1%)
    pallas_call x24, Pallas kernels, call(): pl.pallas_call(body, out_shape=out_shape, in_specs=[VMEM] * len(arrays) +...  26.6 us
    ppermute x9, waiting for transfers between devices, shifted(): lax.ppermute(shard, axis, [(i, (i + by) % devices) for i in range(devices)])  21 us
    ppermute x9, starting transfers between devices, shifted(): lax.ppermute(shard, axis, [(i, (i + by) % devices) for i in range(devices)])  15.3 us
    ppermute x14, starting transfers between devices, other_core(): return lax.ppermute(shard, 'head', [(i, i ^ 1) for i in range(devices)])  3.32 us
    ppermute x14, waiting for transfers between devices, other_core(): return lax.ppermute(shard, 'head', [(i, i ^ 1) for i in range(devices)])  1.7 us
  transfers between devices with their start and end apart: 23, of which 11 were waited for; matrix products, arithmetic and copies ran while one was open for 1% of the time, Pallas kernels for 37%

profile of v6, /device:TPU:0, one launch (start us, length us, event | category | flops | bytes accessed | tf_op | source)
XLA Modules:
  0.0 70.0 jit_solution(660988565384598031)
XLA Ops:
  0.7 0.5 collective-permute-start.1
  1.2 2.6 %collective-permute-start = (bf16[256,768]{1,0:T(8,128)(2,1)}, bf16[256,768]{1,0:T(8,128)(2,1)S(1)}, u32[]{:S(2)}, u32[]{:S(2)}) collective-permute-start(bf16[256,768]{1,0:T(8,128)(2,1)} %refs_0_.9), channel_id=1, source_target_pairs={{0,2},{1,3},{2,0},{3,1},{4,6},{5,7},{6,4},{7,5},{8,10},{9,11},{10,... | collective-permute-start | bytes 1179656 | tf_op jit(solution)/shard_map/ppermute | solution.py:32
  3.8 1.0 %fusion = (bf16[128,768]{1,0:T(8,128)(2,1)S(1)}, bf16[128,768]{1,0:T(8,128)(2,1)S(1)}) fusion(bf16[256,768]{1,0:T(8,128)(2,1)} %refs_0_.9), kind=kLoop, calls=%fused_computation | loop fusion | bytes 786432 | tf_op jit(solution)/shard_map/slice | solution.py:630
  4.8 2.7 %collective-permute-start.5 = (bf16[128,768]{1,0:T(8,128)(2,1)S(1)}, bf16[128,768]{1,0:T(8,128)(2,1)S(1)}, u32[]{:S(2)}, u32[]{:S(2)}) collective-permute-start(bf16[128,768]{1,0:T(8,128)(2,1)S(1)} %get-tuple-element.73), channel_id=1, source_target_pairs={{0,16},{4,20},{8,24},{12,28},{16,0},{20,4},{24,8},{28,12},{1,17},{... | collective-permute-start | bytes 589832 | tf_op jit(solution)/shard_map/ppermute | solution.py:32
  7.6 1.6 %rope_tables.1 = (f32[512,128]{1,0:T(8,128)S(1)}, f32[512,128]{1,0:T(8,128)S(1)}) custom-call(s32[4]{0:T(128)S(1)} %copy-done.6, s32[4]{0:T(128)S(1)} %copy-done.7, bf16[2048,128]{1,0:T(8,128)(2,1)S(1)} %marks.1.refs_2_.refs_11_.refs_12_.refs_10_), custom_call_target="tpu_custom_call" | custom-call | flops 1000000000 | bytes 262 | tf_op jit(solution)/shard_map/rope_tables/pallas_call | solution.py:76
  9.1 0.1 copy-done.4
  9.2 0.8 %widen_caches.1 = (bf16[2,2048,256]{2,1,0:T(8,128)(2,1)S(1)}, bf16[2,2048,256]{2,1,0:T(8,128)(2,1)S(1)}) custom-call(bf16[2048,256]{1,0:T(8,128)(2,1)S(1)} %copy-done.3, bf16[2048,256]{1,0:T(8,128)(2,1)S(1)} %copy-done.4, bf16[2048,128]{1,0:T(8,128)(2,1)S(1)} %marks.1.refs_2_.refs_11_.refs_12_.refs_10_, s32[4]{0:T(128)S(1)} %copy-done.6, ...), custom_call_target="tpu_custom_call" | custom-call | flops 1000000000 | bytes 3407 | tf_op jit(solution)/shard_map/widen_caches/pallas_call | solution.py:76
  10.0 3.6 %collective-permute-done.refs_1_.refs_0_ = bf16[256,768]{1,0:T(8,128)(2,1)S(1)} collective-permute-done((bf16[256,768]{1,0:T(8,128)(2,1)}, bf16[256,768]{1,0:T(8,128)(2,1)S(1)}, u32[]{:S(2)}, u32[]{:S(2)}) %collective-permute-start) | collective-permute-done | bytes 393248 | tf_op jit(solution)/shard_map/ppermute | solution.py:32
  13.8 0.1 collective-permute-start.2
  13.8 0.5 collective-permute-start.3
  14.3 2.8 %collective-permute-start.6 = (bf16[128,768]{1,0:T(8,128)(2,1)S(1)}, bf16[128,768]{1,0:T(8,128)(2,1)S(1)}, u32[]{:S(2)}, u32[]{:S(2)}) collective-permute-start(bf16[128,768]{1,0:T(8,128)(2,1)S(1)} %relay.6.refs_1_), channel_id=1, source_target_pairs={{0,16},{4,20},{8,24},{12,28},{16,0},{20,4},{24,8},{28,12},{1,17},{... | collective-permute-start | bytes 589832 | tf_op jit(solution)/shard_map/ppermute | solution.py:32
  17.2 3.3 %attend_own.2 = (f32[128,768]{1,0:T(8,128)S(1)}, f32[8,128]{1,0:T(8,128)S(1)}, bf16[128,768]{1,0:T(8,128)(2,1)S(1)}) custom-call(bf16[256,768]{1,0:T(8,128)(2,1)S(1)} %copy-done, bf16[256,768]{1,0:T(8,128)(2,1)S(1)} %get-tuple-element.40.refs_1_.refs_12_, bf16[256,768]{1,0:T(8,128)(2,1)S(1)} %collective-permute-done.1.refs_2_, ...), custom_call_target="tpu_custom_call" | custom-call | flops 1107296 | bytes 5971 | tf_op jit(solution)/shard_map/attend_own/pallas_call | solution.py:76
  20.5 1.6 %collective-permute-start.7 = (bf16[128,768]{1,0:T(8,128)(2,1)S(1)}, bf16[128,768]{1,0:T(8,128)(2,1)S(1)}, u32[]{:S(2)}, u32[]{:S(2)}) collective-permute-start(bf16[128,768]{1,0:T(8,128)(2,1)S(1)} %relay.8.refs_13_.refs_0_), channel_id=1, source_target_pairs={{0,2},{1,3},{2,0},{3,1},{4,6},{5,7},{6,4},{7,5},{8,10},{9,11},{10,... | collective-permute-start | bytes 589832 | tf_op jit(solution)/shard_map/ppermute | solution.py:32
  22.1 0.2 collective-permute-start.9
  22.4 3.3 %attend_own.3 = (f32[128,768]{1,0:T(8,128)S(1)}, f32[8,128]{1,0:T(8,128)S(1)}, bf16[128,768]{1,0:T(8,128)(2,1)S(1)}) custom-call(bf16[256,768]{1,0:T(8,128)(2,1)S(1)} %copy-done, bf16[256,768]{1,0:T(8,128)(2,1)S(1)} %get-tuple-element.40.refs_1_.refs_12_, bf16[256,768]{1,0:T(8,128)(2,1)S(1)} %collective-permute-done.1.refs_2_, ...), custom_call_target="tpu_custom_call" | custom-call | flops 1107296 | bytes 6070 | tf_op jit(solution)/shard_map/attend_own/pallas_call | solution.py:76
  25.6 0.9 %collective-permute-done.6.refs_0_ = bf16[128,768]{1,0:T(8,128)(2,1)S(1)} collective-permute-done((bf16[128,768]{1,0:T(8,128)(2,1)S(1)}, bf16[128,768]{1,0:T(8,128)(2,1)S(1)}, u32[]{:S(2)}, u32[]{:S(2)}) %collective-permute-start.6) | collective-permute-done | bytes 196640 | tf_op jit(solution)/shard_map/ppermute | solution.py:32
  26.5 1.4 %collective-permute-done.7.refs_0_ = bf16[128,768]{1,0:T(8,128)(2,1)S(1)} collective-permute-done((bf16[128,768]{1,0:T(8,128)(2,1)S(1)}, bf16[128,768]{1,0:T(8,128)(2,1)S(1)}, u32[]{:S(2)}, u32[]{:S(2)}) %collective-permute-start.7) | collective-permute-done | bytes 196640 | tf_op jit(solution)/shard_map/ppermute | solution.py:32
  27.9 0.1 collective-permute-start.10
  28.0 1.6 %collective-permute-start.8 = (bf16[128,768]{1,0:T(8,128)(2,1)S(1)}, bf16[128,768]{1,0:T(8,128)(2,1)S(1)}, u32[]{:S(2)}, u32[]{:S(2)}) collective-permute-start(bf16[128,768]{1,0:T(8,128)(2,1)S(1)} %relay.9.refs_1_.refs_11_.refs_0_), channel_id=1, source_target_pairs={{0,2},{1,3},{2,0},{3,1},{4,6},{5,7},{6,4},{7,5},{8,10},{9,11},{10,... | collective-permute-start | bytes 589832 | tf_op jit(solution)/shard_map/ppermute | solution.py:32
  29.6 0.2 collective-permute-start.11
  29.8 1.1 %fresh_kv.2 = (bf16[256,256]{1,0:T(8,128)(2,1)S(1)}, bf16[256,256]{1,0:T(8,128)(2,1)S(1)}) custom-call(bf16[256,768]{1,0:T(8,128)(2,1)S(1)} %copy-done, bf16[256,768]{1,0:T(8,128)(2,1)S(1)} %get-tuple-element.40.refs_1_.refs_12_, bf16[256,768]{1,0:T(8,128)(2,1)S(1)} %collective-permute-done.1.refs_2_, bf16[64,768]{1,0:T(8,128)(2,1)S(1)} %collective-permute-done.2.refs_3_, ...), custom_call_target="tpu_custom_call" | custom-call | flops 402653 | bytes 2758 | tf_op jit(solution)/shard_map/fresh_kv/pallas_call | solution.py:76
  30.9 3.5 %attend_partner.2.refs_1_.refs_11_ = bf16[144,768]{1,0:T(8,128)(2,1)S(1)} custom-call(bf16[128,768]{1,0:T(8,128)(2,1)S(1)} %relay.8.refs_13_.refs_0_, bf16[128,768]{1,0:T(8,128)(2,1)S(1)} %relay.10.refs_12_.refs_1_.refs_2_, bf16[128,768]{1,0:T(8,128)(2,1)S(1)} %collective-permute-done.9.refs_2_.refs_4_, ...), custom_call_target="tpu_custom_call" | custom-call | flops 1107296 | bytes 5490 | tf_op jit(solution)/shard_map/attend_partner/pallas_call | solution.py:76
  34.4 0.8 %collective-permute-start.13 = (bf16[144,768]{1,0:T(8,128)(2,1)S(1)}, bf16[144,768]{1,0:T(8,128)(2,1)S(1)}, u32[]{:S(2)}, u32[]{:S(2)}) collective-permute-start(bf16[144,768]{1,0:T(8,128)(2,1)S(1)} %attend_partner.2.refs_1_.refs_11_), channel_id=1, source_target_pairs={{0,16},{4,20},{8,24},{12,28},{16,0},{20,4},{24,8},{28,12},{1,17},{... | collective-permute-start | bytes 663560 | tf_op jit(solution)/shard_map/ppermute | solution.py:32
  35.2 0.2 collective-permute-done.8.refs_0_
  35.5 1.4 %collective-permute-done.12.refs_3_.refs_7_ = bf16[128,768]{1,0:T(8,128)(2,1)S(1)} collective-permute-done((bf16[128,768]{1,0:T(8,128)(2,1)S(1)}, bf16[128,768]{1,0:T(8,128)(2,1)S(1)}, u32[]{:S(2)}, u32[]{:S(2)}) %collective-permute-start.12) | collective-permute-done | bytes 196640 | tf_op jit(solution)/shard_map/ppermute | solution.py:37
  36.9 3.3 %attend_partner.3.refs_13_ = bf16[144,768]{1,0:T(8,128)(2,1)S(1)} custom-call(bf16[128,768]{1,0:T(8,128)(2,1)S(1)} %relay.9.refs_1_.refs_11_.refs_0_, bf16[128,768]{1,0:T(8,128)(2,1)S(1)} %relay.11.refs_1_.refs_12_.refs_3_, bf16[128,768]{1,0:T(8,128)(2,1)S(1)} %collective-permute-done.11.refs_2_.refs_5_, ...), custom_call_target="tpu_custom_call" | custom-call | flops 1107296 | bytes 5490 | tf_op jit(solution)/shard_map/attend_partner/pallas_call | solution.py:76
  40.2 2.0 %collective-permute-start.18 = (bf16[144,768]{1,0:T(8,128)(2,1)S(1)}, bf16[144,768]{1,0:T(8,128)(2,1)S(1)}, u32[]{:S(2)}, u32[]{:S(2)}) collective-permute-start(bf16[144,768]{1,0:T(8,128)(2,1)S(1)} %attend_partner.3.refs_13_), channel_id=1, source_target_pairs={{0,16},{4,20},{8,24},{12,28},{16,0},{20,4},{24,8},{28,12},{1,17},{... | collective-permute-start | bytes 663560 | tf_op jit(solution)/shard_map/ppermute | solution.py:32
  42.2 1.1 %fresh_kv.3 = (bf16[256,256]{1,0:T(8,128)(2,1)S(1)}, bf16[256,256]{1,0:T(8,128)(2,1)S(1)}) custom-call(bf16[128,768]{1,0:T(8,128)(2,1)S(1)} %relay.8.refs_13_.refs_0_, bf16[128,768]{1,0:T(8,128)(2,1)S(1)} %relay.9.refs_1_.refs_11_.refs_0_, bf16[128,768]{1,0:T(8,128)(2,1)S(1)} %relay.10.refs_12_.refs_1_.refs_2_, ...), custom_call_target="tpu_custom_call" | custom-call | flops 402653 | bytes 2758 | tf_op jit(solution)/shard_map/fresh_kv/pallas_call | solution.py:76
  43.3 2.3 %attend_fresh.1 = (f32[256,768]{1,0:T(8,128)S(1)}, f32[8,256]{1,0:T(8,128)S(1)}) custom-call(bf16[128,768]{1,0:T(8,128)(2,1)S(1)} %get-tuple-element.47.refs_1_.refs_0_, bf16[128,768]{1,0:T(8,128)(2,1)S(1)} %get-tuple-element.49.refs_1_, bf16[256,256]{1,0:T(8,128)(2,1)S(1)} %get-tuple-element.50.refs_11_.refs_2_.refs_0_, ...), custom_call_target="tpu_custom_call" | custom-call | flops 201326 | bytes 856 | tf_op jit(solution)/shard_map/attend_fresh/pallas_call | solution.py:76
  45.6 7.4 %collective-permute-done.13.refs_4_ = bf16[144,768]{1,0:T(8,128)(2,1)S(1)} collective-permute-done((bf16[144,768]{1,0:T(8,128)(2,1)S(1)}, bf16[144,768]{1,0:T(8,128)(2,1)S(1)}, u32[]{:S(2)}, u32[]{:S(2)}) %collective-permute-start.13) | collective-permute-done | bytes 221216 | tf_op jit(solution)/shard_map/ppermute | solution.py:32
  53.0 0.8 %combine.2 = (bf16[128,768]{1,0:T(8,128)(2,1)S(1)}, bf16[128,384]{1,0:T(8,128)(2,1)S(1)}, bf16[128,384]{1,0:T(8,128)(2,1)S(1)}) custom-call(f32[128,768]{1,0:T(8,128)S(1)} %get-tuple-element.45.refs_0_, f32[8,128]{1,0:T(8,128)S(1)} %get-tuple-element.46.refs_1_, f32[256,768]{1,0:T(8,128)S(1)} %get-tuple-element.54.refs_2_, ...), custom_call_target="tpu_custom_call" | custom-call | flops 150994 | bytes 3262 | tf_op jit(solution)/shard_map/combine/pallas_call | solution.py:76
  53.9 0.1 collective-permute-start.15
  53.9 0.5 collective-permute-start.16
  54.4 0.7 project.2
  55.1 0.1 collective-permute-done.15.refs_1_
  55.2 0.2 collective-permute-done.16.refs_2_
  55.4 0.6 collective-permute-start.17
  56.0 1.2 %collective-permute-done.18.refs_4_ = bf16[144,768]{1,0:T(8,128)(2,1)S(1)} collective-permute-done((bf16[144,768]{1,0:T(8,128)(2,1)S(1)}, bf16[144,768]{1,0:T(8,128)(2,1)S(1)}, u32[]{:S(2)}, u32[]{:S(2)}) %collective-permute-start.18) | collective-permute-done | bytes 221216 | tf_op jit(solution)/shard_map/ppermute | solution.py:32
  57.2 0.8 %combine.3 = (bf16[128,768]{1,0:T(8,128)(2,1)S(1)}, bf16[128,384]{1,0:T(8,128)(2,1)S(1)}, bf16[128,384]{1,0:T(8,128)(2,1)S(1)}) custom-call(f32[128,768]{1,0:T(8,128)S(1)} %get-tuple-element.62.refs_0_, f32[8,128]{1,0:T(8,128)S(1)} %get-tuple-element.63.refs_1_, f32[256,768]{1,0:T(8,128)S(1)} %get-tuple-element.54.refs_2_, ...), custom_call_target="tpu_custom_call" | custom-call | flops 150994 | bytes 3262 | tf_op jit(solution)/shard_map/combine/pallas_call | solution.py:76
  58.1 0.5 collective-permute-start.21
  58.6 0.1 collective-permute-start.14
  58.7 0.7 project.3
  59.4 0.5 collective-permute-start.19
  59.9 2.8 %collective-permute-done.17.refs_4_.refs_2_ = bf16[128,768]{1,0:T(8,128)(2,1)S(1)} collective-permute-done((bf16[128,768]{1,0:T(8,128)(2,1)S(1)}, bf16[128,768]{1,0:T(8,128)(2,1)S(1)}, u32[]{:S(2)}, u32[]{:S(2)}) %collective-permute-start.17) | collective-permute-done | bytes 196640 | tf_op jit(solution)/shard_map/ppermute | solution.py:32
  62.7 0.6 collective-permute-start.22
  63.3 2.2 %update_caches.1 = (bf16[2048,256]{1,0:T(8,128)(2,1)}, bf16[2048,256]{1,0:T(8,128)(2,1)}, f32[8,128]{1,0:T(8,128)S(1)}) custom-call(bf16[256,256]{1,0:T(8,128)(2,1)S(1)} %get-tuple-element.50.refs_11_.refs_2_.refs_0_, bf16[256,256]{1,0:T(8,128)(2,1)S(1)} %get-tuple-element.51.refs_3_.refs_1_, bf16[256,256]{1,0:T(8,128)(2,1)S(1)} %get-tuple-element.52.refs_4_.refs_2_, ...), custom_call_target="tpu_custom_call" | custom-call | flops 67108 | bytes 2361 | tf_op jit(solution)/shard_map/update_caches/pallas_call | solution.py:76
  65.5 3.6 %collective-permute-done.22.refs_5_ = bf16[128,768]{1,0:T(8,128)(2,1)S(1)} collective-permute-done((bf16[128,768]{1,0:T(8,128)(2,1)S(1)}, bf16[128,768]{1,0:T(8,128)(2,1)S(1)}, u32[]{:S(2)}, u32[]{:S(2)}) %collective-permute-start.22) | collective-permute-done | bytes 196640 | tf_op jit(solution)/shard_map/ppermute | solution.py:32
  69.1 0.9 %finish.1 = bf16[256,768]{1,0:T(8,128)(2,1)} custom-call(bf16[128,768]{1,0:T(8,128)(2,1)S(1)} %get-tuple-element.57.refs_0_, bf16[128,768]{1,0:T(8,128)(2,1)S(1)} %collective-permute-done.14.refs_1_, bf16[128,768]{1,0:T(8,128)(2,1)S(1)} %collective-permute-done.17.refs_4_.refs_2_, bf16[128,768]{1,0:T(8,128)(2,1)S(1)} %get-tuple-element.65.refs_3_, ...), custom_call_target="tpu_custom_call" | custom-call | flops 98 | bytes 786 | tf_op jit(solution)/shard_map/finish/pallas_call | solution.py:76
  (49 shorter events, 0.5 us)
Async XLA Ops:
  0.6 6.9 %copy-start.6 = (s32[4]{0:T(128)S(1)}, s32[4]{0:T(128)}, u32[]{:S(2)}) copy-start(s32[4]{0:T(128)} %refs_6_.3) | copy-start | bytes 52
  0.6 6.9 %copy-start.7 = (s32[4]{0:T(128)S(1)}, s32[4]{0:T(128)}, u32[]{:S(2)}) copy-start(s32[4]{0:T(128)} %refs_1_.4) | copy-start | bytes 52
  0.7 16.5 %collective-permute-start.1 = (bf16[256,768]{1,0:T(8,128)(2,1)}, bf16[256,768]{1,0:T(8,128)(2,1)S(1)}, u32[]{:S(2)}, u32[]{:S(2)}) collective-permute-start(bf16[256,768]{1,0:T(8,128)(2,1)} %refs_0_.9), channel_id=1, source_target_pairs={{0,1},{1,0},{2,3},{3,2},{4,5},{5,4},{6,7},{7,6},{8,9},{9,8},{10,11... | collective-permute-start | bytes 1179656 | tf_op jit(solution)/shard_map/ppermute | solution.py:37
  1.2 12.5 %collective-permute-start = (bf16[256,768]{1,0:T(8,128)(2,1)}, bf16[256,768]{1,0:T(8,128)(2,1)S(1)}, u32[]{:S(2)}, u32[]{:S(2)}) collective-permute-start(bf16[256,768]{1,0:T(8,128)(2,1)} %refs_0_.9), channel_id=1, source_target_pairs={{0,2},{1,3},{2,0},{3,1},{4,6},{5,7},{6,4},{7,5},{8,10},{9,11},{10,... | collective-permute-start | bytes 1179656 | tf_op jit(solution)/shard_map/ppermute | solution.py:32
  4.8 15.7 %collective-permute-start.5 = (bf16[128,768]{1,0:T(8,128)(2,1)S(1)}, bf16[128,768]{1,0:T(8,128)(2,1)S(1)}, u32[]{:S(2)}, u32[]{:S(2)}) collective-permute-start(bf16[128,768]{1,0:T(8,128)(2,1)S(1)} %get-tuple-element.73), channel_id=1, source_target_pairs={{0,16},{4,20},{8,24},{12,28},{16,0},{20,4},{24,8},{28,12},{1,17},{... | collective-permute-start | bytes 589832 | tf_op jit(solution)/shard_map/ppermute | solution.py:32
  7.5 9.7 %slice-start = ((s8[4718592]{0:T(1024)(128)(4,1)}), s8[4194304]{0:T(1024)(128)(4,1)S(1)}, s32[]{:S(2)}) async-start(s8[4718592]{0:T(1024)(128)(4,1)} %bitcast.1), calls=%async_computation | async-start | bytes 8388608
  7.5 1.6 %copy-start.3 = (bf16[2048,256]{1,0:T(8,128)(2,1)S(1)}, bf16[2048,256]{1,0:T(8,128)(2,1)}, u32[]{:S(2)}) copy-start(bf16[2048,256]{1,0:T(8,128)(2,1)} %refs_4_.1) | copy-start | bytes 3145732
  7.5 1.7 %copy-start.4 = (bf16[2048,256]{1,0:T(8,128)(2,1)S(1)}, bf16[2048,256]{1,0:T(8,128)(2,1)}, u32[]{:S(2)}) copy-start(bf16[2048,256]{1,0:T(8,128)(2,1)} %refs_5_.9) | copy-start | bytes 3145732
  7.6 9.6 %slice-start.1 = ((s8[4718592]{0:T(1024)(128)(4,1)}), s8[524288]{0:T(1024)(128)(4,1)S(1)}, s32[]{:S(2)}) async-start(s8[4718592]{0:T(1024)(128)(4,1)} %bitcast.1), calls=%async_computation.1 | async-start | bytes 1048576
  10.0 7.2 %copy-start = (bf16[256,768]{1,0:T(8,128)(2,1)S(1)}, bf16[256,768]{1,0:T(8,128)(2,1)}, u32[]{:S(2)}) copy-start(bf16[256,768]{1,0:T(8,128)(2,1)} %refs_0_.9) | copy-start | bytes 1179652
  10.0 7.2 %copy-start.5 = (f32[3072]{0:T(1024)S(1)}, f32[3072]{0:T(1024)}, u32[]{:S(2)}) copy-start(f32[3072]{0:T(1024)} %param.11) | copy-start | bytes 36868
  13.8 3.4 %collective-permute-start.2 = (bf16[64,768]{1,0:T(8,128)(2,1)S(1)}, bf16[64,768]{1,0:T(8,128)(2,1)S(1)}, u32[]{:S(2)}, u32[]{:S(2)}) collective-permute-start(bf16[64,768]{1,0:T(8,128)(2,1)S(1)} %get-tuple-element.41), channel_id=1, source_target_pairs={{0,1},{1,0},{2,3},{3,2},{4,5},{5,4},{6,7},{7,6},{8,9},{9,8},{10,11... | collective-permute-start | bytes 294920 | tf_op jit(solution)/shard_map/ppermute | solution.py:37
  13.8 3.3 %collective-permute-start.3 = (bf16[64,768]{1,0:T(8,128)(2,1)S(1)}, bf16[64,768]{1,0:T(8,128)(2,1)S(1)}, u32[]{:S(2)}, u32[]{:S(2)}) collective-permute-start(bf16[64,768]{1,0:T(8,128)(2,1)S(1)} %get-tuple-element.42), channel_id=1, source_target_pairs={{0,1},{1,0},{2,3},{3,2},{4,5},{5,4},{6,7},{7,6},{8,9},{9,8},{10,11... | collective-permute-start | bytes 294920 | tf_op jit(solution)/shard_map/ppermute | solution.py:37
  14.3 12.2 %collective-permute-start.6 = (bf16[128,768]{1,0:T(8,128)(2,1)S(1)}, bf16[128,768]{1,0:T(8,128)(2,1)S(1)}, u32[]{:S(2)}, u32[]{:S(2)}) collective-permute-start(bf16[128,768]{1,0:T(8,128)(2,1)S(1)} %relay.6.refs_1_), channel_id=1, source_target_pairs={{0,16},{4,20},{8,24},{12,28},{16,0},{20,4},{24,8},{28,12},{1,17},{... | collective-permute-start | bytes 589832 | tf_op jit(solution)/shard_map/ppermute | solution.py:32
  17.2 5.2 %collective-permute-start.4 = (bf16[128,768]{1,0:T(8,128)(2,1)S(1)}, bf16[128,768]{1,0:T(8,128)(2,1)S(1)}, u32[]{:S(2)}, u32[]{:S(2)}) collective-permute-start(bf16[128,768]{1,0:T(8,128)(2,1)S(1)} %get-tuple-element.48), channel_id=1, source_target_pairs={{0,1},{1,0},{2,3},{3,2},{4,5},{5,4},{6,7},{7,6},{8,9},{9,8},{10,11... | collective-permute-start | bytes 589832 | tf_op jit(solution)/shard_map/ppermute | solution.py:37
  20.5 7.4 %collective-permute-start.7 = (bf16[128,768]{1,0:T(8,128)(2,1)S(1)}, bf16[128,768]{1,0:T(8,128)(2,1)S(1)}, u32[]{:S(2)}, u32[]{:S(2)}) collective-permute-start(bf16[128,768]{1,0:T(8,128)(2,1)S(1)} %relay.8.refs_13_.refs_0_), channel_id=1, source_target_pairs={{0,2},{1,3},{2,0},{3,1},{4,6},{5,7},{6,4},{7,5},{8,10},{9,11},{10,... | collective-permute-start | bytes 589832 | tf_op jit(solution)/shard_map/ppermute | solution.py:32
  22.1 8.7 %collective-permute-start.9 = (bf16[128,768]{1,0:T(8,128)(2,1)S(1)}, bf16[128,768]{1,0:T(8,128)(2,1)S(1)}, u32[]{:S(2)}, u32[]{:S(2)}) collective-permute-start(bf16[128,768]{1,0:T(8,128)(2,1)S(1)} %relay.8.refs_13_.refs_0_), channel_id=1, source_target_pairs={{0,1},{1,0},{2,3},{3,2},{4,5},{5,4},{6,7},{7,6},{8,9},{9,8},{10,11... | collective-permute-start | bytes 589832 | tf_op jit(solution)/shard_map/ppermute | solution.py:37
  22.4 7.4 %copy-start.1 = (bf16[3072,256]{1,0:T(8,128)(2,1)S(1)}, bf16[3072,256]{1,0:T(8,128)(2,1)}, u32[]{:S(2)}) copy-start(bf16[3072,256]{1,0:T(8,128)(2,1)} %refs_9_.1) | copy-start | bytes 4718596
  22.4 7.4 %copy-start.2 = (bf16[3072,256]{1,0:T(8,128)(2,1)S(1)}, bf16[3072,256]{1,0:T(8,128)(2,1)}, u32[]{:S(2)}) copy-start(bf16[3072,256]{1,0:T(8,128)(2,1)} %refs_10_.1) | copy-start | bytes 4718596
  27.9 2.9 %collective-permute-start.10 = (bf16[128,768]{1,0:T(8,128)(2,1)S(1)}, bf16[128,768]{1,0:T(8,128)(2,1)S(1)}, u32[]{:S(2)}, u32[]{:S(2)}) collective-permute-start(bf16[128,768]{1,0:T(8,128)(2,1)S(1)} %relay.10.refs_12_.refs_1_.refs_2_), channel_id=1, source_target_pairs={{0,1},{1,0},{2,3},{3,2},{4,5},{5,4},{6,7},{7,6},{8,9},{9,8},{10,11... | collective-permute-start | bytes 589832 | tf_op jit(solution)/shard_map/ppermute | solution.py:37
  28.0 7.3 %collective-permute-start.8 = (bf16[128,768]{1,0:T(8,128)(2,1)S(1)}, bf16[128,768]{1,0:T(8,128)(2,1)S(1)}, u32[]{:S(2)}, u32[]{:S(2)}) collective-permute-start(bf16[128,768]{1,0:T(8,128)(2,1)S(1)} %relay.9.refs_1_.refs_11_.refs_0_), channel_id=1, source_target_pairs={{0,2},{1,3},{2,0},{3,1},{4,6},{5,7},{6,4},{7,5},{8,10},{9,11},{10,... | collective-permute-start | bytes 589832 | tf_op jit(solution)/shard_map/ppermute | solution.py:32
  29.6 5.8 %collective-permute-start.11 = (bf16[128,768]{1,0:T(8,128)(2,1)S(1)}, bf16[128,768]{1,0:T(8,128)(2,1)S(1)}, u32[]{:S(2)}, u32[]{:S(2)}) collective-permute-start(bf16[128,768]{1,0:T(8,128)(2,1)S(1)} %relay.9.refs_1_.refs_11_.refs_0_), channel_id=1, source_target_pairs={{0,1},{1,0},{2,3},{3,2},{4,5},{5,4},{6,7},{7,6},{8,9},{9,8},{10,11... | collective-permute-start | bytes 589832 | tf_op jit(solution)/shard_map/ppermute | solution.py:37
  34.4 18.7 %collective-permute-start.13 = (bf16[144,768]{1,0:T(8,128)(2,1)S(1)}, bf16[144,768]{1,0:T(8,128)(2,1)S(1)}, u32[]{:S(2)}, u32[]{:S(2)}) collective-permute-start(bf16[144,768]{1,0:T(8,128)(2,1)S(1)} %attend_partner.2.refs_1_.refs_11_), channel_id=1, source_target_pairs={{0,16},{4,20},{8,24},{12,28},{16,0},{20,4},{24,8},{28,12},{1,17},{... | collective-permute-start | bytes 663560 | tf_op jit(solution)/shard_map/ppermute | solution.py:32
  35.3 17.7 %slice-start.2 = ((s8[4718592]{0:T(1024)(128)(4,1)}), s8[4194304]{0:T(1024)(128)(4,1)S(1)}, s32[]{:S(2)}) async-start(s8[4718592]{0:T(1024)(128)(4,1)} %bitcast.3), calls=%async_computation.2 | async-start | bytes 8388608
  35.3 17.7 %slice-start.3 = ((s8[4718592]{0:T(1024)(128)(4,1)}), s8[524288]{0:T(1024)(128)(4,1)S(1)}, s32[]{:S(2)}) async-start(s8[4718592]{0:T(1024)(128)(4,1)} %bitcast.3), calls=%async_computation.3 | async-start | bytes 1048576
  35.4 1.5 %collective-permute-start.12 = (bf16[128,768]{1,0:T(8,128)(2,1)S(1)}, bf16[128,768]{1,0:T(8,128)(2,1)S(1)}, u32[]{:S(2)}, u32[]{:S(2)}) collective-permute-start(bf16[128,768]{1,0:T(8,128)(2,1)S(1)} %relay.11.refs_1_.refs_12_.refs_3_), channel_id=1, source_target_pairs={{0,1},{1,0},{2,3},{3,2},{4,5},{5,4},{6,7},{7,6},{8,9},{9,8},{10,11... | collective-permute-start | bytes 589832 | tf_op jit(solution)/shard_map/ppermute | solution.py:37
  40.2 17.0 %collective-permute-start.18 = (bf16[144,768]{1,0:T(8,128)(2,1)S(1)}, bf16[144,768]{1,0:T(8,128)(2,1)S(1)}, u32[]{:S(2)}, u32[]{:S(2)}) collective-permute-start(bf16[144,768]{1,0:T(8,128)(2,1)S(1)} %attend_partner.3.refs_13_), channel_id=1, source_target_pairs={{0,16},{4,20},{8,24},{12,28},{16,0},{20,4},{24,8},{28,12},{1,17},{... | collective-permute-start | bytes 663560 | tf_op jit(solution)/shard_map/ppermute | solution.py:32
  53.9 1.4 %collective-permute-start.15 = (bf16[128,384]{1,0:T(8,128)(2,1)S(1)}, bf16[128,384]{1,0:T(8,128)(2,1)S(1)}, u32[]{:S(2)}, u32[]{:S(2)}) collective-permute-start(bf16[128,384]{1,0:T(8,128)(2,1)S(1)} %get-tuple-element.60), channel_id=1, source_target_pairs={{0,1},{1,0},{2,3},{3,2},{4,5},{5,4},{6,7},{7,6},{8,9},{9,8},{10,11... | collective-permute-start | bytes 294920 | tf_op jit(solution)/shard_map/ppermute | solution.py:37
  53.9 1.4 %collective-permute-start.16 = (bf16[128,384]{1,0:T(8,128)(2,1)S(1)}, bf16[128,384]{1,0:T(8,128)(2,1)S(1)}, u32[]{:S(2)}, u32[]{:S(2)}) collective-permute-start(bf16[128,384]{1,0:T(8,128)(2,1)S(1)} %get-tuple-element.61), channel_id=1, source_target_pairs={{0,1},{1,0},{2,3},{3,2},{4,5},{5,4},{6,7},{7,6},{8,9},{9,8},{10,11... | collective-permute-start | bytes 294920 | tf_op jit(solution)/shard_map/ppermute | solution.py:37
  55.4 7.2 %collective-permute-start.17 = (bf16[128,768]{1,0:T(8,128)(2,1)S(1)}, bf16[128,768]{1,0:T(8,128)(2,1)S(1)}, u32[]{:S(2)}, u32[]{:S(2)}) collective-permute-start(bf16[128,768]{1,0:T(8,128)(2,1)S(1)} %sum_cores.2.refs_6_), channel_id=1, source_target_pairs={{0,2},{1,3},{2,0},{3,1},{4,6},{5,7},{6,4},{7,5},{8,10},{9,11},{10,... | collective-permute-start | bytes 589832 | tf_op jit(solution)/shard_map/ppermute | solution.py:32
  58.0 1.8 %collective-permute-start.20 = (bf16[128,384]{1,0:T(8,128)(2,1)S(1)}, bf16[128,384]{1,0:T(8,128)(2,1)S(1)}, u32[]{:S(2)}, u32[]{:S(2)}) collective-permute-start(bf16[128,384]{1,0:T(8,128)(2,1)S(1)} %get-tuple-element.68), channel_id=1, source_target_pairs={{0,1},{1,0},{2,3},{3,2},{4,5},{5,4},{6,7},{7,6},{8,9},{9,8},{10,11... | collective-permute-start | bytes 294920 | tf_op jit(solution)/shard_map/ppermute | solution.py:37
  58.1 1.8 %collective-permute-start.21 = (bf16[128,384]{1,0:T(8,128)(2,1)S(1)}, bf16[128,384]{1,0:T(8,128)(2,1)S(1)}, u32[]{:S(2)}, u32[]{:S(2)}) collective-permute-start(bf16[128,384]{1,0:T(8,128)(2,1)S(1)} %get-tuple-element.69), channel_id=1, source_target_pairs={{0,1},{1,0},{2,3},{3,2},{4,5},{5,4},{6,7},{7,6},{8,9},{9,8},{10,11... | collective-permute-start | bytes 294920 | tf_op jit(solution)/shard_map/ppermute | solution.py:37
  58.6 6.9 %collective-permute-start.14 = (bf16[128,768]{1,0:T(8,128)(2,1)S(1)}, bf16[128,768]{1,0:T(8,128)(2,1)S(1)}, u32[]{:S(2)}, u32[]{:S(2)}) collective-permute-start(bf16[128,768]{1,0:T(8,128)(2,1)S(1)} %get-tuple-element.58.refs_3_), channel_id=1, source_target_pairs={{0,1},{1,0},{2,3},{3,2},{4,5},{5,4},{6,7},{7,6},{8,9},{9,8},{10,11... | collective-permute-start | bytes 589832 | tf_op jit(solution)/shard_map/ppermute | solution.py:37
  59.4 6.1 %collective-permute-start.19 = (bf16[128,768]{1,0:T(8,128)(2,1)S(1)}, bf16[128,768]{1,0:T(8,128)(2,1)S(1)}, u32[]{:S(2)}, u32[]{:S(2)}) collective-permute-start(bf16[128,768]{1,0:T(8,128)(2,1)S(1)} %get-tuple-element.66.refs_3_), channel_id=1, source_target_pairs={{0,1},{1,0},{2,3},{3,2},{4,5},{5,4},{6,7},{7,6},{8,9},{9,8},{10,11... | collective-permute-start | bytes 589832 | tf_op jit(solution)/shard_map/ppermute | solution.py:37
  62.7 6.4 %collective-permute-start.22 = (bf16[128,768]{1,0:T(8,128)(2,1)S(1)}, bf16[128,768]{1,0:T(8,128)(2,1)S(1)}, u32[]{:S(2)}, u32[]{:S(2)}) collective-permute-start(bf16[128,768]{1,0:T(8,128)(2,1)S(1)} %sum_cores.3.refs_7_), channel_id=1, source_target_pairs={{0,2},{1,3},{2,0},{3,1},{4,6},{5,7},{6,4},{7,5},{8,10},{9,11},{10,... | collective-permute-start | bytes 589832 | tf_op jit(solution)/shard_map/ppermute | solution.py:32

commit v7 on v6

v7 whole, which is shorter than its diff:
```python
import functools
import math

import jax
import jax.numpy as jnp
from jax import lax
from jax.experimental import pallas as pl
from jax.experimental.pallas import tpu as pltpu
from jax.sharding import PartitionSpec as P

HD = 128
LANES = 128
STAT_ROWS = 8
ROW_TILE = 16
CORES = 2
CHUNK_UNITS = (5, 5, 6)
FAR_PIECES = 3
COST_WEIGHT = 0.0005
FIRST_MICROS = 2
FLOPS_PER_MICRO = 1_000_000_000
MIB = 1 << 20

rope_base = 500000.0
neg_large = -1e30
log2_scale = math.log2(math.e) / math.sqrt(HD)

VMEM = pl.BlockSpec(memory_space=pltpu.VMEM)
ANY = pl.BlockSpec(memory_space=pl.ANY)


def shifted(shard, axis, by):
    devices = lax.axis_size(axis)
    return lax.ppermute(shard, axis, [(i, (i + by) % devices) for i in range(devices)])


def other_core(shard):
    devices = lax.axis_size("head")
    return lax.ppermute(shard, "head", [(i, i ^ 1) for i in range(devices)])


def other_chips(own):
    chips = lax.axis_size("head") // CORES
    return [shifted(own, "head", CORES * k) for k in range(1, chips)]


def place_of(requests):
    member = lax.axis_index("seq")
    return lax.rem(member, requests), lax.div(member, requests)


def source_of(position_in, turn, groups):
    return lax.rem(position_in + (groups - turn), groups)


def dot(left, right):
    return jnp.dot(left, right, preferred_element_type=jnp.float32)


def dot_transposed(left, right):
    return lax.dot_general(
        left, right, (((1,), (1,)), ((), ())), preferred_element_type=jnp.float32
    )


def call(
    kernel, out_shape, arrays, limit, flops, transcendentals, name, earlier=(),
    scratch=(), micros=0,
):
    moved = sum(a.size * a.dtype.itemsize for a in arrays)
    moved += sum(math.prod(s.shape) * s.dtype.itemsize for s in out_shape)
    read = len(arrays)
    skipped = len(earlier)

    def body(*refs):
        kernel(*refs[:read], *refs[read + skipped :])

    return pl.pallas_call(
        body,
        out_shape=out_shape,
        in_specs=[VMEM] * len(arrays) + [ANY] * skipped,
        out_specs=[VMEM] * len(out_shape),
        scratch_shapes=scratch,
        compiler_params=pltpu.CompilerParams(vmem_limit_bytes=limit * MIB),
        cost_estimate=pl.CostEstimate(
            flops=max(int(COST_WEIGHT * flops), int(micros * FLOPS_PER_MICRO)),
            bytes_accessed=int(COST_WEIGHT * moved),
            transcendentals=int(COST_WEIGHT * transcendentals),
        ),
        name=name,
    )(*arrays, *earlier)


def whole_of(blocks):
    parts = [block[...] for block in blocks]
    return jnp.concatenate(parts, 0) if len(parts) > 1 else parts[0]


def relay_kernel(count, *refs):
    whole = whole_of(refs[:count])
    at = 0
    for ref in refs[count:]:
        ref[...] = whole[at : at + ref.shape[0]]
        at = (at + ref.shape[0]) % whole.shape[0]


def relay(blocks, sizes, earlier):
    shapes = [jax.ShapeDtypeStruct((size, *blocks[0].shape[1:]), blocks[0].dtype) for size in sizes]
    kernel = functools.partial(relay_kernel, len(blocks))
    return call(kernel, shapes, [*blocks], 4, 0, 0, "relay", earlier)


def mark_kernel(mark):
    lane = lax.broadcasted_iota(jnp.int32, mark.shape, 1)
    mark[...] = jnp.where(lane == 0, 1.0, 0.0).astype(mark.dtype)


def marks(rows):
    shape = jax.ShapeDtypeStruct((rows, LANES), jnp.bfloat16)
    return call(mark_kernel, [shape], [], 4, 0, 0, "marks", micros=FIRST_MICROS)[0]


def tables_kernel(groups, lengths_in, offsets_in, cosine, sine, *scratch):
    lengths, offsets, semaphores = scratch
    numbers = [
        pltpu.make_async_copy(lengths_in, lengths, semaphores.at[0]),
        pltpu.make_async_copy(offsets_in, offsets, semaphores.at[1]),
    ]
    for copy in numbers:
        copy.start()
    rows = cosine.shape[0] // groups
    for copy in numbers:
        copy.wait()
    request, position_in = place_of(lengths.shape[0])
    lane = lax.broadcasted_iota(jnp.int32, (rows, LANES), 1)
    row = lax.broadcasted_iota(jnp.int32, (rows, LANES), 0)
    half = lax.rem(lane, HD // 2).astype(jnp.float32)
    frequency = jnp.exp2(half * (-2.0 / HD * math.log2(rope_base)))
    sign = jnp.where(lane < HD // 2, -1.0, 1.0)
    for turn in range(groups):
        first = source_of(position_in, turn, groups) * rows
        first = first + offsets[request] + lengths[request]
        angles = (row + first).astype(jnp.float32) * frequency
        part = slice(turn * rows, (turn + 1) * rows)
        cosine[part] = jnp.cos(angles)
        sine[part] = jnp.sin(angles) * sign


def rope_tables(lengths, offsets, groups, rows, earlier):
    table = jax.ShapeDtypeStruct((groups * rows, LANES), jnp.float32)
    return call(
        functools.partial(tables_kernel, groups),
        [table, table],
        [lengths, offsets],
        12,
        0,
        0,
        "rope_tables",
        earlier,
        [
            pltpu.SMEM(lengths.shape, lengths.dtype),
            pltpu.SMEM(offsets.shape, offsets.dtype),
            pltpu.SemaphoreType.DMA((2,)),
        ],
    )


def widen_kernel(keys, values, mark, lengths_in, wide_keys, wide_values, lengths, semaphore):
    number = pltpu.make_async_copy(lengths_in, lengths, semaphore)
    number.start()
    slots = keys.shape[0]
    heads = keys.shape[1] // HD
    for head in range(heads):
        own = slice(head * HD, (head + 1) * HD)
        wide_keys[head, :, :HD] = keys[:, own]
        wide_values[head, :, :HD] = values[:, own]
        wide_values[head, :, HD:] = mark[:slots]
    number.wait()
    request, position_in = place_of(lengths.shape[0])
    slot = lax.broadcasted_iota(jnp.int32, (slots, LANES), 0) + position_in * slots
    lane = lax.broadcasted_iota(jnp.int32, (slots, LANES), 1)
    bias = jnp.where((lane == 0) & (slot >= lengths[request]), neg_large, 0.0).astype(jnp.bfloat16)
    for head in range(heads):
        wide_keys[head, :, HD:] = bias


def widen(keys, values, mark, lengths, earlier):
    slots, width = keys.shape
    wide = jax.ShapeDtypeStruct((width // HD, slots, HD + LANES), jnp.bfloat16)
    return call(
        widen_kernel,
        [wide, wide],
        [keys, values, mark, lengths],
        12,
        0,
        0,
        "widen_caches",
        earlier,
        [pltpu.SMEM(lengths.shape, lengths.dtype), pltpu.SemaphoreType.DMA],
    )


def rotate(vectors, cosine, sine):
    return vectors * cosine + pltpu.roll(vectors, HD // 2, 1) * sine


def project_normed(pieces, gain, weights):
    heads = gain.shape[0]
    width = gain.shape[2]
    me = lax.axis_index("head")
    squares = 0.0
    sums = [0.0] * len(weights)
    for index, piece in enumerate(pieces):
        owner = lax.rem(me + (heads - CORES * (index % (heads // CORES))), heads)
        if index >= heads // CORES:
            owner = owner ^ 1
        wide = piece.astype(jnp.float32)
        scaled = (wide * gain[owner]).astype(jnp.bfloat16)
        along = pl.ds(pl.multiple_of(owner * width, LANES), width)
        for place, weight in enumerate(weights):
            sums[place] = sums[place] + dot(scaled, weight[along, :])
        squares = squares + jnp.sum(wide * wide, -1, keepdims=True)
    factor = lax.rsqrt(squares / (heads * width) + 1e-05)
    return [total * factor for total in sums]


def stat_rows(columns, rows):
    padded = -(-rows // LANES) * LANES
    lane = lax.broadcasted_iota(jnp.int32, (padded, LANES), 1)
    table = jnp.zeros((padded, LANES), jnp.float32)
    for index, column in enumerate(columns):
        if padded > rows:
            filler = jnp.zeros((padded - rows, 1), jnp.float32)
            column = jnp.concatenate([column, filler], 0)
        table = jnp.where(lane == index, column, table)
    return table.T[:STAT_ROWS]


def stat_columns(stats):
    padding = jnp.zeros((LANES - STAT_ROWS, stats.shape[1]), jnp.float32)
    return jnp.concatenate([stats, padding], 0).T


def stat_places(count, width):
    places = []
    for index in range(3 * count):
        row, lane = divmod(index * LANES, width)
        places.append((row * ROW_TILE, lane))
    return [places[3 * chunk : 3 * chunk + 3] for chunk in range(count)]


def tail_rows(count, width):
    return -(-3 * count * LANES // width) * ROW_TILE if count else 0


def split_refs(counts, refs):
    parts = []
    for count in counts:
        parts.append(refs[:count])
        refs = refs[count:]
    return parts, refs


def head_queries(product, cosine, sine):
    return [
        (rotate(product[:, at : at + HD], cosine, sine) * log2_scale).astype(jnp.bfloat16)
        for at in range(0, product.shape[1], HD)
    ]


def stack_heads(queries, head, repeat, at, rows):
    own = queries[head * repeat : (head + 1) * repeat]
    return jnp.concatenate([query[at : at + rows] for query in own], 0)


def weigh(scores, values):
    largest = functools.reduce(
        jnp.maximum, [jnp.max(score, -1, keepdims=True) for score in scores]
    )
    summed = 0.0
    for score, value in zip(scores, values):
        weights = jnp.exp2(score - largest).astype(jnp.bfloat16)
        summed = summed + dot(weights, value)
    denominator = summed[:, HD : HD + 1]
    return summed[:, :HD] / denominator, largest + jnp.log2(denominator)


def attend_kernel(counts, sent, table_at, *refs):
    *blocks, weights, old_stats = split_refs([*counts, 7, max(sent - 1, 0)], refs)[0]
    outputs = refs[sum(counts) + 7 + max(sent - 1, 0) :]
    gain, w_query, cosine, sine, wide_keys, wide_values, mark = weights
    pieces = [whole_of(one) for one in blocks]
    rows = pieces[0].shape[0]
    (product,) = project_normed(pieces, gain, [w_query])
    part = slice(table_at, table_at + rows)
    queries = head_queries(product, cosine[part], sine[part])
    kv_heads = wide_keys.shape[0]
    repeat = len(queries) // kv_heads
    ones = mark[: repeat * rows]
    scores = []
    for head in range(kv_heads):
        stacked = jnp.concatenate([stack_heads(queries, head, repeat, 0, rows), ones], 1)
        scores.append(dot_transposed(stacked, wide_keys[head]))
    columns = []
    for head in range(kv_heads):
        result, logs = weigh([scores[head]], [wide_values[head]])
        for turn in range(repeat):
            at = (head * repeat + turn) * HD
            outputs[0][:rows, at : at + HD] = result[turn * rows : (turn + 1) * rows].astype(
                jnp.bfloat16
            )
            columns.append(logs[turn * rows : (turn + 1) * rows])
    stats = stat_rows(columns, rows)
    if not sent:
        outputs[1][...] = stats
        return
    packed = outputs[0]
    packed[rows:] = jnp.zeros((packed.shape[0] - rows, packed.shape[1]), jnp.bfloat16)
    padding = jnp.zeros((ROW_TILE - STAT_ROWS, LANES), jnp.float32)
    places = stat_places(sent, packed.shape[1])
    for rest, parts in zip([ref[...] for ref in old_stats] + [stats], places):
        rest = jnp.concatenate([rest, padding], 0)
        for row, lane in parts:
            rounded = rest.astype(jnp.bfloat16)
            packed[rows + row : rows + row + ROW_TILE, lane : lane + LANES] = rounded
            rest = rest - rounded.astype(jnp.float32)


def attend(
    pieces, gain, w_query, tables, wide_keys, wide_values, mark, table_at, sent, old_stats, earlier
):
    counts = [len(blocks) for blocks in pieces]
    flat = [block for blocks in pieces for block in blocks]
    rows = sum(block.shape[0] for block in pieces[0])
    out_width = w_query.shape[1]
    slots = wide_keys.shape[1]
    total = rows + tail_rows(sent, out_width)
    out_shape = [jax.ShapeDtypeStruct((total, out_width), jnp.bfloat16)]
    if not sent:
        out_shape.append(jax.ShapeDtypeStruct((STAT_ROWS, LANES), jnp.float32))
    return call(
        functools.partial(attend_kernel, counts, sent, table_at),
        out_shape,
        [*flat, gain, w_query, *tables, wide_keys, wide_values, mark, *old_stats],
        28,
        2 * rows * out_width * (w_query.shape[0] + 4 * slots),
        rows * out_width // HD * slots,
        "attend_partner",
        earlier,
    )


def attend_own_kernel(requests, counts, others, *refs):
    parts, outputs = split_refs([*counts, 9, others, others], refs)
    *blocks, weights, other_keys, other_values = parts
    pieces = [whole_of(one) for one in blocks]
    gain, w_query, w_key, w_value, cosine, sine, wide_keys, wide_values, mark = weights
    partial, stats, new_keys, new_values = outputs
    rows = pieces[0].shape[0]
    groups = others + 1
    query_sum, key_sum, value_sum = project_normed(pieces, gain, [w_query, w_key, w_value])
    cosine, sine = cosine[:rows], sine[:rows]
    queries = head_queries(query_sum, cosine, sine)
    kv_heads = wide_keys.shape[0]
    repeat = len(queries) // kv_heads
    own_keys = []
    for head in range(kv_heads):
        shared = slice(head * HD, (head + 1) * HD)
        own_keys.append(rotate(key_sum[:, shared], cosine, sine).astype(jnp.bfloat16))
        new_keys[:, shared] = own_keys[head]
    own_values = value_sum.astype(jnp.bfloat16)
    new_values[...] = own_values
    ones = mark[:rows]
    position_in = place_of(requests)[1]
    hidden = []
    for turn in range(1, groups):
        later = source_of(position_in, turn, groups) > position_in
        hidden.append(jnp.where(later, ones.astype(jnp.float32) * neg_large, 0.0).astype(jnp.bfloat16))
    fresh_keys = []
    fresh_values = []
    for head in range(kv_heads):
        shared = slice(head * HD, (head + 1) * HD)
        wide = [jnp.concatenate([own_values[:, shared], ones], 1)]
        wide += [jnp.concatenate([ref[:, shared], ones], 1) for ref in other_values]
        fresh_values.append(wide)
        fresh_keys.append(
            [jnp.concatenate([ref[:, shared], bias], 1) for ref, bias in zip(other_keys, hidden)]
        )
    step = min(rows, LANES)
    tiles = [(head, at) for head in range(kv_heads) for at in range(0, rows, step)]
    marked = mark[: repeat * step]

    def scores_of(head, at):
        stacked = stack_heads(queries, head, repeat, at, step)
        token = lax.broadcasted_iota(jnp.int32, (step, rows), 0) + at
        within = lax.broadcasted_iota(jnp.int32, (step, rows), 1)
        causal = jnp.concatenate([jnp.where(within <= token, 0.0, neg_large)] * repeat, 0)
        fresh = dot_transposed(stacked, own_keys[head]) + causal
        stacked = jnp.concatenate([stacked, marked], 1)
        return [dot_transposed(stacked, wide_keys[head]), fresh] + [
            dot_transposed(stacked, keys) for keys in fresh_keys[head]
        ]

    columns = {}
    following = scores_of(*tiles[0])
    for index, (head, at) in enumerate(tiles):
        scores = following
        if index + 1 < len(tiles):
            following = scores_of(*tiles[index + 1])
        result, logs = weigh(scores, [wide_values[head]] + fresh_values[head])
        for turn in range(repeat):
            part = slice(turn * step, (turn + 1) * step)
            to = slice((head * repeat + turn) * HD, (head * repeat + turn + 1) * HD)
            partial[at : at + step, to] = result[part]
            columns.setdefault(head * repeat + turn, []).append(logs[part])
    stats[...] = stat_rows([jnp.concatenate(parts, 0) for parts in columns.values()], rows)


def attend_own(
    requests, pieces, gain, weights, tables, wide_keys, wide_values, mark, other_rows, earlier
):
    counts = [len(blocks) for blocks in pieces]
    flat = [block for blocks in pieces for block in blocks]
    rows = sum(block.shape[0] for block in pieces[0])
    out_width = weights[0].shape[1]
    slots = wide_keys.shape[1]
    new = jax.ShapeDtypeStruct((rows, weights[1].shape[1]), jnp.bfloat16)
    other_keys, other_values = zip(*other_rows)
    return call(
        functools.partial(attend_own_kernel, requests, counts, len(other_rows)),
        [
            jax.ShapeDtypeStruct((rows, out_width), jnp.float32),
            jax.ShapeDtypeStruct((STAT_ROWS, rows), jnp.float32),
            new,
            new,
        ],
        [
            *flat, gain, *weights, *tables, wide_keys, wide_values, mark, *other_keys,
            *other_values,
        ],
        28,
        2 * rows * out_width * (weights[0].shape[0] + 4 * slots),
        rows * out_width // HD * slots,
        "attend_own",
        earlier,
    )


def fresh_kernel(counts, table_at, *refs):
    blocks, refs = split_refs(counts, refs)
    gain, w_key, w_value, cosine, sine, new_keys, new_values = refs
    rows = new_keys.shape[0]
    pieces = [whole_of(one) for one in blocks]
    keys, values = project_normed(pieces, gain, [w_key, w_value])
    cosine = cosine[table_at : table_at + rows]
    sine = sine[table_at : table_at + rows]
    for head in range(keys.shape[1] // HD):
        own = slice(head * HD, (head + 1) * HD)
        new_keys[:, own] = rotate(keys[:, own], cosine, sine).astype(jnp.bfloat16)
    new_values[...] = values.astype(jnp.bfloat16)


def fresh(pieces, gain, w_key, w_value, tables, table_at, earlier):
    flat = [block for blocks in pieces for block in blocks]
    rows = sum(block.shape[0] for block in pieces[0])
    shape = jax.ShapeDtypeStruct((rows, w_key.shape[1]), jnp.bfloat16)
    return call(
        functools.partial(fresh_kernel, [len(blocks) for blocks in pieces], table_at),
        [shape, shape],
        [*flat, gain, w_key, w_value, *tables],
        20,
        4 * rows * w_key.size,
        0,
        "fresh_kv",
        earlier,
    )


def write_rows(target, fresh_rows, first):
    rows = fresh_rows.shape[0]
    slab_rows = target.shape[0]
    span = rows + ROW_TILE
    start = jnp.clip(first, 0, slab_rows - span)
    start = start - lax.rem(start, ROW_TILE)
    window = pl.ds(pl.multiple_of(start, ROW_TILE), span)
    shift = start - first
    place = lax.broadcasted_iota(jnp.int32, (span, rows), 0) + shift
    chosen = place == lax.broadcasted_iota(jnp.int32, (span, rows), 1)
    moved = dot(chosen.astype(jnp.bfloat16), fresh_rows)
    row = lax.broadcasted_iota(jnp.int32, (span, target.shape[1]), 0) + shift
    inside = (row >= 0) & (row < rows)
    old = target[window, :].astype(jnp.float32)
    target[window, :] = jnp.where(inside, moved, old).astype(jnp.bfloat16)


def update_kernel(groups, *refs):
    key_refs, value_refs, refs = refs[:groups], refs[groups : 2 * groups], refs[2 * groups :]
    keys, values, lengths_in, keys_updated, values_updated, done, lengths, semaphore = refs
    number = pltpu.make_async_copy(lengths_in, lengths, semaphore)
    number.start()
    keys_updated[...] = keys[...]
    values_updated[...] = values[...]
    done[...] = jnp.zeros(done.shape, done.dtype)
    number.wait()
    request, position_in = place_of(lengths.shape[0])
    rows = key_refs[0].shape[0]
    for turn in range(groups):
        source = source_of(position_in, turn, groups)
        first = lengths[request] + source * rows - position_in * keys.shape[0]
        write_rows(keys_updated, key_refs[turn][...], first)
        write_rows(values_updated, value_refs[turn][...], first)


def update(lengths, new_keys, new_values, keys, values, earlier):
    groups = len(new_keys)
    slab = jax.ShapeDtypeStruct(keys.shape, keys.dtype)
    return call(
        functools.partial(update_kernel, groups),
        [slab, slab, jax.ShapeDtypeStruct((STAT_ROWS, LANES), jnp.float32)],
        [*new_keys, *new_values, keys, values, lengths],
        20,
        4 * new_keys[0].size * new_keys[0].shape[0] * groups,
        0,
        "update_caches",
        earlier,
        [pltpu.SMEM(lengths.shape, lengths.dtype), pltpu.SemaphoreType.DMA],
    )


def combine_kernel(row_at, sizes, *refs):
    heads = lax.axis_size("head")
    chips = heads // CORES
    outputs = FAR_PIECES * (chips - 1)
    (own_partial, own_stats), refs = refs[:2], refs[2:]
    received = refs[: -2 - outputs]
    w_out, merged_rows, *far = refs[-2 - outputs :]
    width = own_partial.shape[1]
    rows = merged_rows.shape[0]
    part = slice(row_at, row_at + rows)
    logs = [stat_columns(own_stats[...])[part]]
    partials = [own_partial[part]]
    for turn in range(0, len(received), len(sizes)):
        chunks = received[turn : turn + len(sizes)]
        last = chunks[-1]
        columns = []
        for size, places in zip(sizes, stat_places(len(sizes), width)):
            stats = sum(
                last[sizes[-1] + row : sizes[-1] + row + ROW_TILE, lane : lane + LANES].astype(
                    jnp.float32
                )
                for row, lane in places
            )
            columns.append(stat_columns(stats[:STAT_ROWS])[:size])
        logs.append(jnp.concatenate(columns, 0))
        partials.append(jnp.concatenate([ref[:size] for ref, size in zip(chunks, sizes)], 0))
    largest = functools.reduce(jnp.maximum, logs)
    shares = [jnp.exp2(log - largest) for log in logs]
    total = functools.reduce(jnp.add, shares)
    shares = [share / total for share in shares]
    attended = []
    for head in range(width // HD):
        at = slice(head * HD, (head + 1) * HD)
        column = slice(head, head + 1)
        merged = 0.0
        for partial, share in zip(partials, shares):
            merged = merged + partial[:, at].astype(jnp.float32) * share[:, column]
        attended.append(merged.astype(jnp.bfloat16))
    attended = jnp.concatenate(attended, 1)
    merged_rows[...] = attended
    for ahead in range(1, chips):
        result = block_product(attended, w_out, ahead, 1)
        piece = result.shape[1] // FAR_PIECES
        for index in range(FAR_PIECES):
            target = far[FAR_PIECES * (ahead - 1) + index]
            target[...] = result[:, index * piece : (index + 1) * piece]


def block_product(attended, w_out, ahead, flip):
    heads = lax.axis_size("head")
    block_width = w_out.shape[1] // heads
    block = lax.rem(lax.axis_index("head") + CORES * ahead, heads) ^ flip
    along = pl.ds(pl.multiple_of(block * block_width, LANES), block_width)
    return dot(attended, w_out[:, along]).astype(jnp.bfloat16)


def project_kernel(merged_rows, w_out, far, *near):
    attended = merged_rows[...]
    far[...] = block_product(attended, w_out, 0, 1)
    for ahead, target in enumerate(near):
        target[...] = block_product(attended, w_out, ahead, 0)


def combine(row_at, sizes, own, received, w_out, heads, earlier):
    rows = sum(sizes)
    chips = heads // CORES
    width = w_out.shape[1] // heads
    merged = jax.ShapeDtypeStruct((rows, own[0].shape[1]), jnp.bfloat16)
    piece = jax.ShapeDtypeStruct((rows, width // FAR_PIECES), jnp.bfloat16)
    merged, *far = call(
        functools.partial(combine_kernel, row_at, sizes),
        [merged] + [piece] * (FAR_PIECES * (chips - 1)),
        [*own, *received, w_out],
        20,
        rows * w_out.size,
        0,
        "combine",
        earlier,
    )
    return merged, [far[k * FAR_PIECES : (k + 1) * FAR_PIECES] for k in range(chips - 1)]


def project(merged, w_out, heads):
    block = jax.ShapeDtypeStruct((merged.shape[0], w_out.shape[1] // heads), jnp.bfloat16)
    far, *near = call(
        project_kernel,
        [block] * (1 + heads // CORES),
        [merged, w_out],
        20,
        2 * merged.shape[0] * w_out.size,
        0,
        "project",
    )
    return far, near


def sum_kernel(near, *refs):
    *far, result = refs
    total = jnp.concatenate([ref[...] for ref in far], 1).astype(jnp.float32)
    result[...] = (near[...].astype(jnp.float32) + total).astype(result.dtype)


def sum_cores(near, far, earlier):
    shape = jax.ShapeDtypeStruct(near.shape, near.dtype)
    return call(sum_kernel, [shape], [near, *far], 8, near.size, 0, "sum_cores", earlier)[0]


def finish_kernel(counts, *refs):
    groups, (result,) = split_refs(counts, refs)
    at = 0
    for group in groups:
        rows = group[0].shape[0]
        total = sum(ref[...].astype(jnp.float32) for ref in group)
        result[at : at + rows] = total.astype(result.dtype)
        at += rows


def finish(groups, earlier):
    parts = [part for group in groups for part in group]
    rows = sum(group[0].shape[0] for group in groups)
    shape = jax.ShapeDtypeStruct((rows, parts[0].shape[1]), jnp.bfloat16)
    kernel = functools.partial(finish_kernel, [len(group) for group in groups])
    return call(kernel, [shape], parts, 8, 0, 0, "finish", earlier)[0]


def shards(
    tokens,
    norm_gain,
    w_query,
    w_key,
    w_value,
    w_out,
    keys_cache,
    values_cache,
    cached_lengths,
    rope_offsets,
):
    rows, width = tokens.shape
    requests = cached_lengths.shape[0]
    groups = lax.axis_size("seq") // requests
    heads = lax.axis_size("head")
    chips = heads // CORES
    gain = norm_gain.reshape(heads, 1, width)
    sizes = [rows * units // sum(CHUNK_UNITS) for units in CHUNK_UNITS]
    starts = [sum(sizes[:chunk]) for chunk in range(len(sizes))]
    cuts = [tokens[at : at + size] for at, size in zip(starts, sizes)]

    mark = marks(keys_cache.shape[0])
    tables = rope_tables(cached_lengths, rope_offsets, groups, rows, [mark])
    wide_keys, wide_values = widen(keys_cache, values_cache, mark, cached_lengths, tables[:1])

    def send_tokens(piece):
        return [shifted(piece, "seq", turn * requests) for turn in range(1, groups)]

    from_chips = other_chips(tokens)
    arrived = [send_tokens(cuts[0])]
    earlier = [wide_keys]
    (late,) = relay([cuts[1]], sizes[1:2], earlier)
    arrived.append(send_tokens(late))
    own_crossed = other_core(tokens)
    earlier = [late, own_crossed]

    def to_chips(chunk, earlier):
        passed = [relay([piece], sizes[chunk : chunk + 1], earlier)[0] for piece in arrived[chunk]]
        sent = [(piece, other_chips(piece), other_core(piece)) for piece in passed]
        return sent, passed

    def to_cores(chunk, sent, earlier):
        gathered = []
        size = sizes[chunk]
        for own, others, crossed in sent:
            passed = [relay([one], [size, size // 2, size // 2], earlier + [crossed]) for one in others]
            gathered.append(
                [[own]] + [[one[0]] for one in passed] + [[crossed]]
                + [[other_core(part) for part in one[1:]] for one in passed]
            )
            earlier = [one[0] for one in passed]
        return gathered, earlier

    sent_1, earlier = to_chips(0, earlier)
    (late,) = relay([cuts[2]], sizes[2:], from_chips + earlier)
    arrived.append(send_tokens(late))
    sent_2, earlier = to_chips(1, [late])
    gathered_1, earlier = to_cores(0, sent_1, earlier)

    statistics = [0, 2, 1]
    received = [[] for _ in sizes]
    kept = [[] for _ in range(groups)]

    def attend_chunk(chunk, gathered, earlier):
        partials = []
        for turn in range(1, groups):
            packed, *stats = attend(
                gathered[turn - 1], gain, w_query, tables, wide_keys, wide_values, mark,
                turn * rows + starts[chunk], statistics[chunk],
                kept[turn] if statistics[chunk] > 1 else [], earlier,
            )
            kept[turn] += stats
            earlier = [packed]
            partials.append(packed)
        return partials, earlier

    def send_back(chunk, partials):
        received[chunk] = [
            shifted(packed, "seq", -turn * requests) for turn, packed in enumerate(partials, 1)
        ]

    partials, earlier = attend_chunk(0, gathered_1, earlier)
    send_back(0, partials)
    sent_3, earlier = to_chips(2, earlier)
    gathered_2, earlier = to_cores(1, sent_2, earlier)
    partials, earlier = attend_chunk(1, gathered_2, earlier)
    own_along = [
        relay([piece], [rows, rows // 2, rows // 2], earlier) for piece in from_chips
    ]
    own_pieces = [[tokens]] + [[one[0]] for one in own_along] + [[own_crossed]]
    own_pieces += [[other_core(part) for part in one[1:]] for one in own_along]
    earlier = earlier + [one[0] for one in own_along]
    received[0] = [relay([piece], sizes[:1], earlier)[0] for piece in received[0]]
    partials = [relay([piece], piece.shape[:1], received[0])[0] for piece in partials]
    send_back(1, partials)
    gathered_3, earlier = to_cores(2, sent_3, partials)
    partials, earlier = attend_chunk(2, gathered_3, earlier)
    send_back(2, partials)
    gathered = [gathered_1, gathered_2, gathered_3]
    other_rows = []
    for turn in range(1, groups):
        pieces = [sum(blocks, []) for blocks in zip(*[chunk[turn - 1] for chunk in gathered])]
        other_rows.append(fresh(pieces, gain, w_key, w_value, tables, turn * rows, earlier))
        earlier = [other_rows[-1][0]]
    *own_part, own_keys, own_values = attend_own(
        requests, own_pieces, gain, [w_query, w_key, w_value], tables, wide_keys, wide_values,
        mark, other_rows, earlier,
    )
    new_keys, new_values = zip((own_keys, own_values), *other_rows)

    parts = []
    earlier = []
    for chunks in ((0, 1), (2,)):
        merged, fars = combine(
            starts[chunks[0]], [sizes[chunk] for chunk in chunks], own_part,
            [piece for turn in zip(*[received[chunk] for chunk in chunks]) for piece in turn],
            w_out, heads, earlier,
        )
        fars = [[other_core(part) for part in far] for far in fars]
        far, near = project(merged, w_out, heads)
        sums = [sum_cores(one, parts_far, [far]) for one, parts_far in zip(near[1:], fars)]
        from_chips = [shifted(one, "head", CORES * k) for k, one in enumerate(sums, 1)]
        parts.append([near[0], other_core(far), *from_chips])
        earlier = sums
    keys_updated, values_updated, done = update(
        cached_lengths, new_keys, new_values, keys_cache, values_cache, earlier
    )
    return (finish(parts, [done]), keys_updated, values_updated)


def solution(mesh):
    return jax.shard_map(
        shards,
        mesh=mesh,
        in_specs=(
            P("seq", "head"),
            P(),
            P(None, "head"),
            P(None, "head"),
            P(None, "head"),
            P("head", None),
            P("seq", "head"),
            P("seq", "head"),
            P(),
            P(),
        ),
        out_specs=(P("seq", "head"), P("seq", "head"), P("seq", "head")),
        check_vma=False,
    )
```

time: 70.2 us -> 69.9 us (level)
  the two profiles are of different devices: /device:TPU:0 before, /device:TPU:24 now
where the time goes in v7:
time: 69.9 us; the launch traced here: 69.8 us
  Pallas kernels  26.5 us (38%)
  waiting for transfers between devices  24.3 us (35%)
  starting transfers between devices  16.7 us (24%)
  local copies, waits for them, and re-layouts  1.24 us (2%)
  between operations  1.04 us (1%)
    pallas_call x27, Pallas kernels, call(): pl.pallas_call(body, out_shape=out_shape, in_specs=[VMEM] * len(arrays) +...  26.5 us
    ppermute x12, waiting for transfers between devices, shifted(): lax.ppermute(shard, axis, [(i, (i + by) % devices) for i in range(devices)])  21.5 us
    ppermute x12, starting transfers between devices, shifted(): lax.ppermute(shard, axis, [(i, (i + by) % devices) for i in range(devices)])  11.5 us
    ppermute x20, starting transfers between devices, other_core(): return lax.ppermute(shard, 'head', [(i, i ^ 1) for i in range(devices)])  5.22 us
    ppermute x20, waiting for transfers between devices, other_core(): return lax.ppermute(shard, 'head', [(i, i ^ 1) for i in range(devices)])  2.75 us
  transfers between devices with their start and end apart: 32, of which 11 were waited for; matrix products, arithmetic and copies ran while one was open for 1% of the time, Pallas kernels for 37%

profile of v7, /device:TPU:24, one launch (start us, length us, event | category | flops | bytes accessed | tf_op | source)
XLA Modules:
  0.0 69.8 jit_solution(15754817565179352733)
XLA Ops:
  0.6 1.6 %collective-permute-start = (bf16[256,768]{1,0:T(8,128)(2,1)}, bf16[256,768]{1,0:T(8,128)(2,1)S(1)}, u32[]{:S(2)}, u32[]{:S(2)}) collective-permute-start(bf16[256,768]{1,0:T(8,128)(2,1)} %refs_0_.5), channel_id=1, source_target_pairs={{0,2},{1,3},{2,0},{3,1},{4,6},{5,7},{6,4},{7,5},{8,10},{9,11},{10,... | collective-permute-start | bytes 1179656 | tf_op jit(solution)/shard_map/ppermute | solution.py:33
  2.2 1.0 %fusion = (bf16[80,768]{1,0:T(8,128)(2,1)S(1)}, bf16[80,768]{1,0:T(8,128)(2,1)S(1)}) fusion(bf16[256,768]{1,0:T(8,128)(2,1)} %refs_0_.5), kind=kLoop, calls=%fused_computation | loop fusion | bytes 491520 | tf_op jit(solution)/shard_map/slice | solution.py:674
  3.3 0.4 collective-permute-start.2
  3.7 0.2 copy-done.6
  3.9 1.6 %rope_tables.1 = (f32[512,128]{1,0:T(8,128)S(1)}, f32[512,128]{1,0:T(8,128)S(1)}) custom-call(s32[4]{0:T(128)S(1)} %copy-done.6, s32[4]{0:T(128)S(1)} %copy-done.7, bf16[2048,128]{1,0:T(8,128)(2,1)S(1)} %marks.1.refs_2_.refs_11_.refs_13_), custom_call_target="tpu_custom_call" | custom-call | bytes 262 | tf_op jit(solution)/shard_map/rope_tables/pallas_call | solution.py:77
  5.5 0.8 %widen_caches.1 = (bf16[2,2048,256]{2,1,0:T(8,128)(2,1)S(1)}, bf16[2,2048,256]{2,1,0:T(8,128)(2,1)S(1)}) custom-call(bf16[2048,256]{1,0:T(8,128)(2,1)S(1)} %copy-done.2, bf16[2048,256]{1,0:T(8,128)(2,1)S(1)} %copy-done.3, bf16[2048,128]{1,0:T(8,128)(2,1)S(1)} %marks.1.refs_2_.refs_11_.refs_13_, s32[4]{0:T(128)S(1)} %copy-done.6, ...), custom_call_target="tpu_custom_call" | custom-call | bytes 3407 | tf_op jit(solution)/shard_map/widen_caches/pallas_call | solution.py:77
  6.3 2.5 %collective-permute-start.1 = (bf16[80,768]{1,0:T(8,128)(2,1)S(1)}, bf16[80,768]{1,0:T(8,128)(2,1)S(1)}, u32[]{:S(2)}, u32[]{:S(2)}) collective-permute-start(bf16[80,768]{1,0:T(8,128)(2,1)S(1)} %relay.11.refs_1_), channel_id=1, source_target_pairs={{0,16},{4,20},{8,24},{12,28},{16,0},{20,4},{24,8},{28,12},{1,17},{... | collective-permute-start | bytes 368648 | tf_op jit(solution)/shard_map/ppermute | solution.py:33
  8.8 9.5 %collective-permute-done.2.refs_0_ = bf16[80,768]{1,0:T(8,128)(2,1)S(1)} collective-permute-done((bf16[80,768]{1,0:T(8,128)(2,1)S(1)}, bf16[80,768]{1,0:T(8,128)(2,1)S(1)}, u32[]{:S(2)}, u32[]{:S(2)}) %collective-permute-start.2) | collective-permute-done | bytes 122912 | tf_op jit(solution)/shard_map/ppermute | solution.py:33
  18.3 0.1 collective-permute-start.7
  18.6 2.3 %collective-permute-done.1.refs_0_ = bf16[80,768]{1,0:T(8,128)(2,1)S(1)} collective-permute-done((bf16[80,768]{1,0:T(8,128)(2,1)S(1)}, bf16[80,768]{1,0:T(8,128)(2,1)S(1)}, u32[]{:S(2)}, u32[]{:S(2)}) %collective-permute-start.1) | collective-permute-done | bytes 122912 | tf_op jit(solution)/shard_map/ppermute | solution.py:33
  20.9 0.1 collective-permute-start.10
  21.0 0.5 collective-permute-start.4
  21.6 2.6 %collective-permute-done.6.refs_0_ = bf16[80,768]{1,0:T(8,128)(2,1)S(1)} collective-permute-done((bf16[80,768]{1,0:T(8,128)(2,1)S(1)}, bf16[80,768]{1,0:T(8,128)(2,1)S(1)}, u32[]{:S(2)}, u32[]{:S(2)}) %collective-permute-start.6) | collective-permute-done | bytes 122912 | tf_op jit(solution)/shard_map/ppermute | solution.py:33
  24.2 0.5 collective-permute-start.9
  24.7 0.7 %collective-permute-done.8.refs_3_.refs_9_ = bf16[40,768]{1,0:T(8,128)(2,1)S(1)} collective-permute-done((bf16[40,768]{1,0:T(8,128)(2,1)S(1)}, bf16[40,768]{1,0:T(8,128)(2,1)S(1)}, u32[]{:S(2)}, u32[]{:S(2)}) %collective-permute-start.8) | collective-permute-done | bytes 61472 | tf_op jit(solution)/shard_map/ppermute | solution.py:38
  25.5 0.2 collective-permute-done.9.refs_4_.refs_10_
  25.6 2.9 %attend_partner.3 = (bf16[80,768]{1,0:T(8,128)(2,1)S(1)}, f32[8,128]{1,0:T(8,128)S(1)}) custom-call(bf16[80,768]{1,0:T(8,128)(2,1)S(1)} %relay.12.refs_2_.refs_0_, bf16[80,768]{1,0:T(8,128)(2,1)S(1)} %get-tuple-element.46.refs_1_.refs_12_.refs_3_, bf16[80,768]{1,0:T(8,128)(2,1)S(1)} %collective-permute-done.7.refs_2_.refs_6_, ...), custom_call_target="tpu_custom_call" | custom-call | flops 692060 | bytes 5296 | tf_op jit(solution)/shard_map/attend_partner/pallas_call | solution.py:77
  28.6 0.4 collective-permute-start.17
  29.0 1.2 %collective-permute-start.15 = (bf16[96,768]{1,0:T(8,128)(2,1)S(1)}, bf16[96,768]{1,0:T(8,128)(2,1)S(1)}, u32[]{:S(2)}, u32[]{:S(2)}) collective-permute-start(bf16[96,768]{1,0:T(8,128)(2,1)S(1)} %relay.16.refs_1_.refs_0_.refs_2_), channel_id=1, source_target_pairs={{0,2},{1,3},{2,0},{3,1},{4,6},{5,7},{6,4},{7,5},{8,10},{9,11},{10,... | collective-permute-start | bytes 442376 | tf_op jit(solution)/shard_map/ppermute | solution.py:33
  30.2 0.2 collective-permute-start.11
  30.5 0.3 collective-permute-start.12
  30.8 0.7 %collective-permute-done.11.refs_3_.refs_11_ = bf16[40,768]{1,0:T(8,128)(2,1)S(1)} collective-permute-done((bf16[40,768]{1,0:T(8,128)(2,1)S(1)}, bf16[40,768]{1,0:T(8,128)(2,1)S(1)}, u32[]{:S(2)}, u32[]{:S(2)}) %collective-permute-start.11) | collective-permute-done | bytes 61472 | tf_op jit(solution)/shard_map/ppermute | solution.py:38
  31.5 0.2 collective-permute-done.12.refs_4_.refs_12_
  31.7 2.9 %attend_partner.4.refs_1_.refs_0_ = bf16[96,768]{1,0:T(8,128)(2,1)S(1)} custom-call(bf16[80,768]{1,0:T(8,128)(2,1)S(1)} %relay.14.refs_1_.refs_0_, bf16[80,768]{1,0:T(8,128)(2,1)S(1)} %get-tuple-element.52.refs_1_.refs_13_.refs_4_, bf16[80,768]{1,0:T(8,128)(2,1)S(1)} %collective-permute-done.10.refs_2_.refs_7_, ...), custom_call_target="tpu_custom_call" | custom-call | flops 692060 | bytes 5308 | tf_op jit(solution)/shard_map/attend_partner/pallas_call | solution.py:77
  34.6 0.4 collective-permute-start.13
  35.1 0.2 collective-permute-start.14
  35.2 3.0 %collective-permute-done.16.refs_0_ = bf16[80,768]{1,0:T(8,128)(2,1)S(1)} collective-permute-done((bf16[80,768]{1,0:T(8,128)(2,1)S(1)}, bf16[80,768]{1,0:T(8,128)(2,1)S(1)}, u32[]{:S(2)}, u32[]{:S(2)}) %collective-permute-start.16) | collective-permute-done | bytes 122912 | tf_op jit(solution)/shard_map/ppermute | solution.py:33
  38.4 0.5 collective-permute-start.19
  38.9 0.8 %collective-permute-done.18.refs_3_.refs_13_ = bf16[48,768]{1,0:T(8,128)(2,1)S(1)} collective-permute-done((bf16[48,768]{1,0:T(8,128)(2,1)S(1)}, bf16[48,768]{1,0:T(8,128)(2,1)S(1)}, u32[]{:S(2)}, u32[]{:S(2)}) %collective-permute-start.18) | collective-permute-done | bytes 73760 | tf_op jit(solution)/shard_map/ppermute | solution.py:38
  39.7 0.2 collective-permute-done.19.refs_4_.refs_14_
  39.8 3.0 %attend_partner.5.refs_20_ = bf16[112,768]{1,0:T(8,128)(2,1)S(1)} custom-call(bf16[96,768]{1,0:T(8,128)(2,1)S(1)} %relay.16.refs_1_.refs_0_.refs_2_, bf16[96,768]{1,0:T(8,128)(2,1)S(1)} %get-tuple-element.59.refs_1_.refs_12_.refs_5_, bf16[96,768]{1,0:T(8,128)(2,1)S(1)} %collective-permute-done.17.refs_2_.refs_8_, ...), custom_call_target="tpu_custom_call" | custom-call | flops 830472 | bytes 5367 | tf_op jit(solution)/shard_map/attend_partner/pallas_call | solution.py:77
  42.9 2.9 %collective-permute-start.26 = (bf16[112,768]{1,0:T(8,128)(2,1)S(1)}, bf16[112,768]{1,0:T(8,128)(2,1)S(1)}, u32[]{:S(2)}, u32[]{:S(2)}) collective-permute-start(bf16[112,768]{1,0:T(8,128)(2,1)S(1)} %attend_partner.5.refs_20_), channel_id=1, source_target_pairs={{0,16},{4,20},{8,24},{12,28},{16,0},{20,4},{24,8},{28,12},{1,17},{... | collective-permute-start | bytes 516104 | tf_op jit(solution)/shard_map/ppermute | solution.py:33
  45.8 1.3 %fresh_kv.1 = (bf16[256,256]{1,0:T(8,128)(2,1)S(1)}, bf16[256,256]{1,0:T(8,128)(2,1)S(1)}) custom-call(bf16[80,768]{1,0:T(8,128)(2,1)S(1)} %relay.12.refs_2_.refs_0_, bf16[80,768]{1,0:T(8,128)(2,1)S(1)} %relay.14.refs_1_.refs_0_, bf16[96,768]{1,0:T(8,128)(2,1)S(1)} %relay.16.refs_1_.refs_0_.refs_2_, ...), custom_call_target="tpu_custom_call" | custom-call | flops 402653 | bytes 2758 | tf_op jit(solution)/shard_map/fresh_kv/pallas_call | solution.py:77
  47.1 7.8 %attend_own.1 = (f32[256,768]{1,0:T(8,128)S(1)}, f32[8,256]{1,0:T(8,128)S(1)}, bf16[256,256]{1,0:T(8,128)(2,1)S(1)}, bf16[256,256]{1,0:T(8,128)(2,1)S(1)}) custom-call(bf16[256,768]{1,0:T(8,128)(2,1)S(1)} %copy-done.4, bf16[256,768]{1,0:T(8,128)(2,1)S(1)} %get-tuple-element.56.refs_2_.refs_1_, bf16[256,768]{1,0:T(8,128)(2,1)S(1)} %collective-permute-done.3.refs_2_, ...), custom_call_target="tpu_custom_call" | custom-call | flops 2214592 | bytes 8005 | tf_op jit(solution)/shard_map/attend_own/pallas_call | solution.py:77
  54.9 0.8 %combine.2 = (bf16[160,768]{1,0:T(8,128)(2,1)S(1)}, bf16[160,256]{1,0:T(8,128)(2,1)S(1)}, bf16[160,256]{1,0:T(8,128)(2,1)S(1)}, bf16[160,256]{1,0:T(8,128)(2,1)S(1)}) custom-call(f32[256,768]{1,0:T(8,128)S(1)} %get-tuple-element.64.refs_0_, f32[8,256]{1,0:T(8,128)S(1)} %get-tuple-element.65.refs_1_, bf16[80,768]{1,0:T(8,128)(2,1)S(1)} %relay.19.refs_1_.refs_2_, ...), custom_call_target="tpu_custom_call" | custom-call | flops 188743 | bytes 3137 | tf_op jit(solution)/shard_map/combine/pallas_call | solution.py:77
  55.7 0.1 collective-permute-start.22
  55.8 0.4 collective-permute-start.23
  56.3 0.8 %project.2 = (bf16[160,768]{1,0:T(8,128)(2,1)S(1)}, bf16[160,768]{1,0:T(8,128)(2,1)S(1)}, bf16[160,768]{1,0:T(8,128)(2,1)S(1)}) custom-call(bf16[160,768]{1,0:T(8,128)(2,1)S(1)} %get-tuple-element.66.refs_0_, bf16[768,3072]{1,0:T(8,128)(2,1)S(1)} %bitcast.4), custom_call_target="tpu_custom_call" | custom-call | flops 377487 | bytes 2850 | tf_op jit(solution)/shard_map/project/pallas_call | solution.py:77
  57.1 0.5 collective-permute-start.21
  57.7 0.3 collective-permute-start.25
  58.0 0.6 combine.3
  58.8 0.5 collective-permute-start.29
  59.3 0.7 %project.3 = (bf16[96,768]{1,0:T(8,128)(2,1)S(1)}, bf16[96,768]{1,0:T(8,128)(2,1)S(1)}, bf16[96,768]{1,0:T(8,128)(2,1)S(1)}) custom-call(bf16[96,768]{1,0:T(8,128)(2,1)S(1)} %get-tuple-element.73.refs_0_, bf16[768,3072]{1,0:T(8,128)(2,1)S(1)} %bitcast.4), custom_call_target="tpu_custom_call" | custom-call | flops 226492 | bytes 2654 | tf_op jit(solution)/shard_map/project/pallas_call | solution.py:77
  60.1 0.5 collective-permute-start.27
  60.6 1.8 %collective-permute-start.31 = (bf16[96,768]{1,0:T(8,128)(2,1)S(1)}, bf16[96,768]{1,0:T(8,128)(2,1)S(1)}, u32[]{:S(2)}, u32[]{:S(2)}) collective-permute-start(bf16[96,768]{1,0:T(8,128)(2,1)S(1)} %sum_cores.3.refs_7_), channel_id=1, source_target_pairs={{0,2},{1,3},{2,0},{3,1},{4,6},{5,7},{6,4},{7,5},{8,10},{9,11},{10,... | collective-permute-start | bytes 442376 | tf_op jit(solution)/shard_map/ppermute | solution.py:33
  62.5 2.2 %update_caches.1 = (bf16[2048,256]{1,0:T(8,128)(2,1)}, bf16[2048,256]{1,0:T(8,128)(2,1)}, f32[8,128]{1,0:T(8,128)S(1)}) custom-call(bf16[256,256]{1,0:T(8,128)(2,1)S(1)} %get-tuple-element.80.refs_0_, bf16[256,256]{1,0:T(8,128)(2,1)S(1)} %get-tuple-element.62.refs_14_.refs_16_.refs_1_, bf16[256,256]{1,0:T(8,128)(2,1)S(1)} %get-tuple-element.81.refs_2_, ...), custom_call_target="tpu_custom_call" | custom-call | flops 67108 | bytes 2361 | tf_op jit(solution)/shard_map/update_caches/pallas_call | solution.py:77
  64.7 4.2 %collective-permute-done.31.refs_5_ = bf16[96,768]{1,0:T(8,128)(2,1)S(1)} collective-permute-done((bf16[96,768]{1,0:T(8,128)(2,1)S(1)}, bf16[96,768]{1,0:T(8,128)(2,1)S(1)}, u32[]{:S(2)}, u32[]{:S(2)}) %collective-permute-start.31) | collective-permute-done | bytes 147488 | tf_op jit(solution)/shard_map/ppermute | solution.py:33
  68.9 0.9 %finish.1 = bf16[256,768]{1,0:T(8,128)(2,1)} custom-call(bf16[160,768]{1,0:T(8,128)(2,1)S(1)} %get-tuple-element.67.refs_0_, bf16[160,768]{1,0:T(8,128)(2,1)S(1)} %collective-permute-done.21.refs_1_, bf16[160,768]{1,0:T(8,128)(2,1)S(1)} %collective-permute-done.25.refs_2_, bf16[96,768]{1,0:T(8,128)(2,1)S(1)} %get-tuple-element.74.refs_3_, ...), custom_call_target="tpu_custom_call" | custom-call | bytes 786 | tf_op jit(solution)/shard_map/finish/pallas_call | solution.py:77
  (71 shorter events, 1.1 us)
Async XLA Ops:
  0.6 17.9 %collective-permute-start = (bf16[256,768]{1,0:T(8,128)(2,1)}, bf16[256,768]{1,0:T(8,128)(2,1)S(1)}, u32[]{:S(2)}, u32[]{:S(2)}) collective-permute-start(bf16[256,768]{1,0:T(8,128)(2,1)} %refs_0_.5), channel_id=1, source_target_pairs={{0,2},{1,3},{2,0},{3,1},{4,6},{5,7},{6,4},{7,5},{8,10},{9,11},{10,... | collective-permute-start | bytes 1179656 | tf_op jit(solution)/shard_map/ppermute | solution.py:33
  2.2 16.1 %collective-permute-start.3 = (bf16[256,768]{1,0:T(8,128)(2,1)}, bf16[256,768]{1,0:T(8,128)(2,1)S(1)}, u32[]{:S(2)}, u32[]{:S(2)}) collective-permute-start(bf16[256,768]{1,0:T(8,128)(2,1)} %refs_0_.5), channel_id=1, source_target_pairs={{0,1},{1,0},{2,3},{3,2},{4,5},{5,4},{6,7},{7,6},{8,9},{9,8},{10,11... | collective-permute-start | bytes 1179656 | tf_op jit(solution)/shard_map/ppermute | solution.py:38
  3.2 0.7 copy-start.6
  3.2 0.7 copy-start.7
  3.2 2.2 %copy-start.2 = (bf16[2048,256]{1,0:T(8,128)(2,1)S(1)}, bf16[2048,256]{1,0:T(8,128)(2,1)}, u32[]{:S(2)}) copy-start(bf16[2048,256]{1,0:T(8,128)(2,1)} %refs_4_.3) | copy-start | bytes 3145732
  3.2 2.2 %copy-start.3 = (bf16[2048,256]{1,0:T(8,128)(2,1)S(1)}, bf16[2048,256]{1,0:T(8,128)(2,1)}, u32[]{:S(2)}) copy-start(bf16[2048,256]{1,0:T(8,128)(2,1)} %refs_5_.1) | copy-start | bytes 3145732
  3.3 15.0 %collective-permute-start.2 = (bf16[80,768]{1,0:T(8,128)(2,1)S(1)}, bf16[80,768]{1,0:T(8,128)(2,1)S(1)}, u32[]{:S(2)}, u32[]{:S(2)}) collective-permute-start(bf16[80,768]{1,0:T(8,128)(2,1)S(1)} %get-tuple-element.85), channel_id=1, source_target_pairs={{0,16},{4,20},{8,24},{12,28},{16,0},{20,4},{24,8},{28,12},{1,17},{... | collective-permute-start | bytes 368648 | tf_op jit(solution)/shard_map/ppermute | solution.py:33
  3.7 22.0 %slice-start = ((s8[4718592]{0:T(1024)(128)(4,1)}), s8[4194304]{0:T(1024)(128)(4,1)S(1)}, s32[]{:S(2)}) async-start(s8[4718592]{0:T(1024)(128)(4,1)} %bitcast.1), calls=%async_computation | async-start | bytes 8388608
  3.9 21.7 %slice-start.1 = ((s8[4718592]{0:T(1024)(128)(4,1)}), s8[524288]{0:T(1024)(128)(4,1)S(1)}, s32[]{:S(2)}) async-start(s8[4718592]{0:T(1024)(128)(4,1)} %bitcast.1), calls=%async_computation.1 | async-start | bytes 1048576
  6.3 12.2 %copy-start.4 = (bf16[256,768]{1,0:T(8,128)(2,1)S(1)}, bf16[256,768]{1,0:T(8,128)(2,1)}, u32[]{:S(2)}) copy-start(bf16[256,768]{1,0:T(8,128)(2,1)} %refs_0_.5) | copy-start | bytes 1179652
  6.3 19.4 %copy-start.5 = (f32[3072]{0:T(1024)S(1)}, f32[3072]{0:T(1024)}, u32[]{:S(2)}) copy-start(f32[3072]{0:T(1024)} %param.11) | copy-start | bytes 36868
  6.3 14.6 %collective-permute-start.1 = (bf16[80,768]{1,0:T(8,128)(2,1)S(1)}, bf16[80,768]{1,0:T(8,128)(2,1)S(1)}, u32[]{:S(2)}, u32[]{:S(2)}) collective-permute-start(bf16[80,768]{1,0:T(8,128)(2,1)S(1)} %relay.11.refs_1_), channel_id=1, source_target_pairs={{0,16},{4,20},{8,24},{12,28},{16,0},{20,4},{24,8},{28,12},{1,17},{... | collective-permute-start | bytes 368648 | tf_op jit(solution)/shard_map/ppermute | solution.py:33
  18.3 3.2 %collective-permute-start.7 = (bf16[80,768]{1,0:T(8,128)(2,1)S(1)}, bf16[80,768]{1,0:T(8,128)(2,1)S(1)}, u32[]{:S(2)}, u32[]{:S(2)}) collective-permute-start(bf16[80,768]{1,0:T(8,128)(2,1)S(1)} %relay.12.refs_2_.refs_0_), channel_id=1, source_target_pairs={{0,1},{1,0},{2,3},{3,2},{4,5},{5,4},{6,7},{7,6},{8,9},{9,8},{10,11... | collective-permute-start | bytes 368648 | tf_op jit(solution)/shard_map/ppermute | solution.py:38
  18.4 5.7 %collective-permute-start.6 = (bf16[80,768]{1,0:T(8,128)(2,1)S(1)}, bf16[80,768]{1,0:T(8,128)(2,1)S(1)}, u32[]{:S(2)}, u32[]{:S(2)}) collective-permute-start(bf16[80,768]{1,0:T(8,128)(2,1)S(1)} %relay.12.refs_2_.refs_0_), channel_id=1, source_target_pairs={{0,2},{1,3},{2,0},{3,1},{4,6},{5,7},{6,4},{7,5},{8,10},{9,11},{10,... | collective-permute-start | bytes 368648 | tf_op jit(solution)/shard_map/ppermute | solution.py:33
  18.5 10.0 %collective-permute-start.5 = (bf16[96,768]{1,0:T(8,128)(2,1)S(1)}, bf16[96,768]{1,0:T(8,128)(2,1)S(1)}, u32[]{:S(2)}, u32[]{:S(2)}) collective-permute-start(bf16[96,768]{1,0:T(8,128)(2,1)S(1)} %relay.13.refs_1_), channel_id=1, source_target_pairs={{0,16},{4,20},{8,24},{12,28},{16,0},{20,4},{24,8},{28,12},{1,17},{... | collective-permute-start | bytes 442376 | tf_op jit(solution)/shard_map/ppermute | solution.py:33
  20.9 9.3 %collective-permute-start.10 = (bf16[80,768]{1,0:T(8,128)(2,1)S(1)}, bf16[80,768]{1,0:T(8,128)(2,1)S(1)}, u32[]{:S(2)}, u32[]{:S(2)}) collective-permute-start(bf16[80,768]{1,0:T(8,128)(2,1)S(1)} %relay.14.refs_1_.refs_0_), channel_id=1, source_target_pairs={{0,1},{1,0},{2,3},{3,2},{4,5},{5,4},{6,7},{7,6},{8,9},{9,8},{10,11... | collective-permute-start | bytes 368648 | tf_op jit(solution)/shard_map/ppermute | solution.py:38
  21.0 9.2 %collective-permute-start.4 = (bf16[80,768]{1,0:T(8,128)(2,1)S(1)}, bf16[80,768]{1,0:T(8,128)(2,1)S(1)}, u32[]{:S(2)}, u32[]{:S(2)}) collective-permute-start(bf16[80,768]{1,0:T(8,128)(2,1)S(1)} %relay.14.refs_1_.refs_0_), channel_id=1, source_target_pairs={{0,2},{1,3},{2,0},{3,1},{4,6},{5,7},{6,4},{7,5},{8,10},{9,11},{10,... | collective-permute-start | bytes 368648 | tf_op jit(solution)/shard_map/ppermute | solution.py:33
  24.2 1.3 %collective-permute-start.8 = (bf16[40,768]{1,0:T(8,128)(2,1)S(1)}, bf16[40,768]{1,0:T(8,128)(2,1)S(1)}, u32[]{:S(2)}, u32[]{:S(2)}) collective-permute-start(bf16[40,768]{1,0:T(8,128)(2,1)S(1)} %get-tuple-element.47), channel_id=1, source_target_pairs={{0,1},{1,0},{2,3},{3,2},{4,5},{5,4},{6,7},{7,6},{8,9},{9,8},{10,11... | collective-permute-start | bytes 184328 | tf_op jit(solution)/shard_map/ppermute | solution.py:38
  24.2 1.4 %collective-permute-start.9 = (bf16[40,768]{1,0:T(8,128)(2,1)S(1)}, bf16[40,768]{1,0:T(8,128)(2,1)S(1)}, u32[]{:S(2)}, u32[]{:S(2)}) collective-permute-start(bf16[40,768]{1,0:T(8,128)(2,1)S(1)} %get-tuple-element.48), channel_id=1, source_target_pairs={{0,1},{1,0},{2,3},{3,2},{4,5},{5,4},{6,7},{7,6},{8,9},{9,8},{10,11... | collective-permute-start | bytes 184328 | tf_op jit(solution)/shard_map/ppermute | solution.py:38
  28.5 9.7 %collective-permute-start.16 = (bf16[80,768]{1,0:T(8,128)(2,1)S(1)}, bf16[80,768]{1,0:T(8,128)(2,1)S(1)}, u32[]{:S(2)}, u32[]{:S(2)}) collective-permute-start(bf16[80,768]{1,0:T(8,128)(2,1)S(1)} %get-tuple-element.51.refs_1_), channel_id=1, source_target_pairs={{0,16},{4,20},{8,24},{12,28},{16,0},{20,4},{24,8},{28,12},{1,17},{... | collective-permute-start | bytes 368648 | tf_op jit(solution)/shard_map/ppermute | solution.py:33
  28.6 9.7 %collective-permute-start.17 = (bf16[96,768]{1,0:T(8,128)(2,1)S(1)}, bf16[96,768]{1,0:T(8,128)(2,1)S(1)}, u32[]{:S(2)}, u32[]{:S(2)}) collective-permute-start(bf16[96,768]{1,0:T(8,128)(2,1)S(1)} %relay.16.refs_1_.refs_0_.refs_2_), channel_id=1, source_target_pairs={{0,1},{1,0},{2,3},{3,2},{4,5},{5,4},{6,7},{7,6},{8,9},{9,8},{10,11... | collective-permute-start | bytes 442376 | tf_op jit(solution)/shard_map/ppermute | solution.py:38
  29.0 9.3 %collective-permute-start.15 = (bf16[96,768]{1,0:T(8,128)(2,1)S(1)}, bf16[96,768]{1,0:T(8,128)(2,1)S(1)}, u32[]{:S(2)}, u32[]{:S(2)}) collective-permute-start(bf16[96,768]{1,0:T(8,128)(2,1)S(1)} %relay.16.refs_1_.refs_0_.refs_2_), channel_id=1, source_target_pairs={{0,2},{1,3},{2,0},{3,1},{4,6},{5,7},{6,4},{7,5},{8,10},{9,11},{10,... | collective-permute-start | bytes 442376 | tf_op jit(solution)/shard_map/ppermute | solution.py:33
  30.2 1.3 %collective-permute-start.11 = (bf16[40,768]{1,0:T(8,128)(2,1)S(1)}, bf16[40,768]{1,0:T(8,128)(2,1)S(1)}, u32[]{:S(2)}, u32[]{:S(2)}) collective-permute-start(bf16[40,768]{1,0:T(8,128)(2,1)S(1)} %get-tuple-element.53), channel_id=1, source_target_pairs={{0,1},{1,0},{2,3},{3,2},{4,5},{5,4},{6,7},{7,6},{8,9},{9,8},{10,11... | collective-permute-start | bytes 184328 | tf_op jit(solution)/shard_map/ppermute | solution.py:38
  30.5 1.2 %collective-permute-start.12 = (bf16[40,768]{1,0:T(8,128)(2,1)S(1)}, bf16[40,768]{1,0:T(8,128)(2,1)S(1)}, u32[]{:S(2)}, u32[]{:S(2)}) collective-permute-start(bf16[40,768]{1,0:T(8,128)(2,1)S(1)} %get-tuple-element.54), channel_id=1, source_target_pairs={{0,1},{1,0},{2,3},{3,2},{4,5},{5,4},{6,7},{7,6},{8,9},{9,8},{10,11... | collective-permute-start | bytes 184328 | tf_op jit(solution)/shard_map/ppermute | solution.py:38
  34.6 12.4 %collective-permute-start.13 = (bf16[128,768]{1,0:T(8,128)(2,1)S(1)}, bf16[128,768]{1,0:T(8,128)(2,1)S(1)}, u32[]{:S(2)}, u32[]{:S(2)}) collective-permute-start(bf16[128,768]{1,0:T(8,128)(2,1)S(1)} %get-tuple-element.57), channel_id=1, source_target_pairs={{0,1},{1,0},{2,3},{3,2},{4,5},{5,4},{6,7},{7,6},{8,9},{9,8},{10,11... | collective-permute-start | bytes 589832 | tf_op jit(solution)/shard_map/ppermute | solution.py:38
  35.1 12.0 %collective-permute-start.14 = (bf16[128,768]{1,0:T(8,128)(2,1)S(1)}, bf16[128,768]{1,0:T(8,128)(2,1)S(1)}, u32[]{:S(2)}, u32[]{:S(2)}) collective-permute-start(bf16[128,768]{1,0:T(8,128)(2,1)S(1)} %get-tuple-element.58), channel_id=1, source_target_pairs={{0,1},{1,0},{2,3},{3,2},{4,5},{5,4},{6,7},{7,6},{8,9},{9,8},{10,11... | collective-permute-start | bytes 589832 | tf_op jit(solution)/shard_map/ppermute | solution.py:38
  38.2 16.7 %collective-permute-start.20 = (bf16[96,768]{1,0:T(8,128)(2,1)S(1)}, bf16[96,768]{1,0:T(8,128)(2,1)S(1)}, u32[]{:S(2)}, u32[]{:S(2)}) collective-permute-start(bf16[96,768]{1,0:T(8,128)(2,1)S(1)} %relay.20.refs_1_), channel_id=1, source_target_pairs={{0,16},{4,20},{8,24},{12,28},{16,0},{20,4},{24,8},{28,12},{1,17},{... | collective-permute-start | bytes 442376 | tf_op jit(solution)/shard_map/ppermute | solution.py:33
  38.3 1.3 %collective-permute-start.18 = (bf16[48,768]{1,0:T(8,128)(2,1)S(1)}, bf16[48,768]{1,0:T(8,128)(2,1)S(1)}, u32[]{:S(2)}, u32[]{:S(2)}) collective-permute-start(bf16[48,768]{1,0:T(8,128)(2,1)S(1)} %get-tuple-element.60), channel_id=1, source_target_pairs={{0,1},{1,0},{2,3},{3,2},{4,5},{5,4},{6,7},{7,6},{8,9},{9,8},{10,11... | collective-permute-start | bytes 221192 | tf_op jit(solution)/shard_map/ppermute | solution.py:38
  38.4 1.4 %collective-permute-start.19 = (bf16[48,768]{1,0:T(8,128)(2,1)S(1)}, bf16[48,768]{1,0:T(8,128)(2,1)S(1)}, u32[]{:S(2)}, u32[]{:S(2)}) collective-permute-start(bf16[48,768]{1,0:T(8,128)(2,1)S(1)} %get-tuple-element.61), channel_id=1, source_target_pairs={{0,1},{1,0},{2,3},{3,2},{4,5},{5,4},{6,7},{7,6},{8,9},{9,8},{10,11... | collective-permute-start | bytes 221192 | tf_op jit(solution)/shard_map/ppermute | solution.py:38
  39.8 6.0 %copy-start = (bf16[3072,256]{1,0:T(8,128)(2,1)S(1)}, bf16[3072,256]{1,0:T(8,128)(2,1)}, u32[]{:S(2)}) copy-start(bf16[3072,256]{1,0:T(8,128)(2,1)} %refs_7_.1) | copy-start | bytes 4718596
  39.8 6.0 %copy-start.1 = (bf16[3072,256]{1,0:T(8,128)(2,1)S(1)}, bf16[3072,256]{1,0:T(8,128)(2,1)}, u32[]{:S(2)}) copy-start(bf16[3072,256]{1,0:T(8,128)(2,1)} %refs_8_.1) | copy-start | bytes 4718596
  42.9 15.2 %collective-permute-start.26 = (bf16[112,768]{1,0:T(8,128)(2,1)S(1)}, bf16[112,768]{1,0:T(8,128)(2,1)S(1)}, u32[]{:S(2)}, u32[]{:S(2)}) collective-permute-start(bf16[112,768]{1,0:T(8,128)(2,1)S(1)} %attend_partner.5.refs_20_), channel_id=1, source_target_pairs={{0,16},{4,20},{8,24},{12,28},{16,0},{20,4},{24,8},{28,12},{1,17},{... | collective-permute-start | bytes 516104 | tf_op jit(solution)/shard_map/ppermute | solution.py:33
  47.1 7.8 %slice-start.2 = ((s8[4718592]{0:T(1024)(128)(4,1)}), s8[4194304]{0:T(1024)(128)(4,1)S(1)}, s32[]{:S(2)}) async-start(s8[4718592]{0:T(1024)(128)(4,1)} %bitcast.3), calls=%async_computation.2 | async-start | bytes 8388608
  47.1 7.8 %slice-start.3 = ((s8[4718592]{0:T(1024)(128)(4,1)}), s8[524288]{0:T(1024)(128)(4,1)S(1)}, s32[]{:S(2)}) async-start(s8[4718592]{0:T(1024)(128)(4,1)} %bitcast.3), calls=%async_computation.3 | async-start | bytes 1048576
  55.7 1.9 %collective-permute-start.22 = (bf16[160,256]{1,0:T(8,128)(2,1)S(1)}, bf16[160,256]{1,0:T(8,128)(2,1)S(1)}, u32[]{:S(2)}, u32[]{:S(2)}) collective-permute-start(bf16[160,256]{1,0:T(8,128)(2,1)S(1)} %get-tuple-element.70), channel_id=1, source_target_pairs={{0,1},{1,0},{2,3},{3,2},{4,5},{5,4},{6,7},{7,6},{8,9},{9,8},{10,11... | collective-permute-start | bytes 245768 | tf_op jit(solution)/shard_map/ppermute | solution.py:38
  55.8 1.8 %collective-permute-start.23 = (bf16[160,256]{1,0:T(8,128)(2,1)S(1)}, bf16[160,256]{1,0:T(8,128)(2,1)S(1)}, u32[]{:S(2)}, u32[]{:S(2)}) collective-permute-start(bf16[160,256]{1,0:T(8,128)(2,1)S(1)} %get-tuple-element.71), channel_id=1, source_target_pairs={{0,1},{1,0},{2,3},{3,2},{4,5},{5,4},{6,7},{7,6},{8,9},{9,8},{10,11... | collective-permute-start | bytes 245768 | tf_op jit(solution)/shard_map/ppermute | solution.py:38
  56.2 1.4 %collective-permute-start.24 = (bf16[160,256]{1,0:T(8,128)(2,1)S(1)}, bf16[160,256]{1,0:T(8,128)(2,1)S(1)}, u32[]{:S(2)}, u32[]{:S(2)}) collective-permute-start(bf16[160,256]{1,0:T(8,128)(2,1)S(1)} %get-tuple-element.72), channel_id=1, source_target_pairs={{0,1},{1,0},{2,3},{3,2},{4,5},{5,4},{6,7},{7,6},{8,9},{9,8},{10,11... | collective-permute-start | bytes 245768 | tf_op jit(solution)/shard_map/ppermute | solution.py:38
  57.1 7.5 %collective-permute-start.21 = (bf16[160,768]{1,0:T(8,128)(2,1)S(1)}, bf16[160,768]{1,0:T(8,128)(2,1)S(1)}, u32[]{:S(2)}, u32[]{:S(2)}) collective-permute-start(bf16[160,768]{1,0:T(8,128)(2,1)S(1)} %get-tuple-element.68.refs_4_), channel_id=1, source_target_pairs={{0,1},{1,0},{2,3},{3,2},{4,5},{5,4},{6,7},{7,6},{8,9},{9,8},{10,11... | collective-permute-start | bytes 737288 | tf_op jit(solution)/shard_map/ppermute | solution.py:38
  57.7 11.2 %collective-permute-start.25 = (bf16[160,768]{1,0:T(8,128)(2,1)S(1)}, bf16[160,768]{1,0:T(8,128)(2,1)S(1)}, u32[]{:S(2)}, u32[]{:S(2)}) collective-permute-start(bf16[160,768]{1,0:T(8,128)(2,1)S(1)} %sum_cores.2.refs_4_), channel_id=1, source_target_pairs={{0,2},{1,3},{2,0},{3,1},{4,6},{5,7},{6,4},{7,5},{8,10},{9,11},{10,... | collective-permute-start | bytes 737288 | tf_op jit(solution)/shard_map/ppermute | solution.py:33
  58.7 1.4 %collective-permute-start.28 = (bf16[96,256]{1,0:T(8,128)(2,1)S(1)}, bf16[96,256]{1,0:T(8,128)(2,1)S(1)}, u32[]{:S(2)}, u32[]{:S(2)}) collective-permute-start(bf16[96,256]{1,0:T(8,128)(2,1)S(1)} %get-tuple-element.77), channel_id=1, source_target_pairs={{0,1},{1,0},{2,3},{3,2},{4,5},{5,4},{6,7},{7,6},{8,9},{9,8},{10,11... | collective-permute-start | bytes 147464 | tf_op jit(solution)/shard_map/ppermute | solution.py:38
  58.8 1.8 %collective-permute-start.29 = (bf16[96,256]{1,0:T(8,128)(2,1)S(1)}, bf16[96,256]{1,0:T(8,128)(2,1)S(1)}, u32[]{:S(2)}, u32[]{:S(2)}) collective-permute-start(bf16[96,256]{1,0:T(8,128)(2,1)S(1)} %get-tuple-element.78), channel_id=1, source_target_pairs={{0,1},{1,0},{2,3},{3,2},{4,5},{5,4},{6,7},{7,6},{8,9},{9,8},{10,11... | collective-permute-start | bytes 147464 | tf_op jit(solution)/shard_map/ppermute | solution.py:38
  59.3 1.3 %collective-permute-start.30 = (bf16[96,256]{1,0:T(8,128)(2,1)S(1)}, bf16[96,256]{1,0:T(8,128)(2,1)S(1)}, u32[]{:S(2)}, u32[]{:S(2)}) collective-permute-start(bf16[96,256]{1,0:T(8,128)(2,1)S(1)} %get-tuple-element.79), channel_id=1, source_target_pairs={{0,1},{1,0},{2,3},{3,2},{4,5},{5,4},{6,7},{7,6},{8,9},{9,8},{10,11... | collective-permute-start | bytes 147464 | tf_op jit(solution)/shard_map/ppermute | solution.py:38
  60.1 4.6 %collective-permute-start.27 = (bf16[96,768]{1,0:T(8,128)(2,1)S(1)}, bf16[96,768]{1,0:T(8,128)(2,1)S(1)}, u32[]{:S(2)}, u32[]{:S(2)}) collective-permute-start(bf16[96,768]{1,0:T(8,128)(2,1)S(1)} %get-tuple-element.75.refs_4_), channel_id=1, source_target_pairs={{0,1},{1,0},{2,3},{3,2},{4,5},{5,4},{6,7},{7,6},{8,9},{9,8},{10,11... | collective-permute-start | bytes 442376 | tf_op jit(solution)/shard_map/ppermute | solution.py:38
  60.6 8.2 %collective-permute-start.31 = (bf16[96,768]{1,0:T(8,128)(2,1)S(1)}, bf16[96,768]{1,0:T(8,128)(2,1)S(1)}, u32[]{:S(2)}, u32[]{:S(2)}) collective-permute-start(bf16[96,768]{1,0:T(8,128)(2,1)S(1)} %sum_cores.3.refs_7_), channel_id=1, source_target_pairs={{0,2},{1,3},{2,0},{3,1},{4,6},{5,7},{6,4},{7,5},{8,10},{9,11},{10,... | collective-permute-start | bytes 442376 | tf_op jit(solution)/shard_map/ppermute | solution.py:33

commit v8 on v7

v8 whole, which is shorter than its diff:
```python
import functools
import math

import jax
import jax.numpy as jnp
from jax import lax
from jax.experimental import pallas as pl
from jax.experimental.pallas import tpu as pltpu
from jax.sharding import PartitionSpec as P

HD = 128
LANES = 128
STAT_ROWS = 8
ROW_TILE = 16
CORES = 2
CHUNK_UNITS = (7, 9)
PIECES = 2
COST_WEIGHT = 0.0005
FIRST_MICROS = 2
FLOPS_PER_MICRO = 1_000_000_000
MIB = 1 << 20

rope_base = 500000.0
neg_large = -1e30
log2_scale = math.log2(math.e) / math.sqrt(HD)

VMEM = pl.BlockSpec(memory_space=pltpu.VMEM)
ANY = pl.BlockSpec(memory_space=pl.ANY)


def shifted(shard, axis, by):
    devices = lax.axis_size(axis)
    return lax.ppermute(shard, axis, [(i, (i + by) % devices) for i in range(devices)])


def other_core(shard):
    devices = lax.axis_size("head")
    return lax.ppermute(shard, "head", [(i, i ^ 1) for i in range(devices)])


def other_chips(own):
    chips = lax.axis_size("head") // CORES
    return [shifted(own, "head", CORES * k) for k in range(1, chips)]


def place_of(requests):
    member = lax.axis_index("seq")
    return lax.rem(member, requests), lax.div(member, requests)


def source_of(position_in, turn, groups):
    return lax.rem(position_in + (groups - turn), groups)


def dot(left, right):
    return jnp.dot(left, right, preferred_element_type=jnp.float32)


def dot_transposed(left, right):
    return lax.dot_general(
        left, right, (((1,), (1,)), ((), ())), preferred_element_type=jnp.float32
    )


def call(
    kernel, out_shape, arrays, limit, flops, transcendentals, name, earlier=(),
    scratch=(), micros=0,
):
    moved = sum(a.size * a.dtype.itemsize for a in arrays)
    moved += sum(math.prod(s.shape) * s.dtype.itemsize for s in out_shape)
    read = len(arrays)
    skipped = len(earlier)

    def body(*refs):
        kernel(*refs[:read], *refs[read + skipped :])

    return pl.pallas_call(
        body,
        out_shape=out_shape,
        in_specs=[VMEM] * len(arrays) + [ANY] * skipped,
        out_specs=[VMEM] * len(out_shape),
        scratch_shapes=scratch,
        compiler_params=pltpu.CompilerParams(vmem_limit_bytes=limit * MIB),
        cost_estimate=pl.CostEstimate(
            flops=max(int(COST_WEIGHT * flops), int(micros * FLOPS_PER_MICRO)),
            bytes_accessed=int(COST_WEIGHT * moved),
            transcendentals=int(COST_WEIGHT * transcendentals),
        ),
        name=name,
    )(*arrays, *earlier)


def whole_of(blocks):
    parts = [block[...] for block in blocks]
    return jnp.concatenate(parts, 0) if len(parts) > 1 else parts[0]


def relay_kernel(count, *refs):
    whole = whole_of(refs[:count])
    at = 0
    for ref in refs[count:]:
        ref[...] = whole[at : at + ref.shape[0]]
        at = (at + ref.shape[0]) % whole.shape[0]


def relay(blocks, sizes, earlier):
    shapes = [jax.ShapeDtypeStruct((size, *blocks[0].shape[1:]), blocks[0].dtype) for size in sizes]
    kernel = functools.partial(relay_kernel, len(blocks))
    return call(kernel, shapes, [*blocks], 4, 0, 0, "relay", earlier)


def mark_kernel(mark):
    lane = lax.broadcasted_iota(jnp.int32, mark.shape, 1)
    mark[...] = jnp.where(lane == 0, 1.0, 0.0).astype(mark.dtype)


def marks(rows):
    shape = jax.ShapeDtypeStruct((rows, LANES), jnp.bfloat16)
    return call(mark_kernel, [shape], [], 4, 0, 0, "marks", micros=FIRST_MICROS)[0]


def tables_kernel(groups, lengths_in, offsets_in, cosine, sine, *scratch):
    lengths, offsets, semaphores = scratch
    numbers = [
        pltpu.make_async_copy(lengths_in, lengths, semaphores.at[0]),
        pltpu.make_async_copy(offsets_in, offsets, semaphores.at[1]),
    ]
    for copy in numbers:
        copy.start()
    rows = cosine.shape[0] // groups
    for copy in numbers:
        copy.wait()
    request, position_in = place_of(lengths.shape[0])
    lane = lax.broadcasted_iota(jnp.int32, (rows, LANES), 1)
    row = lax.broadcasted_iota(jnp.int32, (rows, LANES), 0)
    half = lax.rem(lane, HD // 2).astype(jnp.float32)
    frequency = jnp.exp2(half * (-2.0 / HD * math.log2(rope_base)))
    sign = jnp.where(lane < HD // 2, -1.0, 1.0)
    for turn in range(groups):
        first = source_of(position_in, turn, groups) * rows
        first = first + offsets[request] + lengths[request]
        angles = (row + first).astype(jnp.float32) * frequency
        part = slice(turn * rows, (turn + 1) * rows)
        cosine[part] = jnp.cos(angles)
        sine[part] = jnp.sin(angles) * sign


def rope_tables(lengths, offsets, groups, rows, earlier):
    table = jax.ShapeDtypeStruct((groups * rows, LANES), jnp.float32)
    return call(
        functools.partial(tables_kernel, groups),
        [table, table],
        [lengths, offsets],
        12,
        0,
        0,
        "rope_tables",
        earlier,
        [
            pltpu.SMEM(lengths.shape, lengths.dtype),
            pltpu.SMEM(offsets.shape, offsets.dtype),
            pltpu.SemaphoreType.DMA((2,)),
        ],
    )


def widen_kernel(keys, values, mark, lengths_in, wide_keys, wide_values, lengths, semaphore):
    number = pltpu.make_async_copy(lengths_in, lengths, semaphore)
    number.start()
    slots = keys.shape[0]
    heads = keys.shape[1] // HD
    for head in range(heads):
        own = slice(head * HD, (head + 1) * HD)
        wide_keys[head, :, :HD] = keys[:, own]
        wide_values[head, :, :HD] = values[:, own]
        wide_values[head, :, HD:] = mark[:slots]
    number.wait()
    request, position_in = place_of(lengths.shape[0])
    slot = lax.broadcasted_iota(jnp.int32, (slots, LANES), 0) + position_in * slots
    lane = lax.broadcasted_iota(jnp.int32, (slots, LANES), 1)
    bias = jnp.where((lane == 0) & (slot >= lengths[request]), neg_large, 0.0).astype(jnp.bfloat16)
    for head in range(heads):
        wide_keys[head, :, HD:] = bias


def widen(keys, values, mark, lengths, earlier):
    slots, width = keys.shape
    wide = jax.ShapeDtypeStruct((width // HD, slots, HD + LANES), jnp.bfloat16)
    return call(
        widen_kernel,
        [wide, wide],
        [keys, values, mark, lengths],
        12,
        0,
        0,
        "widen_caches",
        earlier,
        [pltpu.SMEM(lengths.shape, lengths.dtype), pltpu.SemaphoreType.DMA],
    )


def rotate(vectors, cosine, sine):
    return vectors * cosine + pltpu.roll(vectors, HD // 2, 1) * sine


def project_normed(pieces, gain, weights):
    heads = gain.shape[0]
    width = gain.shape[2]
    me = lax.axis_index("head")
    squares = 0.0
    sums = [0.0] * len(weights)
    for index, piece in enumerate(pieces):
        owner = lax.rem(me + (heads - CORES * (index % (heads // CORES))), heads)
        if index >= heads // CORES:
            owner = owner ^ 1
        wide = piece.astype(jnp.float32)
        scaled = (wide * gain[owner]).astype(jnp.bfloat16)
        along = pl.ds(pl.multiple_of(owner * width, LANES), width)
        for place, weight in enumerate(weights):
            sums[place] = sums[place] + dot(scaled, weight[along, :])
        squares = squares + jnp.sum(wide * wide, -1, keepdims=True)
    factor = lax.rsqrt(squares / (heads * width) + 1e-05)
    return [total * factor for total in sums]


def stat_rows(columns, rows):
    padded = -(-rows // LANES) * LANES
    lane = lax.broadcasted_iota(jnp.int32, (padded, LANES), 1)
    table = jnp.zeros((padded, LANES), jnp.float32)
    for index, column in enumerate(columns):
        if padded > rows:
            filler = jnp.zeros((padded - rows, 1), jnp.float32)
            column = jnp.concatenate([column, filler], 0)
        table = jnp.where(lane == index, column, table)
    return table.T[:STAT_ROWS]


def stat_columns(stats):
    padding = jnp.zeros((LANES - STAT_ROWS, stats.shape[1]), jnp.float32)
    return jnp.concatenate([stats, padding], 0).T


def stat_places(rows, width):
    lanes = -(-rows // LANES) * LANES
    in_row = width // lanes
    return [(part // in_row * ROW_TILE, part % in_row * lanes) for part in range(3)], lanes


def tail_rows(rows, width):
    return stat_places(rows, width)[0][-1][0] + ROW_TILE


def split_refs(counts, refs):
    parts = []
    for count in counts:
        parts.append(refs[:count])
        refs = refs[count:]
    return parts, refs


def head_queries(product, cosine, sine):
    return [
        (rotate(product[:, at : at + HD], cosine, sine) * log2_scale).astype(jnp.bfloat16)
        for at in range(0, product.shape[1], HD)
    ]


def stack_heads(queries, head, repeat, at, rows):
    own = queries[head * repeat : (head + 1) * repeat]
    return jnp.concatenate([query[at : at + rows] for query in own], 0)


def weigh(scores, values):
    largest = functools.reduce(
        jnp.maximum, [jnp.max(score, -1, keepdims=True) for score in scores]
    )
    summed = 0.0
    for score, value in zip(scores, values):
        weights = jnp.exp2(score - largest).astype(jnp.bfloat16)
        summed = summed + dot(weights, value)
    denominator = summed[:, HD : HD + 1]
    return summed[:, :HD] / denominator, largest + jnp.log2(denominator)


def project_kernel(counts, table_at, *refs):
    *blocks, weights = split_refs([*counts, 6], refs)[0]
    queries, keys, values = refs[sum(counts) + 6 :]
    gain, w_query, w_key, w_value, cosine, sine = weights
    part = slice(table_at, table_at + queries.shape[0])
    pieces = [
        one[0][part] if one[0].shape[0] > queries.shape[0] else whole_of(one) for one in blocks
    ]
    query_sum, key_sum, value_sum = project_normed(pieces, gain, [w_query, w_key, w_value])
    cosine, sine = cosine[part], sine[part]
    queries[...] = jnp.concatenate(head_queries(query_sum, cosine, sine), 1)
    for at in range(0, keys.shape[1], HD):
        own = slice(at, at + HD)
        keys[:, own] = rotate(key_sum[:, own], cosine, sine).astype(jnp.bfloat16)
    values[...] = value_sum.astype(jnp.bfloat16)


def project_rows(pieces, gain, weights, tables, table_at, rows, earlier):
    flat = [block for blocks in pieces for block in blocks]
    return call(
        functools.partial(project_kernel, [len(blocks) for blocks in pieces], table_at),
        [jax.ShapeDtypeStruct((rows, weight.shape[1]), jnp.bfloat16) for weight in weights],
        [*flat, gain, *weights, *tables],
        24,
        2 * rows * sum(weight.size for weight in weights),
        0,
        "project_qkv",
        earlier,
    )


def attend_heads(queries, wide_keys, wide_values, mark, fresh, store):
    rows = queries.shape[0]
    kv_heads = wide_keys.shape[0]
    repeat = queries.shape[1] // HD // kv_heads
    marked = mark[: repeat * rows]
    scores = []
    values = []
    for head in range(kv_heads):
        shared = slice(head * HD, (head + 1) * HD)
        stacked = jnp.concatenate(
            [
                queries[:, (head * repeat + turn) * HD : (head * repeat + turn + 1) * HD]
                for turn in range(repeat)
            ],
            0,
        )
        wide = jnp.concatenate([stacked, marked], 1)
        found = [dot_transposed(wide, wide_keys[head])]
        held = [wide_values[head]]
        for keys, new_values, column, bias in fresh:
            if bias is None:
                added = jnp.concatenate([keys[:, shared], column], 1)
                found.append(dot_transposed(wide, added))
            else:
                bias = jnp.concatenate([bias] * repeat, 0)
                found.append(dot_transposed(stacked, keys[:, shared]) + bias)
            held.append(jnp.concatenate([new_values[:, shared], mark[: keys.shape[0]]], 1))
        scores.append(found)
        values.append(held)
    columns = []
    for head in range(kv_heads):
        result, logs = weigh(scores[head], values[head])
        for turn in range(repeat):
            part = slice(turn * rows, (turn + 1) * rows)
            store((head * repeat + turn) * HD, result[part])
            columns.append(logs[part])
    return stat_rows(columns, rows)


def attend_kernel(requests, groups, turn, blocks, queries, wide_keys, wide_values, mark, *refs):
    (new_keys, new_values), (packed,) = split_refs([blocks, blocks], refs)
    rows = queries.shape[0]
    position_in = place_of(requests)[1]
    hidden = position_in > source_of(position_in, turn, groups)
    fresh = []
    for keys, values in zip(new_keys, new_values):
        bias = mark[: keys.shape[0]].astype(jnp.float32) * neg_large
        fresh.append((keys, values, jnp.where(hidden, bias, 0.0).astype(jnp.bfloat16), None))

    def store(at, result):
        packed[:rows, at : at + HD] = result.astype(packed.dtype)

    rest = attend_heads(queries[...], wide_keys, wide_values, mark, fresh, store)
    width = packed.shape[1]
    packed[rows:] = jnp.zeros((packed.shape[0] - rows, width), packed.dtype)
    rest = jnp.concatenate([rest, jnp.zeros((ROW_TILE - STAT_ROWS, rest.shape[1]), jnp.float32)], 0)
    places, lanes = stat_places(rows, width)
    for row, lane in places:
        rounded = rest.astype(packed.dtype)
        packed[rows + row : rows + row + ROW_TILE, lane : lane + lanes] = rounded
        rest = rest - rounded.astype(jnp.float32)


def attend(requests, groups, turn, queries, wides, mark, new_rows, earlier):
    rows, width = queries.shape
    slots = wides[0].shape[1]
    new_keys, new_values = zip(*new_rows)
    shape = jax.ShapeDtypeStruct((rows + tail_rows(rows, width), width), jnp.bfloat16)
    return call(
        functools.partial(attend_kernel, requests, groups, turn, len(new_rows)),
        [shape],
        [queries, *wides, mark, *new_keys, *new_values],
        28,
        8 * rows * width * slots,
        rows * width // HD * slots,
        "attend_partner",
        earlier,
    )[0]


def attend_own_kernel(blocks, queries, wide_keys, wide_values, mark, *refs):
    (new_keys, new_values), (partial, stats) = split_refs([blocks, blocks], refs)
    rows = queries.shape[0]
    fresh = [
        (keys, values, jnp.zeros((keys.shape[0], LANES), jnp.bfloat16), None)
        for keys, values in zip(new_keys[:-1], new_values[:-1])
    ]
    token = lax.broadcasted_iota(jnp.int32, (rows, rows), 0)
    within = lax.broadcasted_iota(jnp.int32, (rows, rows), 1)
    causal = jnp.where(within <= token, 0.0, neg_large)
    fresh.append((new_keys[-1], new_values[-1], None, causal))

    def store(at, result):
        partial[:, at : at + HD] = result

    stats[...] = attend_heads(queries[...], wide_keys, wide_values, mark, fresh, store)


def attend_own(queries, wides, mark, new_rows, earlier):
    rows, width = queries.shape
    slots = wides[0].shape[1]
    new_keys, new_values = zip(*new_rows)
    return call(
        functools.partial(attend_own_kernel, len(new_rows)),
        [
            jax.ShapeDtypeStruct((rows, width), jnp.float32),
            jax.ShapeDtypeStruct((STAT_ROWS, -(-rows // LANES) * LANES), jnp.float32),
        ],
        [queries, *wides, mark, *new_keys, *new_values],
        28,
        8 * rows * width * slots,
        rows * width // HD * slots,
        "attend_own",
        earlier,
    )


def write_rows(target, fresh_rows, first):
    rows = fresh_rows.shape[0]
    slab_rows = target.shape[0]
    span = rows + ROW_TILE
    start = jnp.clip(first, 0, slab_rows - span)
    start = start - lax.rem(start, ROW_TILE)
    window = pl.ds(pl.multiple_of(start, ROW_TILE), span)
    shift = start - first
    place = lax.broadcasted_iota(jnp.int32, (span, rows), 0) + shift
    chosen = place == lax.broadcasted_iota(jnp.int32, (span, rows), 1)
    moved = dot(chosen.astype(jnp.bfloat16), fresh_rows)
    row = lax.broadcasted_iota(jnp.int32, (span, target.shape[1]), 0) + shift
    inside = (row >= 0) & (row < rows)
    old = target[window, :].astype(jnp.float32)
    target[window, :] = jnp.where(inside, moved, old).astype(jnp.bfloat16)


def update_kernel(groups, chunks, *refs):
    (new_keys, new_values, pairs), refs = split_refs([chunks, chunks, groups - 1], refs)
    keys, values, lengths_in, keys_updated, values_updated, done, lengths, semaphore = refs
    number = pltpu.make_async_copy(lengths_in, lengths, semaphore)
    number.start()
    keys_updated[...] = keys[...]
    values_updated[...] = values[...]
    done[...] = jnp.zeros(done.shape, done.dtype)
    number.wait()
    request, position_in = place_of(lengths.shape[0])
    rows = sum(ref.shape[0] for ref in new_keys)
    width = keys.shape[1]
    for turn in range(groups):
        source = source_of(position_in, turn, groups)
        first = lengths[request] + source * rows - position_in * keys.shape[0]
        if turn:
            write_rows(keys_updated, pairs[turn - 1][:, :width], first)
            write_rows(values_updated, pairs[turn - 1][:, width:], first)
        else:
            write_rows(keys_updated, whole_of(new_keys), first)
            write_rows(values_updated, whole_of(new_values), first)


def update(lengths, new_rows, pairs, keys, values, earlier):
    new_keys, new_values = zip(*new_rows)
    slab = jax.ShapeDtypeStruct(keys.shape, keys.dtype)
    return call(
        functools.partial(update_kernel, len(pairs) + 1, len(new_rows)),
        [slab, slab, jax.ShapeDtypeStruct((STAT_ROWS, LANES), jnp.float32)],
        [*new_keys, *new_values, *pairs, keys, values, lengths],
        20,
        0,
        0,
        "update_caches",
        earlier,
        [pltpu.SMEM(lengths.shape, lengths.dtype), pltpu.SemaphoreType.DMA],
    )


def pair_kernel(chunks, *refs):
    (new_keys, new_values), (pair,) = split_refs([chunks, chunks], refs)
    pair[...] = jnp.concatenate([whole_of(new_keys), whole_of(new_values)], 1)


def pair_rows(new_rows, earlier):
    new_keys, new_values = zip(*new_rows)
    rows = sum(keys.shape[0] for keys in new_keys)
    shape = jax.ShapeDtypeStruct((rows, 2 * new_keys[0].shape[1]), new_keys[0].dtype)
    kernel = functools.partial(pair_kernel, len(new_rows))
    return call(kernel, [shape], [*new_keys, *new_values], 8, 0, 0, "pair_rows", earlier)[0]


def combine_kernel(own_partial, own_stats, *refs):
    heads = lax.axis_size("head")
    chips = heads // CORES
    outputs = PIECES * (chips - 1)
    received = refs[: -2 - outputs]
    w_out, merged_rows, *far = refs[-2 - outputs :]
    rows, width = own_partial.shape
    logs = [stat_columns(own_stats[...])[:rows]]
    partials = [own_partial[...]]
    for packed in received:
        places, lanes = stat_places(rows, width)
        stats = sum(
            packed[rows + row : rows + row + ROW_TILE, lane : lane + lanes].astype(jnp.float32)
            for row, lane in places
        )
        logs.append(stat_columns(stats[:STAT_ROWS])[:rows])
        partials.append(packed[:rows])
    largest = functools.reduce(jnp.maximum, logs)
    shares = [jnp.exp2(log - largest) for log in logs]
    total = functools.reduce(jnp.add, shares)
    shares = [share / total for share in shares]
    attended = []
    for head in range(width // HD):
        at = slice(head * HD, (head + 1) * HD)
        column = slice(head, head + 1)
        merged = 0.0
        for partial, share in zip(partials, shares):
            merged = merged + partial[:, at].astype(jnp.float32) * share[:, column]
        attended.append(merged.astype(jnp.bfloat16))
    attended = jnp.concatenate(attended, 1)
    merged_rows[...] = attended
    for ahead in range(1, chips):
        store_pieces(block_product(attended, w_out, ahead, 1), far[PIECES * (ahead - 1) :][:PIECES])


def store_pieces(block, targets):
    width = targets[0].shape[1]
    for index, target in enumerate(targets):
        target[...] = block[:, index * width : (index + 1) * width]


def block_product(attended, w_out, ahead, flip):
    heads = lax.axis_size("head")
    block_width = w_out.shape[1] // heads
    block = lax.rem(lax.axis_index("head") + CORES * ahead, heads) ^ flip
    along = pl.ds(pl.multiple_of(block * block_width, LANES), block_width)
    return dot(attended, w_out[:, along]).astype(jnp.bfloat16)


def near_kernel(merged_rows, w_out, *refs):
    far, near = refs[:PIECES], refs[PIECES:]
    attended = merged_rows[...]
    store_pieces(block_product(attended, w_out, 0, 1), far)
    for ahead, target in enumerate(near):
        target[...] = block_product(attended, w_out, ahead, 0)


def combine(own, received, w_out, heads, earlier):
    chips = heads // CORES
    rows = own[0].shape[0]
    width = w_out.shape[1] // heads
    merged = jax.ShapeDtypeStruct(own[0].shape, jnp.bfloat16)
    piece = jax.ShapeDtypeStruct((rows, width // PIECES), jnp.bfloat16)
    merged, *far = call(
        combine_kernel,
        [merged] + [piece] * (PIECES * (chips - 1)),
        [*own, *received, w_out],
        20,
        rows * w_out.size,
        0,
        "combine",
        earlier,
    )
    return merged, [far[k * PIECES : (k + 1) * PIECES] for k in range(chips - 1)]


def project_near(merged, w_out, heads):
    rows = merged.shape[0]
    width = w_out.shape[1] // heads
    block = jax.ShapeDtypeStruct((rows, width), jnp.bfloat16)
    piece = jax.ShapeDtypeStruct((rows, width // PIECES), jnp.bfloat16)
    outputs = call(
        near_kernel,
        [piece] * PIECES + [block] * (heads // CORES),
        [merged, w_out],
        20,
        2 * rows * w_out.size,
        0,
        "project_near",
    )
    return outputs[:PIECES], outputs[PIECES:]


def sum_kernel(count, near, *refs):
    far, pieces = refs[:count], refs[count:]
    total = jnp.concatenate([ref[...] for ref in far], 1).astype(jnp.float32)
    store_pieces((near[...].astype(jnp.float32) + total).astype(jnp.bfloat16), pieces)


def sum_cores(near, far, pieces, earlier):
    rows, width = near.shape
    shape = jax.ShapeDtypeStruct((rows, width // pieces), near.dtype)
    kernel = functools.partial(sum_kernel, len(far))
    return call(kernel, [shape] * pieces, [near, *far], 8, near.size, 0, "sum_cores", earlier)


def finish_kernel(counts, *refs):
    flat = [count for chunk in counts for count in chunk]
    blocks, (result,) = split_refs(flat, refs)
    at = 0
    for chunk in counts:
        total = 0.0
        for pieces in blocks[: len(chunk)]:
            whole = jnp.concatenate([ref[...] for ref in pieces], 1)
            total = total + whole.astype(jnp.float32)
        blocks = blocks[len(chunk) :]
        result[at : at + total.shape[0]] = total.astype(result.dtype)
        at += total.shape[0]


def finish(chunks, earlier):
    flat = [piece for chunk in chunks for pieces in chunk for piece in pieces]
    rows = sum(chunk[0][0].shape[0] for chunk in chunks)
    width = sum(piece.shape[1] for piece in chunks[0][0])
    shape = jax.ShapeDtypeStruct((rows, width), jnp.bfloat16)
    kernel = functools.partial(finish_kernel, [[len(pieces) for pieces in c] for c in chunks])
    return call(kernel, [shape], flat, 8, 0, 0, "finish", earlier)[0]


def shards(
    tokens,
    norm_gain,
    w_query,
    w_key,
    w_value,
    w_out,
    keys_cache,
    values_cache,
    cached_lengths,
    rope_offsets,
):
    rows, width = tokens.shape
    requests = cached_lengths.shape[0]
    groups = lax.axis_size("seq") // requests
    heads = lax.axis_size("head")
    chips = heads // CORES
    gain = norm_gain.reshape(heads, 1, width)
    sizes = [rows * units // sum(CHUNK_UNITS) for units in CHUNK_UNITS]
    starts = [sum(sizes[:chunk]) for chunk in range(len(sizes))]
    cuts = [tokens[at : at + size] for at, size in zip(starts, sizes)]
    weights = [w_query, w_key, w_value]

    from_chips = [other_chips(cuts[0])]
    crossed = other_core(tokens)
    mark = marks(keys_cache.shape[0])
    tables = rope_tables(cached_lengths, rope_offsets, groups, rows, [mark])
    earlier = [tables[0]]
    for cut in cuts[1:]:
        (late,) = relay([cut], cut.shape[:1], earlier)
        from_chips.append(other_chips(late))
        earlier = [late]
    wides = widen(keys_cache, values_cache, mark, cached_lengths, earlier)
    earlier = [wides[0]]

    def project_chunk(chunk, earlier):
        at, count = starts[chunk], sizes[chunk]
        passed = [relay([piece], [count], earlier)[0] for piece in from_chips[chunk]]
        pieces = [[tokens]] + [[piece] for piece in passed]
        pieces += [[crossed]] + [[other_core(piece)] for piece in passed]
        queries, *new = project_rows(pieces, gain, weights, tables, at, count, passed)
        return queries, new

    def send(piece, sign):
        return [shifted(piece, "seq", sign * turn * requests) for turn in range(1, groups)]

    queries, new = project_chunk(0, earlier)
    own_queries, new_rows = [queries], [new]
    asked = [send(queries, 1)]
    own_parts = []
    for chunk in range(1, len(sizes)):
        queries, new = project_chunk(chunk, [queries])
        own_queries.append(queries)
        new_rows.append(new)
        own_parts.append(attend_own(own_queries[chunk - 1], wides, mark, new_rows[:chunk], [queries]))
        (late,) = relay([queries], [sizes[chunk]], own_parts[-1][:1])
        asked.append(send(late, 1))
        earlier = [late]
    answered = []
    for chunk in range(len(sizes)):
        answers = []
        for turn in range(1, groups):
            answer = attend(
                requests, groups, turn, asked[chunk][turn - 1], wides, mark, new_rows, earlier
            )
            answers.append(shifted(answer, "seq", -turn * requests))
            earlier = [answer]
        answered.append(answers)
        if chunk == len(sizes) - 2:
            own_parts.append(attend_own(own_queries[-1], wides, mark, new_rows, earlier))
            earlier = own_parts[-1][:1]

    parts = []
    landed = []
    for chunk in range(len(sizes)):
        last = chunk == len(sizes) - 1
        merged, fars = combine(own_parts[chunk], answered[chunk], w_out, heads, earlier)
        fars = [[other_core(part) for part in far] for far in fars]
        far, near = project_near(merged, w_out, heads)
        far = [other_core(part) for part in far]
        waited = landed + ([near[0]] if last else far)
        sums = [
            sum_cores(one, parts_far, PIECES if last else 1, waited)
            for one, parts_far in zip(near[1:], fars)
        ]
        arrived = [
            [shifted(piece, "head", CORES * k) for piece in pieces]
            for k, pieces in enumerate(sums, 1)
        ]
        parts.append([[near[0]], far, *arrived])
        landed = [pieces[0] for pieces in arrived]
        earlier = [pieces[0] for pieces in sums]
        if chunk == 0:
            pairs = send(pair_rows(new_rows, earlier), 1)
    keys_updated, values_updated, done = update(
        cached_lengths, new_rows, pairs, keys_cache, values_cache, earlier
    )
    return (finish(parts, [done]), keys_updated, values_updated)


def solution(mesh):
    return jax.shard_map(
        shards,
        mesh=mesh,
        in_specs=(
            P("seq", "head"),
            P(),
            P(None, "head"),
            P(None, "head"),
            P(None, "head"),
            P("head", None),
            P("seq", "head"),
            P("seq", "head"),
            P(),
            P(),
        ),
        out_specs=(P("seq", "head"), P("seq", "head"), P("seq", "head")),
        check_vma=False,
    )
```

time: 69.9 us -> 72 us (1.030)
  the two profiles are of different devices: /device:TPU:24 before, /device:TPU:0 now
where the time goes in v8:
time: 72 us; the launch traced here: 71 us
  waiting for transfers between devices  28.9 us (40%)
  Pallas kernels  22.5 us (31%)
  starting transfers between devices  15.6 us (22%)
  local copies, waits for them, and re-layouts  2.92 us (4%)
  between operations  0.97 us (1%)
    ppermute x10, waiting for transfers between devices, shifted(): lax.ppermute(shard, axis, [(i, (i + by) % devices) for i in range(devices)])  26.6 us
    pallas_call x22, Pallas kernels, call(): pl.pallas_call(body, out_shape=out_shape, in_specs=[VMEM] * len(arrays) +...  22.5 us
    ppermute x10, starting transfers between devices, shifted(): lax.ppermute(shard, axis, [(i, (i + by) % devices) for i in range(devices)])  13.1 us
    ppermute x11, starting transfers between devices, other_core(): return lax.ppermute(shard, 'head', [(i, i ^ 1) for i in range(devices)])  2.45 us
    ppermute x11, waiting for transfers between devices, other_core(): return lax.ppermute(shard, 'head', [(i, i ^ 1) for i in range(devices)])  2.34 us
    slice x2, local copies, waits for them, and re-layouts, shards(): cuts = [tokens[at:at + size] for at, size in zip(starts, sizes)]  2.03 us
  transfers between devices with their start and end apart: 21, of which 12 were waited for; matrix products, arithmetic and copies ran while one was open for 3% of the time, Pallas kernels for 30%

profile of v8, /device:TPU:0, one launch (start us, length us, event | category | flops | bytes accessed | tf_op | source)
XLA Modules:
  0.0 71.0 jit_solution(11284667427526939757)
XLA Ops:
  0.6 0.5 collective-permute-start.1
  1.1 0.9 %slice.6 = bf16[112,768]{1,0:T(8,128)(2,1)S(1)} slice(bf16[256,768]{1,0:T(8,128)(2,1)} %refs_0_.7), slice={[0:112], [0:768]} | slice | bytes 344064 | tf_op jit(solution)/shard_map/slice | solution.py:651
  2.1 2.6 %collective-permute-start = (bf16[112,768]{1,0:T(8,128)(2,1)S(1)}, bf16[112,768]{1,0:T(8,128)(2,1)S(1)}, u32[]{:S(2)}, u32[]{:S(2)}) collective-permute-start(bf16[112,768]{1,0:T(8,128)(2,1)S(1)} %slice.6), channel_id=1, source_target_pairs={{0,2},{1,3},{2,0},{3,1},{4,6},{5,7},{6,4},{7,5},{8,10},{9,11},{10,... | collective-permute-start | bytes 516104 | tf_op jit(solution)/shard_map/ppermute | solution.py:33
  4.7 1.1 %slice.7.refs_0_ = bf16[144,768]{1,0:T(8,128)(2,1)S(1)} slice(bf16[256,768]{1,0:T(8,128)(2,1)} %refs_0_.7), slice={[112:256], [0:768]} | slice | bytes 442368 | tf_op jit(solution)/shard_map/slice | solution.py:651
  5.9 0.8 %copy-done.6 = s32[4]{0:T(128)S(1)} copy-done((s32[4]{0:T(128)S(1)}, s32[4]{0:T(128)}, u32[]{:S(2)}) %copy-start.6) | copy-done | bytes 40
  6.7 1.6 %rope_tables.1 = (f32[512,128]{1,0:T(8,128)S(1)}, f32[512,128]{1,0:T(8,128)S(1)}) custom-call(s32[4]{0:T(128)S(1)} %copy-done.6, s32[4]{0:T(128)S(1)} %copy-done.7, bf16[2048,128]{1,0:T(8,128)(2,1)S(1)} %marks.1.refs_2_.refs_3_), custom_call_target="tpu_custom_call" | custom-call | bytes 262 | tf_op jit(solution)/shard_map/rope_tables/pallas_call | solution.py:77
  8.3 0.1 collective-permute-start.3
  8.4 0.8 %widen_caches.1 = (bf16[2,2048,256]{2,1,0:T(8,128)(2,1)S(1)}, bf16[2,2048,256]{2,1,0:T(8,128)(2,1)S(1)}) custom-call(bf16[2048,256]{1,0:T(8,128)(2,1)S(1)} %copy-done.2, bf16[2048,256]{1,0:T(8,128)(2,1)S(1)} %copy-done.3, bf16[2048,128]{1,0:T(8,128)(2,1)S(1)} %marks.1.refs_2_.refs_3_, s32[4]{0:T(128)S(1)} %copy-done.6, bf16[144,768]{1,0:T(8,128)(2,1)S(1)} %relay.4.refs_4_), custom_call_target="tpu_custom_call" | custom-call | bytes 3407 | tf_op jit(solution)/shard_map/widen_caches/pallas_call | solution.py:77
  9.2 0.5 collective-permute-done.refs_0_
  9.7 0.1 collective-permute-start.2
  9.8 1.4 %collective-permute-done.2.refs_3_ = bf16[112,768]{1,0:T(8,128)(2,1)S(1)} collective-permute-done((bf16[112,768]{1,0:T(8,128)(2,1)S(1)}, bf16[112,768]{1,0:T(8,128)(2,1)S(1)}, u32[]{:S(2)}, u32[]{:S(2)}) %collective-permute-start.2) | collective-permute-done | bytes 172064 | tf_op jit(solution)/shard_map/ppermute | solution.py:38
  11.3 1.4 %project_qkv.2 = (bf16[112,768]{1,0:T(8,128)(2,1)S(1)}, bf16[112,256]{1,0:T(8,128)(2,1)S(1)}, bf16[112,256]{1,0:T(8,128)(2,1)S(1)}) custom-call(bf16[256,768]{1,0:T(8,128)(2,1)S(1)} %copy-done.4, bf16[112,768]{1,0:T(8,128)(2,1)S(1)} %relay.5.refs_1_.refs_10_, bf16[256,768]{1,0:T(8,128)(2,1)S(1)} %collective-permute-done.1.refs_2_, ...), custom_call_target="tpu_custom_call" | custom-call | flops 440401 | bytes 4909 | tf_op jit(solution)/shard_map/project_qkv/pallas_call | solution.py:77
  12.6 3.3 %collective-permute-done.3.refs_0_ = bf16[144,768]{1,0:T(8,128)(2,1)S(1)} collective-permute-done((bf16[144,768]{1,0:T(8,128)(2,1)S(1)}, bf16[144,768]{1,0:T(8,128)(2,1)S(1)}, u32[]{:S(2)}, u32[]{:S(2)}) %collective-permute-start.3) | collective-permute-done | bytes 221216 | tf_op jit(solution)/shard_map/ppermute | solution.py:33
  16.0 0.1 collective-permute-start.4
  16.1 2.7 %collective-permute-start.5 = (bf16[112,768]{1,0:T(8,128)(2,1)S(1)}, bf16[112,768]{1,0:T(8,128)(2,1)S(1)}, u32[]{:S(2)}, u32[]{:S(2)}) collective-permute-start(bf16[112,768]{1,0:T(8,128)(2,1)S(1)} %get-tuple-element.39.refs_1_.refs_0_), channel_id=1, source_target_pairs={{0,16},{4,20},{8,24},{12,28},{16,0},{20,4},{24,8},{28,12},{1,17},{... | collective-permute-start | bytes 516104 | tf_op jit(solution)/shard_map/ppermute | solution.py:33
  18.7 1.5 %project_qkv.3 = (bf16[144,768]{1,0:T(8,128)(2,1)S(1)}, bf16[144,256]{1,0:T(8,128)(2,1)S(1)}, bf16[144,256]{1,0:T(8,128)(2,1)S(1)}) custom-call(bf16[256,768]{1,0:T(8,128)(2,1)S(1)} %copy-done.4, bf16[144,768]{1,0:T(8,128)(2,1)S(1)} %relay.6.refs_1_.refs_10_, bf16[256,768]{1,0:T(8,128)(2,1)S(1)} %collective-permute-done.1.refs_2_, ...), custom_call_target="tpu_custom_call" | custom-call | flops 566231 | bytes 4999 | tf_op jit(solution)/shard_map/project_qkv/pallas_call | solution.py:77
  20.2 2.3 %attend_own.2 = (f32[112,768]{1,0:T(8,128)S(1)}, f32[8,128]{1,0:T(8,128)S(1)}) custom-call(bf16[112,768]{1,0:T(8,128)(2,1)S(1)} %get-tuple-element.39.refs_1_.refs_0_, bf16[2,2048,256]{2,1,0:T(8,128)(2,1)S(1)} %get-tuple-element.37.refs_1_, bf16[2,2048,256]{2,1,0:T(8,128)(2,1)S(1)} %get-tuple-element.40.refs_2_, bf16[2048,128]{1,0:T(8,128)(2,1)S(1)} %marks.1.refs_2_.refs_3_, ...), custom_call_target="tpu_custom_call" | custom-call | flops 704643 | bytes 2676 | tf_op jit(solution)/shard_map/attend_own/pallas_call | solution.py:77
  22.5 1.5 %collective-permute-start.7 = (bf16[144,768]{1,0:T(8,128)(2,1)S(1)}, bf16[144,768]{1,0:T(8,128)(2,1)S(1)}, u32[]{:S(2)}, u32[]{:S(2)}) collective-permute-start(bf16[144,768]{1,0:T(8,128)(2,1)S(1)} %relay.7.refs_8_), channel_id=1, source_target_pairs={{0,16},{4,20},{8,24},{12,28},{16,0},{20,4},{24,8},{28,12},{1,17},{... | collective-permute-start | bytes 663560 | tf_op jit(solution)/shard_map/ppermute | solution.py:33
  24.0 8.6 %collective-permute-done.5.refs_0_ = bf16[112,768]{1,0:T(8,128)(2,1)S(1)} collective-permute-done((bf16[112,768]{1,0:T(8,128)(2,1)S(1)}, bf16[112,768]{1,0:T(8,128)(2,1)S(1)}, u32[]{:S(2)}, u32[]{:S(2)}) %collective-permute-start.5) | collective-permute-done | bytes 172064 | tf_op jit(solution)/shard_map/ppermute | solution.py:33
  32.6 2.5 %attend_partner.2.refs_8_ = bf16[128,768]{1,0:T(8,128)(2,1)S(1)} custom-call(bf16[112,768]{1,0:T(8,128)(2,1)S(1)} %collective-permute-done.5.refs_0_, bf16[2,2048,256]{2,1,0:T(8,128)(2,1)S(1)} %get-tuple-element.37.refs_1_, bf16[2,2048,256]{2,1,0:T(8,128)(2,1)S(1)} %get-tuple-element.40.refs_2_, bf16[2048,128]{1,0:T(8,128)(2,1)S(1)} %marks.1.refs_2_.refs_3_, ...), custom_call_target="tpu_custom_call" | custom-call | flops 704643 | bytes 2674 | tf_op jit(solution)/shard_map/attend_partner/pallas_call | solution.py:77
  35.2 3.2 %attend_own.3 = (f32[144,768]{1,0:T(8,128)S(1)}, f32[8,256]{1,0:T(8,128)S(1)}) custom-call(bf16[144,768]{1,0:T(8,128)(2,1)S(1)} %get-tuple-element.43.refs_6_.refs_0_, bf16[2,2048,256]{2,1,0:T(8,128)(2,1)S(1)} %get-tuple-element.37.refs_1_, bf16[2,2048,256]{2,1,0:T(8,128)(2,1)S(1)} %get-tuple-element.40.refs_2_, bf16[2048,128]{1,0:T(8,128)(2,1)S(1)} %marks.1.refs_2_.refs_3_, ...), custom_call_target="tpu_custom_call" | custom-call | flops 905969 | bytes 2826 | tf_op jit(solution)/shard_map/attend_own/pallas_call | solution.py:77
  38.5 3.1 %attend_partner.3.refs_4_ = bf16[160,768]{1,0:T(8,128)(2,1)S(1)} custom-call(bf16[144,768]{1,0:T(8,128)(2,1)S(1)} %collective-permute-done.7.refs_0_, bf16[2,2048,256]{2,1,0:T(8,128)(2,1)S(1)} %get-tuple-element.37.refs_1_, bf16[2,2048,256]{2,1,0:T(8,128)(2,1)S(1)} %get-tuple-element.40.refs_2_, bf16[2048,128]{1,0:T(8,128)(2,1)S(1)} %marks.1.refs_2_.refs_3_, ...), custom_call_target="tpu_custom_call" | custom-call | flops 905969 | bytes 2723 | tf_op jit(solution)/shard_map/attend_partner/pallas_call | solution.py:77
  41.6 2.9 %collective-permute-start.13 = (bf16[160,768]{1,0:T(8,128)(2,1)S(1)}, bf16[160,768]{1,0:T(8,128)(2,1)S(1)}, u32[]{:S(2)}, u32[]{:S(2)}) collective-permute-start(bf16[160,768]{1,0:T(8,128)(2,1)S(1)} %attend_partner.3.refs_4_), channel_id=1, source_target_pairs={{0,16},{4,20},{8,24},{12,28},{16,0},{20,4},{24,8},{28,12},{1,17},{... | collective-permute-start | bytes 737288 | tf_op jit(solution)/shard_map/ppermute | solution.py:33
  44.5 1.8 %collective-permute-done.6.refs_2_ = bf16[128,768]{1,0:T(8,128)(2,1)S(1)} collective-permute-done((bf16[128,768]{1,0:T(8,128)(2,1)S(1)}, bf16[128,768]{1,0:T(8,128)(2,1)S(1)}, u32[]{:S(2)}, u32[]{:S(2)}) %collective-permute-start.6) | collective-permute-done | bytes 196640 | tf_op jit(solution)/shard_map/ppermute | solution.py:33
  46.3 0.7 combine.2
  47.0 0.7 %project_near.2 = (bf16[112,384]{1,0:T(8,128)(2,1)S(1)}, bf16[112,384]{1,0:T(8,128)(2,1)S(1)}, bf16[112,768]{1,0:T(8,128)(2,1)S(1)}, bf16[112,768]{1,0:T(8,128)(2,1)S(1)}) custom-call(bf16[112,768]{1,0:T(8,128)(2,1)S(1)} %get-tuple-element.49.refs_0_, bf16[768,3072]{1,0:T(8,128)(2,1)S(1)} %bitcast.2), custom_call_target="tpu_custom_call" | custom-call | flops 264241 | bytes 2703 | tf_op jit(solution)/shard_map/project_near/pallas_call | solution.py:77
  47.7 0.1 collective-permute-start.8
  47.8 0.5 collective-permute-start.9
  48.3 0.1 collective-permute-start.10
  48.4 0.4 collective-permute-start.11
  48.8 0.3 collective-permute-done.8.refs_3_.refs_1_
  49.1 0.2 collective-permute-done.9.refs_4_.refs_2_
  49.2 0.4 collective-permute-done.10.refs_1_
  49.6 0.2 collective-permute-done.11.refs_2_
  49.8 0.1 collective-permute-start.12
  49.9 0.1 collective-permute-start.20
  50.0 1.2 %collective-permute-done.13.refs_2_ = bf16[160,768]{1,0:T(8,128)(2,1)S(1)} collective-permute-done((bf16[160,768]{1,0:T(8,128)(2,1)S(1)}, bf16[160,768]{1,0:T(8,128)(2,1)S(1)}, u32[]{:S(2)}, u32[]{:S(2)}) %collective-permute-start.13) | collective-permute-done | bytes 245792 | tf_op jit(solution)/shard_map/ppermute | solution.py:33
  51.2 0.7 %combine.3 = (bf16[144,768]{1,0:T(8,128)(2,1)S(1)}, bf16[144,384]{1,0:T(8,128)(2,1)S(1)}, bf16[144,384]{1,0:T(8,128)(2,1)S(1)}) custom-call(f32[144,768]{1,0:T(8,128)S(1)} %get-tuple-element.48.refs_8_.refs_0_, f32[8,256]{1,0:T(8,128)S(1)} %get-tuple-element.56.refs_1_, bf16[160,768]{1,0:T(8,128)(2,1)S(1)} %collective-permute-done.13.refs_2_, ...), custom_call_target="tpu_custom_call" | custom-call | flops 169869 | bytes 2928 | tf_op jit(solution)/shard_map/combine/pallas_call | solution.py:77
  52.0 0.1 collective-permute-start.16
  52.0 0.5 collective-permute-start.17
  52.5 0.7 %project_near.3 = (bf16[144,384]{1,0:T(8,128)(2,1)S(1)}, bf16[144,384]{1,0:T(8,128)(2,1)S(1)}, bf16[144,768]{1,0:T(8,128)(2,1)S(1)}, bf16[144,768]{1,0:T(8,128)(2,1)S(1)}) custom-call(bf16[144,768]{1,0:T(8,128)(2,1)S(1)} %get-tuple-element.57.refs_0_, bf16[768,3072]{1,0:T(8,128)(2,1)S(1)} %bitcast.2), custom_call_target="tpu_custom_call" | custom-call | flops 339738 | bytes 2801 | tf_op jit(solution)/shard_map/project_near/pallas_call | solution.py:77
  53.3 0.1 collective-permute-start.14
  53.4 3.1 %collective-permute-done.12.refs_3_ = bf16[112,768]{1,0:T(8,128)(2,1)S(1)} collective-permute-done((bf16[112,768]{1,0:T(8,128)(2,1)S(1)}, bf16[112,768]{1,0:T(8,128)(2,1)S(1)}, u32[]{:S(2)}, u32[]{:S(2)}) %collective-permute-start.12) | collective-permute-done | bytes 172064 | tf_op jit(solution)/shard_map/ppermute | solution.py:33
  56.6 3.1 %collective-permute-start.18 = (bf16[144,384]{1,0:T(8,128)(2,1)S(1)}, bf16[144,384]{1,0:T(8,128)(2,1)S(1)}, u32[]{:S(2)}, u32[]{:S(2)}) collective-permute-start(bf16[144,384]{1,0:T(8,128)(2,1)S(1)} %get-tuple-element.64.refs_8_), channel_id=1, source_target_pairs={{0,2},{1,3},{2,0},{3,1},{4,6},{5,7},{6,4},{7,5},{8,10},{9,11},{10,... | collective-permute-start | bytes 331784 | tf_op jit(solution)/shard_map/ppermute | solution.py:33
  59.7 0.1 collective-permute-start.19
  59.7 8.1 %collective-permute-done.20.refs_4_ = bf16[256,512]{1,0:T(8,128)(2,1)S(1)} collective-permute-done((bf16[256,512]{1,0:T(8,128)(2,1)S(1)}, bf16[256,512]{1,0:T(8,128)(2,1)S(1)}, u32[]{:S(2)}, u32[]{:S(2)}) %collective-permute-start.20) | collective-permute-done | bytes 262176 | tf_op jit(solution)/shard_map/ppermute | solution.py:33
  67.8 2.2 %update_caches.1 = (bf16[2048,256]{1,0:T(8,128)(2,1)}, bf16[2048,256]{1,0:T(8,128)(2,1)}, f32[8,128]{1,0:T(8,128)S(1)}) custom-call(bf16[112,256]{1,0:T(8,128)(2,1)S(1)} %get-tuple-element.41.refs_4_.refs_0_, bf16[144,256]{1,0:T(8,128)(2,1)S(1)} %get-tuple-element.46.refs_5_.refs_1_, bf16[112,256]{1,0:T(8,128)(2,1)S(1)} %get-tuple-element.42.refs_5_.refs_6_.refs_2_, ...), custom_call_target="tpu_custom_call" | custom-call | bytes 2361 | tf_op jit(solution)/shard_map/update_caches/pallas_call | solution.py:77
  70.0 0.9 %finish.1 = bf16[256,768]{1,0:T(8,128)(2,1)} custom-call(bf16[112,768]{1,0:T(8,128)(2,1)S(1)} %get-tuple-element.50.refs_0_, bf16[112,384]{1,0:T(8,128)(2,1)S(1)} %collective-permute-done.8.refs_3_.refs_1_, bf16[112,384]{1,0:T(8,128)(2,1)S(1)} %collective-permute-done.9.refs_4_.refs_2_, bf16[112,768]{1,0:T(8,128)(2,1)S(1)} %collective-permute-done.12.refs_3_, ...), custom_call_target="tpu_custom_call" | custom-call | bytes 786 | tf_op jit(solution)/shard_map/finish/pallas_call | solution.py:77
  (44 shorter events, 0.4 us)
Async XLA Ops:
  0.6 10.6 %collective-permute-start.1 = (bf16[256,768]{1,0:T(8,128)(2,1)}, bf16[256,768]{1,0:T(8,128)(2,1)S(1)}, u32[]{:S(2)}, u32[]{:S(2)}) collective-permute-start(bf16[256,768]{1,0:T(8,128)(2,1)} %refs_0_.7), channel_id=1, source_target_pairs={{0,1},{1,0},{2,3},{3,2},{4,5},{5,4},{6,7},{7,6},{8,9},{9,8},{10,11... | collective-permute-start | bytes 1179656 | tf_op jit(solution)/shard_map/ppermute | solution.py:38
  2.1 7.6 %collective-permute-start = (bf16[112,768]{1,0:T(8,128)(2,1)S(1)}, bf16[112,768]{1,0:T(8,128)(2,1)S(1)}, u32[]{:S(2)}, u32[]{:S(2)}) collective-permute-start(bf16[112,768]{1,0:T(8,128)(2,1)S(1)} %slice.6), channel_id=1, source_target_pairs={{0,2},{1,3},{2,0},{3,1},{4,6},{5,7},{6,4},{7,5},{8,10},{9,11},{10,... | collective-permute-start | bytes 516104 | tf_op jit(solution)/shard_map/ppermute | solution.py:33
  4.7 6.5 %slice-start.2 = ((s8[4718592]{0:T(1024)(128)(4,1)}), s8[4194304]{0:T(1024)(128)(4,1)S(1)}, s32[]{:S(2)}) async-start(s8[4718592]{0:T(1024)(128)(4,1)} %bitcast.3), calls=%async_computation.2 | async-start | bytes 8388608
  5.8 0.9 %copy-start.6 = (s32[4]{0:T(128)S(1)}, s32[4]{0:T(128)}, u32[]{:S(2)}) copy-start(s32[4]{0:T(128)} %refs_7_.5) | copy-start | bytes 52
  5.8 0.9 %copy-start.7 = (s32[4]{0:T(128)S(1)}, s32[4]{0:T(128)}, u32[]{:S(2)}) copy-start(s32[4]{0:T(128)} %refs_1_.4) | copy-start | bytes 52
  5.8 2.6 %copy-start.2 = (bf16[2048,256]{1,0:T(8,128)(2,1)S(1)}, bf16[2048,256]{1,0:T(8,128)(2,1)}, u32[]{:S(2)}) copy-start(bf16[2048,256]{1,0:T(8,128)(2,1)} %refs_5_.5) | copy-start | bytes 3145732
  5.8 2.6 %copy-start.3 = (bf16[2048,256]{1,0:T(8,128)(2,1)S(1)}, bf16[2048,256]{1,0:T(8,128)(2,1)}, u32[]{:S(2)}) copy-start(bf16[2048,256]{1,0:T(8,128)(2,1)} %refs_6_.5) | copy-start | bytes 3145732
  5.8 5.4 %slice-start.3 = ((s8[4718592]{0:T(1024)(128)(4,1)}), s8[524288]{0:T(1024)(128)(4,1)S(1)}, s32[]{:S(2)}) async-start(s8[4718592]{0:T(1024)(128)(4,1)} %bitcast.3), calls=%async_computation.3 | async-start | bytes 1048576
  8.3 2.9 %copy-start = (bf16[3072,256]{1,0:T(8,128)(2,1)S(1)}, bf16[3072,256]{1,0:T(8,128)(2,1)}, u32[]{:S(2)}) copy-start(bf16[3072,256]{1,0:T(8,128)(2,1)} %refs_6_.4) | copy-start | bytes 4718596
  8.3 2.9 %copy-start.1 = (bf16[3072,256]{1,0:T(8,128)(2,1)S(1)}, bf16[3072,256]{1,0:T(8,128)(2,1)}, u32[]{:S(2)}) copy-start(bf16[3072,256]{1,0:T(8,128)(2,1)} %refs_7_.4) | copy-start | bytes 4718596
  8.3 2.9 %copy-start.4 = (bf16[256,768]{1,0:T(8,128)(2,1)S(1)}, bf16[256,768]{1,0:T(8,128)(2,1)}, u32[]{:S(2)}) copy-start(bf16[256,768]{1,0:T(8,128)(2,1)} %refs_0_.7) | copy-start | bytes 1179652
  8.3 2.9 %copy-start.5 = (f32[3072]{0:T(1024)S(1)}, f32[3072]{0:T(1024)}, u32[]{:S(2)}) copy-start(f32[3072]{0:T(1024)} %param.11) | copy-start | bytes 36868
  8.3 7.6 %collective-permute-start.3 = (bf16[144,768]{1,0:T(8,128)(2,1)S(1)}, bf16[144,768]{1,0:T(8,128)(2,1)S(1)}, u32[]{:S(2)}, u32[]{:S(2)}) collective-permute-start(bf16[144,768]{1,0:T(8,128)(2,1)S(1)} %relay.4.refs_4_), channel_id=1, source_target_pairs={{0,2},{1,3},{2,0},{3,1},{4,6},{5,7},{6,4},{7,5},{8,10},{9,11},{10,... | collective-permute-start | bytes 663560 | tf_op jit(solution)/shard_map/ppermute | solution.py:33
  9.7 1.5 %collective-permute-start.2 = (bf16[112,768]{1,0:T(8,128)(2,1)S(1)}, bf16[112,768]{1,0:T(8,128)(2,1)S(1)}, u32[]{:S(2)}, u32[]{:S(2)}) collective-permute-start(bf16[112,768]{1,0:T(8,128)(2,1)S(1)} %relay.5.refs_1_.refs_10_), channel_id=1, source_target_pairs={{0,1},{1,0},{2,3},{3,2},{4,5},{5,4},{6,7},{7,6},{8,9},{9,8},{10,11... | collective-permute-start | bytes 516104 | tf_op jit(solution)/shard_map/ppermute | solution.py:38
  16.0 2.7 %collective-permute-start.4 = (bf16[144,768]{1,0:T(8,128)(2,1)S(1)}, bf16[144,768]{1,0:T(8,128)(2,1)S(1)}, u32[]{:S(2)}, u32[]{:S(2)}) collective-permute-start(bf16[144,768]{1,0:T(8,128)(2,1)S(1)} %relay.6.refs_1_.refs_10_), channel_id=1, source_target_pairs={{0,1},{1,0},{2,3},{3,2},{4,5},{5,4},{6,7},{7,6},{8,9},{9,8},{10,11... | collective-permute-start | bytes 663560 | tf_op jit(solution)/shard_map/ppermute | solution.py:38
  16.1 16.6 %collective-permute-start.5 = (bf16[112,768]{1,0:T(8,128)(2,1)S(1)}, bf16[112,768]{1,0:T(8,128)(2,1)S(1)}, u32[]{:S(2)}, u32[]{:S(2)}) collective-permute-start(bf16[112,768]{1,0:T(8,128)(2,1)S(1)} %get-tuple-element.39.refs_1_.refs_0_), channel_id=1, source_target_pairs={{0,16},{4,20},{8,24},{12,28},{16,0},{20,4},{24,8},{28,12},{1,17},{... | collective-permute-start | bytes 516104 | tf_op jit(solution)/shard_map/ppermute | solution.py:33
  22.5 15.9 %collective-permute-start.7 = (bf16[144,768]{1,0:T(8,128)(2,1)S(1)}, bf16[144,768]{1,0:T(8,128)(2,1)S(1)}, u32[]{:S(2)}, u32[]{:S(2)}) collective-permute-start(bf16[144,768]{1,0:T(8,128)(2,1)S(1)} %relay.7.refs_8_), channel_id=1, source_target_pairs={{0,16},{4,20},{8,24},{12,28},{16,0},{20,4},{24,8},{28,12},{1,17},{... | collective-permute-start | bytes 663560 | tf_op jit(solution)/shard_map/ppermute | solution.py:33
  32.6 13.7 %slice-start = ((s8[4718592]{0:T(1024)(128)(4,1)}), s8[4194304]{0:T(1024)(128)(4,1)S(1)}, s32[]{:S(2)}) async-start(s8[4718592]{0:T(1024)(128)(4,1)} %bitcast.1), calls=%async_computation | async-start | bytes 8388608
  35.2 11.2 %slice-start.1 = ((s8[4718592]{0:T(1024)(128)(4,1)}), s8[524288]{0:T(1024)(128)(4,1)S(1)}, s32[]{:S(2)}) async-start(s8[4718592]{0:T(1024)(128)(4,1)} %bitcast.1), calls=%async_computation.1 | async-start | bytes 1048576
  35.2 11.2 %collective-permute-start.6 = (bf16[128,768]{1,0:T(8,128)(2,1)S(1)}, bf16[128,768]{1,0:T(8,128)(2,1)S(1)}, u32[]{:S(2)}, u32[]{:S(2)}) collective-permute-start(bf16[128,768]{1,0:T(8,128)(2,1)S(1)} %attend_partner.2.refs_8_), channel_id=1, source_target_pairs={{0,16},{4,20},{8,24},{12,28},{16,0},{20,4},{24,8},{28,12},{1,17},{... | collective-permute-start | bytes 589832 | tf_op jit(solution)/shard_map/ppermute | solution.py:33
  41.6 9.7 %collective-permute-start.13 = (bf16[160,768]{1,0:T(8,128)(2,1)S(1)}, bf16[160,768]{1,0:T(8,128)(2,1)S(1)}, u32[]{:S(2)}, u32[]{:S(2)}) collective-permute-start(bf16[160,768]{1,0:T(8,128)(2,1)S(1)} %attend_partner.3.refs_4_), channel_id=1, source_target_pairs={{0,16},{4,20},{8,24},{12,28},{16,0},{20,4},{24,8},{28,12},{1,17},{... | collective-permute-start | bytes 737288 | tf_op jit(solution)/shard_map/ppermute | solution.py:33
  47.7 1.3 %collective-permute-start.8 = (bf16[112,384]{1,0:T(8,128)(2,1)S(1)}, bf16[112,384]{1,0:T(8,128)(2,1)S(1)}, u32[]{:S(2)}, u32[]{:S(2)}) collective-permute-start(bf16[112,384]{1,0:T(8,128)(2,1)S(1)} %get-tuple-element.51), channel_id=1, source_target_pairs={{0,1},{1,0},{2,3},{3,2},{4,5},{5,4},{6,7},{7,6},{8,9},{9,8},{10,11... | collective-permute-start | bytes 258056 | tf_op jit(solution)/shard_map/ppermute | solution.py:38
  47.8 1.4 %collective-permute-start.9 = (bf16[112,384]{1,0:T(8,128)(2,1)S(1)}, bf16[112,384]{1,0:T(8,128)(2,1)S(1)}, u32[]{:S(2)}, u32[]{:S(2)}) collective-permute-start(bf16[112,384]{1,0:T(8,128)(2,1)S(1)} %get-tuple-element.52), channel_id=1, source_target_pairs={{0,1},{1,0},{2,3},{3,2},{4,5},{5,4},{6,7},{7,6},{8,9},{9,8},{10,11... | collective-permute-start | bytes 258056 | tf_op jit(solution)/shard_map/ppermute | solution.py:38
  48.3 1.3 %collective-permute-start.10 = (bf16[112,384]{1,0:T(8,128)(2,1)S(1)}, bf16[112,384]{1,0:T(8,128)(2,1)S(1)}, u32[]{:S(2)}, u32[]{:S(2)}) collective-permute-start(bf16[112,384]{1,0:T(8,128)(2,1)S(1)} %get-tuple-element.54), channel_id=1, source_target_pairs={{0,1},{1,0},{2,3},{3,2},{4,5},{5,4},{6,7},{7,6},{8,9},{9,8},{10,11... | collective-permute-start | bytes 258056 | tf_op jit(solution)/shard_map/ppermute | solution.py:38
  48.4 1.4 %collective-permute-start.11 = (bf16[112,384]{1,0:T(8,128)(2,1)S(1)}, bf16[112,384]{1,0:T(8,128)(2,1)S(1)}, u32[]{:S(2)}, u32[]{:S(2)}) collective-permute-start(bf16[112,384]{1,0:T(8,128)(2,1)S(1)} %get-tuple-element.55), channel_id=1, source_target_pairs={{0,1},{1,0},{2,3},{3,2},{4,5},{5,4},{6,7},{7,6},{8,9},{9,8},{10,11... | collective-permute-start | bytes 258056 | tf_op jit(solution)/shard_map/ppermute | solution.py:38
  49.8 6.7 %collective-permute-start.12 = (bf16[112,768]{1,0:T(8,128)(2,1)S(1)}, bf16[112,768]{1,0:T(8,128)(2,1)S(1)}, u32[]{:S(2)}, u32[]{:S(2)}) collective-permute-start(bf16[112,768]{1,0:T(8,128)(2,1)S(1)} %sum_cores.2.refs_4_), channel_id=1, source_target_pairs={{0,2},{1,3},{2,0},{3,1},{4,6},{5,7},{6,4},{7,5},{8,10},{9,11},{10,... | collective-permute-start | bytes 516104 | tf_op jit(solution)/shard_map/ppermute | solution.py:33
  49.9 17.9 %collective-permute-start.20 = (bf16[256,512]{1,0:T(8,128)(2,1)S(1)}, bf16[256,512]{1,0:T(8,128)(2,1)S(1)}, u32[]{:S(2)}, u32[]{:S(2)}) collective-permute-start(bf16[256,512]{1,0:T(8,128)(2,1)S(1)} %pair_rows.1), channel_id=1, source_target_pairs={{0,16},{4,20},{8,24},{12,28},{16,0},{20,4},{24,8},{28,12},{1,17},{... | collective-permute-start | bytes 786440 | tf_op jit(solution)/shard_map/ppermute | solution.py:33
  52.0 4.5 %collective-permute-start.16 = (bf16[144,384]{1,0:T(8,128)(2,1)S(1)}, bf16[144,384]{1,0:T(8,128)(2,1)S(1)}, u32[]{:S(2)}, u32[]{:S(2)}) collective-permute-start(bf16[144,384]{1,0:T(8,128)(2,1)S(1)} %get-tuple-element.62), channel_id=1, source_target_pairs={{0,1},{1,0},{2,3},{3,2},{4,5},{5,4},{6,7},{7,6},{8,9},{9,8},{10,11... | collective-permute-start | bytes 331784 | tf_op jit(solution)/shard_map/ppermute | solution.py:38
  52.0 4.5 %collective-permute-start.17 = (bf16[144,384]{1,0:T(8,128)(2,1)S(1)}, bf16[144,384]{1,0:T(8,128)(2,1)S(1)}, u32[]{:S(2)}, u32[]{:S(2)}) collective-permute-start(bf16[144,384]{1,0:T(8,128)(2,1)S(1)} %get-tuple-element.63), channel_id=1, source_target_pairs={{0,1},{1,0},{2,3},{3,2},{4,5},{5,4},{6,7},{7,6},{8,9},{9,8},{10,11... | collective-permute-start | bytes 331784 | tf_op jit(solution)/shard_map/ppermute | solution.py:38
  53.3 16.7 %collective-permute-start.14 = (bf16[144,384]{1,0:T(8,128)(2,1)S(1)}, bf16[144,384]{1,0:T(8,128)(2,1)S(1)}, u32[]{:S(2)}, u32[]{:S(2)}) collective-permute-start(bf16[144,384]{1,0:T(8,128)(2,1)S(1)} %get-tuple-element.59), channel_id=1, source_target_pairs={{0,1},{1,0},{2,3},{3,2},{4,5},{5,4},{6,7},{7,6},{8,9},{9,8},{10,11... | collective-permute-start | bytes 331784 | tf_op jit(solution)/shard_map/ppermute | solution.py:38
  56.5 13.5 %collective-permute-start.15 = (bf16[144,384]{1,0:T(8,128)(2,1)S(1)}, bf16[144,384]{1,0:T(8,128)(2,1)S(1)}, u32[]{:S(2)}, u32[]{:S(2)}) collective-permute-start(bf16[144,384]{1,0:T(8,128)(2,1)S(1)} %get-tuple-element.60), channel_id=1, source_target_pairs={{0,1},{1,0},{2,3},{3,2},{4,5},{5,4},{6,7},{7,6},{8,9},{9,8},{10,11... | collective-permute-start | bytes 331784 | tf_op jit(solution)/shard_map/ppermute | solution.py:38
  56.6 13.5 %collective-permute-start.18 = (bf16[144,384]{1,0:T(8,128)(2,1)S(1)}, bf16[144,384]{1,0:T(8,128)(2,1)S(1)}, u32[]{:S(2)}, u32[]{:S(2)}) collective-permute-start(bf16[144,384]{1,0:T(8,128)(2,1)S(1)} %get-tuple-element.64.refs_8_), channel_id=1, source_target_pairs={{0,2},{1,3},{2,0},{3,1},{4,6},{5,7},{6,4},{7,5},{8,10},{9,11},{10,... | collective-permute-start | bytes 331784 | tf_op jit(solution)/shard_map/ppermute | solution.py:33
  59.7 10.4 %collective-permute-start.19 = (bf16[144,384]{1,0:T(8,128)(2,1)S(1)}, bf16[144,384]{1,0:T(8,128)(2,1)S(1)}, u32[]{:S(2)}, u32[]{:S(2)}) collective-permute-start(bf16[144,384]{1,0:T(8,128)(2,1)S(1)} %get-tuple-element.65), channel_id=1, source_target_pairs={{0,2},{1,3},{2,0},{3,1},{4,6},{5,7},{6,4},{7,5},{8,10},{9,11},{10,... | collective-permute-start | bytes 331784 | tf_op jit(solution)/shard_map/ppermute | solution.py:33

commit v9 on v6

--- a/solution.py
+++ b/solution.py
@@ -15,7 +15,7 @@
 CORES = 2
 CHUNKS = 2
 COST_WEIGHT = 0.0005
-FIRST_MICROS = 1
+FIRST_MICROS = 2
 FLOPS_PER_MICRO = 1_000_000_000
 MIB = 1 << 20
 
@@ -160,7 +160,6 @@
             pltpu.SMEM(offsets.shape, offsets.dtype),
             pltpu.SemaphoreType.DMA((2,)),
         ],
-        FIRST_MICROS,
     )
 
 
@@ -196,7 +195,6 @@
         "widen_caches",
         earlier,
         [pltpu.SMEM(lengths.shape, lengths.dtype), pltpu.SemaphoreType.DMA],
-        FIRST_MICROS,
     )
 
 
@@ -627,7 +625,6 @@
     chunk_rows = rows // CHUNKS
     gain = norm_gain.reshape(heads, 1, width)
 
-    early = tokens[:chunk_rows]
     mark = marks(keys_cache.shape[0])
     tables = rope_tables(cached_lengths, rope_offsets, groups, rows, [mark])
     wide_keys, wide_values = widen(keys_cache, values_cache, mark, cached_lengths, tables[:1])
@@ -640,46 +637,44 @@
         )
 
     half = chunk_rows // 2
-    first = [shifted(early, "seq", turn * requests) for turn in range(1, groups)]
-    from_chips = other_chips(tokens)
-    (late,) = relay([tokens[chunk_rows:]], [rows - chunk_rows], from_chips + [wide_keys])
+    own, *own_halves = relay([tokens], [rows, chunk_rows, rows - chunk_rows], [mark])
+    first = [shifted(own_halves[0], "seq", turn * requests) for turn in range(1, groups)]
+    from_chips = list(zip(*[other_chips(part) for part in own_halves]))
+    crossed = other_core(own)
+    (late,) = relay(own_halves[1:], [rows - chunk_rows], [wide_keys])
     second = [shifted(late, "seq", turn * requests) for turn in range(1, groups)]
-    own_cuts = [relay([piece], [rows, half, half, rows - chunk_rows], [late]) for piece in from_chips]
-    own_pieces = [[tokens]] + [[cut[0]] for cut in own_cuts] + [[other_core(tokens)]]
+    first = [relay([piece], [chunk_rows], [late])[0] for piece in first]
+    first_from_chips = [other_chips(piece) for piece in first]
+    own_cuts = [relay(pair, [rows, half, half, rows - chunk_rows], first) for pair in from_chips]
+    own_pieces = [[own]] + [[cut[0]] for cut in own_cuts] + [[crossed]]
     own_pieces += [[other_core(block) for block in cut[1:]] for cut in own_cuts]
     own_early = [
         blocks if len(blocks) == 1 else blocks[: len(blocks) - 1] for blocks in own_pieces
     ]
-    *own_part, queries = attend_rows(own_early, True, 0, 0, [cut[0] for cut in own_cuts])
+    earlier = [cut[0] for cut in own_cuts]
+
+    *own_part, queries = attend_rows(own_early, True, 0, 0, earlier)
     own_queries = [queries]
-
-    earlier = [queries]
-    first = [relay([piece], [chunk_rows], earlier)[0] for piece in first]
-    first_from_chips = [other_chips(piece) for piece in first]
-    *late_part, queries = attend_rows(own_pieces, True, 1, 0, first)
-    own_part += late_part
-    own_queries.append(queries)
     earlier = [queries]
     second = [relay([piece], [rows - chunk_rows], earlier)[0] for piece in second]
     second_from_chips = [other_chips(piece) for piece in second]
     earlier = second
 
     def gather_cores(piece, from_chips, earlier):
-        passed = [relay([one], [one.shape[0]], earlier)[0] for one in from_chips]
-        along = [piece] + passed
-        return along + [other_core(one) for one in along], passed
+        size = piece.shape[0]
+        passed = [relay([one], [size, size // 2, size // 2], earlier) for one in from_chips]
+        blocks = [[piece]] + [[one[0]] for one in passed] + [[other_core(piece)]]
+        blocks += [[other_core(part) for part in one[1:]] for one in passed]
+        return blocks, [one[0] for one in passed]
 
     gathered = []
     for piece, from_chips in zip(first, first_from_chips):
-        along, passed = gather_cores(piece, from_chips, earlier)
-        gathered.append([along])
+        blocks, passed = gather_cores(piece, from_chips, earlier)
+        gathered.append([blocks])
         earlier = earlier + passed
-    new_rows = [fresh(own_pieces, gain, w_key, w_value, tables, 0, earlier)]
-    earlier = [new_rows[0][0]]
     received = [[] for _ in range(CHUNKS)]
     for turn in range(1, groups):
-        pieces = [[block] for block in gathered[turn - 1][0]]
-        (packed,) = attend_rows(pieces, False, 0, turn, earlier)
+        (packed,) = attend_rows(gathered[turn - 1][0], False, 0, turn, earlier)
         received[0].append(shifted(packed, "seq", -turn * requests))
         earlier = [packed]
     for blocks, piece, from_chips in zip(gathered, second, second_from_chips):
@@ -687,12 +682,16 @@
         blocks.append(along)
         earlier = earlier + passed
     for turn in range(1, groups):
-        pieces = [[block] for block in gathered[turn - 1][1]]
-        (packed,) = attend_rows(pieces, False, 1, turn, earlier)
+        (packed,) = attend_rows(gathered[turn - 1][1], False, 1, turn, earlier)
         received[1].append(shifted(packed, "seq", -turn * requests))
         earlier = [packed]
+    *late_part, queries = attend_rows(own_pieces, True, 1, 0, earlier)
+    own_part += late_part
+    own_queries.append(queries)
+    new_rows = [fresh(own_pieces, gain, w_key, w_value, tables, 0, [queries])]
+    earlier = [new_rows[0][0]]
     for turn in range(1, groups):
-        pieces = [list(blocks) for blocks in zip(*gathered[turn - 1])]
+        pieces = [sum(blocks, []) for blocks in zip(*gathered[turn - 1])]
         new_rows.append(fresh(pieces, gain, w_key, w_value, tables, turn * rows, earlier))
     new_keys, new_values = zip(*new_rows)
     fresh_part = attend_fresh(requests, own_queries, new_keys, new_values)

time: 70.2 us -> 68.2 us (0.972)
  starting transfers between devices: 18.6 us -> 15.8 us
  Pallas kernels: 26.6 us -> 27.6 us
    ppermute x9 -> x10, starting transfers between devices: 15.3 us -> 11.5 us  [shifted(): lax.ppermute(shard, axis, [(i, (i + by) % devices) for i in range(devices)])]
    ppermute x14 -> x16, starting transfers between devices: 3.32 us -> 4.37 us  [other_core(): return lax.ppermute(shard, 'head', [(i, i ^ 1) for i in range(devices)])]
    slice x1 -> x0, local copies, waits for them, and re-layouts: 1.05 us -> none  [shards(): early = tokens[:chunk_rows]]
    pallas_call x24 -> x25, Pallas kernels: 26.6 us -> 27.6 us  [call(): pl.pallas_call(body, out_shape=out_shape, in_specs=[VMEM] * len(arrays) +...]
    unnamed x24, local copies, waits for them, and re-layouts: 0.14 us -> 0.94 us
    ppermute x14 -> x16, waiting for transfers between devices: 1.7 us -> 2.33 us  [other_core(): return lax.ppermute(shard, 'head', [(i, i ^ 1) for i in range(devices)])]
    ppermute x9 -> x10, waiting for transfers between devices: 21 us -> 20.4 us  [shifted(): lax.ppermute(shard, axis, [(i, (i + by) % devices) for i in range(devices)])]
  transfers between devices with their start and end apart: 23 -> 26, of which waited for: 11 -> 12; matrix products, arithmetic and copies ran while one was open for 1% -> 0% of each run, Pallas kernels for 37% -> 39%
where the time goes in v9:
time: 68.2 us; the launch traced here: 68 us
  Pallas kernels  27.6 us (40%)
  waiting for transfers between devices  22.7 us (33%)
  starting transfers between devices  15.8 us (23%)
  local copies, waits for them, and re-layouts  0.94 us (1%)
  between operations  0.94 us (1%)
    pallas_call x25, Pallas kernels, call(): pl.pallas_call(body, out_shape=out_shape, in_specs=[VMEM] * len(arrays) +...  27.6 us
    ppermute x10, waiting for transfers between devices, shifted(): lax.ppermute(shard, axis, [(i, (i + by) % devices) for i in range(devices)])  20.4 us
    ppermute x10, starting transfers between devices, shifted(): lax.ppermute(shard, axis, [(i, (i + by) % devices) for i in range(devices)])  11.5 us
    ppermute x16, starting transfers between devices, other_core(): return lax.ppermute(shard, 'head', [(i, i ^ 1) for i in range(devices)])  4.37 us
    ppermute x16, waiting for transfers between devices, other_core(): return lax.ppermute(shard, 'head', [(i, i ^ 1) for i in range(devices)])  2.33 us
  transfers between devices with their start and end apart: 26, of which 12 were waited for; matrix products, arithmetic and copies ran while one was open for 0% of the time, Pallas kernels for 39%

profile of v9, /device:TPU:0, one launch (start us, length us, event | category | flops | bytes accessed | tf_op | source)
XLA Modules:
  0.0 68.0 jit_solution(3092216501041250054)
XLA Ops:
  0.7 0.9 %copy-done.5 = bf16[256,768]{1,0:T(8,128)(2,1)S(1)} copy-done((bf16[256,768]{1,0:T(8,128)(2,1)S(1)}, bf16[256,768]{1,0:T(8,128)(2,1)}, u32[]{:S(2)}) %copy-start.5) | copy-done | bytes 393240
  1.7 0.5 collective-permute-start.3
  2.2 3.7 %collective-permute-start.2 = (bf16[128,768]{1,0:T(8,128)(2,1)S(1)}, bf16[128,768]{1,0:T(8,128)(2,1)S(1)}, u32[]{:S(2)}, u32[]{:S(2)}) collective-permute-start(bf16[128,768]{1,0:T(8,128)(2,1)S(1)} %get-tuple-element.48), channel_id=1, source_target_pairs={{0,16},{4,20},{8,24},{12,28},{16,0},{20,4},{24,8},{28,12},{1,17},{... | collective-permute-start | bytes 589832 | tf_op jit(solution)/shard_map/ppermute | solution.py:32
  5.9 1.6 %collective-permute-start = (bf16[128,768]{1,0:T(8,128)(2,1)S(1)}, bf16[128,768]{1,0:T(8,128)(2,1)S(1)}, u32[]{:S(2)}, u32[]{:S(2)}) collective-permute-start(bf16[128,768]{1,0:T(8,128)(2,1)S(1)} %get-tuple-element.48), channel_id=1, source_target_pairs={{0,2},{1,3},{2,0},{3,1},{4,6},{5,7},{6,4},{7,5},{8,10},{9,11},{10,... | collective-permute-start | bytes 589832 | tf_op jit(solution)/shard_map/ppermute | solution.py:32
  7.4 0.5 collective-permute-start.1
  7.9 1.6 %rope_tables.1 = (f32[512,128]{1,0:T(8,128)S(1)}, f32[512,128]{1,0:T(8,128)S(1)}) custom-call(s32[4]{0:T(128)S(1)} %copy-done.6, s32[4]{0:T(128)S(1)} %copy-done.7, bf16[2048,128]{1,0:T(8,128)(2,1)S(1)} %marks.1.refs_1_.refs_2_.refs_11_.refs_12_), custom_call_target="tpu_custom_call" | custom-call | bytes 262 | tf_op jit(solution)/shard_map/rope_tables/pallas_call | solution.py:76
  9.5 0.8 %widen_caches.1 = (bf16[2,2048,256]{2,1,0:T(8,128)(2,1)S(1)}, bf16[2,2048,256]{2,1,0:T(8,128)(2,1)S(1)}) custom-call(bf16[2048,256]{1,0:T(8,128)(2,1)S(1)} %copy-done.2, bf16[2048,256]{1,0:T(8,128)(2,1)S(1)} %copy-done.3, bf16[2048,128]{1,0:T(8,128)(2,1)S(1)} %marks.1.refs_1_.refs_2_.refs_11_.refs_12_, s32[4]{0:T(128)S(1)} %copy-done.6, ...), custom_call_target="tpu_custom_call" | custom-call | bytes 3407 | tf_op jit(solution)/shard_map/widen_caches/pallas_call | solution.py:76
  10.3 0.1 collective-permute-start.7
  10.5 9.6 %collective-permute-done.2.refs_0_ = bf16[128,768]{1,0:T(8,128)(2,1)S(1)} collective-permute-done((bf16[128,768]{1,0:T(8,128)(2,1)S(1)}, bf16[128,768]{1,0:T(8,128)(2,1)S(1)}, u32[]{:S(2)}, u32[]{:S(2)}) %collective-permute-start.2) | collective-permute-done | bytes 196640 | tf_op jit(solution)/shard_map/ppermute | solution.py:32
  20.1 1.8 %collective-permute-start.9 = (bf16[128,768]{1,0:T(8,128)(2,1)S(1)}, bf16[128,768]{1,0:T(8,128)(2,1)S(1)}, u32[]{:S(2)}, u32[]{:S(2)}) collective-permute-start(bf16[128,768]{1,0:T(8,128)(2,1)S(1)} %relay.9.refs_2_.refs_0_), channel_id=1, source_target_pairs={{0,2},{1,3},{2,0},{3,1},{4,6},{5,7},{6,4},{7,5},{8,10},{9,11},{10,... | collective-permute-start | bytes 589832 | tf_op jit(solution)/shard_map/ppermute | solution.py:32
  22.1 0.5 collective-permute-start.5
  22.5 0.8 %collective-permute-done.4.refs_3_ = bf16[64,768]{1,0:T(8,128)(2,1)S(1)} collective-permute-done((bf16[64,768]{1,0:T(8,128)(2,1)S(1)}, bf16[64,768]{1,0:T(8,128)(2,1)S(1)}, u32[]{:S(2)}, u32[]{:S(2)}) %collective-permute-start.4) | collective-permute-done | bytes 98336 | tf_op jit(solution)/shard_map/ppermute | solution.py:37
  23.3 0.2 collective-permute-start.10
  23.5 3.5 %attend_own.2 = (f32[128,768]{1,0:T(8,128)S(1)}, f32[8,128]{1,0:T(8,128)S(1)}, bf16[128,768]{1,0:T(8,128)(2,1)S(1)}) custom-call(bf16[256,768]{1,0:T(8,128)(2,1)S(1)} %get-tuple-element.47.refs_0_, bf16[256,768]{1,0:T(8,128)(2,1)S(1)} %get-tuple-element.52.refs_1_.refs_12_, bf16[256,768]{1,0:T(8,128)(2,1)S(1)} %collective-permute-done.3.refs_2_, ...), custom_call_target="tpu_custom_call" | custom-call | flops 1107296 | bytes 5971 | tf_op jit(solution)/shard_map/attend_own/pallas_call | solution.py:76
  27.1 0.4 collective-permute-start.11
  27.6 0.2 collective-permute-start.12
  27.7 0.8 %collective-permute-start.8 = (bf16[128,768]{1,0:T(8,128)(2,1)S(1)}, bf16[128,768]{1,0:T(8,128)(2,1)S(1)}, u32[]{:S(2)}, u32[]{:S(2)}) collective-permute-start(bf16[128,768]{1,0:T(8,128)(2,1)S(1)} %relay.11.refs_1_.refs_12_.refs_0_), channel_id=1, source_target_pairs={{0,2},{1,3},{2,0},{3,1},{4,6},{5,7},{6,4},{7,5},{8,10},{9,11},{10,... | collective-permute-start | bytes 589832 | tf_op jit(solution)/shard_map/ppermute | solution.py:32
  28.5 0.3 collective-permute-done.12.refs_4_.refs_7_
  28.9 3.5 %attend_partner.2.refs_1_.refs_12_ = bf16[144,768]{1,0:T(8,128)(2,1)S(1)} custom-call(bf16[128,768]{1,0:T(8,128)(2,1)S(1)} %relay.9.refs_2_.refs_0_, bf16[128,768]{1,0:T(8,128)(2,1)S(1)} %get-tuple-element.61.refs_1_.refs_13_.refs_2_, bf16[128,768]{1,0:T(8,128)(2,1)S(1)} %collective-permute-done.10.refs_2_.refs_4_, ...), custom_call_target="tpu_custom_call" | custom-call | flops 1107296 | bytes 5490 | tf_op jit(solution)/shard_map/attend_partner/pallas_call | solution.py:76
  32.4 0.3 collective-permute-start.6
  32.7 2.2 %collective-permute-done.8.refs_0_ = bf16[128,768]{1,0:T(8,128)(2,1)S(1)} collective-permute-done((bf16[128,768]{1,0:T(8,128)(2,1)S(1)}, bf16[128,768]{1,0:T(8,128)(2,1)S(1)}, u32[]{:S(2)}, u32[]{:S(2)}) %collective-permute-start.8) | collective-permute-done | bytes 196640 | tf_op jit(solution)/shard_map/ppermute | solution.py:32
  35.0 0.5 collective-permute-start.15
  35.5 0.8 %collective-permute-done.14.refs_3_.refs_8_ = bf16[64,768]{1,0:T(8,128)(2,1)S(1)} collective-permute-done((bf16[64,768]{1,0:T(8,128)(2,1)S(1)}, bf16[64,768]{1,0:T(8,128)(2,1)S(1)}, u32[]{:S(2)}, u32[]{:S(2)}) %collective-permute-start.14) | collective-permute-done | bytes 98336 | tf_op jit(solution)/shard_map/ppermute | solution.py:37
  36.3 0.2 collective-permute-done.15.refs_4_.refs_9_
  36.4 3.7 %attend_partner.3.refs_13_ = bf16[144,768]{1,0:T(8,128)(2,1)S(1)} custom-call(bf16[128,768]{1,0:T(8,128)(2,1)S(1)} %relay.11.refs_1_.refs_12_.refs_0_, bf16[128,768]{1,0:T(8,128)(2,1)S(1)} %get-tuple-element.64.refs_1_.refs_13_.refs_3_, bf16[128,768]{1,0:T(8,128)(2,1)S(1)} %collective-permute-done.13.refs_2_.refs_5_, ...), custom_call_target="tpu_custom_call" | custom-call | flops 1107296 | bytes 5490 | tf_op jit(solution)/shard_map/attend_partner/pallas_call | solution.py:76
  40.1 0.8 %collective-permute-start.21 = (bf16[144,768]{1,0:T(8,128)(2,1)S(1)}, bf16[144,768]{1,0:T(8,128)(2,1)S(1)}, u32[]{:S(2)}, u32[]{:S(2)}) collective-permute-start(bf16[144,768]{1,0:T(8,128)(2,1)S(1)} %attend_partner.3.refs_13_), channel_id=1, source_target_pairs={{0,16},{4,20},{8,24},{12,28},{16,0},{20,4},{24,8},{28,12},{1,17},{... | collective-permute-start | bytes 663560 | tf_op jit(solution)/shard_map/ppermute | solution.py:32
  41.0 3.5 %attend_own.3 = (f32[128,768]{1,0:T(8,128)S(1)}, f32[8,128]{1,0:T(8,128)S(1)}, bf16[128,768]{1,0:T(8,128)(2,1)S(1)}) custom-call(bf16[256,768]{1,0:T(8,128)(2,1)S(1)} %get-tuple-element.47.refs_0_, bf16[256,768]{1,0:T(8,128)(2,1)S(1)} %get-tuple-element.52.refs_1_.refs_12_, bf16[256,768]{1,0:T(8,128)(2,1)S(1)} %collective-permute-done.3.refs_2_, ...), custom_call_target="tpu_custom_call" | custom-call | flops 1107296 | bytes 6070 | tf_op jit(solution)/shard_map/attend_own/pallas_call | solution.py:76
  44.5 1.2 %fresh_kv.2 = (bf16[256,256]{1,0:T(8,128)(2,1)S(1)}, bf16[256,256]{1,0:T(8,128)(2,1)S(1)}) custom-call(bf16[256,768]{1,0:T(8,128)(2,1)S(1)} %get-tuple-element.47.refs_0_, bf16[256,768]{1,0:T(8,128)(2,1)S(1)} %get-tuple-element.52.refs_1_.refs_12_, bf16[256,768]{1,0:T(8,128)(2,1)S(1)} %collective-permute-done.3.refs_2_, ...), custom_call_target="tpu_custom_call" | custom-call | flops 402653 | bytes 2758 | tf_op jit(solution)/shard_map/fresh_kv/pallas_call | solution.py:76
  45.6 1.1 %fresh_kv.3 = (bf16[256,256]{1,0:T(8,128)(2,1)S(1)}, bf16[256,256]{1,0:T(8,128)(2,1)S(1)}) custom-call(bf16[128,768]{1,0:T(8,128)(2,1)S(1)} %relay.9.refs_2_.refs_0_, bf16[128,768]{1,0:T(8,128)(2,1)S(1)} %relay.11.refs_1_.refs_12_.refs_0_, bf16[128,768]{1,0:T(8,128)(2,1)S(1)} %get-tuple-element.61.refs_1_.refs_13_.refs_2_, ...), custom_call_target="tpu_custom_call" | custom-call | flops 402653 | bytes 2758 | tf_op jit(solution)/shard_map/fresh_kv/pallas_call | solution.py:76
  46.8 2.3 %attend_fresh.1 = (f32[256,768]{1,0:T(8,128)S(1)}, f32[8,256]{1,0:T(8,128)S(1)}) custom-call(bf16[128,768]{1,0:T(8,128)(2,1)S(1)} %get-tuple-element.59.refs_1_.refs_0_, bf16[128,768]{1,0:T(8,128)(2,1)S(1)} %get-tuple-element.67.refs_11_.refs_1_, bf16[256,256]{1,0:T(8,128)(2,1)S(1)} %get-tuple-element.68.refs_15_.refs_2_.refs_0_, ...), custom_call_target="tpu_custom_call" | custom-call | flops 201326 | bytes 856 | tf_op jit(solution)/shard_map/attend_fresh/pallas_call | solution.py:76
  49.1 1.9 %collective-permute-done.16.refs_4_ = bf16[144,768]{1,0:T(8,128)(2,1)S(1)} collective-permute-done((bf16[144,768]{1,0:T(8,128)(2,1)S(1)}, bf16[144,768]{1,0:T(8,128)(2,1)S(1)}, u32[]{:S(2)}, u32[]{:S(2)}) %collective-permute-start.16) | collective-permute-done | bytes 221216 | tf_op jit(solution)/shard_map/ppermute | solution.py:32
  51.0 0.8 %combine.2 = (bf16[128,768]{1,0:T(8,128)(2,1)S(1)}, bf16[128,384]{1,0:T(8,128)(2,1)S(1)}, bf16[128,384]{1,0:T(8,128)(2,1)S(1)}) custom-call(f32[128,768]{1,0:T(8,128)S(1)} %get-tuple-element.57.refs_0_, f32[8,128]{1,0:T(8,128)S(1)} %get-tuple-element.58.refs_1_, f32[256,768]{1,0:T(8,128)S(1)} %get-tuple-element.72.refs_2_, ...), custom_call_target="tpu_custom_call" | custom-call | flops 150994 | bytes 3262 | tf_op jit(solution)/shard_map/combine/pallas_call | solution.py:76
  51.9 0.5 collective-permute-start.19
  52.4 0.7 project.2
  53.1 0.1 collective-permute-done.18.refs_1_
  53.2 0.2 collective-permute-done.19.refs_2_
  53.4 1.0 %collective-permute-start.20 = (bf16[128,768]{1,0:T(8,128)(2,1)S(1)}, bf16[128,768]{1,0:T(8,128)(2,1)S(1)}, u32[]{:S(2)}, u32[]{:S(2)}) collective-permute-start(bf16[128,768]{1,0:T(8,128)(2,1)S(1)} %sum_cores.2.refs_6_), channel_id=1, source_target_pairs={{0,2},{1,3},{2,0},{3,1},{4,6},{5,7},{6,4},{7,5},{8,10},{9,11},{10,... | collective-permute-start | bytes 589832 | tf_op jit(solution)/shard_map/ppermute | solution.py:32
  54.5 0.6 collective-permute-done.21.refs_4_
  55.0 0.8 %combine.3 = (bf16[128,768]{1,0:T(8,128)(2,1)S(1)}, bf16[128,384]{1,0:T(8,128)(2,1)S(1)}, bf16[128,384]{1,0:T(8,128)(2,1)S(1)}) custom-call(f32[128,768]{1,0:T(8,128)S(1)} %get-tuple-element.80.refs_0_, f32[8,128]{1,0:T(8,128)S(1)} %get-tuple-element.81.refs_1_, f32[256,768]{1,0:T(8,128)S(1)} %get-tuple-element.72.refs_2_, ...), custom_call_target="tpu_custom_call" | custom-call | flops 150994 | bytes 3262 | tf_op jit(solution)/shard_map/combine/pallas_call | solution.py:76
  56.0 0.5 collective-permute-start.24
  56.5 0.1 collective-permute-start.17
  56.5 0.7 %project.3 = (bf16[128,768]{1,0:T(8,128)(2,1)S(1)}, bf16[128,768]{1,0:T(8,128)(2,1)S(1)}, bf16[128,768]{1,0:T(8,128)(2,1)S(1)}) custom-call(bf16[128,768]{1,0:T(8,128)(2,1)S(1)} %get-tuple-element.82.refs_0_, bf16[768,3072]{1,0:T(8,128)(2,1)S(1)} %bitcast.4), custom_call_target="tpu_custom_call" | custom-call | flops 301989 | bytes 2752 | tf_op jit(solution)/shard_map/project/pallas_call | solution.py:76
  57.2 0.5 collective-permute-start.22
  57.7 2.9 %collective-permute-done.20.refs_4_.refs_2_ = bf16[128,768]{1,0:T(8,128)(2,1)S(1)} collective-permute-done((bf16[128,768]{1,0:T(8,128)(2,1)S(1)}, bf16[128,768]{1,0:T(8,128)(2,1)S(1)}, u32[]{:S(2)}, u32[]{:S(2)}) %collective-permute-start.20) | collective-permute-done | bytes 196640 | tf_op jit(solution)/shard_map/ppermute | solution.py:32
  60.7 1.0 %collective-permute-start.25 = (bf16[128,768]{1,0:T(8,128)(2,1)S(1)}, bf16[128,768]{1,0:T(8,128)(2,1)S(1)}, u32[]{:S(2)}, u32[]{:S(2)}) collective-permute-start(bf16[128,768]{1,0:T(8,128)(2,1)S(1)} %sum_cores.3.refs_7_), channel_id=1, source_target_pairs={{0,2},{1,3},{2,0},{3,1},{4,6},{5,7},{6,4},{7,5},{8,10},{9,11},{10,... | collective-permute-start | bytes 589832 | tf_op jit(solution)/shard_map/ppermute | solution.py:32
  61.7 2.2 %update_caches.1 = (bf16[2048,256]{1,0:T(8,128)(2,1)}, bf16[2048,256]{1,0:T(8,128)(2,1)}, f32[8,128]{1,0:T(8,128)S(1)}) custom-call(bf16[256,256]{1,0:T(8,128)(2,1)S(1)} %get-tuple-element.68.refs_15_.refs_2_.refs_0_, bf16[256,256]{1,0:T(8,128)(2,1)S(1)} %get-tuple-element.69.refs_3_.refs_1_, bf16[256,256]{1,0:T(8,128)(2,1)S(1)} %get-tuple-element.70.refs_4_.refs_2_, ...), custom_call_target="tpu_custom_call" | custom-call | flops 67108 | bytes 2361 | tf_op jit(solution)/shard_map/update_caches/pallas_call | solution.py:76
  63.9 3.2 %collective-permute-done.25.refs_5_ = bf16[128,768]{1,0:T(8,128)(2,1)S(1)} collective-permute-done((bf16[128,768]{1,0:T(8,128)(2,1)S(1)}, bf16[128,768]{1,0:T(8,128)(2,1)S(1)}, u32[]{:S(2)}, u32[]{:S(2)}) %collective-permute-start.25) | collective-permute-done | bytes 196640 | tf_op jit(solution)/shard_map/ppermute | solution.py:32
  67.1 0.9 %finish.1 = bf16[256,768]{1,0:T(8,128)(2,1)} custom-call(bf16[128,768]{1,0:T(8,128)(2,1)S(1)} %get-tuple-element.75.refs_0_, bf16[128,768]{1,0:T(8,128)(2,1)S(1)} %collective-permute-done.17.refs_1_, bf16[128,768]{1,0:T(8,128)(2,1)S(1)} %collective-permute-done.20.refs_4_.refs_2_, bf16[128,768]{1,0:T(8,128)(2,1)S(1)} %get-tuple-element.83.refs_3_, ...), custom_call_target="tpu_custom_call" | custom-call | flops 98 | bytes 786 | tf_op jit(solution)/shard_map/finish/pallas_call | solution.py:76
  (55 shorter events, 0.8 us)
Async XLA Ops:
  0.6 1.0 %copy-start.5 = (bf16[256,768]{1,0:T(8,128)(2,1)S(1)}, bf16[256,768]{1,0:T(8,128)(2,1)}, u32[]{:S(2)}) copy-start(bf16[256,768]{1,0:T(8,128)(2,1)} %refs_0_.3) | copy-start | bytes 1179652
  0.6 7.3 %copy-start.6 = (s32[4]{0:T(128)S(1)}, s32[4]{0:T(128)}, u32[]{:S(2)}) copy-start(s32[4]{0:T(128)} %refs_6_.7) | copy-start | bytes 52
  0.7 7.2 %copy-start.7 = (s32[4]{0:T(128)S(1)}, s32[4]{0:T(128)}, u32[]{:S(2)}) copy-start(s32[4]{0:T(128)} %refs_1_.4) | copy-start | bytes 52
  0.7 8.8 %copy-start.2 = (bf16[2048,256]{1,0:T(8,128)(2,1)S(1)}, bf16[2048,256]{1,0:T(8,128)(2,1)}, u32[]{:S(2)}) copy-start(bf16[2048,256]{1,0:T(8,128)(2,1)} %refs_4_.1) | copy-start | bytes 3145732
  0.7 8.8 %copy-start.3 = (bf16[2048,256]{1,0:T(8,128)(2,1)S(1)}, bf16[2048,256]{1,0:T(8,128)(2,1)}, u32[]{:S(2)}) copy-start(bf16[2048,256]{1,0:T(8,128)(2,1)} %refs_5_.5) | copy-start | bytes 3145732
  0.7 22.8 %slice-start = ((s8[4718592]{0:T(1024)(128)(4,1)}), s8[4194304]{0:T(1024)(128)(4,1)S(1)}, s32[]{:S(2)}) async-start(s8[4718592]{0:T(1024)(128)(4,1)} %bitcast.1), calls=%async_computation | async-start | bytes 8388608
  1.6 21.9 %slice-start.1 = ((s8[4718592]{0:T(1024)(128)(4,1)}), s8[524288]{0:T(1024)(128)(4,1)S(1)}, s32[]{:S(2)}) async-start(s8[4718592]{0:T(1024)(128)(4,1)} %bitcast.1), calls=%async_computation.1 | async-start | bytes 1048576
  1.7 21.8 %collective-permute-start.3 = (bf16[256,768]{1,0:T(8,128)(2,1)S(1)}, bf16[256,768]{1,0:T(8,128)(2,1)S(1)}, u32[]{:S(2)}, u32[]{:S(2)}) collective-permute-start(bf16[256,768]{1,0:T(8,128)(2,1)S(1)} %get-tuple-element.47.refs_0_), channel_id=1, source_target_pairs={{0,1},{1,0},{2,3},{3,2},{4,5},{5,4},{6,7},{7,6},{8,9},{9,8},{10,11... | collective-permute-start | bytes 1179656 | tf_op jit(solution)/shard_map/ppermute | solution.py:37
  2.2 17.8 %collective-permute-start.2 = (bf16[128,768]{1,0:T(8,128)(2,1)S(1)}, bf16[128,768]{1,0:T(8,128)(2,1)S(1)}, u32[]{:S(2)}, u32[]{:S(2)}) collective-permute-start(bf16[128,768]{1,0:T(8,128)(2,1)S(1)} %get-tuple-element.48), channel_id=1, source_target_pairs={{0,16},{4,20},{8,24},{12,28},{16,0},{20,4},{24,8},{28,12},{1,17},{... | collective-permute-start | bytes 589832 | tf_op jit(solution)/shard_map/ppermute | solution.py:32
  5.9 16.0 %collective-permute-start = (bf16[128,768]{1,0:T(8,128)(2,1)S(1)}, bf16[128,768]{1,0:T(8,128)(2,1)S(1)}, u32[]{:S(2)}, u32[]{:S(2)}) collective-permute-start(bf16[128,768]{1,0:T(8,128)(2,1)S(1)} %get-tuple-element.48), channel_id=1, source_target_pairs={{0,2},{1,3},{2,0},{3,1},{4,6},{5,7},{6,4},{7,5},{8,10},{9,11},{10,... | collective-permute-start | bytes 589832 | tf_op jit(solution)/shard_map/ppermute | solution.py:32
  7.4 14.5 %collective-permute-start.1 = (bf16[128,768]{1,0:T(8,128)(2,1)S(1)}, bf16[128,768]{1,0:T(8,128)(2,1)S(1)}, u32[]{:S(2)}, u32[]{:S(2)}) collective-permute-start(bf16[128,768]{1,0:T(8,128)(2,1)S(1)} %get-tuple-element.49.refs_0_), channel_id=1, source_target_pairs={{0,2},{1,3},{2,0},{3,1},{4,6},{5,7},{6,4},{7,5},{8,10},{9,11},{10,... | collective-permute-start | bytes 589832 | tf_op jit(solution)/shard_map/ppermute | solution.py:32
  10.3 13.2 %copy-start.4 = (f32[3072]{0:T(1024)S(1)}, f32[3072]{0:T(1024)}, u32[]{:S(2)}) copy-start(f32[3072]{0:T(1024)} %param.11) | copy-start | bytes 36868
  10.3 16.7 %collective-permute-start.7 = (bf16[128,768]{1,0:T(8,128)(2,1)S(1)}, bf16[128,768]{1,0:T(8,128)(2,1)S(1)}, u32[]{:S(2)}, u32[]{:S(2)}) collective-permute-start(bf16[128,768]{1,0:T(8,128)(2,1)S(1)} %relay.8.refs_1_), channel_id=1, source_target_pairs={{0,16},{4,20},{8,24},{12,28},{16,0},{20,4},{24,8},{28,12},{1,17},{... | collective-permute-start | bytes 589832 | tf_op jit(solution)/shard_map/ppermute | solution.py:32
  20.1 7.0 %collective-permute-start.9 = (bf16[128,768]{1,0:T(8,128)(2,1)S(1)}, bf16[128,768]{1,0:T(8,128)(2,1)S(1)}, u32[]{:S(2)}, u32[]{:S(2)}) collective-permute-start(bf16[128,768]{1,0:T(8,128)(2,1)S(1)} %relay.9.refs_2_.refs_0_), channel_id=1, source_target_pairs={{0,2},{1,3},{2,0},{3,1},{4,6},{5,7},{6,4},{7,5},{8,10},{9,11},{10,... | collective-permute-start | bytes 589832 | tf_op jit(solution)/shard_map/ppermute | solution.py:32
  22.0 1.4 %collective-permute-start.4 = (bf16[64,768]{1,0:T(8,128)(2,1)S(1)}, bf16[64,768]{1,0:T(8,128)(2,1)S(1)}, u32[]{:S(2)}, u32[]{:S(2)}) collective-permute-start(bf16[64,768]{1,0:T(8,128)(2,1)S(1)} %get-tuple-element.53), channel_id=1, source_target_pairs={{0,1},{1,0},{2,3},{3,2},{4,5},{5,4},{6,7},{7,6},{8,9},{9,8},{10,11... | collective-permute-start | bytes 294920 | tf_op jit(solution)/shard_map/ppermute | solution.py:37
  22.1 1.4 %collective-permute-start.5 = (bf16[64,768]{1,0:T(8,128)(2,1)S(1)}, bf16[64,768]{1,0:T(8,128)(2,1)S(1)}, u32[]{:S(2)}, u32[]{:S(2)}) collective-permute-start(bf16[64,768]{1,0:T(8,128)(2,1)S(1)} %get-tuple-element.54), channel_id=1, source_target_pairs={{0,1},{1,0},{2,3},{3,2},{4,5},{5,4},{6,7},{7,6},{8,9},{9,8},{10,11... | collective-permute-start | bytes 294920 | tf_op jit(solution)/shard_map/ppermute | solution.py:37
  23.3 5.2 %collective-permute-start.10 = (bf16[128,768]{1,0:T(8,128)(2,1)S(1)}, bf16[128,768]{1,0:T(8,128)(2,1)S(1)}, u32[]{:S(2)}, u32[]{:S(2)}) collective-permute-start(bf16[128,768]{1,0:T(8,128)(2,1)S(1)} %relay.9.refs_2_.refs_0_), channel_id=1, source_target_pairs={{0,1},{1,0},{2,3},{3,2},{4,5},{5,4},{6,7},{7,6},{8,9},{9,8},{10,11... | collective-permute-start | bytes 589832 | tf_op jit(solution)/shard_map/ppermute | solution.py:37
  27.1 1.4 %collective-permute-start.11 = (bf16[64,768]{1,0:T(8,128)(2,1)S(1)}, bf16[64,768]{1,0:T(8,128)(2,1)S(1)}, u32[]{:S(2)}, u32[]{:S(2)}) collective-permute-start(bf16[64,768]{1,0:T(8,128)(2,1)S(1)} %get-tuple-element.62), channel_id=1, source_target_pairs={{0,1},{1,0},{2,3},{3,2},{4,5},{5,4},{6,7},{7,6},{8,9},{9,8},{10,11... | collective-permute-start | bytes 294920 | tf_op jit(solution)/shard_map/ppermute | solution.py:37
  27.6 1.3 %collective-permute-start.12 = (bf16[64,768]{1,0:T(8,128)(2,1)S(1)}, bf16[64,768]{1,0:T(8,128)(2,1)S(1)}, u32[]{:S(2)}, u32[]{:S(2)}) collective-permute-start(bf16[64,768]{1,0:T(8,128)(2,1)S(1)} %get-tuple-element.63), channel_id=1, source_target_pairs={{0,1},{1,0},{2,3},{3,2},{4,5},{5,4},{6,7},{7,6},{8,9},{9,8},{10,11... | collective-permute-start | bytes 294920 | tf_op jit(solution)/shard_map/ppermute | solution.py:37
  27.7 7.2 %collective-permute-start.8 = (bf16[128,768]{1,0:T(8,128)(2,1)S(1)}, bf16[128,768]{1,0:T(8,128)(2,1)S(1)}, u32[]{:S(2)}, u32[]{:S(2)}) collective-permute-start(bf16[128,768]{1,0:T(8,128)(2,1)S(1)} %relay.11.refs_1_.refs_12_.refs_0_), channel_id=1, source_target_pairs={{0,2},{1,3},{2,0},{3,1},{4,6},{5,7},{6,4},{7,5},{8,10},{9,11},{10,... | collective-permute-start | bytes 589832 | tf_op jit(solution)/shard_map/ppermute | solution.py:32
  28.5 7.0 %collective-permute-start.13 = (bf16[128,768]{1,0:T(8,128)(2,1)S(1)}, bf16[128,768]{1,0:T(8,128)(2,1)S(1)}, u32[]{:S(2)}, u32[]{:S(2)}) collective-permute-start(bf16[128,768]{1,0:T(8,128)(2,1)S(1)} %relay.11.refs_1_.refs_12_.refs_0_), channel_id=1, source_target_pairs={{0,1},{1,0},{2,3},{3,2},{4,5},{5,4},{6,7},{7,6},{8,9},{9,8},{10,11... | collective-permute-start | bytes 589832 | tf_op jit(solution)/shard_map/ppermute | solution.py:37
  32.3 18.7 %collective-permute-start.16 = (bf16[144,768]{1,0:T(8,128)(2,1)S(1)}, bf16[144,768]{1,0:T(8,128)(2,1)S(1)}, u32[]{:S(2)}, u32[]{:S(2)}) collective-permute-start(bf16[144,768]{1,0:T(8,128)(2,1)S(1)} %attend_partner.2.refs_1_.refs_12_), channel_id=1, source_target_pairs={{0,16},{4,20},{8,24},{12,28},{16,0},{20,4},{24,8},{28,12},{1,17},{... | collective-permute-start | bytes 663560 | tf_op jit(solution)/shard_map/ppermute | solution.py:32
  32.4 8.6 %collective-permute-start.6 = (bf16[128,768]{1,0:T(8,128)(2,1)S(1)}, bf16[128,768]{1,0:T(8,128)(2,1)S(1)}, u32[]{:S(2)}, u32[]{:S(2)}) collective-permute-start(bf16[128,768]{1,0:T(8,128)(2,1)S(1)} %get-tuple-element.60), channel_id=1, source_target_pairs={{0,1},{1,0},{2,3},{3,2},{4,5},{5,4},{6,7},{7,6},{8,9},{9,8},{10,11... | collective-permute-start | bytes 589832 | tf_op jit(solution)/shard_map/ppermute | solution.py:37
  34.9 1.4 %collective-permute-start.14 = (bf16[64,768]{1,0:T(8,128)(2,1)S(1)}, bf16[64,768]{1,0:T(8,128)(2,1)S(1)}, u32[]{:S(2)}, u32[]{:S(2)}) collective-permute-start(bf16[64,768]{1,0:T(8,128)(2,1)S(1)} %get-tuple-element.65), channel_id=1, source_target_pairs={{0,1},{1,0},{2,3},{3,2},{4,5},{5,4},{6,7},{7,6},{8,9},{9,8},{10,11... | collective-permute-start | bytes 294920 | tf_op jit(solution)/shard_map/ppermute | solution.py:37
  35.0 1.4 %collective-permute-start.15 = (bf16[64,768]{1,0:T(8,128)(2,1)S(1)}, bf16[64,768]{1,0:T(8,128)(2,1)S(1)}, u32[]{:S(2)}, u32[]{:S(2)}) collective-permute-start(bf16[64,768]{1,0:T(8,128)(2,1)S(1)} %get-tuple-element.66), channel_id=1, source_target_pairs={{0,1},{1,0},{2,3},{3,2},{4,5},{5,4},{6,7},{7,6},{8,9},{9,8},{10,11... | collective-permute-start | bytes 294920 | tf_op jit(solution)/shard_map/ppermute | solution.py:37
  40.1 4.4 %copy-start = (bf16[3072,256]{1,0:T(8,128)(2,1)S(1)}, bf16[3072,256]{1,0:T(8,128)(2,1)}, u32[]{:S(2)}) copy-start(bf16[3072,256]{1,0:T(8,128)(2,1)} %refs_11_.1) | copy-start | bytes 4718596
  40.1 4.4 %copy-start.1 = (bf16[3072,256]{1,0:T(8,128)(2,1)S(1)}, bf16[3072,256]{1,0:T(8,128)(2,1)}, u32[]{:S(2)}) copy-start(bf16[3072,256]{1,0:T(8,128)(2,1)} %refs_12_.1) | copy-start | bytes 4718596
  40.1 14.9 %collective-permute-start.21 = (bf16[144,768]{1,0:T(8,128)(2,1)S(1)}, bf16[144,768]{1,0:T(8,128)(2,1)S(1)}, u32[]{:S(2)}, u32[]{:S(2)}) collective-permute-start(bf16[144,768]{1,0:T(8,128)(2,1)S(1)} %attend_partner.3.refs_13_), channel_id=1, source_target_pairs={{0,16},{4,20},{8,24},{12,28},{16,0},{20,4},{24,8},{28,12},{1,17},{... | collective-permute-start | bytes 663560 | tf_op jit(solution)/shard_map/ppermute | solution.py:32
  41.0 10.1 %slice-start.2 = ((s8[4718592]{0:T(1024)(128)(4,1)}), s8[524288]{0:T(1024)(128)(4,1)S(1)}, s32[]{:S(2)}) async-start(s8[4718592]{0:T(1024)(128)(4,1)} %bitcast.3), calls=%async_computation.2 | async-start | bytes 1048576
  44.5 6.5 %slice-start.3 = ((s8[4718592]{0:T(1024)(128)(4,1)}), s8[4194304]{0:T(1024)(128)(4,1)S(1)}, s32[]{:S(2)}) async-start(s8[4718592]{0:T(1024)(128)(4,1)} %bitcast.3), calls=%async_computation.3 | async-start | bytes 8388608
  51.9 1.4 %collective-permute-start.18 = (bf16[128,384]{1,0:T(8,128)(2,1)S(1)}, bf16[128,384]{1,0:T(8,128)(2,1)S(1)}, u32[]{:S(2)}, u32[]{:S(2)}) collective-permute-start(bf16[128,384]{1,0:T(8,128)(2,1)S(1)} %get-tuple-element.78), channel_id=1, source_target_pairs={{0,1},{1,0},{2,3},{3,2},{4,5},{5,4},{6,7},{7,6},{8,9},{9,8},{10,11... | collective-permute-start | bytes 294920 | tf_op jit(solution)/shard_map/ppermute | solution.py:37
  51.9 1.4 %collective-permute-start.19 = (bf16[128,384]{1,0:T(8,128)(2,1)S(1)}, bf16[128,384]{1,0:T(8,128)(2,1)S(1)}, u32[]{:S(2)}, u32[]{:S(2)}) collective-permute-start(bf16[128,384]{1,0:T(8,128)(2,1)S(1)} %get-tuple-element.79), channel_id=1, source_target_pairs={{0,1},{1,0},{2,3},{3,2},{4,5},{5,4},{6,7},{7,6},{8,9},{9,8},{10,11... | collective-permute-start | bytes 294920 | tf_op jit(solution)/shard_map/ppermute | solution.py:37
  53.4 7.2 %collective-permute-start.20 = (bf16[128,768]{1,0:T(8,128)(2,1)S(1)}, bf16[128,768]{1,0:T(8,128)(2,1)S(1)}, u32[]{:S(2)}, u32[]{:S(2)}) collective-permute-start(bf16[128,768]{1,0:T(8,128)(2,1)S(1)} %sum_cores.2.refs_6_), channel_id=1, source_target_pairs={{0,2},{1,3},{2,0},{3,1},{4,6},{5,7},{6,4},{7,5},{8,10},{9,11},{10,... | collective-permute-start | bytes 589832 | tf_op jit(solution)/shard_map/ppermute | solution.py:32
  55.9 1.8 %collective-permute-start.23 = (bf16[128,384]{1,0:T(8,128)(2,1)S(1)}, bf16[128,384]{1,0:T(8,128)(2,1)S(1)}, u32[]{:S(2)}, u32[]{:S(2)}) collective-permute-start(bf16[128,384]{1,0:T(8,128)(2,1)S(1)} %get-tuple-element.86), channel_id=1, source_target_pairs={{0,1},{1,0},{2,3},{3,2},{4,5},{5,4},{6,7},{7,6},{8,9},{9,8},{10,11... | collective-permute-start | bytes 294920 | tf_op jit(solution)/shard_map/ppermute | solution.py:37
  56.0 1.8 %collective-permute-start.24 = (bf16[128,384]{1,0:T(8,128)(2,1)S(1)}, bf16[128,384]{1,0:T(8,128)(2,1)S(1)}, u32[]{:S(2)}, u32[]{:S(2)}) collective-permute-start(bf16[128,384]{1,0:T(8,128)(2,1)S(1)} %get-tuple-element.87), channel_id=1, source_target_pairs={{0,1},{1,0},{2,3},{3,2},{4,5},{5,4},{6,7},{7,6},{8,9},{9,8},{10,11... | collective-permute-start | bytes 294920 | tf_op jit(solution)/shard_map/ppermute | solution.py:37
  56.5 7.5 %collective-permute-start.17 = (bf16[128,768]{1,0:T(8,128)(2,1)S(1)}, bf16[128,768]{1,0:T(8,128)(2,1)S(1)}, u32[]{:S(2)}, u32[]{:S(2)}) collective-permute-start(bf16[128,768]{1,0:T(8,128)(2,1)S(1)} %get-tuple-element.76.refs_3_), channel_id=1, source_target_pairs={{0,1},{1,0},{2,3},{3,2},{4,5},{5,4},{6,7},{7,6},{8,9},{9,8},{10,11... | collective-permute-start | bytes 589832 | tf_op jit(solution)/shard_map/ppermute | solution.py:37
  57.2 6.7 %collective-permute-start.22 = (bf16[128,768]{1,0:T(8,128)(2,1)S(1)}, bf16[128,768]{1,0:T(8,128)(2,1)S(1)}, u32[]{:S(2)}, u32[]{:S(2)}) collective-permute-start(bf16[128,768]{1,0:T(8,128)(2,1)S(1)} %get-tuple-element.84.refs_3_), channel_id=1, source_target_pairs={{0,1},{1,0},{2,3},{3,2},{4,5},{5,4},{6,7},{7,6},{8,9},{9,8},{10,11... | collective-permute-start | bytes 589832 | tf_op jit(solution)/shard_map/ppermute | solution.py:37
  60.7 6.4 %collective-permute-start.25 = (bf16[128,768]{1,0:T(8,128)(2,1)S(1)}, bf16[128,768]{1,0:T(8,128)(2,1)S(1)}, u32[]{:S(2)}, u32[]{:S(2)}) collective-permute-start(bf16[128,768]{1,0:T(8,128)(2,1)S(1)} %sum_cores.3.refs_7_), channel_id=1, source_target_pairs={{0,2},{1,3},{2,0},{3,1},{4,6},{5,7},{6,4},{7,5},{8,10},{9,11},{10,... | collective-permute-start | bytes 589832 | tf_op jit(solution)/shard_map/ppermute | solution.py:32

commit v10 on v9

--- a/solution.py
+++ b/solution.py
@@ -637,25 +637,25 @@
         )
 
     half = chunk_rows // 2
-    own, *own_halves = relay([tokens], [rows, chunk_rows, rows - chunk_rows], [mark])
-    first = [shifted(own_halves[0], "seq", turn * requests) for turn in range(1, groups)]
-    from_chips = list(zip(*[other_chips(part) for part in own_halves]))
-    crossed = other_core(own)
-    (late,) = relay(own_halves[1:], [rows - chunk_rows], [wide_keys])
+    from_chips = other_chips(tokens)
+    crossed = other_core(tokens)
+    own, early, late = relay([tokens], [rows, chunk_rows, rows - chunk_rows], [])
+    first = [shifted(early, "seq", turn * requests) for turn in range(1, groups)]
+    (late,) = relay([late], [rows - chunk_rows], from_chips + [wide_keys])
     second = [shifted(late, "seq", turn * requests) for turn in range(1, groups)]
-    first = [relay([piece], [chunk_rows], [late])[0] for piece in first]
-    first_from_chips = [other_chips(piece) for piece in first]
-    own_cuts = [relay(pair, [rows, half, half, rows - chunk_rows], first) for pair in from_chips]
+    own_cuts = [relay([piece], [rows, half, half, rows - chunk_rows], [late]) for piece in from_chips]
     own_pieces = [[own]] + [[cut[0]] for cut in own_cuts] + [[crossed]]
     own_pieces += [[other_core(block) for block in cut[1:]] for cut in own_cuts]
     own_early = [
         blocks if len(blocks) == 1 else blocks[: len(blocks) - 1] for blocks in own_pieces
     ]
     earlier = [cut[0] for cut in own_cuts]
-
-    *own_part, queries = attend_rows(own_early, True, 0, 0, earlier)
+    first = [relay([piece], [chunk_rows], earlier)[0] for piece in first]
+    first_from_chips = [other_chips(piece) for piece in first]
+    *own_part, queries = attend_rows(own_early, True, 0, 0, first)
     own_queries = [queries]
-    earlier = [queries]
+    new_rows = [fresh(own_pieces, gain, w_key, w_value, tables, 0, [queries])]
+    earlier = [new_rows[0][0]]
     second = [relay([piece], [rows - chunk_rows], earlier)[0] for piece in second]
     second_from_chips = [other_chips(piece) for piece in second]
     earlier = second
@@ -677,6 +677,10 @@
         (packed,) = attend_rows(gathered[turn - 1][0], False, 0, turn, earlier)
         received[0].append(shifted(packed, "seq", -turn * requests))
         earlier = [packed]
+    *late_part, queries = attend_rows(own_pieces, True, 1, 0, earlier)
+    own_part += late_part
+    own_queries.append(queries)
+    earlier = [queries]
     for blocks, piece, from_chips in zip(gathered, second, second_from_chips):
         along, passed = gather_cores(piece, from_chips, earlier)
         blocks.append(along)
@@ -685,11 +689,6 @@
         (packed,) = attend_rows(gathered[turn - 1][1], False, 1, turn, earlier)
         received[1].append(shifted(packed, "seq", -turn * requests))
         earlier = [packed]
-    *late_part, queries = attend_rows(own_pieces, True, 1, 0, earlier)
-    own_part += late_part
-    own_queries.append(queries)
-    new_rows = [fresh(own_pieces, gain, w_key, w_value, tables, 0, [queries])]
-    earlier = [new_rows[0][0]]
     for turn in range(1, groups):
         pieces = [sum(blocks, []) for blocks in zip(*gathered[turn - 1])]
         new_rows.append(fresh(pieces, gain, w_key, w_value, tables, turn * rows, earlier))

time: 68.2 us -> 64.9 us (0.952)
  waiting for transfers between devices: 22.7 us -> 15.6 us
  starting transfers between devices: 15.8 us -> 19.4 us
    ppermute x10 -> x9, waiting for transfers between devices: 20.4 us -> 13.3 us  [shifted(): lax.ppermute(shard, axis, [(i, (i + by) % devices) for i in range(devices)])]
    ppermute x10 -> x9, starting transfers between devices: 11.5 us -> 15.7 us  [shifted(): lax.ppermute(shard, axis, [(i, (i + by) % devices) for i in range(devices)])]
  transfers between devices with their start and end apart: 26 -> 25, of which waited for: 12 -> 10; matrix products, arithmetic and copies ran while one was open for 0% -> 0% of each run, Pallas kernels for 39% -> 41%
where the time goes in v10:
time: 64.9 us; the launch traced here: 64.8 us
  Pallas kernels  27.7 us (43%)
  starting transfers between devices  19.4 us (30%)
  waiting for transfers between devices  15.6 us (24%)
  local copies, waits for them, and re-layouts  1.09 us (2%)
  between operations  0.97 us (1%)
    pallas_call x25, Pallas kernels, call(): pl.pallas_call(body, out_shape=out_shape, in_specs=[VMEM] * len(arrays) +...  27.7 us
    ppermute x9, starting transfers between devices, shifted(): lax.ppermute(shard, axis, [(i, (i + by) % devices) for i in range(devices)])  15.7 us
    ppermute x9, waiting for transfers between devices, shifted(): lax.ppermute(shard, axis, [(i, (i + by) % devices) for i in range(devices)])  13.3 us
    ppermute x16, starting transfers between devices, other_core(): return lax.ppermute(shard, 'head', [(i, i ^ 1) for i in range(devices)])  3.72 us
    ppermute x16, waiting for transfers between devices, other_core(): return lax.ppermute(shard, 'head', [(i, i ^ 1) for i in range(devices)])  2.29 us
  transfers between devices with their start and end apart: 25, of which 10 were waited for; matrix products, arithmetic and copies ran while one was open for 0% of the time, Pallas kernels for 41%

profile of v10, /device:TPU:0, one launch (start us, length us, event | category | flops | bytes accessed | tf_op | source)
XLA Modules:
  0.0 64.8 jit_solution(5655902970584343264)
XLA Ops:
  0.6 3.0 %collective-permute-start = (bf16[256,768]{1,0:T(8,128)(2,1)}, bf16[256,768]{1,0:T(8,128)(2,1)S(1)}, u32[]{:S(2)}, u32[]{:S(2)}) collective-permute-start(bf16[256,768]{1,0:T(8,128)(2,1)} %refs_0_.3), channel_id=1, source_target_pairs={{0,2},{1,3},{2,0},{3,1},{4,6},{5,7},{6,4},{7,5},{8,10},{9,11},{10,... | collective-permute-start | bytes 1179656 | tf_op jit(solution)/shard_map/ppermute | solution.py:32
  3.7 1.0 %copy-done.5 = bf16[256,768]{1,0:T(8,128)(2,1)S(1)} copy-done((bf16[256,768]{1,0:T(8,128)(2,1)S(1)}, bf16[256,768]{1,0:T(8,128)(2,1)}, u32[]{:S(2)}) %copy-start.5) | copy-done | bytes 393240
  4.8 2.7 %collective-permute-start.4 = (bf16[128,768]{1,0:T(8,128)(2,1)S(1)}, bf16[128,768]{1,0:T(8,128)(2,1)S(1)}, u32[]{:S(2)}, u32[]{:S(2)}) collective-permute-start(bf16[128,768]{1,0:T(8,128)(2,1)S(1)} %get-tuple-element.56), channel_id=1, source_target_pairs={{0,16},{4,20},{8,24},{12,28},{16,0},{20,4},{24,8},{28,12},{1,17},{... | collective-permute-start | bytes 589832 | tf_op jit(solution)/shard_map/ppermute | solution.py:32
  7.5 1.6 %rope_tables.1 = (f32[512,128]{1,0:T(8,128)S(1)}, f32[512,128]{1,0:T(8,128)S(1)}) custom-call(s32[4]{0:T(128)S(1)} %copy-done.6, s32[4]{0:T(128)S(1)} %copy-done.7, bf16[2048,128]{1,0:T(8,128)(2,1)S(1)} %marks.1.refs_2_.refs_11_.refs_12_), custom_call_target="tpu_custom_call" | custom-call | bytes 262 | tf_op jit(solution)/shard_map/rope_tables/pallas_call | solution.py:76
  9.1 0.8 %widen_caches.1 = (bf16[2,2048,256]{2,1,0:T(8,128)(2,1)S(1)}, bf16[2,2048,256]{2,1,0:T(8,128)(2,1)S(1)}) custom-call(bf16[2048,256]{1,0:T(8,128)(2,1)S(1)} %copy-done.2, bf16[2048,256]{1,0:T(8,128)(2,1)S(1)} %copy-done.3, bf16[2048,128]{1,0:T(8,128)(2,1)S(1)} %marks.1.refs_2_.refs_11_.refs_12_, s32[4]{0:T(128)S(1)} %copy-done.6, ...), custom_call_target="tpu_custom_call" | custom-call | bytes 3407 | tf_op jit(solution)/shard_map/widen_caches/pallas_call | solution.py:76
  9.9 3.1 %collective-permute-done.refs_1_.refs_0_ = bf16[256,768]{1,0:T(8,128)(2,1)S(1)} collective-permute-done((bf16[256,768]{1,0:T(8,128)(2,1)}, bf16[256,768]{1,0:T(8,128)(2,1)S(1)}, u32[]{:S(2)}, u32[]{:S(2)}) %collective-permute-start) | collective-permute-done | bytes 393248 | tf_op jit(solution)/shard_map/ppermute | solution.py:32
  13.1 0.1 collective-permute-start.5
  13.1 2.9 %collective-permute-start.7 = (bf16[128,768]{1,0:T(8,128)(2,1)S(1)}, bf16[128,768]{1,0:T(8,128)(2,1)S(1)}, u32[]{:S(2)}, u32[]{:S(2)}) collective-permute-start(bf16[128,768]{1,0:T(8,128)(2,1)S(1)} %relay.8.refs_1_), channel_id=1, source_target_pairs={{0,16},{4,20},{8,24},{12,28},{16,0},{20,4},{24,8},{28,12},{1,17},{... | collective-permute-start | bytes 589832 | tf_op jit(solution)/shard_map/ppermute | solution.py:32
  16.0 1.2 %collective-permute-done.4.refs_0_ = bf16[128,768]{1,0:T(8,128)(2,1)S(1)} collective-permute-done((bf16[128,768]{1,0:T(8,128)(2,1)S(1)}, bf16[128,768]{1,0:T(8,128)(2,1)S(1)}, u32[]{:S(2)}, u32[]{:S(2)}) %collective-permute-start.4) | collective-permute-done | bytes 196640 | tf_op jit(solution)/shard_map/ppermute | solution.py:32
  17.3 0.5 collective-permute-start.6
  17.8 0.5 collective-permute-start.3
  18.3 0.8 %collective-permute-done.2.refs_3_ = bf16[64,768]{1,0:T(8,128)(2,1)S(1)} collective-permute-done((bf16[64,768]{1,0:T(8,128)(2,1)S(1)}, bf16[64,768]{1,0:T(8,128)(2,1)S(1)}, u32[]{:S(2)}, u32[]{:S(2)}) %collective-permute-start.2) | collective-permute-done | bytes 98336 | tf_op jit(solution)/shard_map/ppermute | solution.py:37
  19.1 0.2 collective-permute-start.8
  19.3 3.5 %attend_own.2 = (f32[128,768]{1,0:T(8,128)S(1)}, f32[8,128]{1,0:T(8,128)S(1)}, bf16[128,768]{1,0:T(8,128)(2,1)S(1)}) custom-call(bf16[256,768]{1,0:T(8,128)(2,1)S(1)} %get-tuple-element.47.refs_0_, bf16[256,768]{1,0:T(8,128)(2,1)S(1)} %get-tuple-element.51.refs_1_, bf16[256,768]{1,0:T(8,128)(2,1)S(1)} %collective-permute-done.1.refs_2_, ...), custom_call_target="tpu_custom_call" | custom-call | flops 1107296 | bytes 5971 | tf_op jit(solution)/shard_map/attend_own/pallas_call | solution.py:76
  22.9 1.1 %fresh_kv.2 = (bf16[256,256]{1,0:T(8,128)(2,1)S(1)}, bf16[256,256]{1,0:T(8,128)(2,1)S(1)}) custom-call(bf16[256,768]{1,0:T(8,128)(2,1)S(1)} %get-tuple-element.47.refs_0_, bf16[256,768]{1,0:T(8,128)(2,1)S(1)} %get-tuple-element.51.refs_1_, bf16[256,768]{1,0:T(8,128)(2,1)S(1)} %collective-permute-done.1.refs_2_, ...), custom_call_target="tpu_custom_call" | custom-call | flops 402653 | bytes 2758 | tf_op jit(solution)/shard_map/fresh_kv/pallas_call | solution.py:76
  24.0 1.7 %collective-permute-done.7.refs_0_ = bf16[128,768]{1,0:T(8,128)(2,1)S(1)} collective-permute-done((bf16[128,768]{1,0:T(8,128)(2,1)S(1)}, bf16[128,768]{1,0:T(8,128)(2,1)S(1)}, u32[]{:S(2)}, u32[]{:S(2)}) %collective-permute-start.7) | collective-permute-done | bytes 196640 | tf_op jit(solution)/shard_map/ppermute | solution.py:32
  25.8 0.1 collective-permute-start.9
  25.9 0.5 collective-permute-start.10
  26.4 1.6 %collective-permute-start.11 = (bf16[128,768]{1,0:T(8,128)(2,1)S(1)}, bf16[128,768]{1,0:T(8,128)(2,1)S(1)}, u32[]{:S(2)}, u32[]{:S(2)}) collective-permute-start(bf16[128,768]{1,0:T(8,128)(2,1)S(1)} %relay.11.refs_1_.refs_12_.refs_0_), channel_id=1, source_target_pairs={{0,2},{1,3},{2,0},{3,1},{4,6},{5,7},{6,4},{7,5},{8,10},{9,11},{10,... | collective-permute-start | bytes 589832 | tf_op jit(solution)/shard_map/ppermute | solution.py:32
  28.0 3.6 %attend_partner.2.refs_13_ = bf16[144,768]{1,0:T(8,128)(2,1)S(1)} custom-call(bf16[128,768]{1,0:T(8,128)(2,1)S(1)} %relay.10.refs_12_.refs_0_, bf16[128,768]{1,0:T(8,128)(2,1)S(1)} %get-tuple-element.62.refs_1_.refs_13_.refs_2_, bf16[128,768]{1,0:T(8,128)(2,1)S(1)} %collective-permute-done.8.refs_2_.refs_4_, ...), custom_call_target="tpu_custom_call" | custom-call | flops 1107296 | bytes 5490 | tf_op jit(solution)/shard_map/attend_partner/pallas_call | solution.py:76
  31.6 0.1 collective-permute-start.12
  31.6 3.8 %attend_own.3 = (f32[128,768]{1,0:T(8,128)S(1)}, f32[8,128]{1,0:T(8,128)S(1)}, bf16[128,768]{1,0:T(8,128)(2,1)S(1)}) custom-call(bf16[256,768]{1,0:T(8,128)(2,1)S(1)} %get-tuple-element.47.refs_0_, bf16[256,768]{1,0:T(8,128)(2,1)S(1)} %get-tuple-element.51.refs_1_, bf16[256,768]{1,0:T(8,128)(2,1)S(1)} %collective-permute-done.1.refs_2_, ...), custom_call_target="tpu_custom_call" | custom-call | flops 1107296 | bytes 6070 | tf_op jit(solution)/shard_map/attend_own/pallas_call | solution.py:76
  35.4 0.6 collective-permute-start.13
  36.0 0.1 collective-permute-start.14
  36.1 0.9 %collective-permute-done.13.refs_3_.refs_8_ = bf16[64,768]{1,0:T(8,128)(2,1)S(1)} collective-permute-done((bf16[64,768]{1,0:T(8,128)(2,1)S(1)}, bf16[64,768]{1,0:T(8,128)(2,1)S(1)}, u32[]{:S(2)}, u32[]{:S(2)}) %collective-permute-start.13) | collective-permute-done | bytes 98336 | tf_op jit(solution)/shard_map/ppermute | solution.py:37
  36.9 0.4 collective-permute-done.14.refs_4_.refs_9_
  37.3 3.5 %attend_partner.3.refs_15_ = bf16[144,768]{1,0:T(8,128)(2,1)S(1)} custom-call(bf16[128,768]{1,0:T(8,128)(2,1)S(1)} %relay.11.refs_1_.refs_12_.refs_0_, bf16[128,768]{1,0:T(8,128)(2,1)S(1)} %get-tuple-element.66.refs_1_.refs_13_.refs_3_, bf16[128,768]{1,0:T(8,128)(2,1)S(1)} %collective-permute-done.12.refs_2_.refs_5_, ...), custom_call_target="tpu_custom_call" | custom-call | flops 1107296 | bytes 5490 | tf_op jit(solution)/shard_map/attend_partner/pallas_call | solution.py:76
  40.8 2.9 %collective-permute-start.20 = (bf16[144,768]{1,0:T(8,128)(2,1)S(1)}, bf16[144,768]{1,0:T(8,128)(2,1)S(1)}, u32[]{:S(2)}, u32[]{:S(2)}) collective-permute-start(bf16[144,768]{1,0:T(8,128)(2,1)S(1)} %attend_partner.3.refs_15_), channel_id=1, source_target_pairs={{0,16},{4,20},{8,24},{12,28},{16,0},{20,4},{24,8},{28,12},{1,17},{... | collective-permute-start | bytes 663560 | tf_op jit(solution)/shard_map/ppermute | solution.py:32
  43.7 1.1 %fresh_kv.3 = (bf16[256,256]{1,0:T(8,128)(2,1)S(1)}, bf16[256,256]{1,0:T(8,128)(2,1)S(1)}) custom-call(bf16[128,768]{1,0:T(8,128)(2,1)S(1)} %relay.10.refs_12_.refs_0_, bf16[128,768]{1,0:T(8,128)(2,1)S(1)} %relay.11.refs_1_.refs_12_.refs_0_, bf16[128,768]{1,0:T(8,128)(2,1)S(1)} %get-tuple-element.62.refs_1_.refs_13_.refs_2_, ...), custom_call_target="tpu_custom_call" | custom-call | flops 402653 | bytes 2758 | tf_op jit(solution)/shard_map/fresh_kv/pallas_call | solution.py:76
  44.8 2.3 %attend_fresh.1 = (f32[256,768]{1,0:T(8,128)S(1)}, f32[8,256]{1,0:T(8,128)S(1)}) custom-call(bf16[128,768]{1,0:T(8,128)(2,1)S(1)} %get-tuple-element.59.refs_11_.refs_0_, bf16[128,768]{1,0:T(8,128)(2,1)S(1)} %get-tuple-element.65.refs_1_.refs_12_, bf16[256,256]{1,0:T(8,128)(2,1)S(1)} %get-tuple-element.61.refs_1_.refs_2_.refs_0_, ...), custom_call_target="tpu_custom_call" | custom-call | flops 201326 | bytes 856 | tf_op jit(solution)/shard_map/attend_fresh/pallas_call | solution.py:76
  47.1 0.8 %combine.2 = (bf16[128,768]{1,0:T(8,128)(2,1)S(1)}, bf16[128,384]{1,0:T(8,128)(2,1)S(1)}, bf16[128,384]{1,0:T(8,128)(2,1)S(1)}) custom-call(f32[128,768]{1,0:T(8,128)S(1)} %get-tuple-element.57.refs_0_, f32[8,128]{1,0:T(8,128)S(1)} %get-tuple-element.58.refs_1_, f32[256,768]{1,0:T(8,128)S(1)} %get-tuple-element.72.refs_2_, ...), custom_call_target="tpu_custom_call" | custom-call | flops 150994 | bytes 3262 | tf_op jit(solution)/shard_map/combine/pallas_call | solution.py:76
  48.0 0.1 collective-permute-start.17
  48.1 0.5 collective-permute-start.18
  48.6 0.7 %project.2 = (bf16[128,768]{1,0:T(8,128)(2,1)S(1)}, bf16[128,768]{1,0:T(8,128)(2,1)S(1)}, bf16[128,768]{1,0:T(8,128)(2,1)S(1)}) custom-call(bf16[128,768]{1,0:T(8,128)(2,1)S(1)} %get-tuple-element.74.refs_0_, bf16[768,3072]{1,0:T(8,128)(2,1)S(1)} %bitcast.4), custom_call_target="tpu_custom_call" | custom-call | flops 301989 | bytes 2752 | tf_op jit(solution)/shard_map/project/pallas_call | solution.py:76
  49.2 0.1 collective-permute-done.17.refs_1_
  49.3 0.2 collective-permute-done.18.refs_2_
  49.6 1.0 %collective-permute-start.19 = (bf16[128,768]{1,0:T(8,128)(2,1)S(1)}, bf16[128,768]{1,0:T(8,128)(2,1)S(1)}, u32[]{:S(2)}, u32[]{:S(2)}) collective-permute-start(bf16[128,768]{1,0:T(8,128)(2,1)S(1)} %sum_cores.2.refs_6_), channel_id=1, source_target_pairs={{0,2},{1,3},{2,0},{3,1},{4,6},{5,7},{6,4},{7,5},{8,10},{9,11},{10,... | collective-permute-start | bytes 589832 | tf_op jit(solution)/shard_map/ppermute | solution.py:32
  50.6 3.6 %collective-permute-done.20.refs_4_ = bf16[144,768]{1,0:T(8,128)(2,1)S(1)} collective-permute-done((bf16[144,768]{1,0:T(8,128)(2,1)S(1)}, bf16[144,768]{1,0:T(8,128)(2,1)S(1)}, u32[]{:S(2)}, u32[]{:S(2)}) %collective-permute-start.20) | collective-permute-done | bytes 221216 | tf_op jit(solution)/shard_map/ppermute | solution.py:32
  54.2 0.8 %combine.3 = (bf16[128,768]{1,0:T(8,128)(2,1)S(1)}, bf16[128,384]{1,0:T(8,128)(2,1)S(1)}, bf16[128,384]{1,0:T(8,128)(2,1)S(1)}) custom-call(f32[128,768]{1,0:T(8,128)S(1)} %get-tuple-element.80.refs_0_, f32[8,128]{1,0:T(8,128)S(1)} %get-tuple-element.81.refs_1_, f32[256,768]{1,0:T(8,128)S(1)} %get-tuple-element.72.refs_2_, ...), custom_call_target="tpu_custom_call" | custom-call | flops 150994 | bytes 3262 | tf_op jit(solution)/shard_map/combine/pallas_call | solution.py:76
  55.0 0.1 collective-permute-start.22
  55.1 0.5 collective-permute-start.23
  55.6 0.1 collective-permute-start.16
  55.7 0.7 %project.3 = (bf16[128,768]{1,0:T(8,128)(2,1)S(1)}, bf16[128,768]{1,0:T(8,128)(2,1)S(1)}, bf16[128,768]{1,0:T(8,128)(2,1)S(1)}) custom-call(bf16[128,768]{1,0:T(8,128)(2,1)S(1)} %get-tuple-element.82.refs_0_, bf16[768,3072]{1,0:T(8,128)(2,1)S(1)} %bitcast.4), custom_call_target="tpu_custom_call" | custom-call | flops 301989 | bytes 2752 | tf_op jit(solution)/shard_map/project/pallas_call | solution.py:76
  56.4 0.5 collective-permute-start.21
  57.0 1.1 %collective-permute-start.24 = (bf16[128,768]{1,0:T(8,128)(2,1)S(1)}, bf16[128,768]{1,0:T(8,128)(2,1)S(1)}, u32[]{:S(2)}, u32[]{:S(2)}) collective-permute-start(bf16[128,768]{1,0:T(8,128)(2,1)S(1)} %sum_cores.3.refs_7_), channel_id=1, source_target_pairs={{0,2},{1,3},{2,0},{3,1},{4,6},{5,7},{6,4},{7,5},{8,10},{9,11},{10,... | collective-permute-start | bytes 589832 | tf_op jit(solution)/shard_map/ppermute | solution.py:32
  58.1 2.2 %update_caches.1 = (bf16[2048,256]{1,0:T(8,128)(2,1)}, bf16[2048,256]{1,0:T(8,128)(2,1)}, f32[8,128]{1,0:T(8,128)S(1)}) custom-call(bf16[256,256]{1,0:T(8,128)(2,1)S(1)} %get-tuple-element.61.refs_1_.refs_2_.refs_0_, bf16[256,256]{1,0:T(8,128)(2,1)S(1)} %get-tuple-element.69.refs_3_.refs_1_, bf16[256,256]{1,0:T(8,128)(2,1)S(1)} %get-tuple-element.70.refs_4_.refs_2_, ...), custom_call_target="tpu_custom_call" | custom-call | flops 67108 | bytes 2361 | tf_op jit(solution)/shard_map/update_caches/pallas_call | solution.py:76
  60.3 3.6 %collective-permute-done.24.refs_5_ = bf16[128,768]{1,0:T(8,128)(2,1)S(1)} collective-permute-done((bf16[128,768]{1,0:T(8,128)(2,1)S(1)}, bf16[128,768]{1,0:T(8,128)(2,1)S(1)}, u32[]{:S(2)}, u32[]{:S(2)}) %collective-permute-start.24) | collective-permute-done | bytes 196640 | tf_op jit(solution)/shard_map/ppermute | solution.py:32
  63.9 0.9 %finish.1 = bf16[256,768]{1,0:T(8,128)(2,1)} custom-call(bf16[128,768]{1,0:T(8,128)(2,1)S(1)} %get-tuple-element.75.refs_0_, bf16[128,768]{1,0:T(8,128)(2,1)S(1)} %collective-permute-done.16.refs_1_, bf16[128,768]{1,0:T(8,128)(2,1)S(1)} %collective-permute-done.19.refs_4_.refs_2_, bf16[128,768]{1,0:T(8,128)(2,1)S(1)} %get-tuple-element.83.refs_3_, ...), custom_call_target="tpu_custom_call" | custom-call | flops 98 | bytes 786 | tf_op jit(solution)/shard_map/finish/pallas_call | solution.py:76
  (53 shorter events, 0.5 us)
Async XLA Ops:
  0.6 12.4 %collective-permute-start = (bf16[256,768]{1,0:T(8,128)(2,1)}, bf16[256,768]{1,0:T(8,128)(2,1)S(1)}, u32[]{:S(2)}, u32[]{:S(2)}) collective-permute-start(bf16[256,768]{1,0:T(8,128)(2,1)} %refs_0_.3), channel_id=1, source_target_pairs={{0,2},{1,3},{2,0},{3,1},{4,6},{5,7},{6,4},{7,5},{8,10},{9,11},{10,... | collective-permute-start | bytes 1179656 | tf_op jit(solution)/shard_map/ppermute | solution.py:32
  3.7 14.1 %collective-permute-start.1 = (bf16[256,768]{1,0:T(8,128)(2,1)}, bf16[256,768]{1,0:T(8,128)(2,1)S(1)}, u32[]{:S(2)}, u32[]{:S(2)}) collective-permute-start(bf16[256,768]{1,0:T(8,128)(2,1)} %refs_0_.3), channel_id=1, source_target_pairs={{0,1},{1,0},{2,3},{3,2},{4,5},{5,4},{6,7},{7,6},{8,9},{9,8},{10,11... | collective-permute-start | bytes 1179656 | tf_op jit(solution)/shard_map/ppermute | solution.py:37
  3.7 1.0 %copy-start.5 = (bf16[256,768]{1,0:T(8,128)(2,1)S(1)}, bf16[256,768]{1,0:T(8,128)(2,1)}, u32[]{:S(2)}) copy-start(bf16[256,768]{1,0:T(8,128)(2,1)} %refs_0_.3) | copy-start | bytes 1179652
  4.7 2.7 %copy-start.6 = (s32[4]{0:T(128)S(1)}, s32[4]{0:T(128)}, u32[]{:S(2)}) copy-start(s32[4]{0:T(128)} %refs_6_.7) | copy-start | bytes 52
  4.8 2.7 %copy-start.7 = (s32[4]{0:T(128)S(1)}, s32[4]{0:T(128)}, u32[]{:S(2)}) copy-start(s32[4]{0:T(128)} %refs_1_.4) | copy-start | bytes 52
  4.8 4.3 %copy-start.2 = (bf16[2048,256]{1,0:T(8,128)(2,1)S(1)}, bf16[2048,256]{1,0:T(8,128)(2,1)}, u32[]{:S(2)}) copy-start(bf16[2048,256]{1,0:T(8,128)(2,1)} %refs_4_.1) | copy-start | bytes 3145732
  4.8 4.3 %copy-start.3 = (bf16[2048,256]{1,0:T(8,128)(2,1)S(1)}, bf16[2048,256]{1,0:T(8,128)(2,1)}, u32[]{:S(2)}) copy-start(bf16[2048,256]{1,0:T(8,128)(2,1)} %refs_5_.5) | copy-start | bytes 3145732
  4.8 12.5 %collective-permute-start.4 = (bf16[128,768]{1,0:T(8,128)(2,1)S(1)}, bf16[128,768]{1,0:T(8,128)(2,1)S(1)}, u32[]{:S(2)}, u32[]{:S(2)}) collective-permute-start(bf16[128,768]{1,0:T(8,128)(2,1)S(1)} %get-tuple-element.56), channel_id=1, source_target_pairs={{0,16},{4,20},{8,24},{12,28},{16,0},{20,4},{24,8},{28,12},{1,17},{... | collective-permute-start | bytes 589832 | tf_op jit(solution)/shard_map/ppermute | solution.py:32
  7.4 11.8 %slice-start = ((s8[4718592]{0:T(1024)(128)(4,1)}), s8[4194304]{0:T(1024)(128)(4,1)S(1)}, s32[]{:S(2)}) async-start(s8[4718592]{0:T(1024)(128)(4,1)} %bitcast.1), calls=%async_computation | async-start | bytes 8388608
  7.5 11.7 %slice-start.1 = ((s8[4718592]{0:T(1024)(128)(4,1)}), s8[524288]{0:T(1024)(128)(4,1)S(1)}, s32[]{:S(2)}) async-start(s8[4718592]{0:T(1024)(128)(4,1)} %bitcast.1), calls=%async_computation.1 | async-start | bytes 1048576
  13.0 6.3 %copy-start.4 = (f32[3072]{0:T(1024)S(1)}, f32[3072]{0:T(1024)}, u32[]{:S(2)}) copy-start(f32[3072]{0:T(1024)} %param.11) | copy-start | bytes 36868
  13.1 9.8 %collective-permute-start.5 = (bf16[128,768]{1,0:T(8,128)(2,1)S(1)}, bf16[128,768]{1,0:T(8,128)(2,1)S(1)}, u32[]{:S(2)}, u32[]{:S(2)}) collective-permute-start(bf16[128,768]{1,0:T(8,128)(2,1)S(1)} %get-tuple-element.60), channel_id=1, source_target_pairs={{0,1},{1,0},{2,3},{3,2},{4,5},{5,4},{6,7},{7,6},{8,9},{9,8},{10,11... | collective-permute-start | bytes 589832 | tf_op jit(solution)/shard_map/ppermute | solution.py:37
  13.1 12.6 %collective-permute-start.7 = (bf16[128,768]{1,0:T(8,128)(2,1)S(1)}, bf16[128,768]{1,0:T(8,128)(2,1)S(1)}, u32[]{:S(2)}, u32[]{:S(2)}) collective-permute-start(bf16[128,768]{1,0:T(8,128)(2,1)S(1)} %relay.8.refs_1_), channel_id=1, source_target_pairs={{0,16},{4,20},{8,24},{12,28},{16,0},{20,4},{24,8},{28,12},{1,17},{... | collective-permute-start | bytes 589832 | tf_op jit(solution)/shard_map/ppermute | solution.py:32
  17.3 8.5 %collective-permute-start.6 = (bf16[128,768]{1,0:T(8,128)(2,1)S(1)}, bf16[128,768]{1,0:T(8,128)(2,1)S(1)}, u32[]{:S(2)}, u32[]{:S(2)}) collective-permute-start(bf16[128,768]{1,0:T(8,128)(2,1)S(1)} %relay.10.refs_12_.refs_0_), channel_id=1, source_target_pairs={{0,2},{1,3},{2,0},{3,1},{4,6},{5,7},{6,4},{7,5},{8,10},{9,11},{10,... | collective-permute-start | bytes 589832 | tf_op jit(solution)/shard_map/ppermute | solution.py:32
  17.8 1.3 %collective-permute-start.2 = (bf16[64,768]{1,0:T(8,128)(2,1)S(1)}, bf16[64,768]{1,0:T(8,128)(2,1)S(1)}, u32[]{:S(2)}, u32[]{:S(2)}) collective-permute-start(bf16[64,768]{1,0:T(8,128)(2,1)S(1)} %get-tuple-element.52), channel_id=1, source_target_pairs={{0,1},{1,0},{2,3},{3,2},{4,5},{5,4},{6,7},{7,6},{8,9},{9,8},{10,11... | collective-permute-start | bytes 294920 | tf_op jit(solution)/shard_map/ppermute | solution.py:37
  17.8 1.5 %collective-permute-start.3 = (bf16[64,768]{1,0:T(8,128)(2,1)S(1)}, bf16[64,768]{1,0:T(8,128)(2,1)S(1)}, u32[]{:S(2)}, u32[]{:S(2)}) collective-permute-start(bf16[64,768]{1,0:T(8,128)(2,1)S(1)} %get-tuple-element.53), channel_id=1, source_target_pairs={{0,1},{1,0},{2,3},{3,2},{4,5},{5,4},{6,7},{7,6},{8,9},{9,8},{10,11... | collective-permute-start | bytes 294920 | tf_op jit(solution)/shard_map/ppermute | solution.py:37
  19.1 8.9 %collective-permute-start.8 = (bf16[128,768]{1,0:T(8,128)(2,1)S(1)}, bf16[128,768]{1,0:T(8,128)(2,1)S(1)}, u32[]{:S(2)}, u32[]{:S(2)}) collective-permute-start(bf16[128,768]{1,0:T(8,128)(2,1)S(1)} %relay.10.refs_12_.refs_0_), channel_id=1, source_target_pairs={{0,1},{1,0},{2,3},{3,2},{4,5},{5,4},{6,7},{7,6},{8,9},{9,8},{10,11... | collective-permute-start | bytes 589832 | tf_op jit(solution)/shard_map/ppermute | solution.py:37
  19.3 3.6 %copy-start = (bf16[3072,256]{1,0:T(8,128)(2,1)S(1)}, bf16[3072,256]{1,0:T(8,128)(2,1)}, u32[]{:S(2)}) copy-start(bf16[3072,256]{1,0:T(8,128)(2,1)} %refs_11_.1) | copy-start | bytes 4718596
  19.3 3.6 %copy-start.1 = (bf16[3072,256]{1,0:T(8,128)(2,1)S(1)}, bf16[3072,256]{1,0:T(8,128)(2,1)}, u32[]{:S(2)}) copy-start(bf16[3072,256]{1,0:T(8,128)(2,1)} %refs_12_.1) | copy-start | bytes 4718596
  25.8 2.2 %collective-permute-start.9 = (bf16[64,768]{1,0:T(8,128)(2,1)S(1)}, bf16[64,768]{1,0:T(8,128)(2,1)S(1)}, u32[]{:S(2)}, u32[]{:S(2)}) collective-permute-start(bf16[64,768]{1,0:T(8,128)(2,1)S(1)} %get-tuple-element.63), channel_id=1, source_target_pairs={{0,1},{1,0},{2,3},{3,2},{4,5},{5,4},{6,7},{7,6},{8,9},{9,8},{10,11... | collective-permute-start | bytes 294920 | tf_op jit(solution)/shard_map/ppermute | solution.py:37
  25.9 2.1 %collective-permute-start.10 = (bf16[64,768]{1,0:T(8,128)(2,1)S(1)}, bf16[64,768]{1,0:T(8,128)(2,1)S(1)}, u32[]{:S(2)}, u32[]{:S(2)}) collective-permute-start(bf16[64,768]{1,0:T(8,128)(2,1)S(1)} %get-tuple-element.64), channel_id=1, source_target_pairs={{0,1},{1,0},{2,3},{3,2},{4,5},{5,4},{6,7},{7,6},{8,9},{9,8},{10,11... | collective-permute-start | bytes 294920 | tf_op jit(solution)/shard_map/ppermute | solution.py:37
  26.4 9.0 %collective-permute-start.11 = (bf16[128,768]{1,0:T(8,128)(2,1)S(1)}, bf16[128,768]{1,0:T(8,128)(2,1)S(1)}, u32[]{:S(2)}, u32[]{:S(2)}) collective-permute-start(bf16[128,768]{1,0:T(8,128)(2,1)S(1)} %relay.11.refs_1_.refs_12_.refs_0_), channel_id=1, source_target_pairs={{0,2},{1,3},{2,0},{3,1},{4,6},{5,7},{6,4},{7,5},{8,10},{9,11},{10,... | collective-permute-start | bytes 589832 | tf_op jit(solution)/shard_map/ppermute | solution.py:32
  31.5 15.6 %collective-permute-start.15 = (bf16[144,768]{1,0:T(8,128)(2,1)S(1)}, bf16[144,768]{1,0:T(8,128)(2,1)S(1)}, u32[]{:S(2)}, u32[]{:S(2)}) collective-permute-start(bf16[144,768]{1,0:T(8,128)(2,1)S(1)} %attend_partner.2.refs_13_), channel_id=1, source_target_pairs={{0,16},{4,20},{8,24},{12,28},{16,0},{20,4},{24,8},{28,12},{1,17},{... | collective-permute-start | bytes 663560 | tf_op jit(solution)/shard_map/ppermute | solution.py:32
  31.6 4.5 %collective-permute-start.12 = (bf16[128,768]{1,0:T(8,128)(2,1)S(1)}, bf16[128,768]{1,0:T(8,128)(2,1)S(1)}, u32[]{:S(2)}, u32[]{:S(2)}) collective-permute-start(bf16[128,768]{1,0:T(8,128)(2,1)S(1)} %relay.11.refs_1_.refs_12_.refs_0_), channel_id=1, source_target_pairs={{0,1},{1,0},{2,3},{3,2},{4,5},{5,4},{6,7},{7,6},{8,9},{9,8},{10,11... | collective-permute-start | bytes 589832 | tf_op jit(solution)/shard_map/ppermute | solution.py:37
  35.4 1.5 %collective-permute-start.13 = (bf16[64,768]{1,0:T(8,128)(2,1)S(1)}, bf16[64,768]{1,0:T(8,128)(2,1)S(1)}, u32[]{:S(2)}, u32[]{:S(2)}) collective-permute-start(bf16[64,768]{1,0:T(8,128)(2,1)S(1)} %get-tuple-element.67), channel_id=1, source_target_pairs={{0,1},{1,0},{2,3},{3,2},{4,5},{5,4},{6,7},{7,6},{8,9},{9,8},{10,11... | collective-permute-start | bytes 294920 | tf_op jit(solution)/shard_map/ppermute | solution.py:37
  36.0 1.3 %collective-permute-start.14 = (bf16[64,768]{1,0:T(8,128)(2,1)S(1)}, bf16[64,768]{1,0:T(8,128)(2,1)S(1)}, u32[]{:S(2)}, u32[]{:S(2)}) collective-permute-start(bf16[64,768]{1,0:T(8,128)(2,1)S(1)} %get-tuple-element.68), channel_id=1, source_target_pairs={{0,1},{1,0},{2,3},{3,2},{4,5},{5,4},{6,7},{7,6},{8,9},{9,8},{10,11... | collective-permute-start | bytes 294920 | tf_op jit(solution)/shard_map/ppermute | solution.py:37
  37.3 9.8 %slice-start.2 = ((s8[4718592]{0:T(1024)(128)(4,1)}), s8[4194304]{0:T(1024)(128)(4,1)S(1)}, s32[]{:S(2)}) async-start(s8[4718592]{0:T(1024)(128)(4,1)} %bitcast.3), calls=%async_computation.2 | async-start | bytes 8388608
  37.3 9.8 %slice-start.3 = ((s8[4718592]{0:T(1024)(128)(4,1)}), s8[524288]{0:T(1024)(128)(4,1)S(1)}, s32[]{:S(2)}) async-start(s8[4718592]{0:T(1024)(128)(4,1)} %bitcast.3), calls=%async_computation.3 | async-start | bytes 1048576
  40.8 13.4 %collective-permute-start.20 = (bf16[144,768]{1,0:T(8,128)(2,1)S(1)}, bf16[144,768]{1,0:T(8,128)(2,1)S(1)}, u32[]{:S(2)}, u32[]{:S(2)}) collective-permute-start(bf16[144,768]{1,0:T(8,128)(2,1)S(1)} %attend_partner.3.refs_15_), channel_id=1, source_target_pairs={{0,16},{4,20},{8,24},{12,28},{16,0},{20,4},{24,8},{28,12},{1,17},{... | collective-permute-start | bytes 663560 | tf_op jit(solution)/shard_map/ppermute | solution.py:32
  48.0 1.4 %collective-permute-start.17 = (bf16[128,384]{1,0:T(8,128)(2,1)S(1)}, bf16[128,384]{1,0:T(8,128)(2,1)S(1)}, u32[]{:S(2)}, u32[]{:S(2)}) collective-permute-start(bf16[128,384]{1,0:T(8,128)(2,1)S(1)} %get-tuple-element.78), channel_id=1, source_target_pairs={{0,1},{1,0},{2,3},{3,2},{4,5},{5,4},{6,7},{7,6},{8,9},{9,8},{10,11... | collective-permute-start | bytes 294920 | tf_op jit(solution)/shard_map/ppermute | solution.py:37
  48.1 1.4 %collective-permute-start.18 = (bf16[128,384]{1,0:T(8,128)(2,1)S(1)}, bf16[128,384]{1,0:T(8,128)(2,1)S(1)}, u32[]{:S(2)}, u32[]{:S(2)}) collective-permute-start(bf16[128,384]{1,0:T(8,128)(2,1)S(1)} %get-tuple-element.79), channel_id=1, source_target_pairs={{0,1},{1,0},{2,3},{3,2},{4,5},{5,4},{6,7},{7,6},{8,9},{9,8},{10,11... | collective-permute-start | bytes 294920 | tf_op jit(solution)/shard_map/ppermute | solution.py:37
  49.6 7.3 %collective-permute-start.19 = (bf16[128,768]{1,0:T(8,128)(2,1)S(1)}, bf16[128,768]{1,0:T(8,128)(2,1)S(1)}, u32[]{:S(2)}, u32[]{:S(2)}) collective-permute-start(bf16[128,768]{1,0:T(8,128)(2,1)S(1)} %sum_cores.2.refs_6_), channel_id=1, source_target_pairs={{0,2},{1,3},{2,0},{3,1},{4,6},{5,7},{6,4},{7,5},{8,10},{9,11},{10,... | collective-permute-start | bytes 589832 | tf_op jit(solution)/shard_map/ppermute | solution.py:32
  55.0 1.8 %collective-permute-start.22 = (bf16[128,384]{1,0:T(8,128)(2,1)S(1)}, bf16[128,384]{1,0:T(8,128)(2,1)S(1)}, u32[]{:S(2)}, u32[]{:S(2)}) collective-permute-start(bf16[128,384]{1,0:T(8,128)(2,1)S(1)} %get-tuple-element.86), channel_id=1, source_target_pairs={{0,1},{1,0},{2,3},{3,2},{4,5},{5,4},{6,7},{7,6},{8,9},{9,8},{10,11... | collective-permute-start | bytes 294920 | tf_op jit(solution)/shard_map/ppermute | solution.py:37
  55.1 1.8 %collective-permute-start.23 = (bf16[128,384]{1,0:T(8,128)(2,1)S(1)}, bf16[128,384]{1,0:T(8,128)(2,1)S(1)}, u32[]{:S(2)}, u32[]{:S(2)}) collective-permute-start(bf16[128,384]{1,0:T(8,128)(2,1)S(1)} %get-tuple-element.87), channel_id=1, source_target_pairs={{0,1},{1,0},{2,3},{3,2},{4,5},{5,4},{6,7},{7,6},{8,9},{9,8},{10,11... | collective-permute-start | bytes 294920 | tf_op jit(solution)/shard_map/ppermute | solution.py:37
  55.6 4.7 %collective-permute-start.16 = (bf16[128,768]{1,0:T(8,128)(2,1)S(1)}, bf16[128,768]{1,0:T(8,128)(2,1)S(1)}, u32[]{:S(2)}, u32[]{:S(2)}) collective-permute-start(bf16[128,768]{1,0:T(8,128)(2,1)S(1)} %get-tuple-element.76.refs_3_), channel_id=1, source_target_pairs={{0,1},{1,0},{2,3},{3,2},{4,5},{5,4},{6,7},{7,6},{8,9},{9,8},{10,11... | collective-permute-start | bytes 589832 | tf_op jit(solution)/shard_map/ppermute | solution.py:37
  56.4 3.9 %collective-permute-start.21 = (bf16[128,768]{1,0:T(8,128)(2,1)S(1)}, bf16[128,768]{1,0:T(8,128)(2,1)S(1)}, u32[]{:S(2)}, u32[]{:S(2)}) collective-permute-start(bf16[128,768]{1,0:T(8,128)(2,1)S(1)} %get-tuple-element.84.refs_3_), channel_id=1, source_target_pairs={{0,1},{1,0},{2,3},{3,2},{4,5},{5,4},{6,7},{7,6},{8,9},{9,8},{10,11... | collective-permute-start | bytes 589832 | tf_op jit(solution)/shard_map/ppermute | solution.py:37
  57.0 6.9 %collective-permute-start.24 = (bf16[128,768]{1,0:T(8,128)(2,1)S(1)}, bf16[128,768]{1,0:T(8,128)(2,1)S(1)}, u32[]{:S(2)}, u32[]{:S(2)}) collective-permute-start(bf16[128,768]{1,0:T(8,128)(2,1)S(1)} %sum_cores.3.refs_7_), channel_id=1, source_target_pairs={{0,2},{1,3},{2,0},{3,1},{4,6},{5,7},{6,4},{7,5},{8,10},{9,11},{10,... | collective-permute-start | bytes 589832 | tf_op jit(solution)/shard_map/ppermute | solution.py:32

commit v11 on v10

--- a/solution.py
+++ b/solution.py
@@ -250,85 +250,126 @@
     return jnp.concatenate(parts, 0) if len(parts) > 1 else parts[0]
 
 
-def attend_kernel(counts, own, row_at, rows, table_at, *refs):
+def head_queries(product, cosine, sine):
+    return [
+        (rotate(product[:, at : at + HD], cosine, sine) * log2_scale).astype(jnp.bfloat16)
+        for at in range(0, product.shape[1], HD)
+    ]
+
+
+def weigh(scores, values):
+    largest = functools.reduce(
+        jnp.maximum, [jnp.max(score, -1, keepdims=True) for score in scores]
+    )
+    summed = 0.0
+    for score, value in zip(scores, values):
+        weights = jnp.exp2(score - largest).astype(jnp.bfloat16)
+        summed = summed + dot(weights, value)
+    denominator = summed[:, HD : HD + 1]
+    return summed[:, :HD] / denominator, largest + jnp.log2(denominator)
+
+
+def attend_heads(queries, wide_keys, wide_values, mark, fresh, store):
+    rows = queries.shape[0]
+    kv_heads = wide_keys.shape[0]
+    repeat = queries.shape[1] // HD // kv_heads
+    marked = mark[: repeat * rows]
+    scores = []
+    values = []
+    for head in range(kv_heads):
+        shared = slice(head * HD, (head + 1) * HD)
+        stacked = jnp.concatenate(
+            [
+                queries[:, (head * repeat + turn) * HD : (head * repeat + turn + 1) * HD]
+                for turn in range(repeat)
+            ],
+            0,
+        )
+        wide = jnp.concatenate([stacked, marked], 1)
+        found = [dot_transposed(wide, wide_keys[head])]
+        held = [wide_values[head]]
+        for keys, new_values, column, bias in fresh:
+            if bias is None:
+                added = jnp.concatenate([keys[:, shared], column], 1)
+                found.append(dot_transposed(wide, added))
+            else:
+                bias = jnp.concatenate([bias] * repeat, 0)
+                found.append(dot_transposed(stacked, keys[:, shared]) + bias)
+            held.append(jnp.concatenate([new_values[:, shared], mark[: keys.shape[0]]], 1))
+        scores.append(found)
+        values.append(held)
+    columns = []
+    for head in range(kv_heads):
+        result, logs = weigh(scores[head], values[head])
+        for turn in range(repeat):
+            part = slice(turn * rows, (turn + 1) * rows)
+            store((head * repeat + turn) * HD, result[part])
+            columns.append(logs[part])
+    return stat_rows(columns, rows)
+
+
+def attend_kernel(counts, groups, requests, turn, row_at, rows, table_at, *refs):
     blocks, refs = split_refs(counts, refs)
-    gain, w_query, cosine, sine, wide_keys, wide_values, mark, *outputs = refs
+    gain, w_query, cosine, sine, wide_keys, wide_values, mark, keys, values, *outputs = refs
     pieces = [rows_of(one, row_at, rows) for one in blocks]
     (product,) = project_normed(pieces, gain, [w_query])
-    cosine = cosine[table_at : table_at + rows]
-    sine = sine[table_at : table_at + rows]
-    kv_heads = wide_keys.shape[0]
-    repeat = product.shape[1] // HD // kv_heads
-    queries = [
-        (rotate(product[:, head * HD : (head + 1) * HD], cosine, sine) * log2_scale).astype(
-            jnp.bfloat16
-        )
-        for head in range(kv_heads * repeat)
-    ]
-    step = min(rows, LANES)
-    mark = mark[: repeat * step]
-    tiles = [(head, at) for head in range(kv_heads) for at in range(0, rows, step)]
-
-    def scores_of(head, at):
-        stacked = jnp.concatenate(
-            [query[at : at + step] for query in queries[head * repeat : (head + 1) * repeat]], 0
-        )
-        return dot_transposed(jnp.concatenate([stacked, mark], 1), wide_keys[head])
-
-    columns = {}
-    following = scores_of(*tiles[0])
-    for index, (head, at) in enumerate(tiles):
-        scores = following
-        if index + 1 < len(tiles):
-            following = scores_of(*tiles[index + 1])
-        largest = jnp.max(scores, -1, keepdims=True)
-        weights = jnp.exp2(scores - largest).astype(jnp.bfloat16)
-        summed = dot(weights, wide_values[head])
-        denominator = summed[:, HD : HD + 1]
-        result = summed[:, :HD] / denominator
-        logs = largest + jnp.log2(denominator)
-        for turn in range(repeat):
-            part = slice(turn * step, (turn + 1) * step)
-            to = slice((head * repeat + turn) * HD, (head * repeat + turn + 1) * HD)
-            outputs[0][at : at + step, to] = result[part].astype(outputs[0].dtype)
-            columns.setdefault(head * repeat + turn, []).append(logs[part])
-    stats = stat_rows([jnp.concatenate(parts, 0) for parts in columns.values()], rows)
-    if own:
+    part = slice(table_at, table_at + rows)
+    queries = jnp.concatenate(head_queries(product, cosine[part], sine[part]), 1)
+    target = outputs[0]
+
+    def store(at, result):
+        target[:rows, at : at + HD] = result.astype(target.dtype)
+
+    if turn:
+        position_in = place_of(requests)[1]
+        hidden = position_in > source_of(position_in, turn, groups)
+        bias = mark[: keys.shape[0]].astype(jnp.float32) * neg_large
+        bias = jnp.where(hidden, bias, 0.0).astype(jnp.bfloat16)
+        fresh = [(keys[...], values[...], bias, None)]
+    else:
+        fresh = []
+        if row_at:
+            fresh.append((keys[:row_at], values[:row_at], jnp.zeros((row_at, LANES), jnp.bfloat16), None))
+        token = lax.broadcasted_iota(jnp.int32, (rows, rows), 0)
+        within = lax.broadcasted_iota(jnp.int32, (rows, rows), 1)
+        causal = jnp.where(within <= token, 0.0, neg_large)
+        own = slice(row_at, row_at + rows)
+        fresh.append((keys[own], values[own], None, causal))
+    stats = attend_heads(queries, wide_keys, wide_values, mark, fresh, store)
+    if not turn:
         outputs[1][...] = stats
-        outputs[2][...] = jnp.concatenate(queries, 1)
         return
-    outputs[0][rows:] = jnp.zeros((ROW_TILE, outputs[0].shape[1]), jnp.bfloat16)
+    target[rows:] = jnp.zeros((ROW_TILE, target.shape[1]), target.dtype)
     rest = jnp.concatenate([stats, jnp.zeros((ROW_TILE - STAT_ROWS, rows), jnp.float32)], 0)
-    for part in range(3):
-        rounded = rest.astype(jnp.bfloat16)
-        outputs[0][rows:, part * rows : (part + 1) * rows] = rounded
+    for index in range(3):
+        rounded = rest.astype(target.dtype)
+        target[rows:, index * rows : (index + 1) * rows] = rounded
         rest = rest - rounded.astype(jnp.float32)
 
 
 def attend(
-    pieces, gain, w_query, tables, wide_keys, wide_values, mark, own, row_at, rows, table_at,
+    pieces, gain, w_query, tables, wides, mark, new_rows, place, turn, row_at, rows, table_at,
     earlier,
 ):
     counts = [len(blocks) for blocks in pieces]
     flat = [block for blocks in pieces for block in blocks]
-    out_width = w_query.shape[1]
-    slots = wide_keys.shape[1]
-    if own:
+    width = w_query.shape[1]
+    slots = wides[0].shape[1]
+    if turn:
+        out_shape = [jax.ShapeDtypeStruct((rows + ROW_TILE, width), jnp.bfloat16)]
+    else:
         out_shape = [
-            jax.ShapeDtypeStruct((rows, out_width), jnp.float32),
+            jax.ShapeDtypeStruct((rows, width), jnp.float32),
             jax.ShapeDtypeStruct((STAT_ROWS, rows), jnp.float32),
-            jax.ShapeDtypeStruct((rows, out_width), jnp.bfloat16),
         ]
-    else:
-        out_shape = [jax.ShapeDtypeStruct((rows + ROW_TILE, out_width), jnp.bfloat16)]
     return call(
-        functools.partial(attend_kernel, counts, own, row_at, rows, table_at),
+        functools.partial(attend_kernel, counts, *place, turn, row_at, rows, table_at),
         out_shape,
-        [*flat, gain, w_query, *tables, wide_keys, wide_values, mark],
+        [*flat, gain, w_query, *tables, *wides, mark, *new_rows],
         28,
-        2 * rows * out_width * (w_query.shape[0] + 4 * slots),
-        rows * out_width // HD * slots,
-        "attend_own" if own else "attend_partner",
+        2 * rows * width * (w_query.shape[0] + 4 * slots),
+        rows * width // HD * slots,
+        "attend_partner" if turn else "attend_own",
         earlier,
     )
 
@@ -378,71 +419,6 @@
     inside = (row >= 0) & (row < rows)
     old = target[window, :].astype(jnp.float32)
     target[window, :] = jnp.where(inside, moved, old).astype(jnp.bfloat16)
-
-
-def attend_fresh_kernel(groups, requests, *refs):
-    query_refs, refs = refs[:CHUNKS], refs[CHUNKS:]
-    key_refs, value_refs, refs = refs[:groups], refs[groups : 2 * groups], refs[2 * groups :]
-    partial, stats = refs
-    position_in = place_of(requests)[1]
-    rows, width = partial.shape
-    kv_heads = key_refs[0].shape[1] // HD
-    repeat = width // HD // kv_heads
-    queries = whole_of(query_refs)
-    token = lax.broadcasted_iota(jnp.int32, (rows, rows), 0)
-    within = lax.broadcasted_iota(jnp.int32, (rows, rows), 1)
-    causal = jnp.where(within <= token, 0.0, neg_large)
-    causal = jnp.concatenate([causal] * repeat, 0)
-    lane = lax.broadcasted_iota(jnp.int32, (rows, LANES), 1)
-    ones = jnp.where(lane == 0, 1.0, 0.0).astype(jnp.bfloat16)
-    hidden = [jnp.zeros((rows, LANES), jnp.bfloat16)]
-    for turn in range(1, groups):
-        later = source_of(position_in, turn, groups) > position_in
-        hidden.append(jnp.where((lane == 0) & later, neg_large, 0.0).astype(jnp.bfloat16))
-    columns = []
-    for head in range(kv_heads):
-        own = [
-            slice((head * repeat + turn) * HD, (head * repeat + turn + 1) * HD)
-            for turn in range(repeat)
-        ]
-        shared = slice(head * HD, (head + 1) * HD)
-        stacked = jnp.concatenate([queries[:, one] for one in own], 0)
-        stacked = jnp.concatenate([stacked, jnp.concatenate([ones] * repeat, 0)], 1)
-        scores = [
-            dot_transposed(stacked, jnp.concatenate([ref[:, shared], bias], 1))
-            for ref, bias in zip(key_refs, hidden)
-        ]
-        scores = jnp.concatenate([scores[0] + causal] + scores[1:], 1)
-        largest = jnp.max(scores, -1, keepdims=True)
-        weights = jnp.exp2(scores - largest).astype(jnp.bfloat16)
-        wide_values = [jnp.concatenate([ref[:, shared], ones], 1) for ref in value_refs]
-        summed = dot(weights, jnp.concatenate(wide_values, 0))
-        denominator = summed[:, HD : HD + 1]
-        result = summed[:, :HD] / denominator
-        logs = largest + jnp.log2(denominator)
-        for turn, one in enumerate(own):
-            part = slice(turn * rows, (turn + 1) * rows)
-            partial[:, one] = result[part]
-            columns.append(logs[part])
-    stats[...] = stat_rows(columns, rows)
-
-
-def attend_fresh(requests, queries, new_keys, new_values):
-    groups = len(new_keys)
-    rows = new_keys[0].shape[0]
-    width = queries[0].shape[1]
-    return call(
-        functools.partial(attend_fresh_kernel, groups, requests),
-        [
-            jax.ShapeDtypeStruct((rows, width), jnp.float32),
-            jax.ShapeDtypeStruct((STAT_ROWS, rows), jnp.float32),
-        ],
-        [*queries, *new_keys, *new_values],
-        24,
-        4 * rows * width * rows * groups,
-        rows * width // HD * rows * groups,
-        "attend_fresh",
-    )
 
 
 def update_kernel(groups, *refs):
@@ -479,18 +455,16 @@
     )
 
 
-def combine_kernel(row_at, own_partial, own_stats, fresh_partial, fresh_stats, *refs):
+def combine_kernel(own_partial, own_stats, *refs):
     heads = lax.axis_size("head")
     chips = heads // CORES
     outputs = 2 * chips - 1
     received = refs[: -1 - outputs]
     w_out, merged_rows = refs[-1 - outputs], refs[-outputs]
     far = refs[1 - outputs :]
-    width = own_partial.shape[1]
-    rows = merged_rows.shape[0]
-    part = slice(row_at, row_at + rows)
+    rows, width = own_partial.shape
     padding = jnp.zeros((LANES - STAT_ROWS, rows), jnp.float32)
-    stats = [own_stats[...], fresh_stats[:, part]]
+    stats = [own_stats[...]]
     for ref in received:
         stats.append(
             sum(
@@ -508,8 +482,7 @@
         own = slice(head * HD, (head + 1) * HD)
         column = slice(head, head + 1)
         merged = own_partial[:, own] * shares[0][:, column]
-        merged = merged + fresh_partial[part, own] * shares[1][:, column]
-        for ref, share in zip(received, shares[2:]):
+        for ref, share in zip(received, shares[1:]):
             merged = merged + ref[:rows, own].astype(jnp.float32) * share[:, column]
         attended.append(merged.astype(jnp.bfloat16))
     attended = jnp.concatenate(attended, 1)
@@ -536,15 +509,16 @@
         target[...] = block_product(attended, w_out, ahead, 0)
 
 
-def combine(row_at, rows, own, fresh_part, received, w_out, heads, earlier):
+def combine(own, received, w_out, heads, earlier):
     chips = heads // CORES
+    rows = own[0].shape[0]
     width = w_out.shape[1] // heads
     merged = jax.ShapeDtypeStruct((rows, own[0].shape[1]), jnp.bfloat16)
     half = jax.ShapeDtypeStruct((rows, width // 2), jnp.bfloat16)
     merged, *far = call(
-        functools.partial(combine_kernel, row_at),
+        combine_kernel,
         [merged] + [half] * (2 * chips - 2),
-        [*own, *fresh_part, *received, w_out],
+        [*own, *received, w_out],
         20,
         rows * w_out.size,
         0,
@@ -629,11 +603,11 @@
     tables = rope_tables(cached_lengths, rope_offsets, groups, rows, [mark])
     wide_keys, wide_values = widen(keys_cache, values_cache, mark, cached_lengths, tables[:1])
 
-    def attend_rows(pieces, own, chunk, turn, earlier):
+    def attend_rows(pieces, turn, chunk, earlier):
         at = chunk * chunk_rows
         return attend(
-            pieces, gain, w_query, tables, wide_keys, wide_values, mark, own, at if own else 0,
-            chunk_rows, turn * rows + at, earlier,
+            pieces, gain, w_query, tables, [wide_keys, wide_values], mark, new_rows[0],
+            (groups, requests), turn, 0 if turn else at, chunk_rows, turn * rows + at, earlier,
         )
 
     half = chunk_rows // 2
@@ -652,10 +626,9 @@
     earlier = [cut[0] for cut in own_cuts]
     first = [relay([piece], [chunk_rows], earlier)[0] for piece in first]
     first_from_chips = [other_chips(piece) for piece in first]
-    *own_part, queries = attend_rows(own_early, True, 0, 0, first)
-    own_queries = [queries]
-    new_rows = [fresh(own_pieces, gain, w_key, w_value, tables, 0, [queries])]
-    earlier = [new_rows[0][0]]
+    new_rows = [fresh(own_pieces, gain, w_key, w_value, tables, 0, first)]
+    own_part = attend_rows(own_early, 0, 0, [new_rows[0][0]])
+    earlier = own_part[:1]
     second = [relay([piece], [rows - chunk_rows], earlier)[0] for piece in second]
     second_from_chips = [other_chips(piece) for piece in second]
     earlier = second
@@ -674,34 +647,23 @@
         earlier = earlier + passed
     received = [[] for _ in range(CHUNKS)]
     for turn in range(1, groups):
-        (packed,) = attend_rows(gathered[turn - 1][0], False, 0, turn, earlier)
+        (packed,) = attend_rows(gathered[turn - 1][0], turn, 0, earlier)
         received[0].append(shifted(packed, "seq", -turn * requests))
         earlier = [packed]
-    *late_part, queries = attend_rows(own_pieces, True, 1, 0, earlier)
-    own_part += late_part
-    own_queries.append(queries)
-    earlier = [queries]
     for blocks, piece, from_chips in zip(gathered, second, second_from_chips):
         along, passed = gather_cores(piece, from_chips, earlier)
         blocks.append(along)
         earlier = earlier + passed
     for turn in range(1, groups):
-        (packed,) = attend_rows(gathered[turn - 1][1], False, 1, turn, earlier)
+        (packed,) = attend_rows(gathered[turn - 1][1], turn, 1, earlier)
         received[1].append(shifted(packed, "seq", -turn * requests))
         earlier = [packed]
-    for turn in range(1, groups):
-        pieces = [sum(blocks, []) for blocks in zip(*gathered[turn - 1])]
-        new_rows.append(fresh(pieces, gain, w_key, w_value, tables, turn * rows, earlier))
-    new_keys, new_values = zip(*new_rows)
-    fresh_part = attend_fresh(requests, own_queries, new_keys, new_values)
+    own_part = [own_part, attend_rows(own_pieces, 0, 1, earlier)]
 
     parts = []
-    earlier = before_sums = []
+    earlier, before_sums = own_part[1][:1], []
     for chunk in range(CHUNKS):
-        merged, fars = combine(
-            chunk * chunk_rows, chunk_rows, own_part[2 * chunk : 2 * chunk + 2], fresh_part,
-            received[chunk], w_out, heads, earlier,
-        )
+        merged, fars = combine(own_part[chunk], received[chunk], w_out, heads, earlier)
         fars = [[other_core(part) for part in far] for far in fars]
         far, near = project(merged, w_out, heads)
         earlier = [far] + before_sums
@@ -709,6 +671,11 @@
         from_chips = [shifted(one, "head", CORES * k) for k, one in enumerate(sums, 1)]
         parts += [near[0], other_core(far), *from_chips]
         earlier, before_sums = sums, from_chips
+    for turn in range(1, groups):
+        pieces = [sum(blocks, []) for blocks in zip(*gathered[turn - 1])]
+        new_rows.append(fresh(pieces, gain, w_key, w_value, tables, turn * rows, earlier))
+        earlier = [new_rows[-1][0]]
+    new_keys, new_values = zip(*new_rows)
     keys_updated, values_updated, done = update(
         cached_lengths, new_keys, new_values, keys_cache, values_cache, earlier
     )

time: 64.9 us -> 68.4 us (1.054)
  waiting for transfers between devices: 15.6 us -> 21.9 us
  Pallas kernels: 27.7 us -> 26.2 us
  starting transfers between devices: 19.4 us -> 18.2 us
    ppermute x9, waiting for transfers between devices: 13.3 us -> 18.8 us  [shifted(): lax.ppermute(shard, axis, [(i, (i + by) % devices) for i in range(devices)])]
    pallas_call x25 -> x24, Pallas kernels: 27.7 us -> 26.2 us  [call(): pl.pallas_call(body, out_shape=out_shape, in_specs=[VMEM] * len(arrays) +...]
    ppermute x9, starting transfers between devices: 15.7 us -> 14.6 us  [shifted(): lax.ppermute(shard, axis, [(i, (i + by) % devices) for i in range(devices)])]
    ppermute x16, waiting for transfers between devices: 2.29 us -> 3.07 us  [other_core(): return lax.ppermute(shard, 'head', [(i, i ^ 1) for i in range(devices)])]
  transfers between devices with their start and end apart: 25 -> 25, of which waited for: 10 -> 14; matrix products, arithmetic and copies ran while one was open for 0% -> 0% of each run, Pallas kernels for 41% -> 37%
where the time goes in v11:
time: 68.4 us; the launch traced here: 68.3 us
  Pallas kernels  26.2 us (38%)
  waiting for transfers between devices  21.9 us (32%)
  starting transfers between devices  18.2 us (27%)
  local copies, waits for them, and re-layouts  1.08 us (2%)
  between operations  0.94 us (1%)
    pallas_call x24, Pallas kernels, call(): pl.pallas_call(body, out_shape=out_shape, in_specs=[VMEM] * len(arrays) +...  26.2 us
    ppermute x9, waiting for transfers between devices, shifted(): lax.ppermute(shard, axis, [(i, (i + by) % devices) for i in range(devices)])  18.8 us
    ppermute x9, starting transfers between devices, shifted(): lax.ppermute(shard, axis, [(i, (i + by) % devices) for i in range(devices)])  14.6 us
    ppermute x16, starting transfers between devices, other_core(): return lax.ppermute(shard, 'head', [(i, i ^ 1) for i in range(devices)])  3.67 us
    ppermute x16, waiting for transfers between devices, other_core(): return lax.ppermute(shard, 'head', [(i, i ^ 1) for i in range(devices)])  3.07 us
  transfers between devices with their start and end apart: 25, of which 14 were waited for; matrix products, arithmetic and copies ran while one was open for 0% of the time, Pallas kernels for 37%

profile of v11, /device:TPU:0, one launch (start us, length us, event | category | flops | bytes accessed | tf_op | source)
XLA Modules:
  0.0 68.3 jit_solution(11680147912576665984)
XLA Ops:
  0.6 3.0 %collective-permute-start = (bf16[256,768]{1,0:T(8,128)(2,1)}, bf16[256,768]{1,0:T(8,128)(2,1)S(1)}, u32[]{:S(2)}, u32[]{:S(2)}) collective-permute-start(bf16[256,768]{1,0:T(8,128)(2,1)} %refs_0_.3), channel_id=1, source_target_pairs={{0,2},{1,3},{2,0},{3,1},{4,6},{5,7},{6,4},{7,5},{8,10},{9,11},{10,... | collective-permute-start | bytes 1179656 | tf_op jit(solution)/shard_map/ppermute | solution.py:32
  3.7 1.0 %copy-done.5 = bf16[256,768]{1,0:T(8,128)(2,1)S(1)} copy-done((bf16[256,768]{1,0:T(8,128)(2,1)S(1)}, bf16[256,768]{1,0:T(8,128)(2,1)}, u32[]{:S(2)}) %copy-start.5) | copy-done | bytes 393240
  4.8 2.7 %collective-permute-start.5 = (bf16[128,768]{1,0:T(8,128)(2,1)S(1)}, bf16[128,768]{1,0:T(8,128)(2,1)S(1)}, u32[]{:S(2)}, u32[]{:S(2)}) collective-permute-start(bf16[128,768]{1,0:T(8,128)(2,1)S(1)} %get-tuple-element.53), channel_id=1, source_target_pairs={{0,16},{4,20},{8,24},{12,28},{16,0},{20,4},{24,8},{28,12},{1,17},{... | collective-permute-start | bytes 589832 | tf_op jit(solution)/shard_map/ppermute | solution.py:32
  7.5 1.6 %rope_tables.1 = (f32[512,128]{1,0:T(8,128)S(1)}, f32[512,128]{1,0:T(8,128)S(1)}) custom-call(s32[4]{0:T(128)S(1)} %copy-done.6, s32[4]{0:T(128)S(1)} %copy-done.7, bf16[2048,128]{1,0:T(8,128)(2,1)S(1)} %marks.1.refs_2_.refs_11_.refs_12_), custom_call_target="tpu_custom_call" | custom-call | bytes 262 | tf_op jit(solution)/shard_map/rope_tables/pallas_call | solution.py:76
  9.1 0.8 %widen_caches.1 = (bf16[2,2048,256]{2,1,0:T(8,128)(2,1)S(1)}, bf16[2,2048,256]{2,1,0:T(8,128)(2,1)S(1)}) custom-call(bf16[2048,256]{1,0:T(8,128)(2,1)S(1)} %copy-done.2, bf16[2048,256]{1,0:T(8,128)(2,1)S(1)} %copy-done.3, bf16[2048,128]{1,0:T(8,128)(2,1)S(1)} %marks.1.refs_2_.refs_11_.refs_12_, s32[4]{0:T(128)S(1)} %copy-done.6, ...), custom_call_target="tpu_custom_call" | custom-call | bytes 3407 | tf_op jit(solution)/shard_map/widen_caches/pallas_call | solution.py:76
  9.9 3.1 %collective-permute-done.refs_1_.refs_0_ = bf16[256,768]{1,0:T(8,128)(2,1)S(1)} collective-permute-done((bf16[256,768]{1,0:T(8,128)(2,1)}, bf16[256,768]{1,0:T(8,128)(2,1)S(1)}, u32[]{:S(2)}, u32[]{:S(2)}) %collective-permute-start) | collective-permute-done | bytes 393248 | tf_op jit(solution)/shard_map/ppermute | solution.py:32
  13.2 2.9 %collective-permute-start.7 = (bf16[128,768]{1,0:T(8,128)(2,1)S(1)}, bf16[128,768]{1,0:T(8,128)(2,1)S(1)}, u32[]{:S(2)}, u32[]{:S(2)}) collective-permute-start(bf16[128,768]{1,0:T(8,128)(2,1)S(1)} %relay.8.refs_1_), channel_id=1, source_target_pairs={{0,16},{4,20},{8,24},{12,28},{16,0},{20,4},{24,8},{28,12},{1,17},{... | collective-permute-start | bytes 589832 | tf_op jit(solution)/shard_map/ppermute | solution.py:32
  16.0 1.2 %collective-permute-done.5.refs_0_ = bf16[128,768]{1,0:T(8,128)(2,1)S(1)} collective-permute-done((bf16[128,768]{1,0:T(8,128)(2,1)S(1)}, bf16[128,768]{1,0:T(8,128)(2,1)S(1)}, u32[]{:S(2)}, u32[]{:S(2)}) %collective-permute-start.5) | collective-permute-done | bytes 196640 | tf_op jit(solution)/shard_map/ppermute | solution.py:32
  17.3 0.5 collective-permute-start.6
  17.8 0.5 collective-permute-start.3
  18.3 0.8 %collective-permute-done.2.refs_3_ = bf16[64,768]{1,0:T(8,128)(2,1)S(1)} collective-permute-done((bf16[64,768]{1,0:T(8,128)(2,1)S(1)}, bf16[64,768]{1,0:T(8,128)(2,1)S(1)}, u32[]{:S(2)}, u32[]{:S(2)}) %collective-permute-start.2) | collective-permute-done | bytes 98336 | tf_op jit(solution)/shard_map/ppermute | solution.py:37
  19.1 0.2 collective-permute-start.8
  19.3 1.1 %fresh_kv.2 = (bf16[256,256]{1,0:T(8,128)(2,1)S(1)}, bf16[256,256]{1,0:T(8,128)(2,1)S(1)}) custom-call(bf16[256,768]{1,0:T(8,128)(2,1)S(1)} %get-tuple-element.43.refs_0_, bf16[256,768]{1,0:T(8,128)(2,1)S(1)} %get-tuple-element.47.refs_1_, bf16[256,768]{1,0:T(8,128)(2,1)S(1)} %collective-permute-done.1.refs_2_, ...), custom_call_target="tpu_custom_call" | custom-call | flops 402653 | bytes 2758 | tf_op jit(solution)/shard_map/fresh_kv/pallas_call | solution.py:76
  20.5 3.8 %attend_own.2 = (f32[128,768]{1,0:T(8,128)S(1)}, f32[8,128]{1,0:T(8,128)S(1)}) custom-call(bf16[256,768]{1,0:T(8,128)(2,1)S(1)} %get-tuple-element.43.refs_0_, bf16[256,768]{1,0:T(8,128)(2,1)S(1)} %get-tuple-element.47.refs_1_, bf16[256,768]{1,0:T(8,128)(2,1)S(1)} %collective-permute-done.1.refs_2_, bf16[64,768]{1,0:T(8,128)(2,1)S(1)} %collective-permute-done.2.refs_3_, ...), custom_call_target="tpu_custom_call" | custom-call | flops 1107296 | bytes 6004 | tf_op jit(solution)/shard_map/attend_own/pallas_call | solution.py:76
  24.2 1.5 %collective-permute-done.7.refs_0_ = bf16[128,768]{1,0:T(8,128)(2,1)S(1)} collective-permute-done((bf16[128,768]{1,0:T(8,128)(2,1)S(1)}, bf16[128,768]{1,0:T(8,128)(2,1)S(1)}, u32[]{:S(2)}, u32[]{:S(2)}) %collective-permute-start.7) | collective-permute-done | bytes 196640 | tf_op jit(solution)/shard_map/ppermute | solution.py:32
  25.8 1.7 %collective-permute-start.12 = (bf16[128,768]{1,0:T(8,128)(2,1)S(1)}, bf16[128,768]{1,0:T(8,128)(2,1)S(1)}, u32[]{:S(2)}, u32[]{:S(2)}) collective-permute-start(bf16[128,768]{1,0:T(8,128)(2,1)S(1)} %relay.11.refs_1_.refs_14_.refs_0_), channel_id=1, source_target_pairs={{0,2},{1,3},{2,0},{3,1},{4,6},{5,7},{6,4},{7,5},{8,10},{9,11},{10,... | collective-permute-start | bytes 589832 | tf_op jit(solution)/shard_map/ppermute | solution.py:32
  27.5 0.5 collective-permute-start.10
  28.0 0.1 collective-permute-start.13
  28.1 0.7 %collective-permute-done.9.refs_3_.refs_6_ = bf16[64,768]{1,0:T(8,128)(2,1)S(1)} collective-permute-done((bf16[64,768]{1,0:T(8,128)(2,1)S(1)}, bf16[64,768]{1,0:T(8,128)(2,1)S(1)}, u32[]{:S(2)}, u32[]{:S(2)}) %collective-permute-start.9) | collective-permute-done | bytes 98336 | tf_op jit(solution)/shard_map/ppermute | solution.py:37
  28.8 0.2 collective-permute-done.10.refs_4_.refs_7_
  29.0 3.7 %attend_partner.2.refs_1_.refs_14_ = bf16[144,768]{1,0:T(8,128)(2,1)S(1)} custom-call(bf16[128,768]{1,0:T(8,128)(2,1)S(1)} %relay.10.refs_11_.refs_0_, bf16[128,768]{1,0:T(8,128)(2,1)S(1)} %get-tuple-element.58.refs_1_.refs_15_.refs_2_, bf16[128,768]{1,0:T(8,128)(2,1)S(1)} %collective-permute-done.8.refs_2_.refs_4_, ...), custom_call_target="tpu_custom_call" | custom-call | flops 1107296 | bytes 5621 | tf_op jit(solution)/shard_map/attend_partner/pallas_call | solution.py:76
  32.8 0.4 collective-permute-start.14
  33.2 0.2 collective-permute-start.15
  33.4 0.8 %collective-permute-done.14.refs_3_.refs_8_ = bf16[64,768]{1,0:T(8,128)(2,1)S(1)} collective-permute-done((bf16[64,768]{1,0:T(8,128)(2,1)S(1)}, bf16[64,768]{1,0:T(8,128)(2,1)S(1)}, u32[]{:S(2)}, u32[]{:S(2)}) %collective-permute-start.14) | collective-permute-done | bytes 98336 | tf_op jit(solution)/shard_map/ppermute | solution.py:37
  34.2 0.4 collective-permute-done.15.refs_4_.refs_9_
  34.5 3.9 %attend_partner.3.refs_15_ = bf16[144,768]{1,0:T(8,128)(2,1)S(1)} custom-call(bf16[128,768]{1,0:T(8,128)(2,1)S(1)} %relay.11.refs_1_.refs_14_.refs_0_, bf16[128,768]{1,0:T(8,128)(2,1)S(1)} %get-tuple-element.61.refs_1_.refs_15_.refs_3_, bf16[128,768]{1,0:T(8,128)(2,1)S(1)} %collective-permute-done.13.refs_2_.refs_5_, ...), custom_call_target="tpu_custom_call" | custom-call | flops 1107296 | bytes 5621 | tf_op jit(solution)/shard_map/attend_partner/pallas_call | solution.py:76
  38.5 2.8 %collective-permute-start.20 = (bf16[144,768]{1,0:T(8,128)(2,1)S(1)}, bf16[144,768]{1,0:T(8,128)(2,1)S(1)}, u32[]{:S(2)}, u32[]{:S(2)}) collective-permute-start(bf16[144,768]{1,0:T(8,128)(2,1)S(1)} %attend_partner.3.refs_15_), channel_id=1, source_target_pairs={{0,16},{4,20},{8,24},{12,28},{16,0},{20,4},{24,8},{28,12},{1,17},{... | collective-permute-start | bytes 663560 | tf_op jit(solution)/shard_map/ppermute | solution.py:32
  41.2 3.9 %attend_own.3 = (f32[128,768]{1,0:T(8,128)S(1)}, f32[8,128]{1,0:T(8,128)S(1)}) custom-call(bf16[256,768]{1,0:T(8,128)(2,1)S(1)} %get-tuple-element.43.refs_0_, bf16[256,768]{1,0:T(8,128)(2,1)S(1)} %get-tuple-element.47.refs_1_, bf16[256,768]{1,0:T(8,128)(2,1)S(1)} %collective-permute-done.1.refs_2_, bf16[64,768]{1,0:T(8,128)(2,1)S(1)} %collective-permute-done.2.refs_3_, ...), custom_call_target="tpu_custom_call" | custom-call | flops 1107296 | bytes 6103 | tf_op jit(solution)/shard_map/attend_own/pallas_call | solution.py:76
  45.1 6.2 %collective-permute-done.11.refs_2_ = bf16[144,768]{1,0:T(8,128)(2,1)S(1)} collective-permute-done((bf16[144,768]{1,0:T(8,128)(2,1)S(1)}, bf16[144,768]{1,0:T(8,128)(2,1)S(1)}, u32[]{:S(2)}, u32[]{:S(2)}) %collective-permute-start.11) | collective-permute-done | bytes 221216 | tf_op jit(solution)/shard_map/ppermute | solution.py:32
  51.4 0.7 %combine.2 = (bf16[128,768]{1,0:T(8,128)(2,1)S(1)}, bf16[128,384]{1,0:T(8,128)(2,1)S(1)}, bf16[128,384]{1,0:T(8,128)(2,1)S(1)}) custom-call(f32[128,768]{1,0:T(8,128)S(1)} %get-tuple-element.56.refs_1_.refs_0_, f32[8,128]{1,0:T(8,128)S(1)} %get-tuple-element.57.refs_1_, bf16[144,768]{1,0:T(8,128)(2,1)S(1)} %collective-permute-done.11.refs_2_, ...), custom_call_target="tpu_custom_call" | custom-call | flops 150994 | bytes 2865 | tf_op jit(solution)/shard_map/combine/pallas_call | solution.py:76
  52.2 0.5 collective-permute-start.18
  52.7 0.7 project.2
  53.4 0.1 collective-permute-done.17.refs_1_
  53.5 0.2 collective-permute-done.18.refs_2_
  53.7 0.5 collective-permute-start.19
  54.2 1.3 %collective-permute-done.20.refs_2_ = bf16[144,768]{1,0:T(8,128)(2,1)S(1)} collective-permute-done((bf16[144,768]{1,0:T(8,128)(2,1)S(1)}, bf16[144,768]{1,0:T(8,128)(2,1)S(1)}, u32[]{:S(2)}, u32[]{:S(2)}) %collective-permute-start.20) | collective-permute-done | bytes 221216 | tf_op jit(solution)/shard_map/ppermute | solution.py:32
  55.6 0.7 %combine.3 = (bf16[128,768]{1,0:T(8,128)(2,1)S(1)}, bf16[128,384]{1,0:T(8,128)(2,1)S(1)}, bf16[128,384]{1,0:T(8,128)(2,1)S(1)}) custom-call(f32[128,768]{1,0:T(8,128)S(1)} %get-tuple-element.64.refs_4_.refs_0_, f32[8,128]{1,0:T(8,128)S(1)} %get-tuple-element.71.refs_1_, bf16[144,768]{1,0:T(8,128)(2,1)S(1)} %collective-permute-done.20.refs_2_, ...), custom_call_target="tpu_custom_call" | custom-call | flops 150994 | bytes 2865 | tf_op jit(solution)/shard_map/combine/pallas_call | solution.py:76
  56.3 0.1 collective-permute-start.22
  56.4 0.5 collective-permute-start.23
  56.9 0.1 collective-permute-start.16
  57.0 0.7 project.3
  57.6 0.5 collective-permute-start.21
  58.1 2.8 %collective-permute-done.19.refs_4_.refs_2_ = bf16[128,768]{1,0:T(8,128)(2,1)S(1)} collective-permute-done((bf16[128,768]{1,0:T(8,128)(2,1)S(1)}, bf16[128,768]{1,0:T(8,128)(2,1)S(1)}, u32[]{:S(2)}, u32[]{:S(2)}) %collective-permute-start.19) | collective-permute-done | bytes 196640 | tf_op jit(solution)/shard_map/ppermute | solution.py:32
  61.0 0.5 collective-permute-start.24
  61.5 1.1 %fresh_kv.3 = (bf16[256,256]{1,0:T(8,128)(2,1)S(1)}, bf16[256,256]{1,0:T(8,128)(2,1)S(1)}) custom-call(bf16[128,768]{1,0:T(8,128)(2,1)S(1)} %relay.10.refs_11_.refs_0_, bf16[128,768]{1,0:T(8,128)(2,1)S(1)} %relay.11.refs_1_.refs_14_.refs_0_, bf16[128,768]{1,0:T(8,128)(2,1)S(1)} %get-tuple-element.58.refs_1_.refs_15_.refs_2_, ...), custom_call_target="tpu_custom_call" | custom-call | flops 402653 | bytes 2758 | tf_op jit(solution)/shard_map/fresh_kv/pallas_call | solution.py:76
  62.6 2.2 %update_caches.1 = (bf16[2048,256]{1,0:T(8,128)(2,1)}, bf16[2048,256]{1,0:T(8,128)(2,1)}, f32[8,128]{1,0:T(8,128)S(1)}) custom-call(bf16[256,256]{1,0:T(8,128)(2,1)S(1)} %get-tuple-element.54.refs_12_.refs_14_.refs_13_.refs_0_, bf16[256,256]{1,0:T(8,128)(2,1)S(1)} %get-tuple-element.78.refs_1_.refs_7_, ...), custom_call_target="tpu_custom_call" | custom-call | flops 67108 | bytes 2361 | tf_op jit(solution)/shard_map/update_caches/pallas_call | solution.py:76
  64.8 2.6 %collective-permute-done.24.refs_5_ = bf16[128,768]{1,0:T(8,128)(2,1)S(1)} collective-permute-done((bf16[128,768]{1,0:T(8,128)(2,1)S(1)}, bf16[128,768]{1,0:T(8,128)(2,1)S(1)}, u32[]{:S(2)}, u32[]{:S(2)}) %collective-permute-start.24) | collective-permute-done | bytes 196640 | tf_op jit(solution)/shard_map/ppermute | solution.py:32
  67.4 0.9 %finish.1 = bf16[256,768]{1,0:T(8,128)(2,1)} custom-call(bf16[128,768]{1,0:T(8,128)(2,1)S(1)} %get-tuple-element.66.refs_0_, bf16[128,768]{1,0:T(8,128)(2,1)S(1)} %collective-permute-done.16.refs_1_, bf16[128,768]{1,0:T(8,128)(2,1)S(1)} %collective-permute-done.19.refs_4_.refs_2_, bf16[128,768]{1,0:T(8,128)(2,1)S(1)} %get-tuple-element.73.refs_3_, ...), custom_call_target="tpu_custom_call" | custom-call | flops 98 | bytes 786 | tf_op jit(solution)/shard_map/finish/pallas_call | solution.py:76
  (52 shorter events, 0.7 us)
Async XLA Ops:
  0.6 12.4 %collective-permute-start = (bf16[256,768]{1,0:T(8,128)(2,1)}, bf16[256,768]{1,0:T(8,128)(2,1)S(1)}, u32[]{:S(2)}, u32[]{:S(2)}) collective-permute-start(bf16[256,768]{1,0:T(8,128)(2,1)} %refs_0_.3), channel_id=1, source_target_pairs={{0,2},{1,3},{2,0},{3,1},{4,6},{5,7},{6,4},{7,5},{8,10},{9,11},{10,... | collective-permute-start | bytes 1179656 | tf_op jit(solution)/shard_map/ppermute | solution.py:32
  3.7 14.1 %collective-permute-start.1 = (bf16[256,768]{1,0:T(8,128)(2,1)}, bf16[256,768]{1,0:T(8,128)(2,1)S(1)}, u32[]{:S(2)}, u32[]{:S(2)}) collective-permute-start(bf16[256,768]{1,0:T(8,128)(2,1)} %refs_0_.3), channel_id=1, source_target_pairs={{0,1},{1,0},{2,3},{3,2},{4,5},{5,4},{6,7},{7,6},{8,9},{9,8},{10,11... | collective-permute-start | bytes 1179656 | tf_op jit(solution)/shard_map/ppermute | solution.py:37
  3.7 1.0 %copy-start.5 = (bf16[256,768]{1,0:T(8,128)(2,1)S(1)}, bf16[256,768]{1,0:T(8,128)(2,1)}, u32[]{:S(2)}) copy-start(bf16[256,768]{1,0:T(8,128)(2,1)} %refs_0_.3) | copy-start | bytes 1179652
  4.7 2.7 %copy-start.6 = (s32[4]{0:T(128)S(1)}, s32[4]{0:T(128)}, u32[]{:S(2)}) copy-start(s32[4]{0:T(128)} %refs_6_.7) | copy-start | bytes 52
  4.8 2.7 %copy-start.7 = (s32[4]{0:T(128)S(1)}, s32[4]{0:T(128)}, u32[]{:S(2)}) copy-start(s32[4]{0:T(128)} %refs_1_.4) | copy-start | bytes 52
  4.8 4.3 %copy-start.2 = (bf16[2048,256]{1,0:T(8,128)(2,1)S(1)}, bf16[2048,256]{1,0:T(8,128)(2,1)}, u32[]{:S(2)}) copy-start(bf16[2048,256]{1,0:T(8,128)(2,1)} %refs_4_.1) | copy-start | bytes 3145732
  4.8 4.3 %copy-start.3 = (bf16[2048,256]{1,0:T(8,128)(2,1)S(1)}, bf16[2048,256]{1,0:T(8,128)(2,1)}, u32[]{:S(2)}) copy-start(bf16[2048,256]{1,0:T(8,128)(2,1)} %refs_5_.1) | copy-start | bytes 3145732
  4.8 12.5 %collective-permute-start.5 = (bf16[128,768]{1,0:T(8,128)(2,1)S(1)}, bf16[128,768]{1,0:T(8,128)(2,1)S(1)}, u32[]{:S(2)}, u32[]{:S(2)}) collective-permute-start(bf16[128,768]{1,0:T(8,128)(2,1)S(1)} %get-tuple-element.53), channel_id=1, source_target_pairs={{0,16},{4,20},{8,24},{12,28},{16,0},{20,4},{24,8},{28,12},{1,17},{... | collective-permute-start | bytes 589832 | tf_op jit(solution)/shard_map/ppermute | solution.py:32
  7.4 13.0 %slice-start = ((s8[4718592]{0:T(1024)(128)(4,1)}), s8[4194304]{0:T(1024)(128)(4,1)S(1)}, s32[]{:S(2)}) async-start(s8[4718592]{0:T(1024)(128)(4,1)} %bitcast.1), calls=%async_computation | async-start | bytes 8388608
  9.1 11.3 %slice-start.1 = ((s8[4718592]{0:T(1024)(128)(4,1)}), s8[524288]{0:T(1024)(128)(4,1)S(1)}, s32[]{:S(2)}) async-start(s8[4718592]{0:T(1024)(128)(4,1)} %bitcast.1), calls=%async_computation.1 | async-start | bytes 1048576
  13.0 6.3 %copy-start = (bf16[3072,256]{1,0:T(8,128)(2,1)S(1)}, bf16[3072,256]{1,0:T(8,128)(2,1)}, u32[]{:S(2)}) copy-start(bf16[3072,256]{1,0:T(8,128)(2,1)} %refs_11_.1) | copy-start | bytes 4718596
  13.0 6.3 %copy-start.1 = (bf16[3072,256]{1,0:T(8,128)(2,1)S(1)}, bf16[3072,256]{1,0:T(8,128)(2,1)}, u32[]{:S(2)}) copy-start(bf16[3072,256]{1,0:T(8,128)(2,1)} %refs_12_.1) | copy-start | bytes 4718596
  13.0 6.3 %copy-start.4 = (f32[3072]{0:T(1024)S(1)}, f32[3072]{0:T(1024)}, u32[]{:S(2)}) copy-start(f32[3072]{0:T(1024)} %param.11) | copy-start | bytes 36868
  13.1 6.2 %collective-permute-start.4 = (bf16[128,768]{1,0:T(8,128)(2,1)S(1)}, bf16[128,768]{1,0:T(8,128)(2,1)S(1)}, u32[]{:S(2)}, u32[]{:S(2)}) collective-permute-start(bf16[128,768]{1,0:T(8,128)(2,1)S(1)} %get-tuple-element.52), channel_id=1, source_target_pairs={{0,1},{1,0},{2,3},{3,2},{4,5},{5,4},{6,7},{7,6},{8,9},{9,8},{10,11... | collective-permute-start | bytes 589832 | tf_op jit(solution)/shard_map/ppermute | solution.py:37
  13.2 12.6 %collective-permute-start.7 = (bf16[128,768]{1,0:T(8,128)(2,1)S(1)}, bf16[128,768]{1,0:T(8,128)(2,1)S(1)}, u32[]{:S(2)}, u32[]{:S(2)}) collective-permute-start(bf16[128,768]{1,0:T(8,128)(2,1)S(1)} %relay.8.refs_1_), channel_id=1, source_target_pairs={{0,16},{4,20},{8,24},{12,28},{16,0},{20,4},{24,8},{28,12},{1,17},{... | collective-permute-start | bytes 589832 | tf_op jit(solution)/shard_map/ppermute | solution.py:32
  17.3 10.1 %collective-permute-start.6 = (bf16[128,768]{1,0:T(8,128)(2,1)S(1)}, bf16[128,768]{1,0:T(8,128)(2,1)S(1)}, u32[]{:S(2)}, u32[]{:S(2)}) collective-permute-start(bf16[128,768]{1,0:T(8,128)(2,1)S(1)} %relay.10.refs_11_.refs_0_), channel_id=1, source_target_pairs={{0,2},{1,3},{2,0},{3,1},{4,6},{5,7},{6,4},{7,5},{8,10},{9,11},{10,... | collective-permute-start | bytes 589832 | tf_op jit(solution)/shard_map/ppermute | solution.py:32
  17.8 1.3 %collective-permute-start.2 = (bf16[64,768]{1,0:T(8,128)(2,1)S(1)}, bf16[64,768]{1,0:T(8,128)(2,1)S(1)}, u32[]{:S(2)}, u32[]{:S(2)}) collective-permute-start(bf16[64,768]{1,0:T(8,128)(2,1)S(1)} %get-tuple-element.48), channel_id=1, source_target_pairs={{0,1},{1,0},{2,3},{3,2},{4,5},{5,4},{6,7},{7,6},{8,9},{9,8},{10,11... | collective-permute-start | bytes 294920 | tf_op jit(solution)/shard_map/ppermute | solution.py:37
  17.8 1.5 %collective-permute-start.3 = (bf16[64,768]{1,0:T(8,128)(2,1)S(1)}, bf16[64,768]{1,0:T(8,128)(2,1)S(1)}, u32[]{:S(2)}, u32[]{:S(2)}) collective-permute-start(bf16[64,768]{1,0:T(8,128)(2,1)S(1)} %get-tuple-element.49), channel_id=1, source_target_pairs={{0,1},{1,0},{2,3},{3,2},{4,5},{5,4},{6,7},{7,6},{8,9},{9,8},{10,11... | collective-permute-start | bytes 294920 | tf_op jit(solution)/shard_map/ppermute | solution.py:37
  19.1 9.0 %collective-permute-start.8 = (bf16[128,768]{1,0:T(8,128)(2,1)S(1)}, bf16[128,768]{1,0:T(8,128)(2,1)S(1)}, u32[]{:S(2)}, u32[]{:S(2)}) collective-permute-start(bf16[128,768]{1,0:T(8,128)(2,1)S(1)} %relay.10.refs_11_.refs_0_), channel_id=1, source_target_pairs={{0,1},{1,0},{2,3},{3,2},{4,5},{5,4},{6,7},{7,6},{8,9},{9,8},{10,11... | collective-permute-start | bytes 589832 | tf_op jit(solution)/shard_map/ppermute | solution.py:37
  25.8 7.0 %collective-permute-start.12 = (bf16[128,768]{1,0:T(8,128)(2,1)S(1)}, bf16[128,768]{1,0:T(8,128)(2,1)S(1)}, u32[]{:S(2)}, u32[]{:S(2)}) collective-permute-start(bf16[128,768]{1,0:T(8,128)(2,1)S(1)} %relay.11.refs_1_.refs_14_.refs_0_), channel_id=1, source_target_pairs={{0,2},{1,3},{2,0},{3,1},{4,6},{5,7},{6,4},{7,5},{8,10},{9,11},{10,... | collective-permute-start | bytes 589832 | tf_op jit(solution)/shard_map/ppermute | solution.py:32
  27.4 1.4 %collective-permute-start.9 = (bf16[64,768]{1,0:T(8,128)(2,1)S(1)}, bf16[64,768]{1,0:T(8,128)(2,1)S(1)}, u32[]{:S(2)}, u32[]{:S(2)}) collective-permute-start(bf16[64,768]{1,0:T(8,128)(2,1)S(1)} %get-tuple-element.59), channel_id=1, source_target_pairs={{0,1},{1,0},{2,3},{3,2},{4,5},{5,4},{6,7},{7,6},{8,9},{9,8},{10,11... | collective-permute-start | bytes 294920 | tf_op jit(solution)/shard_map/ppermute | solution.py:37
  27.5 1.4 %collective-permute-start.10 = (bf16[64,768]{1,0:T(8,128)(2,1)S(1)}, bf16[64,768]{1,0:T(8,128)(2,1)S(1)}, u32[]{:S(2)}, u32[]{:S(2)}) collective-permute-start(bf16[64,768]{1,0:T(8,128)(2,1)S(1)} %get-tuple-element.60), channel_id=1, source_target_pairs={{0,1},{1,0},{2,3},{3,2},{4,5},{5,4},{6,7},{7,6},{8,9},{9,8},{10,11... | collective-permute-start | bytes 294920 | tf_op jit(solution)/shard_map/ppermute | solution.py:37
  28.0 5.4 %collective-permute-start.13 = (bf16[128,768]{1,0:T(8,128)(2,1)S(1)}, bf16[128,768]{1,0:T(8,128)(2,1)S(1)}, u32[]{:S(2)}, u32[]{:S(2)}) collective-permute-start(bf16[128,768]{1,0:T(8,128)(2,1)S(1)} %relay.11.refs_1_.refs_14_.refs_0_), channel_id=1, source_target_pairs={{0,1},{1,0},{2,3},{3,2},{4,5},{5,4},{6,7},{7,6},{8,9},{9,8},{10,11... | collective-permute-start | bytes 589832 | tf_op jit(solution)/shard_map/ppermute | solution.py:37
  32.7 18.7 %collective-permute-start.11 = (bf16[144,768]{1,0:T(8,128)(2,1)S(1)}, bf16[144,768]{1,0:T(8,128)(2,1)S(1)}, u32[]{:S(2)}, u32[]{:S(2)}) collective-permute-start(bf16[144,768]{1,0:T(8,128)(2,1)S(1)} %attend_partner.2.refs_1_.refs_14_), channel_id=1, source_target_pairs={{0,16},{4,20},{8,24},{12,28},{16,0},{20,4},{24,8},{28,12},{1,17},{... | collective-permute-start | bytes 663560 | tf_op jit(solution)/shard_map/ppermute | solution.py:32
  32.8 1.4 %collective-permute-start.14 = (bf16[64,768]{1,0:T(8,128)(2,1)S(1)}, bf16[64,768]{1,0:T(8,128)(2,1)S(1)}, u32[]{:S(2)}, u32[]{:S(2)}) collective-permute-start(bf16[64,768]{1,0:T(8,128)(2,1)S(1)} %get-tuple-element.62), channel_id=1, source_target_pairs={{0,1},{1,0},{2,3},{3,2},{4,5},{5,4},{6,7},{7,6},{8,9},{9,8},{10,11... | collective-permute-start | bytes 294920 | tf_op jit(solution)/shard_map/ppermute | solution.py:37
  33.2 1.3 %collective-permute-start.15 = (bf16[64,768]{1,0:T(8,128)(2,1)S(1)}, bf16[64,768]{1,0:T(8,128)(2,1)S(1)}, u32[]{:S(2)}, u32[]{:S(2)}) collective-permute-start(bf16[64,768]{1,0:T(8,128)(2,1)S(1)} %get-tuple-element.63), channel_id=1, source_target_pairs={{0,1},{1,0},{2,3},{3,2},{4,5},{5,4},{6,7},{7,6},{8,9},{9,8},{10,11... | collective-permute-start | bytes 294920 | tf_op jit(solution)/shard_map/ppermute | solution.py:37
  34.5 16.9 %slice-start.2 = ((s8[4718592]{0:T(1024)(128)(4,1)}), s8[4194304]{0:T(1024)(128)(4,1)S(1)}, s32[]{:S(2)}) async-start(s8[4718592]{0:T(1024)(128)(4,1)} %bitcast.3), calls=%async_computation.2 | async-start | bytes 8388608
  38.5 12.9 %slice-start.3 = ((s8[4718592]{0:T(1024)(128)(4,1)}), s8[524288]{0:T(1024)(128)(4,1)S(1)}, s32[]{:S(2)}) async-start(s8[4718592]{0:T(1024)(128)(4,1)} %bitcast.3), calls=%async_computation.3 | async-start | bytes 1048576
  38.5 17.1 %collective-permute-start.20 = (bf16[144,768]{1,0:T(8,128)(2,1)S(1)}, bf16[144,768]{1,0:T(8,128)(2,1)S(1)}, u32[]{:S(2)}, u32[]{:S(2)}) collective-permute-start(bf16[144,768]{1,0:T(8,128)(2,1)S(1)} %attend_partner.3.refs_15_), channel_id=1, source_target_pairs={{0,16},{4,20},{8,24},{12,28},{16,0},{20,4},{24,8},{28,12},{1,17},{... | collective-permute-start | bytes 663560 | tf_op jit(solution)/shard_map/ppermute | solution.py:32
  52.1 1.4 %collective-permute-start.17 = (bf16[128,384]{1,0:T(8,128)(2,1)S(1)}, bf16[128,384]{1,0:T(8,128)(2,1)S(1)}, u32[]{:S(2)}, u32[]{:S(2)}) collective-permute-start(bf16[128,384]{1,0:T(8,128)(2,1)S(1)} %get-tuple-element.69), channel_id=1, source_target_pairs={{0,1},{1,0},{2,3},{3,2},{4,5},{5,4},{6,7},{7,6},{8,9},{9,8},{10,11... | collective-permute-start | bytes 294920 | tf_op jit(solution)/shard_map/ppermute | solution.py:37
  52.2 1.4 %collective-permute-start.18 = (bf16[128,384]{1,0:T(8,128)(2,1)S(1)}, bf16[128,384]{1,0:T(8,128)(2,1)S(1)}, u32[]{:S(2)}, u32[]{:S(2)}) collective-permute-start(bf16[128,384]{1,0:T(8,128)(2,1)S(1)} %get-tuple-element.70), channel_id=1, source_target_pairs={{0,1},{1,0},{2,3},{3,2},{4,5},{5,4},{6,7},{7,6},{8,9},{9,8},{10,11... | collective-permute-start | bytes 294920 | tf_op jit(solution)/shard_map/ppermute | solution.py:37
  53.7 7.2 %collective-permute-start.19 = (bf16[128,768]{1,0:T(8,128)(2,1)S(1)}, bf16[128,768]{1,0:T(8,128)(2,1)S(1)}, u32[]{:S(2)}, u32[]{:S(2)}) collective-permute-start(bf16[128,768]{1,0:T(8,128)(2,1)S(1)} %sum_cores.2.refs_4_), channel_id=1, source_target_pairs={{0,2},{1,3},{2,0},{3,1},{4,6},{5,7},{6,4},{7,5},{8,10},{9,11},{10,... | collective-permute-start | bytes 589832 | tf_op jit(solution)/shard_map/ppermute | solution.py:32
  56.3 1.8 %collective-permute-start.22 = (bf16[128,384]{1,0:T(8,128)(2,1)S(1)}, bf16[128,384]{1,0:T(8,128)(2,1)S(1)}, u32[]{:S(2)}, u32[]{:S(2)}) collective-permute-start(bf16[128,384]{1,0:T(8,128)(2,1)S(1)} %get-tuple-element.76), channel_id=1, source_target_pairs={{0,1},{1,0},{2,3},{3,2},{4,5},{5,4},{6,7},{7,6},{8,9},{9,8},{10,11... | collective-permute-start | bytes 294920 | tf_op jit(solution)/shard_map/ppermute | solution.py:37
  56.4 1.8 %collective-permute-start.23 = (bf16[128,384]{1,0:T(8,128)(2,1)S(1)}, bf16[128,384]{1,0:T(8,128)(2,1)S(1)}, u32[]{:S(2)}, u32[]{:S(2)}) collective-permute-start(bf16[128,384]{1,0:T(8,128)(2,1)S(1)} %get-tuple-element.77), channel_id=1, source_target_pairs={{0,1},{1,0},{2,3},{3,2},{4,5},{5,4},{6,7},{7,6},{8,9},{9,8},{10,11... | collective-permute-start | bytes 294920 | tf_op jit(solution)/shard_map/ppermute | solution.py:37
  56.9 7.9 %collective-permute-start.16 = (bf16[128,768]{1,0:T(8,128)(2,1)S(1)}, bf16[128,768]{1,0:T(8,128)(2,1)S(1)}, u32[]{:S(2)}, u32[]{:S(2)}) collective-permute-start(bf16[128,768]{1,0:T(8,128)(2,1)S(1)} %get-tuple-element.67.refs_3_), channel_id=1, source_target_pairs={{0,1},{1,0},{2,3},{3,2},{4,5},{5,4},{6,7},{7,6},{8,9},{9,8},{10,11... | collective-permute-start | bytes 589832 | tf_op jit(solution)/shard_map/ppermute | solution.py:37
  57.6 7.1 %collective-permute-start.21 = (bf16[128,768]{1,0:T(8,128)(2,1)S(1)}, bf16[128,768]{1,0:T(8,128)(2,1)S(1)}, u32[]{:S(2)}, u32[]{:S(2)}) collective-permute-start(bf16[128,768]{1,0:T(8,128)(2,1)S(1)} %get-tuple-element.74.refs_3_), channel_id=1, source_target_pairs={{0,1},{1,0},{2,3},{3,2},{4,5},{5,4},{6,7},{7,6},{8,9},{9,8},{10,11... | collective-permute-start | bytes 589832 | tf_op jit(solution)/shard_map/ppermute | solution.py:37
  61.0 6.4 %collective-permute-start.24 = (bf16[128,768]{1,0:T(8,128)(2,1)S(1)}, bf16[128,768]{1,0:T(8,128)(2,1)S(1)}, u32[]{:S(2)}, u32[]{:S(2)}) collective-permute-start(bf16[128,768]{1,0:T(8,128)(2,1)S(1)} %sum_cores.3.refs_15_), channel_id=1, source_target_pairs={{0,2},{1,3},{2,0},{3,1},{4,6},{5,7},{6,4},{7,5},{8,10},{9,11},{10,... | collective-permute-start | bytes 589832 | tf_op jit(solution)/shard_map/ppermute | solution.py:32

commit v12 on v10

--- a/solution.py
+++ b/solution.py
@@ -14,6 +14,7 @@
 ROW_TILE = 16
 CORES = 2
 CHUNKS = 2
+SLOT_TILES = 2
 COST_WEIGHT = 0.0005
 FIRST_MICROS = 2
 FLOPS_PER_MICRO = 1_000_000_000
@@ -265,17 +266,17 @@
         )
         for head in range(kv_heads * repeat)
     ]
-    step = min(rows, LANES)
-    mark = mark[: repeat * step]
-    tiles = [(head, at) for head in range(kv_heads) for at in range(0, rows, step)]
+    mark = mark[: repeat * rows]
+    slots = wide_keys.shape[1] // SLOT_TILES
+    tiles = [(head, at) for head in range(kv_heads) for at in range(0, slots * SLOT_TILES, slots)]
 
     def scores_of(head, at):
-        stacked = jnp.concatenate(
-            [query[at : at + step] for query in queries[head * repeat : (head + 1) * repeat]], 0
-        )
-        return dot_transposed(jnp.concatenate([stacked, mark], 1), wide_keys[head])
-
-    columns = {}
+        stacked = jnp.concatenate(queries[head * repeat : (head + 1) * repeat], 0)
+        wide = jnp.concatenate([stacked, mark], 1)
+        return dot_transposed(wide, wide_keys[head, at : at + slots])
+
+    columns = []
+    found = []
     following = scores_of(*tiles[0])
     for index, (head, at) in enumerate(tiles):
         scores = following
@@ -283,16 +284,21 @@
             following = scores_of(*tiles[index + 1])
         largest = jnp.max(scores, -1, keepdims=True)
         weights = jnp.exp2(scores - largest).astype(jnp.bfloat16)
-        summed = dot(weights, wide_values[head])
+        found.append((largest, dot(weights, wide_values[head, at : at + slots])))
+        if len(found) < SLOT_TILES:
+            continue
+        largest = functools.reduce(jnp.maximum, [tile[0] for tile in found])
+        summed = sum(tile[1] * jnp.exp2(tile[0] - largest) for tile in found)
+        found = []
         denominator = summed[:, HD : HD + 1]
         result = summed[:, :HD] / denominator
         logs = largest + jnp.log2(denominator)
         for turn in range(repeat):
-            part = slice(turn * step, (turn + 1) * step)
+            part = slice(turn * rows, (turn + 1) * rows)
             to = slice((head * repeat + turn) * HD, (head * repeat + turn + 1) * HD)
-            outputs[0][at : at + step, to] = result[part].astype(outputs[0].dtype)
-            columns.setdefault(head * repeat + turn, []).append(logs[part])
-    stats = stat_rows([jnp.concatenate(parts, 0) for parts in columns.values()], rows)
+            outputs[0][:rows, to] = result[part].astype(outputs[0].dtype)
+            columns.append(logs[part])
+    stats = stat_rows(columns, rows)
     if own:
         outputs[1][...] = stats
         outputs[2][...] = jnp.concatenate(queries, 1)
@@ -643,11 +649,11 @@
     first = [shifted(early, "seq", turn * requests) for turn in range(1, groups)]
     (late,) = relay([late], [rows - chunk_rows], from_chips + [wide_keys])
     second = [shifted(late, "seq", turn * requests) for turn in range(1, groups)]
-    own_cuts = [relay([piece], [rows, half, half, rows - chunk_rows], [late]) for piece in from_chips]
+    own_cuts = [relay([piece], [rows, half, half, half, half], [late]) for piece in from_chips]
     own_pieces = [[own]] + [[cut[0]] for cut in own_cuts] + [[crossed]]
     own_pieces += [[other_core(block) for block in cut[1:]] for cut in own_cuts]
     own_early = [
-        blocks if len(blocks) == 1 else blocks[: len(blocks) - 1] for blocks in own_pieces
+        blocks if len(blocks) == 1 else blocks[:2] for blocks in own_pieces
     ]
     earlier = [cut[0] for cut in own_cuts]
     first = [relay([piece], [chunk_rows], earlier)[0] for piece in first]

time: 64.9 us -> 65 us (level)
    ppermute x16 -> x17, waiting for transfers between devices: 2.29 us -> 2.21 us  [other_core(): return lax.ppermute(shard, 'head', [(i, i ^ 1) for i in range(devices)])]
    ppermute x16 -> x17, starting transfers between devices: 3.72 us -> 3.8 us  [other_core(): return lax.ppermute(shard, 'head', [(i, i ^ 1) for i in range(devices)])]
  transfers between devices with their start and end apart: 25 -> 26, of which waited for: 10 -> 10; matrix products, arithmetic and copies ran while one was open for 0% -> 0% of each run, Pallas kernels for 41% -> 42%
where the time goes in v12:
time: 65 us; the launch traced here: 64.9 us
  Pallas kernels  27.9 us (43%)
  starting transfers between devices  19.5 us (30%)
  waiting for transfers between devices  15.5 us (24%)
  local copies, waits for them, and re-layouts  1.09 us (2%)
  between operations  0.97 us (1%)
    pallas_call x25, Pallas kernels, call(): pl.pallas_call(body, out_shape=out_shape, in_specs=[VMEM] * len(arrays) +...  27.9 us
    ppermute x9, starting transfers between devices, shifted(): lax.ppermute(shard, axis, [(i, (i + by) % devices) for i in range(devices)])  15.7 us
    ppermute x9, waiting for transfers between devices, shifted(): lax.ppermute(shard, axis, [(i, (i + by) % devices) for i in range(devices)])  13.2 us
    ppermute x17, starting transfers between devices, other_core(): return lax.ppermute(shard, 'head', [(i, i ^ 1) for i in range(devices)])  3.8 us
    ppermute x17, waiting for transfers between devices, other_core(): return lax.ppermute(shard, 'head', [(i, i ^ 1) for i in range(devices)])  2.21 us
  transfers between devices with their start and end apart: 26, of which 10 were waited for; matrix products, arithmetic and copies ran while one was open for 0% of the time, Pallas kernels for 42%

profile of v12, /device:TPU:0, one launch (start us, length us, event | category | flops | bytes accessed | tf_op | source)
XLA Modules:
  0.0 64.9 jit_solution(1478820794802993710)
XLA Ops:
  0.6 3.0 %collective-permute-start = (bf16[256,768]{1,0:T(8,128)(2,1)}, bf16[256,768]{1,0:T(8,128)(2,1)S(1)}, u32[]{:S(2)}, u32[]{:S(2)}) collective-permute-start(bf16[256,768]{1,0:T(8,128)(2,1)} %refs_0_.3), channel_id=1, source_target_pairs={{0,2},{1,3},{2,0},{3,1},{4,6},{5,7},{6,4},{7,5},{8,10},{9,11},{10,... | collective-permute-start | bytes 1179656 | tf_op jit(solution)/shard_map/ppermute | solution.py:33
  3.7 1.0 %copy-done.5 = bf16[256,768]{1,0:T(8,128)(2,1)S(1)} copy-done((bf16[256,768]{1,0:T(8,128)(2,1)S(1)}, bf16[256,768]{1,0:T(8,128)(2,1)}, u32[]{:S(2)}) %copy-start.5) | copy-done | bytes 393240
  4.8 2.7 %collective-permute-start.4 = (bf16[128,768]{1,0:T(8,128)(2,1)S(1)}, bf16[128,768]{1,0:T(8,128)(2,1)S(1)}, u32[]{:S(2)}, u32[]{:S(2)}) collective-permute-start(bf16[128,768]{1,0:T(8,128)(2,1)S(1)} %get-tuple-element.57), channel_id=1, source_target_pairs={{0,16},{4,20},{8,24},{12,28},{16,0},{20,4},{24,8},{28,12},{1,17},{... | collective-permute-start | bytes 589832 | tf_op jit(solution)/shard_map/ppermute | solution.py:33
  7.5 1.6 %rope_tables.1 = (f32[512,128]{1,0:T(8,128)S(1)}, f32[512,128]{1,0:T(8,128)S(1)}) custom-call(s32[4]{0:T(128)S(1)} %copy-done.6, s32[4]{0:T(128)S(1)} %copy-done.7, bf16[2048,128]{1,0:T(8,128)(2,1)S(1)} %marks.1.refs_2_.refs_11_.refs_13_), custom_call_target="tpu_custom_call" | custom-call | bytes 262 | tf_op jit(solution)/shard_map/rope_tables/pallas_call | solution.py:77
  9.1 0.8 %widen_caches.1 = (bf16[2,2048,256]{2,1,0:T(8,128)(2,1)S(1)}, bf16[2,2048,256]{2,1,0:T(8,128)(2,1)S(1)}) custom-call(bf16[2048,256]{1,0:T(8,128)(2,1)S(1)} %copy-done.2, bf16[2048,256]{1,0:T(8,128)(2,1)S(1)} %copy-done.3, bf16[2048,128]{1,0:T(8,128)(2,1)S(1)} %marks.1.refs_2_.refs_11_.refs_13_, s32[4]{0:T(128)S(1)} %copy-done.6, ...), custom_call_target="tpu_custom_call" | custom-call | bytes 3407 | tf_op jit(solution)/shard_map/widen_caches/pallas_call | solution.py:77
  9.9 3.1 %collective-permute-done.refs_1_.refs_0_ = bf16[256,768]{1,0:T(8,128)(2,1)S(1)} collective-permute-done((bf16[256,768]{1,0:T(8,128)(2,1)}, bf16[256,768]{1,0:T(8,128)(2,1)S(1)}, u32[]{:S(2)}, u32[]{:S(2)}) %collective-permute-start) | collective-permute-done | bytes 393248 | tf_op jit(solution)/shard_map/ppermute | solution.py:33
  13.1 0.1 collective-permute-start.2
  13.1 2.9 %collective-permute-start.8 = (bf16[128,768]{1,0:T(8,128)(2,1)S(1)}, bf16[128,768]{1,0:T(8,128)(2,1)S(1)}, u32[]{:S(2)}, u32[]{:S(2)}) collective-permute-start(bf16[128,768]{1,0:T(8,128)(2,1)S(1)} %relay.8.refs_1_), channel_id=1, source_target_pairs={{0,16},{4,20},{8,24},{12,28},{16,0},{20,4},{24,8},{28,12},{1,17},{... | collective-permute-start | bytes 589832 | tf_op jit(solution)/shard_map/ppermute | solution.py:33
  16.0 1.2 %collective-permute-done.4.refs_0_ = bf16[128,768]{1,0:T(8,128)(2,1)S(1)} collective-permute-done((bf16[128,768]{1,0:T(8,128)(2,1)S(1)}, bf16[128,768]{1,0:T(8,128)(2,1)S(1)}, u32[]{:S(2)}, u32[]{:S(2)}) %collective-permute-start.4) | collective-permute-done | bytes 196640 | tf_op jit(solution)/shard_map/ppermute | solution.py:33
  17.3 0.5 collective-permute-start.7
  17.8 0.5 collective-permute-start.5
  18.4 0.7 %collective-permute-done.3.refs_4_ = bf16[64,768]{1,0:T(8,128)(2,1)S(1)} collective-permute-done((bf16[64,768]{1,0:T(8,128)(2,1)S(1)}, bf16[64,768]{1,0:T(8,128)(2,1)S(1)}, u32[]{:S(2)}, u32[]{:S(2)}) %collective-permute-start.3) | collective-permute-done | bytes 98336 | tf_op jit(solution)/shard_map/ppermute | solution.py:38
  19.1 0.2 collective-permute-start.9
  19.3 3.6 %attend_own.2 = (f32[128,768]{1,0:T(8,128)S(1)}, f32[8,128]{1,0:T(8,128)S(1)}, bf16[128,768]{1,0:T(8,128)(2,1)S(1)}) custom-call(bf16[256,768]{1,0:T(8,128)(2,1)S(1)} %get-tuple-element.48.refs_0_, bf16[256,768]{1,0:T(8,128)(2,1)S(1)} %get-tuple-element.52.refs_1_, bf16[256,768]{1,0:T(8,128)(2,1)S(1)} %collective-permute-done.1.refs_2_, ...), custom_call_target="tpu_custom_call" | custom-call | flops 1107296 | bytes 5971 | tf_op jit(solution)/shard_map/attend_own/pallas_call | solution.py:77
  22.9 1.2 %fresh_kv.2 = (bf16[256,256]{1,0:T(8,128)(2,1)S(1)}, bf16[256,256]{1,0:T(8,128)(2,1)S(1)}) custom-call(bf16[256,768]{1,0:T(8,128)(2,1)S(1)} %get-tuple-element.48.refs_0_, bf16[256,768]{1,0:T(8,128)(2,1)S(1)} %get-tuple-element.52.refs_1_, bf16[256,768]{1,0:T(8,128)(2,1)S(1)} %collective-permute-done.1.refs_2_, ...), custom_call_target="tpu_custom_call" | custom-call | flops 402653 | bytes 2758 | tf_op jit(solution)/shard_map/fresh_kv/pallas_call | solution.py:77
  24.1 1.7 %collective-permute-done.8.refs_0_ = bf16[128,768]{1,0:T(8,128)(2,1)S(1)} collective-permute-done((bf16[128,768]{1,0:T(8,128)(2,1)S(1)}, bf16[128,768]{1,0:T(8,128)(2,1)S(1)}, u32[]{:S(2)}, u32[]{:S(2)}) %collective-permute-start.8) | collective-permute-done | bytes 196640 | tf_op jit(solution)/shard_map/ppermute | solution.py:33
  25.8 0.1 collective-permute-start.10
  25.9 0.5 collective-permute-start.11
  26.4 1.6 %collective-permute-start.12 = (bf16[128,768]{1,0:T(8,128)(2,1)S(1)}, bf16[128,768]{1,0:T(8,128)(2,1)S(1)}, u32[]{:S(2)}, u32[]{:S(2)}) collective-permute-start(bf16[128,768]{1,0:T(8,128)(2,1)S(1)} %relay.11.refs_1_.refs_12_.refs_0_), channel_id=1, source_target_pairs={{0,2},{1,3},{2,0},{3,1},{4,6},{5,7},{6,4},{7,5},{8,10},{9,11},{10,... | collective-permute-start | bytes 589832 | tf_op jit(solution)/shard_map/ppermute | solution.py:33
  28.0 3.6 %attend_partner.2.refs_14_ = bf16[144,768]{1,0:T(8,128)(2,1)S(1)} custom-call(bf16[128,768]{1,0:T(8,128)(2,1)S(1)} %relay.10.refs_12_.refs_0_, bf16[128,768]{1,0:T(8,128)(2,1)S(1)} %get-tuple-element.64.refs_1_.refs_13_.refs_2_, bf16[128,768]{1,0:T(8,128)(2,1)S(1)} %collective-permute-done.9.refs_2_.refs_4_, ...), custom_call_target="tpu_custom_call" | custom-call | flops 1107296 | bytes 5490 | tf_op jit(solution)/shard_map/attend_partner/pallas_call | solution.py:77
  31.6 0.1 collective-permute-start.13
  31.7 3.8 %attend_own.3 = (f32[128,768]{1,0:T(8,128)S(1)}, f32[8,128]{1,0:T(8,128)S(1)}, bf16[128,768]{1,0:T(8,128)(2,1)S(1)}) custom-call(bf16[256,768]{1,0:T(8,128)(2,1)S(1)} %get-tuple-element.48.refs_0_, bf16[256,768]{1,0:T(8,128)(2,1)S(1)} %get-tuple-element.52.refs_1_, bf16[256,768]{1,0:T(8,128)(2,1)S(1)} %collective-permute-done.1.refs_2_, ...), custom_call_target="tpu_custom_call" | custom-call | flops 1107296 | bytes 6070 | tf_op jit(solution)/shard_map/attend_own/pallas_call | solution.py:77
  35.5 0.6 collective-permute-start.14
  36.1 0.1 collective-permute-start.15
  36.1 0.9 %collective-permute-done.14.refs_3_.refs_8_ = bf16[64,768]{1,0:T(8,128)(2,1)S(1)} collective-permute-done((bf16[64,768]{1,0:T(8,128)(2,1)S(1)}, bf16[64,768]{1,0:T(8,128)(2,1)S(1)}, u32[]{:S(2)}, u32[]{:S(2)}) %collective-permute-start.14) | collective-permute-done | bytes 98336 | tf_op jit(solution)/shard_map/ppermute | solution.py:38
  37.0 0.4 collective-permute-done.15.refs_4_.refs_9_
  37.4 3.6 %attend_partner.3.refs_15_ = bf16[144,768]{1,0:T(8,128)(2,1)S(1)} custom-call(bf16[128,768]{1,0:T(8,128)(2,1)S(1)} %relay.11.refs_1_.refs_12_.refs_0_, bf16[128,768]{1,0:T(8,128)(2,1)S(1)} %get-tuple-element.68.refs_1_.refs_13_.refs_3_, bf16[128,768]{1,0:T(8,128)(2,1)S(1)} %collective-permute-done.13.refs_2_.refs_5_, ...), custom_call_target="tpu_custom_call" | custom-call | flops 1107296 | bytes 5490 | tf_op jit(solution)/shard_map/attend_partner/pallas_call | solution.py:77
  40.9 2.9 %collective-permute-start.21 = (bf16[144,768]{1,0:T(8,128)(2,1)S(1)}, bf16[144,768]{1,0:T(8,128)(2,1)S(1)}, u32[]{:S(2)}, u32[]{:S(2)}) collective-permute-start(bf16[144,768]{1,0:T(8,128)(2,1)S(1)} %attend_partner.3.refs_15_), channel_id=1, source_target_pairs={{0,16},{4,20},{8,24},{12,28},{16,0},{20,4},{24,8},{28,12},{1,17},{... | collective-permute-start | bytes 663560 | tf_op jit(solution)/shard_map/ppermute | solution.py:33
  43.8 1.1 %fresh_kv.3 = (bf16[256,256]{1,0:T(8,128)(2,1)S(1)}, bf16[256,256]{1,0:T(8,128)(2,1)S(1)}) custom-call(bf16[128,768]{1,0:T(8,128)(2,1)S(1)} %relay.10.refs_12_.refs_0_, bf16[128,768]{1,0:T(8,128)(2,1)S(1)} %relay.11.refs_1_.refs_12_.refs_0_, bf16[128,768]{1,0:T(8,128)(2,1)S(1)} %get-tuple-element.64.refs_1_.refs_13_.refs_2_, ...), custom_call_target="tpu_custom_call" | custom-call | flops 402653 | bytes 2758 | tf_op jit(solution)/shard_map/fresh_kv/pallas_call | solution.py:77
  44.9 2.3 %attend_fresh.1 = (f32[256,768]{1,0:T(8,128)S(1)}, f32[8,256]{1,0:T(8,128)S(1)}) custom-call(bf16[128,768]{1,0:T(8,128)(2,1)S(1)} %get-tuple-element.60.refs_12_.refs_0_, bf16[128,768]{1,0:T(8,128)(2,1)S(1)} %get-tuple-element.67.refs_1_.refs_12_, bf16[256,256]{1,0:T(8,128)(2,1)S(1)} %get-tuple-element.63.refs_1_.refs_2_.refs_0_, ...), custom_call_target="tpu_custom_call" | custom-call | flops 201326 | bytes 856 | tf_op jit(solution)/shard_map/attend_fresh/pallas_call | solution.py:77
  47.2 0.8 %combine.2 = (bf16[128,768]{1,0:T(8,128)(2,1)S(1)}, bf16[128,384]{1,0:T(8,128)(2,1)S(1)}, bf16[128,384]{1,0:T(8,128)(2,1)S(1)}) custom-call(f32[128,768]{1,0:T(8,128)S(1)} %get-tuple-element.58.refs_0_, f32[8,128]{1,0:T(8,128)S(1)} %get-tuple-element.59.refs_1_, f32[256,768]{1,0:T(8,128)S(1)} %get-tuple-element.74.refs_2_, ...), custom_call_target="tpu_custom_call" | custom-call | flops 150994 | bytes 3262 | tf_op jit(solution)/shard_map/combine/pallas_call | solution.py:77
  48.1 0.1 collective-permute-start.18
  48.2 0.5 collective-permute-start.19
  48.7 0.7 %project.2 = (bf16[128,768]{1,0:T(8,128)(2,1)S(1)}, bf16[128,768]{1,0:T(8,128)(2,1)S(1)}, bf16[128,768]{1,0:T(8,128)(2,1)S(1)}) custom-call(bf16[128,768]{1,0:T(8,128)(2,1)S(1)} %get-tuple-element.76.refs_0_, bf16[768,3072]{1,0:T(8,128)(2,1)S(1)} %bitcast.4), custom_call_target="tpu_custom_call" | custom-call | flops 301989 | bytes 2752 | tf_op jit(solution)/shard_map/project/pallas_call | solution.py:77
  49.4 0.1 collective-permute-done.18.refs_1_
  49.5 0.2 collective-permute-done.19.refs_2_
  49.7 1.0 %collective-permute-start.20 = (bf16[128,768]{1,0:T(8,128)(2,1)S(1)}, bf16[128,768]{1,0:T(8,128)(2,1)S(1)}, u32[]{:S(2)}, u32[]{:S(2)}) collective-permute-start(bf16[128,768]{1,0:T(8,128)(2,1)S(1)} %sum_cores.2.refs_6_), channel_id=1, source_target_pairs={{0,2},{1,3},{2,0},{3,1},{4,6},{5,7},{6,4},{7,5},{8,10},{9,11},{10,... | collective-permute-start | bytes 589832 | tf_op jit(solution)/shard_map/ppermute | solution.py:33
  50.7 3.6 %collective-permute-done.21.refs_4_ = bf16[144,768]{1,0:T(8,128)(2,1)S(1)} collective-permute-done((bf16[144,768]{1,0:T(8,128)(2,1)S(1)}, bf16[144,768]{1,0:T(8,128)(2,1)S(1)}, u32[]{:S(2)}, u32[]{:S(2)}) %collective-permute-start.21) | collective-permute-done | bytes 221216 | tf_op jit(solution)/shard_map/ppermute | solution.py:33
  54.3 0.8 %combine.3 = (bf16[128,768]{1,0:T(8,128)(2,1)S(1)}, bf16[128,384]{1,0:T(8,128)(2,1)S(1)}, bf16[128,384]{1,0:T(8,128)(2,1)S(1)}) custom-call(f32[128,768]{1,0:T(8,128)S(1)} %get-tuple-element.82.refs_0_, f32[8,128]{1,0:T(8,128)S(1)} %get-tuple-element.83.refs_1_, f32[256,768]{1,0:T(8,128)S(1)} %get-tuple-element.74.refs_2_, ...), custom_call_target="tpu_custom_call" | custom-call | flops 150994 | bytes 3262 | tf_op jit(solution)/shard_map/combine/pallas_call | solution.py:77
  55.1 0.1 collective-permute-start.23
  55.2 0.5 collective-permute-start.24
  55.7 0.1 collective-permute-start.17
  55.8 0.7 %project.3 = (bf16[128,768]{1,0:T(8,128)(2,1)S(1)}, bf16[128,768]{1,0:T(8,128)(2,1)S(1)}, bf16[128,768]{1,0:T(8,128)(2,1)S(1)}) custom-call(bf16[128,768]{1,0:T(8,128)(2,1)S(1)} %get-tuple-element.84.refs_0_, bf16[768,3072]{1,0:T(8,128)(2,1)S(1)} %bitcast.4), custom_call_target="tpu_custom_call" | custom-call | flops 301989 | bytes 2752 | tf_op jit(solution)/shard_map/project/pallas_call | solution.py:77
  56.5 0.5 collective-permute-start.22
  57.0 1.1 %collective-permute-start.25 = (bf16[128,768]{1,0:T(8,128)(2,1)S(1)}, bf16[128,768]{1,0:T(8,128)(2,1)S(1)}, u32[]{:S(2)}, u32[]{:S(2)}) collective-permute-start(bf16[128,768]{1,0:T(8,128)(2,1)S(1)} %sum_cores.3.refs_7_), channel_id=1, source_target_pairs={{0,2},{1,3},{2,0},{3,1},{4,6},{5,7},{6,4},{7,5},{8,10},{9,11},{10,... | collective-permute-start | bytes 589832 | tf_op jit(solution)/shard_map/ppermute | solution.py:33
  58.1 2.2 %update_caches.1 = (bf16[2048,256]{1,0:T(8,128)(2,1)}, bf16[2048,256]{1,0:T(8,128)(2,1)}, f32[8,128]{1,0:T(8,128)S(1)}) custom-call(bf16[256,256]{1,0:T(8,128)(2,1)S(1)} %get-tuple-element.63.refs_1_.refs_2_.refs_0_, bf16[256,256]{1,0:T(8,128)(2,1)S(1)} %get-tuple-element.71.refs_3_.refs_1_, bf16[256,256]{1,0:T(8,128)(2,1)S(1)} %get-tuple-element.72.refs_4_.refs_2_, ...), custom_call_target="tpu_custom_call" | custom-call | flops 67108 | bytes 2361 | tf_op jit(solution)/shard_map/update_caches/pallas_call | solution.py:77
  60.3 3.6 %collective-permute-done.25.refs_5_ = bf16[128,768]{1,0:T(8,128)(2,1)S(1)} collective-permute-done((bf16[128,768]{1,0:T(8,128)(2,1)S(1)}, bf16[128,768]{1,0:T(8,128)(2,1)S(1)}, u32[]{:S(2)}, u32[]{:S(2)}) %collective-permute-start.25) | collective-permute-done | bytes 196640 | tf_op jit(solution)/shard_map/ppermute | solution.py:33
  64.0 0.9 %finish.1 = bf16[256,768]{1,0:T(8,128)(2,1)} custom-call(bf16[128,768]{1,0:T(8,128)(2,1)S(1)} %get-tuple-element.77.refs_0_, bf16[128,768]{1,0:T(8,128)(2,1)S(1)} %collective-permute-done.17.refs_1_, bf16[128,768]{1,0:T(8,128)(2,1)S(1)} %collective-permute-done.20.refs_4_.refs_2_, bf16[128,768]{1,0:T(8,128)(2,1)S(1)} %get-tuple-element.85.refs_3_, ...), custom_call_target="tpu_custom_call" | custom-call | flops 98 | bytes 786 | tf_op jit(solution)/shard_map/finish/pallas_call | solution.py:77
  (55 shorter events, 0.6 us)
Async XLA Ops:
  0.6 12.4 %collective-permute-start = (bf16[256,768]{1,0:T(8,128)(2,1)}, bf16[256,768]{1,0:T(8,128)(2,1)S(1)}, u32[]{:S(2)}, u32[]{:S(2)}) collective-permute-start(bf16[256,768]{1,0:T(8,128)(2,1)} %refs_0_.3), channel_id=1, source_target_pairs={{0,2},{1,3},{2,0},{3,1},{4,6},{5,7},{6,4},{7,5},{8,10},{9,11},{10,... | collective-permute-start | bytes 1179656 | tf_op jit(solution)/shard_map/ppermute | solution.py:33
  3.7 14.1 %collective-permute-start.1 = (bf16[256,768]{1,0:T(8,128)(2,1)}, bf16[256,768]{1,0:T(8,128)(2,1)S(1)}, u32[]{:S(2)}, u32[]{:S(2)}) collective-permute-start(bf16[256,768]{1,0:T(8,128)(2,1)} %refs_0_.3), channel_id=1, source_target_pairs={{0,1},{1,0},{2,3},{3,2},{4,5},{5,4},{6,7},{7,6},{8,9},{9,8},{10,11... | collective-permute-start | bytes 1179656 | tf_op jit(solution)/shard_map/ppermute | solution.py:38
  3.7 1.0 %copy-start.5 = (bf16[256,768]{1,0:T(8,128)(2,1)S(1)}, bf16[256,768]{1,0:T(8,128)(2,1)}, u32[]{:S(2)}) copy-start(bf16[256,768]{1,0:T(8,128)(2,1)} %refs_0_.3) | copy-start | bytes 1179652
  4.7 2.7 %copy-start.6 = (s32[4]{0:T(128)S(1)}, s32[4]{0:T(128)}, u32[]{:S(2)}) copy-start(s32[4]{0:T(128)} %refs_6_.7) | copy-start | bytes 52
  4.8 2.7 %copy-start.7 = (s32[4]{0:T(128)S(1)}, s32[4]{0:T(128)}, u32[]{:S(2)}) copy-start(s32[4]{0:T(128)} %refs_1_.4) | copy-start | bytes 52
  4.8 4.3 %copy-start.2 = (bf16[2048,256]{1,0:T(8,128)(2,1)S(1)}, bf16[2048,256]{1,0:T(8,128)(2,1)}, u32[]{:S(2)}) copy-start(bf16[2048,256]{1,0:T(8,128)(2,1)} %refs_4_.1) | copy-start | bytes 3145732
  4.8 4.3 %copy-start.3 = (bf16[2048,256]{1,0:T(8,128)(2,1)S(1)}, bf16[2048,256]{1,0:T(8,128)(2,1)}, u32[]{:S(2)}) copy-start(bf16[2048,256]{1,0:T(8,128)(2,1)} %refs_5_.5) | copy-start | bytes 3145732
  4.8 12.5 %collective-permute-start.4 = (bf16[128,768]{1,0:T(8,128)(2,1)S(1)}, bf16[128,768]{1,0:T(8,128)(2,1)S(1)}, u32[]{:S(2)}, u32[]{:S(2)}) collective-permute-start(bf16[128,768]{1,0:T(8,128)(2,1)S(1)} %get-tuple-element.57), channel_id=1, source_target_pairs={{0,16},{4,20},{8,24},{12,28},{16,0},{20,4},{24,8},{28,12},{1,17},{... | collective-permute-start | bytes 589832 | tf_op jit(solution)/shard_map/ppermute | solution.py:33
  7.4 11.8 %slice-start = ((s8[4718592]{0:T(1024)(128)(4,1)}), s8[4194304]{0:T(1024)(128)(4,1)S(1)}, s32[]{:S(2)}) async-start(s8[4718592]{0:T(1024)(128)(4,1)} %bitcast.1), calls=%async_computation | async-start | bytes 8388608
  7.5 11.7 %slice-start.1 = ((s8[4718592]{0:T(1024)(128)(4,1)}), s8[524288]{0:T(1024)(128)(4,1)S(1)}, s32[]{:S(2)}) async-start(s8[4718592]{0:T(1024)(128)(4,1)} %bitcast.1), calls=%async_computation.1 | async-start | bytes 1048576
  13.0 6.3 %copy-start.4 = (f32[3072]{0:T(1024)S(1)}, f32[3072]{0:T(1024)}, u32[]{:S(2)}) copy-start(f32[3072]{0:T(1024)} %param.11) | copy-start | bytes 36868
  13.1 5.2 %collective-permute-start.2 = (bf16[64,768]{1,0:T(8,128)(2,1)S(1)}, bf16[64,768]{1,0:T(8,128)(2,1)S(1)}, u32[]{:S(2)}, u32[]{:S(2)}) collective-permute-start(bf16[64,768]{1,0:T(8,128)(2,1)S(1)} %get-tuple-element.53), channel_id=1, source_target_pairs={{0,1},{1,0},{2,3},{3,2},{4,5},{5,4},{6,7},{7,6},{8,9},{9,8},{10,11... | collective-permute-start | bytes 294920 | tf_op jit(solution)/shard_map/ppermute | solution.py:38
  13.1 12.6 %collective-permute-start.8 = (bf16[128,768]{1,0:T(8,128)(2,1)S(1)}, bf16[128,768]{1,0:T(8,128)(2,1)S(1)}, u32[]{:S(2)}, u32[]{:S(2)}) collective-permute-start(bf16[128,768]{1,0:T(8,128)(2,1)S(1)} %relay.8.refs_1_), channel_id=1, source_target_pairs={{0,16},{4,20},{8,24},{12,28},{16,0},{20,4},{24,8},{28,12},{1,17},{... | collective-permute-start | bytes 589832 | tf_op jit(solution)/shard_map/ppermute | solution.py:33
  17.3 8.5 %collective-permute-start.7 = (bf16[128,768]{1,0:T(8,128)(2,1)S(1)}, bf16[128,768]{1,0:T(8,128)(2,1)S(1)}, u32[]{:S(2)}, u32[]{:S(2)}) collective-permute-start(bf16[128,768]{1,0:T(8,128)(2,1)S(1)} %relay.10.refs_12_.refs_0_), channel_id=1, source_target_pairs={{0,2},{1,3},{2,0},{3,1},{4,6},{5,7},{6,4},{7,5},{8,10},{9,11},{10,... | collective-permute-start | bytes 589832 | tf_op jit(solution)/shard_map/ppermute | solution.py:33
  17.8 1.3 %collective-permute-start.3 = (bf16[64,768]{1,0:T(8,128)(2,1)S(1)}, bf16[64,768]{1,0:T(8,128)(2,1)S(1)}, u32[]{:S(2)}, u32[]{:S(2)}) collective-permute-start(bf16[64,768]{1,0:T(8,128)(2,1)S(1)} %get-tuple-element.54), channel_id=1, source_target_pairs={{0,1},{1,0},{2,3},{3,2},{4,5},{5,4},{6,7},{7,6},{8,9},{9,8},{10,11... | collective-permute-start | bytes 294920 | tf_op jit(solution)/shard_map/ppermute | solution.py:38
  17.8 5.1 %collective-permute-start.5 = (bf16[64,768]{1,0:T(8,128)(2,1)S(1)}, bf16[64,768]{1,0:T(8,128)(2,1)S(1)}, u32[]{:S(2)}, u32[]{:S(2)}) collective-permute-start(bf16[64,768]{1,0:T(8,128)(2,1)S(1)} %get-tuple-element.61), channel_id=1, source_target_pairs={{0,1},{1,0},{2,3},{3,2},{4,5},{5,4},{6,7},{7,6},{8,9},{9,8},{10,11... | collective-permute-start | bytes 294920 | tf_op jit(solution)/shard_map/ppermute | solution.py:38
  18.3 4.6 %collective-permute-start.6 = (bf16[64,768]{1,0:T(8,128)(2,1)S(1)}, bf16[64,768]{1,0:T(8,128)(2,1)S(1)}, u32[]{:S(2)}, u32[]{:S(2)}) collective-permute-start(bf16[64,768]{1,0:T(8,128)(2,1)S(1)} %get-tuple-element.62), channel_id=1, source_target_pairs={{0,1},{1,0},{2,3},{3,2},{4,5},{5,4},{6,7},{7,6},{8,9},{9,8},{10,11... | collective-permute-start | bytes 294920 | tf_op jit(solution)/shard_map/ppermute | solution.py:38
  19.1 8.9 %collective-permute-start.9 = (bf16[128,768]{1,0:T(8,128)(2,1)S(1)}, bf16[128,768]{1,0:T(8,128)(2,1)S(1)}, u32[]{:S(2)}, u32[]{:S(2)}) collective-permute-start(bf16[128,768]{1,0:T(8,128)(2,1)S(1)} %relay.10.refs_12_.refs_0_), channel_id=1, source_target_pairs={{0,1},{1,0},{2,3},{3,2},{4,5},{5,4},{6,7},{7,6},{8,9},{9,8},{10,11... | collective-permute-start | bytes 589832 | tf_op jit(solution)/shard_map/ppermute | solution.py:38
  19.3 3.6 %copy-start = (bf16[3072,256]{1,0:T(8,128)(2,1)S(1)}, bf16[3072,256]{1,0:T(8,128)(2,1)}, u32[]{:S(2)}) copy-start(bf16[3072,256]{1,0:T(8,128)(2,1)} %refs_11_.1) | copy-start | bytes 4718596
  19.3 3.6 %copy-start.1 = (bf16[3072,256]{1,0:T(8,128)(2,1)S(1)}, bf16[3072,256]{1,0:T(8,128)(2,1)}, u32[]{:S(2)}) copy-start(bf16[3072,256]{1,0:T(8,128)(2,1)} %refs_12_.1) | copy-start | bytes 4718596
  25.8 2.2 %collective-permute-start.10 = (bf16[64,768]{1,0:T(8,128)(2,1)S(1)}, bf16[64,768]{1,0:T(8,128)(2,1)S(1)}, u32[]{:S(2)}, u32[]{:S(2)}) collective-permute-start(bf16[64,768]{1,0:T(8,128)(2,1)S(1)} %get-tuple-element.65), channel_id=1, source_target_pairs={{0,1},{1,0},{2,3},{3,2},{4,5},{5,4},{6,7},{7,6},{8,9},{9,8},{10,11... | collective-permute-start | bytes 294920 | tf_op jit(solution)/shard_map/ppermute | solution.py:38
  25.9 2.1 %collective-permute-start.11 = (bf16[64,768]{1,0:T(8,128)(2,1)S(1)}, bf16[64,768]{1,0:T(8,128)(2,1)S(1)}, u32[]{:S(2)}, u32[]{:S(2)}) collective-permute-start(bf16[64,768]{1,0:T(8,128)(2,1)S(1)} %get-tuple-element.66), channel_id=1, source_target_pairs={{0,1},{1,0},{2,3},{3,2},{4,5},{5,4},{6,7},{7,6},{8,9},{9,8},{10,11... | collective-permute-start | bytes 294920 | tf_op jit(solution)/shard_map/ppermute | solution.py:38
  26.4 9.1 %collective-permute-start.12 = (bf16[128,768]{1,0:T(8,128)(2,1)S(1)}, bf16[128,768]{1,0:T(8,128)(2,1)S(1)}, u32[]{:S(2)}, u32[]{:S(2)}) collective-permute-start(bf16[128,768]{1,0:T(8,128)(2,1)S(1)} %relay.11.refs_1_.refs_12_.refs_0_), channel_id=1, source_target_pairs={{0,2},{1,3},{2,0},{3,1},{4,6},{5,7},{6,4},{7,5},{8,10},{9,11},{10,... | collective-permute-start | bytes 589832 | tf_op jit(solution)/shard_map/ppermute | solution.py:33
  31.6 15.7 %collective-permute-start.16 = (bf16[144,768]{1,0:T(8,128)(2,1)S(1)}, bf16[144,768]{1,0:T(8,128)(2,1)S(1)}, u32[]{:S(2)}, u32[]{:S(2)}) collective-permute-start(bf16[144,768]{1,0:T(8,128)(2,1)S(1)} %attend_partner.2.refs_14_), channel_id=1, source_target_pairs={{0,16},{4,20},{8,24},{12,28},{16,0},{20,4},{24,8},{28,12},{1,17},{... | collective-permute-start | bytes 663560 | tf_op jit(solution)/shard_map/ppermute | solution.py:33
  31.6 4.5 %collective-permute-start.13 = (bf16[128,768]{1,0:T(8,128)(2,1)S(1)}, bf16[128,768]{1,0:T(8,128)(2,1)S(1)}, u32[]{:S(2)}, u32[]{:S(2)}) collective-permute-start(bf16[128,768]{1,0:T(8,128)(2,1)S(1)} %relay.11.refs_1_.refs_12_.refs_0_), channel_id=1, source_target_pairs={{0,1},{1,0},{2,3},{3,2},{4,5},{5,4},{6,7},{7,6},{8,9},{9,8},{10,11... | collective-permute-start | bytes 589832 | tf_op jit(solution)/shard_map/ppermute | solution.py:38
  35.5 1.5 %collective-permute-start.14 = (bf16[64,768]{1,0:T(8,128)(2,1)S(1)}, bf16[64,768]{1,0:T(8,128)(2,1)S(1)}, u32[]{:S(2)}, u32[]{:S(2)}) collective-permute-start(bf16[64,768]{1,0:T(8,128)(2,1)S(1)} %get-tuple-element.69), channel_id=1, source_target_pairs={{0,1},{1,0},{2,3},{3,2},{4,5},{5,4},{6,7},{7,6},{8,9},{9,8},{10,11... | collective-permute-start | bytes 294920 | tf_op jit(solution)/shard_map/ppermute | solution.py:38
  36.1 1.3 %collective-permute-start.15 = (bf16[64,768]{1,0:T(8,128)(2,1)S(1)}, bf16[64,768]{1,0:T(8,128)(2,1)S(1)}, u32[]{:S(2)}, u32[]{:S(2)}) collective-permute-start(bf16[64,768]{1,0:T(8,128)(2,1)S(1)} %get-tuple-element.70), channel_id=1, source_target_pairs={{0,1},{1,0},{2,3},{3,2},{4,5},{5,4},{6,7},{7,6},{8,9},{9,8},{10,11... | collective-permute-start | bytes 294920 | tf_op jit(solution)/shard_map/ppermute | solution.py:38
  37.4 9.9 %slice-start.2 = ((s8[4718592]{0:T(1024)(128)(4,1)}), s8[4194304]{0:T(1024)(128)(4,1)S(1)}, s32[]{:S(2)}) async-start(s8[4718592]{0:T(1024)(128)(4,1)} %bitcast.3), calls=%async_computation.2 | async-start | bytes 8388608
  37.4 9.9 %slice-start.3 = ((s8[4718592]{0:T(1024)(128)(4,1)}), s8[524288]{0:T(1024)(128)(4,1)S(1)}, s32[]{:S(2)}) async-start(s8[4718592]{0:T(1024)(128)(4,1)} %bitcast.3), calls=%async_computation.3 | async-start | bytes 1048576
  40.9 13.4 %collective-permute-start.21 = (bf16[144,768]{1,0:T(8,128)(2,1)S(1)}, bf16[144,768]{1,0:T(8,128)(2,1)S(1)}, u32[]{:S(2)}, u32[]{:S(2)}) collective-permute-start(bf16[144,768]{1,0:T(8,128)(2,1)S(1)} %attend_partner.3.refs_15_), channel_id=1, source_target_pairs={{0,16},{4,20},{8,24},{12,28},{16,0},{20,4},{24,8},{28,12},{1,17},{... | collective-permute-start | bytes 663560 | tf_op jit(solution)/shard_map/ppermute | solution.py:33
  48.1 1.4 %collective-permute-start.18 = (bf16[128,384]{1,0:T(8,128)(2,1)S(1)}, bf16[128,384]{1,0:T(8,128)(2,1)S(1)}, u32[]{:S(2)}, u32[]{:S(2)}) collective-permute-start(bf16[128,384]{1,0:T(8,128)(2,1)S(1)} %get-tuple-element.80), channel_id=1, source_target_pairs={{0,1},{1,0},{2,3},{3,2},{4,5},{5,4},{6,7},{7,6},{8,9},{9,8},{10,11... | collective-permute-start | bytes 294920 | tf_op jit(solution)/shard_map/ppermute | solution.py:38
  48.2 1.4 %collective-permute-start.19 = (bf16[128,384]{1,0:T(8,128)(2,1)S(1)}, bf16[128,384]{1,0:T(8,128)(2,1)S(1)}, u32[]{:S(2)}, u32[]{:S(2)}) collective-permute-start(bf16[128,384]{1,0:T(8,128)(2,1)S(1)} %get-tuple-element.81), channel_id=1, source_target_pairs={{0,1},{1,0},{2,3},{3,2},{4,5},{5,4},{6,7},{7,6},{8,9},{9,8},{10,11... | collective-permute-start | bytes 294920 | tf_op jit(solution)/shard_map/ppermute | solution.py:38
  49.7 7.3 %collective-permute-start.20 = (bf16[128,768]{1,0:T(8,128)(2,1)S(1)}, bf16[128,768]{1,0:T(8,128)(2,1)S(1)}, u32[]{:S(2)}, u32[]{:S(2)}) collective-permute-start(bf16[128,768]{1,0:T(8,128)(2,1)S(1)} %sum_cores.2.refs_6_), channel_id=1, source_target_pairs={{0,2},{1,3},{2,0},{3,1},{4,6},{5,7},{6,4},{7,5},{8,10},{9,11},{10,... | collective-permute-start | bytes 589832 | tf_op jit(solution)/shard_map/ppermute | solution.py:33
  55.1 1.8 %collective-permute-start.23 = (bf16[128,384]{1,0:T(8,128)(2,1)S(1)}, bf16[128,384]{1,0:T(8,128)(2,1)S(1)}, u32[]{:S(2)}, u32[]{:S(2)}) collective-permute-start(bf16[128,384]{1,0:T(8,128)(2,1)S(1)} %get-tuple-element.88), channel_id=1, source_target_pairs={{0,1},{1,0},{2,3},{3,2},{4,5},{5,4},{6,7},{7,6},{8,9},{9,8},{10,11... | collective-permute-start | bytes 294920 | tf_op jit(solution)/shard_map/ppermute | solution.py:38
  55.2 1.8 %collective-permute-start.24 = (bf16[128,384]{1,0:T(8,128)(2,1)S(1)}, bf16[128,384]{1,0:T(8,128)(2,1)S(1)}, u32[]{:S(2)}, u32[]{:S(2)}) collective-permute-start(bf16[128,384]{1,0:T(8,128)(2,1)S(1)} %get-tuple-element.89), channel_id=1, source_target_pairs={{0,1},{1,0},{2,3},{3,2},{4,5},{5,4},{6,7},{7,6},{8,9},{9,8},{10,11... | collective-permute-start | bytes 294920 | tf_op jit(solution)/shard_map/ppermute | solution.py:38
  55.7 4.6 %collective-permute-start.17 = (bf16[128,768]{1,0:T(8,128)(2,1)S(1)}, bf16[128,768]{1,0:T(8,128)(2,1)S(1)}, u32[]{:S(2)}, u32[]{:S(2)}) collective-permute-start(bf16[128,768]{1,0:T(8,128)(2,1)S(1)} %get-tuple-element.78.refs_3_), channel_id=1, source_target_pairs={{0,1},{1,0},{2,3},{3,2},{4,5},{5,4},{6,7},{7,6},{8,9},{9,8},{10,11... | collective-permute-start | bytes 589832 | tf_op jit(solution)/shard_map/ppermute | solution.py:38
  56.5 3.9 %collective-permute-start.22 = (bf16[128,768]{1,0:T(8,128)(2,1)S(1)}, bf16[128,768]{1,0:T(8,128)(2,1)S(1)}, u32[]{:S(2)}, u32[]{:S(2)}) collective-permute-start(bf16[128,768]{1,0:T(8,128)(2,1)S(1)} %get-tuple-element.86.refs_3_), channel_id=1, source_target_pairs={{0,1},{1,0},{2,3},{3,2},{4,5},{5,4},{6,7},{7,6},{8,9},{9,8},{10,11... | collective-permute-start | bytes 589832 | tf_op jit(solution)/shard_map/ppermute | solution.py:38
  57.0 6.9 %collective-permute-start.25 = (bf16[128,768]{1,0:T(8,128)(2,1)S(1)}, bf16[128,768]{1,0:T(8,128)(2,1)S(1)}, u32[]{:S(2)}, u32[]{:S(2)}) collective-permute-start(bf16[128,768]{1,0:T(8,128)(2,1)S(1)} %sum_cores.3.refs_7_), channel_id=1, source_target_pairs={{0,2},{1,3},{2,0},{3,1},{4,6},{5,7},{6,4},{7,5},{8,10},{9,11},{10,... | collective-permute-start | bytes 589832 | tf_op jit(solution)/shard_map/ppermute | solution.py:33

commit v13 on v10

--- a/solution.py
+++ b/solution.py
@@ -14,6 +14,7 @@
 ROW_TILE = 16
 CORES = 2
 CHUNKS = 2
+SLOT_TILES = 4
 COST_WEIGHT = 0.0005
 FIRST_MICROS = 2
 FLOPS_PER_MICRO = 1_000_000_000
@@ -21,6 +22,7 @@
 
 rope_base = 500000.0
 neg_large = -1e30
+least_sum = 2.0**-90
 log2_scale = math.log2(math.e) / math.sqrt(HD)
 
 VMEM = pl.BlockSpec(memory_space=pltpu.VMEM)
@@ -163,7 +165,8 @@
     )
 
 
-def widen_kernel(keys, values, mark, lengths_in, wide_keys, wide_values, lengths, semaphore):
+def widen_kernel(keys, values, mark, lengths_in, wide_keys, wide_values, norms, *scratch):
+    lengths, semaphore = scratch
     number = pltpu.make_async_copy(lengths_in, lengths, semaphore)
     number.start()
     slots = keys.shape[0]
@@ -177,9 +180,16 @@
     request, position_in = place_of(lengths.shape[0])
     slot = lax.broadcasted_iota(jnp.int32, (slots, LANES), 0) + position_in * slots
     lane = lax.broadcasted_iota(jnp.int32, (slots, LANES), 1)
-    bias = jnp.where((lane == 0) & (slot >= lengths[request]), neg_large, 0.0).astype(jnp.bfloat16)
+    bias = jnp.where((lane == 0) & (slot >= lengths[request]), neg_large, 0.0)
+    bias = jnp.where(lane == 1, 1.0, bias).astype(jnp.bfloat16)
+    visible = slot[:, :1] < lengths[request]
+    norms[...] = jnp.full(norms.shape, -1.0, norms.dtype)
     for head in range(heads):
         wide_keys[head, :, HD:] = bias
+        key = keys[:, head * HD : (head + 1) * HD].astype(jnp.float32)
+        squares = jnp.where(visible, jnp.sum(key * key, -1, keepdims=True), -1.0)
+        largest = jnp.max(squares, 0, keepdims=True)
+        norms[head : head + 1] = jnp.broadcast_to(largest, (1, LANES))
 
 
 def widen(keys, values, mark, lengths, earlier):
@@ -187,7 +197,7 @@
     wide = jax.ShapeDtypeStruct((width // HD, slots, HD + LANES), jnp.bfloat16)
     return call(
         widen_kernel,
-        [wide, wide],
+        [wide, wide, jax.ShapeDtypeStruct((STAT_ROWS, LANES), jnp.float32)],
         [keys, values, mark, lengths],
         12,
         0,
@@ -252,7 +262,7 @@
 
 def attend_kernel(counts, own, row_at, rows, table_at, *refs):
     blocks, refs = split_refs(counts, refs)
-    gain, w_query, cosine, sine, wide_keys, wide_values, mark, *outputs = refs
+    gain, w_query, cosine, sine, wide_keys, wide_values, norms, mark, *outputs = refs
     pieces = [rows_of(one, row_at, rows) for one in blocks]
     (product,) = project_normed(pieces, gain, [w_query])
     cosine = cosine[table_at : table_at + rows]
@@ -265,54 +275,80 @@
         )
         for head in range(kv_heads * repeat)
     ]
-    step = min(rows, LANES)
-    mark = mark[: repeat * step]
-    tiles = [(head, at) for head in range(kv_heads) for at in range(0, rows, step)]
-
-    def scores_of(head, at):
-        stacked = jnp.concatenate(
-            [query[at : at + step] for query in queries[head * repeat : (head + 1) * repeat]], 0
-        )
-        return dot_transposed(jnp.concatenate([stacked, mark], 1), wide_keys[head])
-
-    columns = {}
-    following = scores_of(*tiles[0])
-    for index, (head, at) in enumerate(tiles):
-        scores = following
-        if index + 1 < len(tiles):
-            following = scores_of(*tiles[index + 1])
-        largest = jnp.max(scores, -1, keepdims=True)
-        weights = jnp.exp2(scores - largest).astype(jnp.bfloat16)
-        summed = dot(weights, wide_values[head])
-        denominator = summed[:, HD : HD + 1]
-        result = summed[:, :HD] / denominator
-        logs = largest + jnp.log2(denominator)
-        for turn in range(repeat):
-            part = slice(turn * step, (turn + 1) * step)
-            to = slice((head * repeat + turn) * HD, (head * repeat + turn + 1) * HD)
-            outputs[0][at : at + step, to] = result[part].astype(outputs[0].dtype)
-            columns.setdefault(head * repeat + turn, []).append(logs[part])
-    stats = stat_rows([jnp.concatenate(parts, 0) for parts in columns.values()], rows)
     if own:
-        outputs[1][...] = stats
         outputs[2][...] = jnp.concatenate(queries, 1)
-        return
-    outputs[0][rows:] = jnp.zeros((ROW_TILE, outputs[0].shape[1]), jnp.bfloat16)
-    rest = jnp.concatenate([stats, jnp.zeros((ROW_TILE - STAT_ROWS, rows), jnp.float32)], 0)
-    for part in range(3):
-        rounded = rest.astype(jnp.bfloat16)
-        outputs[0][rows:, part * rows : (part + 1) * rows] = rounded
-        rest = rest - rounded.astype(jnp.float32)
+    ones = mark[: repeat * rows]
+    second = lax.broadcasted_iota(jnp.int32, ones.shape, 1) == 1
+    stacked = [
+        jnp.concatenate(queries[head * repeat : (head + 1) * repeat], 0) for head in range(kv_heads)
+    ]
+
+    def store(summed, shifts):
+        columns = []
+        for head in range(kv_heads):
+            denominator = summed[head][:, HD : HD + 1]
+            seen = denominator > 0.0
+            result = summed[head][:, :HD] / jnp.where(seen, denominator, 1.0)
+            logs = shifts[head] + jnp.log2(jnp.where(seen, denominator, 1.0))
+            logs = jnp.where(seen, logs, neg_large)
+            for turn in range(repeat):
+                part = slice(turn * rows, (turn + 1) * rows)
+                at = (head * repeat + turn) * HD
+                outputs[0][:rows, at : at + HD] = result[part].astype(outputs[0].dtype)
+                columns.append(logs[part])
+        stats = stat_rows(columns, rows)
+        if own:
+            outputs[1][...] = stats
+            return
+        outputs[0][rows:] = jnp.zeros((ROW_TILE, outputs[0].shape[1]), jnp.bfloat16)
+        rest = jnp.concatenate([stats, jnp.zeros((ROW_TILE - STAT_ROWS, rows), jnp.float32)], 0)
+        for part in range(3):
+            rounded = rest.astype(jnp.bfloat16)
+            outputs[0][rows:, part * rows : (part + 1) * rows] = rounded
+            rest = rest - rounded.astype(jnp.float32)
+
+    summed = []
+    shifts = []
+    slots = wide_keys.shape[1] // SLOT_TILES
+    for head in range(kv_heads):
+        wide = stacked[head].astype(jnp.float32)
+        square = jnp.sum(wide * wide, -1, keepdims=True)
+        bound = jnp.sqrt(square * jnp.maximum(norms[head : head + 1, :1], 0.0))
+        shift = bound.astype(jnp.bfloat16).astype(jnp.float32)
+        added = jnp.where(second, -shift, ones.astype(jnp.float32)).astype(jnp.bfloat16)
+        wide = jnp.concatenate([stacked[head], added], 1)
+        total = 0.0
+        for at in range(0, slots * SLOT_TILES, slots):
+            scores = dot_transposed(wide, wide_keys[head, at : at + slots])
+            weights = jnp.exp2(scores).astype(jnp.bfloat16)
+            total = total + dot(weights, wide_values[head, at : at + slots])
+        summed.append(total)
+        shifts.append(shift)
+    store(summed, shifts)
+    least = functools.reduce(
+        jnp.minimum, [jnp.min(total[:, HD : HD + 1]) for total in summed]
+    )
+
+    @pl.when((least < least_sum) & (jnp.max(norms[...]) >= 0.0))
+    def _():
+        exact = []
+        largest = []
+        for head in range(kv_heads):
+            scores = dot_transposed(jnp.concatenate([stacked[head], ones], 1), wide_keys[head])
+            largest.append(jnp.max(scores, -1, keepdims=True))
+            weights = jnp.exp2(scores - largest[head]).astype(jnp.bfloat16)
+            exact.append(dot(weights, wide_values[head]))
+        store(exact, largest)
 
 
 def attend(
-    pieces, gain, w_query, tables, wide_keys, wide_values, mark, own, row_at, rows, table_at,
+    pieces, gain, w_query, tables, wides, mark, own, row_at, rows, table_at,
     earlier,
 ):
     counts = [len(blocks) for blocks in pieces]
     flat = [block for blocks in pieces for block in blocks]
     out_width = w_query.shape[1]
-    slots = wide_keys.shape[1]
+    slots = wides[0].shape[1]
     if own:
         out_shape = [
             jax.ShapeDtypeStruct((rows, out_width), jnp.float32),
@@ -324,7 +360,7 @@
     return call(
         functools.partial(attend_kernel, counts, own, row_at, rows, table_at),
         out_shape,
-        [*flat, gain, w_query, *tables, wide_keys, wide_values, mark],
+        [*flat, gain, w_query, *tables, *wides, mark],
         28,
         2 * rows * out_width * (w_query.shape[0] + 4 * slots),
         rows * out_width // HD * slots,
@@ -627,12 +663,12 @@
 
     mark = marks(keys_cache.shape[0])
     tables = rope_tables(cached_lengths, rope_offsets, groups, rows, [mark])
-    wide_keys, wide_values = widen(keys_cache, values_cache, mark, cached_lengths, tables[:1])
+    wides = widen(keys_cache, values_cache, mark, cached_lengths, tables[:1])
 
     def attend_rows(pieces, own, chunk, turn, earlier):
         at = chunk * chunk_rows
         return attend(
-            pieces, gain, w_query, tables, wide_keys, wide_values, mark, own, at if own else 0,
+            pieces, gain, w_query, tables, wides, mark, own, at if own else 0,
             chunk_rows, turn * rows + at, earlier,
         )
 
@@ -641,7 +677,7 @@
     crossed = other_core(tokens)
     own, early, late = relay([tokens], [rows, chunk_rows, rows - chunk_rows], [])
     first = [shifted(early, "seq", turn * requests) for turn in range(1, groups)]
-    (late,) = relay([late], [rows - chunk_rows], from_chips + [wide_keys])
+    (late,) = relay([late], [rows - chunk_rows], from_chips + [wides[0]])
     second = [shifted(late, "seq", turn * requests) for turn in range(1, groups)]
     own_cuts = [relay([piece], [rows, half, half, rows - chunk_rows], [late]) for piece in from_chips]
     own_pieces = [[own]] + [[cut[0]] for cut in own_cuts] + [[crossed]]

time: 64.9 us -> 76 us (1.17)
  Pallas kernels: 27.7 us -> 41 us
  starting transfers between devices: 19.4 us -> 16.9 us
    pallas_call x25, Pallas kernels: 27.7 us -> 41 us  [call(): pl.pallas_call(body, out_shape=out_shape, in_specs=[VMEM] * len(arrays) +...]
    ppermute x9, starting transfers between devices: 15.7 us -> 13.2 us  [shifted(): lax.ppermute(shard, axis, [(i, (i + by) % devices) for i in range(devices)])]
  transfers between devices with their start and end apart: 25 -> 25, of which waited for: 10 -> 9; matrix products, arithmetic and copies ran while one was open for 0% -> 0% of each run, Pallas kernels for 41% -> 53%
where the time goes in v13:
time: 76 us; the launch traced here: 75.7 us
  Pallas kernels  41 us (54%)
  starting transfers between devices  16.9 us (22%)
  waiting for transfers between devices  15.8 us (21%)
  local copies, waits for them, and re-layouts  1.09 us (1%)
  between operations  1 us (1%)
    pallas_call x25, Pallas kernels, call(): pl.pallas_call(body, out_shape=out_shape, in_specs=[VMEM] * len(arrays) +...  41 us
    ppermute x9, waiting for transfers between devices, shifted(): lax.ppermute(shard, axis, [(i, (i + by) % devices) for i in range(devices)])  13.5 us
    ppermute x9, starting transfers between devices, shifted(): lax.ppermute(shard, axis, [(i, (i + by) % devices) for i in range(devices)])  13.2 us
    ppermute x16, starting transfers between devices, other_core(): return lax.ppermute(shard, 'head', [(i, i ^ 1) for i in range(devices)])  3.75 us
    ppermute x16, waiting for transfers between devices, other_core(): return lax.ppermute(shard, 'head', [(i, i ^ 1) for i in range(devices)])  2.29 us
  transfers between devices with their start and end apart: 25, of which 9 were waited for; matrix products, arithmetic and copies ran while one was open for 0% of the time, Pallas kernels for 53%

profile of v13, /device:TPU:0, one launch (start us, length us, event | category | flops | bytes accessed | tf_op | source)
XLA Modules:
  0.0 75.7 jit_solution(11270299981310156887)
XLA Ops:
  0.6 3.0 %collective-permute-start = (bf16[256,768]{1,0:T(8,128)(2,1)}, bf16[256,768]{1,0:T(8,128)(2,1)S(1)}, u32[]{:S(2)}, u32[]{:S(2)}) collective-permute-start(bf16[256,768]{1,0:T(8,128)(2,1)} %refs_0_.3), channel_id=1, source_target_pairs={{0,2},{1,3},{2,0},{3,1},{4,6},{5,7},{6,4},{7,5},{8,10},{9,11},{10,... | collective-permute-start | bytes 1179656 | tf_op jit(solution)/shard_map/ppermute | solution.py:34
  3.7 1.0 %copy-done.5 = bf16[256,768]{1,0:T(8,128)(2,1)S(1)} copy-done((bf16[256,768]{1,0:T(8,128)(2,1)S(1)}, bf16[256,768]{1,0:T(8,128)(2,1)}, u32[]{:S(2)}) %copy-start.5) | copy-done | bytes 393240
  4.8 2.7 %collective-permute-start.4 = (bf16[128,768]{1,0:T(8,128)(2,1)S(1)}, bf16[128,768]{1,0:T(8,128)(2,1)S(1)}, u32[]{:S(2)}, u32[]{:S(2)}) collective-permute-start(bf16[128,768]{1,0:T(8,128)(2,1)S(1)} %get-tuple-element.58), channel_id=1, source_target_pairs={{0,16},{4,20},{8,24},{12,28},{16,0},{20,4},{24,8},{28,12},{1,17},{... | collective-permute-start | bytes 589832 | tf_op jit(solution)/shard_map/ppermute | solution.py:34
  7.5 1.6 %rope_tables.1 = (f32[512,128]{1,0:T(8,128)S(1)}, f32[512,128]{1,0:T(8,128)S(1)}) custom-call(s32[4]{0:T(128)S(1)} %copy-done.6, s32[4]{0:T(128)S(1)} %copy-done.7, bf16[2048,128]{1,0:T(8,128)(2,1)S(1)} %marks.1.refs_2_.refs_12_.refs_13_), custom_call_target="tpu_custom_call" | custom-call | bytes 262 | tf_op jit(solution)/shard_map/rope_tables/pallas_call | solution.py:78
  9.1 1.2 %widen_caches.1 = (bf16[2,2048,256]{2,1,0:T(8,128)(2,1)S(1)}, bf16[2,2048,256]{2,1,0:T(8,128)(2,1)S(1)}, f32[8,128]{1,0:T(8,128)S(1)}) custom-call(bf16[2048,256]{1,0:T(8,128)(2,1)S(1)} %copy-done.2, bf16[2048,256]{1,0:T(8,128)(2,1)S(1)} %copy-done.3, bf16[2048,128]{1,0:T(8,128)(2,1)S(1)} %marks.1.refs_2_.refs_12_.refs_13_, s32[4]{0:T(128)S(1)} %copy-done.6, ...), custom_call_target="tpu_custom_call" | custom-call | bytes 3409 | tf_op jit(solution)/shard_map/widen_caches/pallas_call | solution.py:78
  10.4 2.6 %collective-permute-done.refs_1_.refs_0_ = bf16[256,768]{1,0:T(8,128)(2,1)S(1)} collective-permute-done((bf16[256,768]{1,0:T(8,128)(2,1)}, bf16[256,768]{1,0:T(8,128)(2,1)S(1)}, u32[]{:S(2)}, u32[]{:S(2)}) %collective-permute-start) | collective-permute-done | bytes 393248 | tf_op jit(solution)/shard_map/ppermute | solution.py:34
  13.0 0.1 relay.9
  13.1 0.1 collective-permute-start.5
  13.1 2.9 %collective-permute-start.7 = (bf16[128,768]{1,0:T(8,128)(2,1)S(1)}, bf16[128,768]{1,0:T(8,128)(2,1)S(1)}, u32[]{:S(2)}, u32[]{:S(2)}) collective-permute-start(bf16[128,768]{1,0:T(8,128)(2,1)S(1)} %relay.8.refs_1_), channel_id=1, source_target_pairs={{0,16},{4,20},{8,24},{12,28},{16,0},{20,4},{24,8},{28,12},{1,17},{... | collective-permute-start | bytes 589832 | tf_op jit(solution)/shard_map/ppermute | solution.py:34
  16.0 1.2 %collective-permute-done.4.refs_0_ = bf16[128,768]{1,0:T(8,128)(2,1)S(1)} collective-permute-done((bf16[128,768]{1,0:T(8,128)(2,1)S(1)}, bf16[128,768]{1,0:T(8,128)(2,1)S(1)}, u32[]{:S(2)}, u32[]{:S(2)}) %collective-permute-start.4) | collective-permute-done | bytes 196640 | tf_op jit(solution)/shard_map/ppermute | solution.py:34
  17.3 0.5 collective-permute-start.6
  17.8 0.5 collective-permute-start.3
  18.3 0.8 %collective-permute-done.2.refs_3_ = bf16[64,768]{1,0:T(8,128)(2,1)S(1)} collective-permute-done((bf16[64,768]{1,0:T(8,128)(2,1)S(1)}, bf16[64,768]{1,0:T(8,128)(2,1)S(1)}, u32[]{:S(2)}, u32[]{:S(2)}) %collective-permute-start.2) | collective-permute-done | bytes 98336 | tf_op jit(solution)/shard_map/ppermute | solution.py:39
  19.1 0.2 collective-permute-start.8
  19.3 6.8 %attend_own.2 = (f32[128,768]{1,0:T(8,128)S(1)}, f32[8,128]{1,0:T(8,128)S(1)}, bf16[128,768]{1,0:T(8,128)(2,1)S(1)}) custom-call(bf16[256,768]{1,0:T(8,128)(2,1)S(1)} %get-tuple-element.48.refs_0_, bf16[256,768]{1,0:T(8,128)(2,1)S(1)} %get-tuple-element.52.refs_1_, bf16[256,768]{1,0:T(8,128)(2,1)S(1)} %collective-permute-done.1.refs_2_, ...), custom_call_target="tpu_custom_call" | custom-call | flops 1107296 | bytes 5974 | tf_op jit(solution)/shard_map/attend_own/pallas_call | solution.py:78
  26.1 1.1 %fresh_kv.2 = (bf16[256,256]{1,0:T(8,128)(2,1)S(1)}, bf16[256,256]{1,0:T(8,128)(2,1)S(1)}) custom-call(bf16[256,768]{1,0:T(8,128)(2,1)S(1)} %get-tuple-element.48.refs_0_, bf16[256,768]{1,0:T(8,128)(2,1)S(1)} %get-tuple-element.52.refs_1_, bf16[256,768]{1,0:T(8,128)(2,1)S(1)} %collective-permute-done.1.refs_2_, ...), custom_call_target="tpu_custom_call" | custom-call | flops 402653 | bytes 2758 | tf_op jit(solution)/shard_map/fresh_kv/pallas_call | solution.py:78
  27.4 0.4 collective-permute-start.9
  27.8 0.1 collective-permute-start.10
  27.9 1.6 %collective-permute-start.11 = (bf16[128,768]{1,0:T(8,128)(2,1)S(1)}, bf16[128,768]{1,0:T(8,128)(2,1)S(1)}, u32[]{:S(2)}, u32[]{:S(2)}) collective-permute-start(bf16[128,768]{1,0:T(8,128)(2,1)S(1)} %relay.11.refs_1_.refs_13_.refs_0_), channel_id=1, source_target_pairs={{0,2},{1,3},{2,0},{3,1},{4,6},{5,7},{6,4},{7,5},{8,10},{9,11},{10,... | collective-permute-start | bytes 589832 | tf_op jit(solution)/shard_map/ppermute | solution.py:34
  29.5 6.7 %attend_partner.2.refs_14_ = bf16[144,768]{1,0:T(8,128)(2,1)S(1)} custom-call(bf16[128,768]{1,0:T(8,128)(2,1)S(1)} %relay.10.refs_13_.refs_0_, bf16[128,768]{1,0:T(8,128)(2,1)S(1)} %get-tuple-element.64.refs_1_.refs_14_.refs_2_, bf16[128,768]{1,0:T(8,128)(2,1)S(1)} %collective-permute-done.8.refs_2_.refs_4_, ...), custom_call_target="tpu_custom_call" | custom-call | flops 1107296 | bytes 5492 | tf_op jit(solution)/shard_map/attend_partner/pallas_call | solution.py:78
  36.2 0.1 collective-permute-start.12
  36.4 6.9 %attend_own.3 = (f32[128,768]{1,0:T(8,128)S(1)}, f32[8,128]{1,0:T(8,128)S(1)}, bf16[128,768]{1,0:T(8,128)(2,1)S(1)}) custom-call(bf16[256,768]{1,0:T(8,128)(2,1)S(1)} %get-tuple-element.48.refs_0_, bf16[256,768]{1,0:T(8,128)(2,1)S(1)} %get-tuple-element.52.refs_1_, bf16[256,768]{1,0:T(8,128)(2,1)S(1)} %collective-permute-done.1.refs_2_, ...), custom_call_target="tpu_custom_call" | custom-call | flops 1107296 | bytes 6072 | tf_op jit(solution)/shard_map/attend_own/pallas_call | solution.py:78
  43.3 0.5 collective-permute-start.13
  43.8 0.1 collective-permute-start.14
  43.9 0.9 %collective-permute-done.13.refs_3_.refs_8_ = bf16[64,768]{1,0:T(8,128)(2,1)S(1)} collective-permute-done((bf16[64,768]{1,0:T(8,128)(2,1)S(1)}, bf16[64,768]{1,0:T(8,128)(2,1)S(1)}, u32[]{:S(2)}, u32[]{:S(2)}) %collective-permute-start.13) | collective-permute-done | bytes 98336 | tf_op jit(solution)/shard_map/ppermute | solution.py:39
  44.7 0.4 collective-permute-done.14.refs_4_.refs_9_
  45.1 6.9 %attend_partner.3.refs_15_ = bf16[144,768]{1,0:T(8,128)(2,1)S(1)} custom-call(bf16[128,768]{1,0:T(8,128)(2,1)S(1)} %relay.11.refs_1_.refs_13_.refs_0_, bf16[128,768]{1,0:T(8,128)(2,1)S(1)} %get-tuple-element.68.refs_1_.refs_14_.refs_3_, bf16[128,768]{1,0:T(8,128)(2,1)S(1)} %collective-permute-done.12.refs_2_.refs_5_, ...), custom_call_target="tpu_custom_call" | custom-call | flops 1107296 | bytes 5492 | tf_op jit(solution)/shard_map/attend_partner/pallas_call | solution.py:78
  52.0 0.1 collective-permute-start.20
  52.0 1.1 %fresh_kv.3 = (bf16[256,256]{1,0:T(8,128)(2,1)S(1)}, bf16[256,256]{1,0:T(8,128)(2,1)S(1)}) custom-call(bf16[128,768]{1,0:T(8,128)(2,1)S(1)} %relay.10.refs_13_.refs_0_, bf16[128,768]{1,0:T(8,128)(2,1)S(1)} %relay.11.refs_1_.refs_13_.refs_0_, bf16[128,768]{1,0:T(8,128)(2,1)S(1)} %get-tuple-element.64.refs_1_.refs_14_.refs_2_, ...), custom_call_target="tpu_custom_call" | custom-call | flops 402653 | bytes 2758 | tf_op jit(solution)/shard_map/fresh_kv/pallas_call | solution.py:78
  53.1 2.3 %attend_fresh.1 = (f32[256,768]{1,0:T(8,128)S(1)}, f32[8,256]{1,0:T(8,128)S(1)}) custom-call(bf16[128,768]{1,0:T(8,128)(2,1)S(1)} %get-tuple-element.61.refs_11_.refs_0_, bf16[128,768]{1,0:T(8,128)(2,1)S(1)} %get-tuple-element.67.refs_1_.refs_13_, bf16[256,256]{1,0:T(8,128)(2,1)S(1)} %get-tuple-element.63.refs_1_.refs_2_.refs_0_, ...), custom_call_target="tpu_custom_call" | custom-call | flops 201326 | bytes 856 | tf_op jit(solution)/shard_map/attend_fresh/pallas_call | solution.py:78
  55.5 0.8 %combine.2 = (bf16[128,768]{1,0:T(8,128)(2,1)S(1)}, bf16[128,384]{1,0:T(8,128)(2,1)S(1)}, bf16[128,384]{1,0:T(8,128)(2,1)S(1)}) custom-call(f32[128,768]{1,0:T(8,128)S(1)} %get-tuple-element.59.refs_0_, f32[8,128]{1,0:T(8,128)S(1)} %get-tuple-element.60.refs_1_, f32[256,768]{1,0:T(8,128)S(1)} %get-tuple-element.74.refs_2_, ...), custom_call_target="tpu_custom_call" | custom-call | flops 150994 | bytes 3262 | tf_op jit(solution)/shard_map/combine/pallas_call | solution.py:78
  56.3 0.2 collective-permute-start.17
  56.5 0.4 collective-permute-start.18
  56.9 0.7 project.2
  57.6 0.1 collective-permute-done.17.refs_1_
  57.7 0.2 collective-permute-done.18.refs_2_
  57.9 1.2 %collective-permute-start.19 = (bf16[128,768]{1,0:T(8,128)(2,1)S(1)}, bf16[128,768]{1,0:T(8,128)(2,1)S(1)}, u32[]{:S(2)}, u32[]{:S(2)}) collective-permute-start(bf16[128,768]{1,0:T(8,128)(2,1)S(1)} %sum_cores.2.refs_6_), channel_id=1, source_target_pairs={{0,2},{1,3},{2,0},{3,1},{4,6},{5,7},{6,4},{7,5},{8,10},{9,11},{10,... | collective-permute-start | bytes 589832 | tf_op jit(solution)/shard_map/ppermute | solution.py:34
  59.1 6.1 %collective-permute-done.20.refs_4_ = bf16[144,768]{1,0:T(8,128)(2,1)S(1)} collective-permute-done((bf16[144,768]{1,0:T(8,128)(2,1)S(1)}, bf16[144,768]{1,0:T(8,128)(2,1)S(1)}, u32[]{:S(2)}, u32[]{:S(2)}) %collective-permute-start.20) | collective-permute-done | bytes 221216 | tf_op jit(solution)/shard_map/ppermute | solution.py:34
  65.1 0.8 %combine.3 = (bf16[128,768]{1,0:T(8,128)(2,1)S(1)}, bf16[128,384]{1,0:T(8,128)(2,1)S(1)}, bf16[128,384]{1,0:T(8,128)(2,1)S(1)}) custom-call(f32[128,768]{1,0:T(8,128)S(1)} %get-tuple-element.82.refs_0_, f32[8,128]{1,0:T(8,128)S(1)} %get-tuple-element.83.refs_1_, f32[256,768]{1,0:T(8,128)S(1)} %get-tuple-element.74.refs_2_, ...), custom_call_target="tpu_custom_call" | custom-call | flops 150994 | bytes 3262 | tf_op jit(solution)/shard_map/combine/pallas_call | solution.py:78
  66.0 0.1 collective-permute-start.22
  66.1 0.5 collective-permute-start.23
  66.6 0.1 collective-permute-start.16
  66.6 0.7 project.3
  67.3 0.5 collective-permute-start.21
  67.9 1.2 %collective-permute-start.24 = (bf16[128,768]{1,0:T(8,128)(2,1)S(1)}, bf16[128,768]{1,0:T(8,128)(2,1)S(1)}, u32[]{:S(2)}, u32[]{:S(2)}) collective-permute-start(bf16[128,768]{1,0:T(8,128)(2,1)S(1)} %sum_cores.3.refs_7_), channel_id=1, source_target_pairs={{0,2},{1,3},{2,0},{3,1},{4,6},{5,7},{6,4},{7,5},{8,10},{9,11},{10,... | collective-permute-start | bytes 589832 | tf_op jit(solution)/shard_map/ppermute | solution.py:34
  69.1 2.2 %update_caches.1 = (bf16[2048,256]{1,0:T(8,128)(2,1)}, bf16[2048,256]{1,0:T(8,128)(2,1)}, f32[8,128]{1,0:T(8,128)S(1)}) custom-call(bf16[256,256]{1,0:T(8,128)(2,1)S(1)} %get-tuple-element.63.refs_1_.refs_2_.refs_0_, bf16[256,256]{1,0:T(8,128)(2,1)S(1)} %get-tuple-element.71.refs_3_.refs_1_, bf16[256,256]{1,0:T(8,128)(2,1)S(1)} %get-tuple-element.72.refs_4_.refs_2_, ...), custom_call_target="tpu_custom_call" | custom-call | flops 67108 | bytes 2361 | tf_op jit(solution)/shard_map/update_caches/pallas_call | solution.py:78
  71.3 3.5 %collective-permute-done.24.refs_5_ = bf16[128,768]{1,0:T(8,128)(2,1)S(1)} collective-permute-done((bf16[128,768]{1,0:T(8,128)(2,1)S(1)}, bf16[128,768]{1,0:T(8,128)(2,1)S(1)}, u32[]{:S(2)}, u32[]{:S(2)}) %collective-permute-start.24) | collective-permute-done | bytes 196640 | tf_op jit(solution)/shard_map/ppermute | solution.py:34
  74.8 0.9 %finish.1 = bf16[256,768]{1,0:T(8,128)(2,1)} custom-call(bf16[128,768]{1,0:T(8,128)(2,1)S(1)} %get-tuple-element.77.refs_0_, bf16[128,768]{1,0:T(8,128)(2,1)S(1)} %collective-permute-done.16.refs_1_, bf16[128,768]{1,0:T(8,128)(2,1)S(1)} %collective-permute-done.19.refs_4_.refs_2_, bf16[128,768]{1,0:T(8,128)(2,1)S(1)} %get-tuple-element.85.refs_3_, ...), custom_call_target="tpu_custom_call" | custom-call | flops 98 | bytes 786 | tf_op jit(solution)/shard_map/finish/pallas_call | solution.py:78
  (53 shorter events, 0.4 us)
Async XLA Ops:
  0.6 12.4 %collective-permute-start = (bf16[256,768]{1,0:T(8,128)(2,1)}, bf16[256,768]{1,0:T(8,128)(2,1)S(1)}, u32[]{:S(2)}, u32[]{:S(2)}) collective-permute-start(bf16[256,768]{1,0:T(8,128)(2,1)} %refs_0_.3), channel_id=1, source_target_pairs={{0,2},{1,3},{2,0},{3,1},{4,6},{5,7},{6,4},{7,5},{8,10},{9,11},{10,... | collective-permute-start | bytes 1179656 | tf_op jit(solution)/shard_map/ppermute | solution.py:34
  3.7 14.1 %collective-permute-start.1 = (bf16[256,768]{1,0:T(8,128)(2,1)}, bf16[256,768]{1,0:T(8,128)(2,1)S(1)}, u32[]{:S(2)}, u32[]{:S(2)}) collective-permute-start(bf16[256,768]{1,0:T(8,128)(2,1)} %refs_0_.3), channel_id=1, source_target_pairs={{0,1},{1,0},{2,3},{3,2},{4,5},{5,4},{6,7},{7,6},{8,9},{9,8},{10,11... | collective-permute-start | bytes 1179656 | tf_op jit(solution)/shard_map/ppermute | solution.py:39
  3.7 1.0 %copy-start.5 = (bf16[256,768]{1,0:T(8,128)(2,1)S(1)}, bf16[256,768]{1,0:T(8,128)(2,1)}, u32[]{:S(2)}) copy-start(bf16[256,768]{1,0:T(8,128)(2,1)} %refs_0_.3) | copy-start | bytes 1179652
  4.7 2.7 %copy-start.6 = (s32[4]{0:T(128)S(1)}, s32[4]{0:T(128)}, u32[]{:S(2)}) copy-start(s32[4]{0:T(128)} %refs_6_.7) | copy-start | bytes 52
  4.8 2.7 %copy-start.7 = (s32[4]{0:T(128)S(1)}, s32[4]{0:T(128)}, u32[]{:S(2)}) copy-start(s32[4]{0:T(128)} %refs_1_.4) | copy-start | bytes 52
  4.8 4.3 %copy-start.2 = (bf16[2048,256]{1,0:T(8,128)(2,1)S(1)}, bf16[2048,256]{1,0:T(8,128)(2,1)}, u32[]{:S(2)}) copy-start(bf16[2048,256]{1,0:T(8,128)(2,1)} %refs_4_.1) | copy-start | bytes 3145732
  4.8 4.3 %copy-start.3 = (bf16[2048,256]{1,0:T(8,128)(2,1)S(1)}, bf16[2048,256]{1,0:T(8,128)(2,1)}, u32[]{:S(2)}) copy-start(bf16[2048,256]{1,0:T(8,128)(2,1)} %refs_5_.5) | copy-start | bytes 3145732
  4.8 12.5 %collective-permute-start.4 = (bf16[128,768]{1,0:T(8,128)(2,1)S(1)}, bf16[128,768]{1,0:T(8,128)(2,1)S(1)}, u32[]{:S(2)}, u32[]{:S(2)}) collective-permute-start(bf16[128,768]{1,0:T(8,128)(2,1)S(1)} %get-tuple-element.58), channel_id=1, source_target_pairs={{0,16},{4,20},{8,24},{12,28},{16,0},{20,4},{24,8},{28,12},{1,17},{... | collective-permute-start | bytes 589832 | tf_op jit(solution)/shard_map/ppermute | solution.py:34
  7.4 11.8 %slice-start = ((s8[4718592]{0:T(1024)(128)(4,1)}), s8[4194304]{0:T(1024)(128)(4,1)S(1)}, s32[]{:S(2)}) async-start(s8[4718592]{0:T(1024)(128)(4,1)} %bitcast.1), calls=%async_computation | async-start | bytes 8388608
  7.5 11.7 %slice-start.1 = ((s8[4718592]{0:T(1024)(128)(4,1)}), s8[524288]{0:T(1024)(128)(4,1)S(1)}, s32[]{:S(2)}) async-start(s8[4718592]{0:T(1024)(128)(4,1)} %bitcast.1), calls=%async_computation.1 | async-start | bytes 1048576
  13.0 6.3 %copy-start.4 = (f32[3072]{0:T(1024)S(1)}, f32[3072]{0:T(1024)}, u32[]{:S(2)}) copy-start(f32[3072]{0:T(1024)} %param.11) | copy-start | bytes 36868
  13.1 13.0 %collective-permute-start.5 = (bf16[128,768]{1,0:T(8,128)(2,1)S(1)}, bf16[128,768]{1,0:T(8,128)(2,1)S(1)}, u32[]{:S(2)}, u32[]{:S(2)}) collective-permute-start(bf16[128,768]{1,0:T(8,128)(2,1)S(1)} %get-tuple-element.62), channel_id=1, source_target_pairs={{0,1},{1,0},{2,3},{3,2},{4,5},{5,4},{6,7},{7,6},{8,9},{9,8},{10,11... | collective-permute-start | bytes 589832 | tf_op jit(solution)/shard_map/ppermute | solution.py:39
  13.1 14.1 %collective-permute-start.7 = (bf16[128,768]{1,0:T(8,128)(2,1)S(1)}, bf16[128,768]{1,0:T(8,128)(2,1)S(1)}, u32[]{:S(2)}, u32[]{:S(2)}) collective-permute-start(bf16[128,768]{1,0:T(8,128)(2,1)S(1)} %relay.8.refs_1_), channel_id=1, source_target_pairs={{0,16},{4,20},{8,24},{12,28},{16,0},{20,4},{24,8},{28,12},{1,17},{... | collective-permute-start | bytes 589832 | tf_op jit(solution)/shard_map/ppermute | solution.py:34
  17.3 10.0 %collective-permute-start.6 = (bf16[128,768]{1,0:T(8,128)(2,1)S(1)}, bf16[128,768]{1,0:T(8,128)(2,1)S(1)}, u32[]{:S(2)}, u32[]{:S(2)}) collective-permute-start(bf16[128,768]{1,0:T(8,128)(2,1)S(1)} %relay.10.refs_13_.refs_0_), channel_id=1, source_target_pairs={{0,2},{1,3},{2,0},{3,1},{4,6},{5,7},{6,4},{7,5},{8,10},{9,11},{10,... | collective-permute-start | bytes 589832 | tf_op jit(solution)/shard_map/ppermute | solution.py:34
  17.8 1.3 %collective-permute-start.2 = (bf16[64,768]{1,0:T(8,128)(2,1)S(1)}, bf16[64,768]{1,0:T(8,128)(2,1)S(1)}, u32[]{:S(2)}, u32[]{:S(2)}) collective-permute-start(bf16[64,768]{1,0:T(8,128)(2,1)S(1)} %get-tuple-element.53), channel_id=1, source_target_pairs={{0,1},{1,0},{2,3},{3,2},{4,5},{5,4},{6,7},{7,6},{8,9},{9,8},{10,11... | collective-permute-start | bytes 294920 | tf_op jit(solution)/shard_map/ppermute | solution.py:39
  17.8 1.5 %collective-permute-start.3 = (bf16[64,768]{1,0:T(8,128)(2,1)S(1)}, bf16[64,768]{1,0:T(8,128)(2,1)S(1)}, u32[]{:S(2)}, u32[]{:S(2)}) collective-permute-start(bf16[64,768]{1,0:T(8,128)(2,1)S(1)} %get-tuple-element.54), channel_id=1, source_target_pairs={{0,1},{1,0},{2,3},{3,2},{4,5},{5,4},{6,7},{7,6},{8,9},{9,8},{10,11... | collective-permute-start | bytes 294920 | tf_op jit(solution)/shard_map/ppermute | solution.py:39
  19.1 10.4 %collective-permute-start.8 = (bf16[128,768]{1,0:T(8,128)(2,1)S(1)}, bf16[128,768]{1,0:T(8,128)(2,1)S(1)}, u32[]{:S(2)}, u32[]{:S(2)}) collective-permute-start(bf16[128,768]{1,0:T(8,128)(2,1)S(1)} %relay.10.refs_13_.refs_0_), channel_id=1, source_target_pairs={{0,1},{1,0},{2,3},{3,2},{4,5},{5,4},{6,7},{7,6},{8,9},{9,8},{10,11... | collective-permute-start | bytes 589832 | tf_op jit(solution)/shard_map/ppermute | solution.py:39
  19.3 6.8 %copy-start = (bf16[3072,256]{1,0:T(8,128)(2,1)S(1)}, bf16[3072,256]{1,0:T(8,128)(2,1)}, u32[]{:S(2)}) copy-start(bf16[3072,256]{1,0:T(8,128)(2,1)} %refs_11_.1) | copy-start | bytes 4718596
  19.3 6.8 %copy-start.1 = (bf16[3072,256]{1,0:T(8,128)(2,1)S(1)}, bf16[3072,256]{1,0:T(8,128)(2,1)}, u32[]{:S(2)}) copy-start(bf16[3072,256]{1,0:T(8,128)(2,1)} %refs_12_.1) | copy-start | bytes 4718596
  27.4 2.2 %collective-permute-start.9 = (bf16[64,768]{1,0:T(8,128)(2,1)S(1)}, bf16[64,768]{1,0:T(8,128)(2,1)S(1)}, u32[]{:S(2)}, u32[]{:S(2)}) collective-permute-start(bf16[64,768]{1,0:T(8,128)(2,1)S(1)} %get-tuple-element.65), channel_id=1, source_target_pairs={{0,1},{1,0},{2,3},{3,2},{4,5},{5,4},{6,7},{7,6},{8,9},{9,8},{10,11... | collective-permute-start | bytes 294920 | tf_op jit(solution)/shard_map/ppermute | solution.py:39
  27.8 1.7 %collective-permute-start.10 = (bf16[64,768]{1,0:T(8,128)(2,1)S(1)}, bf16[64,768]{1,0:T(8,128)(2,1)S(1)}, u32[]{:S(2)}, u32[]{:S(2)}) collective-permute-start(bf16[64,768]{1,0:T(8,128)(2,1)S(1)} %get-tuple-element.66), channel_id=1, source_target_pairs={{0,1},{1,0},{2,3},{3,2},{4,5},{5,4},{6,7},{7,6},{8,9},{9,8},{10,11... | collective-permute-start | bytes 294920 | tf_op jit(solution)/shard_map/ppermute | solution.py:39
  27.9 15.3 %collective-permute-start.11 = (bf16[128,768]{1,0:T(8,128)(2,1)S(1)}, bf16[128,768]{1,0:T(8,128)(2,1)S(1)}, u32[]{:S(2)}, u32[]{:S(2)}) collective-permute-start(bf16[128,768]{1,0:T(8,128)(2,1)S(1)} %relay.11.refs_1_.refs_13_.refs_0_), channel_id=1, source_target_pairs={{0,2},{1,3},{2,0},{3,1},{4,6},{5,7},{6,4},{7,5},{8,10},{9,11},{10,... | collective-permute-start | bytes 589832 | tf_op jit(solution)/shard_map/ppermute | solution.py:34
  36.2 19.3 %collective-permute-start.15 = (bf16[144,768]{1,0:T(8,128)(2,1)S(1)}, bf16[144,768]{1,0:T(8,128)(2,1)S(1)}, u32[]{:S(2)}, u32[]{:S(2)}) collective-permute-start(bf16[144,768]{1,0:T(8,128)(2,1)S(1)} %attend_partner.2.refs_14_), channel_id=1, source_target_pairs={{0,16},{4,20},{8,24},{12,28},{16,0},{20,4},{24,8},{28,12},{1,17},{... | collective-permute-start | bytes 663560 | tf_op jit(solution)/shard_map/ppermute | solution.py:34
  36.2 7.6 %collective-permute-start.12 = (bf16[128,768]{1,0:T(8,128)(2,1)S(1)}, bf16[128,768]{1,0:T(8,128)(2,1)S(1)}, u32[]{:S(2)}, u32[]{:S(2)}) collective-permute-start(bf16[128,768]{1,0:T(8,128)(2,1)S(1)} %relay.11.refs_1_.refs_13_.refs_0_), channel_id=1, source_target_pairs={{0,1},{1,0},{2,3},{3,2},{4,5},{5,4},{6,7},{7,6},{8,9},{9,8},{10,11... | collective-permute-start | bytes 589832 | tf_op jit(solution)/shard_map/ppermute | solution.py:39
  43.3 1.5 %collective-permute-start.13 = (bf16[64,768]{1,0:T(8,128)(2,1)S(1)}, bf16[64,768]{1,0:T(8,128)(2,1)S(1)}, u32[]{:S(2)}, u32[]{:S(2)}) collective-permute-start(bf16[64,768]{1,0:T(8,128)(2,1)S(1)} %get-tuple-element.69), channel_id=1, source_target_pairs={{0,1},{1,0},{2,3},{3,2},{4,5},{5,4},{6,7},{7,6},{8,9},{9,8},{10,11... | collective-permute-start | bytes 294920 | tf_op jit(solution)/shard_map/ppermute | solution.py:39
  43.8 1.3 %collective-permute-start.14 = (bf16[64,768]{1,0:T(8,128)(2,1)S(1)}, bf16[64,768]{1,0:T(8,128)(2,1)S(1)}, u32[]{:S(2)}, u32[]{:S(2)}) collective-permute-start(bf16[64,768]{1,0:T(8,128)(2,1)S(1)} %get-tuple-element.70), channel_id=1, source_target_pairs={{0,1},{1,0},{2,3},{3,2},{4,5},{5,4},{6,7},{7,6},{8,9},{9,8},{10,11... | collective-permute-start | bytes 294920 | tf_op jit(solution)/shard_map/ppermute | solution.py:39
  45.1 10.4 %slice-start.2 = ((s8[4718592]{0:T(1024)(128)(4,1)}), s8[4194304]{0:T(1024)(128)(4,1)S(1)}, s32[]{:S(2)}) async-start(s8[4718592]{0:T(1024)(128)(4,1)} %bitcast.3), calls=%async_computation.2 | async-start | bytes 8388608
  45.1 10.4 %slice-start.3 = ((s8[4718592]{0:T(1024)(128)(4,1)}), s8[524288]{0:T(1024)(128)(4,1)S(1)}, s32[]{:S(2)}) async-start(s8[4718592]{0:T(1024)(128)(4,1)} %bitcast.3), calls=%async_computation.3 | async-start | bytes 1048576
  52.0 13.2 %collective-permute-start.20 = (bf16[144,768]{1,0:T(8,128)(2,1)S(1)}, bf16[144,768]{1,0:T(8,128)(2,1)S(1)}, u32[]{:S(2)}, u32[]{:S(2)}) collective-permute-start(bf16[144,768]{1,0:T(8,128)(2,1)S(1)} %attend_partner.3.refs_15_), channel_id=1, source_target_pairs={{0,16},{4,20},{8,24},{12,28},{16,0},{20,4},{24,8},{28,12},{1,17},{... | collective-permute-start | bytes 663560 | tf_op jit(solution)/shard_map/ppermute | solution.py:34
  56.3 1.4 %collective-permute-start.17 = (bf16[128,384]{1,0:T(8,128)(2,1)S(1)}, bf16[128,384]{1,0:T(8,128)(2,1)S(1)}, u32[]{:S(2)}, u32[]{:S(2)}) collective-permute-start(bf16[128,384]{1,0:T(8,128)(2,1)S(1)} %get-tuple-element.80), channel_id=1, source_target_pairs={{0,1},{1,0},{2,3},{3,2},{4,5},{5,4},{6,7},{7,6},{8,9},{9,8},{10,11... | collective-permute-start | bytes 294920 | tf_op jit(solution)/shard_map/ppermute | solution.py:39
  56.5 1.3 %collective-permute-start.18 = (bf16[128,384]{1,0:T(8,128)(2,1)S(1)}, bf16[128,384]{1,0:T(8,128)(2,1)S(1)}, u32[]{:S(2)}, u32[]{:S(2)}) collective-permute-start(bf16[128,384]{1,0:T(8,128)(2,1)S(1)} %get-tuple-element.81), channel_id=1, source_target_pairs={{0,1},{1,0},{2,3},{3,2},{4,5},{5,4},{6,7},{7,6},{8,9},{9,8},{10,11... | collective-permute-start | bytes 294920 | tf_op jit(solution)/shard_map/ppermute | solution.py:39
  57.9 9.9 %collective-permute-start.19 = (bf16[128,768]{1,0:T(8,128)(2,1)S(1)}, bf16[128,768]{1,0:T(8,128)(2,1)S(1)}, u32[]{:S(2)}, u32[]{:S(2)}) collective-permute-start(bf16[128,768]{1,0:T(8,128)(2,1)S(1)} %sum_cores.2.refs_6_), channel_id=1, source_target_pairs={{0,2},{1,3},{2,0},{3,1},{4,6},{5,7},{6,4},{7,5},{8,10},{9,11},{10,... | collective-permute-start | bytes 589832 | tf_op jit(solution)/shard_map/ppermute | solution.py:34
  66.0 1.8 %collective-permute-start.22 = (bf16[128,384]{1,0:T(8,128)(2,1)S(1)}, bf16[128,384]{1,0:T(8,128)(2,1)S(1)}, u32[]{:S(2)}, u32[]{:S(2)}) collective-permute-start(bf16[128,384]{1,0:T(8,128)(2,1)S(1)} %get-tuple-element.88), channel_id=1, source_target_pairs={{0,1},{1,0},{2,3},{3,2},{4,5},{5,4},{6,7},{7,6},{8,9},{9,8},{10,11... | collective-permute-start | bytes 294920 | tf_op jit(solution)/shard_map/ppermute | solution.py:39
  66.1 1.8 %collective-permute-start.23 = (bf16[128,384]{1,0:T(8,128)(2,1)S(1)}, bf16[128,384]{1,0:T(8,128)(2,1)S(1)}, u32[]{:S(2)}, u32[]{:S(2)}) collective-permute-start(bf16[128,384]{1,0:T(8,128)(2,1)S(1)} %get-tuple-element.89), channel_id=1, source_target_pairs={{0,1},{1,0},{2,3},{3,2},{4,5},{5,4},{6,7},{7,6},{8,9},{9,8},{10,11... | collective-permute-start | bytes 294920 | tf_op jit(solution)/shard_map/ppermute | solution.py:39
  66.6 4.7 %collective-permute-start.16 = (bf16[128,768]{1,0:T(8,128)(2,1)S(1)}, bf16[128,768]{1,0:T(8,128)(2,1)S(1)}, u32[]{:S(2)}, u32[]{:S(2)}) collective-permute-start(bf16[128,768]{1,0:T(8,128)(2,1)S(1)} %get-tuple-element.78.refs_3_), channel_id=1, source_target_pairs={{0,1},{1,0},{2,3},{3,2},{4,5},{5,4},{6,7},{7,6},{8,9},{9,8},{10,11... | collective-permute-start | bytes 589832 | tf_op jit(solution)/shard_map/ppermute | solution.py:39
  67.3 4.0 %collective-permute-start.21 = (bf16[128,768]{1,0:T(8,128)(2,1)S(1)}, bf16[128,768]{1,0:T(8,128)(2,1)S(1)}, u32[]{:S(2)}, u32[]{:S(2)}) collective-permute-start(bf16[128,768]{1,0:T(8,128)(2,1)S(1)} %get-tuple-element.86.refs_3_), channel_id=1, source_target_pairs={{0,1},{1,0},{2,3},{3,2},{4,5},{5,4},{6,7},{7,6},{8,9},{9,8},{10,11... | collective-permute-start | bytes 589832 | tf_op jit(solution)/shard_map/ppermute | solution.py:39
  67.9 7.0 %collective-permute-start.24 = (bf16[128,768]{1,0:T(8,128)(2,1)S(1)}, bf16[128,768]{1,0:T(8,128)(2,1)S(1)}, u32[]{:S(2)}, u32[]{:S(2)}) collective-permute-start(bf16[128,768]{1,0:T(8,128)(2,1)S(1)} %sum_cores.3.refs_7_), channel_id=1, source_target_pairs={{0,2},{1,3},{2,0},{3,1},{4,6},{5,7},{6,4},{7,5},{8,10},{9,11},{10,... | collective-permute-start | bytes 589832 | tf_op jit(solution)/shard_map/ppermute | solution.py:34

commit v14 on v10

--- a/solution.py
+++ b/solution.py
@@ -482,10 +482,11 @@
 def combine_kernel(row_at, own_partial, own_stats, fresh_partial, fresh_stats, *refs):
     heads = lax.axis_size("head")
     chips = heads // CORES
-    outputs = 2 * chips - 1
+    outputs = 3 * chips - 2
     received = refs[: -1 - outputs]
     w_out, merged_rows = refs[-1 - outputs], refs[-outputs]
     far = refs[1 - outputs :]
+    near = far[2 * chips - 2 :]
     width = own_partial.shape[1]
     rows = merged_rows.shape[0]
     part = slice(row_at, row_at + rows)
@@ -519,6 +520,8 @@
         middle = result.shape[1] // 2
         far[2 * ahead - 2][...] = result[:, :middle]
         far[2 * ahead - 1][...] = result[:, middle:]
+    for ahead in range(1, chips):
+        near[ahead - 1][...] = block_product(attended, w_out, ahead, 0)
 
 
 def block_product(attended, w_out, ahead, flip):
@@ -529,11 +532,13 @@
     return dot(attended, w_out[:, along]).astype(jnp.bfloat16)
 
 
-def project_kernel(merged_rows, w_out, far, *near):
+def project_kernel(merged_rows, w_out, left, right, near):
     attended = merged_rows[...]
-    far[...] = block_product(attended, w_out, 0, 1)
-    for ahead, target in enumerate(near):
-        target[...] = block_product(attended, w_out, ahead, 0)
+    result = block_product(attended, w_out, 0, 1)
+    middle = result.shape[1] // 2
+    left[...] = result[:, :middle]
+    right[...] = result[:, middle:]
+    near[...] = block_product(attended, w_out, 0, 0)
 
 
 def combine(row_at, rows, own, fresh_part, received, w_out, heads, earlier):
@@ -541,9 +546,10 @@
     width = w_out.shape[1] // heads
     merged = jax.ShapeDtypeStruct((rows, own[0].shape[1]), jnp.bfloat16)
     half = jax.ShapeDtypeStruct((rows, width // 2), jnp.bfloat16)
-    merged, *far = call(
+    near = jax.ShapeDtypeStruct((rows, width), jnp.bfloat16)
+    merged, *blocks = call(
         functools.partial(combine_kernel, row_at),
-        [merged] + [half] * (2 * chips - 2),
+        [merged] + [half] * (2 * chips - 2) + [near] * (chips - 1),
         [*own, *fresh_part, *received, w_out],
         20,
         rows * w_out.size,
@@ -551,21 +557,23 @@
         "combine",
         earlier,
     )
-    return merged, [far[2 * k : 2 * k + 2] for k in range(chips - 1)]
-
-
-def project(merged, w_out, heads):
-    block = jax.ShapeDtypeStruct((merged.shape[0], w_out.shape[1] // heads), jnp.bfloat16)
-    far, *near = call(
+    far = [blocks[2 * k : 2 * k + 2] for k in range(chips - 1)]
+    return merged, far, blocks[2 * chips - 2 :]
+
+
+def project(merged, w_out, heads, earlier):
+    rows, width = merged.shape[0], w_out.shape[1] // heads
+    half = jax.ShapeDtypeStruct((rows, width // 2), jnp.bfloat16)
+    return call(
         project_kernel,
-        [block] * (1 + heads // CORES),
+        [half, half, jax.ShapeDtypeStruct((rows, width), jnp.bfloat16)],
         [merged, w_out],
         20,
-        2 * merged.shape[0] * w_out.size,
+        merged.shape[0] * w_out.size,
         0,
         "project",
-    )
-    return far, near
+        earlier,
+    )
 
 
 def sum_kernel(count, *refs):
@@ -587,22 +595,27 @@
     )[0]
 
 
-def finish_kernel(*refs):
-    *parts, result = refs
-    count = len(parts) // CHUNKS
-    rows = parts[0].shape[0]
-    for chunk in range(CHUNKS):
+def finish_kernel(counts, *refs):
+    flat = [count for chunk in counts for count in chunk]
+    blocks, (result,) = split_refs(flat, refs)
+    at = 0
+    for chunk in counts:
         total = 0.0
-        for ref in parts[chunk * count : (chunk + 1) * count]:
-            total = total + ref[...].astype(jnp.float32)
-        result[chunk * rows : (chunk + 1) * rows] = total.astype(jnp.bfloat16)
-
-
-def finish(parts, earlier):
-    rows, width = parts[0].shape
-    shape = jax.ShapeDtypeStruct((CHUNKS * rows, width), jnp.bfloat16)
-    flops = CHUNKS * rows * width
-    return call(finish_kernel, [shape], parts, 8, flops, 0, "finish", earlier)[0]
+        for pieces in blocks[: len(chunk)]:
+            whole = jnp.concatenate([ref[...] for ref in pieces], 1)
+            total = total + whole.astype(jnp.float32)
+        blocks = blocks[len(chunk) :]
+        result[at : at + total.shape[0]] = total.astype(result.dtype)
+        at += total.shape[0]
+
+
+def finish(chunks, earlier):
+    flat = [piece for chunk in chunks for pieces in chunk for piece in pieces]
+    rows = sum(chunk[0][0].shape[0] for chunk in chunks)
+    width = sum(piece.shape[1] for piece in chunks[0][0])
+    shape = jax.ShapeDtypeStruct((rows, width), jnp.bfloat16)
+    kernel = functools.partial(finish_kernel, [[len(pieces) for pieces in c] for c in chunks])
+    return call(kernel, [shape], flat, 8, 0, 0, "finish", earlier)[0]
 
 
 def shards(
@@ -698,17 +711,16 @@
     parts = []
     earlier = before_sums = []
     for chunk in range(CHUNKS):
-        merged, fars = combine(
+        merged, fars, nears = combine(
             chunk * chunk_rows, chunk_rows, own_part[2 * chunk : 2 * chunk + 2], fresh_part,
             received[chunk], w_out, heads, earlier,
         )
         fars = [[other_core(part) for part in far] for far in fars]
-        far, near = project(merged, w_out, heads)
-        earlier = [far] + before_sums
-        sums = [sum_cores(one, parts_far, earlier) for one, parts_far in zip(near[1:], fars)]
+        sums = [sum_cores(one, far, [merged] + before_sums) for one, far in zip(nears, fars)]
         from_chips = [shifted(one, "head", CORES * k) for k, one in enumerate(sums, 1)]
-        parts += [near[0], other_core(far), *from_chips]
-        earlier, before_sums = sums, from_chips
+        *far, near = project(merged, w_out, heads, sums)
+        parts.append([[near], [other_core(part) for part in far], *[[one] for one in from_chips]])
+        earlier, before_sums = [near], from_chips
     keys_updated, values_updated, done = update(
         cached_lengths, new_keys, new_values, keys_cache, values_cache, earlier
     )

time: 64.9 us -> 65.1 us (level)
    ppermute x9, waiting for transfers between devices: 13.3 us -> 12.4 us  [shifted(): lax.ppermute(shard, axis, [(i, (i + by) % devices) for i in range(devices)])]
    ppermute x16 -> x18, waiting for transfers between devices: 2.29 us -> 2.98 us  [other_core(): return lax.ppermute(shard, 'head', [(i, i ^ 1) for i in range(devices)])]
    ppermute x16 -> x18, starting transfers between devices: 3.72 us -> 4.23 us  [other_core(): return lax.ppermute(shard, 'head', [(i, i ^ 1) for i in range(devices)])]
  transfers between devices with their start and end apart: 25 -> 27, of which waited for: 10 -> 11; matrix products, arithmetic and copies ran while one was open for 0% -> 0% of each run, Pallas kernels for 41% -> 41%
where the time goes in v14:
time: 65.1 us; the launch traced here: 64.9 us
  Pallas kernels  27.7 us (43%)
  starting transfers between devices  19.8 us (30%)
  waiting for transfers between devices  15.3 us (24%)
  local copies, waits for them, and re-layouts  1.09 us (2%)
  between operations  0.98 us (2%)
    pallas_call x25, Pallas kernels, call(): pl.pallas_call(body, out_shape=out_shape, in_specs=[VMEM] * len(arrays) +...  27.7 us
    ppermute x9, starting transfers between devices, shifted(): lax.ppermute(shard, axis, [(i, (i + by) % devices) for i in range(devices)])  15.6 us
    ppermute x9, waiting for transfers between devices, shifted(): lax.ppermute(shard, axis, [(i, (i + by) % devices) for i in range(devices)])  12.4 us
    ppermute x18, starting transfers between devices, other_core(): return lax.ppermute(shard, 'head', [(i, i ^ 1) for i in range(devices)])  4.23 us
    ppermute x18, waiting for transfers between devices, other_core(): return lax.ppermute(shard, 'head', [(i, i ^ 1) for i in range(devices)])  2.98 us
  transfers between devices with their start and end apart: 27, of which 11 were waited for; matrix products, arithmetic and copies ran while one was open for 0% of the time, Pallas kernels for 41%

profile of v14, /device:TPU:0, one launch (start us, length us, event | category | flops | bytes accessed | tf_op | source)
XLA Modules:
  0.0 64.9 jit_solution(11920875667694856229)
XLA Ops:
  0.6 3.0 %collective-permute-start = (bf16[256,768]{1,0:T(8,128)(2,1)}, bf16[256,768]{1,0:T(8,128)(2,1)S(1)}, u32[]{:S(2)}, u32[]{:S(2)}) collective-permute-start(bf16[256,768]{1,0:T(8,128)(2,1)} %refs_0_.3), channel_id=1, source_target_pairs={{0,2},{1,3},{2,0},{3,1},{4,6},{5,7},{6,4},{7,5},{8,10},{9,11},{10,... | collective-permute-start | bytes 1179656 | tf_op jit(solution)/shard_map/ppermute | solution.py:32
  3.7 1.0 %copy-done.5 = bf16[256,768]{1,0:T(8,128)(2,1)S(1)} copy-done((bf16[256,768]{1,0:T(8,128)(2,1)S(1)}, bf16[256,768]{1,0:T(8,128)(2,1)}, u32[]{:S(2)}) %copy-start.5) | copy-done | bytes 393240
  4.8 2.7 %collective-permute-start.4 = (bf16[128,768]{1,0:T(8,128)(2,1)S(1)}, bf16[128,768]{1,0:T(8,128)(2,1)S(1)}, u32[]{:S(2)}, u32[]{:S(2)}) collective-permute-start(bf16[128,768]{1,0:T(8,128)(2,1)S(1)} %get-tuple-element.58), channel_id=1, source_target_pairs={{0,16},{4,20},{8,24},{12,28},{16,0},{20,4},{24,8},{28,12},{1,17},{... | collective-permute-start | bytes 589832 | tf_op jit(solution)/shard_map/ppermute | solution.py:32
  7.5 1.6 %rope_tables.1 = (f32[512,128]{1,0:T(8,128)S(1)}, f32[512,128]{1,0:T(8,128)S(1)}) custom-call(s32[4]{0:T(128)S(1)} %copy-done.6, s32[4]{0:T(128)S(1)} %copy-done.7, bf16[2048,128]{1,0:T(8,128)(2,1)S(1)} %marks.1.refs_2_.refs_11_.refs_12_), custom_call_target="tpu_custom_call" | custom-call | bytes 262 | tf_op jit(solution)/shard_map/rope_tables/pallas_call | solution.py:76
  9.1 0.8 %widen_caches.1 = (bf16[2,2048,256]{2,1,0:T(8,128)(2,1)S(1)}, bf16[2,2048,256]{2,1,0:T(8,128)(2,1)S(1)}) custom-call(bf16[2048,256]{1,0:T(8,128)(2,1)S(1)} %copy-done.2, bf16[2048,256]{1,0:T(8,128)(2,1)S(1)} %copy-done.3, bf16[2048,128]{1,0:T(8,128)(2,1)S(1)} %marks.1.refs_2_.refs_11_.refs_12_, s32[4]{0:T(128)S(1)} %copy-done.6, ...), custom_call_target="tpu_custom_call" | custom-call | bytes 3407 | tf_op jit(solution)/shard_map/widen_caches/pallas_call | solution.py:76
  9.9 3.1 %collective-permute-done.refs_1_.refs_0_ = bf16[256,768]{1,0:T(8,128)(2,1)S(1)} collective-permute-done((bf16[256,768]{1,0:T(8,128)(2,1)}, bf16[256,768]{1,0:T(8,128)(2,1)S(1)}, u32[]{:S(2)}, u32[]{:S(2)}) %collective-permute-start) | collective-permute-done | bytes 393248 | tf_op jit(solution)/shard_map/ppermute | solution.py:32
  13.1 0.1 collective-permute-start.5
  13.1 2.9 %collective-permute-start.7 = (bf16[128,768]{1,0:T(8,128)(2,1)S(1)}, bf16[128,768]{1,0:T(8,128)(2,1)S(1)}, u32[]{:S(2)}, u32[]{:S(2)}) collective-permute-start(bf16[128,768]{1,0:T(8,128)(2,1)S(1)} %relay.8.refs_1_), channel_id=1, source_target_pairs={{0,16},{4,20},{8,24},{12,28},{16,0},{20,4},{24,8},{28,12},{1,17},{... | collective-permute-start | bytes 589832 | tf_op jit(solution)/shard_map/ppermute | solution.py:32
  16.0 1.2 %collective-permute-done.4.refs_0_ = bf16[128,768]{1,0:T(8,128)(2,1)S(1)} collective-permute-done((bf16[128,768]{1,0:T(8,128)(2,1)S(1)}, bf16[128,768]{1,0:T(8,128)(2,1)S(1)}, u32[]{:S(2)}, u32[]{:S(2)}) %collective-permute-start.4) | collective-permute-done | bytes 196640 | tf_op jit(solution)/shard_map/ppermute | solution.py:32
  17.3 0.5 collective-permute-start.6
  17.8 0.5 collective-permute-start.3
  18.3 0.8 %collective-permute-done.2.refs_3_ = bf16[64,768]{1,0:T(8,128)(2,1)S(1)} collective-permute-done((bf16[64,768]{1,0:T(8,128)(2,1)S(1)}, bf16[64,768]{1,0:T(8,128)(2,1)S(1)}, u32[]{:S(2)}, u32[]{:S(2)}) %collective-permute-start.2) | collective-permute-done | bytes 98336 | tf_op jit(solution)/shard_map/ppermute | solution.py:37
  19.1 0.2 collective-permute-start.8
  19.3 3.5 %attend_own.2 = (f32[128,768]{1,0:T(8,128)S(1)}, f32[8,128]{1,0:T(8,128)S(1)}, bf16[128,768]{1,0:T(8,128)(2,1)S(1)}) custom-call(bf16[256,768]{1,0:T(8,128)(2,1)S(1)} %get-tuple-element.49.refs_0_, bf16[256,768]{1,0:T(8,128)(2,1)S(1)} %get-tuple-element.53.refs_1_, bf16[256,768]{1,0:T(8,128)(2,1)S(1)} %collective-permute-done.1.refs_2_, ...), custom_call_target="tpu_custom_call" | custom-call | flops 1107296 | bytes 5971 | tf_op jit(solution)/shard_map/attend_own/pallas_call | solution.py:76
  22.9 1.1 %fresh_kv.2 = (bf16[256,256]{1,0:T(8,128)(2,1)S(1)}, bf16[256,256]{1,0:T(8,128)(2,1)S(1)}) custom-call(bf16[256,768]{1,0:T(8,128)(2,1)S(1)} %get-tuple-element.49.refs_0_, bf16[256,768]{1,0:T(8,128)(2,1)S(1)} %get-tuple-element.53.refs_1_, bf16[256,768]{1,0:T(8,128)(2,1)S(1)} %collective-permute-done.1.refs_2_, ...), custom_call_target="tpu_custom_call" | custom-call | flops 402653 | bytes 2758 | tf_op jit(solution)/shard_map/fresh_kv/pallas_call | solution.py:76
  24.0 1.7 %collective-permute-done.7.refs_0_ = bf16[128,768]{1,0:T(8,128)(2,1)S(1)} collective-permute-done((bf16[128,768]{1,0:T(8,128)(2,1)S(1)}, bf16[128,768]{1,0:T(8,128)(2,1)S(1)}, u32[]{:S(2)}, u32[]{:S(2)}) %collective-permute-start.7) | collective-permute-done | bytes 196640 | tf_op jit(solution)/shard_map/ppermute | solution.py:32
  25.8 0.1 collective-permute-start.9
  25.9 0.5 collective-permute-start.10
  26.4 1.6 %collective-permute-start.11 = (bf16[128,768]{1,0:T(8,128)(2,1)S(1)}, bf16[128,768]{1,0:T(8,128)(2,1)S(1)}, u32[]{:S(2)}, u32[]{:S(2)}) collective-permute-start(bf16[128,768]{1,0:T(8,128)(2,1)S(1)} %relay.11.refs_1_.refs_12_.refs_0_), channel_id=1, source_target_pairs={{0,2},{1,3},{2,0},{3,1},{4,6},{5,7},{6,4},{7,5},{8,10},{9,11},{10,... | collective-permute-start | bytes 589832 | tf_op jit(solution)/shard_map/ppermute | solution.py:32
  28.0 3.6 %attend_partner.2.refs_13_ = bf16[144,768]{1,0:T(8,128)(2,1)S(1)} custom-call(bf16[128,768]{1,0:T(8,128)(2,1)S(1)} %relay.10.refs_12_.refs_0_, bf16[128,768]{1,0:T(8,128)(2,1)S(1)} %get-tuple-element.64.refs_1_.refs_13_.refs_2_, bf16[128,768]{1,0:T(8,128)(2,1)S(1)} %collective-permute-done.8.refs_2_.refs_4_, ...), custom_call_target="tpu_custom_call" | custom-call | flops 1107296 | bytes 5490 | tf_op jit(solution)/shard_map/attend_partner/pallas_call | solution.py:76
  31.6 0.1 collective-permute-start.12
  31.6 3.8 %attend_own.3 = (f32[128,768]{1,0:T(8,128)S(1)}, f32[8,128]{1,0:T(8,128)S(1)}, bf16[128,768]{1,0:T(8,128)(2,1)S(1)}) custom-call(bf16[256,768]{1,0:T(8,128)(2,1)S(1)} %get-tuple-element.49.refs_0_, bf16[256,768]{1,0:T(8,128)(2,1)S(1)} %get-tuple-element.53.refs_1_, bf16[256,768]{1,0:T(8,128)(2,1)S(1)} %collective-permute-done.1.refs_2_, ...), custom_call_target="tpu_custom_call" | custom-call | flops 1107296 | bytes 6070 | tf_op jit(solution)/shard_map/attend_own/pallas_call | solution.py:76
  35.4 0.6 collective-permute-start.13
  36.0 0.1 collective-permute-start.14
  36.1 0.9 %collective-permute-done.13.refs_3_.refs_8_ = bf16[64,768]{1,0:T(8,128)(2,1)S(1)} collective-permute-done((bf16[64,768]{1,0:T(8,128)(2,1)S(1)}, bf16[64,768]{1,0:T(8,128)(2,1)S(1)}, u32[]{:S(2)}, u32[]{:S(2)}) %collective-permute-start.13) | collective-permute-done | bytes 98336 | tf_op jit(solution)/shard_map/ppermute | solution.py:37
  36.9 0.4 collective-permute-done.14.refs_4_.refs_9_
  37.3 3.5 %attend_partner.3.refs_15_ = bf16[144,768]{1,0:T(8,128)(2,1)S(1)} custom-call(bf16[128,768]{1,0:T(8,128)(2,1)S(1)} %relay.11.refs_1_.refs_12_.refs_0_, bf16[128,768]{1,0:T(8,128)(2,1)S(1)} %get-tuple-element.68.refs_1_.refs_13_.refs_3_, bf16[128,768]{1,0:T(8,128)(2,1)S(1)} %collective-permute-done.12.refs_2_.refs_5_, ...), custom_call_target="tpu_custom_call" | custom-call | flops 1107296 | bytes 5490 | tf_op jit(solution)/shard_map/attend_partner/pallas_call | solution.py:76
  40.8 2.9 %collective-permute-start.21 = (bf16[144,768]{1,0:T(8,128)(2,1)S(1)}, bf16[144,768]{1,0:T(8,128)(2,1)S(1)}, u32[]{:S(2)}, u32[]{:S(2)}) collective-permute-start(bf16[144,768]{1,0:T(8,128)(2,1)S(1)} %attend_partner.3.refs_15_), channel_id=1, source_target_pairs={{0,16},{4,20},{8,24},{12,28},{16,0},{20,4},{24,8},{28,12},{1,17},{... | collective-permute-start | bytes 663560 | tf_op jit(solution)/shard_map/ppermute | solution.py:32
  43.7 1.1 %fresh_kv.3 = (bf16[256,256]{1,0:T(8,128)(2,1)S(1)}, bf16[256,256]{1,0:T(8,128)(2,1)S(1)}) custom-call(bf16[128,768]{1,0:T(8,128)(2,1)S(1)} %relay.10.refs_12_.refs_0_, bf16[128,768]{1,0:T(8,128)(2,1)S(1)} %relay.11.refs_1_.refs_12_.refs_0_, bf16[128,768]{1,0:T(8,128)(2,1)S(1)} %get-tuple-element.64.refs_1_.refs_13_.refs_2_, ...), custom_call_target="tpu_custom_call" | custom-call | flops 402653 | bytes 2758 | tf_op jit(solution)/shard_map/fresh_kv/pallas_call | solution.py:76
  44.8 2.3 %attend_fresh.1 = (f32[256,768]{1,0:T(8,128)S(1)}, f32[8,256]{1,0:T(8,128)S(1)}) custom-call(bf16[128,768]{1,0:T(8,128)(2,1)S(1)} %get-tuple-element.61.refs_11_.refs_0_, bf16[128,768]{1,0:T(8,128)(2,1)S(1)} %get-tuple-element.67.refs_1_.refs_12_, bf16[256,256]{1,0:T(8,128)(2,1)S(1)} %get-tuple-element.63.refs_1_.refs_2_.refs_0_, ...), custom_call_target="tpu_custom_call" | custom-call | flops 201326 | bytes 856 | tf_op jit(solution)/shard_map/attend_fresh/pallas_call | solution.py:76
  47.1 1.0 %combine.2 = (bf16[128,768]{1,0:T(8,128)(2,1)S(1)}, bf16[128,384]{1,0:T(8,128)(2,1)S(1)}, bf16[128,384]{1,0:T(8,128)(2,1)S(1)}, bf16[128,768]{1,0:T(8,128)(2,1)S(1)}) custom-call(f32[128,768]{1,0:T(8,128)S(1)} %get-tuple-element.59.refs_0_, f32[8,128]{1,0:T(8,128)S(1)} %get-tuple-element.60.refs_1_, f32[256,768]{1,0:T(8,128)S(1)} %get-tuple-element.74.refs_2_, ...), custom_call_target="tpu_custom_call" | custom-call | flops 150994 | bytes 3360 | tf_op jit(solution)/shard_map/combine/pallas_call | solution.py:76
  48.2 0.5 collective-permute-start.17
  48.7 0.8 %collective-permute-done.16.refs_1_ = bf16[128,384]{1,0:T(8,128)(2,1)S(1)} collective-permute-done((bf16[128,384]{1,0:T(8,128)(2,1)S(1)}, bf16[128,384]{1,0:T(8,128)(2,1)S(1)}, u32[]{:S(2)}, u32[]{:S(2)}) %collective-permute-start.16) | collective-permute-done | bytes 98336 | tf_op jit(solution)/shard_map/ppermute | solution.py:37
  49.5 0.2 collective-permute-done.17.refs_2_
  49.7 1.0 %collective-permute-start.20 = (bf16[128,768]{1,0:T(8,128)(2,1)S(1)}, bf16[128,768]{1,0:T(8,128)(2,1)S(1)}, u32[]{:S(2)}, u32[]{:S(2)}) collective-permute-start(bf16[128,768]{1,0:T(8,128)(2,1)S(1)} %sum_cores.2.refs_2_), channel_id=1, source_target_pairs={{0,2},{1,3},{2,0},{3,1},{4,6},{5,7},{6,4},{7,5},{8,10},{9,11},{10,... | collective-permute-start | bytes 589832 | tf_op jit(solution)/shard_map/ppermute | solution.py:32
  50.7 0.5 project.2
  51.2 3.0 %collective-permute-done.21.refs_4_ = bf16[144,768]{1,0:T(8,128)(2,1)S(1)} collective-permute-done((bf16[144,768]{1,0:T(8,128)(2,1)S(1)}, bf16[144,768]{1,0:T(8,128)(2,1)S(1)}, u32[]{:S(2)}, u32[]{:S(2)}) %collective-permute-start.21) | collective-permute-done | bytes 221216 | tf_op jit(solution)/shard_map/ppermute | solution.py:32
  54.2 1.0 %combine.3 = (bf16[128,768]{1,0:T(8,128)(2,1)S(1)}, bf16[128,384]{1,0:T(8,128)(2,1)S(1)}, bf16[128,384]{1,0:T(8,128)(2,1)S(1)}, bf16[128,768]{1,0:T(8,128)(2,1)S(1)}) custom-call(f32[128,768]{1,0:T(8,128)S(1)} %get-tuple-element.83.refs_0_, f32[8,128]{1,0:T(8,128)S(1)} %get-tuple-element.84.refs_1_, f32[256,768]{1,0:T(8,128)S(1)} %get-tuple-element.74.refs_2_, ...), custom_call_target="tpu_custom_call" | custom-call | flops 150994 | bytes 3360 | tf_op jit(solution)/shard_map/combine/pallas_call | solution.py:76
  55.3 0.5 collective-permute-start.23
  55.8 1.2 %collective-permute-done.20.refs_4_.refs_3_ = bf16[128,768]{1,0:T(8,128)(2,1)S(1)} collective-permute-done((bf16[128,768]{1,0:T(8,128)(2,1)S(1)}, bf16[128,768]{1,0:T(8,128)(2,1)S(1)}, u32[]{:S(2)}, u32[]{:S(2)}) %collective-permute-start.20) | collective-permute-done | bytes 196640 | tf_op jit(solution)/shard_map/ppermute | solution.py:32
  57.0 1.0 %collective-permute-start.26 = (bf16[128,768]{1,0:T(8,128)(2,1)S(1)}, bf16[128,768]{1,0:T(8,128)(2,1)S(1)}, u32[]{:S(2)}, u32[]{:S(2)}) collective-permute-start(bf16[128,768]{1,0:T(8,128)(2,1)S(1)} %sum_cores.3.refs_2_), channel_id=1, source_target_pairs={{0,2},{1,3},{2,0},{3,1},{4,6},{5,7},{6,4},{7,5},{8,10},{9,11},{10,... | collective-permute-start | bytes 589832 | tf_op jit(solution)/shard_map/ppermute | solution.py:32
  58.0 0.5 collective-permute-start.19
  58.5 0.5 project.3
  59.0 0.1 collective-permute-start.24
  59.1 0.5 collective-permute-start.25
  59.6 2.2 %update_caches.1 = (bf16[2048,256]{1,0:T(8,128)(2,1)}, bf16[2048,256]{1,0:T(8,128)(2,1)}, f32[8,128]{1,0:T(8,128)S(1)}) custom-call(bf16[256,256]{1,0:T(8,128)(2,1)S(1)} %get-tuple-element.63.refs_1_.refs_2_.refs_0_, bf16[256,256]{1,0:T(8,128)(2,1)S(1)} %get-tuple-element.71.refs_3_.refs_1_, bf16[256,256]{1,0:T(8,128)(2,1)S(1)} %get-tuple-element.72.refs_4_.refs_2_, ...), custom_call_target="tpu_custom_call" | custom-call | flops 67108 | bytes 2361 | tf_op jit(solution)/shard_map/update_caches/pallas_call | solution.py:76
  61.8 2.2 %collective-permute-done.26.refs_7_ = bf16[128,768]{1,0:T(8,128)(2,1)S(1)} collective-permute-done((bf16[128,768]{1,0:T(8,128)(2,1)S(1)}, bf16[128,768]{1,0:T(8,128)(2,1)S(1)}, u32[]{:S(2)}, u32[]{:S(2)}) %collective-permute-start.26) | collective-permute-done | bytes 196640 | tf_op jit(solution)/shard_map/ppermute | solution.py:32
  64.0 0.9 %finish.1 = bf16[256,768]{1,0:T(8,128)(2,1)} custom-call(bf16[128,768]{1,0:T(8,128)(2,1)S(1)} %get-tuple-element.80.refs_6_.refs_0_, bf16[128,384]{1,0:T(8,128)(2,1)S(1)} %collective-permute-done.18.refs_1_, bf16[128,384]{1,0:T(8,128)(2,1)S(1)} %collective-permute-done.19.refs_2_, bf16[128,768]{1,0:T(8,128)(2,1)S(1)} %collective-permute-done.20.refs_4_.refs_3_, ...), custom_call_target="tpu_custom_call" | custom-call | bytes 786 | tf_op jit(solution)/shard_map/finish/pallas_call | solution.py:76
  (57 shorter events, 0.6 us)
Async XLA Ops:
  0.6 12.4 %collective-permute-start = (bf16[256,768]{1,0:T(8,128)(2,1)}, bf16[256,768]{1,0:T(8,128)(2,1)S(1)}, u32[]{:S(2)}, u32[]{:S(2)}) collective-permute-start(bf16[256,768]{1,0:T(8,128)(2,1)} %refs_0_.3), channel_id=1, source_target_pairs={{0,2},{1,3},{2,0},{3,1},{4,6},{5,7},{6,4},{7,5},{8,10},{9,11},{10,... | collective-permute-start | bytes 1179656 | tf_op jit(solution)/shard_map/ppermute | solution.py:32
  3.7 14.1 %collective-permute-start.1 = (bf16[256,768]{1,0:T(8,128)(2,1)}, bf16[256,768]{1,0:T(8,128)(2,1)S(1)}, u32[]{:S(2)}, u32[]{:S(2)}) collective-permute-start(bf16[256,768]{1,0:T(8,128)(2,1)} %refs_0_.3), channel_id=1, source_target_pairs={{0,1},{1,0},{2,3},{3,2},{4,5},{5,4},{6,7},{7,6},{8,9},{9,8},{10,11... | collective-permute-start | bytes 1179656 | tf_op jit(solution)/shard_map/ppermute | solution.py:37
  3.7 1.0 %copy-start.5 = (bf16[256,768]{1,0:T(8,128)(2,1)S(1)}, bf16[256,768]{1,0:T(8,128)(2,1)}, u32[]{:S(2)}) copy-start(bf16[256,768]{1,0:T(8,128)(2,1)} %refs_0_.3) | copy-start | bytes 1179652
  4.7 2.7 %copy-start.6 = (s32[4]{0:T(128)S(1)}, s32[4]{0:T(128)}, u32[]{:S(2)}) copy-start(s32[4]{0:T(128)} %refs_6_.7) | copy-start | bytes 52
  4.8 2.7 %copy-start.7 = (s32[4]{0:T(128)S(1)}, s32[4]{0:T(128)}, u32[]{:S(2)}) copy-start(s32[4]{0:T(128)} %refs_1_.4) | copy-start | bytes 52
  4.8 4.3 %copy-start.2 = (bf16[2048,256]{1,0:T(8,128)(2,1)S(1)}, bf16[2048,256]{1,0:T(8,128)(2,1)}, u32[]{:S(2)}) copy-start(bf16[2048,256]{1,0:T(8,128)(2,1)} %refs_4_.1) | copy-start | bytes 3145732
  4.8 4.3 %copy-start.3 = (bf16[2048,256]{1,0:T(8,128)(2,1)S(1)}, bf16[2048,256]{1,0:T(8,128)(2,1)}, u32[]{:S(2)}) copy-start(bf16[2048,256]{1,0:T(8,128)(2,1)} %refs_5_.5) | copy-start | bytes 3145732
  4.8 12.5 %collective-permute-start.4 = (bf16[128,768]{1,0:T(8,128)(2,1)S(1)}, bf16[128,768]{1,0:T(8,128)(2,1)S(1)}, u32[]{:S(2)}, u32[]{:S(2)}) collective-permute-start(bf16[128,768]{1,0:T(8,128)(2,1)S(1)} %get-tuple-element.58), channel_id=1, source_target_pairs={{0,16},{4,20},{8,24},{12,28},{16,0},{20,4},{24,8},{28,12},{1,17},{... | collective-permute-start | bytes 589832 | tf_op jit(solution)/shard_map/ppermute | solution.py:32
  7.4 11.8 %slice-start = ((s8[4718592]{0:T(1024)(128)(4,1)}), s8[4194304]{0:T(1024)(128)(4,1)S(1)}, s32[]{:S(2)}) async-start(s8[4718592]{0:T(1024)(128)(4,1)} %bitcast.1), calls=%async_computation | async-start | bytes 8388608
  7.5 11.7 %slice-start.1 = ((s8[4718592]{0:T(1024)(128)(4,1)}), s8[524288]{0:T(1024)(128)(4,1)S(1)}, s32[]{:S(2)}) async-start(s8[4718592]{0:T(1024)(128)(4,1)} %bitcast.1), calls=%async_computation.1 | async-start | bytes 1048576
  13.0 6.3 %copy-start.4 = (f32[3072]{0:T(1024)S(1)}, f32[3072]{0:T(1024)}, u32[]{:S(2)}) copy-start(f32[3072]{0:T(1024)} %param.11) | copy-start | bytes 36868
  13.1 9.8 %collective-permute-start.5 = (bf16[128,768]{1,0:T(8,128)(2,1)S(1)}, bf16[128,768]{1,0:T(8,128)(2,1)S(1)}, u32[]{:S(2)}, u32[]{:S(2)}) collective-permute-start(bf16[128,768]{1,0:T(8,128)(2,1)S(1)} %get-tuple-element.62), channel_id=1, source_target_pairs={{0,1},{1,0},{2,3},{3,2},{4,5},{5,4},{6,7},{7,6},{8,9},{9,8},{10,11... | collective-permute-start | bytes 589832 | tf_op jit(solution)/shard_map/ppermute | solution.py:37
  13.1 12.6 %collective-permute-start.7 = (bf16[128,768]{1,0:T(8,128)(2,1)S(1)}, bf16[128,768]{1,0:T(8,128)(2,1)S(1)}, u32[]{:S(2)}, u32[]{:S(2)}) collective-permute-start(bf16[128,768]{1,0:T(8,128)(2,1)S(1)} %relay.8.refs_1_), channel_id=1, source_target_pairs={{0,16},{4,20},{8,24},{12,28},{16,0},{20,4},{24,8},{28,12},{1,17},{... | collective-permute-start | bytes 589832 | tf_op jit(solution)/shard_map/ppermute | solution.py:32
  17.3 8.5 %collective-permute-start.6 = (bf16[128,768]{1,0:T(8,128)(2,1)S(1)}, bf16[128,768]{1,0:T(8,128)(2,1)S(1)}, u32[]{:S(2)}, u32[]{:S(2)}) collective-permute-start(bf16[128,768]{1,0:T(8,128)(2,1)S(1)} %relay.10.refs_12_.refs_0_), channel_id=1, source_target_pairs={{0,2},{1,3},{2,0},{3,1},{4,6},{5,7},{6,4},{7,5},{8,10},{9,11},{10,... | collective-permute-start | bytes 589832 | tf_op jit(solution)/shard_map/ppermute | solution.py:32
  17.8 1.3 %collective-permute-start.2 = (bf16[64,768]{1,0:T(8,128)(2,1)S(1)}, bf16[64,768]{1,0:T(8,128)(2,1)S(1)}, u32[]{:S(2)}, u32[]{:S(2)}) collective-permute-start(bf16[64,768]{1,0:T(8,128)(2,1)S(1)} %get-tuple-element.54), channel_id=1, source_target_pairs={{0,1},{1,0},{2,3},{3,2},{4,5},{5,4},{6,7},{7,6},{8,9},{9,8},{10,11... | collective-permute-start | bytes 294920 | tf_op jit(solution)/shard_map/ppermute | solution.py:37
  17.8 1.5 %collective-permute-start.3 = (bf16[64,768]{1,0:T(8,128)(2,1)S(1)}, bf16[64,768]{1,0:T(8,128)(2,1)S(1)}, u32[]{:S(2)}, u32[]{:S(2)}) collective-permute-start(bf16[64,768]{1,0:T(8,128)(2,1)S(1)} %get-tuple-element.55), channel_id=1, source_target_pairs={{0,1},{1,0},{2,3},{3,2},{4,5},{5,4},{6,7},{7,6},{8,9},{9,8},{10,11... | collective-permute-start | bytes 294920 | tf_op jit(solution)/shard_map/ppermute | solution.py:37
  19.1 8.9 %collective-permute-start.8 = (bf16[128,768]{1,0:T(8,128)(2,1)S(1)}, bf16[128,768]{1,0:T(8,128)(2,1)S(1)}, u32[]{:S(2)}, u32[]{:S(2)}) collective-permute-start(bf16[128,768]{1,0:T(8,128)(2,1)S(1)} %relay.10.refs_12_.refs_0_), channel_id=1, source_target_pairs={{0,1},{1,0},{2,3},{3,2},{4,5},{5,4},{6,7},{7,6},{8,9},{9,8},{10,11... | collective-permute-start | bytes 589832 | tf_op jit(solution)/shard_map/ppermute | solution.py:37
  19.3 3.6 %copy-start = (bf16[3072,256]{1,0:T(8,128)(2,1)S(1)}, bf16[3072,256]{1,0:T(8,128)(2,1)}, u32[]{:S(2)}) copy-start(bf16[3072,256]{1,0:T(8,128)(2,1)} %refs_11_.1) | copy-start | bytes 4718596
  19.3 3.6 %copy-start.1 = (bf16[3072,256]{1,0:T(8,128)(2,1)S(1)}, bf16[3072,256]{1,0:T(8,128)(2,1)}, u32[]{:S(2)}) copy-start(bf16[3072,256]{1,0:T(8,128)(2,1)} %refs_12_.1) | copy-start | bytes 4718596
  25.8 2.2 %collective-permute-start.9 = (bf16[64,768]{1,0:T(8,128)(2,1)S(1)}, bf16[64,768]{1,0:T(8,128)(2,1)S(1)}, u32[]{:S(2)}, u32[]{:S(2)}) collective-permute-start(bf16[64,768]{1,0:T(8,128)(2,1)S(1)} %get-tuple-element.65), channel_id=1, source_target_pairs={{0,1},{1,0},{2,3},{3,2},{4,5},{5,4},{6,7},{7,6},{8,9},{9,8},{10,11... | collective-permute-start | bytes 294920 | tf_op jit(solution)/shard_map/ppermute | solution.py:37
  25.9 2.1 %collective-permute-start.10 = (bf16[64,768]{1,0:T(8,128)(2,1)S(1)}, bf16[64,768]{1,0:T(8,128)(2,1)S(1)}, u32[]{:S(2)}, u32[]{:S(2)}) collective-permute-start(bf16[64,768]{1,0:T(8,128)(2,1)S(1)} %get-tuple-element.66), channel_id=1, source_target_pairs={{0,1},{1,0},{2,3},{3,2},{4,5},{5,4},{6,7},{7,6},{8,9},{9,8},{10,11... | collective-permute-start | bytes 294920 | tf_op jit(solution)/shard_map/ppermute | solution.py:37
  26.4 9.0 %collective-permute-start.11 = (bf16[128,768]{1,0:T(8,128)(2,1)S(1)}, bf16[128,768]{1,0:T(8,128)(2,1)S(1)}, u32[]{:S(2)}, u32[]{:S(2)}) collective-permute-start(bf16[128,768]{1,0:T(8,128)(2,1)S(1)} %relay.11.refs_1_.refs_12_.refs_0_), channel_id=1, source_target_pairs={{0,2},{1,3},{2,0},{3,1},{4,6},{5,7},{6,4},{7,5},{8,10},{9,11},{10,... | collective-permute-start | bytes 589832 | tf_op jit(solution)/shard_map/ppermute | solution.py:32
  31.5 15.6 %collective-permute-start.15 = (bf16[144,768]{1,0:T(8,128)(2,1)S(1)}, bf16[144,768]{1,0:T(8,128)(2,1)S(1)}, u32[]{:S(2)}, u32[]{:S(2)}) collective-permute-start(bf16[144,768]{1,0:T(8,128)(2,1)S(1)} %attend_partner.2.refs_13_), channel_id=1, source_target_pairs={{0,16},{4,20},{8,24},{12,28},{16,0},{20,4},{24,8},{28,12},{1,17},{... | collective-permute-start | bytes 663560 | tf_op jit(solution)/shard_map/ppermute | solution.py:32
  31.6 4.5 %collective-permute-start.12 = (bf16[128,768]{1,0:T(8,128)(2,1)S(1)}, bf16[128,768]{1,0:T(8,128)(2,1)S(1)}, u32[]{:S(2)}, u32[]{:S(2)}) collective-permute-start(bf16[128,768]{1,0:T(8,128)(2,1)S(1)} %relay.11.refs_1_.refs_12_.refs_0_), channel_id=1, source_target_pairs={{0,1},{1,0},{2,3},{3,2},{4,5},{5,4},{6,7},{7,6},{8,9},{9,8},{10,11... | collective-permute-start | bytes 589832 | tf_op jit(solution)/shard_map/ppermute | solution.py:37
  35.4 1.5 %collective-permute-start.13 = (bf16[64,768]{1,0:T(8,128)(2,1)S(1)}, bf16[64,768]{1,0:T(8,128)(2,1)S(1)}, u32[]{:S(2)}, u32[]{:S(2)}) collective-permute-start(bf16[64,768]{1,0:T(8,128)(2,1)S(1)} %get-tuple-element.69), channel_id=1, source_target_pairs={{0,1},{1,0},{2,3},{3,2},{4,5},{5,4},{6,7},{7,6},{8,9},{9,8},{10,11... | collective-permute-start | bytes 294920 | tf_op jit(solution)/shard_map/ppermute | solution.py:37
  36.0 1.3 %collective-permute-start.14 = (bf16[64,768]{1,0:T(8,128)(2,1)S(1)}, bf16[64,768]{1,0:T(8,128)(2,1)S(1)}, u32[]{:S(2)}, u32[]{:S(2)}) collective-permute-start(bf16[64,768]{1,0:T(8,128)(2,1)S(1)} %get-tuple-element.70), channel_id=1, source_target_pairs={{0,1},{1,0},{2,3},{3,2},{4,5},{5,4},{6,7},{7,6},{8,9},{9,8},{10,11... | collective-permute-start | bytes 294920 | tf_op jit(solution)/shard_map/ppermute | solution.py:37
  37.3 9.8 %slice-start.2 = ((s8[4718592]{0:T(1024)(128)(4,1)}), s8[4194304]{0:T(1024)(128)(4,1)S(1)}, s32[]{:S(2)}) async-start(s8[4718592]{0:T(1024)(128)(4,1)} %bitcast.3), calls=%async_computation.2 | async-start | bytes 8388608
  37.3 9.8 %slice-start.3 = ((s8[4718592]{0:T(1024)(128)(4,1)}), s8[524288]{0:T(1024)(128)(4,1)S(1)}, s32[]{:S(2)}) async-start(s8[4718592]{0:T(1024)(128)(4,1)} %bitcast.3), calls=%async_computation.3 | async-start | bytes 1048576
  40.8 13.4 %collective-permute-start.21 = (bf16[144,768]{1,0:T(8,128)(2,1)S(1)}, bf16[144,768]{1,0:T(8,128)(2,1)S(1)}, u32[]{:S(2)}, u32[]{:S(2)}) collective-permute-start(bf16[144,768]{1,0:T(8,128)(2,1)S(1)} %attend_partner.3.refs_15_), channel_id=1, source_target_pairs={{0,16},{4,20},{8,24},{12,28},{16,0},{20,4},{24,8},{28,12},{1,17},{... | collective-permute-start | bytes 663560 | tf_op jit(solution)/shard_map/ppermute | solution.py:32
  48.2 1.4 %collective-permute-start.16 = (bf16[128,384]{1,0:T(8,128)(2,1)S(1)}, bf16[128,384]{1,0:T(8,128)(2,1)S(1)}, u32[]{:S(2)}, u32[]{:S(2)}) collective-permute-start(bf16[128,384]{1,0:T(8,128)(2,1)S(1)} %get-tuple-element.78), channel_id=1, source_target_pairs={{0,1},{1,0},{2,3},{3,2},{4,5},{5,4},{6,7},{7,6},{8,9},{9,8},{10,11... | collective-permute-start | bytes 294920 | tf_op jit(solution)/shard_map/ppermute | solution.py:37
  48.2 1.4 %collective-permute-start.17 = (bf16[128,384]{1,0:T(8,128)(2,1)S(1)}, bf16[128,384]{1,0:T(8,128)(2,1)S(1)}, u32[]{:S(2)}, u32[]{:S(2)}) collective-permute-start(bf16[128,384]{1,0:T(8,128)(2,1)S(1)} %get-tuple-element.79), channel_id=1, source_target_pairs={{0,1},{1,0},{2,3},{3,2},{4,5},{5,4},{6,7},{7,6},{8,9},{9,8},{10,11... | collective-permute-start | bytes 294920 | tf_op jit(solution)/shard_map/ppermute | solution.py:37
  49.7 7.2 %collective-permute-start.20 = (bf16[128,768]{1,0:T(8,128)(2,1)S(1)}, bf16[128,768]{1,0:T(8,128)(2,1)S(1)}, u32[]{:S(2)}, u32[]{:S(2)}) collective-permute-start(bf16[128,768]{1,0:T(8,128)(2,1)S(1)} %sum_cores.2.refs_2_), channel_id=1, source_target_pairs={{0,2},{1,3},{2,0},{3,1},{4,6},{5,7},{6,4},{7,5},{8,10},{9,11},{10,... | collective-permute-start | bytes 589832 | tf_op jit(solution)/shard_map/ppermute | solution.py:32
  55.2 1.7 %collective-permute-start.22 = (bf16[128,384]{1,0:T(8,128)(2,1)S(1)}, bf16[128,384]{1,0:T(8,128)(2,1)S(1)}, u32[]{:S(2)}, u32[]{:S(2)}) collective-permute-start(bf16[128,384]{1,0:T(8,128)(2,1)S(1)} %get-tuple-element.87), channel_id=1, source_target_pairs={{0,1},{1,0},{2,3},{3,2},{4,5},{5,4},{6,7},{7,6},{8,9},{9,8},{10,11... | collective-permute-start | bytes 294920 | tf_op jit(solution)/shard_map/ppermute | solution.py:37
  55.3 1.7 %collective-permute-start.23 = (bf16[128,384]{1,0:T(8,128)(2,1)S(1)}, bf16[128,384]{1,0:T(8,128)(2,1)S(1)}, u32[]{:S(2)}, u32[]{:S(2)}) collective-permute-start(bf16[128,384]{1,0:T(8,128)(2,1)S(1)} %get-tuple-element.88), channel_id=1, source_target_pairs={{0,1},{1,0},{2,3},{3,2},{4,5},{5,4},{6,7},{7,6},{8,9},{9,8},{10,11... | collective-permute-start | bytes 294920 | tf_op jit(solution)/shard_map/ppermute | solution.py:37
  57.0 7.0 %collective-permute-start.26 = (bf16[128,768]{1,0:T(8,128)(2,1)S(1)}, bf16[128,768]{1,0:T(8,128)(2,1)S(1)}, u32[]{:S(2)}, u32[]{:S(2)}) collective-permute-start(bf16[128,768]{1,0:T(8,128)(2,1)S(1)} %sum_cores.3.refs_2_), channel_id=1, source_target_pairs={{0,2},{1,3},{2,0},{3,1},{4,6},{5,7},{6,4},{7,5},{8,10},{9,11},{10,... | collective-permute-start | bytes 589832 | tf_op jit(solution)/shard_map/ppermute | solution.py:32
  58.0 3.8 %collective-permute-start.18 = (bf16[128,384]{1,0:T(8,128)(2,1)S(1)}, bf16[128,384]{1,0:T(8,128)(2,1)S(1)}, u32[]{:S(2)}, u32[]{:S(2)}) collective-permute-start(bf16[128,384]{1,0:T(8,128)(2,1)S(1)} %get-tuple-element.81), channel_id=1, source_target_pairs={{0,1},{1,0},{2,3},{3,2},{4,5},{5,4},{6,7},{7,6},{8,9},{9,8},{10,11... | collective-permute-start | bytes 294920 | tf_op jit(solution)/shard_map/ppermute | solution.py:37
  58.0 3.8 %collective-permute-start.19 = (bf16[128,384]{1,0:T(8,128)(2,1)S(1)}, bf16[128,384]{1,0:T(8,128)(2,1)S(1)}, u32[]{:S(2)}, u32[]{:S(2)}) collective-permute-start(bf16[128,384]{1,0:T(8,128)(2,1)S(1)} %get-tuple-element.82), channel_id=1, source_target_pairs={{0,1},{1,0},{2,3},{3,2},{4,5},{5,4},{6,7},{7,6},{8,9},{9,8},{10,11... | collective-permute-start | bytes 294920 | tf_op jit(solution)/shard_map/ppermute | solution.py:37
  59.0 2.8 %collective-permute-start.24 = (bf16[128,384]{1,0:T(8,128)(2,1)S(1)}, bf16[128,384]{1,0:T(8,128)(2,1)S(1)}, u32[]{:S(2)}, u32[]{:S(2)}) collective-permute-start(bf16[128,384]{1,0:T(8,128)(2,1)S(1)} %get-tuple-element.90), channel_id=1, source_target_pairs={{0,1},{1,0},{2,3},{3,2},{4,5},{5,4},{6,7},{7,6},{8,9},{9,8},{10,11... | collective-permute-start | bytes 294920 | tf_op jit(solution)/shard_map/ppermute | solution.py:37
  59.1 2.7 %collective-permute-start.25 = (bf16[128,384]{1,0:T(8,128)(2,1)S(1)}, bf16[128,384]{1,0:T(8,128)(2,1)S(1)}, u32[]{:S(2)}, u32[]{:S(2)}) collective-permute-start(bf16[128,384]{1,0:T(8,128)(2,1)S(1)} %get-tuple-element.91), channel_id=1, source_target_pairs={{0,1},{1,0},{2,3},{3,2},{4,5},{5,4},{6,7},{7,6},{8,9},{9,8},{10,11... | collective-permute-start | bytes 294920 | tf_op jit(solution)/shard_map/ppermute | solution.py:37

commit v15 on v11

--- a/solution.py
+++ b/solution.py
@@ -13,7 +13,7 @@
 STAT_ROWS = 8
 ROW_TILE = 16
 CORES = 2
-CHUNKS = 2
+CHUNK_UNITS = (8, 8)
 COST_WEIGHT = 0.0005
 FIRST_MICROS = 2
 FLOPS_PER_MICRO = 1_000_000_000
@@ -223,11 +223,30 @@
 
 
 def stat_rows(columns, rows):
-    lane = lax.broadcasted_iota(jnp.int32, (rows, LANES), 1)
-    table = jnp.zeros((rows, LANES), jnp.float32)
+    padded = -(-rows // LANES) * LANES
+    lane = lax.broadcasted_iota(jnp.int32, (padded, LANES), 1)
+    table = jnp.zeros((padded, LANES), jnp.float32)
     for index, column in enumerate(columns):
+        if padded > rows:
+            filler = jnp.zeros((padded - rows, 1), jnp.float32)
+            column = jnp.concatenate([column, filler], 0)
         table = jnp.where(lane == index, column, table)
     return table.T[:STAT_ROWS]
+
+
+def stat_columns(stats):
+    padding = jnp.zeros((LANES - STAT_ROWS, stats.shape[1]), jnp.float32)
+    return jnp.concatenate([stats, padding], 0).T
+
+
+def stat_places(rows, width):
+    lanes = -(-rows // LANES) * LANES
+    in_row = width // lanes
+    return [(part // in_row * ROW_TILE, part % in_row * lanes) for part in range(3)], lanes
+
+
+def tail_rows(rows, width):
+    return stat_places(rows, width)[0][-1][0] + ROW_TILE
 
 
 def split_refs(counts, refs):
@@ -339,11 +358,12 @@
     if not turn:
         outputs[1][...] = stats
         return
-    target[rows:] = jnp.zeros((ROW_TILE, target.shape[1]), target.dtype)
-    rest = jnp.concatenate([stats, jnp.zeros((ROW_TILE - STAT_ROWS, rows), jnp.float32)], 0)
-    for index in range(3):
+    target[rows:] = jnp.zeros((target.shape[0] - rows, target.shape[1]), target.dtype)
+    places, lanes = stat_places(rows, target.shape[1])
+    rest = jnp.concatenate([stats, jnp.zeros((ROW_TILE - STAT_ROWS, lanes), jnp.float32)], 0)
+    for row, lane in places:
         rounded = rest.astype(target.dtype)
-        target[rows:, index * rows : (index + 1) * rows] = rounded
+        target[rows + row : rows + row + ROW_TILE, lane : lane + lanes] = rounded
         rest = rest - rounded.astype(jnp.float32)
 
 
@@ -356,11 +376,11 @@
     width = w_query.shape[1]
     slots = wides[0].shape[1]
     if turn:
-        out_shape = [jax.ShapeDtypeStruct((rows + ROW_TILE, width), jnp.bfloat16)]
+        out_shape = [jax.ShapeDtypeStruct((rows + tail_rows(rows, width), width), jnp.bfloat16)]
     else:
         out_shape = [
             jax.ShapeDtypeStruct((rows, width), jnp.float32),
-            jax.ShapeDtypeStruct((STAT_ROWS, rows), jnp.float32),
+            jax.ShapeDtypeStruct((STAT_ROWS, -(-rows // LANES) * LANES), jnp.float32),
         ]
     return call(
         functools.partial(attend_kernel, counts, *place, turn, row_at, rows, table_at),
@@ -463,16 +483,14 @@
     w_out, merged_rows = refs[-1 - outputs], refs[-outputs]
     far = refs[1 - outputs :]
     rows, width = own_partial.shape
-    padding = jnp.zeros((LANES - STAT_ROWS, rows), jnp.float32)
-    stats = [own_stats[...]]
+    logs = [stat_columns(own_stats[...])[:rows]]
+    places, lanes = stat_places(rows, width)
     for ref in received:
-        stats.append(
-            sum(
-                ref[rows:, turn * rows : (turn + 1) * rows].astype(jnp.float32)
-                for turn in range(3)
-            )[:STAT_ROWS]
+        stats = sum(
+            ref[rows + row : rows + row + ROW_TILE, lane : lane + lanes].astype(jnp.float32)
+            for row, lane in places
         )
-    logs = [jnp.concatenate([stat, padding], 0).T for stat in stats]
+        logs.append(stat_columns(stats[:STAT_ROWS])[:rows])
     largest = functools.reduce(jnp.maximum, logs)
     shares = [jnp.exp2(log - largest) for log in logs]
     total = functools.reduce(jnp.add, shares)
@@ -542,41 +560,46 @@
     return far, near
 
 
-def sum_kernel(count, *refs):
-    total = refs[0][...].astype(jnp.float32)
-    total = total + jnp.concatenate([ref[...] for ref in refs[1:count]], 1).astype(jnp.float32)
-    refs[count][...] = total.astype(jnp.bfloat16)
-
-
-def sum_cores(near, far, earlier):
-    return call(
-        functools.partial(sum_kernel, 1 + len(far)),
-        [jax.ShapeDtypeStruct(near.shape, near.dtype)],
-        [near, *far],
-        8,
-        near.size,
-        0,
-        "sum_cores",
-        earlier,
-    )[0]
-
-
-def finish_kernel(*refs):
-    *parts, result = refs
-    count = len(parts) // CHUNKS
-    rows = parts[0].shape[0]
-    for chunk in range(CHUNKS):
+def store_pieces(block, targets):
+    width = targets[0].shape[1]
+    for index, target in enumerate(targets):
+        target[...] = block[:, index * width : (index + 1) * width]
+
+
+def sum_kernel(count, near, *refs):
+    far, pieces = refs[:count], refs[count:]
+    total = jnp.concatenate([ref[...] for ref in far], 1).astype(jnp.float32)
+    store_pieces((near[...].astype(jnp.float32) + total).astype(jnp.bfloat16), pieces)
+
+
+def sum_cores(near, far, pieces, earlier):
+    rows, width = near.shape
+    shape = jax.ShapeDtypeStruct((rows, width // pieces), near.dtype)
+    kernel = functools.partial(sum_kernel, len(far))
+    return call(kernel, [shape] * pieces, [near, *far], 8, near.size, 0, "sum_cores", earlier)
+
+
+def finish_kernel(counts, *refs):
+    flat = [count for chunk in counts for count in chunk]
+    blocks, (result,) = split_refs(flat, refs)
+    at = 0
+    for chunk in counts:
         total = 0.0
-        for ref in parts[chunk * count : (chunk + 1) * count]:
-            total = total + ref[...].astype(jnp.float32)
-        result[chunk * rows : (chunk + 1) * rows] = total.astype(jnp.bfloat16)
-
-
-def finish(parts, earlier):
-    rows, width = parts[0].shape
-    shape = jax.ShapeDtypeStruct((CHUNKS * rows, width), jnp.bfloat16)
-    flops = CHUNKS * rows * width
-    return call(finish_kernel, [shape], parts, 8, flops, 0, "finish", earlier)[0]
+        for pieces in blocks[: len(chunk)]:
+            whole = jnp.concatenate([ref[...] for ref in pieces], 1)
+            total = total + whole.astype(jnp.float32)
+        blocks = blocks[len(chunk) :]
+        result[at : at + total.shape[0]] = total.astype(result.dtype)
+        at += total.shape[0]
+
+
+def finish(chunks, earlier):
+    flat = [piece for chunk in chunks for pieces in chunk for piece in pieces]
+    rows = sum(chunk[0][0].shape[0] for chunk in chunks)
+    width = sum(piece.shape[1] for piece in chunks[0][0])
+    shape = jax.ShapeDtypeStruct((rows, width), jnp.bfloat16)
+    kernel = functools.partial(finish_kernel, [[len(pieces) for pieces in c] for c in chunks])
+    return call(kernel, [shape], flat, 8, 0, 0, "finish", earlier)[0]
 
 
 def shards(
@@ -596,7 +619,8 @@
     groups = lax.axis_size("seq") // requests
     heads = lax.axis_size("head")
     chips = heads // CORES
-    chunk_rows = rows // CHUNKS
+    sizes = [rows * units // sum(CHUNK_UNITS) for units in CHUNK_UNITS]
+    starts = [0, sizes[0]]
     gain = norm_gain.reshape(heads, 1, width)
 
     mark = marks(keys_cache.shape[0])
@@ -604,38 +628,43 @@
     wide_keys, wide_values = widen(keys_cache, values_cache, mark, cached_lengths, tables[:1])
 
     def attend_rows(pieces, turn, chunk, earlier):
-        at = chunk * chunk_rows
+        at = starts[chunk]
         return attend(
             pieces, gain, w_query, tables, [wide_keys, wide_values], mark, new_rows[0],
-            (groups, requests), turn, 0 if turn else at, chunk_rows, turn * rows + at, earlier,
+            (groups, requests), turn, 0 if turn else at, sizes[chunk], turn * rows + at, earlier,
         )
 
-    half = chunk_rows // 2
+    def in_halves(size):
+        low = -(-size // (2 * ROW_TILE)) * ROW_TILE
+        return [low, size - low]
+
     from_chips = other_chips(tokens)
     crossed = other_core(tokens)
-    own, early, late = relay([tokens], [rows, chunk_rows, rows - chunk_rows], [])
+    own, early, late = relay([tokens], [rows, *sizes], [])
     first = [shifted(early, "seq", turn * requests) for turn in range(1, groups)]
-    (late,) = relay([late], [rows - chunk_rows], from_chips + [wide_keys])
+    (late,) = relay([late], sizes[1:], from_chips + [wide_keys])
     second = [shifted(late, "seq", turn * requests) for turn in range(1, groups)]
-    own_cuts = [relay([piece], [rows, half, half, rows - chunk_rows], [late]) for piece in from_chips]
+    own_cuts = [
+        relay([piece], [rows, *in_halves(sizes[0]), sizes[1]], [late]) for piece in from_chips
+    ]
     own_pieces = [[own]] + [[cut[0]] for cut in own_cuts] + [[crossed]]
     own_pieces += [[other_core(block) for block in cut[1:]] for cut in own_cuts]
     own_early = [
         blocks if len(blocks) == 1 else blocks[: len(blocks) - 1] for blocks in own_pieces
     ]
     earlier = [cut[0] for cut in own_cuts]
-    first = [relay([piece], [chunk_rows], earlier)[0] for piece in first]
+    first = [relay([piece], sizes[:1], earlier)[0] for piece in first]
     first_from_chips = [other_chips(piece) for piece in first]
     new_rows = [fresh(own_pieces, gain, w_key, w_value, tables, 0, first)]
     own_part = attend_rows(own_early, 0, 0, [new_rows[0][0]])
     earlier = own_part[:1]
-    second = [relay([piece], [rows - chunk_rows], earlier)[0] for piece in second]
+    second = [relay([piece], sizes[1:], earlier)[0] for piece in second]
     second_from_chips = [other_chips(piece) for piece in second]
     earlier = second
 
     def gather_cores(piece, from_chips, earlier):
         size = piece.shape[0]
-        passed = [relay([one], [size, size // 2, size // 2], earlier) for one in from_chips]
+        passed = [relay([one], [size, *in_halves(size)], earlier) for one in from_chips]
         blocks = [[piece]] + [[one[0]] for one in passed] + [[other_core(piece)]]
         blocks += [[other_core(part) for part in one[1:]] for one in passed]
         return blocks, [one[0] for one in passed]
@@ -645,11 +674,13 @@
         blocks, passed = gather_cores(piece, from_chips, earlier)
         gathered.append([blocks])
         earlier = earlier + passed
-    received = [[] for _ in range(CHUNKS)]
+    received = [[] for _ in range(len(sizes))]
     for turn in range(1, groups):
         (packed,) = attend_rows(gathered[turn - 1][0], turn, 0, earlier)
         received[0].append(shifted(packed, "seq", -turn * requests))
         earlier = [packed]
+    own_part = [own_part, attend_rows(own_pieces, 0, 1, earlier)]
+    earlier = [own_part[1][0]]
     for blocks, piece, from_chips in zip(gathered, second, second_from_chips):
         along, passed = gather_cores(piece, from_chips, earlier)
         blocks.append(along)
@@ -658,19 +689,22 @@
         (packed,) = attend_rows(gathered[turn - 1][1], turn, 1, earlier)
         received[1].append(shifted(packed, "seq", -turn * requests))
         earlier = [packed]
-    own_part = [own_part, attend_rows(own_pieces, 0, 1, earlier)]
-
     parts = []
-    earlier, before_sums = own_part[1][:1], []
-    for chunk in range(CHUNKS):
+    before_sums = []
+    for chunk in range(len(sizes)):
         merged, fars = combine(own_part[chunk], received[chunk], w_out, heads, earlier)
         fars = [[other_core(part) for part in far] for far in fars]
         far, near = project(merged, w_out, heads)
         earlier = [far] + before_sums
-        sums = [sum_cores(one, parts_far, earlier) for one, parts_far in zip(near[1:], fars)]
-        from_chips = [shifted(one, "head", CORES * k) for k, one in enumerate(sums, 1)]
-        parts += [near[0], other_core(far), *from_chips]
-        earlier, before_sums = sums, from_chips
+        pieces = 1
+        sums = [sum_cores(one, parts_far, pieces, earlier) for one, parts_far in zip(near[1:], fars)]
+        from_chips = [
+            [shifted(piece, "head", CORES * k) for piece in pieces]
+            for k, pieces in enumerate(sums, 1)
+        ]
+        parts.append([[near[0]], [other_core(far)], *from_chips])
+        earlier = [pieces[0] for pieces in sums]
+        before_sums = [piece for pieces in from_chips for piece in pieces]
     for turn in range(1, groups):
         pieces = [sum(blocks, []) for blocks in zip(*gathered[turn - 1])]
         new_rows.append(fresh(pieces, gain, w_key, w_value, tables, turn * rows, earlier))

time: 68.4 us -> 66.6 us (0.974)
  waiting for transfers between devices: 21.9 us -> 19.9 us
    ppermute x9, waiting for transfers between devices: 18.8 us -> 16.8 us  [shifted(): lax.ppermute(shard, axis, [(i, (i + by) % devices) for i in range(devices)])]
  transfers between devices with their start and end apart: 25 -> 25, of which waited for: 14 -> 13; matrix products, arithmetic and copies ran while one was open for 0% -> 0% of each run, Pallas kernels for 37% -> 38%
where the time goes in v15:
time: 66.6 us; the launch traced here: 66.4 us
  Pallas kernels  26.3 us (39%)
  waiting for transfers between devices  19.9 us (30%)
  starting transfers between devices  18.2 us (27%)
  local copies, waits for them, and re-layouts  1.08 us (2%)
  between operations  0.94 us (1%)
    pallas_call x24, Pallas kernels, call(): pl.pallas_call(body, out_shape=out_shape, in_specs=[VMEM] * len(arrays) +...  26.3 us
    ppermute x9, waiting for transfers between devices, shifted(): lax.ppermute(shard, axis, [(i, (i + by) % devices) for i in range(devices)])  16.8 us
    ppermute x9, starting transfers between devices, shifted(): lax.ppermute(shard, axis, [(i, (i + by) % devices) for i in range(devices)])  14.6 us
    ppermute x16, starting transfers between devices, other_core(): return lax.ppermute(shard, 'head', [(i, i ^ 1) for i in range(devices)])  3.67 us
    ppermute x16, waiting for transfers between devices, other_core(): return lax.ppermute(shard, 'head', [(i, i ^ 1) for i in range(devices)])  3.09 us
  transfers between devices with their start and end apart: 25, of which 13 were waited for; matrix products, arithmetic and copies ran while one was open for 0% of the time, Pallas kernels for 38%

profile of v15, /device:TPU:0, one launch (start us, length us, event | category | flops | bytes accessed | tf_op | source)
XLA Modules:
  0.0 66.4 jit_solution(9521164811411645467)
XLA Ops:
  0.6 3.0 %collective-permute-start = (bf16[256,768]{1,0:T(8,128)(2,1)}, bf16[256,768]{1,0:T(8,128)(2,1)S(1)}, u32[]{:S(2)}, u32[]{:S(2)}) collective-permute-start(bf16[256,768]{1,0:T(8,128)(2,1)} %refs_0_.3), channel_id=1, source_target_pairs={{0,2},{1,3},{2,0},{3,1},{4,6},{5,7},{6,4},{7,5},{8,10},{9,11},{10,... | collective-permute-start | bytes 1179656 | tf_op jit(solution)/shard_map/ppermute | solution.py:32
  3.7 1.0 %copy-done.5 = bf16[256,768]{1,0:T(8,128)(2,1)S(1)} copy-done((bf16[256,768]{1,0:T(8,128)(2,1)S(1)}, bf16[256,768]{1,0:T(8,128)(2,1)}, u32[]{:S(2)}) %copy-start.5) | copy-done | bytes 393240
  4.8 2.7 %collective-permute-start.5 = (bf16[128,768]{1,0:T(8,128)(2,1)S(1)}, bf16[128,768]{1,0:T(8,128)(2,1)S(1)}, u32[]{:S(2)}, u32[]{:S(2)}) collective-permute-start(bf16[128,768]{1,0:T(8,128)(2,1)S(1)} %get-tuple-element.53), channel_id=1, source_target_pairs={{0,16},{4,20},{8,24},{12,28},{16,0},{20,4},{24,8},{28,12},{1,17},{... | collective-permute-start | bytes 589832 | tf_op jit(solution)/shard_map/ppermute | solution.py:32
  7.5 1.6 %rope_tables.1 = (f32[512,128]{1,0:T(8,128)S(1)}, f32[512,128]{1,0:T(8,128)S(1)}) custom-call(s32[4]{0:T(128)S(1)} %copy-done.6, s32[4]{0:T(128)S(1)} %copy-done.7, bf16[2048,128]{1,0:T(8,128)(2,1)S(1)} %marks.1.refs_2_.refs_11_.refs_12_), custom_call_target="tpu_custom_call" | custom-call | bytes 262 | tf_op jit(solution)/shard_map/rope_tables/pallas_call | solution.py:76
  9.1 0.8 %widen_caches.1 = (bf16[2,2048,256]{2,1,0:T(8,128)(2,1)S(1)}, bf16[2,2048,256]{2,1,0:T(8,128)(2,1)S(1)}) custom-call(bf16[2048,256]{1,0:T(8,128)(2,1)S(1)} %copy-done.2, bf16[2048,256]{1,0:T(8,128)(2,1)S(1)} %copy-done.3, bf16[2048,128]{1,0:T(8,128)(2,1)S(1)} %marks.1.refs_2_.refs_11_.refs_12_, s32[4]{0:T(128)S(1)} %copy-done.6, ...), custom_call_target="tpu_custom_call" | custom-call | bytes 3407 | tf_op jit(solution)/shard_map/widen_caches/pallas_call | solution.py:76
  9.9 3.1 %collective-permute-done.refs_1_.refs_0_ = bf16[256,768]{1,0:T(8,128)(2,1)S(1)} collective-permute-done((bf16[256,768]{1,0:T(8,128)(2,1)}, bf16[256,768]{1,0:T(8,128)(2,1)S(1)}, u32[]{:S(2)}, u32[]{:S(2)}) %collective-permute-start) | collective-permute-done | bytes 393248 | tf_op jit(solution)/shard_map/ppermute | solution.py:32
  13.1 0.1 collective-permute-start.4
  13.2 2.9 %collective-permute-start.7 = (bf16[128,768]{1,0:T(8,128)(2,1)S(1)}, bf16[128,768]{1,0:T(8,128)(2,1)S(1)}, u32[]{:S(2)}, u32[]{:S(2)}) collective-permute-start(bf16[128,768]{1,0:T(8,128)(2,1)S(1)} %relay.8.refs_1_), channel_id=1, source_target_pairs={{0,16},{4,20},{8,24},{12,28},{16,0},{20,4},{24,8},{28,12},{1,17},{... | collective-permute-start | bytes 589832 | tf_op jit(solution)/shard_map/ppermute | solution.py:32
  16.0 1.2 %collective-permute-done.5.refs_0_ = bf16[128,768]{1,0:T(8,128)(2,1)S(1)} collective-permute-done((bf16[128,768]{1,0:T(8,128)(2,1)S(1)}, bf16[128,768]{1,0:T(8,128)(2,1)S(1)}, u32[]{:S(2)}, u32[]{:S(2)}) %collective-permute-start.5) | collective-permute-done | bytes 196640 | tf_op jit(solution)/shard_map/ppermute | solution.py:32
  17.3 0.5 collective-permute-start.6
  17.8 0.5 collective-permute-start.3
  18.3 0.8 %collective-permute-done.2.refs_3_ = bf16[64,768]{1,0:T(8,128)(2,1)S(1)} collective-permute-done((bf16[64,768]{1,0:T(8,128)(2,1)S(1)}, bf16[64,768]{1,0:T(8,128)(2,1)S(1)}, u32[]{:S(2)}, u32[]{:S(2)}) %collective-permute-start.2) | collective-permute-done | bytes 98336 | tf_op jit(solution)/shard_map/ppermute | solution.py:37
  19.1 0.2 collective-permute-start.8
  19.3 1.1 %fresh_kv.2 = (bf16[256,256]{1,0:T(8,128)(2,1)S(1)}, bf16[256,256]{1,0:T(8,128)(2,1)S(1)}) custom-call(bf16[256,768]{1,0:T(8,128)(2,1)S(1)} %get-tuple-element.43.refs_0_, bf16[256,768]{1,0:T(8,128)(2,1)S(1)} %get-tuple-element.47.refs_1_, bf16[256,768]{1,0:T(8,128)(2,1)S(1)} %collective-permute-done.1.refs_2_, ...), custom_call_target="tpu_custom_call" | custom-call | flops 402653 | bytes 2758 | tf_op jit(solution)/shard_map/fresh_kv/pallas_call | solution.py:76
  20.5 3.8 %attend_own.2 = (f32[128,768]{1,0:T(8,128)S(1)}, f32[8,128]{1,0:T(8,128)S(1)}) custom-call(bf16[256,768]{1,0:T(8,128)(2,1)S(1)} %get-tuple-element.43.refs_0_, bf16[256,768]{1,0:T(8,128)(2,1)S(1)} %get-tuple-element.47.refs_1_, bf16[256,768]{1,0:T(8,128)(2,1)S(1)} %collective-permute-done.1.refs_2_, bf16[64,768]{1,0:T(8,128)(2,1)S(1)} %collective-permute-done.2.refs_3_, ...), custom_call_target="tpu_custom_call" | custom-call | flops 1107296 | bytes 6004 | tf_op jit(solution)/shard_map/attend_own/pallas_call | solution.py:76
  24.3 1.5 %collective-permute-done.7.refs_0_ = bf16[128,768]{1,0:T(8,128)(2,1)S(1)} collective-permute-done((bf16[128,768]{1,0:T(8,128)(2,1)S(1)}, bf16[128,768]{1,0:T(8,128)(2,1)S(1)}, u32[]{:S(2)}, u32[]{:S(2)}) %collective-permute-start.7) | collective-permute-done | bytes 196640 | tf_op jit(solution)/shard_map/ppermute | solution.py:32
  25.8 1.7 %collective-permute-start.12 = (bf16[128,768]{1,0:T(8,128)(2,1)S(1)}, bf16[128,768]{1,0:T(8,128)(2,1)S(1)}, u32[]{:S(2)}, u32[]{:S(2)}) collective-permute-start(bf16[128,768]{1,0:T(8,128)(2,1)S(1)} %relay.11.refs_1_.refs_14_.refs_0_), channel_id=1, source_target_pairs={{0,2},{1,3},{2,0},{3,1},{4,6},{5,7},{6,4},{7,5},{8,10},{9,11},{10,... | collective-permute-start | bytes 589832 | tf_op jit(solution)/shard_map/ppermute | solution.py:32
  27.4 0.1 collective-permute-start.10
  27.5 0.5 collective-permute-start.9
  28.0 0.1 collective-permute-start.13
  28.1 0.7 %collective-permute-done.10.refs_4_.refs_7_ = bf16[64,768]{1,0:T(8,128)(2,1)S(1)} collective-permute-done((bf16[64,768]{1,0:T(8,128)(2,1)S(1)}, bf16[64,768]{1,0:T(8,128)(2,1)S(1)}, u32[]{:S(2)}, u32[]{:S(2)}) %collective-permute-start.10) | collective-permute-done | bytes 98336 | tf_op jit(solution)/shard_map/ppermute | solution.py:37
  28.8 0.2 collective-permute-done.9.refs_3_.refs_6_
  29.0 3.8 %attend_partner.2.refs_15_ = bf16[144,768]{1,0:T(8,128)(2,1)S(1)} custom-call(bf16[128,768]{1,0:T(8,128)(2,1)S(1)} %relay.10.refs_11_.refs_0_, bf16[128,768]{1,0:T(8,128)(2,1)S(1)} %get-tuple-element.58.refs_1_.refs_15_.refs_2_, bf16[128,768]{1,0:T(8,128)(2,1)S(1)} %collective-permute-done.8.refs_2_.refs_4_, ...), custom_call_target="tpu_custom_call" | custom-call | flops 1107296 | bytes 5621 | tf_op jit(solution)/shard_map/attend_partner/pallas_call | solution.py:76
  32.8 4.2 %attend_own.3 = (f32[128,768]{1,0:T(8,128)S(1)}, f32[8,128]{1,0:T(8,128)S(1)}) custom-call(bf16[256,768]{1,0:T(8,128)(2,1)S(1)} %get-tuple-element.43.refs_0_, bf16[256,768]{1,0:T(8,128)(2,1)S(1)} %get-tuple-element.47.refs_1_, bf16[256,768]{1,0:T(8,128)(2,1)S(1)} %collective-permute-done.1.refs_2_, bf16[64,768]{1,0:T(8,128)(2,1)S(1)} %collective-permute-done.2.refs_3_, ...), custom_call_target="tpu_custom_call" | custom-call | flops 1107296 | bytes 6103 | tf_op jit(solution)/shard_map/attend_own/pallas_call | solution.py:76
  37.0 0.4 collective-permute-start.14
  37.4 0.1 collective-permute-start.15
  37.6 0.8 %collective-permute-done.14.refs_3_.refs_8_ = bf16[64,768]{1,0:T(8,128)(2,1)S(1)} collective-permute-done((bf16[64,768]{1,0:T(8,128)(2,1)S(1)}, bf16[64,768]{1,0:T(8,128)(2,1)S(1)}, u32[]{:S(2)}, u32[]{:S(2)}) %collective-permute-start.14) | collective-permute-done | bytes 98336 | tf_op jit(solution)/shard_map/ppermute | solution.py:37
  38.3 0.4 collective-permute-done.15.refs_4_.refs_9_
  38.7 3.8 %attend_partner.3.refs_4_ = bf16[144,768]{1,0:T(8,128)(2,1)S(1)} custom-call(bf16[128,768]{1,0:T(8,128)(2,1)S(1)} %relay.11.refs_1_.refs_14_.refs_0_, bf16[128,768]{1,0:T(8,128)(2,1)S(1)} %get-tuple-element.62.refs_1_.refs_15_.refs_3_, bf16[128,768]{1,0:T(8,128)(2,1)S(1)} %collective-permute-done.13.refs_2_.refs_5_, ...), custom_call_target="tpu_custom_call" | custom-call | flops 1107296 | bytes 5621 | tf_op jit(solution)/shard_map/attend_partner/pallas_call | solution.py:76
  42.5 2.8 %collective-permute-start.20 = (bf16[144,768]{1,0:T(8,128)(2,1)S(1)}, bf16[144,768]{1,0:T(8,128)(2,1)S(1)}, u32[]{:S(2)}, u32[]{:S(2)}) collective-permute-start(bf16[144,768]{1,0:T(8,128)(2,1)S(1)} %attend_partner.3.refs_4_), channel_id=1, source_target_pairs={{0,16},{4,20},{8,24},{12,28},{16,0},{20,4},{24,8},{28,12},{1,17},{... | collective-permute-start | bytes 663560 | tf_op jit(solution)/shard_map/ppermute | solution.py:32
  45.3 0.8 %collective-permute-done.11.refs_2_ = bf16[144,768]{1,0:T(8,128)(2,1)S(1)} collective-permute-done((bf16[144,768]{1,0:T(8,128)(2,1)S(1)}, bf16[144,768]{1,0:T(8,128)(2,1)S(1)}, u32[]{:S(2)}, u32[]{:S(2)}) %collective-permute-start.11) | collective-permute-done | bytes 221216 | tf_op jit(solution)/shard_map/ppermute | solution.py:32
  46.1 0.7 %combine.2 = (bf16[128,768]{1,0:T(8,128)(2,1)S(1)}, bf16[128,384]{1,0:T(8,128)(2,1)S(1)}, bf16[128,384]{1,0:T(8,128)(2,1)S(1)}) custom-call(f32[128,768]{1,0:T(8,128)S(1)} %get-tuple-element.56.refs_1_.refs_0_, f32[8,128]{1,0:T(8,128)S(1)} %get-tuple-element.57.refs_1_, bf16[144,768]{1,0:T(8,128)(2,1)S(1)} %collective-permute-done.11.refs_2_, ...), custom_call_target="tpu_custom_call" | custom-call | flops 150994 | bytes 2865 | tf_op jit(solution)/shard_map/combine/pallas_call | solution.py:76
  46.9 0.5 collective-permute-start.18
  47.4 0.7 project.2
  48.1 0.1 collective-permute-done.17.refs_1_
  48.2 0.2 collective-permute-done.18.refs_2_
  48.4 0.5 collective-permute-start.19
  48.9 7.0 %collective-permute-done.20.refs_2_ = bf16[144,768]{1,0:T(8,128)(2,1)S(1)} collective-permute-done((bf16[144,768]{1,0:T(8,128)(2,1)S(1)}, bf16[144,768]{1,0:T(8,128)(2,1)S(1)}, u32[]{:S(2)}, u32[]{:S(2)}) %collective-permute-start.20) | collective-permute-done | bytes 221216 | tf_op jit(solution)/shard_map/ppermute | solution.py:32
  55.9 0.7 %combine.3 = (bf16[128,768]{1,0:T(8,128)(2,1)S(1)}, bf16[128,384]{1,0:T(8,128)(2,1)S(1)}, bf16[128,384]{1,0:T(8,128)(2,1)S(1)}) custom-call(f32[128,768]{1,0:T(8,128)S(1)} %get-tuple-element.61.refs_1_.refs_14_.refs_0_, f32[8,128]{1,0:T(8,128)S(1)} %get-tuple-element.71.refs_1_, bf16[144,768]{1,0:T(8,128)(2,1)S(1)} %collective-permute-done.20.refs_2_, ...), custom_call_target="tpu_custom_call" | custom-call | flops 150994 | bytes 2865 | tf_op jit(solution)/shard_map/combine/pallas_call | solution.py:76
  56.8 0.5 collective-permute-start.23
  57.2 0.1 collective-permute-start.16
  57.3 0.7 %project.3 = (bf16[128,768]{1,0:T(8,128)(2,1)S(1)}, bf16[128,768]{1,0:T(8,128)(2,1)S(1)}, bf16[128,768]{1,0:T(8,128)(2,1)S(1)}) custom-call(bf16[128,768]{1,0:T(8,128)(2,1)S(1)} %get-tuple-element.72.refs_0_, bf16[768,3072]{1,0:T(8,128)(2,1)S(1)} %bitcast.4), custom_call_target="tpu_custom_call" | custom-call | flops 301989 | bytes 2752 | tf_op jit(solution)/shard_map/project/pallas_call | solution.py:76
  58.0 0.5 collective-permute-start.21
  58.6 0.5 collective-permute-start.24
  59.1 1.1 %fresh_kv.3 = (bf16[256,256]{1,0:T(8,128)(2,1)S(1)}, bf16[256,256]{1,0:T(8,128)(2,1)S(1)}) custom-call(bf16[128,768]{1,0:T(8,128)(2,1)S(1)} %relay.10.refs_11_.refs_0_, bf16[128,768]{1,0:T(8,128)(2,1)S(1)} %relay.11.refs_1_.refs_14_.refs_0_, bf16[128,768]{1,0:T(8,128)(2,1)S(1)} %get-tuple-element.58.refs_1_.refs_15_.refs_2_, ...), custom_call_target="tpu_custom_call" | custom-call | flops 402653 | bytes 2758 | tf_op jit(solution)/shard_map/fresh_kv/pallas_call | solution.py:76
  60.2 2.2 %update_caches.1 = (bf16[2048,256]{1,0:T(8,128)(2,1)}, bf16[2048,256]{1,0:T(8,128)(2,1)}, f32[8,128]{1,0:T(8,128)S(1)}) custom-call(bf16[256,256]{1,0:T(8,128)(2,1)S(1)} %get-tuple-element.54.refs_12_.refs_14_.refs_13_.refs_0_, bf16[256,256]{1,0:T(8,128)(2,1)S(1)} %get-tuple-element.78.refs_1_.refs_7_, ...), custom_call_target="tpu_custom_call" | custom-call | flops 67108 | bytes 2361 | tf_op jit(solution)/shard_map/update_caches/pallas_call | solution.py:76
  62.4 3.1 %collective-permute-done.24.refs_5_ = bf16[128,768]{1,0:T(8,128)(2,1)S(1)} collective-permute-done((bf16[128,768]{1,0:T(8,128)(2,1)S(1)}, bf16[128,768]{1,0:T(8,128)(2,1)S(1)}, u32[]{:S(2)}, u32[]{:S(2)}) %collective-permute-start.24) | collective-permute-done | bytes 196640 | tf_op jit(solution)/shard_map/ppermute | solution.py:32
  65.5 0.9 %finish.1 = bf16[256,768]{1,0:T(8,128)(2,1)} custom-call(bf16[128,768]{1,0:T(8,128)(2,1)S(1)} %get-tuple-element.66.refs_0_, bf16[128,768]{1,0:T(8,128)(2,1)S(1)} %collective-permute-done.16.refs_1_, bf16[128,768]{1,0:T(8,128)(2,1)S(1)} %collective-permute-done.19.refs_4_.refs_2_, bf16[128,768]{1,0:T(8,128)(2,1)S(1)} %get-tuple-element.73.refs_3_, ...), custom_call_target="tpu_custom_call" | custom-call | bytes 786 | tf_op jit(solution)/shard_map/finish/pallas_call | solution.py:76
  (52 shorter events, 0.6 us)
Async XLA Ops:
  0.6 12.4 %collective-permute-start = (bf16[256,768]{1,0:T(8,128)(2,1)}, bf16[256,768]{1,0:T(8,128)(2,1)S(1)}, u32[]{:S(2)}, u32[]{:S(2)}) collective-permute-start(bf16[256,768]{1,0:T(8,128)(2,1)} %refs_0_.3), channel_id=1, source_target_pairs={{0,2},{1,3},{2,0},{3,1},{4,6},{5,7},{6,4},{7,5},{8,10},{9,11},{10,... | collective-permute-start | bytes 1179656 | tf_op jit(solution)/shard_map/ppermute | solution.py:32
  3.7 14.1 %collective-permute-start.1 = (bf16[256,768]{1,0:T(8,128)(2,1)}, bf16[256,768]{1,0:T(8,128)(2,1)S(1)}, u32[]{:S(2)}, u32[]{:S(2)}) collective-permute-start(bf16[256,768]{1,0:T(8,128)(2,1)} %refs_0_.3), channel_id=1, source_target_pairs={{0,1},{1,0},{2,3},{3,2},{4,5},{5,4},{6,7},{7,6},{8,9},{9,8},{10,11... | collective-permute-start | bytes 1179656 | tf_op jit(solution)/shard_map/ppermute | solution.py:37
  3.7 1.0 %copy-start.5 = (bf16[256,768]{1,0:T(8,128)(2,1)S(1)}, bf16[256,768]{1,0:T(8,128)(2,1)}, u32[]{:S(2)}) copy-start(bf16[256,768]{1,0:T(8,128)(2,1)} %refs_0_.3) | copy-start | bytes 1179652
  4.7 2.7 %copy-start.6 = (s32[4]{0:T(128)S(1)}, s32[4]{0:T(128)}, u32[]{:S(2)}) copy-start(s32[4]{0:T(128)} %refs_6_.7) | copy-start | bytes 52
  4.8 2.7 %copy-start.7 = (s32[4]{0:T(128)S(1)}, s32[4]{0:T(128)}, u32[]{:S(2)}) copy-start(s32[4]{0:T(128)} %refs_1_.4) | copy-start | bytes 52
  4.8 4.3 %copy-start.2 = (bf16[2048,256]{1,0:T(8,128)(2,1)S(1)}, bf16[2048,256]{1,0:T(8,128)(2,1)}, u32[]{:S(2)}) copy-start(bf16[2048,256]{1,0:T(8,128)(2,1)} %refs_4_.1) | copy-start | bytes 3145732
  4.8 4.3 %copy-start.3 = (bf16[2048,256]{1,0:T(8,128)(2,1)S(1)}, bf16[2048,256]{1,0:T(8,128)(2,1)}, u32[]{:S(2)}) copy-start(bf16[2048,256]{1,0:T(8,128)(2,1)} %refs_5_.1) | copy-start | bytes 3145732
  4.8 12.5 %collective-permute-start.5 = (bf16[128,768]{1,0:T(8,128)(2,1)S(1)}, bf16[128,768]{1,0:T(8,128)(2,1)S(1)}, u32[]{:S(2)}, u32[]{:S(2)}) collective-permute-start(bf16[128,768]{1,0:T(8,128)(2,1)S(1)} %get-tuple-element.53), channel_id=1, source_target_pairs={{0,16},{4,20},{8,24},{12,28},{16,0},{20,4},{24,8},{28,12},{1,17},{... | collective-permute-start | bytes 589832 | tf_op jit(solution)/shard_map/ppermute | solution.py:32
  7.4 13.0 %slice-start = ((s8[4718592]{0:T(1024)(128)(4,1)}), s8[4194304]{0:T(1024)(128)(4,1)S(1)}, s32[]{:S(2)}) async-start(s8[4718592]{0:T(1024)(128)(4,1)} %bitcast.1), calls=%async_computation | async-start | bytes 8388608
  9.1 11.4 %slice-start.1 = ((s8[4718592]{0:T(1024)(128)(4,1)}), s8[524288]{0:T(1024)(128)(4,1)S(1)}, s32[]{:S(2)}) async-start(s8[4718592]{0:T(1024)(128)(4,1)} %bitcast.1), calls=%async_computation.1 | async-start | bytes 1048576
  13.0 6.3 %copy-start = (bf16[3072,256]{1,0:T(8,128)(2,1)S(1)}, bf16[3072,256]{1,0:T(8,128)(2,1)}, u32[]{:S(2)}) copy-start(bf16[3072,256]{1,0:T(8,128)(2,1)} %refs_11_.1) | copy-start | bytes 4718596
  13.0 6.3 %copy-start.1 = (bf16[3072,256]{1,0:T(8,128)(2,1)S(1)}, bf16[3072,256]{1,0:T(8,128)(2,1)}, u32[]{:S(2)}) copy-start(bf16[3072,256]{1,0:T(8,128)(2,1)} %refs_12_.1) | copy-start | bytes 4718596
  13.0 6.3 %copy-start.4 = (f32[3072]{0:T(1024)S(1)}, f32[3072]{0:T(1024)}, u32[]{:S(2)}) copy-start(f32[3072]{0:T(1024)} %param.11) | copy-start | bytes 36868
  13.1 6.2 %collective-permute-start.4 = (bf16[128,768]{1,0:T(8,128)(2,1)S(1)}, bf16[128,768]{1,0:T(8,128)(2,1)S(1)}, u32[]{:S(2)}, u32[]{:S(2)}) collective-permute-start(bf16[128,768]{1,0:T(8,128)(2,1)S(1)} %get-tuple-element.52), channel_id=1, source_target_pairs={{0,1},{1,0},{2,3},{3,2},{4,5},{5,4},{6,7},{7,6},{8,9},{9,8},{10,11... | collective-permute-start | bytes 589832 | tf_op jit(solution)/shard_map/ppermute | solution.py:37
  13.2 12.6 %collective-permute-start.7 = (bf16[128,768]{1,0:T(8,128)(2,1)S(1)}, bf16[128,768]{1,0:T(8,128)(2,1)S(1)}, u32[]{:S(2)}, u32[]{:S(2)}) collective-permute-start(bf16[128,768]{1,0:T(8,128)(2,1)S(1)} %relay.8.refs_1_), channel_id=1, source_target_pairs={{0,16},{4,20},{8,24},{12,28},{16,0},{20,4},{24,8},{28,12},{1,17},{... | collective-permute-start | bytes 589832 | tf_op jit(solution)/shard_map/ppermute | solution.py:32
  17.3 10.1 %collective-permute-start.6 = (bf16[128,768]{1,0:T(8,128)(2,1)S(1)}, bf16[128,768]{1,0:T(8,128)(2,1)S(1)}, u32[]{:S(2)}, u32[]{:S(2)}) collective-permute-start(bf16[128,768]{1,0:T(8,128)(2,1)S(1)} %relay.10.refs_11_.refs_0_), channel_id=1, source_target_pairs={{0,2},{1,3},{2,0},{3,1},{4,6},{5,7},{6,4},{7,5},{8,10},{9,11},{10,... | collective-permute-start | bytes 589832 | tf_op jit(solution)/shard_map/ppermute | solution.py:32
  17.8 1.3 %collective-permute-start.2 = (bf16[64,768]{1,0:T(8,128)(2,1)S(1)}, bf16[64,768]{1,0:T(8,128)(2,1)S(1)}, u32[]{:S(2)}, u32[]{:S(2)}) collective-permute-start(bf16[64,768]{1,0:T(8,128)(2,1)S(1)} %get-tuple-element.48), channel_id=1, source_target_pairs={{0,1},{1,0},{2,3},{3,2},{4,5},{5,4},{6,7},{7,6},{8,9},{9,8},{10,11... | collective-permute-start | bytes 294920 | tf_op jit(solution)/shard_map/ppermute | solution.py:37
  17.8 1.5 %collective-permute-start.3 = (bf16[64,768]{1,0:T(8,128)(2,1)S(1)}, bf16[64,768]{1,0:T(8,128)(2,1)S(1)}, u32[]{:S(2)}, u32[]{:S(2)}) collective-permute-start(bf16[64,768]{1,0:T(8,128)(2,1)S(1)} %get-tuple-element.49), channel_id=1, source_target_pairs={{0,1},{1,0},{2,3},{3,2},{4,5},{5,4},{6,7},{7,6},{8,9},{9,8},{10,11... | collective-permute-start | bytes 294920 | tf_op jit(solution)/shard_map/ppermute | solution.py:37
  19.1 9.0 %collective-permute-start.8 = (bf16[128,768]{1,0:T(8,128)(2,1)S(1)}, bf16[128,768]{1,0:T(8,128)(2,1)S(1)}, u32[]{:S(2)}, u32[]{:S(2)}) collective-permute-start(bf16[128,768]{1,0:T(8,128)(2,1)S(1)} %relay.10.refs_11_.refs_0_), channel_id=1, source_target_pairs={{0,1},{1,0},{2,3},{3,2},{4,5},{5,4},{6,7},{7,6},{8,9},{9,8},{10,11... | collective-permute-start | bytes 589832 | tf_op jit(solution)/shard_map/ppermute | solution.py:37
  25.8 11.2 %collective-permute-start.12 = (bf16[128,768]{1,0:T(8,128)(2,1)S(1)}, bf16[128,768]{1,0:T(8,128)(2,1)S(1)}, u32[]{:S(2)}, u32[]{:S(2)}) collective-permute-start(bf16[128,768]{1,0:T(8,128)(2,1)S(1)} %relay.11.refs_1_.refs_14_.refs_0_), channel_id=1, source_target_pairs={{0,2},{1,3},{2,0},{3,1},{4,6},{5,7},{6,4},{7,5},{8,10},{9,11},{10,... | collective-permute-start | bytes 589832 | tf_op jit(solution)/shard_map/ppermute | solution.py:32
  27.4 1.4 %collective-permute-start.10 = (bf16[64,768]{1,0:T(8,128)(2,1)S(1)}, bf16[64,768]{1,0:T(8,128)(2,1)S(1)}, u32[]{:S(2)}, u32[]{:S(2)}) collective-permute-start(bf16[64,768]{1,0:T(8,128)(2,1)S(1)} %get-tuple-element.60), channel_id=1, source_target_pairs={{0,1},{1,0},{2,3},{3,2},{4,5},{5,4},{6,7},{7,6},{8,9},{9,8},{10,11... | collective-permute-start | bytes 294920 | tf_op jit(solution)/shard_map/ppermute | solution.py:37
  27.5 1.4 %collective-permute-start.9 = (bf16[64,768]{1,0:T(8,128)(2,1)S(1)}, bf16[64,768]{1,0:T(8,128)(2,1)S(1)}, u32[]{:S(2)}, u32[]{:S(2)}) collective-permute-start(bf16[64,768]{1,0:T(8,128)(2,1)S(1)} %get-tuple-element.59), channel_id=1, source_target_pairs={{0,1},{1,0},{2,3},{3,2},{4,5},{5,4},{6,7},{7,6},{8,9},{9,8},{10,11... | collective-permute-start | bytes 294920 | tf_op jit(solution)/shard_map/ppermute | solution.py:37
  28.0 9.5 %collective-permute-start.13 = (bf16[128,768]{1,0:T(8,128)(2,1)S(1)}, bf16[128,768]{1,0:T(8,128)(2,1)S(1)}, u32[]{:S(2)}, u32[]{:S(2)}) collective-permute-start(bf16[128,768]{1,0:T(8,128)(2,1)S(1)} %relay.11.refs_1_.refs_14_.refs_0_), channel_id=1, source_target_pairs={{0,1},{1,0},{2,3},{3,2},{4,5},{5,4},{6,7},{7,6},{8,9},{9,8},{10,11... | collective-permute-start | bytes 589832 | tf_op jit(solution)/shard_map/ppermute | solution.py:37
  32.7 13.4 %collective-permute-start.11 = (bf16[144,768]{1,0:T(8,128)(2,1)S(1)}, bf16[144,768]{1,0:T(8,128)(2,1)S(1)}, u32[]{:S(2)}, u32[]{:S(2)}) collective-permute-start(bf16[144,768]{1,0:T(8,128)(2,1)S(1)} %attend_partner.2.refs_15_), channel_id=1, source_target_pairs={{0,16},{4,20},{8,24},{12,28},{16,0},{20,4},{24,8},{28,12},{1,17},{... | collective-permute-start | bytes 663560 | tf_op jit(solution)/shard_map/ppermute | solution.py:32
  37.0 1.4 %collective-permute-start.14 = (bf16[64,768]{1,0:T(8,128)(2,1)S(1)}, bf16[64,768]{1,0:T(8,128)(2,1)S(1)}, u32[]{:S(2)}, u32[]{:S(2)}) collective-permute-start(bf16[64,768]{1,0:T(8,128)(2,1)S(1)} %get-tuple-element.63), channel_id=1, source_target_pairs={{0,1},{1,0},{2,3},{3,2},{4,5},{5,4},{6,7},{7,6},{8,9},{9,8},{10,11... | collective-permute-start | bytes 294920 | tf_op jit(solution)/shard_map/ppermute | solution.py:37
  37.4 1.3 %collective-permute-start.15 = (bf16[64,768]{1,0:T(8,128)(2,1)S(1)}, bf16[64,768]{1,0:T(8,128)(2,1)S(1)}, u32[]{:S(2)}, u32[]{:S(2)}) collective-permute-start(bf16[64,768]{1,0:T(8,128)(2,1)S(1)} %get-tuple-element.64), channel_id=1, source_target_pairs={{0,1},{1,0},{2,3},{3,2},{4,5},{5,4},{6,7},{7,6},{8,9},{9,8},{10,11... | collective-permute-start | bytes 294920 | tf_op jit(solution)/shard_map/ppermute | solution.py:37
  38.7 7.4 %slice-start.2 = ((s8[4718592]{0:T(1024)(128)(4,1)}), s8[4194304]{0:T(1024)(128)(4,1)S(1)}, s32[]{:S(2)}) async-start(s8[4718592]{0:T(1024)(128)(4,1)} %bitcast.3), calls=%async_computation.2 | async-start | bytes 8388608
  38.7 7.4 %slice-start.3 = ((s8[4718592]{0:T(1024)(128)(4,1)}), s8[524288]{0:T(1024)(128)(4,1)S(1)}, s32[]{:S(2)}) async-start(s8[4718592]{0:T(1024)(128)(4,1)} %bitcast.3), calls=%async_computation.3 | async-start | bytes 1048576
  42.5 13.4 %collective-permute-start.20 = (bf16[144,768]{1,0:T(8,128)(2,1)S(1)}, bf16[144,768]{1,0:T(8,128)(2,1)S(1)}, u32[]{:S(2)}, u32[]{:S(2)}) collective-permute-start(bf16[144,768]{1,0:T(8,128)(2,1)S(1)} %attend_partner.3.refs_4_), channel_id=1, source_target_pairs={{0,16},{4,20},{8,24},{12,28},{16,0},{20,4},{24,8},{28,12},{1,17},{... | collective-permute-start | bytes 663560 | tf_op jit(solution)/shard_map/ppermute | solution.py:32
  46.8 1.4 %collective-permute-start.17 = (bf16[128,384]{1,0:T(8,128)(2,1)S(1)}, bf16[128,384]{1,0:T(8,128)(2,1)S(1)}, u32[]{:S(2)}, u32[]{:S(2)}) collective-permute-start(bf16[128,384]{1,0:T(8,128)(2,1)S(1)} %get-tuple-element.69), channel_id=1, source_target_pairs={{0,1},{1,0},{2,3},{3,2},{4,5},{5,4},{6,7},{7,6},{8,9},{9,8},{10,11... | collective-permute-start | bytes 294920 | tf_op jit(solution)/shard_map/ppermute | solution.py:37
  46.9 1.4 %collective-permute-start.18 = (bf16[128,384]{1,0:T(8,128)(2,1)S(1)}, bf16[128,384]{1,0:T(8,128)(2,1)S(1)}, u32[]{:S(2)}, u32[]{:S(2)}) collective-permute-start(bf16[128,384]{1,0:T(8,128)(2,1)S(1)} %get-tuple-element.70), channel_id=1, source_target_pairs={{0,1},{1,0},{2,3},{3,2},{4,5},{5,4},{6,7},{7,6},{8,9},{9,8},{10,11... | collective-permute-start | bytes 294920 | tf_op jit(solution)/shard_map/ppermute | solution.py:37
  48.4 10.1 %collective-permute-start.19 = (bf16[128,768]{1,0:T(8,128)(2,1)S(1)}, bf16[128,768]{1,0:T(8,128)(2,1)S(1)}, u32[]{:S(2)}, u32[]{:S(2)}) collective-permute-start(bf16[128,768]{1,0:T(8,128)(2,1)S(1)} %sum_cores.2.refs_4_), channel_id=1, source_target_pairs={{0,2},{1,3},{2,0},{3,1},{4,6},{5,7},{6,4},{7,5},{8,10},{9,11},{10,... | collective-permute-start | bytes 589832 | tf_op jit(solution)/shard_map/ppermute | solution.py:32
  56.7 1.8 %collective-permute-start.22 = (bf16[128,384]{1,0:T(8,128)(2,1)S(1)}, bf16[128,384]{1,0:T(8,128)(2,1)S(1)}, u32[]{:S(2)}, u32[]{:S(2)}) collective-permute-start(bf16[128,384]{1,0:T(8,128)(2,1)S(1)} %get-tuple-element.76), channel_id=1, source_target_pairs={{0,1},{1,0},{2,3},{3,2},{4,5},{5,4},{6,7},{7,6},{8,9},{9,8},{10,11... | collective-permute-start | bytes 294920 | tf_op jit(solution)/shard_map/ppermute | solution.py:37
  56.8 1.8 %collective-permute-start.23 = (bf16[128,384]{1,0:T(8,128)(2,1)S(1)}, bf16[128,384]{1,0:T(8,128)(2,1)S(1)}, u32[]{:S(2)}, u32[]{:S(2)}) collective-permute-start(bf16[128,384]{1,0:T(8,128)(2,1)S(1)} %get-tuple-element.77), channel_id=1, source_target_pairs={{0,1},{1,0},{2,3},{3,2},{4,5},{5,4},{6,7},{7,6},{8,9},{9,8},{10,11... | collective-permute-start | bytes 294920 | tf_op jit(solution)/shard_map/ppermute | solution.py:37
  57.2 5.1 %collective-permute-start.16 = (bf16[128,768]{1,0:T(8,128)(2,1)S(1)}, bf16[128,768]{1,0:T(8,128)(2,1)S(1)}, u32[]{:S(2)}, u32[]{:S(2)}) collective-permute-start(bf16[128,768]{1,0:T(8,128)(2,1)S(1)} %get-tuple-element.67.refs_3_), channel_id=1, source_target_pairs={{0,1},{1,0},{2,3},{3,2},{4,5},{5,4},{6,7},{7,6},{8,9},{9,8},{10,11... | collective-permute-start | bytes 589832 | tf_op jit(solution)/shard_map/ppermute | solution.py:37
  58.0 4.4 %collective-permute-start.21 = (bf16[128,768]{1,0:T(8,128)(2,1)S(1)}, bf16[128,768]{1,0:T(8,128)(2,1)S(1)}, u32[]{:S(2)}, u32[]{:S(2)}) collective-permute-start(bf16[128,768]{1,0:T(8,128)(2,1)S(1)} %get-tuple-element.74.refs_3_), channel_id=1, source_target_pairs={{0,1},{1,0},{2,3},{3,2},{4,5},{5,4},{6,7},{7,6},{8,9},{9,8},{10,11... | collective-permute-start | bytes 589832 | tf_op jit(solution)/shard_map/ppermute | solution.py:37
  58.6 7.0 %collective-permute-start.24 = (bf16[128,768]{1,0:T(8,128)(2,1)S(1)}, bf16[128,768]{1,0:T(8,128)(2,1)S(1)}, u32[]{:S(2)}, u32[]{:S(2)}) collective-permute-start(bf16[128,768]{1,0:T(8,128)(2,1)S(1)} %sum_cores.3.refs_15_), channel_id=1, source_target_pairs={{0,2},{1,3},{2,0},{3,1},{4,6},{5,7},{6,4},{7,5},{8,10},{9,11},{10,... | collective-permute-start | bytes 589832 | tf_op jit(solution)/shard_map/ppermute | solution.py:32

commit v16 on v10

--- a/solution.py
+++ b/solution.py
@@ -587,22 +587,31 @@
     )[0]
 
 
-def finish_kernel(*refs):
-    *parts, result = refs
+def collect_kernel(count, *refs):
+    *parts, ready, base = refs
+    ready[...] = sum(ref[...].astype(jnp.float32) for ref in parts[:count]).astype(ready.dtype)
+    base[...] = sum(ref[...].astype(jnp.float32) for ref in parts[count:])
+
+
+def finish_kernel(ready, base, *refs):
+    *landed, result = refs
+    rows = ready.shape[0]
+    result[:rows] = ready[...]
+    total = base[...]
+    for ref in landed:
+        total = total + ref[...].astype(jnp.float32)
+    result[rows:] = total.astype(result.dtype)
+
+
+def finish(parts, earlier):
     count = len(parts) // CHUNKS
-    rows = parts[0].shape[0]
-    for chunk in range(CHUNKS):
-        total = 0.0
-        for ref in parts[chunk * count : (chunk + 1) * count]:
-            total = total + ref[...].astype(jnp.float32)
-        result[chunk * rows : (chunk + 1) * rows] = total.astype(jnp.bfloat16)
-
-
-def finish(parts, earlier):
     rows, width = parts[0].shape
-    shape = jax.ShapeDtypeStruct((CHUNKS * rows, width), jnp.bfloat16)
-    flops = CHUNKS * rows * width
-    return call(finish_kernel, [shape], parts, 8, flops, 0, "finish", earlier)[0]
+    shape = jax.ShapeDtypeStruct((rows, width), jnp.bfloat16)
+    base = jax.ShapeDtypeStruct((rows, width), jnp.float32)
+    kernel = functools.partial(collect_kernel, count)
+    found = call(kernel, [shape, base], parts[: count + CORES], 8, 0, 0, "collect", earlier)
+    result = jax.ShapeDtypeStruct((CHUNKS * rows, width), jnp.bfloat16)
+    return call(finish_kernel, [result], [*found, *parts[count + CORES :]], 8, 0, 0, "finish")[0]
 
 
 def shards(

time: 64.9 us -> 64.9 us (level)
    pallas_call x25 -> x26, Pallas kernels: 27.7 us -> 27.7 us  [call(): pl.pallas_call(body, out_shape=out_shape, in_specs=[VMEM] * len(arrays) +...]
  transfers between devices with their start and end apart: 25 -> 25, of which waited for: 10 -> 10; matrix products, arithmetic and copies ran while one was open for 0% -> 0% of each run, Pallas kernels for 41% -> 42%
where the time goes in v16:
time: 64.9 us; the launch traced here: 64.7 us
  Pallas kernels  27.7 us (43%)
  starting transfers between devices  19.4 us (30%)
  waiting for transfers between devices  15.4 us (24%)
  local copies, waits for them, and re-layouts  1.09 us (2%)
  between operations  0.97 us (1%)
    pallas_call x26, Pallas kernels, call(): pl.pallas_call(body, out_shape=out_shape, in_specs=[VMEM] * len(arrays) +...  27.7 us
    ppermute x9, starting transfers between devices, shifted(): lax.ppermute(shard, axis, [(i, (i + by) % devices) for i in range(devices)])  15.7 us
    ppermute x9, waiting for transfers between devices, shifted(): lax.ppermute(shard, axis, [(i, (i + by) % devices) for i in range(devices)])  13.1 us
    ppermute x16, starting transfers between devices, other_core(): return lax.ppermute(shard, 'head', [(i, i ^ 1) for i in range(devices)])  3.72 us
    ppermute x16, waiting for transfers between devices, other_core(): return lax.ppermute(shard, 'head', [(i, i ^ 1) for i in range(devices)])  2.29 us
  transfers between devices with their start and end apart: 25, of which 10 were waited for; matrix products, arithmetic and copies ran while one was open for 0% of the time, Pallas kernels for 42%

profile of v16, /device:TPU:0, one launch (start us, length us, event | category | flops | bytes accessed | tf_op | source)
XLA Modules:
  0.0 64.7 jit_solution(12937704114606340191)
XLA Ops:
  0.6 3.0 %collective-permute-start = (bf16[256,768]{1,0:T(8,128)(2,1)}, bf16[256,768]{1,0:T(8,128)(2,1)S(1)}, u32[]{:S(2)}, u32[]{:S(2)}) collective-permute-start(bf16[256,768]{1,0:T(8,128)(2,1)} %refs_0_.3), channel_id=1, source_target_pairs={{0,2},{1,3},{2,0},{3,1},{4,6},{5,7},{6,4},{7,5},{8,10},{9,11},{10,... | collective-permute-start | bytes 1179656 | tf_op jit(solution)/shard_map/ppermute | solution.py:32
  3.7 1.0 %copy-done.5 = bf16[256,768]{1,0:T(8,128)(2,1)S(1)} copy-done((bf16[256,768]{1,0:T(8,128)(2,1)S(1)}, bf16[256,768]{1,0:T(8,128)(2,1)}, u32[]{:S(2)}) %copy-start.5) | copy-done | bytes 393240
  4.8 2.7 %collective-permute-start.4 = (bf16[128,768]{1,0:T(8,128)(2,1)S(1)}, bf16[128,768]{1,0:T(8,128)(2,1)S(1)}, u32[]{:S(2)}, u32[]{:S(2)}) collective-permute-start(bf16[128,768]{1,0:T(8,128)(2,1)S(1)} %get-tuple-element.58), channel_id=1, source_target_pairs={{0,16},{4,20},{8,24},{12,28},{16,0},{20,4},{24,8},{28,12},{1,17},{... | collective-permute-start | bytes 589832 | tf_op jit(solution)/shard_map/ppermute | solution.py:32
  7.5 1.6 %rope_tables.1 = (f32[512,128]{1,0:T(8,128)S(1)}, f32[512,128]{1,0:T(8,128)S(1)}) custom-call(s32[4]{0:T(128)S(1)} %copy-done.6, s32[4]{0:T(128)S(1)} %copy-done.7, bf16[2048,128]{1,0:T(8,128)(2,1)S(1)} %marks.1.refs_2_.refs_11_.refs_12_), custom_call_target="tpu_custom_call" | custom-call | bytes 262 | tf_op jit(solution)/shard_map/rope_tables/pallas_call | solution.py:76
  9.1 0.8 %widen_caches.1 = (bf16[2,2048,256]{2,1,0:T(8,128)(2,1)S(1)}, bf16[2,2048,256]{2,1,0:T(8,128)(2,1)S(1)}) custom-call(bf16[2048,256]{1,0:T(8,128)(2,1)S(1)} %copy-done.2, bf16[2048,256]{1,0:T(8,128)(2,1)S(1)} %copy-done.3, bf16[2048,128]{1,0:T(8,128)(2,1)S(1)} %marks.1.refs_2_.refs_11_.refs_12_, s32[4]{0:T(128)S(1)} %copy-done.6, ...), custom_call_target="tpu_custom_call" | custom-call | bytes 3407 | tf_op jit(solution)/shard_map/widen_caches/pallas_call | solution.py:76
  9.9 3.1 %collective-permute-done.refs_1_.refs_0_ = bf16[256,768]{1,0:T(8,128)(2,1)S(1)} collective-permute-done((bf16[256,768]{1,0:T(8,128)(2,1)}, bf16[256,768]{1,0:T(8,128)(2,1)S(1)}, u32[]{:S(2)}, u32[]{:S(2)}) %collective-permute-start) | collective-permute-done | bytes 393248 | tf_op jit(solution)/shard_map/ppermute | solution.py:32
  13.1 0.1 collective-permute-start.5
  13.1 2.9 %collective-permute-start.7 = (bf16[128,768]{1,0:T(8,128)(2,1)S(1)}, bf16[128,768]{1,0:T(8,128)(2,1)S(1)}, u32[]{:S(2)}, u32[]{:S(2)}) collective-permute-start(bf16[128,768]{1,0:T(8,128)(2,1)S(1)} %relay.8.refs_1_), channel_id=1, source_target_pairs={{0,16},{4,20},{8,24},{12,28},{16,0},{20,4},{24,8},{28,12},{1,17},{... | collective-permute-start | bytes 589832 | tf_op jit(solution)/shard_map/ppermute | solution.py:32
  16.0 1.2 %collective-permute-done.4.refs_0_ = bf16[128,768]{1,0:T(8,128)(2,1)S(1)} collective-permute-done((bf16[128,768]{1,0:T(8,128)(2,1)S(1)}, bf16[128,768]{1,0:T(8,128)(2,1)S(1)}, u32[]{:S(2)}, u32[]{:S(2)}) %collective-permute-start.4) | collective-permute-done | bytes 196640 | tf_op jit(solution)/shard_map/ppermute | solution.py:32
  17.3 0.5 collective-permute-start.6
  17.8 0.5 collective-permute-start.3
  18.3 0.8 %collective-permute-done.2.refs_3_ = bf16[64,768]{1,0:T(8,128)(2,1)S(1)} collective-permute-done((bf16[64,768]{1,0:T(8,128)(2,1)S(1)}, bf16[64,768]{1,0:T(8,128)(2,1)S(1)}, u32[]{:S(2)}, u32[]{:S(2)}) %collective-permute-start.2) | collective-permute-done | bytes 98336 | tf_op jit(solution)/shard_map/ppermute | solution.py:37
  19.1 0.2 collective-permute-start.8
  19.3 3.5 %attend_own.2 = (f32[128,768]{1,0:T(8,128)S(1)}, f32[8,128]{1,0:T(8,128)S(1)}, bf16[128,768]{1,0:T(8,128)(2,1)S(1)}) custom-call(bf16[256,768]{1,0:T(8,128)(2,1)S(1)} %get-tuple-element.49.refs_0_, bf16[256,768]{1,0:T(8,128)(2,1)S(1)} %get-tuple-element.53.refs_1_, bf16[256,768]{1,0:T(8,128)(2,1)S(1)} %collective-permute-done.1.refs_2_, ...), custom_call_target="tpu_custom_call" | custom-call | flops 1107296 | bytes 5971 | tf_op jit(solution)/shard_map/attend_own/pallas_call | solution.py:76
  22.9 1.1 %fresh_kv.2 = (bf16[256,256]{1,0:T(8,128)(2,1)S(1)}, bf16[256,256]{1,0:T(8,128)(2,1)S(1)}) custom-call(bf16[256,768]{1,0:T(8,128)(2,1)S(1)} %get-tuple-element.49.refs_0_, bf16[256,768]{1,0:T(8,128)(2,1)S(1)} %get-tuple-element.53.refs_1_, bf16[256,768]{1,0:T(8,128)(2,1)S(1)} %collective-permute-done.1.refs_2_, ...), custom_call_target="tpu_custom_call" | custom-call | flops 402653 | bytes 2758 | tf_op jit(solution)/shard_map/fresh_kv/pallas_call | solution.py:76
  24.0 1.7 %collective-permute-done.7.refs_0_ = bf16[128,768]{1,0:T(8,128)(2,1)S(1)} collective-permute-done((bf16[128,768]{1,0:T(8,128)(2,1)S(1)}, bf16[128,768]{1,0:T(8,128)(2,1)S(1)}, u32[]{:S(2)}, u32[]{:S(2)}) %collective-permute-start.7) | collective-permute-done | bytes 196640 | tf_op jit(solution)/shard_map/ppermute | solution.py:32
  25.8 0.1 collective-permute-start.9
  25.9 0.5 collective-permute-start.10
  26.4 1.6 %collective-permute-start.11 = (bf16[128,768]{1,0:T(8,128)(2,1)S(1)}, bf16[128,768]{1,0:T(8,128)(2,1)S(1)}, u32[]{:S(2)}, u32[]{:S(2)}) collective-permute-start(bf16[128,768]{1,0:T(8,128)(2,1)S(1)} %relay.11.refs_1_.refs_12_.refs_0_), channel_id=1, source_target_pairs={{0,2},{1,3},{2,0},{3,1},{4,6},{5,7},{6,4},{7,5},{8,10},{9,11},{10,... | collective-permute-start | bytes 589832 | tf_op jit(solution)/shard_map/ppermute | solution.py:32
  28.0 3.6 %attend_partner.2.refs_13_ = bf16[144,768]{1,0:T(8,128)(2,1)S(1)} custom-call(bf16[128,768]{1,0:T(8,128)(2,1)S(1)} %relay.10.refs_12_.refs_0_, bf16[128,768]{1,0:T(8,128)(2,1)S(1)} %get-tuple-element.64.refs_1_.refs_13_.refs_2_, bf16[128,768]{1,0:T(8,128)(2,1)S(1)} %collective-permute-done.8.refs_2_.refs_4_, ...), custom_call_target="tpu_custom_call" | custom-call | flops 1107296 | bytes 5490 | tf_op jit(solution)/shard_map/attend_partner/pallas_call | solution.py:76
  31.6 0.1 collective-permute-start.12
  31.6 3.8 %attend_own.3 = (f32[128,768]{1,0:T(8,128)S(1)}, f32[8,128]{1,0:T(8,128)S(1)}, bf16[128,768]{1,0:T(8,128)(2,1)S(1)}) custom-call(bf16[256,768]{1,0:T(8,128)(2,1)S(1)} %get-tuple-element.49.refs_0_, bf16[256,768]{1,0:T(8,128)(2,1)S(1)} %get-tuple-element.53.refs_1_, bf16[256,768]{1,0:T(8,128)(2,1)S(1)} %collective-permute-done.1.refs_2_, ...), custom_call_target="tpu_custom_call" | custom-call | flops 1107296 | bytes 6070 | tf_op jit(solution)/shard_map/attend_own/pallas_call | solution.py:76
  35.4 0.6 collective-permute-start.13
  36.0 0.1 collective-permute-start.14
  36.1 0.9 %collective-permute-done.13.refs_3_.refs_8_ = bf16[64,768]{1,0:T(8,128)(2,1)S(1)} collective-permute-done((bf16[64,768]{1,0:T(8,128)(2,1)S(1)}, bf16[64,768]{1,0:T(8,128)(2,1)S(1)}, u32[]{:S(2)}, u32[]{:S(2)}) %collective-permute-start.13) | collective-permute-done | bytes 98336 | tf_op jit(solution)/shard_map/ppermute | solution.py:37
  36.9 0.4 collective-permute-done.14.refs_4_.refs_9_
  37.3 3.5 %attend_partner.3.refs_15_ = bf16[144,768]{1,0:T(8,128)(2,1)S(1)} custom-call(bf16[128,768]{1,0:T(8,128)(2,1)S(1)} %relay.11.refs_1_.refs_12_.refs_0_, bf16[128,768]{1,0:T(8,128)(2,1)S(1)} %get-tuple-element.68.refs_1_.refs_13_.refs_3_, bf16[128,768]{1,0:T(8,128)(2,1)S(1)} %collective-permute-done.12.refs_2_.refs_5_, ...), custom_call_target="tpu_custom_call" | custom-call | flops 1107296 | bytes 5490 | tf_op jit(solution)/shard_map/attend_partner/pallas_call | solution.py:76
  40.8 2.9 %collective-permute-start.20 = (bf16[144,768]{1,0:T(8,128)(2,1)S(1)}, bf16[144,768]{1,0:T(8,128)(2,1)S(1)}, u32[]{:S(2)}, u32[]{:S(2)}) collective-permute-start(bf16[144,768]{1,0:T(8,128)(2,1)S(1)} %attend_partner.3.refs_15_), channel_id=1, source_target_pairs={{0,16},{4,20},{8,24},{12,28},{16,0},{20,4},{24,8},{28,12},{1,17},{... | collective-permute-start | bytes 663560 | tf_op jit(solution)/shard_map/ppermute | solution.py:32
  43.7 1.1 %fresh_kv.3 = (bf16[256,256]{1,0:T(8,128)(2,1)S(1)}, bf16[256,256]{1,0:T(8,128)(2,1)S(1)}) custom-call(bf16[128,768]{1,0:T(8,128)(2,1)S(1)} %relay.10.refs_12_.refs_0_, bf16[128,768]{1,0:T(8,128)(2,1)S(1)} %relay.11.refs_1_.refs_12_.refs_0_, bf16[128,768]{1,0:T(8,128)(2,1)S(1)} %get-tuple-element.64.refs_1_.refs_13_.refs_2_, ...), custom_call_target="tpu_custom_call" | custom-call | flops 402653 | bytes 2758 | tf_op jit(solution)/shard_map/fresh_kv/pallas_call | solution.py:76
  44.8 2.3 %attend_fresh.1 = (f32[256,768]{1,0:T(8,128)S(1)}, f32[8,256]{1,0:T(8,128)S(1)}) custom-call(bf16[128,768]{1,0:T(8,128)(2,1)S(1)} %get-tuple-element.61.refs_11_.refs_0_, bf16[128,768]{1,0:T(8,128)(2,1)S(1)} %get-tuple-element.67.refs_1_.refs_12_, bf16[256,256]{1,0:T(8,128)(2,1)S(1)} %get-tuple-element.63.refs_1_.refs_2_.refs_0_, ...), custom_call_target="tpu_custom_call" | custom-call | flops 201326 | bytes 856 | tf_op jit(solution)/shard_map/attend_fresh/pallas_call | solution.py:76
  47.1 0.8 %combine.2 = (bf16[128,768]{1,0:T(8,128)(2,1)S(1)}, bf16[128,384]{1,0:T(8,128)(2,1)S(1)}, bf16[128,384]{1,0:T(8,128)(2,1)S(1)}) custom-call(f32[128,768]{1,0:T(8,128)S(1)} %get-tuple-element.59.refs_0_, f32[8,128]{1,0:T(8,128)S(1)} %get-tuple-element.60.refs_1_, f32[256,768]{1,0:T(8,128)S(1)} %get-tuple-element.74.refs_2_, ...), custom_call_target="tpu_custom_call" | custom-call | flops 150994 | bytes 3262 | tf_op jit(solution)/shard_map/combine/pallas_call | solution.py:76
  48.0 0.1 collective-permute-start.17
  48.1 0.5 collective-permute-start.18
  48.6 0.7 %project.2 = (bf16[128,768]{1,0:T(8,128)(2,1)S(1)}, bf16[128,768]{1,0:T(8,128)(2,1)S(1)}, bf16[128,768]{1,0:T(8,128)(2,1)S(1)}) custom-call(bf16[128,768]{1,0:T(8,128)(2,1)S(1)} %get-tuple-element.76.refs_0_, bf16[768,3072]{1,0:T(8,128)(2,1)S(1)} %bitcast.4), custom_call_target="tpu_custom_call" | custom-call | flops 301989 | bytes 2752 | tf_op jit(solution)/shard_map/project/pallas_call | solution.py:76
  49.2 0.1 collective-permute-done.17.refs_1_
  49.4 0.2 collective-permute-done.18.refs_2_
  49.6 1.0 %collective-permute-start.19 = (bf16[128,768]{1,0:T(8,128)(2,1)S(1)}, bf16[128,768]{1,0:T(8,128)(2,1)S(1)}, u32[]{:S(2)}, u32[]{:S(2)}) collective-permute-start(bf16[128,768]{1,0:T(8,128)(2,1)S(1)} %sum_cores.2.refs_6_), channel_id=1, source_target_pairs={{0,2},{1,3},{2,0},{3,1},{4,6},{5,7},{6,4},{7,5},{8,10},{9,11},{10,... | collective-permute-start | bytes 589832 | tf_op jit(solution)/shard_map/ppermute | solution.py:32
  50.6 3.6 %collective-permute-done.20.refs_4_ = bf16[144,768]{1,0:T(8,128)(2,1)S(1)} collective-permute-done((bf16[144,768]{1,0:T(8,128)(2,1)S(1)}, bf16[144,768]{1,0:T(8,128)(2,1)S(1)}, u32[]{:S(2)}, u32[]{:S(2)}) %collective-permute-start.20) | collective-permute-done | bytes 221216 | tf_op jit(solution)/shard_map/ppermute | solution.py:32
  54.2 0.8 %combine.3 = (bf16[128,768]{1,0:T(8,128)(2,1)S(1)}, bf16[128,384]{1,0:T(8,128)(2,1)S(1)}, bf16[128,384]{1,0:T(8,128)(2,1)S(1)}) custom-call(f32[128,768]{1,0:T(8,128)S(1)} %get-tuple-element.82.refs_0_, f32[8,128]{1,0:T(8,128)S(1)} %get-tuple-element.83.refs_1_, f32[256,768]{1,0:T(8,128)S(1)} %get-tuple-element.74.refs_2_, ...), custom_call_target="tpu_custom_call" | custom-call | flops 150994 | bytes 3262 | tf_op jit(solution)/shard_map/combine/pallas_call | solution.py:76
  55.1 0.5 collective-permute-start.23
  55.6 0.1 collective-permute-start.16
  55.7 0.7 %project.3 = (bf16[128,768]{1,0:T(8,128)(2,1)S(1)}, bf16[128,768]{1,0:T(8,128)(2,1)S(1)}, bf16[128,768]{1,0:T(8,128)(2,1)S(1)}) custom-call(bf16[128,768]{1,0:T(8,128)(2,1)S(1)} %get-tuple-element.84.refs_0_, bf16[768,3072]{1,0:T(8,128)(2,1)S(1)} %bitcast.4), custom_call_target="tpu_custom_call" | custom-call | flops 301989 | bytes 2752 | tf_op jit(solution)/shard_map/project/pallas_call | solution.py:76
  56.4 0.5 collective-permute-start.21
  57.0 1.1 %collective-permute-start.24 = (bf16[128,768]{1,0:T(8,128)(2,1)S(1)}, bf16[128,768]{1,0:T(8,128)(2,1)S(1)}, u32[]{:S(2)}, u32[]{:S(2)}) collective-permute-start(bf16[128,768]{1,0:T(8,128)(2,1)S(1)} %sum_cores.3.refs_7_), channel_id=1, source_target_pairs={{0,2},{1,3},{2,0},{3,1},{4,6},{5,7},{6,4},{7,5},{8,10},{9,11},{10,... | collective-permute-start | bytes 589832 | tf_op jit(solution)/shard_map/ppermute | solution.py:32
  58.1 2.2 %update_caches.1 = (bf16[2048,256]{1,0:T(8,128)(2,1)}, bf16[2048,256]{1,0:T(8,128)(2,1)}, f32[8,128]{1,0:T(8,128)S(1)}) custom-call(bf16[256,256]{1,0:T(8,128)(2,1)S(1)} %get-tuple-element.63.refs_1_.refs_2_.refs_0_, bf16[256,256]{1,0:T(8,128)(2,1)S(1)} %get-tuple-element.71.refs_3_.refs_1_, bf16[256,256]{1,0:T(8,128)(2,1)S(1)} %get-tuple-element.72.refs_4_.refs_2_, ...), custom_call_target="tpu_custom_call" | custom-call | flops 67108 | bytes 2361 | tf_op jit(solution)/shard_map/update_caches/pallas_call | solution.py:76
  60.3 0.1 collect.1
  60.4 3.5 %collective-permute-done.24.refs_2_ = bf16[128,768]{1,0:T(8,128)(2,1)S(1)} collective-permute-done((bf16[128,768]{1,0:T(8,128)(2,1)S(1)}, bf16[128,768]{1,0:T(8,128)(2,1)S(1)}, u32[]{:S(2)}, u32[]{:S(2)}) %collective-permute-start.24) | collective-permute-done | bytes 196640 | tf_op jit(solution)/shard_map/ppermute | solution.py:32
  63.9 0.8 %finish.1 = bf16[256,768]{1,0:T(8,128)(2,1)} custom-call(bf16[128,768]{1,0:T(8,128)(2,1)S(1)} %get-tuple-element.91.refs_0_, f32[128,768]{1,0:T(8,128)S(1)} %get-tuple-element.92.refs_1_, bf16[128,768]{1,0:T(8,128)(2,1)S(1)} %collective-permute-done.24.refs_2_), custom_call_target="tpu_custom_call" | custom-call | bytes 589 | tf_op jit(solution)/shard_map/finish/pallas_call | solution.py:76
  (54 shorter events, 0.6 us)
Async XLA Ops:
  0.6 12.4 %collective-permute-start = (bf16[256,768]{1,0:T(8,128)(2,1)}, bf16[256,768]{1,0:T(8,128)(2,1)S(1)}, u32[]{:S(2)}, u32[]{:S(2)}) collective-permute-start(bf16[256,768]{1,0:T(8,128)(2,1)} %refs_0_.3), channel_id=1, source_target_pairs={{0,2},{1,3},{2,0},{3,1},{4,6},{5,7},{6,4},{7,5},{8,10},{9,11},{10,... | collective-permute-start | bytes 1179656 | tf_op jit(solution)/shard_map/ppermute | solution.py:32
  3.7 14.1 %collective-permute-start.1 = (bf16[256,768]{1,0:T(8,128)(2,1)}, bf16[256,768]{1,0:T(8,128)(2,1)S(1)}, u32[]{:S(2)}, u32[]{:S(2)}) collective-permute-start(bf16[256,768]{1,0:T(8,128)(2,1)} %refs_0_.3), channel_id=1, source_target_pairs={{0,1},{1,0},{2,3},{3,2},{4,5},{5,4},{6,7},{7,6},{8,9},{9,8},{10,11... | collective-permute-start | bytes 1179656 | tf_op jit(solution)/shard_map/ppermute | solution.py:37
  3.7 1.0 %copy-start.5 = (bf16[256,768]{1,0:T(8,128)(2,1)S(1)}, bf16[256,768]{1,0:T(8,128)(2,1)}, u32[]{:S(2)}) copy-start(bf16[256,768]{1,0:T(8,128)(2,1)} %refs_0_.3) | copy-start | bytes 1179652
  4.7 2.7 %copy-start.6 = (s32[4]{0:T(128)S(1)}, s32[4]{0:T(128)}, u32[]{:S(2)}) copy-start(s32[4]{0:T(128)} %refs_6_.7) | copy-start | bytes 52
  4.8 2.7 %copy-start.7 = (s32[4]{0:T(128)S(1)}, s32[4]{0:T(128)}, u32[]{:S(2)}) copy-start(s32[4]{0:T(128)} %refs_1_.4) | copy-start | bytes 52
  4.8 4.3 %copy-start.2 = (bf16[2048,256]{1,0:T(8,128)(2,1)S(1)}, bf16[2048,256]{1,0:T(8,128)(2,1)}, u32[]{:S(2)}) copy-start(bf16[2048,256]{1,0:T(8,128)(2,1)} %refs_4_.1) | copy-start | bytes 3145732
  4.8 4.3 %copy-start.3 = (bf16[2048,256]{1,0:T(8,128)(2,1)S(1)}, bf16[2048,256]{1,0:T(8,128)(2,1)}, u32[]{:S(2)}) copy-start(bf16[2048,256]{1,0:T(8,128)(2,1)} %refs_5_.5) | copy-start | bytes 3145732
  4.8 12.5 %collective-permute-start.4 = (bf16[128,768]{1,0:T(8,128)(2,1)S(1)}, bf16[128,768]{1,0:T(8,128)(2,1)S(1)}, u32[]{:S(2)}, u32[]{:S(2)}) collective-permute-start(bf16[128,768]{1,0:T(8,128)(2,1)S(1)} %get-tuple-element.58), channel_id=1, source_target_pairs={{0,16},{4,20},{8,24},{12,28},{16,0},{20,4},{24,8},{28,12},{1,17},{... | collective-permute-start | bytes 589832 | tf_op jit(solution)/shard_map/ppermute | solution.py:32
  7.4 11.8 %slice-start = ((s8[4718592]{0:T(1024)(128)(4,1)}), s8[4194304]{0:T(1024)(128)(4,1)S(1)}, s32[]{:S(2)}) async-start(s8[4718592]{0:T(1024)(128)(4,1)} %bitcast.1), calls=%async_computation | async-start | bytes 8388608
  7.5 11.7 %slice-start.1 = ((s8[4718592]{0:T(1024)(128)(4,1)}), s8[524288]{0:T(1024)(128)(4,1)S(1)}, s32[]{:S(2)}) async-start(s8[4718592]{0:T(1024)(128)(4,1)} %bitcast.1), calls=%async_computation.1 | async-start | bytes 1048576
  13.0 6.3 %copy-start.4 = (f32[3072]{0:T(1024)S(1)}, f32[3072]{0:T(1024)}, u32[]{:S(2)}) copy-start(f32[3072]{0:T(1024)} %param.11) | copy-start | bytes 36868
  13.1 9.8 %collective-permute-start.5 = (bf16[128,768]{1,0:T(8,128)(2,1)S(1)}, bf16[128,768]{1,0:T(8,128)(2,1)S(1)}, u32[]{:S(2)}, u32[]{:S(2)}) collective-permute-start(bf16[128,768]{1,0:T(8,128)(2,1)S(1)} %get-tuple-element.62), channel_id=1, source_target_pairs={{0,1},{1,0},{2,3},{3,2},{4,5},{5,4},{6,7},{7,6},{8,9},{9,8},{10,11... | collective-permute-start | bytes 589832 | tf_op jit(solution)/shard_map/ppermute | solution.py:37
  13.1 12.6 %collective-permute-start.7 = (bf16[128,768]{1,0:T(8,128)(2,1)S(1)}, bf16[128,768]{1,0:T(8,128)(2,1)S(1)}, u32[]{:S(2)}, u32[]{:S(2)}) collective-permute-start(bf16[128,768]{1,0:T(8,128)(2,1)S(1)} %relay.8.refs_1_), channel_id=1, source_target_pairs={{0,16},{4,20},{8,24},{12,28},{16,0},{20,4},{24,8},{28,12},{1,17},{... | collective-permute-start | bytes 589832 | tf_op jit(solution)/shard_map/ppermute | solution.py:32
  17.3 8.5 %collective-permute-start.6 = (bf16[128,768]{1,0:T(8,128)(2,1)S(1)}, bf16[128,768]{1,0:T(8,128)(2,1)S(1)}, u32[]{:S(2)}, u32[]{:S(2)}) collective-permute-start(bf16[128,768]{1,0:T(8,128)(2,1)S(1)} %relay.10.refs_12_.refs_0_), channel_id=1, source_target_pairs={{0,2},{1,3},{2,0},{3,1},{4,6},{5,7},{6,4},{7,5},{8,10},{9,11},{10,... | collective-permute-start | bytes 589832 | tf_op jit(solution)/shard_map/ppermute | solution.py:32
  17.8 1.3 %collective-permute-start.2 = (bf16[64,768]{1,0:T(8,128)(2,1)S(1)}, bf16[64,768]{1,0:T(8,128)(2,1)S(1)}, u32[]{:S(2)}, u32[]{:S(2)}) collective-permute-start(bf16[64,768]{1,0:T(8,128)(2,1)S(1)} %get-tuple-element.54), channel_id=1, source_target_pairs={{0,1},{1,0},{2,3},{3,2},{4,5},{5,4},{6,7},{7,6},{8,9},{9,8},{10,11... | collective-permute-start | bytes 294920 | tf_op jit(solution)/shard_map/ppermute | solution.py:37
  17.8 1.5 %collective-permute-start.3 = (bf16[64,768]{1,0:T(8,128)(2,1)S(1)}, bf16[64,768]{1,0:T(8,128)(2,1)S(1)}, u32[]{:S(2)}, u32[]{:S(2)}) collective-permute-start(bf16[64,768]{1,0:T(8,128)(2,1)S(1)} %get-tuple-element.55), channel_id=1, source_target_pairs={{0,1},{1,0},{2,3},{3,2},{4,5},{5,4},{6,7},{7,6},{8,9},{9,8},{10,11... | collective-permute-start | bytes 294920 | tf_op jit(solution)/shard_map/ppermute | solution.py:37
  19.1 8.9 %collective-permute-start.8 = (bf16[128,768]{1,0:T(8,128)(2,1)S(1)}, bf16[128,768]{1,0:T(8,128)(2,1)S(1)}, u32[]{:S(2)}, u32[]{:S(2)}) collective-permute-start(bf16[128,768]{1,0:T(8,128)(2,1)S(1)} %relay.10.refs_12_.refs_0_), channel_id=1, source_target_pairs={{0,1},{1,0},{2,3},{3,2},{4,5},{5,4},{6,7},{7,6},{8,9},{9,8},{10,11... | collective-permute-start | bytes 589832 | tf_op jit(solution)/shard_map/ppermute | solution.py:37
  19.3 3.6 %copy-start = (bf16[3072,256]{1,0:T(8,128)(2,1)S(1)}, bf16[3072,256]{1,0:T(8,128)(2,1)}, u32[]{:S(2)}) copy-start(bf16[3072,256]{1,0:T(8,128)(2,1)} %refs_11_.1) | copy-start | bytes 4718596
  19.3 3.6 %copy-start.1 = (bf16[3072,256]{1,0:T(8,128)(2,1)S(1)}, bf16[3072,256]{1,0:T(8,128)(2,1)}, u32[]{:S(2)}) copy-start(bf16[3072,256]{1,0:T(8,128)(2,1)} %refs_12_.1) | copy-start | bytes 4718596
  25.8 2.2 %collective-permute-start.9 = (bf16[64,768]{1,0:T(8,128)(2,1)S(1)}, bf16[64,768]{1,0:T(8,128)(2,1)S(1)}, u32[]{:S(2)}, u32[]{:S(2)}) collective-permute-start(bf16[64,768]{1,0:T(8,128)(2,1)S(1)} %get-tuple-element.65), channel_id=1, source_target_pairs={{0,1},{1,0},{2,3},{3,2},{4,5},{5,4},{6,7},{7,6},{8,9},{9,8},{10,11... | collective-permute-start | bytes 294920 | tf_op jit(solution)/shard_map/ppermute | solution.py:37
  25.9 2.1 %collective-permute-start.10 = (bf16[64,768]{1,0:T(8,128)(2,1)S(1)}, bf16[64,768]{1,0:T(8,128)(2,1)S(1)}, u32[]{:S(2)}, u32[]{:S(2)}) collective-permute-start(bf16[64,768]{1,0:T(8,128)(2,1)S(1)} %get-tuple-element.66), channel_id=1, source_target_pairs={{0,1},{1,0},{2,3},{3,2},{4,5},{5,4},{6,7},{7,6},{8,9},{9,8},{10,11... | collective-permute-start | bytes 294920 | tf_op jit(solution)/shard_map/ppermute | solution.py:37
  26.4 9.0 %collective-permute-start.11 = (bf16[128,768]{1,0:T(8,128)(2,1)S(1)}, bf16[128,768]{1,0:T(8,128)(2,1)S(1)}, u32[]{:S(2)}, u32[]{:S(2)}) collective-permute-start(bf16[128,768]{1,0:T(8,128)(2,1)S(1)} %relay.11.refs_1_.refs_12_.refs_0_), channel_id=1, source_target_pairs={{0,2},{1,3},{2,0},{3,1},{4,6},{5,7},{6,4},{7,5},{8,10},{9,11},{10,... | collective-permute-start | bytes 589832 | tf_op jit(solution)/shard_map/ppermute | solution.py:32
  31.5 15.6 %collective-permute-start.15 = (bf16[144,768]{1,0:T(8,128)(2,1)S(1)}, bf16[144,768]{1,0:T(8,128)(2,1)S(1)}, u32[]{:S(2)}, u32[]{:S(2)}) collective-permute-start(bf16[144,768]{1,0:T(8,128)(2,1)S(1)} %attend_partner.2.refs_13_), channel_id=1, source_target_pairs={{0,16},{4,20},{8,24},{12,28},{16,0},{20,4},{24,8},{28,12},{1,17},{... | collective-permute-start | bytes 663560 | tf_op jit(solution)/shard_map/ppermute | solution.py:32
  31.6 4.5 %collective-permute-start.12 = (bf16[128,768]{1,0:T(8,128)(2,1)S(1)}, bf16[128,768]{1,0:T(8,128)(2,1)S(1)}, u32[]{:S(2)}, u32[]{:S(2)}) collective-permute-start(bf16[128,768]{1,0:T(8,128)(2,1)S(1)} %relay.11.refs_1_.refs_12_.refs_0_), channel_id=1, source_target_pairs={{0,1},{1,0},{2,3},{3,2},{4,5},{5,4},{6,7},{7,6},{8,9},{9,8},{10,11... | collective-permute-start | bytes 589832 | tf_op jit(solution)/shard_map/ppermute | solution.py:37
  35.4 1.5 %collective-permute-start.13 = (bf16[64,768]{1,0:T(8,128)(2,1)S(1)}, bf16[64,768]{1,0:T(8,128)(2,1)S(1)}, u32[]{:S(2)}, u32[]{:S(2)}) collective-permute-start(bf16[64,768]{1,0:T(8,128)(2,1)S(1)} %get-tuple-element.69), channel_id=1, source_target_pairs={{0,1},{1,0},{2,3},{3,2},{4,5},{5,4},{6,7},{7,6},{8,9},{9,8},{10,11... | collective-permute-start | bytes 294920 | tf_op jit(solution)/shard_map/ppermute | solution.py:37
  36.0 1.3 %collective-permute-start.14 = (bf16[64,768]{1,0:T(8,128)(2,1)S(1)}, bf16[64,768]{1,0:T(8,128)(2,1)S(1)}, u32[]{:S(2)}, u32[]{:S(2)}) collective-permute-start(bf16[64,768]{1,0:T(8,128)(2,1)S(1)} %get-tuple-element.70), channel_id=1, source_target_pairs={{0,1},{1,0},{2,3},{3,2},{4,5},{5,4},{6,7},{7,6},{8,9},{9,8},{10,11... | collective-permute-start | bytes 294920 | tf_op jit(solution)/shard_map/ppermute | solution.py:37
  37.3 9.8 %slice-start.2 = ((s8[4718592]{0:T(1024)(128)(4,1)}), s8[4194304]{0:T(1024)(128)(4,1)S(1)}, s32[]{:S(2)}) async-start(s8[4718592]{0:T(1024)(128)(4,1)} %bitcast.3), calls=%async_computation.2 | async-start | bytes 8388608
  37.3 9.8 %slice-start.3 = ((s8[4718592]{0:T(1024)(128)(4,1)}), s8[524288]{0:T(1024)(128)(4,1)S(1)}, s32[]{:S(2)}) async-start(s8[4718592]{0:T(1024)(128)(4,1)} %bitcast.3), calls=%async_computation.3 | async-start | bytes 1048576
  40.8 13.4 %collective-permute-start.20 = (bf16[144,768]{1,0:T(8,128)(2,1)S(1)}, bf16[144,768]{1,0:T(8,128)(2,1)S(1)}, u32[]{:S(2)}, u32[]{:S(2)}) collective-permute-start(bf16[144,768]{1,0:T(8,128)(2,1)S(1)} %attend_partner.3.refs_15_), channel_id=1, source_target_pairs={{0,16},{4,20},{8,24},{12,28},{16,0},{20,4},{24,8},{28,12},{1,17},{... | collective-permute-start | bytes 663560 | tf_op jit(solution)/shard_map/ppermute | solution.py:32
  48.0 1.4 %collective-permute-start.17 = (bf16[128,384]{1,0:T(8,128)(2,1)S(1)}, bf16[128,384]{1,0:T(8,128)(2,1)S(1)}, u32[]{:S(2)}, u32[]{:S(2)}) collective-permute-start(bf16[128,384]{1,0:T(8,128)(2,1)S(1)} %get-tuple-element.80), channel_id=1, source_target_pairs={{0,1},{1,0},{2,3},{3,2},{4,5},{5,4},{6,7},{7,6},{8,9},{9,8},{10,11... | collective-permute-start | bytes 294920 | tf_op jit(solution)/shard_map/ppermute | solution.py:37
  48.1 1.4 %collective-permute-start.18 = (bf16[128,384]{1,0:T(8,128)(2,1)S(1)}, bf16[128,384]{1,0:T(8,128)(2,1)S(1)}, u32[]{:S(2)}, u32[]{:S(2)}) collective-permute-start(bf16[128,384]{1,0:T(8,128)(2,1)S(1)} %get-tuple-element.81), channel_id=1, source_target_pairs={{0,1},{1,0},{2,3},{3,2},{4,5},{5,4},{6,7},{7,6},{8,9},{9,8},{10,11... | collective-permute-start | bytes 294920 | tf_op jit(solution)/shard_map/ppermute | solution.py:37
  49.6 7.3 %collective-permute-start.19 = (bf16[128,768]{1,0:T(8,128)(2,1)S(1)}, bf16[128,768]{1,0:T(8,128)(2,1)S(1)}, u32[]{:S(2)}, u32[]{:S(2)}) collective-permute-start(bf16[128,768]{1,0:T(8,128)(2,1)S(1)} %sum_cores.2.refs_6_), channel_id=1, source_target_pairs={{0,2},{1,3},{2,0},{3,1},{4,6},{5,7},{6,4},{7,5},{8,10},{9,11},{10,... | collective-permute-start | bytes 589832 | tf_op jit(solution)/shard_map/ppermute | solution.py:32
  55.0 1.8 %collective-permute-start.22 = (bf16[128,384]{1,0:T(8,128)(2,1)S(1)}, bf16[128,384]{1,0:T(8,128)(2,1)S(1)}, u32[]{:S(2)}, u32[]{:S(2)}) collective-permute-start(bf16[128,384]{1,0:T(8,128)(2,1)S(1)} %get-tuple-element.88), channel_id=1, source_target_pairs={{0,1},{1,0},{2,3},{3,2},{4,5},{5,4},{6,7},{7,6},{8,9},{9,8},{10,11... | collective-permute-start | bytes 294920 | tf_op jit(solution)/shard_map/ppermute | solution.py:37
  55.1 1.8 %collective-permute-start.23 = (bf16[128,384]{1,0:T(8,128)(2,1)S(1)}, bf16[128,384]{1,0:T(8,128)(2,1)S(1)}, u32[]{:S(2)}, u32[]{:S(2)}) collective-permute-start(bf16[128,384]{1,0:T(8,128)(2,1)S(1)} %get-tuple-element.89), channel_id=1, source_target_pairs={{0,1},{1,0},{2,3},{3,2},{4,5},{5,4},{6,7},{7,6},{8,9},{9,8},{10,11... | collective-permute-start | bytes 294920 | tf_op jit(solution)/shard_map/ppermute | solution.py:37
  55.6 4.7 %collective-permute-start.16 = (bf16[128,768]{1,0:T(8,128)(2,1)S(1)}, bf16[128,768]{1,0:T(8,128)(2,1)S(1)}, u32[]{:S(2)}, u32[]{:S(2)}) collective-permute-start(bf16[128,768]{1,0:T(8,128)(2,1)S(1)} %get-tuple-element.78.refs_3_), channel_id=1, source_target_pairs={{0,1},{1,0},{2,3},{3,2},{4,5},{5,4},{6,7},{7,6},{8,9},{9,8},{10,11... | collective-permute-start | bytes 589832 | tf_op jit(solution)/shard_map/ppermute | solution.py:37
  56.4 3.9 %collective-permute-start.21 = (bf16[128,768]{1,0:T(8,128)(2,1)S(1)}, bf16[128,768]{1,0:T(8,128)(2,1)S(1)}, u32[]{:S(2)}, u32[]{:S(2)}) collective-permute-start(bf16[128,768]{1,0:T(8,128)(2,1)S(1)} %get-tuple-element.86.refs_3_), channel_id=1, source_target_pairs={{0,1},{1,0},{2,3},{3,2},{4,5},{5,4},{6,7},{7,6},{8,9},{9,8},{10,11... | collective-permute-start | bytes 589832 | tf_op jit(solution)/shard_map/ppermute | solution.py:37
  57.0 6.9 %collective-permute-start.24 = (bf16[128,768]{1,0:T(8,128)(2,1)S(1)}, bf16[128,768]{1,0:T(8,128)(2,1)S(1)}, u32[]{:S(2)}, u32[]{:S(2)}) collective-permute-start(bf16[128,768]{1,0:T(8,128)(2,1)S(1)} %sum_cores.3.refs_7_), channel_id=1, source_target_pairs={{0,2},{1,3},{2,0},{3,1},{4,6},{5,7},{6,4},{7,5},{8,10},{9,11},{10,... | collective-permute-start | bytes 589832 | tf_op jit(solution)/shard_map/ppermute | solution.py:32
